TPU v7x, 32 devices: a whole 2x2x4 slice. The times are simulated.
32 devices in a mesh: groups: 2 (over y), dom: 4 (over x, core), col: 4 (over z).
Axes of the slice: x: 2, y: 2, z: 4, core: 2. Of those that a mesh axis runs over, the one named last changes fastest.
Arguments:
- sigma_next: bfloat16 [8, 2048, 2048], P(('groups', 'dom'), 'col'), parts along dimension 0, as said below
- separator: bfloat16 [8, 2048, 2048], P(('groups', 'dom'), 'col'), parts along dimension 0, as said below
- inverse_pivot: bfloat16 [8, 2048, 2048], P(('groups', 'dom'), 'col'), parts along dimension 0
- coupling_rate: float32 [8], P(('groups', 'dom')), parts along dimension 0, may hold values from 0.15 to 0.45
- lengths: int32 [8], P(('groups', 'dom')), parts along dimension 0, may hold values from 1 to 4, 10 in all
- step_index: int32 [8], P(('groups', 'dom')), parts along dimension 0, may hold values from 0 to 3
- node_class: int32 [4096], P('groups'), parts along dimension 0, may hold values from 0 to 3
Outputs:
- covariance: bfloat16 [8, 2048, 2048], P(('groups', 'dom'), 'col'), parts along dimension 0
- variances: float32 [8, 2048], P(('groups', 'dom'), 'col'), parts along dimension 0
There are 2 independent parts, one for each index of `groups`. A program takes and returns all parts, laid end to end along the dimension named above; each array names one. Nothing has to cross between parts.
Inputs may be any that keep to these rules, and one draw needn't show every extreme that they name: Every block of sigma_next is exactly symmetric. Every block of separator is exactly symmetric.
All inputs are finite; a program needn't handle non-finite values. No bound on the sum of `lengths` on one device may be relied on, other than what follows from the above.
Results may differ from a plain program's by a relative error of at most 0.0027.
Values may be sent and summed in bfloat16 or wider, within the bound.
No kernel may reach another device: no remote copies, remote signals or barrier semaphores. Data moves between devices by JAX's collectives and lax.ppermute only.
A program may use at most 192 MiB of HBM per device.

v0:
```python
import jax
import jax.numpy as jnp
from jax import lax
from jax.sharding import PartitionSpec as P

GX = 64
GY = 32


def passed_along(value, axis, steps):
    count = lax.axis_size(axis)
    initial, last = (max(0, -steps), min(count, count - steps))
    return lax.ppermute(value, axis, [(source, source + steps) for source in range(initial, last)])


def class_weights(node_class):
    picks = (node_class[:, None] == jnp.arange(4)[None, :]).astype(jnp.float32)
    across_weight = picks @ jnp.array([0.25, 0.375, 0.125, 0.5], jnp.float32)
    along_weight = picks @ jnp.array([0.25, 0.125, 0.375, 0.0], jnp.float32)
    return (across_weight, along_weight)


def couple(panel, node_class, rate):
    across_weight, along_weight = class_weights(node_class)
    count = panel.shape[0]
    grid = panel.reshape(count, GY, GX)
    padded = jnp.pad(grid, ((0, 0), (1, 1), (1, 1)))
    across = (padded[:, 1:-1, :-2] + padded[:, 1:-1, 2:]).reshape(count, GY * GX)
    along = (padded[:, :-2, 1:-1] + padded[:, 2:, 1:-1]).reshape(count, GY * GX)
    return rate * (panel + across_weight * across + along_weight * along)


def local(sigma_next, separator, inverse_pivot, coupling_rate, lengths, step_index, node_class):
    shifted = passed_along(separator, "dom", -1)
    prior = jnp.where(step_index[0] == 0, shifted[0], sigma_next[0])
    pivot = inverse_pivot[0].astype(jnp.float32)
    rate = coupling_rate[0]
    coupled = couple(pivot, node_class, rate).astype(jnp.bfloat16)
    panel_rows = coupled.shape[0]
    half = jnp.dot(
        coupled,
        lax.all_gather(prior, "col", axis=0, tiled=True),
        preferred_element_type=jnp.float32,
    ).astype(jnp.bfloat16)
    remade = couple(
        lax.all_gather(inverse_pivot[0], "col", axis=0, tiled=True).astype(jnp.float32),
        node_class,
        rate,
    ).astype(jnp.bfloat16)
    product = lax.dot_general(
        half, remade, (((1,), (1,)), ((), ())), preferred_element_type=jnp.float32
    )
    full = pivot + product
    active = step_index[0] < lengths[0]
    old = sigma_next[0]
    covariance = jnp.where(active, full.astype(jnp.bfloat16), old)
    first_col = lax.axis_index("col") * panel_rows
    new_block = lax.dynamic_slice_in_dim(full, first_col, panel_rows, 1)
    old_block = lax.dynamic_slice_in_dim(old, first_col, panel_rows, 1)
    variances = jnp.where(
        active, jnp.diagonal(new_block), jnp.diagonal(old_block).astype(jnp.float32)
    )
    return (covariance[None], variances[None])


def solution(mesh):
    return jax.shard_map(
        local,
        mesh=mesh,
        in_specs=(
            P(("groups", "dom"), "col", None),
            P(("groups", "dom"), "col", None),
            P(("groups", "dom"), "col", None),
            P(("groups", "dom")),
            P(("groups", "dom")),
            P(("groups", "dom")),
            P("groups"),
        ),
        out_specs=(P(("groups", "dom"), "col", None), P(("groups", "dom"), "col")),
        check_vma=False,
    )
```

profile of v0, /device:TPU:1, one launch (start us, length us, event | category | flops | bytes accessed | tf_op | source)
XLA Modules:
  0.0 349.2 jit_solution(18086054180317907071)
XLA Ops:
  7.2 0.0 all-gather.6.cloned.1.call-start
  7.2 4.1 %copy.13 = bf16[1,512,2048]{1,2,0:T(8,128)(2,1)} copy(bf16[1,512,2048]{2,1,0:T(8,128)(2,1)} %param.13) | data formatting | bytes 4194304 | tf_op args[2]
  11.3 0.0 all-gather.6.cloned.1.call-update
  11.3 0.0 all-gather.4.cloned.1.call-start
  11.4 2.0 collective-permute-start
  14.0 26.0 %collective-permute-done = bf16[1,512,2048]{2,1,0:T(8,128)(2,1)S(1)} collective-permute-done((bf16[1,512,2048]{2,1,0:T(8,128)(2,1)S(1)}, bf16[1,512,2048]{2,1,0:T(8,128)(2,1)S(1)}, u32[]{:S(2)}, u32[]{:S(2)}) %collective-permute-start) | collective-permute-done | bytes 2097184 | tf_op jit(solution)/shard_map/ppermute | solution.py:13
  40.0 3.3 bitcast_select_fusion.1
  44.0 3.0 pad_convert_fusion
  47.0 12.5 %slice_add_fusion.1 = (f32[512,32,64]{0,2,1:T(8,128)}, f32[512,32,64]{0,2,1:T(8,128)}) fusion(f32[512,34,66]{0,2,1:T(8,128)} %pad_convert_fusion), kind=kLoop, calls=%fused_computation.20 | loop fusion | flops 2097152 | bytes 25165824 | tf_op jit(solution)/shard_map/add | solution.py:28
  59.5 5.4 %copy.14 = f32[512,2048]{1,0:T(8,128)} copy(f32[512,2048]{0,1:T(8,128)} %bitcast.68) | data formatting | bytes 8388608 | tf_op jit(solution)/shard_map/reshape | solution.py:28
  64.9 5.6 %copy.15 = f32[512,2048]{1,0:T(8,128)} copy(f32[512,2048]{0,1:T(8,128)} %bitcast.67) | data formatting | bytes 8388608 | tf_op jit(solution)/shard_map/reshape | solution.py:29
  71.3 4.8 %gather_fusion.1 = bf16[512]{0:T(512)(128)(2,1)S(1)} fusion(bf16[512,512]{1,0:T(8,128)(2,1)S(1)} %dynamic-slice_bitcast_fusion, s32[512]{0:T(512)S(1)} %bitcast.63), kind=kCustom, calls=%fused_computation.1 | custom fusion | bytes 6144 | tf_op jit(solution)/shard_map/jit(diagonal)/cond/branch_0_fun/gather | solution.py:61
  76.1 0.5 fusion.16
  76.6 0.5 fusion.15
  77.0 86.4 %all-gather.6.cloned.1.call-done = bf16[1,2048,2048]{1,2,0:T(8,128)(2,1)} async-done(((bf16[1,512,2048]{1,2,0:T(8,128)(2,1)}), bf16[1,2048,2048]{1,2,0:T(8,128)(2,1)}) %all-gather.6.cloned.1.call-update) | async-done | bytes 8388624 | tf_op jit(solution)/shard_map/all_gather | solution.py:46
  163.4 13.1 %convert.13 = f32[2048,32,64]{0,2,1:T(8,128)} convert(bf16[2048,32,64]{0,2,1:T(8,128)(2,1)} %bitcast.65) | non-fusion elementwise | flops 4194304 | bytes 25165824 | tf_op jit(solution)/shard_map/reshape | solution.py:26
  176.5 34.6 %fusion = (f32[2048,32,64]{0,2,1:T(8,128)}, f32[2048,32,64]{0,2,1:T(8,128)}) fusion(f32[2048,32,64]{0,2,1:T(8,128)} %convert.13), kind=kLoop, calls=%fused_computation.6 | loop fusion | flops 8388608 | bytes 50331648 | tf_op jit(solution)/shard_map/add | solution.py:28
  211.1 17.9 %fusion.4 = bf16[2048,2048]{0,1:T(8,128)(2,1)} fusion(f32[2048,32,64]{0,2,1:T(8,128)} %get-tuple-element.3, f32[2048,32,64]{0,2,1:T(8,128)} %get-tuple-element.2, f32[2048]{0:T(1024)S(1)} %bitcast.71, f32[2048]{0:T(1024)S(1)} %bitcast.69, f32[]{:T(128)} %bitcast.62, bf16[1,2048,2048]{1,2,0:T(8,128)(2,1)} %all-gather.6.cloned.1.call-done), kind=kLoop, calls=%fused_computation.11 | loop fusion | flops 29360128 | bytes 50348036 | tf_op jit(solution)/shard_map/convert_element_type | solution.py:49
  228.9 83.9 %all-gather.4.cloned.1.call-done = bf16[2048,2048]{1,0:T(8,128)(2,1)} async-done(((bf16[512,2048]{1,0:T(8,128)(2,1)}), bf16[2048,2048]{1,0:T(8,128)(2,1)}) %all-gather.4.cloned.1.call-update) | async-done | bytes 8388624 | tf_op jit(solution)/shard_map/all_gather | solution.py:42
  312.8 19.2 %convert_add_fusion = f32[512,2048]{1,0:T(8,128)} fusion(bf16[2048,2048]{0,1:T(8,128)(2,1)} %fusion.4, bf16[1,512,2048]{2,1,0:T(8,128)(2,1)} %param.13, bf16[2048,2048]{1,0:T(8,128)(2,1)} %all-gather.4.cloned.1.call-done, f32[512,2048]{1,0:T(8,128)} %copy.15, f32[512,2048]{1,0:T(8,128)} %copy.14, f32[2048]{0:T(1024)S(1)} %bitcast.72, ...), kind=kOutput, calls=%fused_computation.14 | convolution fusion | flops 8600420352 | bytes 31473668 | tf_op jit(solution)/shard_map/dot_general | solution.py:50
  332.1 1.3 constant_dynamic-slice_fusion
  333.4 4.5 %gather_fusion = f32[512]{0:T(512)S(1)} fusion(f32[512,512]{1,0:T(8,128)S(1)} %constant_dynamic-slice_fusion, s32[512]{0:T(512)S(1)} %bitcast.64), kind=kCustom, calls=%fused_computation | custom fusion | bytes 8192 | tf_op jit(solution)/shard_map/jit(diagonal)/cond/branch_0_fun/gather | solution.py:61
  337.9 3.9 %fusion.10 = bf16[1,512,2048]{2,1,0:T(8,128)(2,1)} fusion(bf16[1,512,2048]{2,1,0:T(8,128)(2,1)S(1)} %copy-done.1, f32[512,2048]{1,0:T(8,128)} %convert_add_fusion, pred[]{:T(512)} %bitcast), kind=kLoop, calls=%fused_computation.25 | loop fusion | flops 2097152 | bytes 8388609 | tf_op jit(solution)/shard_map/broadcast_in_dim | solution.py:63
  341.8 0.6 convert_select_fusion
  (15 shorter events, 0.1 us)
Async XLA Ops:
  7.2 4.2 %copy-start.2 = (bf16[1,512,2048]{2,1,0:T(8,128)(2,1)S(1)}, bf16[1,512,2048]{2,1,0:T(8,128)(2,1)}, u32[]{:S(2)}) copy-start(bf16[1,512,2048]{2,1,0:T(8,128)(2,1)} %param.12) | copy-start | bytes 6291460
  7.2 156.2 %all-gather.6.cloned.1.call-start = ((), (), s32[]{:S(2)}) async-start(), calls=%async_computation.1 | async-start | bytes 10485760 | tf_op jit(solution)/shard_map/all_gather | solution.py:46
  11.3 301.5 %all-gather.4.cloned.1.call-start = ((), (), s32[]{:S(2)}) async-start(), calls=%async_computation | async-start | bytes 10485760 | tf_op jit(solution)/shard_map/all_gather | solution.py:42
  11.4 28.6 %collective-permute-start = (bf16[1,512,2048]{2,1,0:T(8,128)(2,1)S(1)}, bf16[1,512,2048]{2,1,0:T(8,128)(2,1)S(1)}, u32[]{:S(2)}, u32[]{:S(2)}) collective-permute-start(bf16[1,512,2048]{2,1,0:T(8,128)(2,1)S(1)} %copy-done.2), channel_id=1, source_target_pairs={{4,0},{8,4},{12,8},{5,1},{9,5},{13,9},{6,2},{10,6},{14,10},{7,3},{... | collective-permute-start | bytes 6291464 | tf_op jit(solution)/shard_map/ppermute | solution.py:13
  40.0 4.0 %copy-start = (bf16[1,512,2048]{1,2,0:T(8,128)(2,1)S(1)}, bf16[1,512,2048]{1,2,0:T(8,128)(2,1)}, u32[]{:S(2)}) copy-start(bf16[1,512,2048]{1,2,0:T(8,128)(2,1)} %copy.13) | copy-start | bytes 6291460
  64.9 6.3 %copy-start.1 = (bf16[1,512,2048]{2,1,0:T(8,128)(2,1)S(1)}, bf16[1,512,2048]{2,1,0:T(8,128)(2,1)}, u32[]{:S(2)}) copy-start(bf16[1,512,2048]{2,1,0:T(8,128)(2,1)} %param.11) | copy-start | bytes 6291460
  64.9 11.2 %copy-start.3 = (s32[2048]{0:T(1024)S(1)}, s32[2048]{0:T(1024)}, u32[]{:S(2)}) copy-start(s32[2048]{0:T(1024)} %param.17) | copy-start | bytes 24580
  64.9 11.2 %copy-start.5 = (bf16[4,1]{0,1:T(2,128)(2,1)S(1)}, bf16[4,1]{0,1:T(2,128)(2,1)}, u32[]{:S(2)}) copy-start(bf16[4,1]{0,1:T(2,128)(2,1)} %constant.92) | copy-start | bytes 28
  64.9 11.7 %copy-start.4 = (bf16[4,1]{0,1:T(2,128)(2,1)S(1)}, bf16[4,1]{0,1:T(2,128)(2,1)}, u32[]{:S(2)}) copy-start(bf16[4,1]{0,1:T(2,128)(2,1)} %constant.91) | copy-start | bytes 28
Sparse Core Ops, SparseCore 0:
  11.4 151.9 all-gather.5
  165.0 147.8 all-gather.3
where the time goes:
time: 350 us; the launch traced here: 349 us
  waiting for transfers between devices  196 us (56%)
  other arithmetic  88.8 us (25%)
  local copies, waits for them, and re-layouts  25.8 us (7%)
  matrix products  20.1 us (6%)
  between operations  16.1 us (5%)
    all_gather x1, waiting for transfers between devices, local(): lax.all_gather(inverse_pivot[0], 'col', axis=0, tiled=True)  86.4 us
    all_gather x1, waiting for transfers between devices, local(): lax.all_gather(prior, 'col', axis=0, tiled=True)  83.9 us
    add x2, other arithmetic, couple(): padded[:, 1:-1, :-2] + padded[:, 1:-1, 2:]  47.1 us
    ppermute x1, waiting for transfers between devices, passed_along(): lax.ppermute(value, axis, [(source, source + steps) for source in range(i...  26 us
    dot_general x1, matrix products, local(): lax.dot_general(half, remade, (((1,), (1,)), ((), ())), preferred_element...  19.2 us
    convert_element_type x1, other arithmetic, local(): remade = couple(lax.all_gather(inverse_pivot[0], 'col', axis=0, tiled=Tru...  17.9 us
    reshape x1, other arithmetic, couple(): grid = panel.reshape(count, GY, GX)  13.1 us
  transfers between devices with their start and end apart: 3, of which 3 were waited for; matrix products, arithmetic and copies ran while one was open for 29% of the time, Pallas kernels for 0%

commit v1 on v0

v1 whole, which is shorter than its diff:
```python
import functools

import jax
import jax.numpy as jnp
from jax import lax
from jax.experimental import pallas as pl
from jax.experimental.pallas import tpu as pltpu
from jax.sharding import PartitionSpec as P

GX = 64
GY = 32
BF16 = jnp.bfloat16
F32 = jnp.float32
MIB = 1 << 20


def passed_along(value, axis, steps):
    count = lax.axis_size(axis)
    initial, last = (max(0, -steps), min(count, count - steps))
    return lax.ppermute(value, axis, [(source, source + steps) for source in range(initial, last)])


def couple_kernel(rate_ref, class_ref, pivot_ref, out_ref, weight_ref):
    nodes = pivot_ref.shape[1]

    @pl.when(pl.program_id(0) == 0)
    def _():
        kind = class_ref[...]
        across = jnp.where(
            kind == 0, 0.25, jnp.where(kind == 1, 0.375, jnp.where(kind == 2, 0.125, 0.5))
        ).astype(F32)
        along = jnp.where(
            kind == 0, 0.25, jnp.where(kind == 1, 0.125, jnp.where(kind == 2, 0.375, 0.0))
        ).astype(F32)
        node = lax.broadcasted_iota(jnp.int32, (1, nodes), 1)
        column = node % GX
        parts = (
            jnp.where(column > 0, across, 0.0),
            jnp.where(column < GX - 1, across, 0.0),
            jnp.where(node >= GX, along, 0.0),
            jnp.where(node < nodes - GX, along, 0.0),
        )
        for which, part in enumerate(parts):
            weight_ref[which] = jnp.broadcast_to(part, (16, nodes))

    rate = rate_ref[0]

    def group(step, carry):
        rows = pl.ds(pl.multiple_of(step * 16, 16), 16)
        value = pivot_ref[rows, :].astype(F32)
        total = (
            value
            + weight_ref[0] * pltpu.roll(value, 1, 1)
            + weight_ref[1] * pltpu.roll(value, nodes - 1, 1)
            + weight_ref[2] * pltpu.roll(value, GX, 1)
            + weight_ref[3] * pltpu.roll(value, nodes - GX, 1)
        )
        out_ref[rows, :] = (rate * total).astype(BF16)
        return carry

    lax.fori_loop(0, pivot_ref.shape[0] // 16, group, 0)


def couple(pivot, node_class, rate):
    rows, nodes = pivot.shape
    chunk = min(rows, 128)
    return pl.pallas_call(
        couple_kernel,
        out_shape=jax.ShapeDtypeStruct((rows, nodes), BF16),
        grid=(rows // chunk,),
        in_specs=[
            pl.BlockSpec(memory_space=pltpu.SMEM),
            pl.BlockSpec((1, nodes), lambda i: (0, 0)),
            pl.BlockSpec((chunk, nodes), lambda i: (i, 0)),
        ],
        out_specs=pl.BlockSpec((chunk, nodes), lambda i: (i, 0)),
        scratch_shapes=[pltpu.VMEM((4, 16, nodes), F32)],
        compiler_params=pltpu.CompilerParams(vmem_limit_bytes=16 * MIB),
        cost_estimate=pl.CostEstimate(
            flops=10 * rows * nodes, bytes_accessed=4 * rows * nodes, transcendentals=0
        ),
        name="couple",
    )(rate, node_class.reshape(1, nodes), pivot)


def turned(block, odd):
    return block + odd * (3 - 2 * block)


def route(source, target, doms):
    pairs = []
    for dom in range(doms):
        odd = dom % 2
        pairs.append((dom * 4 + turned(source, odd), dom * 4 + turned(target, odd)))
    return pairs


def moved(value, source, target):
    return lax.ppermute(value, ("dom", "col"), route(source, target, lax.axis_size("dom")))


def prior_kernel(place_ref, step_ref, shifted_ref, sigma_ref, row_ref, far_ref, near_ref, last_ref):
    odd = place_ref[0]
    width = last_ref.shape[1]

    def fill(source):
        row_ref[...] = source[...]
        for block in (0, 2, 3):
            start = pl.multiple_of(turned(block, odd) * width, 128)
            value = source[:, pl.ds(start, width)]
            at = {0: 0, 2: 1, 3: 2}[block]
            far_ref[:, at * width : (at + 1) * width] = value
            if block >= 2:
                near_ref[:, (block - 2) * width : (block - 1) * width] = value
            if block == 3:
                last_ref[...] = value

    @pl.when(step_ref[0] == 0)
    def _():
        fill(shifted_ref)

    @pl.when(step_ref[0] != 0)
    def _():
        fill(sigma_ref)


def prior_parts(place, step, shifted, sigma):
    rows, nodes = sigma.shape
    chunk = 128
    width = nodes // 4
    out = lambda blocks: jax.ShapeDtypeStruct((rows, blocks * width), BF16)
    spec = lambda blocks: pl.BlockSpec((chunk, blocks * width), lambda i, place, step: (i, 0))
    return pl.pallas_call(
        prior_kernel,
        out_shape=(out(4), out(3), out(2), out(1)),
        grid_spec=pltpu.PrefetchScalarGridSpec(
            num_scalar_prefetch=2,
            grid=(rows // chunk,),
            in_specs=[
                pl.BlockSpec(
                    (chunk, nodes), lambda i, place, step: (jnp.where(step[0] == 0, i, 0), 0)
                ),
                pl.BlockSpec(
                    (chunk, nodes), lambda i, place, step: (jnp.where(step[0] == 0, 0, i), 0)
                ),
            ],
            out_specs=(spec(4), spec(3), spec(2), spec(1)),
        ),
        compiler_params=pltpu.CompilerParams(vmem_limit_bytes=16 * MIB),
        cost_estimate=pl.CostEstimate(
            flops=0, bytes_accessed=7 * rows * nodes, transcendentals=0
        ),
        name="prior_parts",
    )(place, step, shifted, sigma)


def assemble(prior_ref, odd, row_ref, far_ref, near_ref, last_ref):
    width = last_ref.shape[1]

    def put(value, row, column):
        rows = pl.ds(pl.multiple_of(turned(row, odd) * width, 128), width)
        columns = pl.ds(pl.multiple_of(turned(column, odd) * width, 128), width)
        prior_ref[rows, columns] = value

    prior_ref[pl.ds(pl.multiple_of(turned(1, odd) * width, 128), width), :] = row_ref[...]
    for block in (0, 2, 3):
        columns = pl.ds(pl.multiple_of(turned(block, odd) * width, 128), width)
        put(row_ref[:, columns].T, block, 1)
    for at, block in enumerate((0, 2, 3)):
        value = far_ref[:, at * width : (at + 1) * width]
        put(value, 0, block)
        if block:
            put(value.T, block, 0)
    put(near_ref[:, :width], 2, 2)
    value = near_ref[:, width:]
    put(value, 2, 3)
    put(value.T, 3, 2)
    put(last_ref[...], 3, 3)


def half_kernel(count, place_ref, row_ref, far_ref, near_ref, last_ref, *refs):
    coupled_refs, half_refs, prior_ref = refs[:count], refs[count : 2 * count], refs[2 * count]

    @pl.when(place_ref[1] == 1)
    def _():
        assemble(prior_ref, place_ref[0], row_ref, far_ref, near_ref, last_ref)

        def columns_of(step, carry):
            columns = pl.ds(pl.multiple_of(step * 256, 256), 256)
            for coupled_ref, half_ref in zip(coupled_refs, half_refs):
                half_ref[:, columns] = jnp.dot(
                    coupled_ref[...], prior_ref[:, columns], preferred_element_type=F32
                ).astype(BF16)
            return carry

        lax.fori_loop(0, prior_ref.shape[0] // 256, columns_of, 0)


def halves(place, parts, coupled):
    rows, nodes = coupled[0].shape
    count = len(coupled)
    vmem = pl.BlockSpec(memory_space=pltpu.VMEM)
    return pl.pallas_call(
        functools.partial(half_kernel, count),
        out_shape=tuple(jax.ShapeDtypeStruct((rows, nodes), BF16) for _ in coupled),
        in_specs=[pl.BlockSpec(memory_space=pltpu.SMEM)] + [vmem] * (4 + count),
        out_specs=tuple(vmem for _ in coupled),
        scratch_shapes=[pltpu.VMEM((nodes, nodes), BF16)],
        compiler_params=pltpu.CompilerParams(vmem_limit_bytes=40 * MIB),
        cost_estimate=pl.CostEstimate(
            flops=2 * count * rows * nodes * nodes,
            bytes_accessed=(5 + 4 * count) * rows * nodes,
            transcendentals=0,
        ),
        name="halves",
    )(place, *parts, *coupled)


def product_kernel(place_ref, half_ref, c0, c1, c2, c3, out_ref):
    @pl.when(place_ref[1] == 1)
    def _():
        width = out_ref.shape[1] // 4
        for block, coupled_ref in enumerate((c0, c1, c2, c3)):
            start = turned(block, place_ref[0]) * width

            def columns_of(step, carry):
                value = lax.dot_general(
                    half_ref[...],
                    coupled_ref[pl.ds(pl.multiple_of(step * 256, 256), 256), :],
                    (((1,), (1,)), ((), ())),
                    preferred_element_type=F32,
                )
                columns = pl.ds(pl.multiple_of(start + step * 256, 256), 256)
                out_ref[:, columns] = value.astype(BF16)
                return carry

            lax.fori_loop(0, width // 256, columns_of, 0)


def product(place, half, coupled):
    rows, nodes = half.shape
    vmem = pl.BlockSpec(memory_space=pltpu.VMEM)
    return pl.pallas_call(
        product_kernel,
        out_shape=jax.ShapeDtypeStruct((rows, nodes), BF16),
        in_specs=[pl.BlockSpec(memory_space=pltpu.SMEM)] + [vmem] * 5,
        out_specs=vmem,
        compiler_params=pltpu.CompilerParams(vmem_limit_bytes=40 * MIB),
        cost_estimate=pl.CostEstimate(
            flops=2 * rows * nodes * nodes, bytes_accessed=12 * rows * nodes, transcendentals=0
        ),
        name="product",
    )(place, half, *coupled)


def final_kernel(place_ref, active_ref, pivot_ref, q0, q1, q2, q3, sigma_ref, out_ref, var_ref):
    rows, nodes = pivot_ref.shape
    place = place_ref[1]
    start = pl.multiple_of(place_ref[2] * (nodes // 4) + pl.program_id(0) * rows, 128)
    square = (rows, rows)
    on_diagonal = lax.broadcasted_iota(jnp.int32, square, 0) == lax.broadcasted_iota(
        jnp.int32, square, 1
    )

    def diagonal(value):
        return jnp.sum(jnp.where(on_diagonal, value, 0.0), axis=0, keepdims=True)

    for which, product_ref in enumerate((q0, q1, q2, q3)):

        @pl.when((active_ref[0] != 0) & (place == which))
        def _():
            out_ref[...] = (pivot_ref[...].astype(F32) + product_ref[...].astype(F32)).astype(BF16)
            columns = pl.ds(start, rows)
            var_ref[...] = diagonal(
                pivot_ref[:, columns].astype(F32) + product_ref[:, columns].astype(F32)
            )

    @pl.when(active_ref[0] == 0)
    def _():
        out_ref[...] = sigma_ref[...]
        var_ref[...] = diagonal(sigma_ref[:, pl.ds(start, rows)].astype(F32))


def final(place, active, pivot, products, sigma):
    rows, nodes = pivot.shape
    chunk = 128

    def picked(which):
        return pl.BlockSpec(
            (chunk, nodes), lambda i, place, active: (jnp.where(place[1] == which, i, 0), 0)
        )

    return pl.pallas_call(
        final_kernel,
        out_shape=(
            jax.ShapeDtypeStruct((rows, nodes), BF16),
            jax.ShapeDtypeStruct((1, rows), F32),
        ),
        grid_spec=pltpu.PrefetchScalarGridSpec(
            num_scalar_prefetch=2,
            grid=(rows // chunk,),
            in_specs=[pl.BlockSpec((chunk, nodes), lambda i, place, active: (i, 0))]
            + [picked(which) for which in range(4)]
            + [
                pl.BlockSpec(
                    (chunk, nodes), lambda i, place, active: (jnp.where(active[0] == 0, i, 0), 0)
                )
            ],
            out_specs=(
                pl.BlockSpec((chunk, nodes), lambda i, place, active: (i, 0)),
                pl.BlockSpec((1, chunk), lambda i, place, active: (0, i)),
            ),
        ),
        compiler_params=pltpu.CompilerParams(vmem_limit_bytes=16 * MIB),
        cost_estimate=pl.CostEstimate(
            flops=2 * rows * nodes, bytes_accessed=8 * rows * nodes, transcendentals=0
        ),
        name="final",
    )(place, active, pivot, *products, sigma)


def owned(sigma_next, separator, inverse_pivot, coupling_rate, lengths, step_index, node_class):
    sigma, pivot = sigma_next[0], inverse_pivot[0]
    odd = lax.axis_index("dom") % 2
    col = lax.axis_index("col")
    place = jnp.stack([odd, turned(col, odd), col]).astype(jnp.int32)
    active = (step_index < lengths).astype(jnp.int32)

    shifted = passed_along(separator, "dom", -1)[0]
    coupled = couple(pivot, node_class, coupling_rate)
    c2 = moved(coupled, 2, 1)
    c0 = moved(coupled, 0, 1)
    row, far, near, last = prior_parts(place, step_index, shifted, sigma)
    parts = (row, moved(far, 0, 1), moved(near, 2, 1), moved(last, 3, 1))
    c3 = moved(coupled, 3, 1)
    panels = (c0, coupled, c2, c3)
    h0, h1, h2 = halves(place, parts, panels[:3])
    (h3,) = halves(place, parts, panels[3:])
    q3 = product(place, h3, panels)
    r3 = moved(q3, 1, 3)
    q2 = product(place, h2, panels)
    r2 = moved(q2, 1, 2)
    q0 = product(place, h0, panels)
    r0 = moved(q0, 1, 0)
    q1 = product(place, h1, panels)
    covariance, variances = final(place, active, pivot, (r0, q1, r2, r3), sigma)
    return (covariance[None], variances)


def gathered(sigma_next, separator, inverse_pivot, coupling_rate, lengths, step_index, node_class):
    shifted = passed_along(separator, "dom", -1)
    prior = jnp.where(step_index[0] == 0, shifted[0], sigma_next[0])
    pivot = inverse_pivot[0].astype(F32)
    coupled = couple(inverse_pivot[0], node_class, coupling_rate)
    rows = coupled.shape[0]
    half = jnp.dot(
        coupled,
        lax.all_gather(prior, "col", axis=0, tiled=True),
        preferred_element_type=F32,
    ).astype(BF16)
    product = lax.dot_general(
        half,
        lax.all_gather(coupled, "col", axis=0, tiled=True),
        (((1,), (1,)), ((), ())),
        preferred_element_type=F32,
    )
    full = pivot + product
    active = step_index[0] < lengths[0]
    old = sigma_next[0]
    covariance = jnp.where(active, full.astype(BF16), old)
    first_col = lax.axis_index("col") * rows
    new_block = lax.dynamic_slice_in_dim(full, first_col, rows, 1)
    old_block = lax.dynamic_slice_in_dim(old, first_col, rows, 1)
    variances = jnp.where(active, jnp.diagonal(new_block), jnp.diagonal(old_block).astype(F32))
    return (covariance[None], variances[None])


def solution(mesh):
    local = owned if mesh.shape["col"] == 4 and mesh.shape["dom"] % 2 == 0 else gathered
    return jax.shard_map(
        local,
        mesh=mesh,
        in_specs=(
            P(("groups", "dom"), "col", None),
            P(("groups", "dom"), "col", None),
            P(("groups", "dom"), "col", None),
            P(("groups", "dom")),
            P(("groups", "dom")),
            P(("groups", "dom")),
            P("groups"),
        ),
        out_specs=(P(("groups", "dom"), "col", None), P(("groups", "dom"), "col")),
        check_vma=False,
    )
```

time: 350 us -> 184 us (0.53)
  other arithmetic: 88.8 us -> 0.08 us
  waiting for transfers between devices: 196 us -> 119 us
  Pallas kernels: 0 us -> 32.2 us
  matrix products: 20.1 us -> 0 us
  local copies, waits for them, and re-layouts: 25.8 us -> 6.68 us
  starting transfers between devices: 2.04 us -> 20.3 us
  between operations: 16.1 us -> 2.81 us
    all_gather x2 -> x0, waiting for transfers between devices: 170 us -> none  [the longest x1 86.4 us: local(): lax.all_gather(inverse_pivot[0], 'col', axis=0, tiled=True)]
    ppermute x0 -> x9, waiting for transfers between devices: none -> 105 us  [moved(): lax.ppermute(value, ('dom', 'col'), route(source, target, lax.axis_size('...]
    add x2 -> x0, other arithmetic: 47.1 us -> none  [couple(): padded[:, 1:-1, :-2] + padded[:, 1:-1, 2:]]
    pallas_call x0 -> x9, Pallas kernels: none -> 32.2 us  [the longest x4 16.9 us: product(): pl.pallas_call(product_kernel, out_shape=jax.ShapeDtypeStruct((rows, node...]
    dot_general x3 -> x0, matrix products: 20.1 us -> none  [the longest x1 19.2 us: local(): lax.dot_general(half, remade, (((1,), (1,)), ((), ())), preferred_element...]
    ppermute x0 -> x9, starting transfers between devices: none -> 18.4 us  [moved(): lax.ppermute(value, ('dom', 'col'), route(source, target, lax.axis_size('...]
    convert_element_type x1 -> x0, other arithmetic: 17.9 us -> none  [local(): remade = couple(lax.all_gather(inverse_pivot[0], 'col', axis=0, tiled=Tru...]
    reshape x1 -> x0, other arithmetic: 13.1 us -> none  [couple(): grid = panel.reshape(count, GY, GX)]
  transfers between devices with their start and end apart: 3 -> 10, of which waited for: 3 -> 3; matrix products, arithmetic and copies ran while one was open for 29% -> 0% of each run, Pallas kernels for 0% -> 14%
where the time goes in v1:
time: 184 us; the launch traced here: 181 us
  waiting for transfers between devices  119 us (65%)
  Pallas kernels  32.2 us (18%)
  starting transfers between devices  20.3 us (11%)
  local copies, waits for them, and re-layouts  6.68 us (4%)
  between operations  2.81 us (2%)
    ppermute x9, waiting for transfers between devices, moved(): lax.ppermute(value, ('dom', 'col'), route(source, target, lax.axis_size('...  105 us
    ppermute x9, starting transfers between devices, moved(): lax.ppermute(value, ('dom', 'col'), route(source, target, lax.axis_size('...  18.4 us
    pallas_call x4, Pallas kernels, product(): pl.pallas_call(product_kernel, out_shape=jax.ShapeDtypeStruct((rows, node...  16.9 us
    ppermute x1, waiting for transfers between devices, passed_along(): lax.ppermute(value, axis, [(source, source + steps) for source in range(i...  13.4 us
    unnamed x24, local copies, waits for them, and re-layouts  6.68 us
    pallas_call x1, Pallas kernels, couple(): pl.pallas_call(couple_kernel, out_shape=jax.ShapeDtypeStruct((rows, nodes...  5.52 us
    pallas_call x2, Pallas kernels, halves(): pl.pallas_call(functools.partial(half_kernel, count), out_shape=tuple((ja...  3.99 us
  transfers between devices with their start and end apart: 10, of which 3 were waited for; matrix products, arithmetic and copies ran while one was open for 0% of the time, Pallas kernels for 14%

profile of v1, /device:TPU:1, one launch (start us, length us, event | category | flops | bytes accessed | tf_op | source)
XLA Modules:
  0.0 180.6 jit_solution(6701018870895792432)
XLA Ops:
  0.6 2.0 %collective-permute-start = (bf16[1,512,2048]{2,1,0:T(8,128)(2,1)}, bf16[1,512,2048]{2,1,0:T(8,128)(2,1)}, u32[]{:S(2)}, u32[]{:S(2)}) collective-permute-start(bf16[1,512,2048]{2,1,0:T(8,128)(2,1)} %param.8), channel_id=1, source_target_pairs={{4,0},{8,4},{12,8},{5,1},{9,5},{13,9},{6,2},{10,6},{14,10},{7,3},{... | collective-permute-start | bytes 6291464 | tf_op jit(solution)/shard_map/ppermute | solution.py:20
  3.3 1.6 copy-done.1
  5.5 5.5 %couple.1.refs_1_.c1 = bf16[512,2048]{1,0:T(8,128)(2,1)} custom-call(f32[1]{0:T(128)S(6)} %copy.9.rate_ref, s32[1,2048]{1,0:T(1,128)S(1)} %bitcast.12, bf16[512,2048]{1,0:T(8,128)(2,1)S(1)} %bitcast.10), custom_call_target="tpu_custom_call" | custom-call | flops 10485760 | bytes 4194304 | tf_op jit(solution)/shard_map/couple/pallas_call | solution.py:67
  11.1 2.0 %collective-permute-start.5 = (bf16[512,2048]{1,0:T(8,128)(2,1)}, bf16[512,2048]{1,0:T(8,128)(2,1)}, u32[]{:S(2)}, u32[]{:S(2)}) collective-permute-start(bf16[512,2048]{1,0:T(8,128)(2,1)} %couple.1.refs_1_.c1), channel_id=1, source_target_pairs={{2,1},{5,6},{10,9},{13,14},{18,17},{21,22},{26,25},{29,30}} | collective-permute-start | bytes 6291464 | tf_op jit(solution)/shard_map/ppermute | solution.py:99
  13.0 2.0 %collective-permute-start.4 = (bf16[512,2048]{1,0:T(8,128)(2,1)}, bf16[512,2048]{1,0:T(8,128)(2,1)}, u32[]{:S(2)}, u32[]{:S(2)}) collective-permute-start(bf16[512,2048]{1,0:T(8,128)(2,1)} %couple.1.refs_1_.c1), channel_id=1, source_target_pairs={{0,1},{7,6},{8,9},{15,14},{16,17},{23,22},{24,25},{31,30}} | collective-permute-start | bytes 6291464 | tf_op jit(solution)/shard_map/ppermute | solution.py:99
  15.8 13.4 %collective-permute-done = bf16[1,512,2048]{2,1,0:T(8,128)(2,1)} collective-permute-done((bf16[1,512,2048]{2,1,0:T(8,128)(2,1)}, bf16[1,512,2048]{2,1,0:T(8,128)(2,1)}, u32[]{:S(2)}, u32[]{:S(2)}) %collective-permute-start) | collective-permute-done | bytes 2097184 | tf_op jit(solution)/shard_map/ppermute | solution.py:20
  29.2 3.1 %prior_parts.1 = (bf16[512,2048]{1,0:T(8,128)(2,1)S(1)}, bf16[512,1536]{1,0:T(8,128)(2,1)S(1)}, bf16[512,1024]{1,0:T(8,128)(2,1)S(1)}, bf16[512,512]{1,0:T(8,128)(2,1)S(1)}) custom-call(s32[3]{0:T(128)S(1)} %pad_add_fusion.place_ref, s32[1]{0:T(128)S(6)} %copy.11.step_ref, bf16[512,2048]{1,0:T(8,128)(2,1)} %bitcast.4.shifted_ref, bf16[512,2048]{1,0:T(8,128)(2,1)S(1)} %bitcast.8), custom_call_target="tpu_custom_call" | custom-call | bytes 7340032 | tf_op jit(solution)/shard_map/prior_parts/pallas_call | solution.py:133
  32.2 0.8 collective-permute-start.1
  33.7 5.4 %collective-permute-start.6 = (bf16[512,2048]{1,0:T(8,128)(2,1)}, bf16[512,2048]{1,0:T(8,128)(2,1)S(1)}, u32[]{:S(2)}, u32[]{:S(2)}) collective-permute-start(bf16[512,2048]{1,0:T(8,128)(2,1)} %couple.1.refs_1_.c1), channel_id=1, source_target_pairs={{3,1},{4,6},{11,9},{12,14},{19,17},{20,22},{27,25},{28,30}} | collective-permute-start | bytes 6291464 | tf_op jit(solution)/shard_map/ppermute | solution.py:99
  39.2 4.6 %collective-permute-start.3 = (bf16[512,512]{1,0:T(8,128)(2,1)S(1)}, bf16[512,512]{1,0:T(8,128)(2,1)S(1)}, u32[]{:S(2)}, u32[]{:S(2)}) collective-permute-start(bf16[512,512]{1,0:T(8,128)(2,1)S(1)} %get-tuple-element.14), channel_id=1, source_target_pairs={{3,1},{4,6},{11,9},{12,14},{19,17},{20,22},{27,25},{28,30}} | collective-permute-start | bytes 1572872 | tf_op jit(solution)/shard_map/ppermute | solution.py:99
  43.9 41.1 %collective-permute-done.3.last_ref = bf16[512,512]{1,0:T(8,128)(2,1)S(1)} collective-permute-done((bf16[512,512]{1,0:T(8,128)(2,1)S(1)}, bf16[512,512]{1,0:T(8,128)(2,1)S(1)}, u32[]{:S(2)}, u32[]{:S(2)}) %collective-permute-start.3) | collective-permute-done | bytes 524320 | tf_op jit(solution)/shard_map/ppermute | solution.py:99
  85.0 3.4 %halves.2 = (bf16[512,2048]{1,0:T(8,128)(2,1)S(1)}, bf16[512,2048]{1,0:T(8,128)(2,1)S(1)}, bf16[512,2048]{1,0:T(8,128)(2,1)S(1)}) custom-call(s32[3]{0:T(128)S(1)} %pad_add_fusion.place_ref, bf16[512,2048]{1,0:T(8,128)(2,1)S(1)} %get-tuple-element.11.row_ref, bf16[512,1536]{1,0:T(8,128)(2,1)S(1)} %collective-permute-done.1.far_ref, ...), custom_call_target="tpu_custom_call" | custom-call | flops 12884901888 | bytes 17825792 | tf_op jit(solution)/shard_map/halves/pallas_call | solution.py:203
  88.5 1.4 copy-done.10
  89.8 5.0 %product.6 = bf16[512,2048]{1,0:T(8,128)(2,1)} custom-call(s32[3]{0:T(128)S(1)} %pad_add_fusion.place_ref, bf16[512,2048]{1,0:T(8,128)(2,1)S(1)} %get-tuple-element.17.half_ref, bf16[512,2048]{1,0:T(8,128)(2,1)} %collective-permute-done.4.refs_0_.c0, bf16[512,2048]{1,0:T(8,128)(2,1)} %couple.1.refs_1_.c1, ...), custom_call_target="tpu_custom_call" | custom-call | flops 4294967296 | bytes 12582912 | tf_op jit(solution)/shard_map/product/pallas_call | solution.py:243
  94.8 0.8 collective-permute-start.8
  95.6 4.4 %product.4 = bf16[512,2048]{1,0:T(8,128)(2,1)} custom-call(s32[3]{0:T(128)S(1)} %pad_add_fusion.place_ref, bf16[512,2048]{1,0:T(8,128)(2,1)S(1)} %get-tuple-element.15.half_ref, bf16[512,2048]{1,0:T(8,128)(2,1)} %collective-permute-done.4.refs_0_.c0, bf16[512,2048]{1,0:T(8,128)(2,1)} %couple.1.refs_1_.c1, ...), custom_call_target="tpu_custom_call" | custom-call | flops 4294967296 | bytes 12582912 | tf_op jit(solution)/shard_map/product/pallas_call | solution.py:243
  100.0 0.8 collective-permute-start.7
  100.8 1.4 copy-done.9
  102.8 4.5 %product.7 = bf16[512,2048]{1,0:T(8,128)(2,1)} custom-call(s32[3]{0:T(128)S(1)} %pad_add_fusion.place_ref, bf16[512,2048]{1,0:T(8,128)(2,1)S(1)} %halves.3.half_ref, bf16[512,2048]{1,0:T(8,128)(2,1)} %collective-permute-done.4.refs_0_.c0, bf16[512,2048]{1,0:T(8,128)(2,1)} %couple.1.refs_1_.c1, bf16[512,2048]{1,0:T(8,128)(2,1)} %collective-permute-done.5.refs_2_.c2, ...), custom_call_target="tpu_custom_call" | custom-call | flops 4294967296 | bytes 12582912 | tf_op jit(solution)/shard_map/product/pallas_call | solution.py:243
  107.3 1.3 collective-permute-start.9
  109.3 1.6 copy-done.5
  110.8 3.0 %product.5.q1 = bf16[512,2048]{1,0:T(8,128)(2,1)S(1)} custom-call(s32[3]{0:T(128)S(1)} %pad_add_fusion.place_ref, bf16[512,2048]{1,0:T(8,128)(2,1)S(1)} %copy-done.11, bf16[512,2048]{1,0:T(8,128)(2,1)} %collective-permute-done.4.refs_0_.c0, bf16[512,2048]{1,0:T(8,128)(2,1)} %couple.1.refs_1_.c1, bf16[512,2048]{1,0:T(8,128)(2,1)} %collective-permute-done.5.refs_2_.c2, ...), custom_call_target="tpu_custom_call" | custom-call | flops 4294967296 | bytes 12582912 | tf_op jit(solution)/shard_map/product/pallas_call | solution.py:243
  113.9 64.0 %collective-permute-done.9.q3 = bf16[512,2048]{1,0:T(8,128)(2,1)S(1)} collective-permute-done((bf16[512,2048]{1,0:T(8,128)(2,1)}, bf16[512,2048]{1,0:T(8,128)(2,1)S(1)}, u32[]{:S(2)}, u32[]{:S(2)}) %collective-permute-start.9) | collective-permute-done | bytes 2097184 | tf_op jit(solution)/shard_map/ppermute | solution.py:99
  177.9 2.7 %final.1 = (bf16[512,2048]{1,0:T(8,128)(2,1)}, f32[1,512]{1,0:T(1,128)}) custom-call(s32[3]{0:T(128)S(1)} %pad_add_fusion.place_ref, s32[1]{0:T(128)S(6)} %convert_element_type.3.active_ref, bf16[512,2048]{1,0:T(8,128)(2,1)S(1)} %bitcast.11, bf16[512,2048]{1,0:T(8,128)(2,1)S(1)} %collective-permute-done.7.q0, bf16[512,2048]{1,0:T(8,128)(2,1)S(1)} %product.5.q1, ...), custom_call_target="tpu_custom_call" | custom-call | flops 2097152 | bytes 8388608 | tf_op jit(solution)/shard_map/final/pallas_call | solution.py:293
  (30 shorter events, 2.1 us)
Async XLA Ops:
  0.6 28.5 %collective-permute-start = (bf16[1,512,2048]{2,1,0:T(8,128)(2,1)}, bf16[1,512,2048]{2,1,0:T(8,128)(2,1)}, u32[]{:S(2)}, u32[]{:S(2)}) collective-permute-start(bf16[1,512,2048]{2,1,0:T(8,128)(2,1)} %param.8), channel_id=1, source_target_pairs={{4,0},{8,4},{12,8},{5,1},{9,5},{13,9},{6,2},{10,6},{14,10},{7,3},{... | collective-permute-start | bytes 6291464 | tf_op jit(solution)/shard_map/ppermute | solution.py:20
  3.2 1.6 copy-start.1
  4.8 0.7 copy-start.3
  5.5 23.6 %copy-start = (bf16[1,512,2048]{2,1,0:T(8,128)(2,1)S(1)}, bf16[1,512,2048]{2,1,0:T(8,128)(2,1)}, u32[]{:S(2)}) copy-start(bf16[1,512,2048]{2,1,0:T(8,128)(2,1)} %param.7) | copy-start | bytes 6291460
  11.1 28.1 %collective-permute-start.5 = (bf16[512,2048]{1,0:T(8,128)(2,1)}, bf16[512,2048]{1,0:T(8,128)(2,1)}, u32[]{:S(2)}, u32[]{:S(2)}) collective-permute-start(bf16[512,2048]{1,0:T(8,128)(2,1)} %couple.1.refs_1_.c1), channel_id=1, source_target_pairs={{2,1},{5,6},{10,9},{13,14},{18,17},{21,22},{26,25},{29,30}} | collective-permute-start | bytes 6291464 | tf_op jit(solution)/shard_map/ppermute | solution.py:99
  13.0 30.8 %collective-permute-start.4 = (bf16[512,2048]{1,0:T(8,128)(2,1)}, bf16[512,2048]{1,0:T(8,128)(2,1)}, u32[]{:S(2)}, u32[]{:S(2)}) collective-permute-start(bf16[512,2048]{1,0:T(8,128)(2,1)} %couple.1.refs_1_.c1), channel_id=1, source_target_pairs={{0,1},{7,6},{8,9},{15,14},{16,17},{23,22},{24,25},{31,30}} | collective-permute-start | bytes 6291464 | tf_op jit(solution)/shard_map/ppermute | solution.py:99
  32.2 56.2 %copy-start.6 = (bf16[512,2048]{1,0:T(8,128)(2,1)}, bf16[512,2048]{1,0:T(8,128)(2,1)S(1)}, u32[]{:S(2)}) copy-start(bf16[512,2048]{1,0:T(8,128)(2,1)S(1)} %get-tuple-element.11.row_ref) | copy-start | bytes 6291460
  32.2 52.7 %collective-permute-start.1 = (bf16[512,1536]{1,0:T(8,128)(2,1)S(1)}, bf16[512,1536]{1,0:T(8,128)(2,1)S(1)}, u32[]{:S(2)}, u32[]{:S(2)}) collective-permute-start(bf16[512,1536]{1,0:T(8,128)(2,1)S(1)} %get-tuple-element.12), channel_id=1, source_target_pairs={{0,1},{7,6},{8,9},{15,14},{16,17},{23,22},{24,25},{31,30}} | collective-permute-start | bytes 4718600 | tf_op jit(solution)/shard_map/ppermute | solution.py:99
  33.0 52.0 %collective-permute-start.2 = (bf16[512,1024]{1,0:T(8,128)(2,1)S(1)}, bf16[512,1024]{1,0:T(8,128)(2,1)S(1)}, u32[]{:S(2)}, u32[]{:S(2)}) collective-permute-start(bf16[512,1024]{1,0:T(8,128)(2,1)S(1)} %get-tuple-element.13), channel_id=1, source_target_pairs={{2,1},{5,6},{10,9},{13,14},{18,17},{21,22},{26,25},{29,30}} | collective-permute-start | bytes 3145736 | tf_op jit(solution)/shard_map/ppermute | solution.py:99
  33.7 56.1 %collective-permute-start.6 = (bf16[512,2048]{1,0:T(8,128)(2,1)}, bf16[512,2048]{1,0:T(8,128)(2,1)S(1)}, u32[]{:S(2)}, u32[]{:S(2)}) collective-permute-start(bf16[512,2048]{1,0:T(8,128)(2,1)} %couple.1.refs_1_.c1), channel_id=1, source_target_pairs={{3,1},{4,6},{11,9},{12,14},{19,17},{20,22},{27,25},{28,30}} | collective-permute-start | bytes 6291464 | tf_op jit(solution)/shard_map/ppermute | solution.py:99
  39.2 45.8 %collective-permute-start.3 = (bf16[512,512]{1,0:T(8,128)(2,1)S(1)}, bf16[512,512]{1,0:T(8,128)(2,1)S(1)}, u32[]{:S(2)}, u32[]{:S(2)}) collective-permute-start(bf16[512,512]{1,0:T(8,128)(2,1)S(1)} %get-tuple-element.14), channel_id=1, source_target_pairs={{3,1},{4,6},{11,9},{12,14},{19,17},{20,22},{27,25},{28,30}} | collective-permute-start | bytes 1572872 | tf_op jit(solution)/shard_map/ppermute | solution.py:99
  85.0 3.5 %copy-start.8 = (bf16[512,1536]{1,0:T(8,128)(2,1)}, bf16[512,1536]{1,0:T(8,128)(2,1)S(1)}, u32[]{:S(2)}) copy-start(bf16[512,1536]{1,0:T(8,128)(2,1)S(1)} %collective-permute-done.1.far_ref) | copy-start | bytes 4718596
  88.4 1.4 copy-start.10
  89.8 12.9 %copy-start.4 = (bf16[512,2048]{1,0:T(8,128)(2,1)}, bf16[512,2048]{1,0:T(8,128)(2,1)S(1)}, u32[]{:S(2)}) copy-start(bf16[512,2048]{1,0:T(8,128)(2,1)S(1)} %collective-permute-done.6.c3.refs_0_) | copy-start | bytes 6291460
  94.8 19.0 %collective-permute-start.8 = (bf16[512,2048]{1,0:T(8,128)(2,1)}, bf16[512,2048]{1,0:T(8,128)(2,1)S(1)}, u32[]{:S(2)}, u32[]{:S(2)}) collective-permute-start(bf16[512,2048]{1,0:T(8,128)(2,1)} %product.6), channel_id=1, source_target_pairs={{1,2},{6,5},{9,10},{14,13},{17,18},{22,21},{25,26},{30,29}} | collective-permute-start | bytes 6291464 | tf_op jit(solution)/shard_map/ppermute | solution.py:99
  95.6 5.2 %copy-start.7 = (bf16[512,2048]{1,0:T(8,128)(2,1)S(1)}, bf16[512,2048]{1,0:T(8,128)(2,1)}, u32[]{:S(2)}) copy-start(bf16[512,2048]{1,0:T(8,128)(2,1)} %copy-done.6) | copy-start | bytes 6291460
  100.0 13.9 %collective-permute-start.7 = (bf16[512,2048]{1,0:T(8,128)(2,1)}, bf16[512,2048]{1,0:T(8,128)(2,1)S(1)}, u32[]{:S(2)}, u32[]{:S(2)}) collective-permute-start(bf16[512,2048]{1,0:T(8,128)(2,1)} %product.4), channel_id=1, source_target_pairs={{1,0},{6,7},{9,8},{14,15},{17,16},{22,23},{25,24},{30,31}} | collective-permute-start | bytes 6291464 | tf_op jit(solution)/shard_map/ppermute | solution.py:99
  100.8 1.4 copy-start.9
  102.8 6.5 %copy-start.11 = (bf16[512,2048]{1,0:T(8,128)(2,1)S(1)}, bf16[512,2048]{1,0:T(8,128)(2,1)}, u32[]{:S(2)}) copy-start(bf16[512,2048]{1,0:T(8,128)(2,1)} %copy-done.10) | copy-start | bytes 6291460
  107.3 70.6 %collective-permute-start.9 = (bf16[512,2048]{1,0:T(8,128)(2,1)}, bf16[512,2048]{1,0:T(8,128)(2,1)S(1)}, u32[]{:S(2)}, u32[]{:S(2)}) collective-permute-start(bf16[512,2048]{1,0:T(8,128)(2,1)} %product.7), channel_id=1, source_target_pairs={{1,3},{6,4},{9,11},{14,12},{17,19},{22,20},{25,27},{30,28}} | collective-permute-start | bytes 6291464 | tf_op jit(solution)/shard_map/ppermute | solution.py:99
  109.3 1.6 copy-start.5
  110.8 67.0 %copy-start.2 = (bf16[1,512,2048]{2,1,0:T(8,128)(2,1)S(1)}, bf16[1,512,2048]{2,1,0:T(8,128)(2,1)}, u32[]{:S(2)}) copy-start(bf16[1,512,2048]{2,1,0:T(8,128)(2,1)} %param.9) | copy-start | bytes 6291460

commit v2 on v1

v2 whole, which is shorter than its diff:
```python
import functools

import jax
import jax.numpy as jnp
from jax import lax
from jax.experimental import pallas as pl
from jax.experimental.pallas import tpu as pltpu
from jax.sharding import PartitionSpec as P

GX = 64
GY = 32
BF16 = jnp.bfloat16
F32 = jnp.float32
MIB = 1 << 20


def passed_along(value, axis, steps):
    count = lax.axis_size(axis)
    initial, last = (max(0, -steps), min(count, count - steps))
    return lax.ppermute(value, axis, [(source, source + steps) for source in range(initial, last)])


LIGHT = pl.CostEstimate(flops=1 << 20, bytes_accessed=1 << 16, transcendentals=0)


def couple_kernel(rate_ref, class_ref, pivot_ref, out_ref, weight_ref):
    nodes = pivot_ref.shape[1]

    @pl.when(pl.program_id(0) == 0)
    def _():
        kind = class_ref[...]
        across = jnp.where(
            kind == 0, 0.25, jnp.where(kind == 1, 0.375, jnp.where(kind == 2, 0.125, 0.5))
        ).astype(F32)
        along = jnp.where(
            kind == 0, 0.25, jnp.where(kind == 1, 0.125, jnp.where(kind == 2, 0.375, 0.0))
        ).astype(F32)
        node = lax.broadcasted_iota(jnp.int32, (1, nodes), 1)
        column = node % GX
        parts = (
            jnp.where(column > 0, across, 0.0),
            jnp.where(column < GX - 1, across, 0.0),
            jnp.where(node >= GX, along, 0.0),
            jnp.where(node < nodes - GX, along, 0.0),
        )
        for which, part in enumerate(parts):
            weight_ref[which] = jnp.broadcast_to(part, (16, nodes))

    rate = rate_ref[0]

    def group(step, carry):
        rows = pl.ds(pl.multiple_of(step * 16, 16), 16)
        value = pivot_ref[rows, :].astype(F32)
        total = (
            value
            + weight_ref[0] * pltpu.roll(value, 1, 1)
            + weight_ref[1] * pltpu.roll(value, nodes - 1, 1)
            + weight_ref[2] * pltpu.roll(value, GX, 1)
            + weight_ref[3] * pltpu.roll(value, nodes - GX, 1)
        )
        out_ref[rows, :] = (rate * total).astype(BF16)
        return carry

    lax.fori_loop(0, pivot_ref.shape[0] // 16, group, 0)


def couple(pivot, node_class, rate):
    rows, nodes = pivot.shape
    chunk = min(rows, 128)
    return pl.pallas_call(
        couple_kernel,
        out_shape=jax.ShapeDtypeStruct((rows, nodes), BF16),
        grid=(rows // chunk,),
        in_specs=[
            pl.BlockSpec(memory_space=pltpu.SMEM),
            pl.BlockSpec((1, nodes), lambda i: (0, 0)),
            pl.BlockSpec((chunk, nodes), lambda i: (i, 0)),
        ],
        out_specs=pl.BlockSpec((chunk, nodes), lambda i: (i, 0)),
        scratch_shapes=[pltpu.VMEM((4, 16, nodes), F32)],
        compiler_params=pltpu.CompilerParams(vmem_limit_bytes=8 * MIB),
        cost_estimate=LIGHT,
        name="couple",
    )(rate, node_class.reshape(1, nodes), pivot)


def turned(block, odd):
    return block + odd * (3 - 2 * block)


def route(source, target, doms):
    pairs = []
    for dom in range(doms):
        odd = dom % 2
        pairs.append((dom * 4 + turned(source, odd), dom * 4 + turned(target, odd)))
    return pairs


def moved(value, source, target):
    return lax.ppermute(value, ("dom", "col"), route(source, target, lax.axis_size("dom")))


def couple_here(place, pivot, node_class, rate):
    rows, nodes = pivot.shape
    chunk = 128

    def kernel(place_ref, *refs):
        @pl.when(place_ref[1] == 1)
        def _():
            couple_kernel(*refs)

    return pl.pallas_call(
        kernel,
        out_shape=jax.ShapeDtypeStruct((rows, nodes), BF16),
        grid_spec=pltpu.PrefetchScalarGridSpec(
            num_scalar_prefetch=1,
            grid=(rows // chunk,),
            in_specs=[
                pl.BlockSpec(memory_space=pltpu.SMEM),
                pl.BlockSpec((1, nodes), lambda i, place: (0, 0)),
                pl.BlockSpec((chunk, nodes), lambda i, place: (i, 0)),
            ],
            out_specs=pl.BlockSpec((chunk, nodes), lambda i, place: (i, 0)),
            scratch_shapes=[pltpu.VMEM((4, 16, nodes), F32)],
        ),
        compiler_params=pltpu.CompilerParams(vmem_limit_bytes=8 * MIB),
        cost_estimate=LIGHT,
        name="couple_here",
    )(place, rate, node_class.reshape(1, nodes), pivot)


def turn_kernel(place_ref, coupled_ref, *refs):
    @pl.when(place_ref[1] == 1)
    def _():
        refs[-1][...] = coupled_ref[...].T


def turn(place, panel, coupled, across):
    rows, nodes = coupled.shape
    chunk = 128
    ratio = rows // chunk
    return pl.pallas_call(
        turn_kernel,
        out_shape=jax.ShapeDtypeStruct((nodes, nodes), BF16),
        grid_spec=pltpu.PrefetchScalarGridSpec(
            num_scalar_prefetch=1,
            grid=(ratio,),
            in_specs=[pl.BlockSpec((chunk, nodes), lambda i, place: (i, 0))]
            + ([] if across is None else [pl.BlockSpec(memory_space=pl.ANY)]),
            out_specs=pl.BlockSpec(
                (nodes, chunk), lambda i, place: (0, turned(panel, place[0]) * ratio + i)
            ),
        ),
        input_output_aliases={} if across is None else {2: 0},
        compiler_params=pltpu.CompilerParams(vmem_limit_bytes=8 * MIB),
        cost_estimate=LIGHT,
        name="turn",
    )(place, coupled, *(() if across is None else (across,)))


def multiply_kernel(place_ref, left_ref, right_ref, out_ref):
    @pl.when(place_ref[1] == 1)
    def _():
        out_ref[...] = jnp.dot(
            left_ref[...], right_ref[...], preferred_element_type=F32
        ).astype(BF16)


def multiply(place, left, right, first=lambda odd: 0, count=4):
    rows, nodes = left.shape
    width = nodes // 4
    return pl.pallas_call(
        multiply_kernel,
        out_shape=jax.ShapeDtypeStruct((rows, count * width), BF16),
        grid_spec=pltpu.PrefetchScalarGridSpec(
            num_scalar_prefetch=1,
            grid=(count,),
            in_specs=[
                pl.BlockSpec((rows, nodes), lambda n, place: (0, 0)),
                pl.BlockSpec((nodes, width), lambda n, place: (0, first(place[0]) + n)),
            ],
            out_specs=pl.BlockSpec((rows, width), lambda n, place: (0, n)),
        ),
        compiler_params=pltpu.CompilerParams(vmem_limit_bytes=16 * MIB),
        cost_estimate=LIGHT,
        name="multiply",
    )(place, left, right)


def prior_kernel(step_ref, shifted_ref, sigma_ref, out_ref):
    @pl.when(step_ref[0] == 0)
    def _():
        out_ref[...] = shifted_ref[...]

    @pl.when(step_ref[0] != 0)
    def _():
        out_ref[...] = sigma_ref[...]


def near_kernel(place_ref, step_ref, shifted_ref, sigma_ref, near_ref, last_ref):
    width = last_ref.shape[1]
    prior_kernel(step_ref, shifted_ref, sigma_ref, near_ref)
    start = pl.multiple_of((1 - place_ref[0]) * width, 128)
    last_ref[...] = near_ref[:, pl.ds(start, width)]


def far_kernel(place_ref, step_ref, shifted_ref, sigma_ref, near_ref, other_ref, far_ref):
    width = near_ref.shape[1] // 2
    prior_kernel(step_ref, shifted_ref, sigma_ref, other_ref)
    start = pl.multiple_of(place_ref[0] * width, 128)
    far_ref[:, :width] = other_ref[:, pl.ds(start, width)]
    far_ref[:, width:] = near_ref[...]


def prior_half(kernel, side, sent, place, step, shifted, sigma, *more):
    rows, nodes = sigma.shape
    chunk = 128
    width = nodes // 4
    half = lambda column: pl.BlockSpec((chunk, 2 * width), column)
    return pl.pallas_call(
        kernel,
        out_shape=(
            jax.ShapeDtypeStruct((rows, 2 * width), BF16),
            jax.ShapeDtypeStruct((rows, sent * width), BF16),
        ),
        grid_spec=pltpu.PrefetchScalarGridSpec(
            num_scalar_prefetch=2,
            grid=(rows // chunk,),
            in_specs=[
                half(lambda i, place, step: (jnp.where(step[0] == 0, i, 0), 0)),
                half(lambda i, place, step: (jnp.where(step[0] == 0, 0, i), side(place[0]))),
            ]
            + [half(lambda i, place, step: (i, 0))] * len(more),
            out_specs=(
                half(lambda i, place, step: (i, 0)),
                pl.BlockSpec((chunk, sent * width), lambda i, place, step: (i, 0)),
            ),
        ),
        compiler_params=pltpu.CompilerParams(vmem_limit_bytes=12 * MIB),
        cost_estimate=LIGHT,
        name="prior_half",
    )(place, step, shifted, sigma, *more)


def assemble_kernel(place_ref, near_own, other_own, near_two, last_three, far_zero, out_ref):
    @pl.when(place_ref[1] == 1)
    def _():
        odd = place_ref[0]
        width = last_three.shape[1]

        def at(block):
            return pl.ds(pl.multiple_of(block * width, 128), width)

        near = 2 * (1 - odd)
        half = pl.ds(pl.multiple_of(near * width, 128), 2 * width)
        row = [turned(block, odd) for block in range(4)]
        other = pl.ds(pl.multiple_of(2 * odd * width, 128), 2 * width)
        out_ref[at(row[1]), half] = near_own[...]
        out_ref[at(row[1]), other] = other_own[...]
        out_ref[at(row[2]), half] = near_two[...]
        out_ref[at(row[0]), at(row[0])] = far_zero[:, :width]
        out_ref[at(row[0]), half] = far_zero[:, width:]
        out_ref[at(row[3]), at(row[3])] = last_three[...]
        for step in range(2):
            out_ref[at(near + step), at(row[1])] = near_own[:, step * width : (1 + step) * width].T
            out_ref[at(near + step), at(row[0])] = far_zero[:, (1 + step) * width : (2 + step) * width].T
        out_ref[at(row[0]), at(row[1])] = other_own[:, at(odd)].T
        out_ref[at(row[3]), at(row[2])] = near_two[:, at(1 - odd)].T


def assemble(place, *parts):
    nodes = 2 * parts[0].shape[1]
    vmem = pl.BlockSpec(memory_space=pltpu.VMEM)
    return pl.pallas_call(
        assemble_kernel,
        out_shape=jax.ShapeDtypeStruct((nodes, nodes), BF16),
        in_specs=[pl.BlockSpec(memory_space=pltpu.SMEM)] + [vmem] * 5,
        out_specs=vmem,
        compiler_params=pltpu.CompilerParams(vmem_limit_bytes=20 * MIB),
        cost_estimate=LIGHT,
        name="assemble",
    )(place, *parts)


def final_kernel(
    place_ref, active_ref, pivot_ref, q0, q0_last, q1, q2, q2_last, q3_near, q3_other, sigma_ref, out_ref, var_ref
):
    rows, nodes = pivot_ref.shape
    width = nodes // 4
    odd, place = place_ref[0], place_ref[1]
    here = pl.multiple_of(pl.program_id(0) * rows, 128)
    square = (rows, rows)
    on_diagonal = lax.broadcasted_iota(jnp.int32, square, 0) == lax.broadcasted_iota(
        jnp.int32, square, 1
    )

    def at(block, count=1):
        return pl.ds(pl.multiple_of(block * width, 128), count * width)

    def own(block):
        return pl.ds(pl.multiple_of(block * width + here, 128), rows)

    def diagonal(value):
        return jnp.sum(jnp.where(on_diagonal, value, 0.0), axis=0, keepdims=True)

    def add(columns, product):
        out_ref[:, columns] = (pivot_ref[:, columns].astype(F32) + product.astype(F32)).astype(BF16)

    def trace(product):
        var_ref[...] = diagonal(
            pivot_ref[:, own(place_ref[2])].astype(F32) + product.astype(F32)
        )

    active = active_ref[0] != 0

    @pl.when(active & (place == 0))
    def _():
        add(at(odd, 3), q0[...])
        add(at(3 - 3 * odd), q0_last[...])
        trace(q0[:, own(2 * odd)])

    @pl.when(active & (place == 1))
    def _():
        add(slice(None), q1[...])
        trace(q1[:, own(place_ref[2])])

    @pl.when(active & (place == 2))
    def _():
        add(at(odd, 3), q2[...])
        add(at(3 - 3 * odd), q2_last[...])
        trace(q2[:, own(2 - 2 * odd)])

    @pl.when(active & (place == 3))
    def _():
        add(at(2 - 2 * odd, 2), q3_near[...])
        add(at(2 * odd, 2), q3_other[...])
        trace(q3_near[:, own(1 - odd)])

    @pl.when(active_ref[0] == 0)
    def _():
        out_ref[...] = sigma_ref[...]
        var_ref[...] = diagonal(sigma_ref[:, own(place_ref[2])].astype(F32))


def final(place, active, pivot, products, sigma):
    rows, nodes = pivot.shape
    chunk = 128
    width = nodes // 4

    def picked(which, blocks):
        return pl.BlockSpec(
            (chunk, blocks * width), lambda i, place, active: (jnp.where(place[1] == which, i, 0), 0)
        )

    return pl.pallas_call(
        final_kernel,
        out_shape=(
            jax.ShapeDtypeStruct((rows, nodes), BF16),
            jax.ShapeDtypeStruct((1, rows), F32),
        ),
        grid_spec=pltpu.PrefetchScalarGridSpec(
            num_scalar_prefetch=2,
            grid=(rows // chunk,),
            in_specs=[
                pl.BlockSpec((chunk, nodes), lambda i, place, active: (i, 0)),
                picked(0, 3),
                picked(0, 1),
                picked(1, 4),
                picked(2, 3),
                picked(2, 1),
                picked(3, 2),
                picked(3, 2),
                pl.BlockSpec(
                    (chunk, nodes), lambda i, place, active: (jnp.where(active[0] == 0, i, 0), 0)
                ),
            ],
            out_specs=(
                pl.BlockSpec((chunk, nodes), lambda i, place, active: (i, 0)),
                pl.BlockSpec((1, chunk), lambda i, place, active: (0, i)),
            ),
        ),
        compiler_params=pltpu.CompilerParams(vmem_limit_bytes=16 * MIB),
        cost_estimate=LIGHT,
        name="final",
    )(place, active, pivot, *products, sigma)


def owned(sigma_next, separator, inverse_pivot, coupling_rate, lengths, step_index, node_class):
    sigma, pivot = sigma_next[0], inverse_pivot[0]
    odd = lax.axis_index("dom") % 2
    col = lax.axis_index("col")
    place = jnp.stack([odd, turned(col, odd), col]).astype(jnp.int32)
    active = (step_index < lengths).astype(jnp.int32)
    width = pivot.shape[1] // 4

    half = 2 * width

    p2 = moved(pivot, 2, 1)
    p0 = moved(pivot, 0, 1)
    near = lax.dynamic_slice_in_dim(separator[0], odd * half, half, 1)
    other = lax.dynamic_slice_in_dim(separator[0], (1 - odd) * half, half, 1)
    near = passed_along(near, "dom", -1)
    other = passed_along(other, "dom", -1)
    c1 = couple(pivot, node_class, coupling_rate)
    across = turn(place, 1, c1, None)

    near = lax.optimization_barrier((near, across))[0]
    near, last = prior_half(near_kernel, lambda odd: 1 - odd, 1, place, step_index, near, sigma)
    near_two, last_three = moved(near, 2, 1), moved(last, 3, 1)
    other, far = prior_half(far_kernel, lambda odd: odd, 3, place, step_index, other, sigma, near)
    far_zero = moved(far, 0, 1)
    c2 = couple_here(place, p2, node_class, coupling_rate)
    across = turn(place, 2, c2, across)
    c0 = couple_here(place, p0, node_class, coupling_rate)
    across = turn(place, 0, c0, across)
    c3 = lax.optimization_barrier((c1, last_three, near_two, far_zero, across))[0]
    c3 = moved(c3, 3, 1)
    prior = assemble(place, near, other, near_two, last_three, far_zero)
    h2 = multiply(place, c2, prior)
    most = lambda odd: odd
    rest = lambda odd: 3 - 3 * odd
    q2 = moved(multiply(place, h2, across, most, 3), 1, 2)
    h0 = multiply(place, c0, prior)
    q0 = moved(multiply(place, h0, across, most, 3), 1, 0)
    h1 = multiply(place, c1, prior)

    across = turn(place, 3, c3, across)
    h3 = multiply(place, c3, prior)
    q3_near = moved(multiply(place, h3, across, lambda odd: 2 - 2 * odd, 2), 1, 3)
    q3_other = moved(multiply(place, h3, across, lambda odd: 2 * odd, 2), 1, 3)
    q2_last = moved(multiply(place, h2, across, rest, 1), 1, 2)
    q0_last = moved(multiply(place, h0, across, rest, 1), 1, 0)
    q1 = multiply(place, h1, across)
    products = (q0, q0_last, q1, q2, q2_last, q3_near, q3_other)
    covariance, variances = final(place, active, pivot, products, sigma)
    return (covariance[None], variances)


def gathered(sigma_next, separator, inverse_pivot, coupling_rate, lengths, step_index, node_class):
    shifted = passed_along(separator, "dom", -1)
    prior = jnp.where(step_index[0] == 0, shifted[0], sigma_next[0])
    pivot = inverse_pivot[0].astype(F32)
    coupled = couple(inverse_pivot[0], node_class, coupling_rate)
    rows = coupled.shape[0]
    half = jnp.dot(
        coupled,
        lax.all_gather(prior, "col", axis=0, tiled=True),
        preferred_element_type=F32,
    ).astype(BF16)
    product = lax.dot_general(
        half,
        lax.all_gather(coupled, "col", axis=0, tiled=True),
        (((1,), (1,)), ((), ())),
        preferred_element_type=F32,
    )
    full = pivot + product
    active = step_index[0] < lengths[0]
    old = sigma_next[0]
    covariance = jnp.where(active, full.astype(BF16), old)
    first_col = lax.axis_index("col") * rows
    new_block = lax.dynamic_slice_in_dim(full, first_col, rows, 1)
    old_block = lax.dynamic_slice_in_dim(old, first_col, rows, 1)
    variances = jnp.where(active, jnp.diagonal(new_block), jnp.diagonal(old_block).astype(F32))
    return (covariance[None], variances[None])


def solution(mesh):
    local = owned if mesh.shape["col"] == 4 and mesh.shape["dom"] % 2 == 0 else gathered
    return jax.shard_map(
        local,
        mesh=mesh,
        in_specs=(
            P(("groups", "dom"), "col", None),
            P(("groups", "dom"), "col", None),
            P(("groups", "dom"), "col", None),
            P(("groups", "dom")),
            P(("groups", "dom")),
            P(("groups", "dom")),
            P("groups"),
        ),
        out_specs=(P(("groups", "dom"), "col", None), P(("groups", "dom"), "col")),
        check_vma=False,
    )
```

time: 184 us -> 141 us (0.77)
  the two profiles are of different devices: /device:TPU:1 before, /device:TPU:0 now
where the time goes in v2:
time: 141 us; the launch traced here: 140 us
  waiting for transfers between devices  79.9 us (57%)
  Pallas kernels  34.7 us (25%)
  starting transfers between devices  19.2 us (14%)
  local copies, waits for them, and re-layouts  3.56 us (3%)
  between operations  2.95 us (2%)
    ppermute x12, waiting for transfers between devices, moved(): lax.ppermute(value, ('dom', 'col'), route(source, target, lax.axis_size('...  79.9 us
    ppermute x12, starting transfers between devices, moved(): lax.ppermute(value, ('dom', 'col'), route(source, target, lax.axis_size('...  16.7 us
    pallas_call x11, Pallas kernels, multiply(): pl.pallas_call(multiply_kernel, out_shape=jax.ShapeDtypeStruct((rows, cou...  13.4 us
    pallas_call x2, Pallas kernels, couple_here(): pl.pallas_call(kernel, out_shape=jax.ShapeDtypeStruct((rows, nodes), BF16...  5.65 us
    pallas_call x4, Pallas kernels, turn(): pl.pallas_call(turn_kernel, out_shape=jax.ShapeDtypeStruct((nodes, nodes)...  4.85 us
    pallas_call x1, Pallas kernels, couple(): pl.pallas_call(couple_kernel, out_shape=jax.ShapeDtypeStruct((rows, nodes...  4.74 us
    dynamic_slice x1, local copies, waits for them, and re-layouts, owned(): other = lax.dynamic_slice_in_dim(separator[0], (1 - odd) * half, half, 1)  3.19 us
  transfers between devices with their start and end apart: 14, of which 4 were waited for; matrix products, arithmetic and copies ran while one was open for 0% of the time, Pallas kernels for 23%

profile of v2, /device:TPU:0, one launch (start us, length us, event | category | flops | bytes accessed | tf_op | source)
XLA Modules:
  0.0 140.4 jit_solution(2305537544981443088)
XLA Ops:
  0.7 3.2 %dynamic-slice_bitcast_fusion = (bf16[512,1024]{1,0:T(8,128)(2,1)}, bf16[512,1024]{1,0:T(8,128)(2,1)}) fusion(bf16[1,512,2048]{2,1,0:T(8,128)(2,1)} %param.8, s32[]{:T(128)S(6)} %select_n.15, s32[]{:T(128)S(6)} %select_n.14), kind=kLoop, calls=%fused_computation | loop fusion | bytes 4194312 | tf_op jit(solution)/shard_map/dynamic_slice | solution.py:401
  3.9 1.3 collective-permute-start.1
  5.1 1.3 collective-permute-start.2
  6.5 2.0 %collective-permute-start.6 = (bf16[512,2048]{1,0:T(8,128)(2,1)S(1)}, bf16[512,2048]{1,0:T(8,128)(2,1)}, u32[]{:S(2)}, u32[]{:S(2)}) collective-permute-start(bf16[512,2048]{1,0:T(8,128)(2,1)S(1)} %bitcast.14), channel_id=1, source_target_pairs={{2,1},{5,6},{10,9},{13,14},{18,17},{21,22},{26,25},{29,30}} | collective-permute-start | bytes 6291464 | tf_op jit(solution)/shard_map/ppermute | solution.py:100
  8.4 5.6 %collective-permute-start = (bf16[512,2048]{1,0:T(8,128)(2,1)S(1)}, bf16[512,2048]{1,0:T(8,128)(2,1)}, u32[]{:S(2)}, u32[]{:S(2)}) collective-permute-start(bf16[512,2048]{1,0:T(8,128)(2,1)S(1)} %bitcast.15), channel_id=1, source_target_pairs={{0,1},{7,6},{8,9},{15,14},{16,17},{23,22},{24,25},{31,30}} | collective-permute-start | bytes 6291464 | tf_op jit(solution)/shard_map/ppermute | solution.py:100
  15.3 4.7 %couple.1.coupled_ref.left_ref = bf16[512,2048]{1,0:T(8,128)(2,1)S(1)} custom-call(f32[1]{0:T(128)S(6)} %copy.15.refs_0_.rate_ref, s32[1,2048]{1,0:T(1,128)S(1)} %bitcast.18, bf16[512,2048]{1,0:T(8,128)(2,1)S(1)} %bitcast.16), custom_call_target="tpu_custom_call" | custom-call | flops 1048576 | bytes 65536 | tf_op jit(solution)/shard_map/couple/pallas_call | solution.py:70
  21.8 1.8 %prior_half.2 = (bf16[512,1024]{1,0:T(8,128)(2,1)S(1)}, bf16[512,512]{1,0:T(8,128)(2,1)S(1)}) custom-call(s32[3]{0:T(128)S(1)} %pad_add_fusion.place_ref, s32[1]{0:T(128)S(6)} %copy.17.step_ref, bf16[512,1024]{1,0:T(8,128)(2,1)} %collective-permute-done.1.shifted_ref, bf16[512,2048]{1,0:T(8,128)(2,1)S(1)} %bitcast.11), custom_call_target="tpu_custom_call" | custom-call | flops 1048576 | bytes 65536 | tf_op jit(solution)/shard_map/prior_half/pallas_call | solution.py:220
  24.6 1.4 collective-permute-start.5
  27.4 2.8 %couple_here.3.coupled_ref.left_ref = bf16[512,2048]{1,0:T(8,128)(2,1)S(1)} custom-call(s32[3]{0:T(128)S(1)} %pad_add_fusion.place_ref, f32[1]{0:T(128)S(6)} %copy.15.refs_0_.rate_ref, s32[1,2048]{1,0:T(1,128)S(1)} %bitcast.19, bf16[512,2048]{1,0:T(8,128)(2,1)} %collective-permute-done.6.refs_2_), custom_call_target="tpu_custom_call" | custom-call | flops 1048576 | bytes 65536 | tf_op jit(solution)/shard_map/couple_here/pallas_call | solution.py:112
  31.5 4.8 %collective-permute-done.refs_2_ = bf16[512,2048]{1,0:T(8,128)(2,1)} collective-permute-done((bf16[512,2048]{1,0:T(8,128)(2,1)S(1)}, bf16[512,2048]{1,0:T(8,128)(2,1)}, u32[]{:S(2)}, u32[]{:S(2)}) %collective-permute-start) | collective-permute-done | bytes 2097184 | tf_op jit(solution)/shard_map/ppermute | solution.py:100
  36.2 2.8 %couple_here.2.left_ref.coupled_ref = bf16[512,2048]{1,0:T(8,128)(2,1)S(1)} custom-call(s32[3]{0:T(128)S(1)} %pad_add_fusion.place_ref, f32[1]{0:T(128)S(6)} %copy.15.refs_0_.rate_ref, s32[1,2048]{1,0:T(1,128)S(1)} %bitcast.20, bf16[512,2048]{1,0:T(8,128)(2,1)} %collective-permute-done.refs_2_), custom_call_target="tpu_custom_call" | custom-call | flops 1048576 | bytes 65536 | tf_op jit(solution)/shard_map/couple_here/pallas_call | solution.py:112
  40.3 18.4 %collective-permute-done.5.far_zero = bf16[512,1536]{1,0:T(8,128)(2,1)S(1)} collective-permute-done((bf16[512,1536]{1,0:T(8,128)(2,1)S(1)}, bf16[512,1536]{1,0:T(8,128)(2,1)S(1)}, u32[]{:S(2)}, u32[]{:S(2)}) %collective-permute-start.5) | collective-permute-done | bytes 1572896 | tf_op jit(solution)/shard_map/ppermute | solution.py:100
  60.1 1.4 %multiply.16.left_ref = bf16[512,2048]{1,0:T(8,128)(2,1)S(1)} custom-call(s32[3]{0:T(128)S(1)} %pad_add_fusion.place_ref, bf16[512,2048]{1,0:T(8,128)(2,1)S(1)} %couple_here.3.coupled_ref.left_ref, bf16[2048,2048]{1,0:T(8,128)(2,1)S(1)} %assemble.1.right_ref), custom_call_target="tpu_custom_call" | custom-call | flops 1048576 | bytes 65536 | tf_op jit(solution)/shard_map/multiply/pallas_call | solution.py:172
  61.5 1.3 multiply.17
  63.5 1.4 %multiply.11.left_ref = bf16[512,2048]{1,0:T(8,128)(2,1)S(1)} custom-call(s32[3]{0:T(128)S(1)} %pad_add_fusion.place_ref, bf16[512,2048]{1,0:T(8,128)(2,1)S(1)} %couple_here.2.left_ref.coupled_ref, bf16[2048,2048]{1,0:T(8,128)(2,1)S(1)} %assemble.1.right_ref), custom_call_target="tpu_custom_call" | custom-call | flops 1048576 | bytes 65536 | tf_op jit(solution)/shard_map/multiply/pallas_call | solution.py:172
  65.0 1.3 multiply.12
  66.2 1.3 collective-permute-start.7
  67.6 1.4 %multiply.19.left_ref = bf16[512,2048]{1,0:T(8,128)(2,1)S(1)} custom-call(s32[3]{0:T(128)S(1)} %pad_add_fusion.place_ref, bf16[512,2048]{1,0:T(8,128)(2,1)S(1)} %collective-permute-done.8.coupled_ref.left_ref, bf16[2048,2048]{1,0:T(8,128)(2,1)S(1)} %assemble.1.right_ref), custom_call_target="tpu_custom_call" | custom-call | flops 1048576 | bytes 65536 | tf_op jit(solution)/shard_map/multiply/pallas_call | solution.py:172
  74.7 1.3 collective-permute-start.9
  78.0 1.4 %multiply.14.left_ref = bf16[512,2048]{1,0:T(8,128)(2,1)S(1)} custom-call(s32[3]{0:T(128)S(1)} %pad_add_fusion.place_ref, bf16[512,2048]{1,0:T(8,128)(2,1)S(1)} %couple.1.coupled_ref.left_ref, bf16[2048,2048]{1,0:T(8,128)(2,1)S(1)} %assemble.1.right_ref), custom_call_target="tpu_custom_call" | custom-call | flops 1048576 | bytes 65536 | tf_op jit(solution)/shard_map/multiply/pallas_call | solution.py:172
  79.5 1.4 %multiply.15.q1 = bf16[512,2048]{1,0:T(8,128)(2,1)S(1)} custom-call(s32[3]{0:T(128)S(1)} %pad_add_fusion.place_ref, bf16[512,2048]{1,0:T(8,128)(2,1)S(1)} %multiply.14.left_ref, bf16[2048,2048]{1,0:T(8,128)(2,1)S(1)} %turn.7.right_ref), custom_call_target="tpu_custom_call" | custom-call | flops 1048576 | bytes 65536 | tf_op jit(solution)/shard_map/multiply/pallas_call | solution.py:172
  80.9 27.6 %collective-permute-done.7.q0 = bf16[512,1536]{1,0:T(8,128)(2,1)S(1)} collective-permute-done((bf16[512,1536]{1,0:T(8,128)(2,1)S(1)}, bf16[512,1536]{1,0:T(8,128)(2,1)S(1)}, u32[]{:S(2)}, u32[]{:S(2)}) %collective-permute-start.7) | collective-permute-done | bytes 1572896 | tf_op jit(solution)/shard_map/ppermute | solution.py:100
  108.5 29.1 %collective-permute-done.9.q0_last = bf16[512,512]{1,0:T(8,128)(2,1)S(1)} collective-permute-done((bf16[512,512]{1,0:T(8,128)(2,1)S(1)}, bf16[512,512]{1,0:T(8,128)(2,1)S(1)}, u32[]{:S(2)}, u32[]{:S(2)}) %collective-permute-start.9) | collective-permute-done | bytes 524320 | tf_op jit(solution)/shard_map/ppermute | solution.py:100
  137.6 2.7 %final.1 = (bf16[512,2048]{1,0:T(8,128)(2,1)}, f32[1,512]{1,0:T(1,128)}) custom-call(s32[3]{0:T(128)S(1)} %pad_add_fusion.place_ref, s32[1]{0:T(128)S(6)} %convert_element_type.3.active_ref, bf16[512,2048]{1,0:T(8,128)(2,1)S(1)} %bitcast.17, bf16[512,1536]{1,0:T(8,128)(2,1)S(1)} %collective-permute-done.7.q0, ...), custom_call_target="tpu_custom_call" | custom-call | flops 1048576 | bytes 65536 | tf_op jit(solution)/shard_map/final/pallas_call | solution.py:355
  (34 shorter events, 15.6 us)
Async XLA Ops:
  0.7 5.8 %copy-start.1 = (bf16[1,512,2048]{2,1,0:T(8,128)(2,1)S(1)}, bf16[1,512,2048]{2,1,0:T(8,128)(2,1)}, u32[]{:S(2)}) copy-start(bf16[1,512,2048]{2,1,0:T(8,128)(2,1)} %param.9) | copy-start | bytes 6291460
  0.7 14.7 %copy-start.2 = (s32[2048]{0:T(1024)S(1)}, s32[2048]{0:T(1024)}, u32[]{:S(2)}) copy-start(s32[2048]{0:T(1024)} %param.13) | copy-start | bytes 24580
  3.9 17.5 %collective-permute-start.1 = (bf16[512,1024]{1,0:T(8,128)(2,1)}, bf16[512,1024]{1,0:T(8,128)(2,1)}, u32[]{:S(2)}, u32[]{:S(2)}) collective-permute-start(bf16[512,1024]{1,0:T(8,128)(2,1)} %get-tuple-element.19), channel_id=1, source_target_pairs={{4,0},{8,4},{12,8},{5,1},{9,5},{13,9},{6,2},{10,6},{14,10},{7,3},{... | collective-permute-start | bytes 3145736 | tf_op jit(solution)/shard_map/ppermute | solution.py:20
  5.1 18.4 %collective-permute-start.2 = (bf16[512,1024]{1,0:T(8,128)(2,1)}, bf16[512,1024]{1,0:T(8,128)(2,1)S(1)}, u32[]{:S(2)}, u32[]{:S(2)}) collective-permute-start(bf16[512,1024]{1,0:T(8,128)(2,1)} %get-tuple-element.18), channel_id=1, source_target_pairs={{4,0},{8,4},{12,8},{5,1},{9,5},{13,9},{6,2},{10,6},{14,10},{7,3},{... | collective-permute-start | bytes 3145736 | tf_op jit(solution)/shard_map/ppermute | solution.py:20
  6.5 20.9 %collective-permute-start.6 = (bf16[512,2048]{1,0:T(8,128)(2,1)S(1)}, bf16[512,2048]{1,0:T(8,128)(2,1)}, u32[]{:S(2)}, u32[]{:S(2)}) collective-permute-start(bf16[512,2048]{1,0:T(8,128)(2,1)S(1)} %bitcast.14), channel_id=1, source_target_pairs={{2,1},{5,6},{10,9},{13,14},{18,17},{21,22},{26,25},{29,30}} | collective-permute-start | bytes 6291464 | tf_op jit(solution)/shard_map/ppermute | solution.py:100
  8.4 27.8 %collective-permute-start = (bf16[512,2048]{1,0:T(8,128)(2,1)S(1)}, bf16[512,2048]{1,0:T(8,128)(2,1)}, u32[]{:S(2)}, u32[]{:S(2)}) collective-permute-start(bf16[512,2048]{1,0:T(8,128)(2,1)S(1)} %bitcast.15), channel_id=1, source_target_pairs={{0,1},{7,6},{8,9},{15,14},{16,17},{23,22},{24,25},{31,30}} | collective-permute-start | bytes 6291464 | tf_op jit(solution)/shard_map/ppermute | solution.py:100
  20.2 1.6 %copy-start = (bf16[1,512,2048]{2,1,0:T(8,128)(2,1)S(1)}, bf16[1,512,2048]{2,1,0:T(8,128)(2,1)}, u32[]{:S(2)}) copy-start(bf16[1,512,2048]{2,1,0:T(8,128)(2,1)} %param.7) | copy-start | bytes 6291460
  24.6 34.1 %collective-permute-start.5 = (bf16[512,1536]{1,0:T(8,128)(2,1)S(1)}, bf16[512,1536]{1,0:T(8,128)(2,1)S(1)}, u32[]{:S(2)}, u32[]{:S(2)}) collective-permute-start(bf16[512,1536]{1,0:T(8,128)(2,1)S(1)} %get-tuple-element.14), channel_id=1, source_target_pairs={{0,1},{7,6},{8,9},{15,14},{16,17},{23,22},{24,25},{31,30}} | collective-permute-start | bytes 4718600 | tf_op jit(solution)/shard_map/ppermute | solution.py:100
  26.0 14.3 %collective-permute-start.3 = (bf16[512,1024]{1,0:T(8,128)(2,1)S(1)}, bf16[512,1024]{1,0:T(8,128)(2,1)S(1)}, u32[]{:S(2)}, u32[]{:S(2)}) collective-permute-start(bf16[512,1024]{1,0:T(8,128)(2,1)S(1)} %get-tuple-element.11.near_ref.near_own), channel_id=1, source_target_pairs={{2,1},{5,6},{10,9},{13,14},{18,17},{21,22},{26,25},{29,30}} | collective-permute-start | bytes 3145736 | tf_op jit(solution)/shard_map/ppermute | solution.py:100
  26.7 13.6 %collective-permute-start.4 = (bf16[512,512]{1,0:T(8,128)(2,1)S(1)}, bf16[512,512]{1,0:T(8,128)(2,1)S(1)}, u32[]{:S(2)}, u32[]{:S(2)}) collective-permute-start(bf16[512,512]{1,0:T(8,128)(2,1)S(1)} %get-tuple-element.13), channel_id=1, source_target_pairs={{3,1},{4,6},{11,9},{12,14},{19,17},{20,22},{27,25},{28,30}} | collective-permute-start | bytes 1572872 | tf_op jit(solution)/shard_map/ppermute | solution.py:100
  58.7 8.8 %collective-permute-start.8 = (bf16[512,2048]{1,0:T(8,128)(2,1)S(1)}, bf16[512,2048]{1,0:T(8,128)(2,1)S(1)}, u32[]{:S(2)}, u32[]{:S(2)}) collective-permute-start(bf16[512,2048]{1,0:T(8,128)(2,1)S(1)} %couple.1.coupled_ref.left_ref), channel_id=1, source_target_pairs={{3,1},{4,6},{11,9},{12,14},{19,17},{20,22},{27,25},{28,30}} | collective-permute-start | bytes 6291464 | tf_op jit(solution)/shard_map/ppermute | solution.py:100
  62.8 13.9 %collective-permute-start.10 = (bf16[512,1536]{1,0:T(8,128)(2,1)S(1)}, bf16[512,1536]{1,0:T(8,128)(2,1)S(1)}, u32[]{:S(2)}, u32[]{:S(2)}) collective-permute-start(bf16[512,1536]{1,0:T(8,128)(2,1)S(1)} %multiply.17), channel_id=1, source_target_pairs={{1,2},{6,5},{9,10},{14,13},{17,18},{22,21},{25,26},{30,29}} | collective-permute-start | bytes 4718600 | tf_op jit(solution)/shard_map/ppermute | solution.py:100
  66.2 42.3 %collective-permute-start.7 = (bf16[512,1536]{1,0:T(8,128)(2,1)S(1)}, bf16[512,1536]{1,0:T(8,128)(2,1)S(1)}, u32[]{:S(2)}, u32[]{:S(2)}) collective-permute-start(bf16[512,1536]{1,0:T(8,128)(2,1)S(1)} %multiply.12), channel_id=1, source_target_pairs={{1,0},{6,7},{9,8},{14,15},{17,16},{22,23},{25,24},{30,31}} | collective-permute-start | bytes 4718600 | tf_op jit(solution)/shard_map/ppermute | solution.py:100
  72.3 65.3 %collective-permute-start.12 = (bf16[512,1024]{1,0:T(8,128)(2,1)S(1)}, bf16[512,1024]{1,0:T(8,128)(2,1)S(1)}, u32[]{:S(2)}, u32[]{:S(2)}) collective-permute-start(bf16[512,1024]{1,0:T(8,128)(2,1)S(1)} %multiply.20), channel_id=1, source_target_pairs={{1,3},{6,4},{9,11},{14,12},{17,19},{22,20},{25,27},{30,28}} | collective-permute-start | bytes 3145736 | tf_op jit(solution)/shard_map/ppermute | solution.py:100
  73.0 64.6 %collective-permute-start.13 = (bf16[512,1024]{1,0:T(8,128)(2,1)S(1)}, bf16[512,1024]{1,0:T(8,128)(2,1)S(1)}, u32[]{:S(2)}, u32[]{:S(2)}) collective-permute-start(bf16[512,1024]{1,0:T(8,128)(2,1)S(1)} %multiply.21), channel_id=1, source_target_pairs={{1,3},{6,4},{9,11},{14,12},{17,19},{22,20},{25,27},{30,28}} | collective-permute-start | bytes 3145736 | tf_op jit(solution)/shard_map/ppermute | solution.py:100
  74.7 63.0 %collective-permute-start.9 = (bf16[512,512]{1,0:T(8,128)(2,1)S(1)}, bf16[512,512]{1,0:T(8,128)(2,1)S(1)}, u32[]{:S(2)}, u32[]{:S(2)}) collective-permute-start(bf16[512,512]{1,0:T(8,128)(2,1)S(1)} %multiply.13), channel_id=1, source_target_pairs={{1,0},{6,7},{9,8},{14,15},{17,16},{22,23},{25,24},{30,31}} | collective-permute-start | bytes 1572872 | tf_op jit(solution)/shard_map/ppermute | solution.py:100
  76.7 60.9 %collective-permute-start.11 = (bf16[512,512]{1,0:T(8,128)(2,1)S(1)}, bf16[512,512]{1,0:T(8,128)(2,1)S(1)}, u32[]{:S(2)}, u32[]{:S(2)}) collective-permute-start(bf16[512,512]{1,0:T(8,128)(2,1)S(1)} %multiply.18), channel_id=1, source_target_pairs={{1,2},{6,5},{9,10},{14,13},{17,18},{22,21},{25,26},{30,29}} | collective-permute-start | bytes 1572872 | tf_op jit(solution)/shard_map/ppermute | solution.py:100

commit v3 on v2

--- a/solution.py
+++ b/solution.py
@@ -197,52 +197,50 @@
         out_ref[...] = sigma_ref[...]
 
 
-def near_kernel(place_ref, step_ref, shifted_ref, sigma_ref, near_ref, last_ref):
+def parts_kernel(place_ref, step_ref, shifted_ref, sigma_ref, row_ref, far_ref, near_ref, last_ref):
+    odd = place_ref[0]
     width = last_ref.shape[1]
-    prior_kernel(step_ref, shifted_ref, sigma_ref, near_ref)
-    start = pl.multiple_of((1 - place_ref[0]) * width, 128)
-    last_ref[...] = near_ref[:, pl.ds(start, width)]
-
-
-def far_kernel(place_ref, step_ref, shifted_ref, sigma_ref, near_ref, other_ref, far_ref):
-    width = near_ref.shape[1] // 2
-    prior_kernel(step_ref, shifted_ref, sigma_ref, other_ref)
-    start = pl.multiple_of(place_ref[0] * width, 128)
-    far_ref[:, :width] = other_ref[:, pl.ds(start, width)]
-    far_ref[:, width:] = near_ref[...]
-
-
-def prior_half(kernel, side, sent, place, step, shifted, sigma, *more):
+
+    def at(block, count=1):
+        return pl.ds(pl.multiple_of(block * width, 128), count * width)
+
+    prior_kernel(step_ref, shifted_ref, sigma_ref, row_ref)
+    near = row_ref[:, at(2 - 2 * odd, 2)]
+    near_ref[...] = near
+    far_ref[:, width:] = near
+    far_ref[:, :width] = row_ref[:, at(3 * odd)]
+    last_ref[...] = row_ref[:, at(3 - 3 * odd)]
+
+
+def prior_parts(place, step, shifted, sigma):
     rows, nodes = sigma.shape
     chunk = 128
     width = nodes // 4
-    half = lambda column: pl.BlockSpec((chunk, 2 * width), column)
-    return pl.pallas_call(
-        kernel,
-        out_shape=(
-            jax.ShapeDtypeStruct((rows, 2 * width), BF16),
-            jax.ShapeDtypeStruct((rows, sent * width), BF16),
-        ),
+    out = lambda blocks: jax.ShapeDtypeStruct((rows, blocks * width), BF16)
+    spec = lambda blocks: pl.BlockSpec((chunk, blocks * width), lambda i, place, step: (i, 0))
+    return pl.pallas_call(
+        parts_kernel,
+        out_shape=(out(4), out(3), out(2), out(1)),
         grid_spec=pltpu.PrefetchScalarGridSpec(
             num_scalar_prefetch=2,
             grid=(rows // chunk,),
             in_specs=[
-                half(lambda i, place, step: (jnp.where(step[0] == 0, i, 0), 0)),
-                half(lambda i, place, step: (jnp.where(step[0] == 0, 0, i), side(place[0]))),
-            ]
-            + [half(lambda i, place, step: (i, 0))] * len(more),
-            out_specs=(
-                half(lambda i, place, step: (i, 0)),
-                pl.BlockSpec((chunk, sent * width), lambda i, place, step: (i, 0)),
-            ),
+                pl.BlockSpec(
+                    (chunk, nodes), lambda i, place, step: (jnp.where(step[0] == 0, i, 0), 0)
+                ),
+                pl.BlockSpec(
+                    (chunk, nodes), lambda i, place, step: (jnp.where(step[0] == 0, 0, i), 0)
+                ),
+            ],
+            out_specs=(spec(4), spec(3), spec(2), spec(1)),
         ),
         compiler_params=pltpu.CompilerParams(vmem_limit_bytes=12 * MIB),
         cost_estimate=LIGHT,
-        name="prior_half",
-    )(place, step, shifted, sigma, *more)
-
-
-def assemble_kernel(place_ref, near_own, other_own, near_two, last_three, far_zero, out_ref):
+        name="prior_parts",
+    )(place, step, shifted, sigma)
+
+
+def assemble_kernel(place_ref, own, near_two, last_three, far_zero, out_ref):
     @pl.when(place_ref[1] == 1)
     def _():
         odd = place_ref[0]
@@ -254,27 +252,26 @@
         near = 2 * (1 - odd)
         half = pl.ds(pl.multiple_of(near * width, 128), 2 * width)
         row = [turned(block, odd) for block in range(4)]
-        other = pl.ds(pl.multiple_of(2 * odd * width, 128), 2 * width)
-        out_ref[at(row[1]), half] = near_own[...]
-        out_ref[at(row[1]), other] = other_own[...]
+        out_ref[at(row[1]), :] = own[...]
         out_ref[at(row[2]), half] = near_two[...]
         out_ref[at(row[0]), at(row[0])] = far_zero[:, :width]
         out_ref[at(row[0]), half] = far_zero[:, width:]
         out_ref[at(row[3]), at(row[3])] = last_three[...]
         for step in range(2):
-            out_ref[at(near + step), at(row[1])] = near_own[:, step * width : (1 + step) * width].T
-            out_ref[at(near + step), at(row[0])] = far_zero[:, (1 + step) * width : (2 + step) * width].T
-        out_ref[at(row[0]), at(row[1])] = other_own[:, at(odd)].T
+            out_ref[at(near + step), at(row[1])] = own[:, at(near + step)].T
+            piece = slice((1 + step) * width, (2 + step) * width)
+            out_ref[at(near + step), at(row[0])] = far_zero[:, piece].T
+        out_ref[at(row[0]), at(row[1])] = own[:, at(row[0])].T
         out_ref[at(row[3]), at(row[2])] = near_two[:, at(1 - odd)].T
 
 
 def assemble(place, *parts):
-    nodes = 2 * parts[0].shape[1]
+    nodes = parts[0].shape[1]
     vmem = pl.BlockSpec(memory_space=pltpu.VMEM)
     return pl.pallas_call(
         assemble_kernel,
         out_shape=jax.ShapeDtypeStruct((nodes, nodes), BF16),
-        in_specs=[pl.BlockSpec(memory_space=pltpu.SMEM)] + [vmem] * 5,
+        in_specs=[pl.BlockSpec(memory_space=pltpu.SMEM)] + [vmem] * 4,
         out_specs=vmem,
         compiler_params=pltpu.CompilerParams(vmem_limit_bytes=20 * MIB),
         cost_estimate=LIGHT,
@@ -327,7 +324,7 @@
     @pl.when(active & (place == 2))
     def _():
         add(at(odd, 3), q2[...])
-        add(at(3 - 3 * odd), q2_last[...])
+        add(at(3 - 3 * odd), q2_last[:, pl.ds(here, rows)].T)
         trace(q2[:, own(2 - 2 * odd)])
 
     @pl.when(active & (place == 3))
@@ -367,7 +364,7 @@
                 picked(0, 1),
                 picked(1, 4),
                 picked(2, 3),
-                picked(2, 1),
+                pl.BlockSpec((rows, width), lambda i, place, active: (0, 0)),
                 picked(3, 2),
                 picked(3, 2),
                 pl.BlockSpec(
@@ -393,44 +390,43 @@
     active = (step_index < lengths).astype(jnp.int32)
     width = pivot.shape[1] // 4
 
-    half = 2 * width
-
+
+    shifted = passed_along(separator, "dom", -1)[0]
     p2 = moved(pivot, 2, 1)
     p0 = moved(pivot, 0, 1)
-    near = lax.dynamic_slice_in_dim(separator[0], odd * half, half, 1)
-    other = lax.dynamic_slice_in_dim(separator[0], (1 - odd) * half, half, 1)
-    near = passed_along(near, "dom", -1)
-    other = passed_along(other, "dom", -1)
     c1 = couple(pivot, node_class, coupling_rate)
     across = turn(place, 1, c1, None)
 
-    near = lax.optimization_barrier((near, across))[0]
-    near, last = prior_half(near_kernel, lambda odd: 1 - odd, 1, place, step_index, near, sigma)
-    near_two, last_three = moved(near, 2, 1), moved(last, 3, 1)
-    other, far = prior_half(far_kernel, lambda odd: odd, 3, place, step_index, other, sigma, near)
-    far_zero = moved(far, 0, 1)
+    shifted = lax.optimization_barrier((shifted, p2, p0, across))[0]
+    row, far, near, last = prior_parts(place, step_index, shifted, sigma)
+    far_zero, near_two, last_three = moved(far, 0, 1), moved(near, 2, 1), moved(last, 3, 1)
+
+    p2 = lax.optimization_barrier((p2, last))[0]
     c2 = couple_here(place, p2, node_class, coupling_rate)
     across = turn(place, 2, c2, across)
     c0 = couple_here(place, p0, node_class, coupling_rate)
     across = turn(place, 0, c0, across)
     c3 = lax.optimization_barrier((c1, last_three, near_two, far_zero, across))[0]
     c3 = moved(c3, 3, 1)
-    prior = assemble(place, near, other, near_two, last_three, far_zero)
-    h2 = multiply(place, c2, prior)
+    prior = assemble(place, row, near_two, last_three, far_zero)
     most = lambda odd: odd
     rest = lambda odd: 3 - 3 * odd
-    q2 = moved(multiply(place, h2, across, most, 3), 1, 2)
-    h0 = multiply(place, c0, prior)
+    h2 = multiply(place, c2, prior)
+    q2 = multiply(place, h2, across, most, 3)
+    h0 = multiply(place, lax.optimization_barrier((c0, q2))[0], prior)
+    q2 = moved(q2, 1, 2)
     q0 = moved(multiply(place, h0, across, most, 3), 1, 0)
-    h1 = multiply(place, c1, prior)
 
     across = turn(place, 3, c3, across)
     h3 = multiply(place, c3, prior)
     q3_near = moved(multiply(place, h3, across, lambda odd: 2 - 2 * odd, 2), 1, 3)
-    q3_other = moved(multiply(place, h3, across, lambda odd: 2 * odd, 2), 1, 3)
-    q2_last = moved(multiply(place, h2, across, rest, 1), 1, 2)
-    q0_last = moved(multiply(place, h0, across, rest, 1), 1, 0)
+    q3_other = multiply(place, h3, across, lambda odd: 2 * odd, 2)
+    q0_last = multiply(place, h0, across, rest, 1)
+    h1 = multiply(place, lax.optimization_barrier((c1, q2, q3_other, q0_last))[0], prior)
+    q3_other, q0_last = moved(q3_other, 1, 3), moved(q0_last, 1, 0)
     q1 = multiply(place, h1, across)
+    q2_last = lax.optimization_barrier((q3_near, q0, q1))[0]
+    q2_last = moved(lax.dynamic_slice_in_dim(q2_last, odd * width, width, 1), 3, 2)
     products = (q0, q0_last, q1, q2, q2_last, q3_near, q3_other)
     covariance, variances = final(place, active, pivot, products, sigma)
     return (covariance[None], variances)

time: 141 us -> 148 us (1.050)
  waiting for transfers between devices: 79.9 us -> 70.1 us
  local copies, waits for them, and re-layouts: 3.56 us -> 10.7 us
  Pallas kernels: 34.7 us -> 40.1 us
  starting transfers between devices: 19.2 us -> 23.5 us
    unnamed x6 -> x28, local copies, waits for them, and re-layouts: 0.37 us -> 10.7 us
    ppermute x12, waiting for transfers between devices: 79.9 us -> 70.1 us  [moved(): lax.ppermute(value, ('dom', 'col'), route(source, target, lax.axis_size('...]
    ppermute x12, starting transfers between devices: 16.7 us -> 22.2 us  [moved(): lax.ppermute(value, ('dom', 'col'), route(source, target, lax.axis_size('...]
    pallas_call x11 -> x10, Pallas kernels: 13.4 us -> 17.5 us  [multiply(): pl.pallas_call(multiply_kernel, out_shape=jax.ShapeDtypeStruct((rows, cou...]
    dynamic_slice x1, local copies, waits for them, and re-layouts: 3.19 us -> 0.04 us  [owned(): lax.dynamic_slice_in_dim(q2_last, odd * width, width, 1)]
    pallas_call x1, Pallas kernels: 2.74 us -> 4.72 us  [final(): pl.pallas_call(final_kernel, out_shape=(jax.ShapeDtypeStruct((rows, nodes...]
  transfers between devices with their start and end apart: 14 -> 13, of which waited for: 4 -> 4; matrix products, arithmetic and copies ran while one was open for 0% -> 0% of each run, Pallas kernels for 23% -> 23%
where the time goes in v3:
time: 148 us; the launch traced here: 147 us
  waiting for transfers between devices  70.1 us (47%)
  Pallas kernels  40.1 us (27%)
  starting transfers between devices  23.5 us (16%)
  local copies, waits for them, and re-layouts  10.7 us (7%)
  between operations  2.94 us (2%)
    ppermute x12, waiting for transfers between devices, moved(): lax.ppermute(value, ('dom', 'col'), route(source, target, lax.axis_size('...  70.1 us
    ppermute x12, starting transfers between devices, moved(): lax.ppermute(value, ('dom', 'col'), route(source, target, lax.axis_size('...  22.2 us
    pallas_call x10, Pallas kernels, multiply(): pl.pallas_call(multiply_kernel, out_shape=jax.ShapeDtypeStruct((rows, cou...  17.5 us
    unnamed x28, local copies, waits for them, and re-layouts  10.7 us
    pallas_call x2, Pallas kernels, couple_here(): pl.pallas_call(kernel, out_shape=jax.ShapeDtypeStruct((rows, nodes), BF16...  5.65 us
    pallas_call x4, Pallas kernels, turn(): pl.pallas_call(turn_kernel, out_shape=jax.ShapeDtypeStruct((nodes, nodes)...  4.85 us
    pallas_call x1, Pallas kernels, couple(): pl.pallas_call(couple_kernel, out_shape=jax.ShapeDtypeStruct((rows, nodes...  4.74 us
    pallas_call x1, Pallas kernels, final(): pl.pallas_call(final_kernel, out_shape=(jax.ShapeDtypeStruct((rows, nodes...  4.72 us
  transfers between devices with their start and end apart: 13, of which 4 were waited for; matrix products, arithmetic and copies ran while one was open for 0% of the time, Pallas kernels for 23%

profile of v3, /device:TPU:0, one launch (start us, length us, event | category | flops | bytes accessed | tf_op | source)
XLA Modules:
  0.0 147.4 jit_solution(14627878423447125423)
XLA Ops:
  1.9 2.0 %collective-permute-start.1 = (bf16[512,2048]{1,0:T(8,128)(2,1)}, bf16[512,2048]{1,0:T(8,128)(2,1)}, u32[]{:S(2)}, u32[]{:S(2)}) collective-permute-start(bf16[512,2048]{1,0:T(8,128)(2,1)} %bitcast.12), channel_id=1, source_target_pairs={{2,1},{5,6},{10,9},{13,14},{18,17},{21,22},{26,25},{29,30}} | collective-permute-start | bytes 6291464 | tf_op jit(solution)/shard_map/ppermute | solution.py:100
  4.0 5.6 %collective-permute-start = (bf16[512,2048]{1,0:T(8,128)(2,1)}, bf16[512,2048]{1,0:T(8,128)(2,1)}, u32[]{:S(2)}, u32[]{:S(2)}) collective-permute-start(bf16[512,2048]{1,0:T(8,128)(2,1)} %bitcast.13), channel_id=1, source_target_pairs={{0,1},{7,6},{8,9},{15,14},{16,17},{23,22},{24,25},{31,30}} | collective-permute-start | bytes 6291464 | tf_op jit(solution)/shard_map/ppermute | solution.py:100
  10.8 1.6 %copy-done.8 = bf16[1,512,2048]{2,1,0:T(8,128)(2,1)S(1)} copy-done((bf16[1,512,2048]{2,1,0:T(8,128)(2,1)S(1)}, bf16[1,512,2048]{2,1,0:T(8,128)(2,1)}, u32[]{:S(2)}) %copy-start.8) | copy-done | bytes 2097176
  13.1 4.7 %couple.1.coupled_ref.left_ref = bf16[512,2048]{1,0:T(8,128)(2,1)S(1)} custom-call(f32[1]{0:T(128)S(6)} %copy.15.refs_0_.rate_ref, s32[1,2048]{1,0:T(1,128)S(1)} %bitcast.16, bf16[512,2048]{1,0:T(8,128)(2,1)S(1)} %bitcast.14), custom_call_target="tpu_custom_call" | custom-call | flops 1048576 | bytes 65536 | tf_op jit(solution)/shard_map/couple/pallas_call | solution.py:70
  19.2 12.8 %collective-permute-done.refs_2_ = bf16[512,2048]{1,0:T(8,128)(2,1)} collective-permute-done((bf16[512,2048]{1,0:T(8,128)(2,1)}, bf16[512,2048]{1,0:T(8,128)(2,1)}, u32[]{:S(2)}, u32[]{:S(2)}) %collective-permute-start) | collective-permute-done | bytes 2097184 | tf_op jit(solution)/shard_map/ppermute | solution.py:100
  32.0 2.1 %prior_parts.1 = (bf16[512,2048]{1,0:T(8,128)(2,1)S(1)}, bf16[512,1536]{1,0:T(8,128)(2,1)S(1)}, bf16[512,1024]{1,0:T(8,128)(2,1)S(1)}, bf16[512,512]{1,0:T(8,128)(2,1)S(1)}) custom-call(s32[3]{0:T(128)S(1)} %pad_add_fusion.place_ref, s32[1]{0:T(128)S(6)} %copy.17.step_ref, bf16[512,2048]{1,0:T(8,128)(2,1)} %bitcast.5.shifted_ref, bf16[512,2048]{1,0:T(8,128)(2,1)S(1)} %bitcast.10), custom_call_target="tpu_custom_call" | custom-call | flops 1048576 | bytes 65536 | tf_op jit(solution)/shard_map/prior_parts/pallas_call | solution.py:221
  34.1 4.5 %collective-permute-start.5 = (bf16[512,1536]{1,0:T(8,128)(2,1)S(1)}, bf16[512,1536]{1,0:T(8,128)(2,1)S(1)}, u32[]{:S(2)}, u32[]{:S(2)}) collective-permute-start(bf16[512,1536]{1,0:T(8,128)(2,1)S(1)} %get-tuple-element.19), channel_id=1, source_target_pairs={{0,1},{7,6},{8,9},{15,14},{16,17},{23,22},{24,25},{31,30}} | collective-permute-start | bytes 4718600 | tf_op jit(solution)/shard_map/ppermute | solution.py:100
  40.0 2.8 %couple_here.3.left_ref.coupled_ref = bf16[512,2048]{1,0:T(8,128)(2,1)S(1)} custom-call(s32[3]{0:T(128)S(1)} %pad_add_fusion.place_ref, f32[1]{0:T(128)S(6)} %copy.15.refs_0_.rate_ref, s32[1,2048]{1,0:T(1,128)S(1)} %bitcast.17, bf16[512,2048]{1,0:T(8,128)(2,1)} %collective-permute-done.1.refs_2_), custom_call_target="tpu_custom_call" | custom-call | flops 1048576 | bytes 65536 | tf_op jit(solution)/shard_map/couple_here/pallas_call | solution.py:112
  44.1 2.8 %couple_here.2.coupled_ref.left_ref = bf16[512,2048]{1,0:T(8,128)(2,1)S(1)} custom-call(s32[3]{0:T(128)S(1)} %pad_add_fusion.place_ref, f32[1]{0:T(128)S(6)} %copy.15.refs_0_.rate_ref, s32[1,2048]{1,0:T(1,128)S(1)} %bitcast.18, bf16[512,2048]{1,0:T(8,128)(2,1)} %collective-permute-done.refs_2_), custom_call_target="tpu_custom_call" | custom-call | flops 1048576 | bytes 65536 | tf_op jit(solution)/shard_map/couple_here/pallas_call | solution.py:112
  48.1 13.9 %collective-permute-done.5.far_zero = bf16[512,1536]{1,0:T(8,128)(2,1)S(1)} collective-permute-done((bf16[512,1536]{1,0:T(8,128)(2,1)S(1)}, bf16[512,1536]{1,0:T(8,128)(2,1)S(1)}, u32[]{:S(2)}, u32[]{:S(2)}) %collective-permute-start.5) | collective-permute-done | bytes 1572896 | tf_op jit(solution)/shard_map/ppermute | solution.py:100
  64.8 2.9 %multiply.11 = bf16[512,1536]{1,0:T(8,128)(2,1)} custom-call(s32[3]{0:T(128)S(1)} %pad_add_fusion.place_ref, bf16[512,2048]{1,0:T(8,128)(2,1)S(1)} %multiply.10.left_ref, bf16[2048,2048]{1,0:T(8,128)(2,1)S(1)} %turn.6.right_ref.refs_0_), custom_call_target="tpu_custom_call" | custom-call | flops 1048576 | bytes 65536 | tf_op jit(solution)/shard_map/multiply/pallas_call | solution.py:172
  67.7 1.9 %collective-permute-start.9 = (bf16[512,1536]{1,0:T(8,128)(2,1)}, bf16[512,1536]{1,0:T(8,128)(2,1)}, u32[]{:S(2)}, u32[]{:S(2)}) collective-permute-start(bf16[512,1536]{1,0:T(8,128)(2,1)} %multiply.11), channel_id=1, source_target_pairs={{1,2},{6,5},{9,10},{14,13},{17,18},{22,21},{25,26},{30,29}} | collective-permute-start | bytes 4718600 | tf_op jit(solution)/shard_map/ppermute | solution.py:100
  71.1 2.6 %multiply.13 = bf16[512,1536]{1,0:T(8,128)(2,1)} custom-call(s32[3]{0:T(128)S(1)} %pad_add_fusion.place_ref, bf16[512,2048]{1,0:T(8,128)(2,1)S(1)} %multiply.12.left_ref, bf16[2048,2048]{1,0:T(8,128)(2,1)S(1)} %turn.6.right_ref.refs_0_), custom_call_target="tpu_custom_call" | custom-call | flops 1048576 | bytes 65536 | tf_op jit(solution)/shard_map/multiply/pallas_call | solution.py:172
  76.2 1.4 multiply.15.left_ref
  77.7 2.1 %multiply.19 = bf16[512,1024]{1,0:T(8,128)(2,1)} custom-call(s32[3]{0:T(128)S(1)} %pad_add_fusion.place_ref, bf16[512,2048]{1,0:T(8,128)(2,1)S(1)} %multiply.15.left_ref, bf16[2048,2048]{1,0:T(8,128)(2,1)S(1)} %turn.7.right_ref), custom_call_target="tpu_custom_call" | custom-call | flops 1048576 | bytes 65536 | tf_op jit(solution)/shard_map/multiply/pallas_call | solution.py:172
  80.5 2.0 %multiply.16 = bf16[512,1024]{1,0:T(8,128)(2,1)} custom-call(s32[3]{0:T(128)S(1)} %pad_add_fusion.place_ref, bf16[512,2048]{1,0:T(8,128)(2,1)S(1)} %multiply.15.left_ref, bf16[2048,2048]{1,0:T(8,128)(2,1)S(1)} %turn.7.right_ref), custom_call_target="tpu_custom_call" | custom-call | flops 1048576 | bytes 65536 | tf_op jit(solution)/shard_map/multiply/pallas_call | solution.py:172
  82.5 1.6 %collective-permute-start.12 = (bf16[512,1024]{1,0:T(8,128)(2,1)}, bf16[512,1024]{1,0:T(8,128)(2,1)}, u32[]{:S(2)}, u32[]{:S(2)}) collective-permute-start(bf16[512,1024]{1,0:T(8,128)(2,1)} %multiply.16), channel_id=1, source_target_pairs={{1,3},{6,4},{9,11},{14,12},{17,19},{22,20},{25,27},{30,28}} | collective-permute-start | bytes 3145736 | tf_op jit(solution)/shard_map/ppermute | solution.py:100
  84.1 3.4 %copy-done.1 = bf16[2048,2048]{1,0:T(8,128)(2,1)S(1)} copy-done((bf16[2048,2048]{1,0:T(8,128)(2,1)S(1)}, bf16[2048,2048]{1,0:T(8,128)(2,1)}, u32[]{:S(2)}) %copy-start.1) | copy-done | bytes 8388632
  87.5 1.6 %copy-done.5 = bf16[512,2048]{1,0:T(8,128)(2,1)S(1)} copy-done((bf16[512,2048]{1,0:T(8,128)(2,1)S(1)}, bf16[512,2048]{1,0:T(8,128)(2,1)}, u32[]{:S(2)}) %copy-start.5) | copy-done | bytes 2097176
  89.8 1.7 %collective-permute-start.8 = (bf16[512,512]{1,0:T(8,128)(2,1)S(1)}, bf16[512,512]{1,0:T(8,128)(2,1)S(1)}, u32[]{:S(2)}, u32[]{:S(2)}) collective-permute-start(bf16[512,512]{1,0:T(8,128)(2,1)S(1)} %multiply.14), channel_id=1, source_target_pairs={{1,0},{6,7},{9,8},{14,15},{17,16},{22,23},{25,24},{30,31}} | collective-permute-start | bytes 1572872 | tf_op jit(solution)/shard_map/ppermute | solution.py:100
  91.6 3.4 %copy-done.3 = bf16[2048,2048]{1,0:T(8,128)(2,1)S(1)} copy-done((bf16[2048,2048]{1,0:T(8,128)(2,1)S(1)}, bf16[2048,2048]{1,0:T(8,128)(2,1)}, u32[]{:S(2)}) %copy-start.3) | copy-done | bytes 8388632
  97.9 39.2 %collective-permute-done.6.q0 = bf16[512,1536]{1,0:T(8,128)(2,1)} collective-permute-done((bf16[512,1536]{1,0:T(8,128)(2,1)}, bf16[512,1536]{1,0:T(8,128)(2,1)}, u32[]{:S(2)}, u32[]{:S(2)}) %collective-permute-start.6) | collective-permute-done | bytes 1572896 | tf_op jit(solution)/shard_map/ppermute | solution.py:100
  138.5 4.1 %collective-permute-done.8.q0_last = bf16[512,512]{1,0:T(8,128)(2,1)S(1)} collective-permute-done((bf16[512,512]{1,0:T(8,128)(2,1)S(1)}, bf16[512,512]{1,0:T(8,128)(2,1)S(1)}, u32[]{:S(2)}, u32[]{:S(2)}) %collective-permute-start.8) | collective-permute-done | bytes 524320 | tf_op jit(solution)/shard_map/ppermute | solution.py:100
  142.6 4.7 %final.1 = (bf16[512,2048]{1,0:T(8,128)(2,1)}, f32[1,512]{1,0:T(1,128)}) custom-call(s32[3]{0:T(128)S(1)} %pad_add_fusion.place_ref, s32[1]{0:T(128)S(6)} %convert_element_type.3.active_ref, bf16[512,2048]{1,0:T(8,128)(2,1)S(1)} %bitcast.15, bf16[512,1536]{1,0:T(8,128)(2,1)} %collective-permute-done.6.q0, ...), custom_call_target="tpu_custom_call" | custom-call | flops 1048576 | bytes 65536 | tf_op jit(solution)/shard_map/final/pallas_call | solution.py:352
  (53 shorter events, 18.9 us)
Async XLA Ops:
  0.6 18.5 %collective-permute-start.2 = (bf16[1,512,2048]{2,1,0:T(8,128)(2,1)}, bf16[1,512,2048]{2,1,0:T(8,128)(2,1)}, u32[]{:S(2)}, u32[]{:S(2)}) collective-permute-start(bf16[1,512,2048]{2,1,0:T(8,128)(2,1)} %param.8), channel_id=1, source_target_pairs={{4,0},{8,4},{12,8},{5,1},{9,5},{13,9},{6,2},{10,6},{14,10},{7,3},{... | collective-permute-start | bytes 6291464 | tf_op jit(solution)/shard_map/ppermute | solution.py:20
  1.9 17.2 %collective-permute-start.1 = (bf16[512,2048]{1,0:T(8,128)(2,1)}, bf16[512,2048]{1,0:T(8,128)(2,1)}, u32[]{:S(2)}, u32[]{:S(2)}) collective-permute-start(bf16[512,2048]{1,0:T(8,128)(2,1)} %bitcast.12), channel_id=1, source_target_pairs={{2,1},{5,6},{10,9},{13,14},{18,17},{21,22},{26,25},{29,30}} | collective-permute-start | bytes 6291464 | tf_op jit(solution)/shard_map/ppermute | solution.py:100
  4.0 28.1 %collective-permute-start = (bf16[512,2048]{1,0:T(8,128)(2,1)}, bf16[512,2048]{1,0:T(8,128)(2,1)}, u32[]{:S(2)}, u32[]{:S(2)}) collective-permute-start(bf16[512,2048]{1,0:T(8,128)(2,1)} %bitcast.13), channel_id=1, source_target_pairs={{0,1},{7,6},{8,9},{15,14},{16,17},{23,22},{24,25},{31,30}} | collective-permute-start | bytes 6291464 | tf_op jit(solution)/shard_map/ppermute | solution.py:100
  17.9 14.1 %copy-start.6 = (bf16[1,512,2048]{2,1,0:T(8,128)(2,1)S(1)}, bf16[1,512,2048]{2,1,0:T(8,128)(2,1)}, u32[]{:S(2)}) copy-start(bf16[1,512,2048]{2,1,0:T(8,128)(2,1)} %param.7) | copy-start | bytes 6291460
  32.0 8.0 %copy-start.11 = (s32[2048]{0:T(1024)S(1)}, s32[2048]{0:T(1024)}, u32[]{:S(2)}) copy-start(s32[2048]{0:T(1024)} %param.13) | copy-start | bytes 24580
  34.1 27.9 %collective-permute-start.5 = (bf16[512,1536]{1,0:T(8,128)(2,1)S(1)}, bf16[512,1536]{1,0:T(8,128)(2,1)S(1)}, u32[]{:S(2)}, u32[]{:S(2)}) collective-permute-start(bf16[512,1536]{1,0:T(8,128)(2,1)S(1)} %get-tuple-element.19), channel_id=1, source_target_pairs={{0,1},{7,6},{8,9},{15,14},{16,17},{23,22},{24,25},{31,30}} | collective-permute-start | bytes 4718600 | tf_op jit(solution)/shard_map/ppermute | solution.py:100
  38.6 9.6 %collective-permute-start.3 = (bf16[512,1024]{1,0:T(8,128)(2,1)S(1)}, bf16[512,1024]{1,0:T(8,128)(2,1)S(1)}, u32[]{:S(2)}, u32[]{:S(2)}) collective-permute-start(bf16[512,1024]{1,0:T(8,128)(2,1)S(1)} %get-tuple-element.18), channel_id=1, source_target_pairs={{2,1},{5,6},{10,9},{13,14},{18,17},{21,22},{26,25},{29,30}} | collective-permute-start | bytes 3145736 | tf_op jit(solution)/shard_map/ppermute | solution.py:100
  39.3 8.8 %collective-permute-start.4 = (bf16[512,512]{1,0:T(8,128)(2,1)S(1)}, bf16[512,512]{1,0:T(8,128)(2,1)S(1)}, u32[]{:S(2)}, u32[]{:S(2)}) collective-permute-start(bf16[512,512]{1,0:T(8,128)(2,1)S(1)} %get-tuple-element.15), channel_id=1, source_target_pairs={{3,1},{4,6},{11,9},{12,14},{19,17},{20,22},{27,25},{28,30}} | collective-permute-start | bytes 1572872 | tf_op jit(solution)/shard_map/ppermute | solution.py:100
  62.0 13.0 %collective-permute-start.7 = (bf16[512,2048]{1,0:T(8,128)(2,1)S(1)}, bf16[512,2048]{1,0:T(8,128)(2,1)S(1)}, u32[]{:S(2)}, u32[]{:S(2)}) collective-permute-start(bf16[512,2048]{1,0:T(8,128)(2,1)S(1)} %couple.1.coupled_ref.left_ref), channel_id=1, source_target_pairs={{3,1},{4,6},{11,9},{12,14},{19,17},{20,22},{27,25},{28,30}} | collective-permute-start | bytes 6291464 | tf_op jit(solution)/shard_map/ppermute | solution.py:100
  63.4 12.8 %copy-start.2 = (bf16[2048,2048]{1,0:T(8,128)(2,1)}, bf16[2048,2048]{1,0:T(8,128)(2,1)S(1)}, u32[]{:S(2)}) copy-start(bf16[2048,2048]{1,0:T(8,128)(2,1)S(1)} %assemble.1.right_ref) | copy-start | bytes 25165828
  67.7 23.8 %collective-permute-start.9 = (bf16[512,1536]{1,0:T(8,128)(2,1)}, bf16[512,1536]{1,0:T(8,128)(2,1)}, u32[]{:S(2)}, u32[]{:S(2)}) collective-permute-start(bf16[512,1536]{1,0:T(8,128)(2,1)} %multiply.11), channel_id=1, source_target_pairs={{1,2},{6,5},{9,10},{14,13},{17,18},{22,21},{25,26},{30,29}} | collective-permute-start | bytes 4718600 | tf_op jit(solution)/shard_map/ppermute | solution.py:100
  71.0 2.6 %copy-start.4 = (bf16[512,2048]{1,0:T(8,128)(2,1)}, bf16[512,2048]{1,0:T(8,128)(2,1)S(1)}, u32[]{:S(2)}) copy-start(bf16[512,2048]{1,0:T(8,128)(2,1)S(1)} %multiply.12.left_ref) | copy-start | bytes 6291460
  73.7 63.4 %collective-permute-start.6 = (bf16[512,1536]{1,0:T(8,128)(2,1)}, bf16[512,1536]{1,0:T(8,128)(2,1)}, u32[]{:S(2)}, u32[]{:S(2)}) collective-permute-start(bf16[512,1536]{1,0:T(8,128)(2,1)} %multiply.13), channel_id=1, source_target_pairs={{1,0},{6,7},{9,8},{14,15},{17,16},{22,23},{25,24},{30,31}} | collective-permute-start | bytes 4718600 | tf_op jit(solution)/shard_map/ppermute | solution.py:100
  76.2 4.3 %copy-start = (bf16[2048,2048]{1,0:T(8,128)(2,1)}, bf16[2048,2048]{1,0:T(8,128)(2,1)S(1)}, u32[]{:S(2)}) copy-start(bf16[2048,2048]{1,0:T(8,128)(2,1)S(1)} %turn.7.right_ref) | copy-start | bytes 25165828
  79.8 57.3 %collective-permute-start.10 = (bf16[512,1024]{1,0:T(8,128)(2,1)}, bf16[512,1024]{1,0:T(8,128)(2,1)S(1)}, u32[]{:S(2)}, u32[]{:S(2)}) collective-permute-start(bf16[512,1024]{1,0:T(8,128)(2,1)} %multiply.19), channel_id=1, source_target_pairs={{1,3},{6,4},{9,11},{14,12},{17,19},{22,20},{25,27},{30,28}} | collective-permute-start | bytes 3145736 | tf_op jit(solution)/shard_map/ppermute | solution.py:100
  82.5 60.1 %collective-permute-start.12 = (bf16[512,1024]{1,0:T(8,128)(2,1)}, bf16[512,1024]{1,0:T(8,128)(2,1)}, u32[]{:S(2)}, u32[]{:S(2)}) collective-permute-start(bf16[512,1024]{1,0:T(8,128)(2,1)} %multiply.16), channel_id=1, source_target_pairs={{1,3},{6,4},{9,11},{14,12},{17,19},{22,20},{25,27},{30,28}} | collective-permute-start | bytes 3145736 | tf_op jit(solution)/shard_map/ppermute | solution.py:100
  84.1 3.4 %copy-start.1 = (bf16[2048,2048]{1,0:T(8,128)(2,1)S(1)}, bf16[2048,2048]{1,0:T(8,128)(2,1)}, u32[]{:S(2)}) copy-start(bf16[2048,2048]{1,0:T(8,128)(2,1)} %copy-done) | copy-start | bytes 25165828
  89.1 7.3 %slice-start = ((s8[8388608]{0:T(1024)(128)(4,1)}), s8[4194304]{0:T(1024)(128)(4,1)S(1)}, s32[]{:S(2)}) async-start(s8[8388608]{0:T(1024)(128)(4,1)} %bitcast.8), calls=%async_computation | async-start | bytes 8388608
  89.8 6.6 %slice-start.1 = ((s8[8388608]{0:T(1024)(128)(4,1)}), s8[4194304]{0:T(1024)(128)(4,1)S(1)}, s32[]{:S(2)}) async-start(s8[8388608]{0:T(1024)(128)(4,1)} %bitcast.8), calls=%async_computation.1 | async-start | bytes 8388608
  89.8 52.8 %collective-permute-start.8 = (bf16[512,512]{1,0:T(8,128)(2,1)S(1)}, bf16[512,512]{1,0:T(8,128)(2,1)S(1)}, u32[]{:S(2)}, u32[]{:S(2)}) collective-permute-start(bf16[512,512]{1,0:T(8,128)(2,1)S(1)} %multiply.14), channel_id=1, source_target_pairs={{1,0},{6,7},{9,8},{14,15},{17,16},{22,23},{25,24},{30,31}} | collective-permute-start | bytes 1572872 | tf_op jit(solution)/shard_map/ppermute | solution.py:100
  91.6 3.4 %copy-start.3 = (bf16[2048,2048]{1,0:T(8,128)(2,1)S(1)}, bf16[2048,2048]{1,0:T(8,128)(2,1)}, u32[]{:S(2)}) copy-start(bf16[2048,2048]{1,0:T(8,128)(2,1)} %copy-done.2) | copy-start | bytes 25165828
  96.4 46.2 %copy-start.7 = (bf16[1,512,2048]{2,1,0:T(8,128)(2,1)S(1)}, bf16[1,512,2048]{2,1,0:T(8,128)(2,1)}, u32[]{:S(2)}) copy-start(bf16[1,512,2048]{2,1,0:T(8,128)(2,1)} %param.7) | copy-start | bytes 6291460
  96.4 46.2 %copy-start.9 = (bf16[1,512,2048]{2,1,0:T(8,128)(2,1)S(1)}, bf16[1,512,2048]{2,1,0:T(8,128)(2,1)}, u32[]{:S(2)}) copy-start(bf16[1,512,2048]{2,1,0:T(8,128)(2,1)} %param.9) | copy-start | bytes 6291460
  137.1 5.5 %collective-permute-start.11 = (bf16[512,512]{1,0:T(8,128)(2,1)S(1)}, bf16[512,512]{1,0:T(8,128)(2,1)S(1)}, u32[]{:S(2)}, u32[]{:S(2)}) collective-permute-start(bf16[512,512]{1,0:T(8,128)(2,1)S(1)} %constant_dynamic-slice_fusion), channel_id=1, source_target_pairs={{3,2},{4,5},{11,10},{12,13},{19,18},{20,21},{27,26},{28,29}} | collective-permute-start | bytes 1572872 | tf_op jit(solution)/shard_map/ppermute | solution.py:100
  (3 other events, 3.9 us)

commit v4 on v3

--- a/solution.py
+++ b/solution.py
@@ -78,7 +78,7 @@
         ],
         out_specs=pl.BlockSpec((chunk, nodes), lambda i: (i, 0)),
         scratch_shapes=[pltpu.VMEM((4, 16, nodes), F32)],
-        compiler_params=pltpu.CompilerParams(vmem_limit_bytes=8 * MIB),
+        compiler_params=pltpu.CompilerParams(vmem_limit_bytes=6 * MIB),
         cost_estimate=LIGHT,
         name="couple",
     )(rate, node_class.reshape(1, nodes), pivot)
@@ -135,56 +135,90 @@
         refs[-1][...] = coupled_ref[...].T
 
 
-def turn(place, panel, coupled, across):
+def turn(place, panel, part, coupled, across):
     rows, nodes = coupled.shape
     chunk = 128
-    ratio = rows // chunk
+    steps = rows // chunk
+    ratio = nodes // 4 // chunk
     return pl.pallas_call(
         turn_kernel,
         out_shape=jax.ShapeDtypeStruct((nodes, nodes), BF16),
         grid_spec=pltpu.PrefetchScalarGridSpec(
             num_scalar_prefetch=1,
-            grid=(ratio,),
+            grid=(steps,),
             in_specs=[pl.BlockSpec((chunk, nodes), lambda i, place: (i, 0))]
             + ([] if across is None else [pl.BlockSpec(memory_space=pl.ANY)]),
             out_specs=pl.BlockSpec(
-                (nodes, chunk), lambda i, place: (0, turned(panel, place[0]) * ratio + i)
+                (nodes, chunk),
+                lambda i, place: (0, turned(panel, place[0]) * ratio + part * steps + i),
             ),
         ),
         input_output_aliases={} if across is None else {2: 0},
-        compiler_params=pltpu.CompilerParams(vmem_limit_bytes=8 * MIB),
+        compiler_params=pltpu.CompilerParams(vmem_limit_bytes=4 * MIB),
         cost_estimate=LIGHT,
         name="turn",
     )(place, coupled, *(() if across is None else (across,)))
 
 
-def multiply_kernel(place_ref, left_ref, right_ref, out_ref):
+def multiply_kernel(first, count, lefts, place_ref, *refs):
+    left_refs, right_ref, out_ref = refs[:lefts], refs[lefts], refs[-1]
+    width = right_ref.shape[0] // 4
+
     @pl.when(place_ref[1] == 1)
     def _():
-        out_ref[...] = jnp.dot(
-            left_ref[...], right_ref[...], preferred_element_type=F32
-        ).astype(BF16)
-
-
-def multiply(place, left, right, first=lambda odd: 0, count=4):
-    rows, nodes = left.shape
-    width = nodes // 4
-    return pl.pallas_call(
-        multiply_kernel,
+        def block(step, carry):
+            source = pl.multiple_of((first(place_ref[0]) + step) * width, 128)
+            target = pl.multiple_of(step * width, 128)
+            row = 0
+            for left_ref in left_refs:
+                rows = left_ref.shape[0]
+                out_ref[row : row + rows, pl.ds(target, width)] = jnp.dot(
+                    left_ref[...], right_ref[:, pl.ds(source, width)], preferred_element_type=F32
+                ).astype(BF16)
+                row += rows
+            return carry
+
+        lax.fori_loop(0, count, block, 0)
+
+
+def multiply(place, lefts, right, first=lambda odd: 0, count=4):
+    rows = sum(left.shape[0] for left in lefts)
+    width = right.shape[0] // 4
+    vmem = pl.BlockSpec(memory_space=pltpu.VMEM)
+    return pl.pallas_call(
+        functools.partial(multiply_kernel, first, count, len(lefts)),
         out_shape=jax.ShapeDtypeStruct((rows, count * width), BF16),
-        grid_spec=pltpu.PrefetchScalarGridSpec(
-            num_scalar_prefetch=1,
-            grid=(count,),
-            in_specs=[
-                pl.BlockSpec((rows, nodes), lambda n, place: (0, 0)),
-                pl.BlockSpec((nodes, width), lambda n, place: (0, first(place[0]) + n)),
-            ],
-            out_specs=pl.BlockSpec((rows, width), lambda n, place: (0, n)),
-        ),
-        compiler_params=pltpu.CompilerParams(vmem_limit_bytes=16 * MIB),
+        in_specs=[pl.BlockSpec(memory_space=pltpu.SMEM)] + [vmem] * (len(lefts) + 1),
+        out_specs=vmem,
+        compiler_params=pltpu.CompilerParams(vmem_limit_bytes=6 * MIB),
         cost_estimate=LIGHT,
         name="multiply",
-    )(place, left, right)
+    )(place, *lefts, right)
+
+
+def zero_kernel(place_ref, left_ref, right_ref, two_ref, out_ref):
+    odd = place_ref[0]
+    width = right_ref.shape[0] // 4
+    multiply_kernel(lambda odd: 2 * odd, 2, 1, place_ref, left_ref, right_ref, out_ref)
+
+    @pl.when(place_ref[1] == 1)
+    def _():
+        out_ref[:, 2 * width :] = two_ref[:, pl.ds(pl.multiple_of(2 * odd * width, 128), width)]
+
+
+def product_zero(place, half, across, two):
+    rows = half.shape[0]
+    width = across.shape[0] // 4
+    vmem = pl.BlockSpec(memory_space=pltpu.VMEM)
+    return pl.pallas_call(
+        zero_kernel,
+        out_shape=jax.ShapeDtypeStruct((rows, 3 * width), BF16),
+        in_specs=[pl.BlockSpec(memory_space=pltpu.SMEM)] + [vmem] * 3,
+        out_specs=vmem,
+        compiler_params=pltpu.CompilerParams(vmem_limit_bytes=6 * MIB),
+        cost_estimate=LIGHT,
+        name="product_zero",
+    )(place, half, across, two)
 
 
 def prior_kernel(step_ref, shifted_ref, sigma_ref, out_ref):
@@ -234,7 +268,7 @@
             ],
             out_specs=(spec(4), spec(3), spec(2), spec(1)),
         ),
-        compiler_params=pltpu.CompilerParams(vmem_limit_bytes=12 * MIB),
+        compiler_params=pltpu.CompilerParams(vmem_limit_bytes=8 * MIB),
         cost_estimate=LIGHT,
         name="prior_parts",
     )(place, step, shifted, sigma)
@@ -273,14 +307,17 @@
         out_shape=jax.ShapeDtypeStruct((nodes, nodes), BF16),
         in_specs=[pl.BlockSpec(memory_space=pltpu.SMEM)] + [vmem] * 4,
         out_specs=vmem,
-        compiler_params=pltpu.CompilerParams(vmem_limit_bytes=20 * MIB),
+        compiler_params=pltpu.CompilerParams(vmem_limit_bytes=6 * MIB),
         cost_estimate=LIGHT,
         name="assemble",
     )(place, *parts)
 
 
 def final_kernel(
-    place_ref, active_ref, pivot_ref, q0, q0_last, q1, q2, q2_last, q3_near, q3_other, sigma_ref, out_ref, var_ref
+    place_ref, active_ref, pivot_ref, sigma_ref,
+    q0, q0_two, q0_last, q2, q2_last, q3_near, q3_other,
+    q01, q11, q21, q31,
+    out_ref, var_ref,
 ):
     rows, nodes = pivot_ref.shape
     width = nodes // 4
@@ -312,19 +349,23 @@
 
     @pl.when(active & (place == 0))
     def _():
-        add(at(odd, 3), q0[...])
-        add(at(3 - 3 * odd), q0_last[...])
-        trace(q0[:, own(2 * odd)])
+        add(at(2 * odd, 2), q0[...])
+        add(at(turned(3, odd)), q0_last[:, pl.ds(here, rows)].T)
+        add(at(turned(2, odd)), q0_two[:, pl.ds(here, rows)].T)
+        trace(q0[:, own(odd)])
 
     @pl.when(active & (place == 1))
     def _():
-        add(slice(None), q1[...])
-        trace(q1[:, own(place_ref[2])])
+        add(at(turned(0, odd)), q01[...].T)
+        add(at(turned(1, odd)), q11[...])
+        add(at(turned(2, odd)), q21[...].T)
+        add(at(turned(3, odd)), q31[...].T)
+        trace(q11[:, pl.ds(here, rows)])
 
     @pl.when(active & (place == 2))
     def _():
         add(at(odd, 3), q2[...])
-        add(at(3 - 3 * odd), q2_last[:, pl.ds(here, rows)].T)
+        add(at(turned(3, odd)), q2_last[:, pl.ds(here, rows)].T)
         trace(q2[:, own(2 - 2 * odd)])
 
     @pl.when(active & (place == 3))
@@ -339,7 +380,7 @@
         var_ref[...] = diagonal(sigma_ref[:, own(place_ref[2])].astype(F32))
 
 
-def final(place, active, pivot, products, sigma):
+def final(place, active, pivot, sigma, received, kept):
     rows, nodes = pivot.shape
     chunk = 128
     width = nodes // 4
@@ -349,6 +390,16 @@
             (chunk, blocks * width), lambda i, place, active: (jnp.where(place[1] == which, i, 0), 0)
         )
 
+    def turned_block(start):
+        return pl.BlockSpec(
+            (rows, chunk),
+            lambda i, place, active: (
+                0,
+                jnp.where(place[1] == 1, start(place[0]) * (width // chunk) + i, 0),
+            ),
+        )
+
+    whole = pl.BlockSpec((rows, width), lambda i, place, active: (0, 0))
     return pl.pallas_call(
         final_kernel,
         out_shape=(
@@ -360,26 +411,30 @@
             grid=(rows // chunk,),
             in_specs=[
                 pl.BlockSpec((chunk, nodes), lambda i, place, active: (i, 0)),
-                picked(0, 3),
-                picked(0, 1),
-                picked(1, 4),
-                picked(2, 3),
-                pl.BlockSpec((rows, width), lambda i, place, active: (0, 0)),
-                picked(3, 2),
-                picked(3, 2),
                 pl.BlockSpec(
                     (chunk, nodes), lambda i, place, active: (jnp.where(active[0] == 0, i, 0), 0)
                 ),
+                picked(0, 2),
+                pl.BlockSpec((rows, width), lambda i, place, active: (0, 2)),
+                whole,
+                picked(2, 3),
+                whole,
+                picked(3, 2),
+                picked(3, 2),
+                turned_block(lambda odd: 1 - odd),
+                picked(1, 1),
+                turned_block(lambda odd: 1),
+                turned_block(lambda odd: 1 - odd),
             ],
             out_specs=(
                 pl.BlockSpec((chunk, nodes), lambda i, place, active: (i, 0)),
                 pl.BlockSpec((1, chunk), lambda i, place, active: (0, i)),
             ),
         ),
-        compiler_params=pltpu.CompilerParams(vmem_limit_bytes=16 * MIB),
+        compiler_params=pltpu.CompilerParams(vmem_limit_bytes=12 * MIB),
         cost_estimate=LIGHT,
         name="final",
-    )(place, active, pivot, *products, sigma)
+    )(place, active, pivot, sigma, *received, *kept)
 
 
 def owned(sigma_next, separator, inverse_pivot, coupling_rate, lengths, step_index, node_class):
@@ -388,47 +443,47 @@
     col = lax.axis_index("col")
     place = jnp.stack([odd, turned(col, odd), col]).astype(jnp.int32)
     active = (step_index < lengths).astype(jnp.int32)
-    width = pivot.shape[1] // 4
-
+    rows, width = pivot.shape[0], pivot.shape[1] // 4
+    after = lambda value, *others: lax.optimization_barrier((value, *others))[0]
 
     shifted = passed_along(separator, "dom", -1)[0]
     p2 = moved(pivot, 2, 1)
     p0 = moved(pivot, 0, 1)
     c1 = couple(pivot, node_class, coupling_rate)
-    across = turn(place, 1, c1, None)
-
-    shifted = lax.optimization_barrier((shifted, p2, p0, across))[0]
-    row, far, near, last = prior_parts(place, step_index, shifted, sigma)
-    far_zero, near_two, last_three = moved(far, 0, 1), moved(near, 2, 1), moved(last, 3, 1)
-
-    p2 = lax.optimization_barrier((p2, last))[0]
-    c2 = couple_here(place, p2, node_class, coupling_rate)
-    across = turn(place, 2, c2, across)
-    c0 = couple_here(place, p0, node_class, coupling_rate)
-    across = turn(place, 0, c0, across)
-    c3 = lax.optimization_barrier((c1, last_three, near_two, far_zero, across))[0]
-    c3 = moved(c3, 3, 1)
+    c3a = moved(c1[: rows // 2], 3, 1)
+    across = turn(place, 1, 0, c1, None)
+
+    row, far, near, last = prior_parts(place, step_index, after(shifted, across), sigma)
+    far_zero, near_two, last_three = moved(far, 0, 1), moved(near, 2, 1), moved(after(last, p2, p0), 3, 1)
+
+    c2 = couple_here(place, after(p2, last), node_class, coupling_rate)
+    across = turn(place, 2, 0, c2, across)
+    c0 = couple_here(place, after(p0, c3a, across), node_class, coupling_rate)
+    across = turn(place, 0, 0, c0, across)
+    c3b = moved(after(c1[rows // 2 :], last_three, across), 3, 1)
     prior = assemble(place, row, near_two, last_three, far_zero)
-    most = lambda odd: odd
-    rest = lambda odd: 3 - 3 * odd
-    h2 = multiply(place, c2, prior)
-    q2 = multiply(place, h2, across, most, 3)
-    h0 = multiply(place, lax.optimization_barrier((c0, q2))[0], prior)
-    q2 = moved(q2, 1, 2)
-    q0 = moved(multiply(place, h0, across, most, 3), 1, 0)
-
-    across = turn(place, 3, c3, across)
-    h3 = multiply(place, c3, prior)
-    q3_near = moved(multiply(place, h3, across, lambda odd: 2 - 2 * odd, 2), 1, 3)
-    q3_other = multiply(place, h3, across, lambda odd: 2 * odd, 2)
-    q0_last = multiply(place, h0, across, rest, 1)
-    h1 = multiply(place, lax.optimization_barrier((c1, q2, q3_other, q0_last))[0], prior)
-    q3_other, q0_last = moved(q3_other, 1, 3), moved(q0_last, 1, 0)
-    q1 = multiply(place, h1, across)
-    q2_last = lax.optimization_barrier((q3_near, q0, q1))[0]
+
+    h2 = multiply(place, [c2], prior)
+    q2_own = multiply(place, [h2], across, lambda odd: odd, 3)
+    q2 = moved(q2_own, 1, 2)
+    h0 = multiply(place, [after(c0, q2_own)], prior)
+    q0_own = product_zero(place, h0, across, q2_own)
+    q0 = moved(q0_own, 1, 0)
+
+    across = turn(place, 3, 0, c3a, across)
+    across = turn(place, 3, 1, c3b, across)
+    h3 = multiply(place, [c3a, c3b], prior)
+    q3_near = moved(multiply(place, [h3], across, lambda odd: 2 - 2 * odd, 2), 1, 3)
+    q3_own = multiply(place, [h3], across, lambda odd: 2 * odd, 2)
+    q3_other = moved(q3_own, 1, 3)
+    q0_last = moved(lax.dynamic_slice_in_dim(q3_own, odd * width, width, 1), 1, 0)
+    h1 = multiply(place, [after(c1, q2, q3_own)], prior)
+    q11 = multiply(place, [h1], across, lambda odd: 1 + odd, 1)
+    q2_last = after(q3_near, q0, q11)
     q2_last = moved(lax.dynamic_slice_in_dim(q2_last, odd * width, width, 1), 3, 2)
-    products = (q0, q0_last, q1, q2, q2_last, q3_near, q3_other)
-    covariance, variances = final(place, active, pivot, products, sigma)
+    received = (q0, q0, q0_last, q2, q2_last, q3_near, q3_other)
+    kept = (q0_own, q11, q2_own, q3_own)
+    covariance, variances = final(place, active, pivot, sigma, received, kept)
     return (covariance[None], variances)
 
 

time: 148 us -> 148 us (level)
  waiting for transfers between devices: 70.1 us -> 76.6 us
  Pallas kernels: 40.1 us -> 34.6 us
  starting transfers between devices: 23.5 us -> 21.9 us
    pallas_call x10 -> x9, Pallas kernels: 17.5 us -> 9.99 us  [the longest x8 7.39 us: multiply(): pl.pallas_call(functools.partial(multiply_kernel, first, count, len(lefts...]
    ppermute x12 -> x13, waiting for transfers between devices: 70.1 us -> 76.6 us  [moved(): lax.ppermute(value, ('dom', 'col'), route(source, target, lax.axis_size('...]
    unnamed x28 -> x22, local copies, waits for them, and re-layouts: 10.7 us -> 8.87 us
    ppermute x12 -> x13, starting transfers between devices: 22.2 us -> 20.6 us  [moved(): lax.ppermute(value, ('dom', 'col'), route(source, target, lax.axis_size('...]
    pallas_call x4 -> x5, Pallas kernels: 4.85 us -> 5.42 us  [turn(): pl.pallas_call(turn_kernel, out_shape=jax.ShapeDtypeStruct((nodes, nodes)...]
  transfers between devices with their start and end apart: 13 -> 14, of which waited for: 4 -> 4; matrix products, arithmetic and copies ran while one was open for 0% -> 2% of each run, Pallas kernels for 23% -> 20%
where the time goes in v4:
time: 148 us
  waiting for transfers between devices  76.6 us (52%)
  Pallas kernels  34.6 us (23%)
  starting transfers between devices  21.9 us (15%)
  local copies, waits for them, and re-layouts  11.4 us (8%)
  between operations  2.93 us (2%)
    ppermute x13, waiting for transfers between devices, moved(): lax.ppermute(value, ('dom', 'col'), route(source, target, lax.axis_size('...  76.6 us
    ppermute x13, starting transfers between devices, moved(): lax.ppermute(value, ('dom', 'col'), route(source, target, lax.axis_size('...  20.6 us
    unnamed x22, local copies, waits for them, and re-layouts  8.87 us
    pallas_call x8, Pallas kernels, multiply(): pl.pallas_call(functools.partial(multiply_kernel, first, count, len(lefts...  7.39 us
    pallas_call x2, Pallas kernels, couple_here(): pl.pallas_call(kernel, out_shape=jax.ShapeDtypeStruct((rows, nodes), BF16...  5.65 us
    pallas_call x5, Pallas kernels, turn(): pl.pallas_call(turn_kernel, out_shape=jax.ShapeDtypeStruct((nodes, nodes)...  5.42 us
    pallas_call x1, Pallas kernels, final(): pl.pallas_call(final_kernel, out_shape=(jax.ShapeDtypeStruct((rows, nodes...  5.24 us
    pallas_call x1, Pallas kernels, couple(): pl.pallas_call(couple_kernel, out_shape=jax.ShapeDtypeStruct((rows, nodes...  4.74 us
  transfers between devices with their start and end apart: 14, of which 4 were waited for; matrix products, arithmetic and copies ran while one was open for 2% of the time, Pallas kernels for 20%

profile of v4, /device:TPU:0, one launch (start us, length us, event | category | flops | bytes accessed | tf_op | source)
XLA Modules:
  0.0 147.6 jit_solution(6674702330457204464)
XLA Ops:
  0.6 1.3 collective-permute-start.3
  1.9 2.0 %collective-permute-start.2 = (bf16[512,2048]{1,0:T(8,128)(2,1)}, bf16[512,2048]{1,0:T(8,128)(2,1)}, u32[]{:S(2)}, u32[]{:S(2)}) collective-permute-start(bf16[512,2048]{1,0:T(8,128)(2,1)} %bitcast.10), channel_id=1, source_target_pairs={{2,1},{5,6},{10,9},{13,14},{18,17},{21,22},{26,25},{29,30}} | collective-permute-start | bytes 6291464 | tf_op jit(solution)/shard_map/ppermute | solution.py:100
  4.0 5.5 %collective-permute-start = (bf16[512,2048]{1,0:T(8,128)(2,1)}, bf16[512,2048]{1,0:T(8,128)(2,1)}, u32[]{:S(2)}, u32[]{:S(2)}) collective-permute-start(bf16[512,2048]{1,0:T(8,128)(2,1)} %bitcast.11), channel_id=1, source_target_pairs={{0,1},{7,6},{8,9},{15,14},{16,17},{23,22},{24,25},{31,30}} | collective-permute-start | bytes 6291464 | tf_op jit(solution)/shard_map/ppermute | solution.py:100
  10.2 1.6 %copy-done.6 = bf16[1,512,2048]{2,1,0:T(8,128)(2,1)S(1)} copy-done((bf16[1,512,2048]{2,1,0:T(8,128)(2,1)S(1)}, bf16[1,512,2048]{2,1,0:T(8,128)(2,1)}, u32[]{:S(2)}) %copy-start.6) | copy-done | bytes 2097176
  12.4 4.7 %couple.1.coupled_ref.refs_0_ = bf16[512,2048]{1,0:T(8,128)(2,1)S(1)} custom-call(f32[1]{0:T(128)S(6)} %copy.17.rate_ref.refs_0_, s32[1,2048]{1,0:T(1,128)S(1)} %bitcast.14, bf16[512,2048]{1,0:T(8,128)(2,1)S(1)} %bitcast.12), custom_call_target="tpu_custom_call" | custom-call | flops 1048576 | bytes 65536 | tf_op jit(solution)/shard_map/couple/pallas_call | solution.py:70
  17.2 1.4 fusion
  21.7 3.0 %prior_parts.1 = (bf16[512,2048]{1,0:T(8,128)(2,1)S(1)}, bf16[512,1536]{1,0:T(8,128)(2,1)S(1)}, bf16[512,1024]{1,0:T(8,128)(2,1)S(1)}, bf16[512,512]{1,0:T(8,128)(2,1)S(1)}) custom-call(s32[3]{0:T(128)S(1)} %pad_add_fusion.place_ref, s32[1]{0:T(128)S(6)} %copy.19.step_ref, bf16[512,2048]{1,0:T(8,128)(2,1)} %bitcast.6.shifted_ref, bf16[512,2048]{1,0:T(8,128)(2,1)S(1)} %bitcast.8), custom_call_target="tpu_custom_call" | custom-call | flops 1048576 | bytes 65536 | tf_op jit(solution)/shard_map/prior_parts/pallas_call | solution.py:255
  24.8 1.4 collective-permute-start.6
  26.9 15.9 %collective-permute-done.refs_2_ = bf16[512,2048]{1,0:T(8,128)(2,1)} collective-permute-done((bf16[512,2048]{1,0:T(8,128)(2,1)}, bf16[512,2048]{1,0:T(8,128)(2,1)}, u32[]{:S(2)}, u32[]{:S(2)}) %collective-permute-start) | collective-permute-done | bytes 2097184 | tf_op jit(solution)/shard_map/ppermute | solution.py:100
  43.5 2.8 %couple_here.2.coupled_ref.refs_0_ = bf16[512,2048]{1,0:T(8,128)(2,1)S(1)} custom-call(s32[3]{0:T(128)S(1)} %pad_add_fusion.place_ref, f32[1]{0:T(128)S(6)} %copy.17.rate_ref.refs_0_, s32[1,2048]{1,0:T(1,128)S(1)} %bitcast.15, bf16[512,2048]{1,0:T(8,128)(2,1)} %collective-permute-done.2.refs_2_), custom_call_target="tpu_custom_call" | custom-call | flops 1048576 | bytes 65536 | tf_op jit(solution)/shard_map/couple_here/pallas_call | solution.py:112
  47.6 2.8 %couple_here.3.coupled_ref.refs_0_ = bf16[512,2048]{1,0:T(8,128)(2,1)S(1)} custom-call(s32[3]{0:T(128)S(1)} %pad_add_fusion.place_ref, f32[1]{0:T(128)S(6)} %copy.17.rate_ref.refs_0_, s32[1,2048]{1,0:T(1,128)S(1)} %bitcast.16, bf16[512,2048]{1,0:T(8,128)(2,1)} %collective-permute-done.refs_2_), custom_call_target="tpu_custom_call" | custom-call | flops 1048576 | bytes 65536 | tf_op jit(solution)/shard_map/couple_here/pallas_call | solution.py:112
  52.4 13.2 %collective-permute-done.6.far_zero = bf16[512,1536]{1,0:T(8,128)(2,1)S(1)} collective-permute-done((bf16[512,1536]{1,0:T(8,128)(2,1)S(1)}, bf16[512,1536]{1,0:T(8,128)(2,1)S(1)}, u32[]{:S(2)}, u32[]{:S(2)}) %collective-permute-start.6) | collective-permute-done | bytes 1572896 | tf_op jit(solution)/shard_map/ppermute | solution.py:100
  66.7 2.2 %multiply.9.two_ref.q21 = bf16[512,1536]{1,0:T(8,128)(2,1)} custom-call(s32[3]{0:T(128)S(1)} %pad_add_fusion.place_ref, bf16[512,2048]{1,0:T(8,128)(2,1)S(1)} %multiply.8.refs_0_, bf16[2048,2048]{1,0:T(8,128)(2,1)S(1)} %turn.7.refs_1_.right_ref.refs_0_), custom_call_target="tpu_custom_call" | custom-call | flops 1048576 | bytes 65536 | tf_op jit(solution)/shard_map/multiply/pallas_call | solution.py:188
  68.9 1.9 %collective-permute-start.10 = (bf16[512,1536]{1,0:T(8,128)(2,1)}, bf16[512,1536]{1,0:T(8,128)(2,1)}, u32[]{:S(2)}, u32[]{:S(2)}) collective-permute-start(bf16[512,1536]{1,0:T(8,128)(2,1)} %multiply.9.two_ref.q21), channel_id=1, source_target_pairs={{1,2},{6,5},{9,10},{14,13},{17,18},{22,21},{25,26},{30,29}} | collective-permute-start | bytes 4718600 | tf_op jit(solution)/shard_map/ppermute | solution.py:100
  71.3 2.6 %product_zero.1.q01 = bf16[512,1536]{1,0:T(8,128)(2,1)} custom-call(s32[3]{0:T(128)S(1)} %pad_add_fusion.place_ref, bf16[512,2048]{1,0:T(8,128)(2,1)S(1)} %multiply.10.left_ref, bf16[2048,2048]{1,0:T(8,128)(2,1)S(1)} %turn.7.refs_1_.right_ref.refs_0_, bf16[512,1536]{1,0:T(8,128)(2,1)} %multiply.9.two_ref.q21), custom_call_target="tpu_custom_call" | custom-call | flops 1048576 | bytes 65536 | tf_op jit(solution)/shard_map/product_zero/pallas_call | solution.py:213
  77.6 1.9 %multiply.13 = bf16[512,1024]{1,0:T(8,128)(2,1)} custom-call(s32[3]{0:T(128)S(1)} %pad_add_fusion.place_ref, bf16[512,2048]{1,0:T(8,128)(2,1)S(1)} %multiply.11.refs_0_, bf16[2048,2048]{1,0:T(8,128)(2,1)S(1)} %turn.9.refs_1_), custom_call_target="tpu_custom_call" | custom-call | flops 1048576 | bytes 65536 | tf_op jit(solution)/shard_map/multiply/pallas_call | solution.py:188
  79.5 1.9 %collective-permute-start.11 = (bf16[512,1024]{1,0:T(8,128)(2,1)}, bf16[512,1024]{1,0:T(8,128)(2,1)}, u32[]{:S(2)}, u32[]{:S(2)}) collective-permute-start(bf16[512,1024]{1,0:T(8,128)(2,1)} %multiply.13), channel_id=1, source_target_pairs={{1,3},{6,4},{9,11},{14,12},{17,19},{22,20},{25,27},{30,28}} | collective-permute-start | bytes 3145736 | tf_op jit(solution)/shard_map/ppermute | solution.py:100
  82.0 1.7 %collective-permute-start.13 = (bf16[512,1024]{1,0:T(8,128)(2,1)S(1)}, bf16[512,1024]{1,0:T(8,128)(2,1)}, u32[]{:S(2)}, u32[]{:S(2)}) collective-permute-start(bf16[512,1024]{1,0:T(8,128)(2,1)S(1)} %multiply.12.q31), channel_id=1, source_target_pairs={{1,3},{6,4},{9,11},{14,12},{17,19},{22,20},{25,27},{30,28}} | collective-permute-start | bytes 3145736 | tf_op jit(solution)/shard_map/ppermute | solution.py:100
  83.8 1.3 collective-permute-start.9
  85.1 3.4 %copy-done.3 = bf16[2048,2048]{1,0:T(8,128)(2,1)S(1)} copy-done((bf16[2048,2048]{1,0:T(8,128)(2,1)S(1)}, bf16[2048,2048]{1,0:T(8,128)(2,1)}, u32[]{:S(2)}) %copy-start.3) | copy-done | bytes 8388632
  89.0 2.8 %copy-done.1 = bf16[2048,2048]{1,0:T(8,128)(2,1)S(1)} copy-done((bf16[2048,2048]{1,0:T(8,128)(2,1)S(1)}, bf16[2048,2048]{1,0:T(8,128)(2,1)}, u32[]{:S(2)}) %copy-start.1) | copy-done | bytes 8388632
  92.4 44.4 %collective-permute-done.7.q0.q0_two = bf16[512,1536]{1,0:T(8,128)(2,1)} collective-permute-done((bf16[512,1536]{1,0:T(8,128)(2,1)}, bf16[512,1536]{1,0:T(8,128)(2,1)}, u32[]{:S(2)}, u32[]{:S(2)}) %collective-permute-start.7) | collective-permute-done | bytes 1572896 | tf_op jit(solution)/shard_map/ppermute | solution.py:100
  139.2 3.1 %collective-permute-done.9.q0_last = bf16[512,512]{1,0:T(8,128)(2,1)S(1)} collective-permute-done((bf16[512,512]{1,0:T(8,128)(2,1)S(1)}, bf16[512,512]{1,0:T(8,128)(2,1)S(1)}, u32[]{:S(2)}, u32[]{:S(2)}) %collective-permute-start.9) | collective-permute-done | bytes 524320 | tf_op jit(solution)/shard_map/ppermute | solution.py:100
  142.3 5.2 %final.1 = (bf16[512,2048]{1,0:T(8,128)(2,1)}, f32[1,512]{1,0:T(1,128)}) custom-call(s32[3]{0:T(128)S(1)} %pad_add_fusion.place_ref, s32[1]{0:T(128)S(6)} %convert_element_type.3.active_ref, bf16[512,2048]{1,0:T(8,128)(2,1)S(1)} %bitcast.13, bf16[512,2048]{1,0:T(8,128)(2,1)S(1)} %bitcast.9, bf16[512,1536]{1,0:T(8,128)(2,1)} %collective-permute-done.7.q0.q0_two, ...), custom_call_target="tpu_custom_call" | custom-call | flops 1048576 | bytes 65536 | tf_op jit(solution)/shard_map/final/pallas_call | solution.py:403
  (50 shorter events, 16.4 us)
Async XLA Ops:
  0.6 20.7 %collective-permute-start.3 = (bf16[1,512,2048]{2,1,0:T(8,128)(2,1)}, bf16[1,512,2048]{2,1,0:T(8,128)(2,1)}, u32[]{:S(2)}, u32[]{:S(2)}) collective-permute-start(bf16[1,512,2048]{2,1,0:T(8,128)(2,1)} %param.8), channel_id=1, source_target_pairs={{4,0},{8,4},{12,8},{5,1},{9,5},{13,9},{6,2},{10,6},{14,10},{7,3},{... | collective-permute-start | bytes 6291464 | tf_op jit(solution)/shard_map/ppermute | solution.py:20
  1.9 25.0 %collective-permute-start.2 = (bf16[512,2048]{1,0:T(8,128)(2,1)}, bf16[512,2048]{1,0:T(8,128)(2,1)}, u32[]{:S(2)}, u32[]{:S(2)}) collective-permute-start(bf16[512,2048]{1,0:T(8,128)(2,1)} %bitcast.10), channel_id=1, source_target_pairs={{2,1},{5,6},{10,9},{13,14},{18,17},{21,22},{26,25},{29,30}} | collective-permute-start | bytes 6291464 | tf_op jit(solution)/shard_map/ppermute | solution.py:100
  4.0 38.9 %collective-permute-start = (bf16[512,2048]{1,0:T(8,128)(2,1)}, bf16[512,2048]{1,0:T(8,128)(2,1)}, u32[]{:S(2)}, u32[]{:S(2)}) collective-permute-start(bf16[512,2048]{1,0:T(8,128)(2,1)} %bitcast.11), channel_id=1, source_target_pairs={{0,1},{7,6},{8,9},{15,14},{16,17},{23,22},{24,25},{31,30}} | collective-permute-start | bytes 6291464 | tf_op jit(solution)/shard_map/ppermute | solution.py:100
  10.2 1.6 %copy-start.6 = (bf16[1,512,2048]{2,1,0:T(8,128)(2,1)S(1)}, bf16[1,512,2048]{2,1,0:T(8,128)(2,1)}, u32[]{:S(2)}) copy-start(bf16[1,512,2048]{2,1,0:T(8,128)(2,1)} %param.9) | copy-start | bytes 6291460
  18.6 28.9 %collective-permute-start.1 = (bf16[256,2048]{1,0:T(8,128)(2,1)}, bf16[256,2048]{1,0:T(8,128)(2,1)S(1)}, u32[]{:S(2)}, u32[]{:S(2)}) collective-permute-start(bf16[256,2048]{1,0:T(8,128)(2,1)} %get-tuple-element.31), channel_id=1, source_target_pairs={{3,1},{4,6},{11,9},{12,14},{19,17},{20,22},{27,25},{28,30}} | collective-permute-start | bytes 3145736 | tf_op jit(solution)/shard_map/ppermute | solution.py:100
  20.1 1.6 %copy-start.4 = (bf16[1,512,2048]{2,1,0:T(8,128)(2,1)S(1)}, bf16[1,512,2048]{2,1,0:T(8,128)(2,1)}, u32[]{:S(2)}) copy-start(bf16[1,512,2048]{2,1,0:T(8,128)(2,1)} %param.7) | copy-start | bytes 6291460
  21.7 21.8 %copy-start.9 = (s32[2048]{0:T(1024)S(1)}, s32[2048]{0:T(1024)}, u32[]{:S(2)}) copy-start(s32[2048]{0:T(1024)} %param.13) | copy-start | bytes 24580
  24.8 40.9 %collective-permute-start.6 = (bf16[512,1536]{1,0:T(8,128)(2,1)S(1)}, bf16[512,1536]{1,0:T(8,128)(2,1)S(1)}, u32[]{:S(2)}, u32[]{:S(2)}) collective-permute-start(bf16[512,1536]{1,0:T(8,128)(2,1)S(1)} %get-tuple-element.23), channel_id=1, source_target_pairs={{0,1},{7,6},{8,9},{15,14},{16,17},{23,22},{24,25},{31,30}} | collective-permute-start | bytes 4718600 | tf_op jit(solution)/shard_map/ppermute | solution.py:100
  26.2 26.2 %collective-permute-start.4 = (bf16[512,1024]{1,0:T(8,128)(2,1)S(1)}, bf16[512,1024]{1,0:T(8,128)(2,1)S(1)}, u32[]{:S(2)}, u32[]{:S(2)}) collective-permute-start(bf16[512,1024]{1,0:T(8,128)(2,1)S(1)} %get-tuple-element.21), channel_id=1, source_target_pairs={{2,1},{5,6},{10,9},{13,14},{18,17},{21,22},{26,25},{29,30}} | collective-permute-start | bytes 3145736 | tf_op jit(solution)/shard_map/ppermute | solution.py:100
  42.8 8.8 %collective-permute-start.5 = (bf16[512,512]{1,0:T(8,128)(2,1)S(1)}, bf16[512,512]{1,0:T(8,128)(2,1)S(1)}, u32[]{:S(2)}, u32[]{:S(2)}) collective-permute-start(bf16[512,512]{1,0:T(8,128)(2,1)S(1)} %get-tuple-element.22), channel_id=1, source_target_pairs={{3,1},{4,6},{11,9},{12,14},{19,17},{20,22},{27,25},{28,30}} | collective-permute-start | bytes 1572872 | tf_op jit(solution)/shard_map/ppermute | solution.py:100
  50.4 1.2 copy-start.10
  51.7 24.4 %collective-permute-start.8 = (bf16[256,2048]{1,0:T(8,128)(2,1)S(1)}, bf16[256,2048]{1,0:T(8,128)(2,1)S(1)}, u32[]{:S(2)}, u32[]{:S(2)}) collective-permute-start(bf16[256,2048]{1,0:T(8,128)(2,1)S(1)} %copy-done.10), channel_id=1, source_target_pairs={{3,1},{4,6},{11,9},{12,14},{19,17},{20,22},{27,25},{28,30}} | collective-permute-start | bytes 3145736 | tf_op jit(solution)/shard_map/ppermute | solution.py:100
  66.2 9.9 %copy-start.2 = (bf16[2048,2048]{1,0:T(8,128)(2,1)}, bf16[2048,2048]{1,0:T(8,128)(2,1)S(1)}, u32[]{:S(2)}) copy-start(bf16[2048,2048]{1,0:T(8,128)(2,1)S(1)} %assemble.1.refs_1_.refs_2_) | copy-start | bytes 25165828
  68.9 16.2 %collective-permute-start.10 = (bf16[512,1536]{1,0:T(8,128)(2,1)}, bf16[512,1536]{1,0:T(8,128)(2,1)}, u32[]{:S(2)}, u32[]{:S(2)}) collective-permute-start(bf16[512,1536]{1,0:T(8,128)(2,1)} %multiply.9.two_ref.q21), channel_id=1, source_target_pairs={{1,2},{6,5},{9,10},{14,13},{17,18},{22,21},{25,26},{30,29}} | collective-permute-start | bytes 4718600 | tf_op jit(solution)/shard_map/ppermute | solution.py:100
  73.9 62.9 %collective-permute-start.7 = (bf16[512,1536]{1,0:T(8,128)(2,1)}, bf16[512,1536]{1,0:T(8,128)(2,1)}, u32[]{:S(2)}, u32[]{:S(2)}) collective-permute-start(bf16[512,1536]{1,0:T(8,128)(2,1)} %product_zero.1.q01), channel_id=1, source_target_pairs={{1,0},{6,7},{9,8},{14,15},{17,16},{22,23},{25,24},{30,31}} | collective-permute-start | bytes 4718600 | tf_op jit(solution)/shard_map/ppermute | solution.py:100
  77.6 3.9 %copy-start = (bf16[2048,2048]{1,0:T(8,128)(2,1)}, bf16[2048,2048]{1,0:T(8,128)(2,1)S(1)}, u32[]{:S(2)}) copy-start(bf16[2048,2048]{1,0:T(8,128)(2,1)S(1)} %turn.9.refs_1_) | copy-start | bytes 25165828
  79.5 12.9 %collective-permute-start.11 = (bf16[512,1024]{1,0:T(8,128)(2,1)}, bf16[512,1024]{1,0:T(8,128)(2,1)}, u32[]{:S(2)}, u32[]{:S(2)}) collective-permute-start(bf16[512,1024]{1,0:T(8,128)(2,1)} %multiply.13), channel_id=1, source_target_pairs={{1,3},{6,4},{9,11},{14,12},{17,19},{22,20},{25,27},{30,28}} | collective-permute-start | bytes 3145736 | tf_op jit(solution)/shard_map/ppermute | solution.py:100
  82.0 60.3 %collective-permute-start.13 = (bf16[512,1024]{1,0:T(8,128)(2,1)S(1)}, bf16[512,1024]{1,0:T(8,128)(2,1)}, u32[]{:S(2)}, u32[]{:S(2)}) collective-permute-start(bf16[512,1024]{1,0:T(8,128)(2,1)S(1)} %multiply.12.q31), channel_id=1, source_target_pairs={{1,3},{6,4},{9,11},{14,12},{17,19},{22,20},{25,27},{30,28}} | collective-permute-start | bytes 3145736 | tf_op jit(solution)/shard_map/ppermute | solution.py:100
  83.8 58.5 %collective-permute-start.9 = (bf16[512,512]{1,0:T(8,128)(2,1)S(1)}, bf16[512,512]{1,0:T(8,128)(2,1)S(1)}, u32[]{:S(2)}, u32[]{:S(2)}) collective-permute-start(bf16[512,512]{1,0:T(8,128)(2,1)S(1)} %constant_dynamic-slice_fusion.1), channel_id=1, source_target_pairs={{1,0},{6,7},{9,8},{14,15},{17,16},{22,23},{25,24},{30,31}} | collective-permute-start | bytes 1572872 | tf_op jit(solution)/shard_map/ppermute | solution.py:100
  85.1 3.4 %copy-start.3 = (bf16[2048,2048]{1,0:T(8,128)(2,1)S(1)}, bf16[2048,2048]{1,0:T(8,128)(2,1)}, u32[]{:S(2)}) copy-start(bf16[2048,2048]{1,0:T(8,128)(2,1)} %copy-done.2) | copy-start | bytes 25165828
  88.5 3.4 %copy-start.1 = (bf16[2048,2048]{1,0:T(8,128)(2,1)S(1)}, bf16[2048,2048]{1,0:T(8,128)(2,1)}, u32[]{:S(2)}) copy-start(bf16[2048,2048]{1,0:T(8,128)(2,1)} %copy-done) | copy-start | bytes 25165828
  91.9 50.5 %copy-start.5 = (bf16[1,512,2048]{2,1,0:T(8,128)(2,1)S(1)}, bf16[1,512,2048]{2,1,0:T(8,128)(2,1)}, u32[]{:S(2)}) copy-start(bf16[1,512,2048]{2,1,0:T(8,128)(2,1)} %param.7) | copy-start | bytes 6291460
  91.9 50.5 %copy-start.7 = (bf16[1,512,2048]{2,1,0:T(8,128)(2,1)S(1)}, bf16[1,512,2048]{2,1,0:T(8,128)(2,1)}, u32[]{:S(2)}) copy-start(bf16[1,512,2048]{2,1,0:T(8,128)(2,1)} %param.9) | copy-start | bytes 6291460
  137.9 4.4 %collective-permute-start.12 = (bf16[512,512]{1,0:T(8,128)(2,1)S(1)}, bf16[512,512]{1,0:T(8,128)(2,1)S(1)}, u32[]{:S(2)}, u32[]{:S(2)}) collective-permute-start(bf16[512,512]{1,0:T(8,128)(2,1)S(1)} %constant_dynamic-slice_fusion), channel_id=1, source_target_pairs={{3,2},{4,5},{11,10},{12,13},{19,18},{20,21},{27,26},{28,29}} | collective-permute-start | bytes 1572872 | tf_op jit(solution)/shard_map/ppermute | solution.py:100
  (1 other events, 0.7 us)

commit v5 on v4

--- a/solution.py
+++ b/solution.py
@@ -64,17 +64,18 @@
     lax.fori_loop(0, pivot_ref.shape[0] // 16, group, 0)
 
 
-def couple(pivot, node_class, rate):
-    rows, nodes = pivot.shape
+def couple(pivot, node_class, rate, part=0, parts=1):
+    rows, nodes = pivot.shape[0] // parts, pivot.shape[1]
     chunk = min(rows, 128)
+    steps = rows // chunk
     return pl.pallas_call(
         couple_kernel,
         out_shape=jax.ShapeDtypeStruct((rows, nodes), BF16),
-        grid=(rows // chunk,),
+        grid=(steps,),
         in_specs=[
             pl.BlockSpec(memory_space=pltpu.SMEM),
             pl.BlockSpec((1, nodes), lambda i: (0, 0)),
-            pl.BlockSpec((chunk, nodes), lambda i: (i, 0)),
+            pl.BlockSpec((chunk, nodes), lambda i: (part * steps + i, 0)),
         ],
         out_specs=pl.BlockSpec((chunk, nodes), lambda i: (i, 0)),
         scratch_shapes=[pltpu.VMEM((4, 16, nodes), F32)],
@@ -196,29 +197,29 @@
     )(place, *lefts, right)
 
 
-def zero_kernel(place_ref, left_ref, right_ref, two_ref, out_ref):
+def two_kernel(place_ref, left_ref, right_ref, zero_ref, out_ref):
     odd = place_ref[0]
     width = right_ref.shape[0] // 4
-    multiply_kernel(lambda odd: 2 * odd, 2, 1, place_ref, left_ref, right_ref, out_ref)
+    multiply_kernel(lambda odd: 1, 2, 1, place_ref, left_ref, right_ref, out_ref)
 
     @pl.when(place_ref[1] == 1)
     def _():
-        out_ref[:, 2 * width :] = two_ref[:, pl.ds(pl.multiple_of(2 * odd * width, 128), width)]
-
-
-def product_zero(place, half, across, two):
+        out_ref[:, 2 * width :] = zero_ref[:, pl.ds(pl.multiple_of((2 - 2 * odd) * width, 128), width)]
+
+
+def product_two(place, half, across, zero):
     rows = half.shape[0]
     width = across.shape[0] // 4
     vmem = pl.BlockSpec(memory_space=pltpu.VMEM)
     return pl.pallas_call(
-        zero_kernel,
+        two_kernel,
         out_shape=jax.ShapeDtypeStruct((rows, 3 * width), BF16),
         in_specs=[pl.BlockSpec(memory_space=pltpu.SMEM)] + [vmem] * 3,
         out_specs=vmem,
         compiler_params=pltpu.CompilerParams(vmem_limit_bytes=6 * MIB),
         cost_estimate=LIGHT,
-        name="product_zero",
-    )(place, half, across, two)
+        name="product_two",
+    )(place, half, across, zero)
 
 
 def prior_kernel(step_ref, shifted_ref, sigma_ref, out_ref):
@@ -315,7 +316,7 @@
 
 def final_kernel(
     place_ref, active_ref, pivot_ref, sigma_ref,
-    q0, q0_two, q0_last, q2, q2_last, q3_near, q3_other,
+    q0, q0_last, q2, q2_zero, q2_last, q3_two, q3_other, q3_last,
     q01, q11, q21, q31,
     out_ref, var_ref,
 ):
@@ -349,10 +350,9 @@
 
     @pl.when(active & (place == 0))
     def _():
-        add(at(2 * odd, 2), q0[...])
+        add(at(odd, 3), q0[...])
         add(at(turned(3, odd)), q0_last[:, pl.ds(here, rows)].T)
-        add(at(turned(2, odd)), q0_two[:, pl.ds(here, rows)].T)
-        trace(q0[:, own(odd)])
+        trace(q0[:, own(2 * odd)])
 
     @pl.when(active & (place == 1))
     def _():
@@ -364,15 +364,17 @@
 
     @pl.when(active & (place == 2))
     def _():
-        add(at(odd, 3), q2[...])
+        add(at(turned(0, odd)), q2_zero[:, pl.ds(here, rows)].T)
+        add(at(1, 2), q2[...])
         add(at(turned(3, odd)), q2_last[:, pl.ds(here, rows)].T)
-        trace(q2[:, own(2 - 2 * odd)])
+        trace(q2[:, own(1 - odd)])
 
     @pl.when(active & (place == 3))
     def _():
-        add(at(2 - 2 * odd, 2), q3_near[...])
         add(at(2 * odd, 2), q3_other[...])
-        trace(q3_near[:, own(1 - odd)])
+        add(at(turned(2, odd)), q3_two[...])
+        add(at(turned(3, odd)), q3_last[...])
+        trace(q3_last[:, pl.ds(here, rows)])
 
     @pl.when(active_ref[0] == 0)
     def _():
@@ -399,7 +401,7 @@
             ),
         )
 
-    whole = pl.BlockSpec((rows, width), lambda i, place, active: (0, 0))
+    whole = lambda block: pl.BlockSpec((rows, width), lambda i, place, active: (0, block))
     return pl.pallas_call(
         final_kernel,
         out_shape=(
@@ -414,16 +416,17 @@
                 pl.BlockSpec(
                     (chunk, nodes), lambda i, place, active: (jnp.where(active[0] == 0, i, 0), 0)
                 ),
-                picked(0, 2),
-                pl.BlockSpec((rows, width), lambda i, place, active: (0, 2)),
-                whole,
-                picked(2, 3),
-                whole,
+                picked(0, 3),
+                whole(0),
+                picked(2, 2),
+                whole(2),
+                whole(0),
+                picked(3, 1),
                 picked(3, 2),
-                picked(3, 2),
-                turned_block(lambda odd: 1 - odd),
+                picked(3, 1),
+                turned_block(lambda odd: 1),
                 picked(1, 1),
-                turned_block(lambda odd: 1),
+                turned_block(lambda odd: odd),
                 turned_block(lambda odd: 1 - odd),
             ],
             out_specs=(
@@ -449,39 +452,44 @@
     shifted = passed_along(separator, "dom", -1)[0]
     p2 = moved(pivot, 2, 1)
     p0 = moved(pivot, 0, 1)
-    c1 = couple(pivot, node_class, coupling_rate)
-    c3a = moved(c1[: rows // 2], 3, 1)
-    across = turn(place, 1, 0, c1, None)
+    c1 = [couple(pivot, node_class, coupling_rate, part, 2) for part in range(2)]
+    across = turn(place, 1, 0, c1[0], None)
+    across = turn(place, 1, 1, c1[1], across)
 
     row, far, near, last = prior_parts(place, step_index, after(shifted, across), sigma)
-    far_zero, near_two, last_three = moved(far, 0, 1), moved(near, 2, 1), moved(after(last, p2, p0), 3, 1)
+    far_zero, near_two, last_three = moved(far, 0, 1), moved(near, 2, 1), moved(last, 3, 1)
 
     c2 = couple_here(place, after(p2, last), node_class, coupling_rate)
     across = turn(place, 2, 0, c2, across)
-    c0 = couple_here(place, after(p0, c3a, across), node_class, coupling_rate)
+    c0 = couple_here(place, after(p0, across), node_class, coupling_rate)
     across = turn(place, 0, 0, c0, across)
-    c3b = moved(after(c1[rows // 2 :], last_three, across), 3, 1)
+    c3 = [
+        moved(after(c1[0], last_three, near_two, across), 3, 1),
+        moved(after(c1[1], far_zero), 3, 1),
+    ]
     prior = assemble(place, row, near_two, last_three, far_zero)
 
-    h2 = multiply(place, [c2], prior)
-    q2_own = multiply(place, [h2], across, lambda odd: odd, 3)
+    h0 = multiply(place, [c0], prior)
+    q0_own = multiply(place, [h0], across, lambda odd: odd, 3)
+    q0 = moved(q0_own, 1, 0)
+    h2 = multiply(place, [after(c2, q0_own)], prior)
+    q2_own = product_two(place, h2, across, q0_own)
     q2 = moved(q2_own, 1, 2)
-    h0 = multiply(place, [after(c0, q2_own)], prior)
-    q0_own = product_zero(place, h0, across, q2_own)
-    q0 = moved(q0_own, 1, 0)
-
-    across = turn(place, 3, 0, c3a, across)
-    across = turn(place, 3, 1, c3b, across)
-    h3 = multiply(place, [c3a, c3b], prior)
-    q3_near = moved(multiply(place, [h3], across, lambda odd: 2 - 2 * odd, 2), 1, 3)
+
+    h3 = multiply(place, c3, prior)
+    q3_two = moved(multiply(place, [h3], across, lambda odd: 2 - odd, 1), 1, 3)
     q3_own = multiply(place, [h3], across, lambda odd: 2 * odd, 2)
     q3_other = moved(q3_own, 1, 3)
-    q0_last = moved(lax.dynamic_slice_in_dim(q3_own, odd * width, width, 1), 1, 0)
-    h1 = multiply(place, [after(c1, q2, q3_own)], prior)
+    q30 = lax.dynamic_slice_in_dim(q3_own, odd * width, width, 1)
+    q0_last = moved(q30, 1, 0)
+    across = turn(place, 3, 0, c3[0], after(across, q30))
+    across = turn(place, 3, 1, c3[1], across)
+    q33 = multiply(place, [h3], across, lambda odd: 3 - 3 * odd, 1)
+    q3_last = moved(q33, 1, 3)
+    q2_last = moved(after(q3_two, q0, q33), 3, 2)
+    h1 = multiply(place, [after(c1[0], q33), c1[1]], prior)
     q11 = multiply(place, [h1], across, lambda odd: 1 + odd, 1)
-    q2_last = after(q3_near, q0, q11)
-    q2_last = moved(lax.dynamic_slice_in_dim(q2_last, odd * width, width, 1), 3, 2)
-    received = (q0, q0, q0_last, q2, q2_last, q3_near, q3_other)
+    received = (q0, q0_last, q2, q2, q2_last, q3_two, q3_other, q3_last)
     kept = (q0_own, q11, q2_own, q3_own)
     covariance, variances = final(place, active, pivot, sigma, received, kept)
     return (covariance[None], variances)

time: 148 us -> 139 us (0.939)
  waiting for transfers between devices: 76.6 us -> 60.9 us
  local copies, waits for them, and re-layouts: 11.4 us -> 19.3 us
    ppermute x13 -> x14, waiting for transfers between devices: 76.6 us -> 60.9 us  [moved(): lax.ppermute(value, ('dom', 'col'), route(source, target, lax.axis_size('...]
    unnamed x22 -> x40, local copies, waits for them, and re-layouts: 8.87 us -> 18.2 us
    pallas_call x2, Pallas kernels: 5.65 us -> 3.45 us  [couple_here(): pl.pallas_call(kernel, out_shape=jax.ShapeDtypeStruct((rows, nodes), BF16...]
    pallas_call x8 -> x9, Pallas kernels: 7.39 us -> 8.58 us  [multiply(): pl.pallas_call(functools.partial(multiply_kernel, first, count, len(lefts...]
    ppermute x13 -> x14, starting transfers between devices: 20.6 us -> 19.8 us  [moved(): lax.ppermute(value, ('dom', 'col'), route(source, target, lax.axis_size('...]
    pallas_call x5 -> x6, Pallas kernels: 5.42 us -> 5.98 us  [turn(): pl.pallas_call(turn_kernel, out_shape=jax.ShapeDtypeStruct((nodes, nodes)...]
    pallas_call x1 -> x2, Pallas kernels: 4.74 us -> 4.81 us  [couple(): pl.pallas_call(couple_kernel, out_shape=jax.ShapeDtypeStruct((rows, nodes...]
  transfers between devices with their start and end apart: 14 -> 15, of which waited for: 4 -> 4; matrix products, arithmetic and copies ran while one was open for 2% -> 1% of each run, Pallas kernels for 20% -> 21%
where the time goes in v5:
time: 139 us
  waiting for transfers between devices  60.9 us (44%)
  Pallas kernels  34.3 us (25%)
  starting transfers between devices  21.1 us (15%)
  local copies, waits for them, and re-layouts  19.3 us (14%)
  between operations  3.02 us (2%)
    ppermute x14, waiting for transfers between devices, moved(): lax.ppermute(value, ('dom', 'col'), route(source, target, lax.axis_size('...  60.9 us
    ppermute x14, starting transfers between devices, moved(): lax.ppermute(value, ('dom', 'col'), route(source, target, lax.axis_size('...  19.8 us
    unnamed x40, local copies, waits for them, and re-layouts  18.2 us
    pallas_call x9, Pallas kernels, multiply(): pl.pallas_call(functools.partial(multiply_kernel, first, count, len(lefts...  8.58 us
    pallas_call x6, Pallas kernels, turn(): pl.pallas_call(turn_kernel, out_shape=jax.ShapeDtypeStruct((nodes, nodes)...  5.98 us
    pallas_call x1, Pallas kernels, final(): pl.pallas_call(final_kernel, out_shape=(jax.ShapeDtypeStruct((rows, nodes...  5.3 us
    pallas_call x2, Pallas kernels, couple(): pl.pallas_call(couple_kernel, out_shape=jax.ShapeDtypeStruct((rows, nodes...  4.81 us
    pallas_call x2, Pallas kernels, couple_here(): pl.pallas_call(kernel, out_shape=jax.ShapeDtypeStruct((rows, nodes), BF16...  3.45 us
  transfers between devices with their start and end apart: 15, of which 4 were waited for; matrix products, arithmetic and copies ran while one was open for 1% of the time, Pallas kernels for 21%

profile of v5, /device:TPU:0, one launch (start us, length us, event | category | flops | bytes accessed | tf_op | source)
XLA Modules:
  0.0 138.7 jit_solution(16715433343840338790)
XLA Ops:
  1.9 2.0 %collective-permute-start.1 = (bf16[512,2048]{1,0:T(8,128)(2,1)}, bf16[512,2048]{1,0:T(8,128)(2,1)}, u32[]{:S(2)}, u32[]{:S(2)}) collective-permute-start(bf16[512,2048]{1,0:T(8,128)(2,1)} %bitcast.10), channel_id=1, source_target_pairs={{2,1},{5,6},{10,9},{13,14},{18,17},{21,22},{26,25},{29,30}} | collective-permute-start | bytes 6291464 | tf_op jit(solution)/shard_map/ppermute | solution.py:101
  3.9 4.4 %collective-permute-start = (bf16[512,2048]{1,0:T(8,128)(2,1)}, bf16[512,2048]{1,0:T(8,128)(2,1)S(1)}, u32[]{:S(2)}, u32[]{:S(2)}) collective-permute-start(bf16[512,2048]{1,0:T(8,128)(2,1)} %bitcast.11), channel_id=1, source_target_pairs={{0,1},{7,6},{8,9},{15,14},{16,17},{23,22},{24,25},{31,30}} | collective-permute-start | bytes 6291464 | tf_op jit(solution)/shard_map/ppermute | solution.py:101
  9.6 1.6 %copy-done.6 = bf16[1,512,2048]{2,1,0:T(8,128)(2,1)S(1)} copy-done((bf16[1,512,2048]{2,1,0:T(8,128)(2,1)S(1)}, bf16[1,512,2048]{2,1,0:T(8,128)(2,1)}, u32[]{:S(2)}) %copy-start.6) | copy-done | bytes 2097176
  11.9 2.4 %couple.3.coupled_ref.refs_0_ = bf16[256,2048]{1,0:T(8,128)(2,1)S(1)} custom-call(f32[1]{0:T(128)S(6)} %copy.19.rate_ref.refs_0_, s32[1,2048]{1,0:T(1,128)S(1)} %bitcast.17, bf16[512,2048]{1,0:T(8,128)(2,1)S(1)} %bitcast.12), custom_call_target="tpu_custom_call" | custom-call | flops 1048576 | bytes 65536 | tf_op jit(solution)/shard_map/couple/pallas_call | solution.py:71
  14.3 2.4 %couple.2.coupled_ref.refs_1_ = bf16[256,2048]{1,0:T(8,128)(2,1)S(1)} custom-call(f32[1]{0:T(128)S(6)} %copy.19.rate_ref.refs_0_, s32[1,2048]{1,0:T(1,128)S(1)} %bitcast.18, bf16[512,2048]{1,0:T(8,128)(2,1)S(1)} %bitcast.13), custom_call_target="tpu_custom_call" | custom-call | flops 1048576 | bytes 65536 | tf_op jit(solution)/shard_map/couple/pallas_call | solution.py:71
  19.3 3.0 %prior_parts.1 = (bf16[512,2048]{1,0:T(8,128)(2,1)S(1)}, bf16[512,1536]{1,0:T(8,128)(2,1)S(1)}, bf16[512,1024]{1,0:T(8,128)(2,1)S(1)}, bf16[512,512]{1,0:T(8,128)(2,1)S(1)}) custom-call(s32[3]{0:T(128)S(1)} %pad_add_fusion.place_ref, s32[1]{0:T(128)S(6)} %copy.21.step_ref, bf16[512,2048]{1,0:T(8,128)(2,1)} %bitcast.6.shifted_ref, bf16[512,2048]{1,0:T(8,128)(2,1)S(1)} %bitcast.15), custom_call_target="tpu_custom_call" | custom-call | flops 1048576 | bytes 65536 | tf_op jit(solution)/shard_map/prior_parts/pallas_call | solution.py:256
  22.4 1.6 %collective-permute-start.5 = (bf16[512,1536]{1,0:T(8,128)(2,1)S(1)}, bf16[512,1536]{1,0:T(8,128)(2,1)S(1)}, u32[]{:S(2)}, u32[]{:S(2)}) collective-permute-start(bf16[512,1536]{1,0:T(8,128)(2,1)S(1)} %get-tuple-element.23), channel_id=1, source_target_pairs={{0,1},{7,6},{8,9},{15,14},{16,17},{23,22},{24,25},{31,30}} | collective-permute-start | bytes 4718600 | tf_op jit(solution)/shard_map/ppermute | solution.py:101
  25.5 2.8 %couple_here.2.coupled_ref.refs_0_ = bf16[512,2048]{1,0:T(8,128)(2,1)S(1)} custom-call(s32[3]{0:T(128)S(1)} %pad_add_fusion.place_ref, f32[1]{0:T(128)S(6)} %copy.19.rate_ref.refs_0_, s32[1,2048]{1,0:T(1,128)S(1)} %bitcast.19, bf16[512,2048]{1,0:T(8,128)(2,1)} %collective-permute-done.1.refs_2_), custom_call_target="tpu_custom_call" | custom-call | flops 1048576 | bytes 65536 | tf_op jit(solution)/shard_map/couple_here/pallas_call | solution.py:113
  29.5 2.5 %collective-permute-done.refs_2_ = bf16[512,2048]{1,0:T(8,128)(2,1)S(1)} collective-permute-done((bf16[512,2048]{1,0:T(8,128)(2,1)}, bf16[512,2048]{1,0:T(8,128)(2,1)S(1)}, u32[]{:S(2)}, u32[]{:S(2)}) %collective-permute-start) | collective-permute-done | bytes 2097184 | tf_op jit(solution)/shard_map/ppermute | solution.py:101
  34.6 19.7 %collective-permute-done.5.far_zero = bf16[512,1536]{1,0:T(8,128)(2,1)S(1)} collective-permute-done((bf16[512,1536]{1,0:T(8,128)(2,1)S(1)}, bf16[512,1536]{1,0:T(8,128)(2,1)S(1)}, u32[]{:S(2)}, u32[]{:S(2)}) %collective-permute-start.5) | collective-permute-done | bytes 1572896 | tf_op jit(solution)/shard_map/ppermute | solution.py:101
  56.2 2.2 %multiply.10.zero_ref.q01 = bf16[512,1536]{1,0:T(8,128)(2,1)} custom-call(s32[3]{0:T(128)S(1)} %pad_add_fusion.place_ref, bf16[512,2048]{1,0:T(8,128)(2,1)S(1)} %multiply.9.refs_0_, bf16[2048,2048]{1,0:T(8,128)(2,1)S(1)} %turn.9.refs_1_.right_ref.refs_0_), custom_call_target="tpu_custom_call" | custom-call | flops 1048576 | bytes 65536 | tf_op jit(solution)/shard_map/multiply/pallas_call | solution.py:189
  60.2 2.6 %product_two.1.q21 = bf16[512,1536]{1,0:T(8,128)(2,1)} custom-call(s32[3]{0:T(128)S(1)} %pad_add_fusion.place_ref, bf16[512,2048]{1,0:T(8,128)(2,1)S(1)} %multiply.13.left_ref, bf16[2048,2048]{1,0:T(8,128)(2,1)S(1)} %turn.9.refs_1_.right_ref.refs_0_, bf16[512,1536]{1,0:T(8,128)(2,1)} %multiply.10.zero_ref.q01), custom_call_target="tpu_custom_call" | custom-call | flops 1048576 | bytes 65536 | tf_op jit(solution)/shard_map/product_two/pallas_call | solution.py:214
  62.8 1.9 %collective-permute-start.10 = (bf16[512,1536]{1,0:T(8,128)(2,1)}, bf16[512,1536]{1,0:T(8,128)(2,1)}, u32[]{:S(2)}, u32[]{:S(2)}) collective-permute-start(bf16[512,1536]{1,0:T(8,128)(2,1)} %product_two.1.q21), channel_id=1, source_target_pairs={{1,2},{6,5},{9,10},{14,13},{17,18},{22,21},{25,26},{30,29}} | collective-permute-start | bytes 4718600 | tf_op jit(solution)/shard_map/ppermute | solution.py:101
  66.0 1.3 multiply.14
  67.3 1.4 %collective-permute-start.11 = (bf16[512,512]{1,0:T(8,128)(2,1)}, bf16[512,512]{1,0:T(8,128)(2,1)}, u32[]{:S(2)}, u32[]{:S(2)}) collective-permute-start(bf16[512,512]{1,0:T(8,128)(2,1)} %multiply.14), channel_id=1, source_target_pairs={{1,3},{6,4},{9,11},{14,12},{17,19},{22,20},{25,27},{30,28}} | collective-permute-start | bytes 1572872 | tf_op jit(solution)/shard_map/ppermute | solution.py:101
  68.8 1.6 %multiply.12.q31 = bf16[512,1024]{1,0:T(8,128)(2,1)} custom-call(s32[3]{0:T(128)S(1)} %pad_add_fusion.place_ref, bf16[512,2048]{1,0:T(8,128)(2,1)S(1)} %multiply.11.refs_0_, bf16[2048,2048]{1,0:T(8,128)(2,1)S(1)} %turn.9.refs_1_.right_ref.refs_0_), custom_call_target="tpu_custom_call" | custom-call | flops 1048576 | bytes 65536 | tf_op jit(solution)/shard_map/multiply/pallas_call | solution.py:189
  70.4 1.7 %collective-permute-start.13 = (bf16[512,1024]{1,0:T(8,128)(2,1)}, bf16[512,1024]{1,0:T(8,128)(2,1)}, u32[]{:S(2)}, u32[]{:S(2)}) collective-permute-start(bf16[512,1024]{1,0:T(8,128)(2,1)} %multiply.12.q31), channel_id=1, source_target_pairs={{1,3},{6,4},{9,11},{14,12},{17,19},{22,20},{25,27},{30,28}} | collective-permute-start | bytes 3145736 | tf_op jit(solution)/shard_map/ppermute | solution.py:101
  74.4 3.4 %copy-done.1 = bf16[2048,2048]{1,0:T(8,128)(2,1)S(1)} copy-done((bf16[2048,2048]{1,0:T(8,128)(2,1)S(1)}, bf16[2048,2048]{1,0:T(8,128)(2,1)}, u32[]{:S(2)}) %copy-start.1) | copy-done | bytes 8388632
  81.2 3.5 %copy-done.2 = bf16[2048,2048]{1,0:T(8,128)(2,1)} copy-done((bf16[2048,2048]{1,0:T(8,128)(2,1)}, bf16[2048,2048]{1,0:T(8,128)(2,1)S(1)}, u32[]{:S(2)}) %copy-start.2) | copy-done | bytes 8388632
  84.7 3.4 %copy-done.3 = bf16[2048,2048]{1,0:T(8,128)(2,1)S(1)} copy-done((bf16[2048,2048]{1,0:T(8,128)(2,1)S(1)}, bf16[2048,2048]{1,0:T(8,128)(2,1)}, u32[]{:S(2)}) %copy-start.3) | copy-done | bytes 8388632
  89.3 1.8 %collective-permute-done.6.q0 = bf16[512,1536]{1,0:T(8,128)(2,1)} collective-permute-done((bf16[512,1536]{1,0:T(8,128)(2,1)}, bf16[512,1536]{1,0:T(8,128)(2,1)}, u32[]{:S(2)}, u32[]{:S(2)}) %collective-permute-start.6) | collective-permute-done | bytes 1572896 | tf_op jit(solution)/shard_map/ppermute | solution.py:101
  93.3 2.6 %copy-done.4 = bf16[2048,2048]{1,0:T(8,128)(2,1)S(1)} copy-done((bf16[2048,2048]{1,0:T(8,128)(2,1)S(1)}, bf16[2048,2048]{1,0:T(8,128)(2,1)}, u32[]{:S(2)}) %copy-start.4) | copy-done | bytes 8388632
  96.5 36.8 %collective-permute-done.9.q0_last = bf16[512,512]{1,0:T(8,128)(2,1)S(1)} collective-permute-done((bf16[512,512]{1,0:T(8,128)(2,1)S(1)}, bf16[512,512]{1,0:T(8,128)(2,1)S(1)}, u32[]{:S(2)}, u32[]{:S(2)}) %collective-permute-start.9) | collective-permute-done | bytes 524320 | tf_op jit(solution)/shard_map/ppermute | solution.py:101
  133.4 5.3 %final.1 = (bf16[512,2048]{1,0:T(8,128)(2,1)}, f32[1,512]{1,0:T(1,128)}) custom-call(s32[3]{0:T(128)S(1)} %pad_add_fusion.place_ref, s32[1]{0:T(128)S(6)} %convert_element_type.3.active_ref, bf16[512,2048]{1,0:T(8,128)(2,1)S(1)} %bitcast.14, bf16[512,2048]{1,0:T(8,128)(2,1)S(1)} %bitcast.16, bf16[512,1536]{1,0:T(8,128)(2,1)} %collective-permute-done.6.q0, ...), custom_call_target="tpu_custom_call" | custom-call | flops 1048576 | bytes 65536 | tf_op jit(solution)/shard_map/final/pallas_call | solution.py:405
  (72 shorter events, 23.6 us)
Async XLA Ops:
  0.6 18.0 %collective-permute-start.2 = (bf16[1,512,2048]{2,1,0:T(8,128)(2,1)}, bf16[1,512,2048]{2,1,0:T(8,128)(2,1)}, u32[]{:S(2)}, u32[]{:S(2)}) collective-permute-start(bf16[1,512,2048]{2,1,0:T(8,128)(2,1)} %param.8), channel_id=1, source_target_pairs={{4,0},{8,4},{12,8},{5,1},{9,5},{13,9},{6,2},{10,6},{14,10},{7,3},{... | collective-permute-start | bytes 6291464 | tf_op jit(solution)/shard_map/ppermute | solution.py:20
  1.9 23.5 %collective-permute-start.1 = (bf16[512,2048]{1,0:T(8,128)(2,1)}, bf16[512,2048]{1,0:T(8,128)(2,1)}, u32[]{:S(2)}, u32[]{:S(2)}) collective-permute-start(bf16[512,2048]{1,0:T(8,128)(2,1)} %bitcast.10), channel_id=1, source_target_pairs={{2,1},{5,6},{10,9},{13,14},{18,17},{21,22},{26,25},{29,30}} | collective-permute-start | bytes 6291464 | tf_op jit(solution)/shard_map/ppermute | solution.py:101
  3.9 28.1 %collective-permute-start = (bf16[512,2048]{1,0:T(8,128)(2,1)}, bf16[512,2048]{1,0:T(8,128)(2,1)S(1)}, u32[]{:S(2)}, u32[]{:S(2)}) collective-permute-start(bf16[512,2048]{1,0:T(8,128)(2,1)} %bitcast.11), channel_id=1, source_target_pairs={{0,1},{7,6},{8,9},{15,14},{16,17},{23,22},{24,25},{31,30}} | collective-permute-start | bytes 6291464 | tf_op jit(solution)/shard_map/ppermute | solution.py:101
  16.7 37.7 %copy-start.8 = (bf16[256,2048]{1,0:T(8,128)(2,1)}, bf16[256,2048]{1,0:T(8,128)(2,1)S(1)}, u32[]{:S(2)}) copy-start(bf16[256,2048]{1,0:T(8,128)(2,1)S(1)} %couple.2.coupled_ref.refs_1_) | copy-start | bytes 3145732
  19.3 6.1 %copy-start.17 = (s32[2048]{0:T(1024)S(1)}, s32[2048]{0:T(1024)}, u32[]{:S(2)}) copy-start(s32[2048]{0:T(1024)} %param.13) | copy-start | bytes 24580
  22.4 32.0 %collective-permute-start.5 = (bf16[512,1536]{1,0:T(8,128)(2,1)S(1)}, bf16[512,1536]{1,0:T(8,128)(2,1)S(1)}, u32[]{:S(2)}, u32[]{:S(2)}) collective-permute-start(bf16[512,1536]{1,0:T(8,128)(2,1)S(1)} %get-tuple-element.23), channel_id=1, source_target_pairs={{0,1},{7,6},{8,9},{15,14},{16,17},{23,22},{24,25},{31,30}} | collective-permute-start | bytes 4718600 | tf_op jit(solution)/shard_map/ppermute | solution.py:101
  24.0 9.9 %collective-permute-start.3 = (bf16[512,1024]{1,0:T(8,128)(2,1)S(1)}, bf16[512,1024]{1,0:T(8,128)(2,1)S(1)}, u32[]{:S(2)}, u32[]{:S(2)}) collective-permute-start(bf16[512,1024]{1,0:T(8,128)(2,1)S(1)} %get-tuple-element.22), channel_id=1, source_target_pairs={{2,1},{5,6},{10,9},{13,14},{18,17},{21,22},{26,25},{29,30}} | collective-permute-start | bytes 3145736 | tf_op jit(solution)/shard_map/ppermute | solution.py:101
  24.7 9.1 %collective-permute-start.4 = (bf16[512,512]{1,0:T(8,128)(2,1)S(1)}, bf16[512,512]{1,0:T(8,128)(2,1)S(1)}, u32[]{:S(2)}, u32[]{:S(2)}) collective-permute-start(bf16[512,512]{1,0:T(8,128)(2,1)S(1)} %get-tuple-element.18), channel_id=1, source_target_pairs={{3,1},{4,6},{11,9},{12,14},{19,17},{20,22},{27,25},{28,30}} | collective-permute-start | bytes 1572872 | tf_op jit(solution)/shard_map/ppermute | solution.py:101
  33.9 34.9 %copy-start = (bf16[2048,2048]{1,0:T(8,128)(2,1)}, bf16[2048,2048]{1,0:T(8,128)(2,1)S(1)}, u32[]{:S(2)}) copy-start(bf16[2048,2048]{1,0:T(8,128)(2,1)S(1)} %turn.9.refs_1_.right_ref.refs_0_) | copy-start | bytes 25165828
  33.9 30.8 %collective-permute-start.7 = (bf16[256,2048]{1,0:T(8,128)(2,1)S(1)}, bf16[256,2048]{1,0:T(8,128)(2,1)S(1)}, u32[]{:S(2)}, u32[]{:S(2)}) collective-permute-start(bf16[256,2048]{1,0:T(8,128)(2,1)S(1)} %couple.3.coupled_ref.refs_0_), channel_id=1, source_target_pairs={{3,1},{4,6},{11,9},{12,14},{19,17},{20,22},{27,25},{28,30}} | collective-permute-start | bytes 3145736 | tf_op jit(solution)/shard_map/ppermute | solution.py:101
  54.4 10.3 %collective-permute-start.8 = (bf16[256,2048]{1,0:T(8,128)(2,1)S(1)}, bf16[256,2048]{1,0:T(8,128)(2,1)S(1)}, u32[]{:S(2)}, u32[]{:S(2)}) collective-permute-start(bf16[256,2048]{1,0:T(8,128)(2,1)S(1)} %couple.2.coupled_ref.refs_1_), channel_id=1, source_target_pairs={{3,1},{4,6},{11,9},{12,14},{19,17},{20,22},{27,25},{28,30}} | collective-permute-start | bytes 3145736 | tf_op jit(solution)/shard_map/ppermute | solution.py:101
  55.7 9.0 %copy-start.5 = (bf16[2048,2048]{1,0:T(8,128)(2,1)}, bf16[2048,2048]{1,0:T(8,128)(2,1)S(1)}, u32[]{:S(2)}) copy-start(bf16[2048,2048]{1,0:T(8,128)(2,1)S(1)} %assemble.1.refs_1_.refs_2_) | copy-start | bytes 25165828
  58.4 32.8 %collective-permute-start.6 = (bf16[512,1536]{1,0:T(8,128)(2,1)}, bf16[512,1536]{1,0:T(8,128)(2,1)}, u32[]{:S(2)}, u32[]{:S(2)}) collective-permute-start(bf16[512,1536]{1,0:T(8,128)(2,1)} %multiply.10.zero_ref.q01), channel_id=1, source_target_pairs={{1,0},{6,7},{9,8},{14,15},{17,16},{22,23},{25,24},{30,31}} | collective-permute-start | bytes 4718600 | tf_op jit(solution)/shard_map/ppermute | solution.py:101
  62.8 33.7 %collective-permute-start.10 = (bf16[512,1536]{1,0:T(8,128)(2,1)}, bf16[512,1536]{1,0:T(8,128)(2,1)}, u32[]{:S(2)}, u32[]{:S(2)}) collective-permute-start(bf16[512,1536]{1,0:T(8,128)(2,1)} %product_two.1.q21), channel_id=1, source_target_pairs={{1,2},{6,5},{9,10},{14,13},{17,18},{22,21},{25,26},{30,29}} | collective-permute-start | bytes 4718600 | tf_op jit(solution)/shard_map/ppermute | solution.py:101
  67.3 21.3 %collective-permute-start.11 = (bf16[512,512]{1,0:T(8,128)(2,1)}, bf16[512,512]{1,0:T(8,128)(2,1)}, u32[]{:S(2)}, u32[]{:S(2)}) collective-permute-start(bf16[512,512]{1,0:T(8,128)(2,1)} %multiply.14), channel_id=1, source_target_pairs={{1,3},{6,4},{9,11},{14,12},{17,19},{22,20},{25,27},{30,28}} | collective-permute-start | bytes 1572872 | tf_op jit(solution)/shard_map/ppermute | solution.py:101
  70.4 63.0 %collective-permute-start.13 = (bf16[512,1024]{1,0:T(8,128)(2,1)}, bf16[512,1024]{1,0:T(8,128)(2,1)}, u32[]{:S(2)}, u32[]{:S(2)}) collective-permute-start(bf16[512,1024]{1,0:T(8,128)(2,1)} %multiply.12.q31), channel_id=1, source_target_pairs={{1,3},{6,4},{9,11},{14,12},{17,19},{22,20},{25,27},{30,28}} | collective-permute-start | bytes 3145736 | tf_op jit(solution)/shard_map/ppermute | solution.py:101
  73.1 60.2 %collective-permute-start.9 = (bf16[512,512]{1,0:T(8,128)(2,1)S(1)}, bf16[512,512]{1,0:T(8,128)(2,1)S(1)}, u32[]{:S(2)}, u32[]{:S(2)}) collective-permute-start(bf16[512,512]{1,0:T(8,128)(2,1)S(1)} %constant_dynamic-slice_fusion), channel_id=1, source_target_pairs={{1,0},{6,7},{9,8},{14,15},{17,16},{22,23},{25,24},{30,31}} | collective-permute-start | bytes 1572872 | tf_op jit(solution)/shard_map/ppermute | solution.py:101
  79.0 13.5 %slice-start = ((s8[8388608]{0:T(1024)(128)(4,1)}), s8[4194304]{0:T(1024)(128)(4,1)S(1)}, s32[]{:S(2)}) async-start(s8[8388608]{0:T(1024)(128)(4,1)} %bitcast.8), calls=%async_computation | async-start | bytes 8388608
  80.3 12.3 %slice-start.1 = ((s8[8388608]{0:T(1024)(128)(4,1)}), s8[4194304]{0:T(1024)(128)(4,1)S(1)}, s32[]{:S(2)}) async-start(s8[8388608]{0:T(1024)(128)(4,1)} %bitcast.8), calls=%async_computation.1 | async-start | bytes 8388608
  88.1 4.5 %copy-start.9 = (bf16[256,2048]{1,0:T(8,128)(2,1)S(1)}, bf16[256,2048]{1,0:T(8,128)(2,1)}, u32[]{:S(2)}) copy-start(bf16[256,2048]{1,0:T(8,128)(2,1)} %copy-done.8) | copy-start | bytes 3145732
  88.6 7.9 %collective-permute-start.14 = (bf16[512,512]{1,0:T(8,128)(2,1)S(1)}, bf16[512,512]{1,0:T(8,128)(2,1)S(1)}, u32[]{:S(2)}, u32[]{:S(2)}) collective-permute-start(bf16[512,512]{1,0:T(8,128)(2,1)S(1)} %multiply.15), channel_id=1, source_target_pairs={{1,3},{6,4},{9,11},{14,12},{17,19},{22,20},{25,27},{30,28}} | collective-permute-start | bytes 1572872 | tf_op jit(solution)/shard_map/ppermute | solution.py:101
  91.2 42.1 %collective-permute-start.12 = (bf16[512,512]{1,0:T(8,128)(2,1)}, bf16[512,512]{1,0:T(8,128)(2,1)S(1)}, u32[]{:S(2)}, u32[]{:S(2)}) collective-permute-start(bf16[512,512]{1,0:T(8,128)(2,1)} %collective-permute-done.11.q3_two), channel_id=1, source_target_pairs={{3,2},{4,5},{11,10},{12,13},{19,18},{20,21},{27,26},{28,29}} | collective-permute-start | bytes 1572872 | tf_op jit(solution)/shard_map/ppermute | solution.py:101
  96.0 37.4 %copy-start.7 = (bf16[1,512,2048]{2,1,0:T(8,128)(2,1)S(1)}, bf16[1,512,2048]{2,1,0:T(8,128)(2,1)}, u32[]{:S(2)}) copy-start(bf16[1,512,2048]{2,1,0:T(8,128)(2,1)} %param.9) | copy-start | bytes 6291460
  96.0 37.4 %copy-start.11 = (bf16[1,512,2048]{2,1,0:T(8,128)(2,1)S(1)}, bf16[1,512,2048]{2,1,0:T(8,128)(2,1)}, u32[]{:S(2)}) copy-start(bf16[1,512,2048]{2,1,0:T(8,128)(2,1)} %param.7) | copy-start | bytes 6291460
  (11 other events, 22.3 us)

commit v6 on v5

--- a/solution.py
+++ b/solution.py
@@ -222,24 +222,51 @@
     )(place, half, across, zero)
 
 
-def prior_kernel(step_ref, shifted_ref, sigma_ref, out_ref):
-    @pl.when(step_ref[0] == 0)
+def three_kernel(place_ref, left_ref, right_ref, out_ref, zero_ref):
+    width = zero_ref.shape[1]
+    multiply_kernel(lambda odd: 2 * odd, 2, 1, place_ref, left_ref, right_ref, out_ref)
+
+    @pl.when(place_ref[1] == 1)
+    def _():
+        zero_ref[...] = out_ref[:, pl.ds(pl.multiple_of(place_ref[0] * width, 128), width)]
+
+
+def product_three(place, half, across):
+    rows = half.shape[0]
+    width = across.shape[0] // 4
+    vmem = pl.BlockSpec(memory_space=pltpu.VMEM)
+    return pl.pallas_call(
+        three_kernel,
+        out_shape=(
+            jax.ShapeDtypeStruct((rows, 2 * width), BF16),
+            jax.ShapeDtypeStruct((rows, width), BF16),
+        ),
+        in_specs=[pl.BlockSpec(memory_space=pltpu.SMEM)] + [vmem] * 2,
+        out_specs=(vmem, vmem),
+        compiler_params=pltpu.CompilerParams(vmem_limit_bytes=6 * MIB),
+        cost_estimate=LIGHT,
+        name="product_three",
+    )(place, half, across)
+
+
+def prior_kernel(place_ref, shifted_ref, sigma_ref, out_ref):
+    @pl.when(place_ref[3] == 0)
     def _():
         out_ref[...] = shifted_ref[...]
 
-    @pl.when(step_ref[0] != 0)
+    @pl.when(place_ref[3] != 0)
     def _():
         out_ref[...] = sigma_ref[...]
 
 
-def parts_kernel(place_ref, step_ref, shifted_ref, sigma_ref, row_ref, far_ref, near_ref, last_ref):
+def parts_kernel(place_ref, shifted_ref, sigma_ref, row_ref, far_ref, near_ref, last_ref):
     odd = place_ref[0]
     width = last_ref.shape[1]
 
     def at(block, count=1):
         return pl.ds(pl.multiple_of(block * width, 128), count * width)
 
-    prior_kernel(step_ref, shifted_ref, sigma_ref, row_ref)
+    prior_kernel(place_ref, shifted_ref, sigma_ref, row_ref)
     near = row_ref[:, at(2 - 2 * odd, 2)]
     near_ref[...] = near
     far_ref[:, width:] = near
@@ -247,24 +274,24 @@
     last_ref[...] = row_ref[:, at(3 - 3 * odd)]
 
 
-def prior_parts(place, step, shifted, sigma):
+def prior_parts(place, shifted, sigma):
     rows, nodes = sigma.shape
     chunk = 128
     width = nodes // 4
     out = lambda blocks: jax.ShapeDtypeStruct((rows, blocks * width), BF16)
-    spec = lambda blocks: pl.BlockSpec((chunk, blocks * width), lambda i, place, step: (i, 0))
+    spec = lambda blocks: pl.BlockSpec((chunk, blocks * width), lambda i, place: (i, 0))
     return pl.pallas_call(
         parts_kernel,
         out_shape=(out(4), out(3), out(2), out(1)),
         grid_spec=pltpu.PrefetchScalarGridSpec(
-            num_scalar_prefetch=2,
+            num_scalar_prefetch=1,
             grid=(rows // chunk,),
             in_specs=[
                 pl.BlockSpec(
-                    (chunk, nodes), lambda i, place, step: (jnp.where(step[0] == 0, i, 0), 0)
+                    (chunk, nodes), lambda i, place: (jnp.where(place[3] == 0, i, 0), 0)
                 ),
                 pl.BlockSpec(
-                    (chunk, nodes), lambda i, place, step: (jnp.where(step[0] == 0, 0, i), 0)
+                    (chunk, nodes), lambda i, place: (jnp.where(place[3] == 0, 0, i), 0)
                 ),
             ],
             out_specs=(spec(4), spec(3), spec(2), spec(1)),
@@ -272,7 +299,7 @@
         compiler_params=pltpu.CompilerParams(vmem_limit_bytes=8 * MIB),
         cost_estimate=LIGHT,
         name="prior_parts",
-    )(place, step, shifted, sigma)
+    )(place, shifted, sigma)
 
 
 def assemble_kernel(place_ref, own, near_two, last_three, far_zero, out_ref):
@@ -315,7 +342,7 @@
 
 
 def final_kernel(
-    place_ref, active_ref, pivot_ref, sigma_ref,
+    place_ref, pivot_ref, sigma_ref,
     q0, q0_last, q2, q2_zero, q2_last, q3_two, q3_other, q3_last,
     q01, q11, q21, q31,
     out_ref, var_ref,
@@ -346,7 +373,7 @@
             pivot_ref[:, own(place_ref[2])].astype(F32) + product.astype(F32)
         )
 
-    active = active_ref[0] != 0
+    active = place_ref[4] != 0
 
     @pl.when(active & (place == 0))
     def _():
@@ -376,32 +403,32 @@
         add(at(turned(3, odd)), q3_last[...])
         trace(q3_last[:, pl.ds(here, rows)])
 
-    @pl.when(active_ref[0] == 0)
+    @pl.when(place_ref[4] == 0)
     def _():
         out_ref[...] = sigma_ref[...]
         var_ref[...] = diagonal(sigma_ref[:, own(place_ref[2])].astype(F32))
 
 
-def final(place, active, pivot, sigma, received, kept):
+def final(place, pivot, sigma, received, kept):
     rows, nodes = pivot.shape
     chunk = 128
     width = nodes // 4
 
     def picked(which, blocks):
         return pl.BlockSpec(
-            (chunk, blocks * width), lambda i, place, active: (jnp.where(place[1] == which, i, 0), 0)
+            (chunk, blocks * width), lambda i, place: (jnp.where(place[1] == which, i, 0), 0)
         )
 
     def turned_block(start):
         return pl.BlockSpec(
             (rows, chunk),
-            lambda i, place, active: (
+            lambda i, place: (
                 0,
                 jnp.where(place[1] == 1, start(place[0]) * (width // chunk) + i, 0),
             ),
         )
 
-    whole = lambda block: pl.BlockSpec((rows, width), lambda i, place, active: (0, block))
+    whole = lambda block: pl.BlockSpec((rows, width), lambda i, place: (0, block))
     return pl.pallas_call(
         final_kernel,
         out_shape=(
@@ -409,12 +436,12 @@
             jax.ShapeDtypeStruct((1, rows), F32),
         ),
         grid_spec=pltpu.PrefetchScalarGridSpec(
-            num_scalar_prefetch=2,
+            num_scalar_prefetch=1,
             grid=(rows // chunk,),
             in_specs=[
-                pl.BlockSpec((chunk, nodes), lambda i, place, active: (i, 0)),
+                pl.BlockSpec((chunk, nodes), lambda i, place: (i, 0)),
                 pl.BlockSpec(
-                    (chunk, nodes), lambda i, place, active: (jnp.where(active[0] == 0, i, 0), 0)
+                    (chunk, nodes), lambda i, place: (jnp.where(place[4] == 0, i, 0), 0)
                 ),
                 picked(0, 3),
                 whole(0),
@@ -430,23 +457,22 @@
                 turned_block(lambda odd: 1 - odd),
             ],
             out_specs=(
-                pl.BlockSpec((chunk, nodes), lambda i, place, active: (i, 0)),
-                pl.BlockSpec((1, chunk), lambda i, place, active: (0, i)),
+                pl.BlockSpec((chunk, nodes), lambda i, place: (i, 0)),
+                pl.BlockSpec((1, chunk), lambda i, place: (0, i)),
             ),
         ),
         compiler_params=pltpu.CompilerParams(vmem_limit_bytes=12 * MIB),
         cost_estimate=LIGHT,
         name="final",
-    )(place, active, pivot, sigma, *received, *kept)
+    )(place, pivot, sigma, *received, *kept)
 
 
 def owned(sigma_next, separator, inverse_pivot, coupling_rate, lengths, step_index, node_class):
     sigma, pivot = sigma_next[0], inverse_pivot[0]
     odd = lax.axis_index("dom") % 2
     col = lax.axis_index("col")
-    place = jnp.stack([odd, turned(col, odd), col]).astype(jnp.int32)
-    active = (step_index < lengths).astype(jnp.int32)
-    rows, width = pivot.shape[0], pivot.shape[1] // 4
+    step = step_index[0]
+    place = jnp.stack([odd, turned(col, odd), col, step, step < lengths[0]]).astype(jnp.int32)
     after = lambda value, *others: lax.optimization_barrier((value, *others))[0]
 
     shifted = passed_along(separator, "dom", -1)[0]
@@ -456,7 +482,7 @@
     across = turn(place, 1, 0, c1[0], None)
     across = turn(place, 1, 1, c1[1], across)
 
-    row, far, near, last = prior_parts(place, step_index, after(shifted, across), sigma)
+    row, far, near, last = prior_parts(place, after(shifted, across), sigma)
     far_zero, near_two, last_three = moved(far, 0, 1), moved(near, 2, 1), moved(last, 3, 1)
 
     c2 = couple_here(place, after(p2, last), node_class, coupling_rate)
@@ -478,9 +504,8 @@
 
     h3 = multiply(place, c3, prior)
     q3_two = moved(multiply(place, [h3], across, lambda odd: 2 - odd, 1), 1, 3)
-    q3_own = multiply(place, [h3], across, lambda odd: 2 * odd, 2)
+    q3_own, q30 = product_three(place, h3, across)
     q3_other = moved(q3_own, 1, 3)
-    q30 = lax.dynamic_slice_in_dim(q3_own, odd * width, width, 1)
     q0_last = moved(q30, 1, 0)
     across = turn(place, 3, 0, c3[0], after(across, q30))
     across = turn(place, 3, 1, c3[1], across)
@@ -491,7 +516,7 @@
     q11 = multiply(place, [h1], across, lambda odd: 1 + odd, 1)
     received = (q0, q0_last, q2, q2, q2_last, q3_two, q3_other, q3_last)
     kept = (q0_own, q11, q2_own, q3_own)
-    covariance, variances = final(place, active, pivot, sigma, received, kept)
+    covariance, variances = final(place, pivot, sigma, received, kept)
     return (covariance[None], variances)
 
 

time: 139 us -> 131 us (0.942)
  the two profiles are of different devices: /device:TPU:0 before, /device:TPU:2 now
where the time goes in v6:
time: 131 us
  waiting for transfers between devices  79.3 us (61%)
  Pallas kernels  26.7 us (20%)
  starting transfers between devices  19.6 us (15%)
  between operations  2.96 us (2%)
  local copies, waits for them, and re-layouts  2.39 us (2%)
    ppermute x14, waiting for transfers between devices, moved(): lax.ppermute(value, ('dom', 'col'), route(source, target, lax.axis_size('...  71.3 us
    ppermute x14, starting transfers between devices, moved(): lax.ppermute(value, ('dom', 'col'), route(source, target, lax.axis_size('...  17.7 us
    ppermute x1, waiting for transfers between devices, passed_along(): lax.ppermute(value, axis, [(source, source + steps) for source in range(i...  7.96 us
    pallas_call x6, Pallas kernels, turn(): pl.pallas_call(turn_kernel, out_shape=jax.ShapeDtypeStruct((nodes, nodes)...  5.99 us
    pallas_call x2, Pallas kernels, couple(): pl.pallas_call(couple_kernel, out_shape=jax.ShapeDtypeStruct((rows, nodes...  4.81 us
    pallas_call x8, Pallas kernels, multiply(): pl.pallas_call(functools.partial(multiply_kernel, first, count, len(lefts...  4.4 us
    pallas_call x2, Pallas kernels, couple_here(): pl.pallas_call(kernel, out_shape=jax.ShapeDtypeStruct((rows, nodes), BF16...  3.45 us
    pallas_call x1, Pallas kernels, final(): pl.pallas_call(final_kernel, out_shape=(jax.ShapeDtypeStruct((rows, nodes...  3.35 us
  transfers between devices with their start and end apart: 15, of which 4 were waited for; matrix products, arithmetic and copies ran while one was open for 0% of the time, Pallas kernels for 18%

profile of v6, /device:TPU:2, one launch (start us, length us, event | category | flops | bytes accessed | tf_op | source)
XLA Modules:
  0.0 130.9 jit_solution(16015144258741614971)
XLA Ops:
  0.6 1.9 %collective-permute-start.2 = (bf16[1,512,2048]{2,1,0:T(8,128)(2,1)}, bf16[1,512,2048]{2,1,0:T(8,128)(2,1)}, u32[]{:S(2)}, u32[]{:S(2)}) collective-permute-start(bf16[1,512,2048]{2,1,0:T(8,128)(2,1)} %param.8), channel_id=1, source_target_pairs={{4,0},{8,4},{12,8},{5,1},{9,5},{13,9},{6,2},{10,6},{14,10},{7,3},{... | collective-permute-start | bytes 6291464 | tf_op jit(solution)/shard_map/ppermute | solution.py:20
  2.6 2.0 %collective-permute-start.1 = (bf16[512,2048]{1,0:T(8,128)(2,1)}, bf16[512,2048]{1,0:T(8,128)(2,1)}, u32[]{:S(2)}, u32[]{:S(2)}) collective-permute-start(bf16[512,2048]{1,0:T(8,128)(2,1)} %bitcast.8), channel_id=1, source_target_pairs={{2,1},{5,6},{10,9},{13,14},{18,17},{21,22},{26,25},{29,30}} | collective-permute-start | bytes 6291464 | tf_op jit(solution)/shard_map/ppermute | solution.py:101
  4.5 2.9 %collective-permute-start = (bf16[512,2048]{1,0:T(8,128)(2,1)}, bf16[512,2048]{1,0:T(8,128)(2,1)S(1)}, u32[]{:S(2)}, u32[]{:S(2)}) collective-permute-start(bf16[512,2048]{1,0:T(8,128)(2,1)} %bitcast.9), channel_id=1, source_target_pairs={{0,1},{7,6},{8,9},{15,14},{16,17},{23,22},{24,25},{31,30}} | collective-permute-start | bytes 6291464 | tf_op jit(solution)/shard_map/ppermute | solution.py:101
  9.5 1.6 %copy-done = bf16[1,512,2048]{2,1,0:T(8,128)(2,1)S(1)} copy-done((bf16[1,512,2048]{2,1,0:T(8,128)(2,1)S(1)}, bf16[1,512,2048]{2,1,0:T(8,128)(2,1)}, u32[]{:S(2)}) %copy-start) | copy-done | bytes 2097176
  11.8 2.4 %couple.3.coupled_ref.refs_0_ = bf16[256,2048]{1,0:T(8,128)(2,1)S(1)} custom-call(f32[1]{0:T(128)S(6)} %copy.19.rate_ref.refs_0_, s32[1,2048]{1,0:T(1,128)S(1)} %bitcast.15, bf16[512,2048]{1,0:T(8,128)(2,1)S(1)} %bitcast.10), custom_call_target="tpu_custom_call" | custom-call | flops 1048576 | bytes 65536 | tf_op jit(solution)/shard_map/couple/pallas_call | solution.py:71
  14.2 2.4 %couple.2.coupled_ref.refs_1_ = bf16[256,2048]{1,0:T(8,128)(2,1)S(1)} custom-call(f32[1]{0:T(128)S(6)} %copy.19.rate_ref.refs_0_, s32[1,2048]{1,0:T(1,128)S(1)} %bitcast.16, bf16[512,2048]{1,0:T(8,128)(2,1)S(1)} %bitcast.11), custom_call_target="tpu_custom_call" | custom-call | flops 1048576 | bytes 65536 | tf_op jit(solution)/shard_map/couple/pallas_call | solution.py:71
  16.6 0.9 turn.6.refs_0_
  17.5 0.9 turn.7.refs_0_
  18.4 8.0 %collective-permute-done.2 = bf16[1,512,2048]{2,1,0:T(8,128)(2,1)} collective-permute-done((bf16[1,512,2048]{2,1,0:T(8,128)(2,1)}, bf16[1,512,2048]{2,1,0:T(8,128)(2,1)}, u32[]{:S(2)}, u32[]{:S(2)}) %collective-permute-start.2) | collective-permute-done | bytes 2097184 | tf_op jit(solution)/shard_map/ppermute | solution.py:20
  26.4 3.0 %prior_parts.1 = (bf16[512,2048]{1,0:T(8,128)(2,1)S(1)}, bf16[512,1536]{1,0:T(8,128)(2,1)S(1)}, bf16[512,1024]{1,0:T(8,128)(2,1)S(1)}, bf16[512,512]{1,0:T(8,128)(2,1)S(1)}) custom-call(s32[5]{0:T(128)S(1)} %stack.16.place_ref, bf16[512,2048]{1,0:T(8,128)(2,1)} %bitcast.6.shifted_ref, bf16[512,2048]{1,0:T(8,128)(2,1)S(1)} %bitcast.13), custom_call_target="tpu_custom_call" | custom-call | flops 1048576 | bytes 65536 | tf_op jit(solution)/shard_map/prior_parts/pallas_call | solution.py:283
  29.5 3.6 %collective-permute-start.5 = (bf16[512,1536]{1,0:T(8,128)(2,1)S(1)}, bf16[512,1536]{1,0:T(8,128)(2,1)S(1)}, u32[]{:S(2)}, u32[]{:S(2)}) collective-permute-start(bf16[512,1536]{1,0:T(8,128)(2,1)S(1)} %get-tuple-element.25), channel_id=1, source_target_pairs={{0,1},{7,6},{8,9},{15,14},{16,17},{23,22},{24,25},{31,30}} | collective-permute-start | bytes 4718600 | tf_op jit(solution)/shard_map/ppermute | solution.py:101
  34.5 2.8 %couple_here.2.coupled_ref.refs_0_ = bf16[512,2048]{1,0:T(8,128)(2,1)S(1)} custom-call(s32[5]{0:T(128)S(1)} %stack.16.place_ref, f32[1]{0:T(128)S(6)} %copy.19.rate_ref.refs_0_, s32[1,2048]{1,0:T(1,128)S(1)} %bitcast.17, bf16[512,2048]{1,0:T(8,128)(2,1)} %collective-permute-done.1.refs_2_), custom_call_target="tpu_custom_call" | custom-call | flops 1048576 | bytes 65536 | tf_op jit(solution)/shard_map/couple_here/pallas_call | solution.py:113
  37.3 1.2 turn.8.refs_0_
  39.2 1.2 turn.9.refs_1_.right_ref.refs_0_
  41.2 12.4 %collective-permute-done.5.far_zero = bf16[512,1536]{1,0:T(8,128)(2,1)S(1)} collective-permute-done((bf16[512,1536]{1,0:T(8,128)(2,1)S(1)}, bf16[512,1536]{1,0:T(8,128)(2,1)S(1)}, u32[]{:S(2)}, u32[]{:S(2)}) %collective-permute-start.5) | collective-permute-done | bytes 1572896 | tf_op jit(solution)/shard_map/ppermute | solution.py:101
  56.0 1.3 collective-permute-start.6
  58.4 0.8 collective-permute-start.10
  62.3 1.3 collective-permute-start.9
  63.6 0.9 turn.10.refs_0_
  64.5 0.9 turn.11.refs_1_
  66.7 22.2 %collective-permute-done.6.q0 = bf16[512,1536]{1,0:T(8,128)(2,1)S(1)} collective-permute-done((bf16[512,1536]{1,0:T(8,128)(2,1)S(1)}, bf16[512,1536]{1,0:T(8,128)(2,1)S(1)}, u32[]{:S(2)}, u32[]{:S(2)}) %collective-permute-start.6) | collective-permute-done | bytes 1572896 | tf_op jit(solution)/shard_map/ppermute | solution.py:101
  88.9 0.9 collective-permute-start.12
  90.9 36.7 %collective-permute-done.9.q0_last = bf16[512,512]{1,0:T(8,128)(2,1)S(1)} collective-permute-done((bf16[512,512]{1,0:T(8,128)(2,1)S(1)}, bf16[512,512]{1,0:T(8,128)(2,1)S(1)}, u32[]{:S(2)}, u32[]{:S(2)}) %collective-permute-start.9) | collective-permute-done | bytes 524320 | tf_op jit(solution)/shard_map/ppermute | solution.py:101
  127.6 3.3 %final.1 = (bf16[512,2048]{1,0:T(8,128)(2,1)}, f32[1,512]{1,0:T(1,128)}) custom-call(s32[5]{0:T(128)S(1)} %stack.16.place_ref, bf16[512,2048]{1,0:T(8,128)(2,1)S(1)} %bitcast.12, bf16[512,2048]{1,0:T(8,128)(2,1)S(1)} %bitcast.14, bf16[512,1536]{1,0:T(8,128)(2,1)S(1)} %collective-permute-done.6.q0, bf16[512,512]{1,0:T(8,128)(2,1)S(1)} %collective-permute-done.9.q0_last, ...), custom_call_target="tpu_custom_call" | custom-call | flops 1048576 | bytes 65536 | tf_op jit(solution)/shard_map/final/pallas_call | solution.py:432
  (40 shorter events, 12.5 us)
Async XLA Ops:
  0.6 25.8 %collective-permute-start.2 = (bf16[1,512,2048]{2,1,0:T(8,128)(2,1)}, bf16[1,512,2048]{2,1,0:T(8,128)(2,1)}, u32[]{:S(2)}, u32[]{:S(2)}) collective-permute-start(bf16[1,512,2048]{2,1,0:T(8,128)(2,1)} %param.8), channel_id=1, source_target_pairs={{4,0},{8,4},{12,8},{5,1},{9,5},{13,9},{6,2},{10,6},{14,10},{7,3},{... | collective-permute-start | bytes 6291464 | tf_op jit(solution)/shard_map/ppermute | solution.py:20
  2.6 31.9 %collective-permute-start.1 = (bf16[512,2048]{1,0:T(8,128)(2,1)}, bf16[512,2048]{1,0:T(8,128)(2,1)}, u32[]{:S(2)}, u32[]{:S(2)}) collective-permute-start(bf16[512,2048]{1,0:T(8,128)(2,1)} %bitcast.8), channel_id=1, source_target_pairs={{2,1},{5,6},{10,9},{13,14},{18,17},{21,22},{26,25},{29,30}} | collective-permute-start | bytes 6291464 | tf_op jit(solution)/shard_map/ppermute | solution.py:101
  4.5 34.0 %collective-permute-start = (bf16[512,2048]{1,0:T(8,128)(2,1)}, bf16[512,2048]{1,0:T(8,128)(2,1)S(1)}, u32[]{:S(2)}, u32[]{:S(2)}) collective-permute-start(bf16[512,2048]{1,0:T(8,128)(2,1)} %bitcast.9), channel_id=1, source_target_pairs={{0,1},{7,6},{8,9},{15,14},{16,17},{23,22},{24,25},{31,30}} | collective-permute-start | bytes 6291464 | tf_op jit(solution)/shard_map/ppermute | solution.py:101
  9.5 1.6 %copy-start = (bf16[1,512,2048]{2,1,0:T(8,128)(2,1)S(1)}, bf16[1,512,2048]{2,1,0:T(8,128)(2,1)}, u32[]{:S(2)}) copy-start(bf16[1,512,2048]{2,1,0:T(8,128)(2,1)} %param.9) | copy-start | bytes 6291460
  11.1 0.7 copy-start.3
  17.5 8.9 %copy-start.2 = (bf16[1,512,2048]{2,1,0:T(8,128)(2,1)S(1)}, bf16[1,512,2048]{2,1,0:T(8,128)(2,1)}, u32[]{:S(2)}) copy-start(bf16[1,512,2048]{2,1,0:T(8,128)(2,1)} %param.7) | copy-start | bytes 6291460
  26.4 8.1 %copy-start.4 = (s32[2048]{0:T(1024)S(1)}, s32[2048]{0:T(1024)}, u32[]{:S(2)}) copy-start(s32[2048]{0:T(1024)} %param.13) | copy-start | bytes 24580
  29.5 24.1 %collective-permute-start.5 = (bf16[512,1536]{1,0:T(8,128)(2,1)S(1)}, bf16[512,1536]{1,0:T(8,128)(2,1)S(1)}, u32[]{:S(2)}, u32[]{:S(2)}) collective-permute-start(bf16[512,1536]{1,0:T(8,128)(2,1)S(1)} %get-tuple-element.25), channel_id=1, source_target_pairs={{0,1},{7,6},{8,9},{15,14},{16,17},{23,22},{24,25},{31,30}} | collective-permute-start | bytes 4718600 | tf_op jit(solution)/shard_map/ppermute | solution.py:101
  33.1 7.4 %collective-permute-start.3 = (bf16[512,1024]{1,0:T(8,128)(2,1)S(1)}, bf16[512,1024]{1,0:T(8,128)(2,1)S(1)}, u32[]{:S(2)}, u32[]{:S(2)}) collective-permute-start(bf16[512,1024]{1,0:T(8,128)(2,1)S(1)} %get-tuple-element.24), channel_id=1, source_target_pairs={{2,1},{5,6},{10,9},{13,14},{18,17},{21,22},{26,25},{29,30}} | collective-permute-start | bytes 3145736 | tf_op jit(solution)/shard_map/ppermute | solution.py:101
  33.8 6.6 %collective-permute-start.4 = (bf16[512,512]{1,0:T(8,128)(2,1)S(1)}, bf16[512,512]{1,0:T(8,128)(2,1)S(1)}, u32[]{:S(2)}, u32[]{:S(2)}) collective-permute-start(bf16[512,512]{1,0:T(8,128)(2,1)S(1)} %get-tuple-element.20), channel_id=1, source_target_pairs={{3,1},{4,6},{11,9},{12,14},{19,17},{20,22},{27,25},{28,30}} | collective-permute-start | bytes 1572872 | tf_op jit(solution)/shard_map/ppermute | solution.py:101
  40.5 18.7 %collective-permute-start.7 = (bf16[256,2048]{1,0:T(8,128)(2,1)S(1)}, bf16[256,2048]{1,0:T(8,128)(2,1)S(1)}, u32[]{:S(2)}, u32[]{:S(2)}) collective-permute-start(bf16[256,2048]{1,0:T(8,128)(2,1)S(1)} %couple.3.coupled_ref.refs_0_), channel_id=1, source_target_pairs={{3,1},{4,6},{11,9},{12,14},{19,17},{20,22},{27,25},{28,30}} | collective-permute-start | bytes 3145736 | tf_op jit(solution)/shard_map/ppermute | solution.py:101
  53.6 5.6 %collective-permute-start.8 = (bf16[256,2048]{1,0:T(8,128)(2,1)S(1)}, bf16[256,2048]{1,0:T(8,128)(2,1)S(1)}, u32[]{:S(2)}, u32[]{:S(2)}) collective-permute-start(bf16[256,2048]{1,0:T(8,128)(2,1)S(1)} %couple.2.coupled_ref.refs_1_), channel_id=1, source_target_pairs={{3,1},{4,6},{11,9},{12,14},{19,17},{20,22},{27,25},{28,30}} | collective-permute-start | bytes 3145736 | tf_op jit(solution)/shard_map/ppermute | solution.py:101
  56.0 32.9 %collective-permute-start.6 = (bf16[512,1536]{1,0:T(8,128)(2,1)S(1)}, bf16[512,1536]{1,0:T(8,128)(2,1)S(1)}, u32[]{:S(2)}, u32[]{:S(2)}) collective-permute-start(bf16[512,1536]{1,0:T(8,128)(2,1)S(1)} %multiply.9.zero_ref.q01), channel_id=1, source_target_pairs={{1,0},{6,7},{9,8},{14,15},{17,16},{22,23},{25,24},{30,31}} | collective-permute-start | bytes 4718600 | tf_op jit(solution)/shard_map/ppermute | solution.py:101
  58.4 32.5 %collective-permute-start.10 = (bf16[512,1536]{1,0:T(8,128)(2,1)S(1)}, bf16[512,1536]{1,0:T(8,128)(2,1)S(1)}, u32[]{:S(2)}, u32[]{:S(2)}) collective-permute-start(bf16[512,1536]{1,0:T(8,128)(2,1)S(1)} %product_two.1.q21), channel_id=1, source_target_pairs={{1,2},{6,5},{9,10},{14,13},{17,18},{22,21},{25,26},{30,29}} | collective-permute-start | bytes 4718600 | tf_op jit(solution)/shard_map/ppermute | solution.py:101
  60.3 5.7 %collective-permute-start.11 = (bf16[512,512]{1,0:T(8,128)(2,1)S(1)}, bf16[512,512]{1,0:T(8,128)(2,1)S(1)}, u32[]{:S(2)}, u32[]{:S(2)}) collective-permute-start(bf16[512,512]{1,0:T(8,128)(2,1)S(1)} %multiply.12), channel_id=1, source_target_pairs={{1,3},{6,4},{9,11},{14,12},{17,19},{22,20},{25,27},{30,28}} | collective-permute-start | bytes 1572872 | tf_op jit(solution)/shard_map/ppermute | solution.py:101
  61.6 66.0 %collective-permute-start.13 = (bf16[512,1024]{1,0:T(8,128)(2,1)S(1)}, bf16[512,1024]{1,0:T(8,128)(2,1)S(1)}, u32[]{:S(2)}, u32[]{:S(2)}) collective-permute-start(bf16[512,1024]{1,0:T(8,128)(2,1)S(1)} %get-tuple-element.32.q31), channel_id=1, source_target_pairs={{1,3},{6,4},{9,11},{14,12},{17,19},{22,20},{25,27},{30,28}} | collective-permute-start | bytes 3145736 | tf_op jit(solution)/shard_map/ppermute | solution.py:101
  62.3 65.3 %collective-permute-start.9 = (bf16[512,512]{1,0:T(8,128)(2,1)S(1)}, bf16[512,512]{1,0:T(8,128)(2,1)S(1)}, u32[]{:S(2)}, u32[]{:S(2)}) collective-permute-start(bf16[512,512]{1,0:T(8,128)(2,1)S(1)} %get-tuple-element.28), channel_id=1, source_target_pairs={{1,0},{6,7},{9,8},{14,15},{17,16},{22,23},{25,24},{30,31}} | collective-permute-start | bytes 1572872 | tf_op jit(solution)/shard_map/ppermute | solution.py:101
  66.0 24.9 %collective-permute-start.14 = (bf16[512,512]{1,0:T(8,128)(2,1)S(1)}, bf16[512,512]{1,0:T(8,128)(2,1)S(1)}, u32[]{:S(2)}, u32[]{:S(2)}) collective-permute-start(bf16[512,512]{1,0:T(8,128)(2,1)S(1)} %multiply.13), channel_id=1, source_target_pairs={{1,3},{6,4},{9,11},{14,12},{17,19},{22,20},{25,27},{30,28}} | collective-permute-start | bytes 1572872 | tf_op jit(solution)/shard_map/ppermute | solution.py:101
  88.9 38.7 %collective-permute-start.12 = (bf16[512,512]{1,0:T(8,128)(2,1)S(1)}, bf16[512,512]{1,0:T(8,128)(2,1)S(1)}, u32[]{:S(2)}, u32[]{:S(2)}) collective-permute-start(bf16[512,512]{1,0:T(8,128)(2,1)S(1)} %collective-permute-done.11.q3_two), channel_id=1, source_target_pairs={{3,2},{4,5},{11,10},{12,13},{19,18},{20,21},{27,26},{28,29}} | collective-permute-start | bytes 1572872 | tf_op jit(solution)/shard_map/ppermute | solution.py:101
  90.3 37.3 %copy-start.1 = (bf16[1,512,2048]{2,1,0:T(8,128)(2,1)S(1)}, bf16[1,512,2048]{2,1,0:T(8,128)(2,1)}, u32[]{:S(2)}) copy-start(bf16[1,512,2048]{2,1,0:T(8,128)(2,1)} %param.9) | copy-start | bytes 6291460

commit v7 on v6

--- a/solution.py
+++ b/solution.py
@@ -222,31 +222,54 @@
     )(place, half, across, zero)
 
 
-def three_kernel(place_ref, left_ref, right_ref, out_ref, zero_ref):
-    width = zero_ref.shape[1]
-    multiply_kernel(lambda odd: 2 * odd, 2, 1, place_ref, left_ref, right_ref, out_ref)
-
-    @pl.when(place_ref[1] == 1)
-    def _():
-        zero_ref[...] = out_ref[:, pl.ds(pl.multiple_of(place_ref[0] * width, 128), width)]
-
-
-def product_three(place, half, across):
+def ends_kernel(place_ref, left_ref, right_ref, zero_ref, two_ref):
+    for block, out_ref in ((0, zero_ref), (2, two_ref)):
+        first = lambda odd: turned(block, odd)
+        multiply_kernel(first, 1, 1, place_ref, left_ref, right_ref, out_ref)
+
+
+def product_ends(place, half, across):
     rows = half.shape[0]
     width = across.shape[0] // 4
     vmem = pl.BlockSpec(memory_space=pltpu.VMEM)
     return pl.pallas_call(
-        three_kernel,
-        out_shape=(
-            jax.ShapeDtypeStruct((rows, 2 * width), BF16),
-            jax.ShapeDtypeStruct((rows, width), BF16),
-        ),
+        ends_kernel,
+        out_shape=(jax.ShapeDtypeStruct((rows, width), BF16),) * 2,
         in_specs=[pl.BlockSpec(memory_space=pltpu.SMEM)] + [vmem] * 2,
         out_specs=(vmem, vmem),
         compiler_params=pltpu.CompilerParams(vmem_limit_bytes=6 * MIB),
         cost_estimate=LIGHT,
-        name="product_three",
+        name="product_ends",
     )(place, half, across)
+
+
+def other_kernel(place_ref, left_ref, right_ref, zero_ref, out_ref):
+    odd = place_ref[0]
+    width = zero_ref.shape[1]
+
+    @pl.when(place_ref[1] == 1)
+    def _():
+        out_ref[:, pl.ds(pl.multiple_of(odd * width, 128), width)] = zero_ref[...]
+        source = pl.multiple_of((1 + odd) * width, 128)
+        target = pl.multiple_of((1 - odd) * width, 128)
+        out_ref[:, pl.ds(target, width)] = jnp.dot(
+            left_ref[...], right_ref[:, pl.ds(source, width)], preferred_element_type=F32
+        ).astype(BF16)
+
+
+def product_other(place, half, across, zero):
+    rows = half.shape[0]
+    width = across.shape[0] // 4
+    vmem = pl.BlockSpec(memory_space=pltpu.VMEM)
+    return pl.pallas_call(
+        other_kernel,
+        out_shape=jax.ShapeDtypeStruct((rows, 2 * width), BF16),
+        in_specs=[pl.BlockSpec(memory_space=pltpu.SMEM)] + [vmem] * 3,
+        out_specs=vmem,
+        compiler_params=pltpu.CompilerParams(vmem_limit_bytes=6 * MIB),
+        cost_estimate=LIGHT,
+        name="product_other",
+    )(place, half, across, zero)
 
 
 def prior_kernel(place_ref, shifted_ref, sigma_ref, out_ref):
@@ -259,7 +282,7 @@
         out_ref[...] = sigma_ref[...]
 
 
-def parts_kernel(place_ref, shifted_ref, sigma_ref, row_ref, far_ref, near_ref, last_ref):
+def parts_kernel(place_ref, shifted_ref, sigma_ref, row_ref, two_ref, zero_ref, last_ref):
     odd = place_ref[0]
     width = last_ref.shape[1]
 
@@ -267,11 +290,12 @@
         return pl.ds(pl.multiple_of(block * width, 128), count * width)
 
     prior_kernel(place_ref, shifted_ref, sigma_ref, row_ref)
-    near = row_ref[:, at(2 - 2 * odd, 2)]
-    near_ref[...] = near
-    far_ref[:, width:] = near
-    far_ref[:, :width] = row_ref[:, at(3 * odd)]
-    last_ref[...] = row_ref[:, at(3 - 3 * odd)]
+    first, last = row_ref[:, at(3 * odd)], row_ref[:, at(3 - 3 * odd)]
+    two_ref[:, :width] = first
+    two_ref[:, width:] = row_ref[:, at(2 - 2 * odd, 2)]
+    zero_ref[:, :width] = first
+    zero_ref[:, width:] = last
+    last_ref[...] = last
 
 
 def prior_parts(place, shifted, sigma):
@@ -302,29 +326,28 @@
     )(place, shifted, sigma)
 
 
-def assemble_kernel(place_ref, own, near_two, last_three, far_zero, out_ref):
+def assemble_kernel(place_ref, own, two, zero, three, out_ref):
     @pl.when(place_ref[1] == 1)
     def _():
         odd = place_ref[0]
-        width = last_three.shape[1]
-
-        def at(block):
-            return pl.ds(pl.multiple_of(block * width, 128), width)
+        width = three.shape[1]
+
+        def at(block, count=1):
+            return pl.ds(pl.multiple_of(block * width, 128), count * width)
 
         near = 2 * (1 - odd)
-        half = pl.ds(pl.multiple_of(near * width, 128), 2 * width)
         row = [turned(block, odd) for block in range(4)]
         out_ref[at(row[1]), :] = own[...]
-        out_ref[at(row[2]), half] = near_two[...]
-        out_ref[at(row[0]), at(row[0])] = far_zero[:, :width]
-        out_ref[at(row[0]), half] = far_zero[:, width:]
-        out_ref[at(row[3]), at(row[3])] = last_three[...]
-        for step in range(2):
-            out_ref[at(near + step), at(row[1])] = own[:, at(near + step)].T
-            piece = slice((1 + step) * width, (2 + step) * width)
-            out_ref[at(near + step), at(row[0])] = far_zero[:, piece].T
-        out_ref[at(row[0]), at(row[1])] = own[:, at(row[0])].T
-        out_ref[at(row[3]), at(row[2])] = near_two[:, at(1 - odd)].T
+        out_ref[at(row[2]), at(row[0])] = two[:, :width]
+        out_ref[at(row[2]), at(near, 2)] = two[:, width:]
+        out_ref[at(row[0]), at(row[0])] = zero[:, :width]
+        out_ref[at(row[0]), at(row[3])] = zero[:, width:]
+        out_ref[at(row[3]), at(row[3])] = three[...]
+        for block in (0, 2, 3):
+            out_ref[at(row[block]), at(row[1])] = own[:, at(row[block])].T
+        out_ref[at(row[0]), at(row[2])] = two[:, :width].T
+        out_ref[at(row[3]), at(row[2])] = two[:, at(2 - odd)].T
+        out_ref[at(row[3]), at(row[0])] = zero[:, width:].T
 
 
 def assemble(place, *parts):
@@ -341,75 +364,99 @@
     )(place, *parts)
 
 
-def final_kernel(
-    place_ref, pivot_ref, sigma_ref,
-    q0, q0_last, q2, q2_zero, q2_last, q3_two, q3_other, q3_last,
-    q01, q11, q21, q31,
-    out_ref, var_ref,
-):
+def finish_kernel(place_ref, pivot_ref, *refs):
+    sigma_ref, q0, q2, q2_zero, q3_two, q3_other, q01, q11, q21, out_ref, var_ref = refs
     rows, nodes = pivot_ref.shape
     width = nodes // 4
     odd, place = place_ref[0], place_ref[1]
     here = pl.multiple_of(pl.program_id(0) * rows, 128)
+    diagonal = diagonal_of(rows)
+
+    def at(block, count=1):
+        return pl.ds(pl.multiple_of(block * width, 128), count * width)
+
+    def own(block):
+        return pl.ds(pl.multiple_of(block * width + here, 128), rows)
+
+    def add(columns, product):
+        out_ref[:, columns] = (pivot_ref[:, columns].astype(F32) + product.astype(F32)).astype(BF16)
+
+    def trace(product):
+        var_ref[...] = diagonal(pivot_ref[:, own(place_ref[2])].astype(F32) + product.astype(F32))
+
+    active = place_ref[4] != 0
+
+    @pl.when(active & (place == 0))
+    def _():
+        add(at(odd, 3), q0[...])
+        trace(q0[:, own(2 * odd)])
+
+    @pl.when(active & (place == 1))
+    def _():
+        add(at(turned(0, odd)), q01[...].T)
+        add(at(turned(1, odd)), q11[...])
+        add(at(turned(2, odd)), q21[...].T)
+        trace(q11[:, pl.ds(here, rows)])
+
+    @pl.when(active & (place == 2))
+    def _():
+        add(at(turned(0, odd)), q2_zero[:, pl.ds(here, rows)].T)
+        add(at(1, 2), q2[...])
+        trace(q2[:, own(1 - odd)])
+
+    @pl.when(active & (place == 3))
+    def _():
+        add(at(2 * odd, 2), q3_other[...])
+        add(at(turned(2, odd)), q3_two[...])
+
+    @pl.when(jnp.logical_not(active))
+    def _():
+        out_ref[...] = sigma_ref[...]
+        var_ref[...] = diagonal(sigma_ref[:, own(place_ref[2])].astype(F32))
+
+
+def diagonal_of(rows):
     square = (rows, rows)
     on_diagonal = lax.broadcasted_iota(jnp.int32, square, 0) == lax.broadcasted_iota(
         jnp.int32, square, 1
     )
-
-    def at(block, count=1):
-        return pl.ds(pl.multiple_of(block * width, 128), count * width)
-
-    def own(block):
-        return pl.ds(pl.multiple_of(block * width + here, 128), rows)
-
-    def diagonal(value):
-        return jnp.sum(jnp.where(on_diagonal, value, 0.0), axis=0, keepdims=True)
-
-    def add(columns, product):
-        out_ref[:, columns] = (pivot_ref[:, columns].astype(F32) + product.astype(F32)).astype(BF16)
-
-    def trace(product):
-        var_ref[...] = diagonal(
-            pivot_ref[:, own(place_ref[2])].astype(F32) + product.astype(F32)
+    return lambda value: jnp.sum(jnp.where(on_diagonal, value, 0.0), axis=0, keepdims=True)
+
+
+def last_kernel(place_ref, pivot_ref, *refs):
+    q0_last, q2_last, q3_last, q31, old_ref, old_var_ref, out_ref, var_ref = refs
+    rows = pivot_ref.shape[0]
+    place = place_ref[1]
+    here = pl.ds(pl.multiple_of(pl.program_id(0) * rows, 128), rows)
+    active = place_ref[4] != 0
+
+    def add(product):
+        out_ref[...] = (pivot_ref[...].astype(F32) + product.astype(F32)).astype(BF16)
+
+    out_ref[...] = old_ref[...]
+    var_ref[...] = old_var_ref[...]
+
+    @pl.when(active & (place == 0))
+    def _():
+        add(q0_last[:, here].T)
+
+    @pl.when(active & (place == 1))
+    def _():
+        add(q31[...].T)
+
+    @pl.when(active & (place == 2))
+    def _():
+        add(q2_last[:, here].T)
+
+    @pl.when(active & (place == 3))
+    def _():
+        add(q3_last[...])
+        var_ref[...] = diagonal_of(rows)(
+            pivot_ref[:, here].astype(F32) + q3_last[:, here].astype(F32)
         )
 
-    active = place_ref[4] != 0
-
-    @pl.when(active & (place == 0))
-    def _():
-        add(at(odd, 3), q0[...])
-        add(at(turned(3, odd)), q0_last[:, pl.ds(here, rows)].T)
-        trace(q0[:, own(2 * odd)])
-
-    @pl.when(active & (place == 1))
-    def _():
-        add(at(turned(0, odd)), q01[...].T)
-        add(at(turned(1, odd)), q11[...])
-        add(at(turned(2, odd)), q21[...].T)
-        add(at(turned(3, odd)), q31[...].T)
-        trace(q11[:, pl.ds(here, rows)])
-
-    @pl.when(active & (place == 2))
-    def _():
-        add(at(turned(0, odd)), q2_zero[:, pl.ds(here, rows)].T)
-        add(at(1, 2), q2[...])
-        add(at(turned(3, odd)), q2_last[:, pl.ds(here, rows)].T)
-        trace(q2[:, own(1 - odd)])
-
-    @pl.when(active & (place == 3))
-    def _():
-        add(at(2 * odd, 2), q3_other[...])
-        add(at(turned(2, odd)), q3_two[...])
-        add(at(turned(3, odd)), q3_last[...])
-        trace(q3_last[:, pl.ds(here, rows)])
-
-    @pl.when(place_ref[4] == 0)
-    def _():
-        out_ref[...] = sigma_ref[...]
-        var_ref[...] = diagonal(sigma_ref[:, own(place_ref[2])].astype(F32))
-
-
-def final(place, pivot, sigma, received, kept):
+
+def finish(place, pivot, sigma, products):
     rows, nodes = pivot.shape
     chunk = 128
     width = nodes // 4
@@ -428,9 +475,8 @@
             ),
         )
 
-    whole = lambda block: pl.BlockSpec((rows, width), lambda i, place: (0, block))
-    return pl.pallas_call(
-        final_kernel,
+    return pl.pallas_call(
+        finish_kernel,
         out_shape=(
             jax.ShapeDtypeStruct((rows, nodes), BF16),
             jax.ShapeDtypeStruct((1, rows), F32),
@@ -440,21 +486,15 @@
             grid=(rows // chunk,),
             in_specs=[
                 pl.BlockSpec((chunk, nodes), lambda i, place: (i, 0)),
-                pl.BlockSpec(
-                    (chunk, nodes), lambda i, place: (jnp.where(place[4] == 0, i, 0), 0)
-                ),
+                pl.BlockSpec((chunk, nodes), lambda i, place: (jnp.where(place[4] == 0, i, 0), 0)),
                 picked(0, 3),
-                whole(0),
                 picked(2, 2),
-                whole(2),
-                whole(0),
+                pl.BlockSpec((rows, width), lambda i, place: (0, 2)),
                 picked(3, 1),
                 picked(3, 2),
-                picked(3, 1),
                 turned_block(lambda odd: 1),
                 picked(1, 1),
                 turned_block(lambda odd: odd),
-                turned_block(lambda odd: 1 - odd),
             ],
             out_specs=(
                 pl.BlockSpec((chunk, nodes), lambda i, place: (i, 0)),
@@ -463,8 +503,45 @@
         ),
         compiler_params=pltpu.CompilerParams(vmem_limit_bytes=12 * MIB),
         cost_estimate=LIGHT,
-        name="final",
-    )(place, pivot, sigma, *received, *kept)
+        name="finish",
+    )(place, pivot, sigma, *products)
+
+
+def finish_last(place, pivot, products, covariance, variances):
+    rows, nodes = pivot.shape
+    chunk = 128
+    width = nodes // 4
+    column = lambda place: 3 - 3 * place[0]
+    whole = pl.BlockSpec((rows, width), lambda i, place: (0, 0))
+    block = pl.BlockSpec((chunk, width), lambda i, place: (i, column(place)))
+    variance = pl.BlockSpec((1, chunk), lambda i, place: (0, i))
+    return pl.pallas_call(
+        last_kernel,
+        out_shape=(
+            jax.ShapeDtypeStruct((rows, nodes), BF16),
+            jax.ShapeDtypeStruct((1, rows), F32),
+        ),
+        grid_spec=pltpu.PrefetchScalarGridSpec(
+            num_scalar_prefetch=1,
+            grid=(rows // chunk,),
+            in_specs=[
+                block,
+                whole,
+                whole,
+                pl.BlockSpec((chunk, width), lambda i, place: (i, 0)),
+                pl.BlockSpec(
+                    (rows, chunk), lambda i, place: (0, (1 - place[0]) * (width // chunk) + i)
+                ),
+                block,
+                variance,
+            ],
+            out_specs=(block, variance),
+        ),
+        input_output_aliases={6: 0, 7: 1},
+        compiler_params=pltpu.CompilerParams(vmem_limit_bytes=12 * MIB),
+        cost_estimate=LIGHT,
+        name="finish_last",
+    )(place, pivot, *products, covariance, variances)
 
 
 def owned(sigma_next, separator, inverse_pivot, coupling_rate, lengths, step_index, node_class):
@@ -476,24 +553,24 @@
     after = lambda value, *others: lax.optimization_barrier((value, *others))[0]
 
     shifted = passed_along(separator, "dom", -1)[0]
+    p0 = moved(pivot, 0, 1)
     p2 = moved(pivot, 2, 1)
-    p0 = moved(pivot, 0, 1)
     c1 = [couple(pivot, node_class, coupling_rate, part, 2) for part in range(2)]
     across = turn(place, 1, 0, c1[0], None)
     across = turn(place, 1, 1, c1[1], across)
 
-    row, far, near, last = prior_parts(place, after(shifted, across), sigma)
-    far_zero, near_two, last_three = moved(far, 0, 1), moved(near, 2, 1), moved(last, 3, 1)
-
-    c2 = couple_here(place, after(p2, last), node_class, coupling_rate)
+    row, two, zero, last = prior_parts(place, after(shifted, across), sigma)
+    zero, two, three = moved(zero, 0, 1), moved(two, 2, 1), moved(last, 3, 1)
+
+    c0 = couple_here(place, after(p0, last), node_class, coupling_rate)
+    across = turn(place, 0, 0, c0, across)
+    c2 = couple_here(place, after(p2, across), node_class, coupling_rate)
     across = turn(place, 2, 0, c2, across)
-    c0 = couple_here(place, after(p0, across), node_class, coupling_rate)
-    across = turn(place, 0, 0, c0, across)
     c3 = [
-        moved(after(c1[0], last_three, near_two, across), 3, 1),
-        moved(after(c1[1], far_zero), 3, 1),
+        moved(after(c1[0], three, zero, across), 3, 1),
+        moved(after(c1[1], two), 3, 1),
     ]
-    prior = assemble(place, row, near_two, last_three, far_zero)
+    prior = assemble(place, row, two, zero, three)
 
     h0 = multiply(place, [c0], prior)
     q0_own = multiply(place, [h0], across, lambda odd: odd, 3)
@@ -503,20 +580,21 @@
     q2 = moved(q2_own, 1, 2)
 
     h3 = multiply(place, c3, prior)
-    q3_two = moved(multiply(place, [h3], across, lambda odd: 2 - odd, 1), 1, 3)
-    q3_own, q30 = product_three(place, h3, across)
+    q30, q32 = product_ends(place, h3, across)
+    q0_last, q3_two = moved(q30, 1, 0), moved(q32, 1, 3)
+    q3_own = product_other(place, h3, across, q30)
     q3_other = moved(q3_own, 1, 3)
-    q0_last = moved(q30, 1, 0)
-    across = turn(place, 3, 0, c3[0], after(across, q30))
-    across = turn(place, 3, 1, c3[1], across)
+    across = turn(place, 3, 0, c3[0], after(across, q3_own, q0_last))
+    across = turn(place, 3, 1, c3[1], after(across, q3_two))
     q33 = multiply(place, [h3], across, lambda odd: 3 - 3 * odd, 1)
     q3_last = moved(q33, 1, 3)
-    q2_last = moved(after(q3_two, q0, q33), 3, 2)
     h1 = multiply(place, [after(c1[0], q33), c1[1]], prior)
     q11 = multiply(place, [h1], across, lambda odd: 1 + odd, 1)
-    received = (q0, q0_last, q2, q2, q2_last, q3_two, q3_other, q3_last)
-    kept = (q0_own, q11, q2_own, q3_own)
-    covariance, variances = final(place, pivot, sigma, received, kept)
+    q2_last = moved(after(q3_two, q0, q33), 3, 2)
+    products = (q0, q2, q2, q3_two, q3_other, q0_own, q11, q2_own)
+    covariance, variances = finish(place, pivot, sigma, products)
+    products = (q0_last, q2_last, q3_last, q3_own)
+    covariance, variances = finish_last(place, pivot, products, covariance, variances)
     return (covariance[None], variances)
 
 

time: 131 us -> 154 us (1.18)
  the two profiles are of different devices: /device:TPU:2 before, /device:TPU:1 now
where the time goes in v7:
time: 154 us; the launch traced here: 152 us
  waiting for transfers between devices  72 us (47%)
  starting transfers between devices  45.3 us (29%)
  Pallas kernels  29.1 us (19%)
  between operations  2.95 us (2%)
  local copies, waits for them, and re-layouts  2.39 us (2%)
    ppermute x14, waiting for transfers between devices, moved(): lax.ppermute(value, ('dom', 'col'), route(source, target, lax.axis_size('...  59.2 us
    ppermute x14, starting transfers between devices, moved(): lax.ppermute(value, ('dom', 'col'), route(source, target, lax.axis_size('...  43.3 us
    ppermute x1, waiting for transfers between devices, passed_along(): lax.ppermute(value, axis, [(source, source + steps) for source in range(i...  12.8 us
    pallas_call x6, Pallas kernels, turn(): pl.pallas_call(turn_kernel, out_shape=jax.ShapeDtypeStruct((nodes, nodes)...  5.99 us
    pallas_call x2, Pallas kernels, couple(): pl.pallas_call(couple_kernel, out_shape=jax.ShapeDtypeStruct((rows, nodes...  4.81 us
    pallas_call x7, Pallas kernels, multiply(): pl.pallas_call(functools.partial(multiply_kernel, first, count, len(lefts...  4.03 us
    pallas_call x1, Pallas kernels, finish_last(): pl.pallas_call(last_kernel, out_shape=(jax.ShapeDtypeStruct((rows, nodes)...  3.89 us
    pallas_call x2, Pallas kernels, couple_here(): pl.pallas_call(kernel, out_shape=jax.ShapeDtypeStruct((rows, nodes), BF16...  3.45 us
  transfers between devices with their start and end apart: 15, of which 6 were waited for; matrix products, arithmetic and copies ran while one was open for 0% of the time, Pallas kernels for 17%

profile of v7, /device:TPU:1, one launch (start us, length us, event | category | flops | bytes accessed | tf_op | source)
XLA Modules:
  0.0 151.8 jit_solution(14652935611878764216)
XLA Ops:
  0.6 2.0 %collective-permute-start = (bf16[1,512,2048]{2,1,0:T(8,128)(2,1)}, bf16[1,512,2048]{2,1,0:T(8,128)(2,1)}, u32[]{:S(2)}, u32[]{:S(2)}) collective-permute-start(bf16[1,512,2048]{2,1,0:T(8,128)(2,1)} %param.8), channel_id=1, source_target_pairs={{4,0},{8,4},{12,8},{5,1},{9,5},{13,9},{6,2},{10,6},{14,10},{7,3},{... | collective-permute-start | bytes 6291464 | tf_op jit(solution)/shard_map/ppermute | solution.py:20
  2.6 2.0 %collective-permute-start.4 = (bf16[512,2048]{1,0:T(8,128)(2,1)}, bf16[512,2048]{1,0:T(8,128)(2,1)}, u32[]{:S(2)}, u32[]{:S(2)}) collective-permute-start(bf16[512,2048]{1,0:T(8,128)(2,1)} %bitcast.8), channel_id=1, source_target_pairs={{0,1},{7,6},{8,9},{15,14},{16,17},{23,22},{24,25},{31,30}} | collective-permute-start | bytes 6291464 | tf_op jit(solution)/shard_map/ppermute | solution.py:101
  7.4 1.6 %copy-done = bf16[1,512,2048]{2,1,0:T(8,128)(2,1)S(1)} copy-done((bf16[1,512,2048]{2,1,0:T(8,128)(2,1)S(1)}, bf16[1,512,2048]{2,1,0:T(8,128)(2,1)}, u32[]{:S(2)}) %copy-start) | copy-done | bytes 2097176
  9.7 2.4 %couple.2.coupled_ref.refs_0_ = bf16[256,2048]{1,0:T(8,128)(2,1)S(1)} custom-call(f32[1]{0:T(128)S(6)} %copy.23.rate_ref.refs_0_, s32[1,2048]{1,0:T(1,128)S(1)} %bitcast.16, bf16[512,2048]{1,0:T(8,128)(2,1)S(1)} %bitcast.10), custom_call_target="tpu_custom_call" | custom-call | flops 1048576 | bytes 65536 | tf_op jit(solution)/shard_map/couple/pallas_call | solution.py:71
  12.1 2.4 %couple.3.coupled_ref.refs_1_ = bf16[256,2048]{1,0:T(8,128)(2,1)S(1)} custom-call(f32[1]{0:T(128)S(6)} %copy.23.rate_ref.refs_0_, s32[1,2048]{1,0:T(1,128)S(1)} %bitcast.17, bf16[512,2048]{1,0:T(8,128)(2,1)S(1)} %bitcast.11), custom_call_target="tpu_custom_call" | custom-call | flops 1048576 | bytes 65536 | tf_op jit(solution)/shard_map/couple/pallas_call | solution.py:71
  16.3 12.8 %collective-permute-done = bf16[1,512,2048]{2,1,0:T(8,128)(2,1)} collective-permute-done((bf16[1,512,2048]{2,1,0:T(8,128)(2,1)}, bf16[1,512,2048]{2,1,0:T(8,128)(2,1)}, u32[]{:S(2)}, u32[]{:S(2)}) %collective-permute-start) | collective-permute-done | bytes 2097184 | tf_op jit(solution)/shard_map/ppermute | solution.py:20
  29.2 2.1 %prior_parts.1 = (bf16[512,2048]{1,0:T(8,128)(2,1)S(1)}, bf16[512,1536]{1,0:T(8,128)(2,1)S(1)}, bf16[512,1024]{1,0:T(8,128)(2,1)S(1)}, bf16[512,512]{1,0:T(8,128)(2,1)S(1)}) custom-call(s32[5]{0:T(128)S(1)} %stack.16.place_ref, bf16[512,2048]{1,0:T(8,128)(2,1)} %bitcast.5.shifted_ref, bf16[512,2048]{1,0:T(8,128)(2,1)S(1)} %bitcast.14), custom_call_target="tpu_custom_call" | custom-call | flops 1048576 | bytes 65536 | tf_op jit(solution)/shard_map/prior_parts/pallas_call | solution.py:307
  32.7 5.3 %collective-permute-start.1 = (bf16[512,512]{1,0:T(8,128)(2,1)S(1)}, bf16[512,512]{1,0:T(8,128)(2,1)S(1)}, u32[]{:S(2)}, u32[]{:S(2)}) collective-permute-start(bf16[512,512]{1,0:T(8,128)(2,1)S(1)} %get-tuple-element.23), channel_id=1, source_target_pairs={{3,1},{4,6},{11,9},{12,14},{19,17},{20,22},{27,25},{28,30}} | collective-permute-start | bytes 1572872 | tf_op jit(solution)/shard_map/ppermute | solution.py:101
  38.1 2.8 %couple_here.2.coupled_ref.refs_0_ = bf16[512,2048]{1,0:T(8,128)(2,1)S(1)} custom-call(s32[5]{0:T(128)S(1)} %stack.16.place_ref, f32[1]{0:T(128)S(6)} %copy.23.rate_ref.refs_0_, s32[1,2048]{1,0:T(1,128)S(1)} %bitcast.18, bf16[512,2048]{1,0:T(8,128)(2,1)} %collective-permute-done.4.refs_2_), custom_call_target="tpu_custom_call" | custom-call | flops 1048576 | bytes 65536 | tf_op jit(solution)/shard_map/couple_here/pallas_call | solution.py:113
  40.9 1.2 turn.8.refs_0_
  42.8 1.2 turn.9.right_ref.refs_1_.refs_0_
  44.0 3.2 %collective-permute-done.1.three = bf16[512,512]{1,0:T(8,128)(2,1)S(1)} collective-permute-done((bf16[512,512]{1,0:T(8,128)(2,1)S(1)}, bf16[512,512]{1,0:T(8,128)(2,1)S(1)}, u32[]{:S(2)}, u32[]{:S(2)}) %collective-permute-start.1) | collective-permute-done | bytes 524320 | tf_op jit(solution)/shard_map/ppermute | solution.py:101
  47.2 7.9 %collective-permute-start.5 = (bf16[256,2048]{1,0:T(8,128)(2,1)S(1)}, bf16[256,2048]{1,0:T(8,128)(2,1)S(1)}, u32[]{:S(2)}, u32[]{:S(2)}) collective-permute-start(bf16[256,2048]{1,0:T(8,128)(2,1)S(1)} %couple.2.coupled_ref.refs_0_), channel_id=1, source_target_pairs={{3,1},{4,6},{11,9},{12,14},{19,17},{20,22},{27,25},{28,30}} | collective-permute-start | bytes 3145736 | tf_op jit(solution)/shard_map/ppermute | solution.py:101
  55.1 18.4 %collective-permute-start.7 = (bf16[256,2048]{1,0:T(8,128)(2,1)S(1)}, bf16[256,2048]{1,0:T(8,128)(2,1)S(1)}, u32[]{:S(2)}, u32[]{:S(2)}) collective-permute-start(bf16[256,2048]{1,0:T(8,128)(2,1)S(1)} %couple.3.coupled_ref.refs_1_), channel_id=1, source_target_pairs={{3,1},{4,6},{11,9},{12,14},{19,17},{20,22},{27,25},{28,30}} | collective-permute-start | bytes 3145736 | tf_op jit(solution)/shard_map/ppermute | solution.py:101
  77.9 7.3 %collective-permute-done.7.refs_1_.coupled_ref = bf16[256,2048]{1,0:T(8,128)(2,1)S(1)} collective-permute-done((bf16[256,2048]{1,0:T(8,128)(2,1)S(1)}, bf16[256,2048]{1,0:T(8,128)(2,1)S(1)}, u32[]{:S(2)}, u32[]{:S(2)}) %collective-permute-start.7) | collective-permute-done | bytes 1048608 | tf_op jit(solution)/shard_map/ppermute | solution.py:101
  87.0 1.3 collective-permute-start.9
  88.9 1.3 collective-permute-start.14
  91.1 28.4 %collective-permute-done.9.refs_4_ = bf16[512,512]{1,0:T(8,128)(2,1)S(1)} collective-permute-done((bf16[512,512]{1,0:T(8,128)(2,1)S(1)}, bf16[512,512]{1,0:T(8,128)(2,1)S(1)}, u32[]{:S(2)}, u32[]{:S(2)}) %collective-permute-start.9) | collective-permute-done | bytes 524320 | tf_op jit(solution)/shard_map/ppermute | solution.py:101
  121.2 1.3 collective-permute-start.11
  122.5 1.3 collective-permute-start.12
  124.9 5.8 %collective-permute-done.14.refs_5_ = bf16[512,1024]{1,0:T(8,128)(2,1)S(1)} collective-permute-done((bf16[512,1024]{1,0:T(8,128)(2,1)S(1)}, bf16[512,1024]{1,0:T(8,128)(2,1)S(1)}, u32[]{:S(2)}, u32[]{:S(2)}) %collective-permute-start.14) | collective-permute-done | bytes 1048608 | tf_op jit(solution)/shard_map/ppermute | solution.py:101
  130.7 2.7 %finish.1 = (bf16[512,2048]{1,0:T(8,128)(2,1)}, f32[1,512]{1,0:T(1,128)}) custom-call(s32[5]{0:T(128)S(1)} %stack.16.place_ref, bf16[512,2048]{1,0:T(8,128)(2,1)S(1)} %bitcast.12, bf16[512,2048]{1,0:T(8,128)(2,1)S(1)} %bitcast.15, bf16[512,1536]{1,0:T(8,128)(2,1)S(1)} %collective-permute-done.10.refs_1_, ...), custom_call_target="tpu_custom_call" | custom-call | flops 1048576 | bytes 65536 | tf_op jit(solution)/shard_map/finish/pallas_call | solution.py:478
  133.4 14.5 %collective-permute-done.12.refs_2_ = bf16[512,512]{1,0:T(8,128)(2,1)S(1)} collective-permute-done((bf16[512,512]{1,0:T(8,128)(2,1)S(1)}, bf16[512,512]{1,0:T(8,128)(2,1)S(1)}, u32[]{:S(2)}, u32[]{:S(2)}) %collective-permute-start.12) | collective-permute-done | bytes 524320 | tf_op jit(solution)/shard_map/ppermute | solution.py:101
  147.9 3.9 %finish_last.1 = (bf16[512,2048]{1,0:T(8,128)(2,1)}, f32[1,512]{1,0:T(1,128)}) custom-call(s32[5]{0:T(128)S(1)} %stack.16.place_ref, bf16[512,2048]{1,0:T(8,128)(2,1)S(1)} %bitcast.13, bf16[512,512]{1,0:T(8,128)(2,1)S(1)} %collective-permute-done.8.refs_0_, ...), custom_call_target="tpu_custom_call", output_to_operand_aliasing={{0}: (6, {}), {1}: (7, {})} | custom-call | flops 1048576 | bytes 65536 | tf_op jit(solution)/shard_map/finish_last/pallas_call | solution.py:518
  (41 shorter events, 15.7 us)
Async XLA Ops:
  0.6 28.5 %collective-permute-start = (bf16[1,512,2048]{2,1,0:T(8,128)(2,1)}, bf16[1,512,2048]{2,1,0:T(8,128)(2,1)}, u32[]{:S(2)}, u32[]{:S(2)}) collective-permute-start(bf16[1,512,2048]{2,1,0:T(8,128)(2,1)} %param.8), channel_id=1, source_target_pairs={{4,0},{8,4},{12,8},{5,1},{9,5},{13,9},{6,2},{10,6},{14,10},{7,3},{... | collective-permute-start | bytes 6291464 | tf_op jit(solution)/shard_map/ppermute | solution.py:20
  2.6 35.5 %collective-permute-start.4 = (bf16[512,2048]{1,0:T(8,128)(2,1)}, bf16[512,2048]{1,0:T(8,128)(2,1)}, u32[]{:S(2)}, u32[]{:S(2)}) collective-permute-start(bf16[512,2048]{1,0:T(8,128)(2,1)} %bitcast.8), channel_id=1, source_target_pairs={{0,1},{7,6},{8,9},{15,14},{16,17},{23,22},{24,25},{31,30}} | collective-permute-start | bytes 6291464 | tf_op jit(solution)/shard_map/ppermute | solution.py:101
  4.6 37.6 %collective-permute-start.3 = (bf16[512,2048]{1,0:T(8,128)(2,1)}, bf16[512,2048]{1,0:T(8,128)(2,1)S(1)}, u32[]{:S(2)}, u32[]{:S(2)}) collective-permute-start(bf16[512,2048]{1,0:T(8,128)(2,1)} %bitcast.9), channel_id=1, source_target_pairs={{2,1},{5,6},{10,9},{13,14},{18,17},{21,22},{26,25},{29,30}} | collective-permute-start | bytes 6291464 | tf_op jit(solution)/shard_map/ppermute | solution.py:101
  7.4 1.6 %copy-start = (bf16[1,512,2048]{2,1,0:T(8,128)(2,1)S(1)}, bf16[1,512,2048]{2,1,0:T(8,128)(2,1)}, u32[]{:S(2)}) copy-start(bf16[1,512,2048]{2,1,0:T(8,128)(2,1)} %param.9) | copy-start | bytes 6291460
  9.0 0.7 copy-start.3
  15.4 13.8 %copy-start.2 = (bf16[1,512,2048]{2,1,0:T(8,128)(2,1)S(1)}, bf16[1,512,2048]{2,1,0:T(8,128)(2,1)}, u32[]{:S(2)}) copy-start(bf16[1,512,2048]{2,1,0:T(8,128)(2,1)} %param.7) | copy-start | bytes 6291460
  29.2 8.9 %copy-start.4 = (s32[2048]{0:T(1024)S(1)}, s32[2048]{0:T(1024)}, u32[]{:S(2)}) copy-start(s32[2048]{0:T(1024)} %param.13) | copy-start | bytes 24580
  31.2 23.9 %collective-permute-start.6 = (bf16[512,1536]{1,0:T(8,128)(2,1)S(1)}, bf16[512,1536]{1,0:T(8,128)(2,1)S(1)}, u32[]{:S(2)}, u32[]{:S(2)}) collective-permute-start(bf16[512,1536]{1,0:T(8,128)(2,1)S(1)} %get-tuple-element.28), channel_id=1, source_target_pairs={{2,1},{5,6},{10,9},{13,14},{18,17},{21,22},{26,25},{29,30}} | collective-permute-start | bytes 4718600 | tf_op jit(solution)/shard_map/ppermute | solution.py:101
  32.0 15.2 %collective-permute-start.2 = (bf16[512,1024]{1,0:T(8,128)(2,1)S(1)}, bf16[512,1024]{1,0:T(8,128)(2,1)S(1)}, u32[]{:S(2)}, u32[]{:S(2)}) collective-permute-start(bf16[512,1024]{1,0:T(8,128)(2,1)S(1)} %get-tuple-element.24), channel_id=1, source_target_pairs={{0,1},{7,6},{8,9},{15,14},{16,17},{23,22},{24,25},{31,30}} | collective-permute-start | bytes 3145736 | tf_op jit(solution)/shard_map/ppermute | solution.py:101
  32.7 14.4 %collective-permute-start.1 = (bf16[512,512]{1,0:T(8,128)(2,1)S(1)}, bf16[512,512]{1,0:T(8,128)(2,1)S(1)}, u32[]{:S(2)}, u32[]{:S(2)}) collective-permute-start(bf16[512,512]{1,0:T(8,128)(2,1)S(1)} %get-tuple-element.23), channel_id=1, source_target_pairs={{3,1},{4,6},{11,9},{12,14},{19,17},{20,22},{27,25},{28,30}} | collective-permute-start | bytes 1572872 | tf_op jit(solution)/shard_map/ppermute | solution.py:101
  47.2 30.7 %collective-permute-start.5 = (bf16[256,2048]{1,0:T(8,128)(2,1)S(1)}, bf16[256,2048]{1,0:T(8,128)(2,1)S(1)}, u32[]{:S(2)}, u32[]{:S(2)}) collective-permute-start(bf16[256,2048]{1,0:T(8,128)(2,1)S(1)} %couple.2.coupled_ref.refs_0_), channel_id=1, source_target_pairs={{3,1},{4,6},{11,9},{12,14},{19,17},{20,22},{27,25},{28,30}} | collective-permute-start | bytes 3145736 | tf_op jit(solution)/shard_map/ppermute | solution.py:101
  55.1 30.1 %collective-permute-start.7 = (bf16[256,2048]{1,0:T(8,128)(2,1)S(1)}, bf16[256,2048]{1,0:T(8,128)(2,1)S(1)}, u32[]{:S(2)}, u32[]{:S(2)}) collective-permute-start(bf16[256,2048]{1,0:T(8,128)(2,1)S(1)} %couple.3.coupled_ref.refs_1_), channel_id=1, source_target_pairs={{3,1},{4,6},{11,9},{12,14},{19,17},{20,22},{27,25},{28,30}} | collective-permute-start | bytes 3145736 | tf_op jit(solution)/shard_map/ppermute | solution.py:101
  75.2 45.9 %collective-permute-start.10 = (bf16[512,1536]{1,0:T(8,128)(2,1)S(1)}, bf16[512,1536]{1,0:T(8,128)(2,1)S(1)}, u32[]{:S(2)}, u32[]{:S(2)}) collective-permute-start(bf16[512,1536]{1,0:T(8,128)(2,1)S(1)} %multiply.9.zero_ref.refs_6_), channel_id=1, source_target_pairs={{1,0},{6,7},{9,8},{14,15},{17,16},{22,23},{25,24},{30,31}} | collective-permute-start | bytes 4718600 | tf_op jit(solution)/shard_map/ppermute | solution.py:101
  77.1 47.8 %collective-permute-start.13 = (bf16[512,1536]{1,0:T(8,128)(2,1)S(1)}, bf16[512,1536]{1,0:T(8,128)(2,1)S(1)}, u32[]{:S(2)}, u32[]{:S(2)}) collective-permute-start(bf16[512,1536]{1,0:T(8,128)(2,1)S(1)} %product_two.1.refs_8_), channel_id=1, source_target_pairs={{1,2},{6,5},{9,10},{14,13},{17,18},{22,21},{25,26},{30,29}} | collective-permute-start | bytes 4718600 | tf_op jit(solution)/shard_map/ppermute | solution.py:101
  86.3 3.9 %collective-permute-start.8 = (bf16[512,512]{1,0:T(8,128)(2,1)S(1)}, bf16[512,512]{1,0:T(8,128)(2,1)S(1)}, u32[]{:S(2)}, u32[]{:S(2)}) collective-permute-start(bf16[512,512]{1,0:T(8,128)(2,1)S(1)} %get-tuple-element.31.zero_ref), channel_id=1, source_target_pairs={{1,0},{6,7},{9,8},{14,15},{17,16},{22,23},{25,24},{30,31}} | collective-permute-start | bytes 1572872 | tf_op jit(solution)/shard_map/ppermute | solution.py:101
  87.0 32.5 %collective-permute-start.9 = (bf16[512,512]{1,0:T(8,128)(2,1)S(1)}, bf16[512,512]{1,0:T(8,128)(2,1)S(1)}, u32[]{:S(2)}, u32[]{:S(2)}) collective-permute-start(bf16[512,512]{1,0:T(8,128)(2,1)S(1)} %get-tuple-element.32), channel_id=1, source_target_pairs={{1,3},{6,4},{9,11},{14,12},{17,19},{22,20},{25,27},{30,28}} | collective-permute-start | bytes 1572872 | tf_op jit(solution)/shard_map/ppermute | solution.py:101
  88.9 41.9 %collective-permute-start.14 = (bf16[512,1024]{1,0:T(8,128)(2,1)S(1)}, bf16[512,1024]{1,0:T(8,128)(2,1)S(1)}, u32[]{:S(2)}, u32[]{:S(2)}) collective-permute-start(bf16[512,1024]{1,0:T(8,128)(2,1)S(1)} %product_other.1.refs_3_), channel_id=1, source_target_pairs={{1,3},{6,4},{9,11},{14,12},{17,19},{22,20},{25,27},{30,28}} | collective-permute-start | bytes 3145736 | tf_op jit(solution)/shard_map/ppermute | solution.py:101
  121.2 12.3 %collective-permute-start.11 = (bf16[512,512]{1,0:T(8,128)(2,1)S(1)}, bf16[512,512]{1,0:T(8,128)(2,1)S(1)}, u32[]{:S(2)}, u32[]{:S(2)}) collective-permute-start(bf16[512,512]{1,0:T(8,128)(2,1)S(1)} %collective-permute-done.9.refs_4_), channel_id=1, source_target_pairs={{3,2},{4,5},{11,10},{12,13},{19,18},{20,21},{27,26},{28,29}} | collective-permute-start | bytes 1572872 | tf_op jit(solution)/shard_map/ppermute | solution.py:101
  122.5 25.4 %collective-permute-start.12 = (bf16[512,512]{1,0:T(8,128)(2,1)S(1)}, bf16[512,512]{1,0:T(8,128)(2,1)S(1)}, u32[]{:S(2)}, u32[]{:S(2)}) collective-permute-start(bf16[512,512]{1,0:T(8,128)(2,1)S(1)} %multiply.10), channel_id=1, source_target_pairs={{1,3},{6,4},{9,11},{14,12},{17,19},{22,20},{25,27},{30,28}} | collective-permute-start | bytes 1572872 | tf_op jit(solution)/shard_map/ppermute | solution.py:101
  124.3 6.4 %copy-start.1 = (bf16[1,512,2048]{2,1,0:T(8,128)(2,1)S(1)}, bf16[1,512,2048]{2,1,0:T(8,128)(2,1)}, u32[]{:S(2)}) copy-start(bf16[1,512,2048]{2,1,0:T(8,128)(2,1)} %param.9) | copy-start | bytes 6291460

commit v8 on v6

--- a/solution.py
+++ b/solution.py
@@ -136,11 +136,10 @@
         refs[-1][...] = coupled_ref[...].T
 
 
-def turn(place, panel, part, coupled, across):
+def turn(place, panel, coupled, across):
     rows, nodes = coupled.shape
     chunk = 128
     steps = rows // chunk
-    ratio = nodes // 4 // chunk
     return pl.pallas_call(
         turn_kernel,
         out_shape=jax.ShapeDtypeStruct((nodes, nodes), BF16),
@@ -150,8 +149,7 @@
             in_specs=[pl.BlockSpec((chunk, nodes), lambda i, place: (i, 0))]
             + ([] if across is None else [pl.BlockSpec(memory_space=pl.ANY)]),
             out_specs=pl.BlockSpec(
-                (nodes, chunk),
-                lambda i, place: (0, turned(panel, place[0]) * ratio + part * steps + i),
+                (nodes, chunk), lambda i, place: (0, turned(panel, place[0]) * steps + i)
             ),
         ),
         input_output_aliases={} if across is None else {2: 0},
@@ -222,31 +220,54 @@
     )(place, half, across, zero)
 
 
-def three_kernel(place_ref, left_ref, right_ref, out_ref, zero_ref):
-    width = zero_ref.shape[1]
-    multiply_kernel(lambda odd: 2 * odd, 2, 1, place_ref, left_ref, right_ref, out_ref)
-
-    @pl.when(place_ref[1] == 1)
-    def _():
-        zero_ref[...] = out_ref[:, pl.ds(pl.multiple_of(place_ref[0] * width, 128), width)]
-
-
-def product_three(place, half, across):
+def ends_kernel(place_ref, left_ref, right_ref, zero_ref, two_ref):
+    for block, out_ref in ((0, zero_ref), (2, two_ref)):
+        first = lambda odd: turned(block, odd)
+        multiply_kernel(first, 1, 1, place_ref, left_ref, right_ref, out_ref)
+
+
+def product_ends(place, half, across):
     rows = half.shape[0]
     width = across.shape[0] // 4
     vmem = pl.BlockSpec(memory_space=pltpu.VMEM)
     return pl.pallas_call(
-        three_kernel,
-        out_shape=(
-            jax.ShapeDtypeStruct((rows, 2 * width), BF16),
-            jax.ShapeDtypeStruct((rows, width), BF16),
-        ),
+        ends_kernel,
+        out_shape=(jax.ShapeDtypeStruct((rows, width), BF16),) * 2,
         in_specs=[pl.BlockSpec(memory_space=pltpu.SMEM)] + [vmem] * 2,
         out_specs=(vmem, vmem),
         compiler_params=pltpu.CompilerParams(vmem_limit_bytes=6 * MIB),
         cost_estimate=LIGHT,
-        name="product_three",
+        name="product_ends",
     )(place, half, across)
+
+
+def other_kernel(place_ref, left_ref, right_ref, zero_ref, out_ref):
+    odd = place_ref[0]
+    width = zero_ref.shape[1]
+
+    @pl.when(place_ref[1] == 1)
+    def _():
+        out_ref[:, pl.ds(pl.multiple_of(odd * width, 128), width)] = zero_ref[...]
+        source = pl.multiple_of((1 + odd) * width, 128)
+        target = pl.multiple_of((1 - odd) * width, 128)
+        out_ref[:, pl.ds(target, width)] = jnp.dot(
+            left_ref[...], right_ref[:, pl.ds(source, width)], preferred_element_type=F32
+        ).astype(BF16)
+
+
+def product_other(place, half, across, zero):
+    rows = half.shape[0]
+    width = across.shape[0] // 4
+    vmem = pl.BlockSpec(memory_space=pltpu.VMEM)
+    return pl.pallas_call(
+        other_kernel,
+        out_shape=jax.ShapeDtypeStruct((rows, 2 * width), BF16),
+        in_specs=[pl.BlockSpec(memory_space=pltpu.SMEM)] + [vmem] * 3,
+        out_specs=vmem,
+        compiler_params=pltpu.CompilerParams(vmem_limit_bytes=6 * MIB),
+        cost_estimate=LIGHT,
+        name="product_other",
+    )(place, half, across, zero)
 
 
 def prior_kernel(place_ref, shifted_ref, sigma_ref, out_ref):
@@ -259,7 +280,7 @@
         out_ref[...] = sigma_ref[...]
 
 
-def parts_kernel(place_ref, shifted_ref, sigma_ref, row_ref, far_ref, near_ref, last_ref):
+def parts_kernel(place_ref, shifted_ref, sigma_ref, row_ref, two_ref, zero_ref, last_ref):
     odd = place_ref[0]
     width = last_ref.shape[1]
 
@@ -267,11 +288,12 @@
         return pl.ds(pl.multiple_of(block * width, 128), count * width)
 
     prior_kernel(place_ref, shifted_ref, sigma_ref, row_ref)
-    near = row_ref[:, at(2 - 2 * odd, 2)]
-    near_ref[...] = near
-    far_ref[:, width:] = near
-    far_ref[:, :width] = row_ref[:, at(3 * odd)]
-    last_ref[...] = row_ref[:, at(3 - 3 * odd)]
+    first, last = row_ref[:, at(3 * odd)], row_ref[:, at(3 - 3 * odd)]
+    two_ref[:, :width] = first
+    two_ref[:, width:] = row_ref[:, at(2 - 2 * odd, 2)]
+    zero_ref[:, :width] = first
+    zero_ref[:, width:] = last
+    last_ref[...] = last
 
 
 def prior_parts(place, shifted, sigma):
@@ -302,29 +324,28 @@
     )(place, shifted, sigma)
 
 
-def assemble_kernel(place_ref, own, near_two, last_three, far_zero, out_ref):
+def assemble_kernel(place_ref, own, two, zero, three, out_ref):
     @pl.when(place_ref[1] == 1)
     def _():
         odd = place_ref[0]
-        width = last_three.shape[1]
-
-        def at(block):
-            return pl.ds(pl.multiple_of(block * width, 128), width)
+        width = three.shape[1]
+
+        def at(block, count=1):
+            return pl.ds(pl.multiple_of(block * width, 128), count * width)
 
         near = 2 * (1 - odd)
-        half = pl.ds(pl.multiple_of(near * width, 128), 2 * width)
         row = [turned(block, odd) for block in range(4)]
         out_ref[at(row[1]), :] = own[...]
-        out_ref[at(row[2]), half] = near_two[...]
-        out_ref[at(row[0]), at(row[0])] = far_zero[:, :width]
-        out_ref[at(row[0]), half] = far_zero[:, width:]
-        out_ref[at(row[3]), at(row[3])] = last_three[...]
-        for step in range(2):
-            out_ref[at(near + step), at(row[1])] = own[:, at(near + step)].T
-            piece = slice((1 + step) * width, (2 + step) * width)
-            out_ref[at(near + step), at(row[0])] = far_zero[:, piece].T
-        out_ref[at(row[0]), at(row[1])] = own[:, at(row[0])].T
-        out_ref[at(row[3]), at(row[2])] = near_two[:, at(1 - odd)].T
+        out_ref[at(row[2]), at(row[0])] = two[:, :width]
+        out_ref[at(row[2]), at(near, 2)] = two[:, width:]
+        out_ref[at(row[0]), at(row[0])] = zero[:, :width]
+        out_ref[at(row[0]), at(row[3])] = zero[:, width:]
+        out_ref[at(row[3]), at(row[3])] = three[...]
+        for block in (0, 2, 3):
+            out_ref[at(row[block]), at(row[1])] = own[:, at(row[block])].T
+        out_ref[at(row[0]), at(row[2])] = two[:, :width].T
+        out_ref[at(row[3]), at(row[2])] = two[:, at(2 - odd)].T
+        out_ref[at(row[3]), at(row[0])] = zero[:, width:].T
 
 
 def assemble(place, *parts):
@@ -339,6 +360,22 @@
         cost_estimate=LIGHT,
         name="assemble",
     )(place, *parts)
+
+
+def tick(place, value):
+    def kernel(place_ref, value_ref, out_ref):
+        for which in range(place.shape[0]):
+            out_ref[which] = place_ref[which]
+
+    scalars = pl.BlockSpec(memory_space=pltpu.SMEM)
+    return pl.pallas_call(
+        kernel,
+        out_shape=jax.ShapeDtypeStruct(place.shape, place.dtype),
+        in_specs=[scalars, pl.BlockSpec(memory_space=pl.ANY)],
+        out_specs=scalars,
+        cost_estimate=LIGHT,
+        name="tick",
+    )(place, value)
 
 
 def final_kernel(
@@ -476,24 +513,20 @@
     after = lambda value, *others: lax.optimization_barrier((value, *others))[0]
 
     shifted = passed_along(separator, "dom", -1)[0]
+    p0 = moved(pivot, 0, 1)
     p2 = moved(pivot, 2, 1)
-    p0 = moved(pivot, 0, 1)
-    c1 = [couple(pivot, node_class, coupling_rate, part, 2) for part in range(2)]
-    across = turn(place, 1, 0, c1[0], None)
-    across = turn(place, 1, 1, c1[1], across)
-
-    row, far, near, last = prior_parts(place, after(shifted, across), sigma)
-    far_zero, near_two, last_three = moved(far, 0, 1), moved(near, 2, 1), moved(last, 3, 1)
-
-    c2 = couple_here(place, after(p2, last), node_class, coupling_rate)
-    across = turn(place, 2, 0, c2, across)
-    c0 = couple_here(place, after(p0, across), node_class, coupling_rate)
-    across = turn(place, 0, 0, c0, across)
-    c3 = [
-        moved(after(c1[0], last_three, near_two, across), 3, 1),
-        moved(after(c1[1], far_zero), 3, 1),
-    ]
-    prior = assemble(place, row, near_two, last_three, far_zero)
+    c1 = couple(pivot, node_class, coupling_rate)
+    across = turn(place, 1, c1, None)
+
+    row, two, zero, last = prior_parts(place, after(shifted, across), sigma)
+    zero, two, three = moved(zero, 0, 1), moved(two, 2, 1), moved(last, 3, 1)
+
+    c0 = couple_here(place, after(p0, last), node_class, coupling_rate)
+    across = turn(place, 0, c0, across)
+    c2 = couple_here(place, after(p2, across), node_class, coupling_rate)
+    across = turn(place, 2, c2, across)
+    c3 = moved(after(c1, three, zero, two, across), 3, 1)
+    prior = assemble(place, row, two, zero, three)
 
     h0 = multiply(place, [c0], prior)
     q0_own = multiply(place, [h0], across, lambda odd: odd, 3)
@@ -502,21 +535,21 @@
     q2_own = product_two(place, h2, across, q0_own)
     q2 = moved(q2_own, 1, 2)
 
-    h3 = multiply(place, c3, prior)
-    q3_two = moved(multiply(place, [h3], across, lambda odd: 2 - odd, 1), 1, 3)
-    q3_own, q30 = product_three(place, h3, across)
+    h3 = multiply(place, [c3], prior)
+    q30, q32 = product_ends(place, h3, across)
+    q0_last, q3_two = moved(q30, 1, 0), moved(q32, 1, 3)
+    q3_own = product_other(place, h3, across, q30)
     q3_other = moved(q3_own, 1, 3)
-    q0_last = moved(q30, 1, 0)
-    across = turn(place, 3, 0, c3[0], after(across, q30))
-    across = turn(place, 3, 1, c3[1], across)
+    across = turn(place, 3, c3, after(across, q3_own))
     q33 = multiply(place, [h3], across, lambda odd: 3 - 3 * odd, 1)
     q3_last = moved(q33, 1, 3)
-    q2_last = moved(after(q3_two, q0, q33), 3, 2)
-    h1 = multiply(place, [after(c1[0], q33), c1[1]], prior)
+    place_then = tick(tick(place, q0_last), q3_two)
+    q2_last = moved(after(q3_two, q0, q33, place_then), 3, 2)
+    h1 = multiply(place, [after(c1, q33)], prior)
     q11 = multiply(place, [h1], across, lambda odd: 1 + odd, 1)
     received = (q0, q0_last, q2, q2, q2_last, q3_two, q3_other, q3_last)
     kept = (q0_own, q11, q2_own, q3_own)
-    covariance, variances = final(place, pivot, sigma, received, kept)
+    covariance, variances = final(place_then, pivot, sigma, received, kept)
     return (covariance[None], variances)
 
 

time: 131 us -> 152 us (1.16)
  the two profiles are of different devices: /device:TPU:2 before, /device:TPU:21 now
where the time goes in v8:
time: 152 us; the launch traced here: 151 us
  Pallas kernels  81.5 us (54%)
  waiting for transfers between devices  34.7 us (23%)
  starting transfers between devices  23.8 us (16%)
  local copies, waits for them, and re-layouts  7.95 us (5%)
  between operations  2.97 us (2%)
    pallas_call x7, Pallas kernels, multiply(): pl.pallas_call(functools.partial(multiply_kernel, first, count, len(lefts...  32.8 us
    ppermute x13, waiting for transfers between devices, moved(): lax.ppermute(value, ('dom', 'col'), route(source, target, lax.axis_size('...  23.2 us
    ppermute x13, starting transfers between devices, moved(): lax.ppermute(value, ('dom', 'col'), route(source, target, lax.axis_size('...  21.2 us
    pallas_call x2, Pallas kernels, couple_here(): pl.pallas_call(kernel, out_shape=jax.ShapeDtypeStruct((rows, nodes), BF16...  12.7 us
    ppermute x1, waiting for transfers between devices, passed_along(): lax.ppermute(value, axis, [(source, source + steps) for source in range(i...  11.5 us
    unnamed x30, local copies, waits for them, and re-layouts  7.86 us
    pallas_call x4, Pallas kernels, turn(): pl.pallas_call(turn_kernel, out_shape=jax.ShapeDtypeStruct((nodes, nodes)...  7.85 us
    pallas_call x1, Pallas kernels, final(): pl.pallas_call(final_kernel, out_shape=(jax.ShapeDtypeStruct((rows, nodes...  5.2 us
  transfers between devices with their start and end apart: 14, of which 3 were waited for; matrix products, arithmetic and copies ran while one was open for 0% of the time, Pallas kernels for 51%

profile of v8, /device:TPU:21, one launch (start us, length us, event | category | flops | bytes accessed | tf_op | source)
XLA Modules:
  0.0 150.9 jit_solution(15963071649029093285)
XLA Ops:
  0.6 2.6 %collective-permute-start = (bf16[1,512,2048]{2,1,0:T(8,128)(2,1)}, bf16[1,512,2048]{2,1,0:T(8,128)(2,1)}, u32[]{:S(2)}, u32[]{:S(2)}) collective-permute-start(bf16[1,512,2048]{2,1,0:T(8,128)(2,1)} %param.8), channel_id=1, source_target_pairs={{4,0},{8,4},{12,8},{5,1},{9,5},{13,9},{6,2},{10,6},{14,10},{7,3},{... | collective-permute-start | bytes 6291464 | tf_op jit(solution)/shard_map/ppermute | solution.py:20
  10.2 4.7 %couple.1.coupled_ref.refs_0_ = bf16[512,2048]{1,0:T(8,128)(2,1)S(1)} custom-call(f32[1]{0:T(128)S(6)} %copy.15.rate_ref.refs_0_, s32[1,2048]{1,0:T(1,128)S(1)} %bitcast.14, bf16[512,2048]{1,0:T(8,128)(2,1)S(1)} %bitcast.10), custom_call_target="tpu_custom_call" | custom-call | flops 1048576 | bytes 65536 | tf_op jit(solution)/shard_map/couple/pallas_call | solution.py:71
  16.9 11.5 %collective-permute-done = bf16[1,512,2048]{2,1,0:T(8,128)(2,1)} collective-permute-done((bf16[1,512,2048]{2,1,0:T(8,128)(2,1)}, bf16[1,512,2048]{2,1,0:T(8,128)(2,1)}, u32[]{:S(2)}, u32[]{:S(2)}) %collective-permute-start) | collective-permute-done | bytes 2097184 | tf_op jit(solution)/shard_map/ppermute | solution.py:20
  28.3 3.1 %prior_parts.1 = (bf16[512,2048]{1,0:T(8,128)(2,1)S(1)}, bf16[512,1536]{1,0:T(8,128)(2,1)S(1)}, bf16[512,1024]{1,0:T(8,128)(2,1)S(1)}, bf16[512,512]{1,0:T(8,128)(2,1)S(1)}) custom-call(s32[5]{0:T(128)S(1)} %stack.16.place_ref, bf16[512,2048]{1,0:T(8,128)(2,1)} %bitcast.5.shifted_ref, bf16[512,2048]{1,0:T(8,128)(2,1)S(1)} %bitcast.12), custom_call_target="tpu_custom_call" | custom-call | flops 1048576 | bytes 65536 | tf_op jit(solution)/shard_map/prior_parts/pallas_call | solution.py:305
  35.3 6.4 %couple_here.2.coupled_ref.refs_0_ = bf16[512,2048]{1,0:T(8,128)(2,1)S(1)} custom-call(s32[5]{0:T(128)S(1)} %stack.16.place_ref, f32[1]{0:T(128)S(6)} %copy.15.rate_ref.refs_0_, s32[1,2048]{1,0:T(1,128)S(1)} %bitcast.15, bf16[512,2048]{1,0:T(8,128)(2,1)} %collective-permute-done.5.refs_2_), custom_call_target="tpu_custom_call" | custom-call | flops 1048576 | bytes 65536 | tf_op jit(solution)/shard_map/couple_here/pallas_call | solution.py:113
  43.7 6.4 %couple_here.3.coupled_ref.refs_0_ = bf16[512,2048]{1,0:T(8,128)(2,1)S(1)} custom-call(s32[5]{0:T(128)S(1)} %stack.16.place_ref, f32[1]{0:T(128)S(6)} %copy.15.rate_ref.refs_0_, s32[1,2048]{1,0:T(1,128)S(1)} %bitcast.16, bf16[512,2048]{1,0:T(8,128)(2,1)} %collective-permute-done.4.refs_2_), custom_call_target="tpu_custom_call" | custom-call | flops 1048576 | bytes 65536 | tf_op jit(solution)/shard_map/couple_here/pallas_call | solution.py:113
  50.0 2.0 %turn.6.right_ref.refs_1_.refs_0_ = bf16[2048,2048]{1,0:T(8,128)(2,1)S(1)} custom-call(s32[5]{0:T(128)S(1)} %stack.16.place_ref, bf16[512,2048]{1,0:T(8,128)(2,1)S(1)} %couple_here.3.coupled_ref.refs_0_, bf16[2048,2048]{1,0:T(8,128)(2,1)S(1)} %turn.5.refs_0_), custom_call_target="tpu_custom_call", output_to_operand_aliasing={{}: (2, {})} | custom-call | flops 1048576 | bytes 65536 | tf_op jit(solution)/shard_map/turn/pallas_call | solution.py:143
  52.0 6.2 %collective-permute-done.3.two = bf16[512,1536]{1,0:T(8,128)(2,1)S(1)} collective-permute-done((bf16[512,1536]{1,0:T(8,128)(2,1)S(1)}, bf16[512,1536]{1,0:T(8,128)(2,1)S(1)}, u32[]{:S(2)}, u32[]{:S(2)}) %collective-permute-start.3) | collective-permute-done | bytes 1572896 | tf_op jit(solution)/shard_map/ppermute | solution.py:101
  61.4 5.6 %multiply.8.refs_0_ = bf16[512,2048]{1,0:T(8,128)(2,1)S(1)} custom-call(s32[5]{0:T(128)S(1)} %stack.16.place_ref, bf16[512,2048]{1,0:T(8,128)(2,1)S(1)} %couple_here.2.coupled_ref.refs_0_, bf16[2048,2048]{1,0:T(8,128)(2,1)S(1)} %assemble.1.refs_1_), custom_call_target="tpu_custom_call" | custom-call | flops 1048576 | bytes 65536 | tf_op jit(solution)/shard_map/multiply/pallas_call | solution.py:187
  67.0 5.5 %multiply.9.zero_ref.q01 = bf16[512,1536]{1,0:T(8,128)(2,1)} custom-call(s32[5]{0:T(128)S(1)} %stack.16.place_ref, bf16[512,2048]{1,0:T(8,128)(2,1)S(1)} %multiply.8.refs_0_, bf16[2048,2048]{1,0:T(8,128)(2,1)S(1)} %turn.6.right_ref.refs_1_.refs_0_), custom_call_target="tpu_custom_call" | custom-call | flops 1048576 | bytes 65536 | tf_op jit(solution)/shard_map/multiply/pallas_call | solution.py:187
  72.6 2.4 %collective-permute-start.9 = (bf16[512,1536]{1,0:T(8,128)(2,1)}, bf16[512,1536]{1,0:T(8,128)(2,1)}, u32[]{:S(2)}, u32[]{:S(2)}) collective-permute-start(bf16[512,1536]{1,0:T(8,128)(2,1)} %multiply.9.zero_ref.q01), channel_id=1, source_target_pairs={{1,0},{6,7},{9,8},{14,15},{17,16},{22,23},{25,24},{30,31}} | collective-permute-start | bytes 4718600 | tf_op jit(solution)/shard_map/ppermute | solution.py:101
  75.0 5.6 %multiply.10.left_ref = bf16[512,2048]{1,0:T(8,128)(2,1)S(1)} custom-call(s32[5]{0:T(128)S(1)} %stack.16.place_ref, bf16[512,2048]{1,0:T(8,128)(2,1)S(1)} %couple_here.3.coupled_ref.refs_0_, bf16[2048,2048]{1,0:T(8,128)(2,1)S(1)} %assemble.1.refs_1_), custom_call_target="tpu_custom_call" | custom-call | flops 1048576 | bytes 65536 | tf_op jit(solution)/shard_map/multiply/pallas_call | solution.py:187
  80.6 5.2 %product_two.1.q21 = bf16[512,1536]{1,0:T(8,128)(2,1)} custom-call(s32[5]{0:T(128)S(1)} %stack.16.place_ref, bf16[512,2048]{1,0:T(8,128)(2,1)S(1)} %multiply.10.left_ref, bf16[2048,2048]{1,0:T(8,128)(2,1)S(1)} %turn.6.right_ref.refs_1_.refs_0_, bf16[512,1536]{1,0:T(8,128)(2,1)} %multiply.9.zero_ref.q01), custom_call_target="tpu_custom_call" | custom-call | flops 1048576 | bytes 65536 | tf_op jit(solution)/shard_map/product_two/pallas_call | solution.py:212
  85.7 2.5 %collective-permute-start.10 = (bf16[512,1536]{1,0:T(8,128)(2,1)}, bf16[512,1536]{1,0:T(8,128)(2,1)}, u32[]{:S(2)}, u32[]{:S(2)}) collective-permute-start(bf16[512,1536]{1,0:T(8,128)(2,1)} %product_two.1.q21), channel_id=1, source_target_pairs={{1,2},{6,5},{9,10},{14,13},{17,18},{22,21},{25,26},{30,29}} | collective-permute-start | bytes 4718600 | tf_op jit(solution)/shard_map/ppermute | solution.py:101
  88.2 5.6 %multiply.7.left_ref.refs_0_ = bf16[512,2048]{1,0:T(8,128)(2,1)S(1)} custom-call(s32[5]{0:T(128)S(1)} %stack.16.place_ref, bf16[512,2048]{1,0:T(8,128)(2,1)S(1)} %collective-permute-done.6.refs_0_.coupled_ref, bf16[2048,2048]{1,0:T(8,128)(2,1)S(1)} %assemble.1.refs_1_), custom_call_target="tpu_custom_call" | custom-call | flops 1048576 | bytes 65536 | tf_op jit(solution)/shard_map/multiply/pallas_call | solution.py:187
  93.8 3.9 %product_ends.1 = (bf16[512,512]{1,0:T(8,128)(2,1)S(1)}, bf16[512,512]{1,0:T(8,128)(2,1)}) custom-call(s32[5]{0:T(128)S(1)} %stack.16.place_ref, bf16[512,2048]{1,0:T(8,128)(2,1)S(1)} %multiply.7.left_ref.refs_0_, bf16[2048,2048]{1,0:T(8,128)(2,1)S(1)} %turn.6.right_ref.refs_1_.refs_0_), custom_call_target="tpu_custom_call" | custom-call | flops 1048576 | bytes 65536 | tf_op jit(solution)/shard_map/product_ends/pallas_call | solution.py:233
  99.0 2.1 %collective-permute-start.8 = (bf16[512,512]{1,0:T(8,128)(2,1)}, bf16[512,512]{1,0:T(8,128)(2,1)}, u32[]{:S(2)}, u32[]{:S(2)}) collective-permute-start(bf16[512,512]{1,0:T(8,128)(2,1)} %get-tuple-element.27), channel_id=1, source_target_pairs={{1,3},{6,4},{9,11},{14,12},{17,19},{22,20},{25,27},{30,28}} | collective-permute-start | bytes 1572872 | tf_op jit(solution)/shard_map/ppermute | solution.py:101
  102.9 2.3 %collective-permute-start.12 = (bf16[512,1024]{1,0:T(8,128)(2,1)S(1)}, bf16[512,1024]{1,0:T(8,128)(2,1)}, u32[]{:S(2)}, u32[]{:S(2)}) collective-permute-start(bf16[512,1024]{1,0:T(8,128)(2,1)S(1)} %product_other.1.q31), channel_id=1, source_target_pairs={{1,3},{6,4},{9,11},{14,12},{17,19},{22,20},{25,27},{30,28}} | collective-permute-start | bytes 3145736 | tf_op jit(solution)/shard_map/ppermute | solution.py:101
  107.2 3.1 %multiply.11 = bf16[512,512]{1,0:T(8,128)(2,1)} custom-call(s32[5]{0:T(128)S(1)} %stack.16.place_ref, bf16[512,2048]{1,0:T(8,128)(2,1)S(1)} %multiply.7.left_ref.refs_0_, bf16[2048,2048]{1,0:T(8,128)(2,1)S(1)} %turn.7.refs_1_), custom_call_target="tpu_custom_call" | custom-call | flops 1048576 | bytes 65536 | tf_op jit(solution)/shard_map/multiply/pallas_call | solution.py:187
  110.5 17.0 %collective-permute-done.7.value_ref.q0_last = bf16[512,512]{1,0:T(8,128)(2,1)S(1)} collective-permute-done((bf16[512,512]{1,0:T(8,128)(2,1)S(1)}, bf16[512,512]{1,0:T(8,128)(2,1)S(1)}, u32[]{:S(2)}, u32[]{:S(2)}) %collective-permute-start.7) | collective-permute-done | bytes 524320 | tf_op jit(solution)/shard_map/ppermute | solution.py:101
  128.4 2.1 %collective-permute-start.13 = (bf16[512,512]{1,0:T(8,128)(2,1)}, bf16[512,512]{1,0:T(8,128)(2,1)}, u32[]{:S(2)}, u32[]{:S(2)}) collective-permute-start(bf16[512,512]{1,0:T(8,128)(2,1)} %multiply.11), channel_id=1, source_target_pairs={{1,3},{6,4},{9,11},{14,12},{17,19},{22,20},{25,27},{30,28}} | collective-permute-start | bytes 1572872 | tf_op jit(solution)/shard_map/ppermute | solution.py:101
  133.7 3.4 %copy-done.3 = bf16[2048,2048]{1,0:T(8,128)(2,1)S(1)} copy-done((bf16[2048,2048]{1,0:T(8,128)(2,1)S(1)}, bf16[2048,2048]{1,0:T(8,128)(2,1)}, u32[]{:S(2)}) %copy-start.3) | copy-done | bytes 8388632
  137.7 5.6 %multiply.12.refs_0_ = bf16[512,2048]{1,0:T(8,128)(2,1)S(1)} custom-call(s32[5]{0:T(128)S(1)} %copy-done.11, bf16[512,2048]{1,0:T(8,128)(2,1)S(1)} %couple.1.coupled_ref.refs_0_, bf16[2048,2048]{1,0:T(8,128)(2,1)S(1)} %copy-done.3), custom_call_target="tpu_custom_call" | custom-call | flops 1048576 | bytes 65536 | tf_op jit(solution)/shard_map/multiply/pallas_call | solution.py:187
  145.7 5.2 %final.1 = (bf16[512,2048]{1,0:T(8,128)(2,1)}, f32[1,512]{1,0:T(1,128)}) custom-call(s32[5]{0:T(128)S(1)} %copy-done.14, bf16[512,2048]{1,0:T(8,128)(2,1)S(1)} %bitcast.11, bf16[512,2048]{1,0:T(8,128)(2,1)S(1)} %bitcast.13, bf16[512,1536]{1,0:T(8,128)(2,1)} %collective-permute-done.9.q0, bf16[512,512]{1,0:T(8,128)(2,1)S(1)} %copy-done.9, ...), custom_call_target="tpu_custom_call" | custom-call | flops 1048576 | bytes 65536 | tf_op jit(solution)/shard_map/final/pallas_call | solution.py:469
  (57 shorter events, 28.1 us)
Async XLA Ops:
  0.6 27.7 %collective-permute-start = (bf16[1,512,2048]{2,1,0:T(8,128)(2,1)}, bf16[1,512,2048]{2,1,0:T(8,128)(2,1)}, u32[]{:S(2)}, u32[]{:S(2)}) collective-permute-start(bf16[1,512,2048]{2,1,0:T(8,128)(2,1)} %param.8), channel_id=1, source_target_pairs={{4,0},{8,4},{12,8},{5,1},{9,5},{13,9},{6,2},{10,6},{14,10},{7,3},{... | collective-permute-start | bytes 6291464 | tf_op jit(solution)/shard_map/ppermute | solution.py:20
  3.2 32.1 %collective-permute-start.5 = (bf16[512,2048]{1,0:T(8,128)(2,1)}, bf16[512,2048]{1,0:T(8,128)(2,1)}, u32[]{:S(2)}, u32[]{:S(2)}) collective-permute-start(bf16[512,2048]{1,0:T(8,128)(2,1)} %bitcast.8), channel_id=1, source_target_pairs={{0,1},{7,6},{8,9},{15,14},{16,17},{23,22},{24,25},{31,30}} | collective-permute-start | bytes 6291464 | tf_op jit(solution)/shard_map/ppermute | solution.py:101
  4.5 39.1 %collective-permute-start.4 = (bf16[512,2048]{1,0:T(8,128)(2,1)}, bf16[512,2048]{1,0:T(8,128)(2,1)}, u32[]{:S(2)}, u32[]{:S(2)}) collective-permute-start(bf16[512,2048]{1,0:T(8,128)(2,1)} %bitcast.9), channel_id=1, source_target_pairs={{2,1},{5,6},{10,9},{13,14},{18,17},{21,22},{26,25},{29,30}} | collective-permute-start | bytes 6291464 | tf_op jit(solution)/shard_map/ppermute | solution.py:101
  7.9 99.3 %copy-start.10 = (s32[5]{0:T(128)}, s32[5]{0:T(128)S(1)}, u32[]{:S(2)}) copy-start(s32[5]{0:T(128)S(1)} %stack.16.place_ref) | copy-start | bytes 64
  14.9 13.4 %copy-start.6 = (bf16[1,512,2048]{2,1,0:T(8,128)(2,1)S(1)}, bf16[1,512,2048]{2,1,0:T(8,128)(2,1)}, u32[]{:S(2)}) copy-start(bf16[1,512,2048]{2,1,0:T(8,128)(2,1)} %param.7) | copy-start | bytes 6291460
  28.3 7.0 %copy-start.13 = (s32[2048]{0:T(1024)S(1)}, s32[2048]{0:T(1024)}, u32[]{:S(2)}) copy-start(s32[2048]{0:T(1024)} %param.13) | copy-start | bytes 24580
  31.4 26.8 %collective-permute-start.3 = (bf16[512,1536]{1,0:T(8,128)(2,1)S(1)}, bf16[512,1536]{1,0:T(8,128)(2,1)S(1)}, u32[]{:S(2)}, u32[]{:S(2)}) collective-permute-start(bf16[512,1536]{1,0:T(8,128)(2,1)S(1)} %get-tuple-element.21), channel_id=1, source_target_pairs={{2,1},{5,6},{10,9},{13,14},{18,17},{21,22},{26,25},{29,30}} | collective-permute-start | bytes 4718600 | tf_op jit(solution)/shard_map/ppermute | solution.py:101
  32.7 19.3 %collective-permute-start.2 = (bf16[512,1024]{1,0:T(8,128)(2,1)S(1)}, bf16[512,1024]{1,0:T(8,128)(2,1)S(1)}, u32[]{:S(2)}, u32[]{:S(2)}) collective-permute-start(bf16[512,1024]{1,0:T(8,128)(2,1)S(1)} %get-tuple-element.20), channel_id=1, source_target_pairs={{0,1},{7,6},{8,9},{15,14},{16,17},{23,22},{24,25},{31,30}} | collective-permute-start | bytes 3145736 | tf_op jit(solution)/shard_map/ppermute | solution.py:101
  34.0 18.0 %collective-permute-start.1 = (bf16[512,512]{1,0:T(8,128)(2,1)S(1)}, bf16[512,512]{1,0:T(8,128)(2,1)S(1)}, u32[]{:S(2)}, u32[]{:S(2)}) collective-permute-start(bf16[512,512]{1,0:T(8,128)(2,1)S(1)} %get-tuple-element.19), channel_id=1, source_target_pairs={{3,1},{4,6},{11,9},{12,14},{19,17},{20,22},{27,25},{28,30}} | collective-permute-start | bytes 1572872 | tf_op jit(solution)/shard_map/ppermute | solution.py:101
  58.2 30.0 %collective-permute-start.6 = (bf16[512,2048]{1,0:T(8,128)(2,1)S(1)}, bf16[512,2048]{1,0:T(8,128)(2,1)S(1)}, u32[]{:S(2)}, u32[]{:S(2)}) collective-permute-start(bf16[512,2048]{1,0:T(8,128)(2,1)S(1)} %couple.1.coupled_ref.refs_0_), channel_id=1, source_target_pairs={{3,1},{4,6},{11,9},{12,14},{19,17},{20,22},{27,25},{28,30}} | collective-permute-start | bytes 6291464 | tf_op jit(solution)/shard_map/ppermute | solution.py:101
  61.4 26.8 %copy-start.2 = (bf16[2048,2048]{1,0:T(8,128)(2,1)}, bf16[2048,2048]{1,0:T(8,128)(2,1)S(1)}, u32[]{:S(2)}) copy-start(bf16[2048,2048]{1,0:T(8,128)(2,1)S(1)} %assemble.1.refs_1_) | copy-start | bytes 25165828
  72.6 60.4 %collective-permute-start.9 = (bf16[512,1536]{1,0:T(8,128)(2,1)}, bf16[512,1536]{1,0:T(8,128)(2,1)}, u32[]{:S(2)}, u32[]{:S(2)}) collective-permute-start(bf16[512,1536]{1,0:T(8,128)(2,1)} %multiply.9.zero_ref.q01), channel_id=1, source_target_pairs={{1,0},{6,7},{9,8},{14,15},{17,16},{22,23},{25,24},{30,31}} | collective-permute-start | bytes 4718600 | tf_op jit(solution)/shard_map/ppermute | solution.py:101
  85.7 59.5 %collective-permute-start.10 = (bf16[512,1536]{1,0:T(8,128)(2,1)}, bf16[512,1536]{1,0:T(8,128)(2,1)}, u32[]{:S(2)}, u32[]{:S(2)}) collective-permute-start(bf16[512,1536]{1,0:T(8,128)(2,1)} %product_two.1.q21), channel_id=1, source_target_pairs={{1,2},{6,5},{9,10},{14,13},{17,18},{22,21},{25,26},{30,29}} | collective-permute-start | bytes 4718600 | tf_op jit(solution)/shard_map/ppermute | solution.py:101
  97.7 29.9 %collective-permute-start.7 = (bf16[512,512]{1,0:T(8,128)(2,1)S(1)}, bf16[512,512]{1,0:T(8,128)(2,1)S(1)}, u32[]{:S(2)}, u32[]{:S(2)}) collective-permute-start(bf16[512,512]{1,0:T(8,128)(2,1)S(1)} %get-tuple-element.26.zero_ref), channel_id=1, source_target_pairs={{1,0},{6,7},{9,8},{14,15},{17,16},{22,23},{25,24},{30,31}} | collective-permute-start | bytes 1572872 | tf_op jit(solution)/shard_map/ppermute | solution.py:101
  99.0 32.7 %collective-permute-start.8 = (bf16[512,512]{1,0:T(8,128)(2,1)}, bf16[512,512]{1,0:T(8,128)(2,1)}, u32[]{:S(2)}, u32[]{:S(2)}) collective-permute-start(bf16[512,512]{1,0:T(8,128)(2,1)} %get-tuple-element.27), channel_id=1, source_target_pairs={{1,3},{6,4},{9,11},{14,12},{17,19},{22,20},{25,27},{30,28}} | collective-permute-start | bytes 1572872 | tf_op jit(solution)/shard_map/ppermute | solution.py:101
  102.9 42.3 %collective-permute-start.12 = (bf16[512,1024]{1,0:T(8,128)(2,1)S(1)}, bf16[512,1024]{1,0:T(8,128)(2,1)}, u32[]{:S(2)}, u32[]{:S(2)}) collective-permute-start(bf16[512,1024]{1,0:T(8,128)(2,1)S(1)} %product_other.1.q31), channel_id=1, source_target_pairs={{1,3},{6,4},{9,11},{14,12},{17,19},{22,20},{25,27},{30,28}} | collective-permute-start | bytes 3145736 | tf_op jit(solution)/shard_map/ppermute | solution.py:101
  107.2 3.4 %copy-start = (bf16[2048,2048]{1,0:T(8,128)(2,1)}, bf16[2048,2048]{1,0:T(8,128)(2,1)S(1)}, u32[]{:S(2)}) copy-start(bf16[2048,2048]{1,0:T(8,128)(2,1)S(1)} %turn.7.refs_1_) | copy-start | bytes 25165828
  128.4 16.8 %collective-permute-start.13 = (bf16[512,512]{1,0:T(8,128)(2,1)}, bf16[512,512]{1,0:T(8,128)(2,1)}, u32[]{:S(2)}, u32[]{:S(2)}) collective-permute-start(bf16[512,512]{1,0:T(8,128)(2,1)} %multiply.11), channel_id=1, source_target_pairs={{1,3},{6,4},{9,11},{14,12},{17,19},{22,20},{25,27},{30,28}} | collective-permute-start | bytes 1572872 | tf_op jit(solution)/shard_map/ppermute | solution.py:101
  133.0 12.3 %collective-permute-start.11 = (bf16[512,512]{1,0:T(8,128)(2,1)}, bf16[512,512]{1,0:T(8,128)(2,1)S(1)}, u32[]{:S(2)}, u32[]{:S(2)}) collective-permute-start(bf16[512,512]{1,0:T(8,128)(2,1)} %collective-permute-done.8.value_ref.q3_two), channel_id=1, source_target_pairs={{3,2},{4,5},{11,10},{12,13},{19,18},{20,21},{27,26},{28,29}} | collective-permute-start | bytes 1572872 | tf_op jit(solution)/shard_map/ppermute | solution.py:101
  133.7 3.4 %copy-start.3 = (bf16[2048,2048]{1,0:T(8,128)(2,1)S(1)}, bf16[2048,2048]{1,0:T(8,128)(2,1)}, u32[]{:S(2)}) copy-start(bf16[2048,2048]{1,0:T(8,128)(2,1)} %copy-done.2) | copy-start | bytes 25165828
  137.7 5.6 %copy-start.1 = (bf16[2048,2048]{1,0:T(8,128)(2,1)S(1)}, bf16[2048,2048]{1,0:T(8,128)(2,1)}, u32[]{:S(2)}) copy-start(bf16[2048,2048]{1,0:T(8,128)(2,1)} %copy-done) | copy-start | bytes 25165828
  143.4 2.2 %copy-start.7 = (bf16[1,512,2048]{2,1,0:T(8,128)(2,1)S(1)}, bf16[1,512,2048]{2,1,0:T(8,128)(2,1)}, u32[]{:S(2)}) copy-start(bf16[1,512,2048]{2,1,0:T(8,128)(2,1)} %param.7) | copy-start | bytes 6291460
  143.4 2.3 %copy-start.9 = (bf16[512,512]{1,0:T(8,128)(2,1)S(1)}, bf16[512,512]{1,0:T(8,128)(2,1)}, u32[]{:S(2)}) copy-start(bf16[512,512]{1,0:T(8,128)(2,1)} %copy-done.8) | copy-start | bytes 1572868
  143.4 2.3 %copy-start.14 = (s32[5]{0:T(128)S(1)}, s32[5]{0:T(128)}, u32[]{:S(2)}) copy-start(s32[5]{0:T(128)} %tick.3.place_ref) | copy-start | bytes 64
  (5 other events, 5.7 us)

commit v9 on v6

--- a/solution.py
+++ b/solution.py
@@ -21,6 +21,7 @@
 
 
 LIGHT = pl.CostEstimate(flops=1 << 20, bytes_accessed=1 << 16, transcendentals=0)
+HEAVY = pl.CostEstimate(flops=8000000000, bytes_accessed=1 << 16, transcendentals=0)
 
 
 def couple_kernel(rate_ref, class_ref, pivot_ref, out_ref, weight_ref):
@@ -222,31 +223,55 @@
     )(place, half, across, zero)
 
 
-def three_kernel(place_ref, left_ref, right_ref, out_ref, zero_ref):
-    width = zero_ref.shape[1]
-    multiply_kernel(lambda odd: 2 * odd, 2, 1, place_ref, left_ref, right_ref, out_ref)
-
-    @pl.when(place_ref[1] == 1)
-    def _():
-        zero_ref[...] = out_ref[:, pl.ds(pl.multiple_of(place_ref[0] * width, 128), width)]
-
-
-def product_three(place, half, across):
+def ends_kernel(place_ref, left_ref, right_ref, zero_ref, two_ref):
+    for block, out_ref in ((0, zero_ref), (2, two_ref)):
+        first = lambda odd: turned(block, odd)
+        multiply_kernel(first, 1, 1, place_ref, left_ref, right_ref, out_ref)
+
+
+def product_ends(place, half, across):
     rows = half.shape[0]
     width = across.shape[0] // 4
     vmem = pl.BlockSpec(memory_space=pltpu.VMEM)
     return pl.pallas_call(
-        three_kernel,
-        out_shape=(
-            jax.ShapeDtypeStruct((rows, 2 * width), BF16),
-            jax.ShapeDtypeStruct((rows, width), BF16),
-        ),
+        ends_kernel,
+        out_shape=(jax.ShapeDtypeStruct((rows, width), BF16),) * 2,
         in_specs=[pl.BlockSpec(memory_space=pltpu.SMEM)] + [vmem] * 2,
         out_specs=(vmem, vmem),
         compiler_params=pltpu.CompilerParams(vmem_limit_bytes=6 * MIB),
         cost_estimate=LIGHT,
-        name="product_three",
+        name="product_ends",
     )(place, half, across)
+
+
+def rest_kernel(place_ref, left_ref, right_ref, zero_ref, out_ref):
+    odd = place_ref[0]
+    width = zero_ref.shape[1]
+
+    @pl.when(place_ref[1] == 1)
+    def _():
+        out_ref[:, pl.ds(pl.multiple_of(odd * width, 128), width)] = zero_ref[...]
+        for source, target in ((1 + odd, 1 - odd), (3 - 3 * odd, 2)):
+            source = pl.multiple_of(source * width, 128)
+            target = pl.multiple_of(target * width, 128)
+            out_ref[:, pl.ds(target, width)] = jnp.dot(
+                left_ref[...], right_ref[:, pl.ds(source, width)], preferred_element_type=F32
+            ).astype(BF16)
+
+
+def product_rest(place, half, across, zero):
+    rows = half.shape[0]
+    width = across.shape[0] // 4
+    vmem = pl.BlockSpec(memory_space=pltpu.VMEM)
+    return pl.pallas_call(
+        rest_kernel,
+        out_shape=jax.ShapeDtypeStruct((rows, 3 * width), BF16),
+        in_specs=[pl.BlockSpec(memory_space=pltpu.SMEM)] + [vmem] * 3,
+        out_specs=vmem,
+        compiler_params=pltpu.CompilerParams(vmem_limit_bytes=6 * MIB),
+        cost_estimate=LIGHT,
+        name="product_rest",
+    )(place, half, across, zero)
 
 
 def prior_kernel(place_ref, shifted_ref, sigma_ref, out_ref):
@@ -341,9 +366,26 @@
     )(place, *parts)
 
 
+def tick(place, *values, cost=HEAVY):
+    def kernel(place_ref, *refs):
+        for which in range(place.shape[0]):
+            refs[-1][which] = place_ref[which]
+
+    scalars = pl.BlockSpec(memory_space=pltpu.SMEM)
+    return pl.pallas_call(
+        kernel,
+        out_shape=jax.ShapeDtypeStruct(place.shape, place.dtype),
+        in_specs=[scalars] + [pl.BlockSpec(memory_space=pl.ANY)] * len(values),
+        out_specs=scalars,
+        compiler_params=pltpu.CompilerParams(vmem_limit_bytes=MIB),
+        cost_estimate=cost,
+        name="tick",
+    )(place, *values)
+
+
 def final_kernel(
     place_ref, pivot_ref, sigma_ref,
-    q0, q0_last, q2, q2_zero, q2_last, q3_two, q3_other, q3_last,
+    q0, q0_last, q2, q2_zero, q2_last, q3_two, q3,
     q01, q11, q21, q31,
     out_ref, var_ref,
 ):
@@ -398,10 +440,10 @@
 
     @pl.when(active & (place == 3))
     def _():
-        add(at(2 * odd, 2), q3_other[...])
+        add(at(2 * odd, 2), q3[:, : 2 * width])
         add(at(turned(2, odd)), q3_two[...])
-        add(at(turned(3, odd)), q3_last[...])
-        trace(q3_last[:, pl.ds(here, rows)])
+        add(at(turned(3, odd)), q3[:, 2 * width :])
+        trace(q3[:, own(2)])
 
     @pl.when(place_ref[4] == 0)
     def _():
@@ -449,8 +491,7 @@
                 whole(2),
                 whole(0),
                 picked(3, 1),
-                picked(3, 2),
-                picked(3, 1),
+                picked(3, 3),
                 turned_block(lambda odd: 1),
                 picked(1, 1),
                 turned_block(lambda odd: odd),
@@ -503,19 +544,19 @@
     q2 = moved(q2_own, 1, 2)
 
     h3 = multiply(place, c3, prior)
-    q3_two = moved(multiply(place, [h3], across, lambda odd: 2 - odd, 1), 1, 3)
-    q3_own, q30 = product_three(place, h3, across)
-    q3_other = moved(q3_own, 1, 3)
-    q0_last = moved(q30, 1, 0)
+    q30, q32 = product_ends(place, h3, across)
+    q0_last, q3_two = moved(q30, 1, 0), moved(q32, 1, 3)
     across = turn(place, 3, 0, c3[0], after(across, q30))
     across = turn(place, 3, 1, c3[1], across)
-    q33 = multiply(place, [h3], across, lambda odd: 3 - 3 * odd, 1)
-    q3_last = moved(q33, 1, 3)
-    q2_last = moved(after(q3_two, q0, q33), 3, 2)
-    h1 = multiply(place, [after(c1[0], q33), c1[1]], prior)
+    q3_own = product_rest(place, h3, across, q30)
+    q3 = moved(q3_own, 1, 3)
+    q2_last = moved(q3_two, 3, 2)
+    h1 = multiply(place, [after(c1[0], q3_own), c1[1]], prior)
     q11 = multiply(place, [h1], across, lambda odd: 1 + odd, 1)
-    received = (q0, q0_last, q2, q2, q2_last, q3_two, q3_other, q3_last)
+    received = (q0, q0_last, q2, q2, q2_last, q3_two, q3)
     kept = (q0_own, q11, q2_own, q3_own)
+    place = tick(place, q0, cost=LIGHT)
+    place = tick(tick(place, q0_last, q2), q2_last)
     covariance, variances = final(place, pivot, sigma, received, kept)
     return (covariance[None], variances)
 

time: 131 us -> 130 us (level)
  waiting for transfers between devices: 79.3 us -> 76.1 us
  Pallas kernels: 26.7 us -> 28.1 us
    pallas_call x1 -> x5, Pallas kernels: 0.56 us -> 4.7 us  [the longest x3 3.41 us: tick(): pl.pallas_call(kernel, out_shape=jax.ShapeDtypeStruct(place.shape, place....]
    ppermute x14 -> x13, waiting for transfers between devices: 71.3 us -> 68.2 us  [moved(): lax.ppermute(value, ('dom', 'col'), route(source, target, lax.axis_size('...]
    pallas_call x8 -> x6, Pallas kernels: 4.4 us -> 3.3 us  [multiply(): pl.pallas_call(functools.partial(multiply_kernel, first, count, len(lefts...]
    ppermute x14 -> x13, starting transfers between devices: 17.7 us -> 16.9 us  [moved(): lax.ppermute(value, ('dom', 'col'), route(source, target, lax.axis_size('...]
  transfers between devices with their start and end apart: 15 -> 14, of which waited for: 4 -> 4; matrix products, arithmetic and copies ran while one was open for 0% -> 0% of each run, Pallas kernels for 18% -> 20%
where the time goes in v9:
time: 130 us; the launch traced here: 129 us
  waiting for transfers between devices  76.1 us (59%)
  Pallas kernels  28.1 us (22%)
  starting transfers between devices  18.8 us (14%)
  between operations  2.98 us (2%)
  local copies, waits for them, and re-layouts  2.8 us (2%)
    ppermute x13, waiting for transfers between devices, moved(): lax.ppermute(value, ('dom', 'col'), route(source, target, lax.axis_size('...  68.2 us
    ppermute x13, starting transfers between devices, moved(): lax.ppermute(value, ('dom', 'col'), route(source, target, lax.axis_size('...  16.9 us
    ppermute x1, waiting for transfers between devices, passed_along(): lax.ppermute(value, axis, [(source, source + steps) for source in range(i...  7.96 us
    pallas_call x6, Pallas kernels, turn(): pl.pallas_call(turn_kernel, out_shape=jax.ShapeDtypeStruct((nodes, nodes)...  5.99 us
    pallas_call x2, Pallas kernels, couple(): pl.pallas_call(couple_kernel, out_shape=jax.ShapeDtypeStruct((rows, nodes...  4.81 us
    pallas_call x2, Pallas kernels, couple_here(): pl.pallas_call(kernel, out_shape=jax.ShapeDtypeStruct((rows, nodes), BF16...  3.45 us
    pallas_call x3, Pallas kernels, tick(): pl.pallas_call(kernel, out_shape=jax.ShapeDtypeStruct(place.shape, place....  3.41 us
    pallas_call x6, Pallas kernels, multiply(): pl.pallas_call(functools.partial(multiply_kernel, first, count, len(lefts...  3.3 us
  transfers between devices with their start and end apart: 14, of which 4 were waited for; matrix products, arithmetic and copies ran while one was open for 0% of the time, Pallas kernels for 20%

profile of v9, /device:TPU:2, one launch (start us, length us, event | category | flops | bytes accessed | tf_op | source)
XLA Modules:
  0.0 128.8 jit_solution(575087893484146855)
XLA Ops:
  0.6 1.9 %collective-permute-start.2 = (bf16[1,512,2048]{2,1,0:T(8,128)(2,1)}, bf16[1,512,2048]{2,1,0:T(8,128)(2,1)}, u32[]{:S(2)}, u32[]{:S(2)}) collective-permute-start(bf16[1,512,2048]{2,1,0:T(8,128)(2,1)} %param.8), channel_id=1, source_target_pairs={{4,0},{8,4},{12,8},{5,1},{9,5},{13,9},{6,2},{10,6},{14,10},{7,3},{... | collective-permute-start | bytes 6291464 | tf_op jit(solution)/shard_map/ppermute | solution.py:20
  2.6 2.0 %collective-permute-start.1 = (bf16[512,2048]{1,0:T(8,128)(2,1)}, bf16[512,2048]{1,0:T(8,128)(2,1)}, u32[]{:S(2)}, u32[]{:S(2)}) collective-permute-start(bf16[512,2048]{1,0:T(8,128)(2,1)} %bitcast.8), channel_id=1, source_target_pairs={{2,1},{5,6},{10,9},{13,14},{18,17},{21,22},{26,25},{29,30}} | collective-permute-start | bytes 6291464 | tf_op jit(solution)/shard_map/ppermute | solution.py:102
  4.5 2.9 %collective-permute-start = (bf16[512,2048]{1,0:T(8,128)(2,1)}, bf16[512,2048]{1,0:T(8,128)(2,1)S(1)}, u32[]{:S(2)}, u32[]{:S(2)}) collective-permute-start(bf16[512,2048]{1,0:T(8,128)(2,1)} %bitcast.9), channel_id=1, source_target_pairs={{0,1},{7,6},{8,9},{15,14},{16,17},{23,22},{24,25},{31,30}} | collective-permute-start | bytes 6291464 | tf_op jit(solution)/shard_map/ppermute | solution.py:102
  9.5 1.6 %copy-done = bf16[1,512,2048]{2,1,0:T(8,128)(2,1)S(1)} copy-done((bf16[1,512,2048]{2,1,0:T(8,128)(2,1)S(1)}, bf16[1,512,2048]{2,1,0:T(8,128)(2,1)}, u32[]{:S(2)}) %copy-start) | copy-done | bytes 2097176
  11.8 2.4 %couple.3.coupled_ref.refs_0_ = bf16[256,2048]{1,0:T(8,128)(2,1)S(1)} custom-call(f32[1]{0:T(128)S(6)} %copy.19.rate_ref.refs_0_, s32[1,2048]{1,0:T(1,128)S(1)} %bitcast.15, bf16[512,2048]{1,0:T(8,128)(2,1)S(1)} %bitcast.10), custom_call_target="tpu_custom_call" | custom-call | flops 1048576 | bytes 65536 | tf_op jit(solution)/shard_map/couple/pallas_call | solution.py:72
  14.2 2.4 %couple.2.coupled_ref.refs_1_ = bf16[256,2048]{1,0:T(8,128)(2,1)S(1)} custom-call(f32[1]{0:T(128)S(6)} %copy.19.rate_ref.refs_0_, s32[1,2048]{1,0:T(1,128)S(1)} %bitcast.16, bf16[512,2048]{1,0:T(8,128)(2,1)S(1)} %bitcast.11), custom_call_target="tpu_custom_call" | custom-call | flops 1048576 | bytes 65536 | tf_op jit(solution)/shard_map/couple/pallas_call | solution.py:72
  16.6 0.9 turn.6.refs_0_
  17.5 0.9 turn.7.refs_0_
  18.4 8.0 %collective-permute-done.2 = bf16[1,512,2048]{2,1,0:T(8,128)(2,1)} collective-permute-done((bf16[1,512,2048]{2,1,0:T(8,128)(2,1)}, bf16[1,512,2048]{2,1,0:T(8,128)(2,1)}, u32[]{:S(2)}, u32[]{:S(2)}) %collective-permute-start.2) | collective-permute-done | bytes 2097184 | tf_op jit(solution)/shard_map/ppermute | solution.py:20
  26.4 2.1 %prior_parts.1 = (bf16[512,2048]{1,0:T(8,128)(2,1)S(1)}, bf16[512,1536]{1,0:T(8,128)(2,1)S(1)}, bf16[512,1024]{1,0:T(8,128)(2,1)S(1)}, bf16[512,512]{1,0:T(8,128)(2,1)S(1)}) custom-call(s32[5]{0:T(128)S(1)} %stack.16.place_ref, bf16[512,2048]{1,0:T(8,128)(2,1)} %bitcast.5.shifted_ref, bf16[512,2048]{1,0:T(8,128)(2,1)S(1)} %bitcast.13), custom_call_target="tpu_custom_call" | custom-call | flops 1048576 | bytes 65536 | tf_op jit(solution)/shard_map/prior_parts/pallas_call | solution.py:308
  28.5 3.6 %collective-permute-start.5 = (bf16[512,1536]{1,0:T(8,128)(2,1)S(1)}, bf16[512,1536]{1,0:T(8,128)(2,1)S(1)}, u32[]{:S(2)}, u32[]{:S(2)}) collective-permute-start(bf16[512,1536]{1,0:T(8,128)(2,1)S(1)} %get-tuple-element.24), channel_id=1, source_target_pairs={{0,1},{7,6},{8,9},{15,14},{16,17},{23,22},{24,25},{31,30}} | collective-permute-start | bytes 4718600 | tf_op jit(solution)/shard_map/ppermute | solution.py:102
  33.5 2.8 %couple_here.2.coupled_ref.refs_0_ = bf16[512,2048]{1,0:T(8,128)(2,1)S(1)} custom-call(s32[5]{0:T(128)S(1)} %stack.16.place_ref, f32[1]{0:T(128)S(6)} %copy.19.rate_ref.refs_0_, s32[1,2048]{1,0:T(1,128)S(1)} %bitcast.17, bf16[512,2048]{1,0:T(8,128)(2,1)} %collective-permute-done.1.refs_2_), custom_call_target="tpu_custom_call" | custom-call | flops 1048576 | bytes 65536 | tf_op jit(solution)/shard_map/couple_here/pallas_call | solution.py:114
  36.3 1.2 turn.8.refs_0_
  38.2 1.2 turn.9.refs_1_.right_ref.refs_0_
  40.2 13.7 %collective-permute-done.5.far_zero = bf16[512,1536]{1,0:T(8,128)(2,1)S(1)} collective-permute-done((bf16[512,1536]{1,0:T(8,128)(2,1)S(1)}, bf16[512,1536]{1,0:T(8,128)(2,1)S(1)}, u32[]{:S(2)}, u32[]{:S(2)}) %collective-permute-start.5) | collective-permute-done | bytes 1572896 | tf_op jit(solution)/shard_map/ppermute | solution.py:102
  56.3 1.3 %collective-permute-start.6 = (bf16[512,1536]{1,0:T(8,128)(2,1)S(1)}, bf16[512,1536]{1,0:T(8,128)(2,1)S(1)}, u32[]{:S(2)}, u32[]{:S(2)}) collective-permute-start(bf16[512,1536]{1,0:T(8,128)(2,1)S(1)} %multiply.7.zero_ref.q01), channel_id=1, source_target_pairs={{1,0},{6,7},{9,8},{14,15},{17,16},{22,23},{25,24},{30,31}} | collective-permute-start | bytes 4718600 | tf_op jit(solution)/shard_map/ppermute | solution.py:102
  61.4 1.3 %collective-permute-start.9 = (bf16[512,512]{1,0:T(8,128)(2,1)S(1)}, bf16[512,512]{1,0:T(8,128)(2,1)S(1)}, u32[]{:S(2)}, u32[]{:S(2)}) collective-permute-start(bf16[512,512]{1,0:T(8,128)(2,1)S(1)} %get-tuple-element.27.zero_ref), channel_id=1, source_target_pairs={{1,0},{6,7},{9,8},{14,15},{17,16},{22,23},{25,24},{30,31}} | collective-permute-start | bytes 1572872 | tf_op jit(solution)/shard_map/ppermute | solution.py:102
  63.6 0.9 turn.11.right_ref.refs_1_
  67.8 21.4 %collective-permute-done.6.refs_0_.q0 = bf16[512,1536]{1,0:T(8,128)(2,1)S(1)} collective-permute-done((bf16[512,1536]{1,0:T(8,128)(2,1)S(1)}, bf16[512,1536]{1,0:T(8,128)(2,1)S(1)}, u32[]{:S(2)}, u32[]{:S(2)}) %collective-permute-start.6) | collective-permute-done | bytes 1572896 | tf_op jit(solution)/shard_map/ppermute | solution.py:102
  89.2 1.1 tick.3.place_ref
  90.4 33.0 %collective-permute-done.9.refs_0_.q0_last = bf16[512,512]{1,0:T(8,128)(2,1)S(1)} collective-permute-done((bf16[512,512]{1,0:T(8,128)(2,1)S(1)}, bf16[512,512]{1,0:T(8,128)(2,1)S(1)}, u32[]{:S(2)}, u32[]{:S(2)}) %collective-permute-start.9) | collective-permute-done | bytes 524320 | tf_op jit(solution)/shard_map/ppermute | solution.py:102
  123.4 1.1 tick.4.place_ref
  124.5 1.1 tick.5.place_ref
  126.1 2.7 %final.1 = (bf16[512,2048]{1,0:T(8,128)(2,1)}, f32[1,512]{1,0:T(1,128)}) custom-call(s32[5]{0:T(128)S(1)} %tick.5.place_ref, bf16[512,2048]{1,0:T(8,128)(2,1)S(1)} %bitcast.12, bf16[512,2048]{1,0:T(8,128)(2,1)S(1)} %bitcast.14, bf16[512,1536]{1,0:T(8,128)(2,1)S(1)} %collective-permute-done.6.refs_0_.q0, ...), custom_call_target="tpu_custom_call" | custom-call | flops 1048576 | bytes 65536 | tf_op jit(solution)/shard_map/final/pallas_call | solution.py:474
  (40 shorter events, 14.2 us)
Async XLA Ops:
  0.6 25.8 %collective-permute-start.2 = (bf16[1,512,2048]{2,1,0:T(8,128)(2,1)}, bf16[1,512,2048]{2,1,0:T(8,128)(2,1)}, u32[]{:S(2)}, u32[]{:S(2)}) collective-permute-start(bf16[1,512,2048]{2,1,0:T(8,128)(2,1)} %param.8), channel_id=1, source_target_pairs={{4,0},{8,4},{12,8},{5,1},{9,5},{13,9},{6,2},{10,6},{14,10},{7,3},{... | collective-permute-start | bytes 6291464 | tf_op jit(solution)/shard_map/ppermute | solution.py:20
  2.6 30.9 %collective-permute-start.1 = (bf16[512,2048]{1,0:T(8,128)(2,1)}, bf16[512,2048]{1,0:T(8,128)(2,1)}, u32[]{:S(2)}, u32[]{:S(2)}) collective-permute-start(bf16[512,2048]{1,0:T(8,128)(2,1)} %bitcast.8), channel_id=1, source_target_pairs={{2,1},{5,6},{10,9},{13,14},{18,17},{21,22},{26,25},{29,30}} | collective-permute-start | bytes 6291464 | tf_op jit(solution)/shard_map/ppermute | solution.py:102
  4.5 33.0 %collective-permute-start = (bf16[512,2048]{1,0:T(8,128)(2,1)}, bf16[512,2048]{1,0:T(8,128)(2,1)S(1)}, u32[]{:S(2)}, u32[]{:S(2)}) collective-permute-start(bf16[512,2048]{1,0:T(8,128)(2,1)} %bitcast.9), channel_id=1, source_target_pairs={{0,1},{7,6},{8,9},{15,14},{16,17},{23,22},{24,25},{31,30}} | collective-permute-start | bytes 6291464 | tf_op jit(solution)/shard_map/ppermute | solution.py:102
  9.5 1.6 %copy-start = (bf16[1,512,2048]{2,1,0:T(8,128)(2,1)S(1)}, bf16[1,512,2048]{2,1,0:T(8,128)(2,1)}, u32[]{:S(2)}) copy-start(bf16[1,512,2048]{2,1,0:T(8,128)(2,1)} %param.9) | copy-start | bytes 6291460
  11.1 0.7 copy-start.3
  17.5 8.9 %copy-start.2 = (bf16[1,512,2048]{2,1,0:T(8,128)(2,1)S(1)}, bf16[1,512,2048]{2,1,0:T(8,128)(2,1)}, u32[]{:S(2)}) copy-start(bf16[1,512,2048]{2,1,0:T(8,128)(2,1)} %param.7) | copy-start | bytes 6291460
  26.4 7.1 %copy-start.4 = (s32[2048]{0:T(1024)S(1)}, s32[2048]{0:T(1024)}, u32[]{:S(2)}) copy-start(s32[2048]{0:T(1024)} %param.13) | copy-start | bytes 24580
  28.5 25.4 %collective-permute-start.5 = (bf16[512,1536]{1,0:T(8,128)(2,1)S(1)}, bf16[512,1536]{1,0:T(8,128)(2,1)S(1)}, u32[]{:S(2)}, u32[]{:S(2)}) collective-permute-start(bf16[512,1536]{1,0:T(8,128)(2,1)S(1)} %get-tuple-element.24), channel_id=1, source_target_pairs={{0,1},{7,6},{8,9},{15,14},{16,17},{23,22},{24,25},{31,30}} | collective-permute-start | bytes 4718600 | tf_op jit(solution)/shard_map/ppermute | solution.py:102
  32.1 7.4 %collective-permute-start.3 = (bf16[512,1024]{1,0:T(8,128)(2,1)S(1)}, bf16[512,1024]{1,0:T(8,128)(2,1)S(1)}, u32[]{:S(2)}, u32[]{:S(2)}) collective-permute-start(bf16[512,1024]{1,0:T(8,128)(2,1)S(1)} %get-tuple-element.23), channel_id=1, source_target_pairs={{2,1},{5,6},{10,9},{13,14},{18,17},{21,22},{26,25},{29,30}} | collective-permute-start | bytes 3145736 | tf_op jit(solution)/shard_map/ppermute | solution.py:102
  32.8 6.6 %collective-permute-start.4 = (bf16[512,512]{1,0:T(8,128)(2,1)S(1)}, bf16[512,512]{1,0:T(8,128)(2,1)S(1)}, u32[]{:S(2)}, u32[]{:S(2)}) collective-permute-start(bf16[512,512]{1,0:T(8,128)(2,1)S(1)} %get-tuple-element.19), channel_id=1, source_target_pairs={{3,1},{4,6},{11,9},{12,14},{19,17},{20,22},{27,25},{28,30}} | collective-permute-start | bytes 1572872 | tf_op jit(solution)/shard_map/ppermute | solution.py:102
  39.5 20.1 %collective-permute-start.7 = (bf16[256,2048]{1,0:T(8,128)(2,1)S(1)}, bf16[256,2048]{1,0:T(8,128)(2,1)S(1)}, u32[]{:S(2)}, u32[]{:S(2)}) collective-permute-start(bf16[256,2048]{1,0:T(8,128)(2,1)S(1)} %couple.3.coupled_ref.refs_0_), channel_id=1, source_target_pairs={{3,1},{4,6},{11,9},{12,14},{19,17},{20,22},{27,25},{28,30}} | collective-permute-start | bytes 3145736 | tf_op jit(solution)/shard_map/ppermute | solution.py:102
  53.9 5.6 %collective-permute-start.8 = (bf16[256,2048]{1,0:T(8,128)(2,1)S(1)}, bf16[256,2048]{1,0:T(8,128)(2,1)S(1)}, u32[]{:S(2)}, u32[]{:S(2)}) collective-permute-start(bf16[256,2048]{1,0:T(8,128)(2,1)S(1)} %couple.2.coupled_ref.refs_1_), channel_id=1, source_target_pairs={{3,1},{4,6},{11,9},{12,14},{19,17},{20,22},{27,25},{28,30}} | collective-permute-start | bytes 3145736 | tf_op jit(solution)/shard_map/ppermute | solution.py:102
  56.3 32.9 %collective-permute-start.6 = (bf16[512,1536]{1,0:T(8,128)(2,1)S(1)}, bf16[512,1536]{1,0:T(8,128)(2,1)S(1)}, u32[]{:S(2)}, u32[]{:S(2)}) collective-permute-start(bf16[512,1536]{1,0:T(8,128)(2,1)S(1)} %multiply.7.zero_ref.q01), channel_id=1, source_target_pairs={{1,0},{6,7},{9,8},{14,15},{17,16},{22,23},{25,24},{30,31}} | collective-permute-start | bytes 4718600 | tf_op jit(solution)/shard_map/ppermute | solution.py:102
  58.7 31.6 %collective-permute-start.10 = (bf16[512,1536]{1,0:T(8,128)(2,1)S(1)}, bf16[512,1536]{1,0:T(8,128)(2,1)S(1)}, u32[]{:S(2)}, u32[]{:S(2)}) collective-permute-start(bf16[512,1536]{1,0:T(8,128)(2,1)S(1)} %product_two.1.q21), channel_id=1, source_target_pairs={{1,2},{6,5},{9,10},{14,13},{17,18},{22,21},{25,26},{30,29}} | collective-permute-start | bytes 4718600 | tf_op jit(solution)/shard_map/ppermute | solution.py:102
  60.7 6.4 %collective-permute-start.11 = (bf16[512,512]{1,0:T(8,128)(2,1)S(1)}, bf16[512,512]{1,0:T(8,128)(2,1)S(1)}, u32[]{:S(2)}, u32[]{:S(2)}) collective-permute-start(bf16[512,512]{1,0:T(8,128)(2,1)S(1)} %get-tuple-element.29), channel_id=1, source_target_pairs={{1,3},{6,4},{9,11},{14,12},{17,19},{22,20},{25,27},{30,28}} | collective-permute-start | bytes 1572872 | tf_op jit(solution)/shard_map/ppermute | solution.py:102
  61.4 62.0 %collective-permute-start.9 = (bf16[512,512]{1,0:T(8,128)(2,1)S(1)}, bf16[512,512]{1,0:T(8,128)(2,1)S(1)}, u32[]{:S(2)}, u32[]{:S(2)}) collective-permute-start(bf16[512,512]{1,0:T(8,128)(2,1)S(1)} %get-tuple-element.27.zero_ref), channel_id=1, source_target_pairs={{1,0},{6,7},{9,8},{14,15},{17,16},{22,23},{25,24},{30,31}} | collective-permute-start | bytes 1572872 | tf_op jit(solution)/shard_map/ppermute | solution.py:102
  65.2 60.5 %collective-permute-start.13 = (bf16[512,1536]{1,0:T(8,128)(2,1)S(1)}, bf16[512,1536]{1,0:T(8,128)(2,1)S(1)}, u32[]{:S(2)}, u32[]{:S(2)}) collective-permute-start(bf16[512,1536]{1,0:T(8,128)(2,1)S(1)} %product_rest.1.q31), channel_id=1, source_target_pairs={{1,3},{6,4},{9,11},{14,12},{17,19},{22,20},{25,27},{30,28}} | collective-permute-start | bytes 4718600 | tf_op jit(solution)/shard_map/ppermute | solution.py:102
  67.1 57.4 %collective-permute-start.12 = (bf16[512,512]{1,0:T(8,128)(2,1)S(1)}, bf16[512,512]{1,0:T(8,128)(2,1)S(1)}, u32[]{:S(2)}, u32[]{:S(2)}) collective-permute-start(bf16[512,512]{1,0:T(8,128)(2,1)S(1)} %collective-permute-done.11.q3_two), channel_id=1, source_target_pairs={{3,2},{4,5},{11,10},{12,13},{19,18},{20,21},{27,26},{28,29}} | collective-permute-start | bytes 1572872 | tf_op jit(solution)/shard_map/ppermute | solution.py:102
  124.5 1.6 %copy-start.1 = (bf16[1,512,2048]{2,1,0:T(8,128)(2,1)S(1)}, bf16[1,512,2048]{2,1,0:T(8,128)(2,1)}, u32[]{:S(2)}) copy-start(bf16[1,512,2048]{2,1,0:T(8,128)(2,1)} %param.9) | copy-start | bytes 6291460

commit v10 on v9

--- a/solution.py
+++ b/solution.py
@@ -21,7 +21,7 @@
 
 
 LIGHT = pl.CostEstimate(flops=1 << 20, bytes_accessed=1 << 16, transcendentals=0)
-HEAVY = pl.CostEstimate(flops=8000000000, bytes_accessed=1 << 16, transcendentals=0)
+HEAVY = pl.CostEstimate(flops=14000000000, bytes_accessed=1 << 16, transcendentals=0)
 
 
 def couple_kernel(rate_ref, class_ref, pivot_ref, out_ref, weight_ref):
@@ -383,9 +383,9 @@
     )(place, *values)
 
 
-def final_kernel(
+def finish_kernel(
     place_ref, pivot_ref, sigma_ref,
-    q0, q0_last, q2, q2_zero, q2_last, q3_two, q3,
+    q0, q0_last, q2, q2_zero, q3_two,
     q01, q11, q21, q31,
     out_ref, var_ref,
 ):
@@ -393,19 +393,13 @@
     width = nodes // 4
     odd, place = place_ref[0], place_ref[1]
     here = pl.multiple_of(pl.program_id(0) * rows, 128)
-    square = (rows, rows)
-    on_diagonal = lax.broadcasted_iota(jnp.int32, square, 0) == lax.broadcasted_iota(
-        jnp.int32, square, 1
-    )
+    diagonal = diagonal_of(rows)
 
     def at(block, count=1):
         return pl.ds(pl.multiple_of(block * width, 128), count * width)
 
     def own(block):
         return pl.ds(pl.multiple_of(block * width + here, 128), rows)
-
-    def diagonal(value):
-        return jnp.sum(jnp.where(on_diagonal, value, 0.0), axis=0, keepdims=True)
 
     def add(columns, product):
         out_ref[:, columns] = (pivot_ref[:, columns].astype(F32) + product.astype(F32)).astype(BF16)
@@ -435,15 +429,11 @@
     def _():
         add(at(turned(0, odd)), q2_zero[:, pl.ds(here, rows)].T)
         add(at(1, 2), q2[...])
-        add(at(turned(3, odd)), q2_last[:, pl.ds(here, rows)].T)
         trace(q2[:, own(1 - odd)])
 
     @pl.when(active & (place == 3))
     def _():
-        add(at(2 * odd, 2), q3[:, : 2 * width])
         add(at(turned(2, odd)), q3_two[...])
-        add(at(turned(3, odd)), q3[:, 2 * width :])
-        trace(q3[:, own(2)])
 
     @pl.when(place_ref[4] == 0)
     def _():
@@ -451,7 +441,7 @@
         var_ref[...] = diagonal(sigma_ref[:, own(place_ref[2])].astype(F32))
 
 
-def final(place, pivot, sigma, received, kept):
+def finish(place, pivot, sigma, received, kept):
     rows, nodes = pivot.shape
     chunk = 128
     width = nodes // 4
@@ -472,7 +462,7 @@
 
     whole = lambda block: pl.BlockSpec((rows, width), lambda i, place: (0, block))
     return pl.pallas_call(
-        final_kernel,
+        finish_kernel,
         out_shape=(
             jax.ShapeDtypeStruct((rows, nodes), BF16),
             jax.ShapeDtypeStruct((1, rows), F32),
@@ -489,9 +479,7 @@
                 whole(0),
                 picked(2, 2),
                 whole(2),
-                whole(0),
                 picked(3, 1),
-                picked(3, 3),
                 turned_block(lambda odd: 1),
                 picked(1, 1),
                 turned_block(lambda odd: odd),
@@ -503,9 +491,94 @@
             ),
         ),
         compiler_params=pltpu.CompilerParams(vmem_limit_bytes=12 * MIB),
-        cost_estimate=LIGHT,
-        name="final",
+        cost_estimate=HEAVY,
+        name="finish",
     )(place, pivot, sigma, *received, *kept)
+
+
+def last_kernel(place_ref, pivot_ref, q2_last, q3, old_ref, old_var_ref, out_ref, var_ref, sum_ref, sems):
+    rows, nodes = pivot_ref.shape
+    width = nodes // 4
+    chunk = 128
+    odd, place = place_ref[0], place_ref[1]
+    active = place_ref[4] != 0
+
+    def at(block, count=1):
+        return pl.ds(pl.multiple_of(block * width, 128), count * width)
+
+    def copies(here, pieces):
+        return [
+            pltpu.make_async_copy(
+                sum_ref.at[here, source], out_ref.at[here, target], sems.at[which, here.start // chunk]
+            )
+            for which, (source, target, _) in enumerate(pieces)
+        ]
+
+    def write(pieces):
+        for start in range(0, rows, chunk):
+            here = pl.ds(start, chunk)
+            for source, target, product in pieces:
+                value = pivot_ref[here, target].astype(F32) + product(here).astype(F32)
+                sum_ref[here, source] = value.astype(BF16)
+            for copy in copies(here, pieces):
+                copy.start()
+        for start in range(0, rows, chunk):
+            for copy in copies(pl.ds(start, chunk), pieces):
+                copy.wait()
+
+    var_ref[...] = old_var_ref[...]
+
+    @pl.when(active & (place == 2))
+    def _():
+        write([(pl.ds(0, width), at(3 - 3 * odd), lambda here: q2_last[:, here].T)])
+
+    @pl.when(active & (place == 3))
+    def _():
+        both, last = pl.ds(0, 2 * width), pl.ds(2 * width, width)
+        for start in range(0, rows, chunk):
+            here = pl.ds(start, chunk)
+            own = pl.ds(pl.multiple_of(place_ref[2] * width + start, 128), chunk)
+            value = pivot_ref[here, own].astype(F32)
+            value = value + q3[here, pl.ds(2 * width + start, chunk)].astype(F32)
+            var_ref[:, here] = diagonal_of(chunk)(value)
+        write(
+            [
+                (both, at(2 * odd, 2), lambda here: q3[here, both]),
+                (last, at(3 - 3 * odd), lambda here: q3[here, last]),
+            ]
+        )
+
+
+def diagonal_of(rows):
+    square = (rows, rows)
+    on_diagonal = lax.broadcasted_iota(jnp.int32, square, 0) == lax.broadcasted_iota(
+        jnp.int32, square, 1
+    )
+    return lambda value: jnp.sum(jnp.where(on_diagonal, value, 0.0), axis=0, keepdims=True)
+
+
+def finish_last(place, pivot, q2_last, q3, covariance, variances):
+    rows, nodes = pivot.shape
+    width = nodes // 4
+    vmem = pl.BlockSpec(memory_space=pltpu.VMEM)
+    anywhere = pl.BlockSpec(memory_space=pl.ANY)
+    return pl.pallas_call(
+        last_kernel,
+        out_shape=(
+            jax.ShapeDtypeStruct((rows, nodes), BF16),
+            jax.ShapeDtypeStruct((1, rows), F32),
+        ),
+        in_specs=[pl.BlockSpec(memory_space=pltpu.SMEM)] + [vmem] * 3 + [anywhere, vmem],
+        out_specs=(anywhere, vmem),
+        scratch_shapes=[
+            pltpu.VMEM((rows, 3 * width), BF16),
+            pltpu.SemaphoreType.DMA((2, rows // 128)),
+        ],
+        input_output_aliases={4: 0},
+        compiler_params=pltpu.CompilerParams(vmem_limit_bytes=8 * MIB),
+        cost_estimate=LIGHT,
+        name="finish_last",
+    )(place, pivot, q2_last, q3, covariance, variances)
 
 
 def owned(sigma_next, separator, inverse_pivot, coupling_rate, lengths, step_index, node_class):
@@ -553,11 +626,11 @@
     q2_last = moved(q3_two, 3, 2)
     h1 = multiply(place, [after(c1[0], q3_own), c1[1]], prior)
     q11 = multiply(place, [h1], across, lambda odd: 1 + odd, 1)
-    received = (q0, q0_last, q2, q2, q2_last, q3_two, q3)
+    received = (q0, q0_last, q2, q2, q3_two)
     kept = (q0_own, q11, q2_own, q3_own)
-    place = tick(place, q0, cost=LIGHT)
-    place = tick(tick(place, q0_last, q2), q2_last)
-    covariance, variances = final(place, pivot, sigma, received, kept)
+    place_then = tick(place, q0, cost=LIGHT)
+    covariance, variances = finish(place_then, pivot, sigma, received, kept)
+    covariance, variances = finish_last(place, pivot, q2_last, q3, covariance, variances)
     return (covariance[None], variances)
 
 

time: 130 us -> 129 us (level)
  the two profiles are of different devices: /device:TPU:2 before, /device:TPU:6 now
where the time goes in v10:
time: 129 us; the launch traced here: 128 us
  waiting for transfers between devices  76 us (59%)
  Pallas kernels  27.7 us (21%)
  starting transfers between devices  18.9 us (15%)
  between operations  3.11 us (2%)
  local copies, waits for them, and re-layouts  2.39 us (2%)
    ppermute x13, waiting for transfers between devices, moved(): lax.ppermute(value, ('dom', 'col'), route(source, target, lax.axis_size('...  68 us
    ppermute x13, starting transfers between devices, moved(): lax.ppermute(value, ('dom', 'col'), route(source, target, lax.axis_size('...  17 us
    ppermute x1, waiting for transfers between devices, passed_along(): lax.ppermute(value, axis, [(source, source + steps) for source in range(i...  7.96 us
    pallas_call x6, Pallas kernels, turn(): pl.pallas_call(turn_kernel, out_shape=jax.ShapeDtypeStruct((nodes, nodes)...  5.99 us
    pallas_call x2, Pallas kernels, couple(): pl.pallas_call(couple_kernel, out_shape=jax.ShapeDtypeStruct((rows, nodes...  4.81 us
    pallas_call x2, Pallas kernels, couple_here(): pl.pallas_call(kernel, out_shape=jax.ShapeDtypeStruct((rows, nodes), BF16...  3.45 us
    pallas_call x6, Pallas kernels, multiply(): pl.pallas_call(functools.partial(multiply_kernel, first, count, len(lefts...  3.3 us
    pallas_call x1, Pallas kernels, finish(): pl.pallas_call(finish_kernel, out_shape=(jax.ShapeDtypeStruct((rows, node...  3.3 us
  transfers between devices with their start and end apart: 14, of which 4 were waited for; matrix products, arithmetic and copies ran while one was open for 0% of the time, Pallas kernels for 21%

profile of v10, /device:TPU:6, one launch (start us, length us, event | category | flops | bytes accessed | tf_op | source)
XLA Modules:
  0.0 128.0 jit_solution(10506080499768341793)
XLA Ops:
  0.6 1.9 %collective-permute-start = (bf16[1,512,2048]{2,1,0:T(8,128)(2,1)}, bf16[1,512,2048]{2,1,0:T(8,128)(2,1)}, u32[]{:S(2)}, u32[]{:S(2)}) collective-permute-start(bf16[1,512,2048]{2,1,0:T(8,128)(2,1)} %param.8), channel_id=1, source_target_pairs={{4,0},{8,4},{12,8},{5,1},{9,5},{13,9},{6,2},{10,6},{14,10},{7,3},{... | collective-permute-start | bytes 6291464 | tf_op jit(solution)/shard_map/ppermute | solution.py:20
  2.6 2.0 %collective-permute-start.4 = (bf16[512,2048]{1,0:T(8,128)(2,1)}, bf16[512,2048]{1,0:T(8,128)(2,1)}, u32[]{:S(2)}, u32[]{:S(2)}) collective-permute-start(bf16[512,2048]{1,0:T(8,128)(2,1)} %bitcast.8), channel_id=1, source_target_pairs={{2,1},{5,6},{10,9},{13,14},{18,17},{21,22},{26,25},{29,30}} | collective-permute-start | bytes 6291464 | tf_op jit(solution)/shard_map/ppermute | solution.py:102
  4.5 2.9 %collective-permute-start.3 = (bf16[512,2048]{1,0:T(8,128)(2,1)}, bf16[512,2048]{1,0:T(8,128)(2,1)S(1)}, u32[]{:S(2)}, u32[]{:S(2)}) collective-permute-start(bf16[512,2048]{1,0:T(8,128)(2,1)} %bitcast.9), channel_id=1, source_target_pairs={{0,1},{7,6},{8,9},{15,14},{16,17},{23,22},{24,25},{31,30}} | collective-permute-start | bytes 6291464 | tf_op jit(solution)/shard_map/ppermute | solution.py:102
  9.5 1.6 %copy-done = bf16[1,512,2048]{2,1,0:T(8,128)(2,1)S(1)} copy-done((bf16[1,512,2048]{2,1,0:T(8,128)(2,1)S(1)}, bf16[1,512,2048]{2,1,0:T(8,128)(2,1)}, u32[]{:S(2)}) %copy-start) | copy-done | bytes 2097176
  11.8 2.4 %couple.2.coupled_ref.refs_0_ = bf16[256,2048]{1,0:T(8,128)(2,1)S(1)} custom-call(f32[1]{0:T(128)S(6)} %copy.21.rate_ref.refs_0_, s32[1,2048]{1,0:T(1,128)S(1)} %bitcast.16, bf16[512,2048]{1,0:T(8,128)(2,1)S(1)} %bitcast.10), custom_call_target="tpu_custom_call" | custom-call | flops 1048576 | bytes 65536 | tf_op jit(solution)/shard_map/couple/pallas_call | solution.py:72
  14.2 2.4 %couple.3.coupled_ref.refs_1_ = bf16[256,2048]{1,0:T(8,128)(2,1)S(1)} custom-call(f32[1]{0:T(128)S(6)} %copy.21.rate_ref.refs_0_, s32[1,2048]{1,0:T(1,128)S(1)} %bitcast.17, bf16[512,2048]{1,0:T(8,128)(2,1)S(1)} %bitcast.11), custom_call_target="tpu_custom_call" | custom-call | flops 1048576 | bytes 65536 | tf_op jit(solution)/shard_map/couple/pallas_call | solution.py:72
  16.6 0.9 turn.6.refs_0_
  17.5 0.9 turn.7.refs_0_
  18.4 8.0 %collective-permute-done = bf16[1,512,2048]{2,1,0:T(8,128)(2,1)} collective-permute-done((bf16[1,512,2048]{2,1,0:T(8,128)(2,1)}, bf16[1,512,2048]{2,1,0:T(8,128)(2,1)}, u32[]{:S(2)}, u32[]{:S(2)}) %collective-permute-start) | collective-permute-done | bytes 2097184 | tf_op jit(solution)/shard_map/ppermute | solution.py:20
  26.4 2.1 %prior_parts.1 = (bf16[512,2048]{1,0:T(8,128)(2,1)S(1)}, bf16[512,1536]{1,0:T(8,128)(2,1)S(1)}, bf16[512,1024]{1,0:T(8,128)(2,1)S(1)}, bf16[512,512]{1,0:T(8,128)(2,1)S(1)}) custom-call(s32[5]{0:T(128)S(1)} %stack.16.place_ref, bf16[512,2048]{1,0:T(8,128)(2,1)} %bitcast.5.shifted_ref, bf16[512,2048]{1,0:T(8,128)(2,1)S(1)} %bitcast.14), custom_call_target="tpu_custom_call" | custom-call | flops 1048576 | bytes 65536 | tf_op jit(solution)/shard_map/prior_parts/pallas_call | solution.py:308
  28.5 3.6 %collective-permute-start.6 = (bf16[512,1536]{1,0:T(8,128)(2,1)S(1)}, bf16[512,1536]{1,0:T(8,128)(2,1)S(1)}, u32[]{:S(2)}, u32[]{:S(2)}) collective-permute-start(bf16[512,1536]{1,0:T(8,128)(2,1)S(1)} %get-tuple-element.26), channel_id=1, source_target_pairs={{0,1},{7,6},{8,9},{15,14},{16,17},{23,22},{24,25},{31,30}} | collective-permute-start | bytes 4718600 | tf_op jit(solution)/shard_map/ppermute | solution.py:102
  33.5 2.8 %couple_here.2.coupled_ref.refs_0_ = bf16[512,2048]{1,0:T(8,128)(2,1)S(1)} custom-call(s32[5]{0:T(128)S(1)} %stack.16.place_ref, f32[1]{0:T(128)S(6)} %copy.21.rate_ref.refs_0_, s32[1,2048]{1,0:T(1,128)S(1)} %bitcast.18, bf16[512,2048]{1,0:T(8,128)(2,1)} %collective-permute-done.4.refs_2_), custom_call_target="tpu_custom_call" | custom-call | flops 1048576 | bytes 65536 | tf_op jit(solution)/shard_map/couple_here/pallas_call | solution.py:114
  36.3 1.2 turn.8.refs_0_
  38.2 1.2 turn.9.right_ref.refs_0_.refs_1_
  40.2 13.4 %collective-permute-done.6.far_zero = bf16[512,1536]{1,0:T(8,128)(2,1)S(1)} collective-permute-done((bf16[512,1536]{1,0:T(8,128)(2,1)S(1)}, bf16[512,1536]{1,0:T(8,128)(2,1)S(1)}, u32[]{:S(2)}, u32[]{:S(2)}) %collective-permute-start.6) | collective-permute-done | bytes 1572896 | tf_op jit(solution)/shard_map/ppermute | solution.py:102
  56.0 1.3 %collective-permute-start.11 = (bf16[512,1536]{1,0:T(8,128)(2,1)S(1)}, bf16[512,1536]{1,0:T(8,128)(2,1)S(1)}, u32[]{:S(2)}, u32[]{:S(2)}) collective-permute-start(bf16[512,1536]{1,0:T(8,128)(2,1)S(1)} %multiply.8.zero_ref.q01), channel_id=1, source_target_pairs={{1,0},{6,7},{9,8},{14,15},{17,16},{22,23},{25,24},{30,31}} | collective-permute-start | bytes 4718600 | tf_op jit(solution)/shard_map/ppermute | solution.py:102
  61.0 1.3 %collective-permute-start.12 = (bf16[512,512]{1,0:T(8,128)(2,1)S(1)}, bf16[512,512]{1,0:T(8,128)(2,1)S(1)}, u32[]{:S(2)}, u32[]{:S(2)}) collective-permute-start(bf16[512,512]{1,0:T(8,128)(2,1)S(1)} %get-tuple-element.30.zero_ref), channel_id=1, source_target_pairs={{1,0},{6,7},{9,8},{14,15},{17,16},{22,23},{25,24},{30,31}} | collective-permute-start | bytes 1572872 | tf_op jit(solution)/shard_map/ppermute | solution.py:102
  62.3 0.9 turn.10.refs_0_
  63.2 0.9 turn.11.right_ref.refs_1_
  67.6 21.3 %collective-permute-done.11.refs_0_.q0 = bf16[512,1536]{1,0:T(8,128)(2,1)S(1)} collective-permute-done((bf16[512,1536]{1,0:T(8,128)(2,1)S(1)}, bf16[512,1536]{1,0:T(8,128)(2,1)S(1)}, u32[]{:S(2)}, u32[]{:S(2)}) %collective-permute-start.11) | collective-permute-done | bytes 1572896 | tf_op jit(solution)/shard_map/ppermute | solution.py:102
  88.9 1.1 tick.1.place_ref
  90.0 33.4 %collective-permute-done.12.q0_last = bf16[512,512]{1,0:T(8,128)(2,1)S(1)} collective-permute-done((bf16[512,512]{1,0:T(8,128)(2,1)S(1)}, bf16[512,512]{1,0:T(8,128)(2,1)S(1)}, u32[]{:S(2)}, u32[]{:S(2)}) %collective-permute-start.12) | collective-permute-done | bytes 524320 | tf_op jit(solution)/shard_map/ppermute | solution.py:102
  123.4 3.3 %finish.1 = (bf16[512,2048]{1,0:T(8,128)(2,1)}, f32[1,512]{1,0:T(1,128)S(1)}) custom-call(s32[5]{0:T(128)S(1)} %tick.1.place_ref, bf16[512,2048]{1,0:T(8,128)(2,1)S(1)} %bitcast.12, bf16[512,2048]{1,0:T(8,128)(2,1)S(1)} %bitcast.15, bf16[512,1536]{1,0:T(8,128)(2,1)S(1)} %collective-permute-done.11.refs_0_.q0, ...), custom_call_target="tpu_custom_call" | custom-call | flops 14000000000 | bytes 65536 | tf_op jit(solution)/shard_map/finish/pallas_call | solution.py:464
  126.7 1.2 finish_last.1
  (39 shorter events, 13.1 us)
Async XLA Ops:
  0.6 25.8 %collective-permute-start = (bf16[1,512,2048]{2,1,0:T(8,128)(2,1)}, bf16[1,512,2048]{2,1,0:T(8,128)(2,1)}, u32[]{:S(2)}, u32[]{:S(2)}) collective-permute-start(bf16[1,512,2048]{2,1,0:T(8,128)(2,1)} %param.8), channel_id=1, source_target_pairs={{4,0},{8,4},{12,8},{5,1},{9,5},{13,9},{6,2},{10,6},{14,10},{7,3},{... | collective-permute-start | bytes 6291464 | tf_op jit(solution)/shard_map/ppermute | solution.py:20
  2.6 30.9 %collective-permute-start.4 = (bf16[512,2048]{1,0:T(8,128)(2,1)}, bf16[512,2048]{1,0:T(8,128)(2,1)}, u32[]{:S(2)}, u32[]{:S(2)}) collective-permute-start(bf16[512,2048]{1,0:T(8,128)(2,1)} %bitcast.8), channel_id=1, source_target_pairs={{2,1},{5,6},{10,9},{13,14},{18,17},{21,22},{26,25},{29,30}} | collective-permute-start | bytes 6291464 | tf_op jit(solution)/shard_map/ppermute | solution.py:102
  4.5 33.0 %collective-permute-start.3 = (bf16[512,2048]{1,0:T(8,128)(2,1)}, bf16[512,2048]{1,0:T(8,128)(2,1)S(1)}, u32[]{:S(2)}, u32[]{:S(2)}) collective-permute-start(bf16[512,2048]{1,0:T(8,128)(2,1)} %bitcast.9), channel_id=1, source_target_pairs={{0,1},{7,6},{8,9},{15,14},{16,17},{23,22},{24,25},{31,30}} | collective-permute-start | bytes 6291464 | tf_op jit(solution)/shard_map/ppermute | solution.py:102
  9.5 1.6 %copy-start = (bf16[1,512,2048]{2,1,0:T(8,128)(2,1)S(1)}, bf16[1,512,2048]{2,1,0:T(8,128)(2,1)}, u32[]{:S(2)}) copy-start(bf16[1,512,2048]{2,1,0:T(8,128)(2,1)} %param.9) | copy-start | bytes 6291460
  11.1 0.7 copy-start.3
  17.5 8.9 %copy-start.2 = (bf16[1,512,2048]{2,1,0:T(8,128)(2,1)S(1)}, bf16[1,512,2048]{2,1,0:T(8,128)(2,1)}, u32[]{:S(2)}) copy-start(bf16[1,512,2048]{2,1,0:T(8,128)(2,1)} %param.7) | copy-start | bytes 6291460
  26.4 7.1 %copy-start.4 = (s32[2048]{0:T(1024)S(1)}, s32[2048]{0:T(1024)}, u32[]{:S(2)}) copy-start(s32[2048]{0:T(1024)} %param.13) | copy-start | bytes 24580
  28.5 25.1 %collective-permute-start.6 = (bf16[512,1536]{1,0:T(8,128)(2,1)S(1)}, bf16[512,1536]{1,0:T(8,128)(2,1)S(1)}, u32[]{:S(2)}, u32[]{:S(2)}) collective-permute-start(bf16[512,1536]{1,0:T(8,128)(2,1)S(1)} %get-tuple-element.26), channel_id=1, source_target_pairs={{0,1},{7,6},{8,9},{15,14},{16,17},{23,22},{24,25},{31,30}} | collective-permute-start | bytes 4718600 | tf_op jit(solution)/shard_map/ppermute | solution.py:102
  32.1 7.4 %collective-permute-start.2 = (bf16[512,1024]{1,0:T(8,128)(2,1)S(1)}, bf16[512,1024]{1,0:T(8,128)(2,1)S(1)}, u32[]{:S(2)}, u32[]{:S(2)}) collective-permute-start(bf16[512,1024]{1,0:T(8,128)(2,1)S(1)} %get-tuple-element.22), channel_id=1, source_target_pairs={{2,1},{5,6},{10,9},{13,14},{18,17},{21,22},{26,25},{29,30}} | collective-permute-start | bytes 3145736 | tf_op jit(solution)/shard_map/ppermute | solution.py:102
  32.8 6.6 %collective-permute-start.1 = (bf16[512,512]{1,0:T(8,128)(2,1)S(1)}, bf16[512,512]{1,0:T(8,128)(2,1)S(1)}, u32[]{:S(2)}, u32[]{:S(2)}) collective-permute-start(bf16[512,512]{1,0:T(8,128)(2,1)S(1)} %get-tuple-element.21), channel_id=1, source_target_pairs={{3,1},{4,6},{11,9},{12,14},{19,17},{20,22},{27,25},{28,30}} | collective-permute-start | bytes 1572872 | tf_op jit(solution)/shard_map/ppermute | solution.py:102
  39.5 19.7 %collective-permute-start.5 = (bf16[256,2048]{1,0:T(8,128)(2,1)S(1)}, bf16[256,2048]{1,0:T(8,128)(2,1)S(1)}, u32[]{:S(2)}, u32[]{:S(2)}) collective-permute-start(bf16[256,2048]{1,0:T(8,128)(2,1)S(1)} %couple.2.coupled_ref.refs_0_), channel_id=1, source_target_pairs={{3,1},{4,6},{11,9},{12,14},{19,17},{20,22},{27,25},{28,30}} | collective-permute-start | bytes 3145736 | tf_op jit(solution)/shard_map/ppermute | solution.py:102
  53.6 5.6 %collective-permute-start.7 = (bf16[256,2048]{1,0:T(8,128)(2,1)S(1)}, bf16[256,2048]{1,0:T(8,128)(2,1)S(1)}, u32[]{:S(2)}, u32[]{:S(2)}) collective-permute-start(bf16[256,2048]{1,0:T(8,128)(2,1)S(1)} %couple.3.coupled_ref.refs_1_), channel_id=1, source_target_pairs={{3,1},{4,6},{11,9},{12,14},{19,17},{20,22},{27,25},{28,30}} | collective-permute-start | bytes 3145736 | tf_op jit(solution)/shard_map/ppermute | solution.py:102
  56.0 32.9 %collective-permute-start.11 = (bf16[512,1536]{1,0:T(8,128)(2,1)S(1)}, bf16[512,1536]{1,0:T(8,128)(2,1)S(1)}, u32[]{:S(2)}, u32[]{:S(2)}) collective-permute-start(bf16[512,1536]{1,0:T(8,128)(2,1)S(1)} %multiply.8.zero_ref.q01), channel_id=1, source_target_pairs={{1,0},{6,7},{9,8},{14,15},{17,16},{22,23},{25,24},{30,31}} | collective-permute-start | bytes 4718600 | tf_op jit(solution)/shard_map/ppermute | solution.py:102
  58.4 31.6 %collective-permute-start.13 = (bf16[512,1536]{1,0:T(8,128)(2,1)S(1)}, bf16[512,1536]{1,0:T(8,128)(2,1)S(1)}, u32[]{:S(2)}, u32[]{:S(2)}) collective-permute-start(bf16[512,1536]{1,0:T(8,128)(2,1)S(1)} %product_two.1.q21), channel_id=1, source_target_pairs={{1,2},{6,5},{9,10},{14,13},{17,18},{22,21},{25,26},{30,29}} | collective-permute-start | bytes 4718600 | tf_op jit(solution)/shard_map/ppermute | solution.py:102
  60.3 6.4 %collective-permute-start.8 = (bf16[512,512]{1,0:T(8,128)(2,1)S(1)}, bf16[512,512]{1,0:T(8,128)(2,1)S(1)}, u32[]{:S(2)}, u32[]{:S(2)}) collective-permute-start(bf16[512,512]{1,0:T(8,128)(2,1)S(1)} %get-tuple-element.29), channel_id=1, source_target_pairs={{1,3},{6,4},{9,11},{14,12},{17,19},{22,20},{25,27},{30,28}} | collective-permute-start | bytes 1572872 | tf_op jit(solution)/shard_map/ppermute | solution.py:102
  61.0 62.4 %collective-permute-start.12 = (bf16[512,512]{1,0:T(8,128)(2,1)S(1)}, bf16[512,512]{1,0:T(8,128)(2,1)S(1)}, u32[]{:S(2)}, u32[]{:S(2)}) collective-permute-start(bf16[512,512]{1,0:T(8,128)(2,1)S(1)} %get-tuple-element.30.zero_ref), channel_id=1, source_target_pairs={{1,0},{6,7},{9,8},{14,15},{17,16},{22,23},{25,24},{30,31}} | collective-permute-start | bytes 1572872 | tf_op jit(solution)/shard_map/ppermute | solution.py:102
  64.8 61.8 %collective-permute-start.10 = (bf16[512,1536]{1,0:T(8,128)(2,1)S(1)}, bf16[512,1536]{1,0:T(8,128)(2,1)S(1)}, u32[]{:S(2)}, u32[]{:S(2)}) collective-permute-start(bf16[512,1536]{1,0:T(8,128)(2,1)S(1)} %product_rest.1.q31), channel_id=1, source_target_pairs={{1,3},{6,4},{9,11},{14,12},{17,19},{22,20},{25,27},{30,28}} | collective-permute-start | bytes 4718600 | tf_op jit(solution)/shard_map/ppermute | solution.py:102
  66.2 57.2 %copy-start.1 = (bf16[1,512,2048]{2,1,0:T(8,128)(2,1)S(1)}, bf16[1,512,2048]{2,1,0:T(8,128)(2,1)}, u32[]{:S(2)}) copy-start(bf16[1,512,2048]{2,1,0:T(8,128)(2,1)} %param.9) | copy-start | bytes 6291460
  66.7 59.9 %collective-permute-start.9 = (bf16[512,512]{1,0:T(8,128)(2,1)S(1)}, bf16[512,512]{1,0:T(8,128)(2,1)S(1)}, u32[]{:S(2)}, u32[]{:S(2)}) collective-permute-start(bf16[512,512]{1,0:T(8,128)(2,1)S(1)} %collective-permute-done.8.q3_two), channel_id=1, source_target_pairs={{3,2},{4,5},{11,10},{12,13},{19,18},{20,21},{27,26},{28,29}} | collective-permute-start | bytes 1572872 | tf_op jit(solution)/shard_map/ppermute | solution.py:102

commit v11 on v10

--- a/solution.py
+++ b/solution.py
@@ -21,6 +21,7 @@
 
 
 LIGHT = pl.CostEstimate(flops=1 << 20, bytes_accessed=1 << 16, transcendentals=0)
+MEDIUM = pl.CostEstimate(flops=2000000000, bytes_accessed=1 << 16, transcendentals=0)
 HEAVY = pl.CostEstimate(flops=14000000000, bytes_accessed=1 << 16, transcendentals=0)
 
 
@@ -223,25 +224,68 @@
     )(place, half, across, zero)
 
 
-def ends_kernel(place_ref, left_ref, right_ref, zero_ref, two_ref):
-    for block, out_ref in ((0, zero_ref), (2, two_ref)):
-        first = lambda odd: turned(block, odd)
-        multiply_kernel(first, 1, 1, place_ref, left_ref, right_ref, out_ref)
-
-
-def product_ends(place, half, across):
-    rows = half.shape[0]
-    width = across.shape[0] // 4
+def half_kernel(place_ref, left_ref, right_ref, one_ref, out_ref):
+    width = one_ref.shape[1]
+
+    @pl.when(place_ref[1] == 1)
+    def _():
+        def block(step, carry):
+            which = turned(step + (step > 0).astype(jnp.int32), place_ref[0])
+            columns = pl.ds(pl.multiple_of(which * width, 128), width)
+            out_ref[:, columns] = jnp.dot(
+                left_ref[...], right_ref[:, columns], preferred_element_type=F32
+            ).astype(BF16)
+            return carry
+
+        lax.fori_loop(0, 3, block, 0)
+        columns = pl.ds(pl.multiple_of(turned(1, place_ref[0]) * width, 128), width)
+        out_ref[:, columns] = one_ref[...]
+
+
+def half_product(place, left, right, one):
     vmem = pl.BlockSpec(memory_space=pltpu.VMEM)
     return pl.pallas_call(
-        ends_kernel,
-        out_shape=(jax.ShapeDtypeStruct((rows, width), BF16),) * 2,
-        in_specs=[pl.BlockSpec(memory_space=pltpu.SMEM)] + [vmem] * 2,
-        out_specs=(vmem, vmem),
+        half_kernel,
+        out_shape=jax.ShapeDtypeStruct(left.shape, BF16),
+        in_specs=[pl.BlockSpec(memory_space=pltpu.SMEM)] + [vmem] * 3,
+        out_specs=vmem,
         compiler_params=pltpu.CompilerParams(vmem_limit_bytes=6 * MIB),
         cost_estimate=LIGHT,
-        name="product_ends",
-    )(place, half, across)
+        name="half_product",
+    )(place, left, right, one)
+
+
+def column_kernel(place_ref, own_ref, first_ref, second_ref, *refs):
+    column_ref, out_refs = refs[0], refs[1:]
+
+    @pl.when(place_ref[1] == 1)
+    def _():
+        width = own_ref.shape[0]
+        for block in range(4):
+            rows = pl.ds(block * width, width)
+            column_ref[rows, :] = own_ref[:, rows].T
+        for left_ref, out_ref in zip((first_ref, second_ref), out_refs):
+            out_ref[...] = jnp.dot(
+                left_ref[...], column_ref[...], preferred_element_type=F32
+            ).astype(BF16)
+
+
+def own_column(place, own, first, second):
+    rows, nodes = own.shape
+    vmem = pl.BlockSpec(memory_space=pltpu.VMEM)
+    return pl.pallas_call(
+        column_kernel,
+        out_shape=(
+            jax.ShapeDtypeStruct((nodes, rows), BF16),
+            jax.ShapeDtypeStruct((rows, rows), BF16),
+            jax.ShapeDtypeStruct((rows, rows), BF16),
+        ),
+        in_specs=[pl.BlockSpec(memory_space=pltpu.SMEM)] + [vmem] * 3,
+        out_specs=(vmem, vmem, vmem),
+        compiler_params=pltpu.CompilerParams(vmem_limit_bytes=6 * MIB),
+        cost_estimate=LIGHT,
+        name="own_column",
+    )(place, own, first, second)
 
 
 def rest_kernel(place_ref, left_ref, right_ref, zero_ref, out_ref):
@@ -327,7 +371,7 @@
     )(place, shifted, sigma)
 
 
-def assemble_kernel(place_ref, own, near_two, last_three, far_zero, out_ref):
+def assemble_kernel(place_ref, own, column, near_two, last_three, far_zero, out_ref):
     @pl.when(place_ref[1] == 1)
     def _():
         odd = place_ref[0]
@@ -344,11 +388,11 @@
         out_ref[at(row[0]), at(row[0])] = far_zero[:, :width]
         out_ref[at(row[0]), half] = far_zero[:, width:]
         out_ref[at(row[3]), at(row[3])] = last_three[...]
+        for block in (0, 2, 3):
+            out_ref[at(row[block]), at(row[1])] = column[at(row[block]), :]
         for step in range(2):
-            out_ref[at(near + step), at(row[1])] = own[:, at(near + step)].T
             piece = slice((1 + step) * width, (2 + step) * width)
             out_ref[at(near + step), at(row[0])] = far_zero[:, piece].T
-        out_ref[at(row[0]), at(row[1])] = own[:, at(row[0])].T
         out_ref[at(row[3]), at(row[2])] = near_two[:, at(1 - odd)].T
 
 
@@ -358,7 +402,7 @@
     return pl.pallas_call(
         assemble_kernel,
         out_shape=jax.ShapeDtypeStruct((nodes, nodes), BF16),
-        in_specs=[pl.BlockSpec(memory_space=pltpu.SMEM)] + [vmem] * 4,
+        in_specs=[pl.BlockSpec(memory_space=pltpu.SMEM)] + [vmem] * 5,
         out_specs=vmem,
         compiler_params=pltpu.CompilerParams(vmem_limit_bytes=6 * MIB),
         cost_estimate=LIGHT,
@@ -603,32 +647,35 @@
     across = turn(place, 2, 0, c2, across)
     c0 = couple_here(place, after(p0, across), node_class, coupling_rate)
     across = turn(place, 0, 0, c0, across)
+    column, h0_one, h2_one = own_column(place, row, c0, c2)
     c3 = [
         moved(after(c1[0], last_three, near_two, across), 3, 1),
-        moved(after(c1[1], far_zero), 3, 1),
+        moved(after(c1[1], far_zero, h2_one), 3, 1),
     ]
-    prior = assemble(place, row, near_two, last_three, far_zero)
-
-    h0 = multiply(place, [c0], prior)
+    prior = assemble(place, row, column, near_two, last_three, far_zero)
+
+    h0 = half_product(place, c0, prior, h0_one)
     q0_own = multiply(place, [h0], across, lambda odd: odd, 3)
     q0 = moved(q0_own, 1, 0)
-    h2 = multiply(place, [after(c2, q0_own)], prior)
+    h2 = half_product(place, after(c2, q0_own), prior, h2_one)
     q2_own = product_two(place, h2, across, q0_own)
     q2 = moved(q2_own, 1, 2)
 
     h3 = multiply(place, c3, prior)
-    q30, q32 = product_ends(place, h3, across)
-    q0_last, q3_two = moved(q30, 1, 0), moved(q32, 1, 3)
-    across = turn(place, 3, 0, c3[0], after(across, q30))
+    q30 = multiply(place, [h3], across, lambda odd: 3 * odd, 1)
+    q0_last = moved(q30, 1, 0)
+    q32 = multiply(place, [after(h3, q30)], across, lambda odd: 2 - odd, 1)
+    q3_two = moved(q32, 1, 3)
+    across = turn(place, 3, 0, c3[0], after(across, q32))
     across = turn(place, 3, 1, c3[1], across)
     q3_own = product_rest(place, h3, across, q30)
     q3 = moved(q3_own, 1, 3)
-    q2_last = moved(q3_two, 3, 2)
     h1 = multiply(place, [after(c1[0], q3_own), c1[1]], prior)
     q11 = multiply(place, [h1], across, lambda odd: 1 + odd, 1)
     received = (q0, q0_last, q2, q2, q3_two)
     kept = (q0_own, q11, q2_own, q3_own)
-    place_then = tick(place, q0, cost=LIGHT)
+    place_then = tick(tick(place, q0, cost=LIGHT), q0_last, cost=MEDIUM)
+    q2_last = moved(after(q3_two, place_then), 3, 2)
     covariance, variances = finish(place_then, pivot, sigma, received, kept)
     covariance, variances = finish_last(place, pivot, q2_last, q3, covariance, variances)
     return (covariance[None], variances)

time: 129 us -> 125 us (0.969)
  the two profiles are of different devices: /device:TPU:6 before, /device:TPU:1 now
where the time goes in v11:
time: 125 us; the launch traced here: 124 us
  waiting for transfers between devices  60.6 us (48%)
  Pallas kernels  30.5 us (24%)
  starting transfers between devices  27.2 us (22%)
  between operations  3.12 us (2%)
  local copies, waits for them, and re-layouts  2.39 us (2%)
    ppermute x13, waiting for transfers between devices, moved(): lax.ppermute(value, ('dom', 'col'), route(source, target, lax.axis_size('...  47.7 us
    ppermute x13, starting transfers between devices, moved(): lax.ppermute(value, ('dom', 'col'), route(source, target, lax.axis_size('...  25.3 us
    ppermute x1, waiting for transfers between devices, passed_along(): lax.ppermute(value, axis, [(source, source + steps) for source in range(i...  12.8 us
    pallas_call x6, Pallas kernels, turn(): pl.pallas_call(turn_kernel, out_shape=jax.ShapeDtypeStruct((nodes, nodes)...  5.99 us
    pallas_call x2, Pallas kernels, couple(): pl.pallas_call(couple_kernel, out_shape=jax.ShapeDtypeStruct((rows, nodes...  4.81 us
    pallas_call x6, Pallas kernels, multiply(): pl.pallas_call(functools.partial(multiply_kernel, first, count, len(lefts...  3.48 us
    pallas_call x2, Pallas kernels, couple_here(): pl.pallas_call(kernel, out_shape=jax.ShapeDtypeStruct((rows, nodes), BF16...  3.45 us
    pallas_call x1, Pallas kernels, finish(): pl.pallas_call(finish_kernel, out_shape=(jax.ShapeDtypeStruct((rows, node...  2.68 us
  transfers between devices with their start and end apart: 14, of which 7 were waited for; matrix products, arithmetic and copies ran while one was open for 0% of the time, Pallas kernels for 23%

profile of v11, /device:TPU:1, one launch (start us, length us, event | category | flops | bytes accessed | tf_op | source)
XLA Modules:
  0.0 123.8 jit_solution(11133196410061385431)
XLA Ops:
  0.6 2.0 %collective-permute-start = (bf16[1,512,2048]{2,1,0:T(8,128)(2,1)}, bf16[1,512,2048]{2,1,0:T(8,128)(2,1)}, u32[]{:S(2)}, u32[]{:S(2)}) collective-permute-start(bf16[1,512,2048]{2,1,0:T(8,128)(2,1)} %param.8), channel_id=1, source_target_pairs={{4,0},{8,4},{12,8},{5,1},{9,5},{13,9},{6,2},{10,6},{14,10},{7,3},{... | collective-permute-start | bytes 6291464 | tf_op jit(solution)/shard_map/ppermute | solution.py:20
  2.6 2.0 %collective-permute-start.4 = (bf16[512,2048]{1,0:T(8,128)(2,1)}, bf16[512,2048]{1,0:T(8,128)(2,1)}, u32[]{:S(2)}, u32[]{:S(2)}) collective-permute-start(bf16[512,2048]{1,0:T(8,128)(2,1)} %bitcast.8), channel_id=1, source_target_pairs={{2,1},{5,6},{10,9},{13,14},{18,17},{21,22},{26,25},{29,30}} | collective-permute-start | bytes 6291464 | tf_op jit(solution)/shard_map/ppermute | solution.py:103
  7.4 1.6 %copy-done = bf16[1,512,2048]{2,1,0:T(8,128)(2,1)S(1)} copy-done((bf16[1,512,2048]{2,1,0:T(8,128)(2,1)S(1)}, bf16[1,512,2048]{2,1,0:T(8,128)(2,1)}, u32[]{:S(2)}) %copy-start) | copy-done | bytes 2097176
  9.7 2.4 %couple.2.coupled_ref.refs_0_ = bf16[256,2048]{1,0:T(8,128)(2,1)S(1)} custom-call(f32[1]{0:T(128)S(6)} %copy.21.rate_ref.refs_0_, s32[1,2048]{1,0:T(1,128)S(1)} %bitcast.16, bf16[512,2048]{1,0:T(8,128)(2,1)S(1)} %bitcast.10), custom_call_target="tpu_custom_call" | custom-call | flops 1048576 | bytes 65536 | tf_op jit(solution)/shard_map/couple/pallas_call | solution.py:73
  12.1 2.4 %couple.3.coupled_ref.refs_1_ = bf16[256,2048]{1,0:T(8,128)(2,1)S(1)} custom-call(f32[1]{0:T(128)S(6)} %copy.21.rate_ref.refs_0_, s32[1,2048]{1,0:T(1,128)S(1)} %bitcast.17, bf16[512,2048]{1,0:T(8,128)(2,1)S(1)} %bitcast.11), custom_call_target="tpu_custom_call" | custom-call | flops 1048576 | bytes 65536 | tf_op jit(solution)/shard_map/couple/pallas_call | solution.py:73
  16.3 12.8 %collective-permute-done = bf16[1,512,2048]{2,1,0:T(8,128)(2,1)} collective-permute-done((bf16[1,512,2048]{2,1,0:T(8,128)(2,1)}, bf16[1,512,2048]{2,1,0:T(8,128)(2,1)}, u32[]{:S(2)}, u32[]{:S(2)}) %collective-permute-start) | collective-permute-done | bytes 2097184 | tf_op jit(solution)/shard_map/ppermute | solution.py:20
  29.2 2.1 %prior_parts.1 = (bf16[512,2048]{1,0:T(8,128)(2,1)S(1)}, bf16[512,1536]{1,0:T(8,128)(2,1)S(1)}, bf16[512,1024]{1,0:T(8,128)(2,1)S(1)}, bf16[512,512]{1,0:T(8,128)(2,1)S(1)}) custom-call(s32[5]{0:T(128)S(1)} %stack.16.place_ref, bf16[512,2048]{1,0:T(8,128)(2,1)} %bitcast.5.shifted_ref, bf16[512,2048]{1,0:T(8,128)(2,1)S(1)} %bitcast.14), custom_call_target="tpu_custom_call" | custom-call | flops 1048576 | bytes 65536 | tf_op jit(solution)/shard_map/prior_parts/pallas_call | solution.py:352
  32.7 5.3 %collective-permute-start.1 = (bf16[512,512]{1,0:T(8,128)(2,1)S(1)}, bf16[512,512]{1,0:T(8,128)(2,1)S(1)}, u32[]{:S(2)}, u32[]{:S(2)}) collective-permute-start(bf16[512,512]{1,0:T(8,128)(2,1)S(1)} %get-tuple-element.24), channel_id=1, source_target_pairs={{3,1},{4,6},{11,9},{12,14},{19,17},{20,22},{27,25},{28,30}} | collective-permute-start | bytes 1572872 | tf_op jit(solution)/shard_map/ppermute | solution.py:103
  38.1 2.8 %couple_here.2.coupled_ref.second_ref.left_ref = bf16[512,2048]{1,0:T(8,128)(2,1)S(1)} custom-call(s32[5]{0:T(128)S(1)} %stack.16.place_ref, f32[1]{0:T(128)S(6)} %copy.21.rate_ref.refs_0_, s32[1,2048]{1,0:T(1,128)S(1)} %bitcast.18, bf16[512,2048]{1,0:T(8,128)(2,1)} %collective-permute-done.4.refs_2_), custom_call_target="tpu_custom_call" | custom-call | flops 1048576 | bytes 65536 | tf_op jit(solution)/shard_map/couple_here/pallas_call | solution.py:115
  40.9 1.2 turn.8.refs_0_
  42.8 1.2 turn.9.refs_1_.refs_0_.right_ref
  44.6 5.3 %collective-permute-done.1.last_three = bf16[512,512]{1,0:T(8,128)(2,1)S(1)} collective-permute-done((bf16[512,512]{1,0:T(8,128)(2,1)S(1)}, bf16[512,512]{1,0:T(8,128)(2,1)S(1)}, u32[]{:S(2)}, u32[]{:S(2)}) %collective-permute-start.1) | collective-permute-done | bytes 524320 | tf_op jit(solution)/shard_map/ppermute | solution.py:103
  49.8 8.2 %collective-permute-start.5 = (bf16[256,2048]{1,0:T(8,128)(2,1)S(1)}, bf16[256,2048]{1,0:T(8,128)(2,1)S(1)}, u32[]{:S(2)}, u32[]{:S(2)}) collective-permute-start(bf16[256,2048]{1,0:T(8,128)(2,1)S(1)} %couple.2.coupled_ref.refs_0_), channel_id=1, source_target_pairs={{3,1},{4,6},{11,9},{12,14},{19,17},{20,22},{27,25},{28,30}} | collective-permute-start | bytes 3145736 | tf_op jit(solution)/shard_map/ppermute | solution.py:103
  58.1 1.4 %collective-permute-start.7 = (bf16[256,2048]{1,0:T(8,128)(2,1)S(1)}, bf16[256,2048]{1,0:T(8,128)(2,1)S(1)}, u32[]{:S(2)}, u32[]{:S(2)}) collective-permute-start(bf16[256,2048]{1,0:T(8,128)(2,1)S(1)} %couple.3.coupled_ref.refs_1_), channel_id=1, source_target_pairs={{3,1},{4,6},{11,9},{12,14},{19,17},{20,22},{27,25},{28,30}} | collective-permute-start | bytes 3145736 | tf_op jit(solution)/shard_map/ppermute | solution.py:103
  63.8 5.9 %collective-permute-done.5.refs_0_.coupled_ref = bf16[256,2048]{1,0:T(8,128)(2,1)S(1)} collective-permute-done((bf16[256,2048]{1,0:T(8,128)(2,1)S(1)}, bf16[256,2048]{1,0:T(8,128)(2,1)S(1)}, u32[]{:S(2)}, u32[]{:S(2)}) %collective-permute-start.5) | collective-permute-done | bytes 1048608 | tf_op jit(solution)/shard_map/ppermute | solution.py:103
  69.7 11.3 %collective-permute-done.7.refs_1_.coupled_ref = bf16[256,2048]{1,0:T(8,128)(2,1)S(1)} collective-permute-done((bf16[256,2048]{1,0:T(8,128)(2,1)S(1)}, bf16[256,2048]{1,0:T(8,128)(2,1)S(1)}, u32[]{:S(2)}, u32[]{:S(2)}) %collective-permute-start.7) | collective-permute-done | bytes 1048608 | tf_op jit(solution)/shard_map/ppermute | solution.py:103
  83.6 1.3 %collective-permute-start.8 = (bf16[512,512]{1,0:T(8,128)(2,1)S(1)}, bf16[512,512]{1,0:T(8,128)(2,1)S(1)}, u32[]{:S(2)}, u32[]{:S(2)}) collective-permute-start(bf16[512,512]{1,0:T(8,128)(2,1)S(1)} %multiply.8), channel_id=1, source_target_pairs={{1,3},{6,4},{9,11},{14,12},{17,19},{22,20},{25,27},{30,28}} | collective-permute-start | bytes 1572872 | tf_op jit(solution)/shard_map/ppermute | solution.py:103
  87.2 1.3 %collective-permute-start.12 = (bf16[512,1536]{1,0:T(8,128)(2,1)S(1)}, bf16[512,1536]{1,0:T(8,128)(2,1)S(1)}, u32[]{:S(2)}, u32[]{:S(2)}) collective-permute-start(bf16[512,1536]{1,0:T(8,128)(2,1)S(1)} %product_rest.1.q31), channel_id=1, source_target_pairs={{1,3},{6,4},{9,11},{14,12},{17,19},{22,20},{25,27},{30,28}} | collective-permute-start | bytes 4718600 | tf_op jit(solution)/shard_map/ppermute | solution.py:103
  92.0 12.4 %collective-permute-done.8.q3_two = bf16[512,512]{1,0:T(8,128)(2,1)S(1)} collective-permute-done((bf16[512,512]{1,0:T(8,128)(2,1)S(1)}, bf16[512,512]{1,0:T(8,128)(2,1)S(1)}, u32[]{:S(2)}, u32[]{:S(2)}) %collective-permute-start.8) | collective-permute-done | bytes 524320 | tf_op jit(solution)/shard_map/ppermute | solution.py:103
  104.3 1.3 %collective-permute-start.11 = (bf16[512,512]{1,0:T(8,128)(2,1)S(1)}, bf16[512,512]{1,0:T(8,128)(2,1)S(1)}, u32[]{:S(2)}, u32[]{:S(2)}) collective-permute-start(bf16[512,512]{1,0:T(8,128)(2,1)S(1)} %collective-permute-done.8.q3_two), channel_id=1, source_target_pairs={{3,2},{4,5},{11,10},{12,13},{19,18},{20,21},{27,26},{28,29}} | collective-permute-start | bytes 1572872 | tf_op jit(solution)/shard_map/ppermute | solution.py:103
  105.7 2.7 %finish.1 = (bf16[512,2048]{1,0:T(8,128)(2,1)}, f32[1,512]{1,0:T(1,128)S(1)}) custom-call(s32[5]{0:T(128)S(1)} %tick.3.place_ref, bf16[512,2048]{1,0:T(8,128)(2,1)S(1)} %bitcast.12, bf16[512,2048]{1,0:T(8,128)(2,1)S(1)} %bitcast.15, bf16[512,1536]{1,0:T(8,128)(2,1)S(1)} %collective-permute-done.9.refs_0_.q0, ...), custom_call_target="tpu_custom_call" | custom-call | flops 14000000000 | bytes 65536 | tf_op jit(solution)/shard_map/finish/pallas_call | solution.py:508
  108.4 3.4 %collective-permute-done.11.q2_last = bf16[512,512]{1,0:T(8,128)(2,1)S(1)} collective-permute-done((bf16[512,512]{1,0:T(8,128)(2,1)S(1)}, bf16[512,512]{1,0:T(8,128)(2,1)S(1)}, u32[]{:S(2)}, u32[]{:S(2)}) %collective-permute-start.11) | collective-permute-done | bytes 524320 | tf_op jit(solution)/shard_map/ppermute | solution.py:103
  111.7 9.5 %collective-permute-done.12.q3 = bf16[512,1536]{1,0:T(8,128)(2,1)S(1)} collective-permute-done((bf16[512,1536]{1,0:T(8,128)(2,1)S(1)}, bf16[512,1536]{1,0:T(8,128)(2,1)S(1)}, u32[]{:S(2)}, u32[]{:S(2)}) %collective-permute-start.12) | collective-permute-done | bytes 1572896 | tf_op jit(solution)/shard_map/ppermute | solution.py:103
  121.2 2.4 %finish_last.1 = (bf16[512,2048]{1,0:T(8,128)(2,1)}, f32[1,512]{1,0:T(1,128)}) custom-call(s32[5]{0:T(128)S(1)} %stack.16.place_ref, bf16[512,2048]{1,0:T(8,128)(2,1)S(1)} %bitcast.13, bf16[512,512]{1,0:T(8,128)(2,1)S(1)} %collective-permute-done.11.q2_last, bf16[512,1536]{1,0:T(8,128)(2,1)S(1)} %collective-permute-done.12.q3, ...), custom_call_target="tpu_custom_call", output_to_operand_aliasing={{0}: (4, {})} | custom-call | flops 1048576 | bytes 65536 | tf_op jit(solution)/shard_map/finish_last/pallas_call | solution.py:609
  (42 shorter events, 18.6 us)
Async XLA Ops:
  0.6 28.5 %collective-permute-start = (bf16[1,512,2048]{2,1,0:T(8,128)(2,1)}, bf16[1,512,2048]{2,1,0:T(8,128)(2,1)}, u32[]{:S(2)}, u32[]{:S(2)}) collective-permute-start(bf16[1,512,2048]{2,1,0:T(8,128)(2,1)} %param.8), channel_id=1, source_target_pairs={{4,0},{8,4},{12,8},{5,1},{9,5},{13,9},{6,2},{10,6},{14,10},{7,3},{... | collective-permute-start | bytes 6291464 | tf_op jit(solution)/shard_map/ppermute | solution.py:20
  2.6 35.5 %collective-permute-start.4 = (bf16[512,2048]{1,0:T(8,128)(2,1)}, bf16[512,2048]{1,0:T(8,128)(2,1)}, u32[]{:S(2)}, u32[]{:S(2)}) collective-permute-start(bf16[512,2048]{1,0:T(8,128)(2,1)} %bitcast.8), channel_id=1, source_target_pairs={{2,1},{5,6},{10,9},{13,14},{18,17},{21,22},{26,25},{29,30}} | collective-permute-start | bytes 6291464 | tf_op jit(solution)/shard_map/ppermute | solution.py:103
  4.6 37.6 %collective-permute-start.3 = (bf16[512,2048]{1,0:T(8,128)(2,1)}, bf16[512,2048]{1,0:T(8,128)(2,1)S(1)}, u32[]{:S(2)}, u32[]{:S(2)}) collective-permute-start(bf16[512,2048]{1,0:T(8,128)(2,1)} %bitcast.9), channel_id=1, source_target_pairs={{0,1},{7,6},{8,9},{15,14},{16,17},{23,22},{24,25},{31,30}} | collective-permute-start | bytes 6291464 | tf_op jit(solution)/shard_map/ppermute | solution.py:103
  7.4 1.6 %copy-start = (bf16[1,512,2048]{2,1,0:T(8,128)(2,1)S(1)}, bf16[1,512,2048]{2,1,0:T(8,128)(2,1)}, u32[]{:S(2)}) copy-start(bf16[1,512,2048]{2,1,0:T(8,128)(2,1)} %param.9) | copy-start | bytes 6291460
  9.0 0.7 copy-start.3
  15.4 13.8 %copy-start.2 = (bf16[1,512,2048]{2,1,0:T(8,128)(2,1)S(1)}, bf16[1,512,2048]{2,1,0:T(8,128)(2,1)}, u32[]{:S(2)}) copy-start(bf16[1,512,2048]{2,1,0:T(8,128)(2,1)} %param.7) | copy-start | bytes 6291460
  29.2 8.9 %copy-start.4 = (s32[2048]{0:T(1024)S(1)}, s32[2048]{0:T(1024)}, u32[]{:S(2)}) copy-start(s32[2048]{0:T(1024)} %param.13) | copy-start | bytes 24580
  31.2 26.8 %collective-permute-start.6 = (bf16[512,1536]{1,0:T(8,128)(2,1)S(1)}, bf16[512,1536]{1,0:T(8,128)(2,1)S(1)}, u32[]{:S(2)}, u32[]{:S(2)}) collective-permute-start(bf16[512,1536]{1,0:T(8,128)(2,1)S(1)} %get-tuple-element.29), channel_id=1, source_target_pairs={{0,1},{7,6},{8,9},{15,14},{16,17},{23,22},{24,25},{31,30}} | collective-permute-start | bytes 4718600 | tf_op jit(solution)/shard_map/ppermute | solution.py:103
  32.0 17.8 %collective-permute-start.2 = (bf16[512,1024]{1,0:T(8,128)(2,1)S(1)}, bf16[512,1024]{1,0:T(8,128)(2,1)S(1)}, u32[]{:S(2)}, u32[]{:S(2)}) collective-permute-start(bf16[512,1024]{1,0:T(8,128)(2,1)S(1)} %get-tuple-element.25), channel_id=1, source_target_pairs={{2,1},{5,6},{10,9},{13,14},{18,17},{21,22},{26,25},{29,30}} | collective-permute-start | bytes 3145736 | tf_op jit(solution)/shard_map/ppermute | solution.py:103
  32.7 17.1 %collective-permute-start.1 = (bf16[512,512]{1,0:T(8,128)(2,1)S(1)}, bf16[512,512]{1,0:T(8,128)(2,1)S(1)}, u32[]{:S(2)}, u32[]{:S(2)}) collective-permute-start(bf16[512,512]{1,0:T(8,128)(2,1)S(1)} %get-tuple-element.24), channel_id=1, source_target_pairs={{3,1},{4,6},{11,9},{12,14},{19,17},{20,22},{27,25},{28,30}} | collective-permute-start | bytes 1572872 | tf_op jit(solution)/shard_map/ppermute | solution.py:103
  49.8 19.9 %collective-permute-start.5 = (bf16[256,2048]{1,0:T(8,128)(2,1)S(1)}, bf16[256,2048]{1,0:T(8,128)(2,1)S(1)}, u32[]{:S(2)}, u32[]{:S(2)}) collective-permute-start(bf16[256,2048]{1,0:T(8,128)(2,1)S(1)} %couple.2.coupled_ref.refs_0_), channel_id=1, source_target_pairs={{3,1},{4,6},{11,9},{12,14},{19,17},{20,22},{27,25},{28,30}} | collective-permute-start | bytes 3145736 | tf_op jit(solution)/shard_map/ppermute | solution.py:103
  58.1 22.9 %collective-permute-start.7 = (bf16[256,2048]{1,0:T(8,128)(2,1)S(1)}, bf16[256,2048]{1,0:T(8,128)(2,1)S(1)}, u32[]{:S(2)}, u32[]{:S(2)}) collective-permute-start(bf16[256,2048]{1,0:T(8,128)(2,1)S(1)} %couple.3.coupled_ref.refs_1_), channel_id=1, source_target_pairs={{3,1},{4,6},{11,9},{12,14},{19,17},{20,22},{27,25},{28,30}} | collective-permute-start | bytes 3145736 | tf_op jit(solution)/shard_map/ppermute | solution.py:103
  61.1 28.5 %collective-permute-start.9 = (bf16[512,1536]{1,0:T(8,128)(2,1)S(1)}, bf16[512,1536]{1,0:T(8,128)(2,1)S(1)}, u32[]{:S(2)}, u32[]{:S(2)}) collective-permute-start(bf16[512,1536]{1,0:T(8,128)(2,1)S(1)} %multiply.9.zero_ref.q01), channel_id=1, source_target_pairs={{1,0},{6,7},{9,8},{14,15},{17,16},{22,23},{25,24},{30,31}} | collective-permute-start | bytes 4718600 | tf_op jit(solution)/shard_map/ppermute | solution.py:103
  63.0 42.7 %collective-permute-start.13 = (bf16[512,1536]{1,0:T(8,128)(2,1)S(1)}, bf16[512,1536]{1,0:T(8,128)(2,1)S(1)}, u32[]{:S(2)}, u32[]{:S(2)}) collective-permute-start(bf16[512,1536]{1,0:T(8,128)(2,1)S(1)} %product_two.1.q21), channel_id=1, source_target_pairs={{1,2},{6,5},{9,10},{14,13},{17,18},{22,21},{25,26},{30,29}} | collective-permute-start | bytes 4718600 | tf_op jit(solution)/shard_map/ppermute | solution.py:103
  82.1 8.7 %collective-permute-start.10 = (bf16[512,512]{1,0:T(8,128)(2,1)S(1)}, bf16[512,512]{1,0:T(8,128)(2,1)S(1)}, u32[]{:S(2)}, u32[]{:S(2)}) collective-permute-start(bf16[512,512]{1,0:T(8,128)(2,1)S(1)} %multiply.7.zero_ref), channel_id=1, source_target_pairs={{1,0},{6,7},{9,8},{14,15},{17,16},{22,23},{25,24},{30,31}} | collective-permute-start | bytes 1572872 | tf_op jit(solution)/shard_map/ppermute | solution.py:103
  83.6 20.8 %collective-permute-start.8 = (bf16[512,512]{1,0:T(8,128)(2,1)S(1)}, bf16[512,512]{1,0:T(8,128)(2,1)S(1)}, u32[]{:S(2)}, u32[]{:S(2)}) collective-permute-start(bf16[512,512]{1,0:T(8,128)(2,1)S(1)} %multiply.8), channel_id=1, source_target_pairs={{1,3},{6,4},{9,11},{14,12},{17,19},{22,20},{25,27},{30,28}} | collective-permute-start | bytes 1572872 | tf_op jit(solution)/shard_map/ppermute | solution.py:103
  87.2 34.0 %collective-permute-start.12 = (bf16[512,1536]{1,0:T(8,128)(2,1)S(1)}, bf16[512,1536]{1,0:T(8,128)(2,1)S(1)}, u32[]{:S(2)}, u32[]{:S(2)}) collective-permute-start(bf16[512,1536]{1,0:T(8,128)(2,1)S(1)} %product_rest.1.q31), channel_id=1, source_target_pairs={{1,3},{6,4},{9,11},{14,12},{17,19},{22,20},{25,27},{30,28}} | collective-permute-start | bytes 4718600 | tf_op jit(solution)/shard_map/ppermute | solution.py:103
  90.8 14.9 %copy-start.1 = (bf16[1,512,2048]{2,1,0:T(8,128)(2,1)S(1)}, bf16[1,512,2048]{2,1,0:T(8,128)(2,1)}, u32[]{:S(2)}) copy-start(bf16[1,512,2048]{2,1,0:T(8,128)(2,1)} %param.9) | copy-start | bytes 6291460
  104.3 7.4 %collective-permute-start.11 = (bf16[512,512]{1,0:T(8,128)(2,1)S(1)}, bf16[512,512]{1,0:T(8,128)(2,1)S(1)}, u32[]{:S(2)}, u32[]{:S(2)}) collective-permute-start(bf16[512,512]{1,0:T(8,128)(2,1)S(1)} %collective-permute-done.8.q3_two), channel_id=1, source_target_pairs={{3,2},{4,5},{11,10},{12,13},{19,18},{20,21},{27,26},{28,29}} | collective-permute-start | bytes 1572872 | tf_op jit(solution)/shard_map/ppermute | solution.py:103

commit v12 on v11

--- a/solution.py
+++ b/solution.py
@@ -199,14 +199,28 @@
     )(place, *lefts, right)
 
 
+def pack(value, out_ref, column):
+    half = value.shape[0] // 2
+    for part in range(2):
+        rows = pl.ds(part * half, half)
+        pack_rows(part, value[part * half : (part + 1) * half], out_ref.at[rows], column)
+
+
 def two_kernel(place_ref, left_ref, right_ref, zero_ref, out_ref):
     odd = place_ref[0]
     width = right_ref.shape[0] // 4
-    multiply_kernel(lambda odd: 1, 2, 1, place_ref, left_ref, right_ref, out_ref)
+
+    def product(block):
+        columns = pl.ds(pl.multiple_of(block * width, 128), width)
+        value = jnp.dot(left_ref[...], right_ref[:, columns], preferred_element_type=F32)
+        return value.astype(BF16)
 
     @pl.when(place_ref[1] == 1)
     def _():
-        out_ref[:, 2 * width :] = zero_ref[:, pl.ds(pl.multiple_of((2 - 2 * odd) * width, 128), width)]
+        out_ref[:, :width] = product(1 + odd)
+        zero = pl.ds(pl.multiple_of((2 - 2 * odd) * width, 128), width)
+        out_ref[:, width : 2 * width] = zero_ref[:, zero]
+        pack(product(2 - odd), out_ref, 2 * width)
 
 
 def product_two(place, half, across, zero):
@@ -215,7 +229,7 @@
     vmem = pl.BlockSpec(memory_space=pltpu.VMEM)
     return pl.pallas_call(
         two_kernel,
-        out_shape=jax.ShapeDtypeStruct((rows, 3 * width), BF16),
+        out_shape=jax.ShapeDtypeStruct((rows, 11 * width // 4), BF16),
         in_specs=[pl.BlockSpec(memory_space=pltpu.SMEM)] + [vmem] * 3,
         out_specs=vmem,
         compiler_params=pltpu.CompilerParams(vmem_limit_bytes=6 * MIB),
@@ -292,15 +306,16 @@
     odd = place_ref[0]
     width = zero_ref.shape[1]
 
+    def product(block):
+        columns = pl.ds(pl.multiple_of(block * width, 128), width)
+        value = jnp.dot(left_ref[...], right_ref[:, columns], preferred_element_type=F32)
+        return value.astype(BF16)
+
     @pl.when(place_ref[1] == 1)
     def _():
         out_ref[:, pl.ds(pl.multiple_of(odd * width, 128), width)] = zero_ref[...]
-        for source, target in ((1 + odd, 1 - odd), (3 - 3 * odd, 2)):
-            source = pl.multiple_of(source * width, 128)
-            target = pl.multiple_of(target * width, 128)
-            out_ref[:, pl.ds(target, width)] = jnp.dot(
-                left_ref[...], right_ref[:, pl.ds(source, width)], preferred_element_type=F32
-            ).astype(BF16)
+        out_ref[:, pl.ds(pl.multiple_of((1 - odd) * width, 128), width)] = product(1 + odd)
+        pack(product(3 - 3 * odd), out_ref, 2 * width)
 
 
 def product_rest(place, half, across, zero):
@@ -309,7 +324,7 @@
     vmem = pl.BlockSpec(memory_space=pltpu.VMEM)
     return pl.pallas_call(
         rest_kernel,
-        out_shape=jax.ShapeDtypeStruct((rows, 3 * width), BF16),
+        out_shape=jax.ShapeDtypeStruct((rows, 11 * width // 4), BF16),
         in_specs=[pl.BlockSpec(memory_space=pltpu.SMEM)] + [vmem] * 3,
         out_specs=vmem,
         compiler_params=pltpu.CompilerParams(vmem_limit_bytes=6 * MIB),
@@ -318,6 +333,33 @@
     )(place, half, across, zero)
 
 
+def pack_rows(part, value, out_ref, column):
+    half, width = value.shape
+    quarter = half // 2
+    if part == 0:
+        out_ref[:, column : column + half] = value[:, :half]
+        out_ref[:, column + half : column + half + quarter] = value[:, half : half + quarter]
+    else:
+        out_ref[:, column : column + half] = value[:, half:]
+        beside = slice(column + half, column + half + quarter)
+        out_ref[:quarter, beside] = value[quarter:, :quarter]
+        out_ref[quarter:, beside] = value[quarter:, quarter:half]
+
+
+def unpacked_rows(part, packed_ref, column):
+    quarter = packed_ref.shape[0] // 4
+    half = 2 * quarter
+    beside = slice(column + half, column + half + quarter)
+    rows = slice(part * quarter, (part + 1) * quarter)
+    diagonal = packed_ref[rows, column : column + half]
+    lower = [packed_ref[start : start + quarter, beside] for start in (half, half + quarter)]
+    if part < 2:
+        return diagonal, jnp.concatenate([packed_ref[rows, beside], lower[part].T], axis=1)
+    if part == 2:
+        return packed_ref[:half, beside].T, diagonal
+    return jnp.concatenate(lower, axis=1), diagonal
+
+
 def prior_kernel(place_ref, shifted_ref, sigma_ref, out_ref):
     @pl.when(place_ref[3] == 0)
     def _():
@@ -330,28 +372,32 @@
 
 def parts_kernel(place_ref, shifted_ref, sigma_ref, row_ref, far_ref, near_ref, last_ref):
     odd = place_ref[0]
-    width = last_ref.shape[1]
+    width = row_ref.shape[1] // 4
 
     def at(block, count=1):
         return pl.ds(pl.multiple_of(block * width, 128), count * width)
 
     prior_kernel(place_ref, shifted_ref, sigma_ref, row_ref)
-    near = row_ref[:, at(2 - 2 * odd, 2)]
-    near_ref[...] = near
-    far_ref[:, width:] = near
-    far_ref[:, :width] = row_ref[:, at(3 * odd)]
-    last_ref[...] = row_ref[:, at(3 - 3 * odd)]
+    far_ref[:, : 2 * width] = row_ref[:, at(2 - 2 * odd, 2)]
+    near_ref[:, :width] = row_ref[:, at(3 - 3 * odd)]
+    for part in range(2):
+
+        @pl.when(pl.program_id(0) == part)
+        def _():
+            pack_rows(part, row_ref[:, at(3 * odd)], far_ref, 2 * width)
+            pack_rows(part, row_ref[:, at(2 - odd)], near_ref, width)
+            pack_rows(part, row_ref[:, at(3 - 3 * odd)], last_ref, 0)
 
 
 def prior_parts(place, shifted, sigma):
     rows, nodes = sigma.shape
-    chunk = 128
+    chunk = rows // 2
     width = nodes // 4
-    out = lambda blocks: jax.ShapeDtypeStruct((rows, blocks * width), BF16)
-    spec = lambda blocks: pl.BlockSpec((chunk, blocks * width), lambda i, place: (i, 0))
+    out = lambda quarters: jax.ShapeDtypeStruct((rows, quarters * width // 4), BF16)
+    spec = lambda quarters: pl.BlockSpec((chunk, quarters * width // 4), lambda i, place: (i, 0))
     return pl.pallas_call(
         parts_kernel,
-        out_shape=(out(4), out(3), out(2), out(1)),
+        out_shape=(out(16), out(11), out(7), out(3)),
         grid_spec=pltpu.PrefetchScalarGridSpec(
             num_scalar_prefetch=1,
             grid=(rows // chunk,),
@@ -363,9 +409,9 @@
                     (chunk, nodes), lambda i, place: (jnp.where(place[3] == 0, 0, i), 0)
                 ),
             ],
-            out_specs=(spec(4), spec(3), spec(2), spec(1)),
+            out_specs=(spec(16), spec(11), spec(7), spec(3)),
         ),
-        compiler_params=pltpu.CompilerParams(vmem_limit_bytes=8 * MIB),
+        compiler_params=pltpu.CompilerParams(vmem_limit_bytes=14 * MIB),
         cost_estimate=LIGHT,
         name="prior_parts",
     )(place, shifted, sigma)
@@ -375,25 +421,29 @@
     @pl.when(place_ref[1] == 1)
     def _():
         odd = place_ref[0]
-        width = last_three.shape[1]
-
-        def at(block):
-            return pl.ds(pl.multiple_of(block * width, 128), width)
+        width = own.shape[0]
+        half, quarter = width // 2, width // 4
+
+        def at(block, count=1):
+            return pl.ds(pl.multiple_of(block * width, 128), count * width)
 
         near = 2 * (1 - odd)
-        half = pl.ds(pl.multiple_of(near * width, 128), 2 * width)
         row = [turned(block, odd) for block in range(4)]
         out_ref[at(row[1]), :] = own[...]
-        out_ref[at(row[2]), half] = near_two[...]
-        out_ref[at(row[0]), at(row[0])] = far_zero[:, :width]
-        out_ref[at(row[0]), half] = far_zero[:, width:]
-        out_ref[at(row[3]), at(row[3])] = last_three[...]
+        out_ref[at(row[2]), at(row[3])] = near_two[:, :width]
+        out_ref[at(row[3]), at(row[2])] = near_two[:, :width].T
+        out_ref[at(row[0]), at(near, 2)] = far_zero[:, : 2 * width]
+        for step in range(2):
+            out_ref[at(near + step), at(row[0])] = far_zero[:, step * width : (1 + step) * width].T
         for block in (0, 2, 3):
             out_ref[at(row[block]), at(row[1])] = column[at(row[block]), :]
-        for step in range(2):
-            piece = slice((1 + step) * width, (2 + step) * width)
-            out_ref[at(near + step), at(row[0])] = far_zero[:, piece].T
-        out_ref[at(row[3]), at(row[2])] = near_two[:, at(1 - odd)].T
+        packed = ((0, far_zero, 2 * width), (2, near_two, width), (3, last_three, 0))
+        for block, packed_ref, start in packed:
+            for part in range(4):
+                rows = pl.ds(pl.multiple_of(row[block] * width + part * quarter, 128), quarter)
+                for side, value in enumerate(unpacked_rows(part, packed_ref, start)):
+                    columns = pl.ds(pl.multiple_of(row[block] * width + side * half, 128), half)
+                    out_ref[rows, columns] = value
 
 
 def assemble(place, *parts):
@@ -429,7 +479,7 @@
 
 def finish_kernel(
     place_ref, pivot_ref, sigma_ref,
-    q0, q0_last, q2, q2_zero, q3_two,
+    q0, q0_last, q2, q3_two,
     q01, q11, q21, q31,
     out_ref, var_ref,
 ):
@@ -471,9 +521,17 @@
 
     @pl.when(active & (place == 2))
     def _():
-        add(at(turned(0, odd)), q2_zero[:, pl.ds(here, rows)].T)
-        add(at(1, 2), q2[...])
-        trace(q2[:, own(1 - odd)])
+        add(at(turned(0, odd)), q2[pl.ds(0, width), pl.ds(pl.multiple_of(width + here, 128), rows)].T)
+        add(at(turned(1, odd)), q2[pl.ds(here, rows), pl.ds(0, width)])
+        start = pl.program_id(0) % 2 * rows + 2 * width
+        trace(q2[pl.ds(here, rows), pl.ds(pl.multiple_of(start, 128), rows)])
+        for part in range(4):
+
+            @pl.when(pl.program_id(0) == part)
+            def _():
+                for side, value in enumerate(unpacked_rows(part, q2, 2 * width)):
+                    start = turned(2, odd) * width + side * width // 2
+                    add(pl.ds(pl.multiple_of(start, 128), width // 2), value)
 
     @pl.when(active & (place == 3))
     def _():
@@ -521,12 +579,11 @@
                 ),
                 picked(0, 3),
                 whole(0),
-                picked(2, 2),
-                whole(2),
+                pl.BlockSpec((rows, 11 * width // 4), lambda i, place: (0, 0)),
                 picked(3, 1),
                 turned_block(lambda odd: 1),
                 picked(1, 1),
-                turned_block(lambda odd: odd),
+                turned_block(lambda odd: 0),
                 turned_block(lambda odd: 1 - odd),
             ],
             out_specs=(
@@ -550,31 +607,32 @@
     def at(block, count=1):
         return pl.ds(pl.multiple_of(block * width, 128), count * width)
 
-    def copies(here, pieces):
+    def copies(part, pieces):
+        here = pl.ds(part * chunk, chunk)
         return [
             pltpu.make_async_copy(
-                sum_ref.at[here, source], out_ref.at[here, target], sems.at[which, here.start // chunk]
+                sum_ref.at[here, source], out_ref.at[here, target], sems.at[which, part]
             )
             for which, (source, target, _) in enumerate(pieces)
         ]
 
     def write(pieces):
-        for start in range(0, rows, chunk):
-            here = pl.ds(start, chunk)
+        for part in range(4):
+            here = pl.ds(part * chunk, chunk)
             for source, target, product in pieces:
-                value = pivot_ref[here, target].astype(F32) + product(here).astype(F32)
+                value = pivot_ref[here, target].astype(F32) + product(part, here).astype(F32)
                 sum_ref[here, source] = value.astype(BF16)
-            for copy in copies(here, pieces):
+            for copy in copies(part, pieces):
                 copy.start()
-        for start in range(0, rows, chunk):
-            for copy in copies(pl.ds(start, chunk), pieces):
+        for part in range(4):
+            for copy in copies(part, pieces):
                 copy.wait()
 
     var_ref[...] = old_var_ref[...]
 
     @pl.when(active & (place == 2))
     def _():
-        write([(pl.ds(0, width), at(3 - 3 * odd), lambda here: q2_last[:, here].T)])
+        write([(pl.ds(0, width), at(3 - 3 * odd), lambda part, here: q2_last[:, here].T)])
 
     @pl.when(active & (place == 3))
     def _():
@@ -583,12 +641,16 @@
             here = pl.ds(start, chunk)
             own = pl.ds(pl.multiple_of(place_ref[2] * width + start, 128), chunk)
             value = pivot_ref[here, own].astype(F32)
-            value = value + q3[here, pl.ds(2 * width + start, chunk)].astype(F32)
+            value = value + q3[here, pl.ds(2 * width + start % (2 * chunk), chunk)].astype(F32)
             var_ref[:, here] = diagonal_of(chunk)(value)
         write(
             [
-                (both, at(2 * odd, 2), lambda here: q3[here, both]),
-                (last, at(3 - 3 * odd), lambda here: q3[here, last]),
+                (both, at(2 * odd, 2), lambda part, here: q3[here, both]),
+                (
+                    last,
+                    at(3 - 3 * odd),
+                    lambda part, here: jnp.concatenate(unpacked_rows(part, q3, 2 * width), axis=1),
+                ),
             ]
         )
 
@@ -672,7 +734,7 @@
     q3 = moved(q3_own, 1, 3)
     h1 = multiply(place, [after(c1[0], q3_own), c1[1]], prior)
     q11 = multiply(place, [h1], across, lambda odd: 1 + odd, 1)
-    received = (q0, q0_last, q2, q2, q3_two)
+    received = (q0, q0_last, q2, q3_two)
     kept = (q0_own, q11, q2_own, q3_own)
     place_then = tick(tick(place, q0, cost=LIGHT), q0_last, cost=MEDIUM)
     q2_last = moved(after(q3_two, place_then), 3, 2)

time: 125 us -> 127 us (1.016)
  the two profiles are of different devices: /device:TPU:1 before, /device:TPU:0 now
where the time goes in v12:
time: 127 us; the launch traced here: 126 us
  waiting for transfers between devices  72.9 us (57%)
  Pallas kernels  29.3 us (23%)
  starting transfers between devices  17.6 us (14%)
  between operations  3.14 us (2%)
  local copies, waits for them, and re-layouts  3.06 us (2%)
    ppermute x13, waiting for transfers between devices, moved(): lax.ppermute(value, ('dom', 'col'), route(source, target, lax.axis_size('...  72.9 us
    ppermute x13, starting transfers between devices, moved(): lax.ppermute(value, ('dom', 'col'), route(source, target, lax.axis_size('...  16.3 us
    pallas_call x6, Pallas kernels, turn(): pl.pallas_call(turn_kernel, out_shape=jax.ShapeDtypeStruct((nodes, nodes)...  5.99 us
    pallas_call x2, Pallas kernels, couple(): pl.pallas_call(couple_kernel, out_shape=jax.ShapeDtypeStruct((rows, nodes...  4.81 us
    pallas_call x6, Pallas kernels, multiply(): pl.pallas_call(functools.partial(multiply_kernel, first, count, len(lefts...  3.48 us
    pallas_call x2, Pallas kernels, couple_here(): pl.pallas_call(kernel, out_shape=jax.ShapeDtypeStruct((rows, nodes), BF16...  3.45 us
    unnamed x10, local copies, waits for them, and re-layouts  2.97 us
    pallas_call x1, Pallas kernels, finish(): pl.pallas_call(finish_kernel, out_shape=(jax.ShapeDtypeStruct((rows, node...  2.63 us
  transfers between devices with their start and end apart: 14, of which 4 were waited for; matrix products, arithmetic and copies ran while one was open for 0% of the time, Pallas kernels for 22%

profile of v12, /device:TPU:0, one launch (start us, length us, event | category | flops | bytes accessed | tf_op | source)
XLA Modules:
  0.0 126.0 jit_solution(8337219365615016798)
XLA Ops:
  0.6 1.3 %collective-permute-start = (bf16[1,512,2048]{2,1,0:T(8,128)(2,1)}, bf16[1,512,2048]{2,1,0:T(8,128)(2,1)}, u32[]{:S(2)}, u32[]{:S(2)}) collective-permute-start(bf16[1,512,2048]{2,1,0:T(8,128)(2,1)} %param.8), channel_id=1, source_target_pairs={{4,0},{8,4},{12,8},{5,1},{9,5},{13,9},{6,2},{10,6},{14,10},{7,3},{... | collective-permute-start | bytes 6291464 | tf_op jit(solution)/shard_map/ppermute | solution.py:20
  1.9 2.0 %collective-permute-start.4 = (bf16[512,2048]{1,0:T(8,128)(2,1)}, bf16[512,2048]{1,0:T(8,128)(2,1)}, u32[]{:S(2)}, u32[]{:S(2)}) collective-permute-start(bf16[512,2048]{1,0:T(8,128)(2,1)} %bitcast.8), channel_id=1, source_target_pairs={{2,1},{5,6},{10,9},{13,14},{18,17},{21,22},{26,25},{29,30}} | collective-permute-start | bytes 6291464 | tf_op jit(solution)/shard_map/ppermute | solution.py:103
  3.9 4.4 %collective-permute-start.3 = (bf16[512,2048]{1,0:T(8,128)(2,1)}, bf16[512,2048]{1,0:T(8,128)(2,1)S(1)}, u32[]{:S(2)}, u32[]{:S(2)}) collective-permute-start(bf16[512,2048]{1,0:T(8,128)(2,1)} %bitcast.9), channel_id=1, source_target_pairs={{0,1},{7,6},{8,9},{15,14},{16,17},{23,22},{24,25},{31,30}} | collective-permute-start | bytes 6291464 | tf_op jit(solution)/shard_map/ppermute | solution.py:103
  10.3 1.6 %copy-done = bf16[1,512,2048]{2,1,0:T(8,128)(2,1)S(1)} copy-done((bf16[1,512,2048]{2,1,0:T(8,128)(2,1)S(1)}, bf16[1,512,2048]{2,1,0:T(8,128)(2,1)}, u32[]{:S(2)}) %copy-start) | copy-done | bytes 2097176
  12.6 2.4 %couple.2.coupled_ref.refs_0_ = bf16[256,2048]{1,0:T(8,128)(2,1)S(1)} custom-call(f32[1]{0:T(128)S(6)} %copy.21.rate_ref.refs_0_, s32[1,2048]{1,0:T(1,128)S(1)} %bitcast.16, bf16[512,2048]{1,0:T(8,128)(2,1)S(1)} %bitcast.10), custom_call_target="tpu_custom_call" | custom-call | flops 1048576 | bytes 65536 | tf_op jit(solution)/shard_map/couple/pallas_call | solution.py:73
  15.0 2.4 %couple.3.coupled_ref.refs_1_ = bf16[256,2048]{1,0:T(8,128)(2,1)S(1)} custom-call(f32[1]{0:T(128)S(6)} %copy.21.rate_ref.refs_0_, s32[1,2048]{1,0:T(1,128)S(1)} %bitcast.17, bf16[512,2048]{1,0:T(8,128)(2,1)S(1)} %bitcast.11), custom_call_target="tpu_custom_call" | custom-call | flops 1048576 | bytes 65536 | tf_op jit(solution)/shard_map/couple/pallas_call | solution.py:73
  17.5 0.9 turn.6.refs_0_
  18.4 0.9 turn.7.refs_0_
  20.0 2.2 %prior_parts.1 = (bf16[512,2048]{1,0:T(8,128)(2,1)S(1)}, bf16[512,1408]{1,0:T(8,128)(2,1)S(1)}, bf16[512,896]{1,0:T(8,128)(2,1)S(1)}, bf16[512,384]{1,0:T(8,128)(2,1)S(1)}) custom-call(s32[5]{0:T(128)S(1)} %stack.16.place_ref, bf16[512,2048]{1,0:T(8,128)(2,1)} %bitcast.5.shifted_ref, bf16[512,2048]{1,0:T(8,128)(2,1)S(1)} %bitcast.14), custom_call_target="tpu_custom_call" | custom-call | flops 1048576 | bytes 65536 | tf_op jit(solution)/shard_map/prior_parts/pallas_call | solution.py:398
  22.1 1.6 %collective-permute-start.6 = (bf16[512,1408]{1,0:T(8,128)(2,1)S(1)}, bf16[512,1408]{1,0:T(8,128)(2,1)S(1)}, u32[]{:S(2)}, u32[]{:S(2)}) collective-permute-start(bf16[512,1408]{1,0:T(8,128)(2,1)S(1)} %get-tuple-element.29), channel_id=1, source_target_pairs={{0,1},{7,6},{8,9},{15,14},{16,17},{23,22},{24,25},{31,30}} | collective-permute-start | bytes 4325384 | tf_op jit(solution)/shard_map/ppermute | solution.py:103
  25.2 2.8 %couple_here.2.coupled_ref.second_ref.left_ref = bf16[512,2048]{1,0:T(8,128)(2,1)S(1)} custom-call(s32[5]{0:T(128)S(1)} %stack.16.place_ref, f32[1]{0:T(128)S(6)} %copy.21.rate_ref.refs_0_, s32[1,2048]{1,0:T(1,128)S(1)} %bitcast.18, bf16[512,2048]{1,0:T(8,128)(2,1)} %collective-permute-done.4.refs_2_), custom_call_target="tpu_custom_call" | custom-call | flops 1048576 | bytes 65536 | tf_op jit(solution)/shard_map/couple_here/pallas_call | solution.py:115
  28.0 1.2 turn.8.refs_0_
  29.3 2.8 %collective-permute-done.3.refs_2_ = bf16[512,2048]{1,0:T(8,128)(2,1)S(1)} collective-permute-done((bf16[512,2048]{1,0:T(8,128)(2,1)}, bf16[512,2048]{1,0:T(8,128)(2,1)S(1)}, u32[]{:S(2)}, u32[]{:S(2)}) %collective-permute-start.3) | collective-permute-done | bytes 2097184 | tf_op jit(solution)/shard_map/ppermute | solution.py:103
  32.7 1.2 turn.9.refs_1_.refs_0_.right_ref
  35.2 16.4 %collective-permute-done.6.far_zero = bf16[512,1408]{1,0:T(8,128)(2,1)S(1)} collective-permute-done((bf16[512,1408]{1,0:T(8,128)(2,1)S(1)}, bf16[512,1408]{1,0:T(8,128)(2,1)S(1)}, u32[]{:S(2)}, u32[]{:S(2)}) %collective-permute-start.6) | collective-permute-done | bytes 1441824 | tf_op jit(solution)/shard_map/ppermute | solution.py:103
  54.0 1.3 %collective-permute-start.9 = (bf16[512,1536]{1,0:T(8,128)(2,1)S(1)}, bf16[512,1536]{1,0:T(8,128)(2,1)S(1)}, u32[]{:S(2)}, u32[]{:S(2)}) collective-permute-start(bf16[512,1536]{1,0:T(8,128)(2,1)S(1)} %multiply.9.zero_ref.q01), channel_id=1, source_target_pairs={{1,0},{6,7},{9,8},{14,15},{17,16},{22,23},{25,24},{30,31}} | collective-permute-start | bytes 4718600 | tf_op jit(solution)/shard_map/ppermute | solution.py:103
  58.5 1.3 %collective-permute-start.10 = (bf16[512,512]{1,0:T(8,128)(2,1)S(1)}, bf16[512,512]{1,0:T(8,128)(2,1)S(1)}, u32[]{:S(2)}, u32[]{:S(2)}) collective-permute-start(bf16[512,512]{1,0:T(8,128)(2,1)S(1)} %multiply.7.zero_ref), channel_id=1, source_target_pairs={{1,0},{6,7},{9,8},{14,15},{17,16},{22,23},{25,24},{30,31}} | collective-permute-start | bytes 1572872 | tf_op jit(solution)/shard_map/ppermute | solution.py:103
  61.9 0.9 turn.11.right_ref.refs_1_
  65.3 21.5 %collective-permute-done.9.refs_0_.q0 = bf16[512,1536]{1,0:T(8,128)(2,1)S(1)} collective-permute-done((bf16[512,1536]{1,0:T(8,128)(2,1)S(1)}, bf16[512,1536]{1,0:T(8,128)(2,1)S(1)}, u32[]{:S(2)}, u32[]{:S(2)}) %collective-permute-start.9) | collective-permute-done | bytes 1572896 | tf_op jit(solution)/shard_map/ppermute | solution.py:103
  86.8 1.1 tick.2.place_ref
  87.9 32.2 %collective-permute-done.10.refs_0_.q0_last = bf16[512,512]{1,0:T(8,128)(2,1)S(1)} collective-permute-done((bf16[512,512]{1,0:T(8,128)(2,1)S(1)}, bf16[512,512]{1,0:T(8,128)(2,1)S(1)}, u32[]{:S(2)}, u32[]{:S(2)}) %collective-permute-start.10) | collective-permute-done | bytes 524320 | tf_op jit(solution)/shard_map/ppermute | solution.py:103
  120.1 1.1 tick.3.place_ref
  122.0 2.6 %finish.1 = (bf16[512,2048]{1,0:T(8,128)(2,1)}, f32[1,512]{1,0:T(1,128)S(1)}) custom-call(s32[5]{0:T(128)S(1)} %tick.3.place_ref, bf16[512,2048]{1,0:T(8,128)(2,1)S(1)} %bitcast.12, bf16[512,2048]{1,0:T(8,128)(2,1)S(1)} %bitcast.15, bf16[512,1536]{1,0:T(8,128)(2,1)S(1)} %collective-permute-done.9.refs_0_.q0, ...), custom_call_target="tpu_custom_call" | custom-call | flops 14000000000 | bytes 65536 | tf_op jit(solution)/shard_map/finish/pallas_call | solution.py:566
  124.6 1.2 finish_last.1
  (42 shorter events, 15.5 us)
Async XLA Ops:
  0.6 18.6 %collective-permute-start = (bf16[1,512,2048]{2,1,0:T(8,128)(2,1)}, bf16[1,512,2048]{2,1,0:T(8,128)(2,1)}, u32[]{:S(2)}, u32[]{:S(2)}) collective-permute-start(bf16[1,512,2048]{2,1,0:T(8,128)(2,1)} %param.8), channel_id=1, source_target_pairs={{4,0},{8,4},{12,8},{5,1},{9,5},{13,9},{6,2},{10,6},{14,10},{7,3},{... | collective-permute-start | bytes 6291464 | tf_op jit(solution)/shard_map/ppermute | solution.py:20
  1.9 23.3 %collective-permute-start.4 = (bf16[512,2048]{1,0:T(8,128)(2,1)}, bf16[512,2048]{1,0:T(8,128)(2,1)}, u32[]{:S(2)}, u32[]{:S(2)}) collective-permute-start(bf16[512,2048]{1,0:T(8,128)(2,1)} %bitcast.8), channel_id=1, source_target_pairs={{2,1},{5,6},{10,9},{13,14},{18,17},{21,22},{26,25},{29,30}} | collective-permute-start | bytes 6291464 | tf_op jit(solution)/shard_map/ppermute | solution.py:103
  3.9 28.1 %collective-permute-start.3 = (bf16[512,2048]{1,0:T(8,128)(2,1)}, bf16[512,2048]{1,0:T(8,128)(2,1)S(1)}, u32[]{:S(2)}, u32[]{:S(2)}) collective-permute-start(bf16[512,2048]{1,0:T(8,128)(2,1)} %bitcast.9), channel_id=1, source_target_pairs={{0,1},{7,6},{8,9},{15,14},{16,17},{23,22},{24,25},{31,30}} | collective-permute-start | bytes 6291464 | tf_op jit(solution)/shard_map/ppermute | solution.py:103
  10.3 1.6 %copy-start = (bf16[1,512,2048]{2,1,0:T(8,128)(2,1)S(1)}, bf16[1,512,2048]{2,1,0:T(8,128)(2,1)}, u32[]{:S(2)}) copy-start(bf16[1,512,2048]{2,1,0:T(8,128)(2,1)} %param.9) | copy-start | bytes 6291460
  11.9 0.7 copy-start.3
  18.4 1.6 %copy-start.2 = (bf16[1,512,2048]{2,1,0:T(8,128)(2,1)S(1)}, bf16[1,512,2048]{2,1,0:T(8,128)(2,1)}, u32[]{:S(2)}) copy-start(bf16[1,512,2048]{2,1,0:T(8,128)(2,1)} %param.7) | copy-start | bytes 6291460
  19.9 5.3 %copy-start.4 = (s32[2048]{0:T(1024)S(1)}, s32[2048]{0:T(1024)}, u32[]{:S(2)}) copy-start(s32[2048]{0:T(1024)} %param.13) | copy-start | bytes 24580
  22.1 29.4 %collective-permute-start.6 = (bf16[512,1408]{1,0:T(8,128)(2,1)S(1)}, bf16[512,1408]{1,0:T(8,128)(2,1)S(1)}, u32[]{:S(2)}, u32[]{:S(2)}) collective-permute-start(bf16[512,1408]{1,0:T(8,128)(2,1)S(1)} %get-tuple-element.29), channel_id=1, source_target_pairs={{0,1},{7,6},{8,9},{15,14},{16,17},{23,22},{24,25},{31,30}} | collective-permute-start | bytes 4325384 | tf_op jit(solution)/shard_map/ppermute | solution.py:103
  23.8 10.7 %collective-permute-start.2 = (bf16[512,896]{1,0:T(8,128)(2,1)S(1)}, bf16[512,896]{1,0:T(8,128)(2,1)S(1)}, u32[]{:S(2)}, u32[]{:S(2)}) collective-permute-start(bf16[512,896]{1,0:T(8,128)(2,1)S(1)} %get-tuple-element.25), channel_id=1, source_target_pairs={{2,1},{5,6},{10,9},{13,14},{18,17},{21,22},{26,25},{29,30}} | collective-permute-start | bytes 2752520 | tf_op jit(solution)/shard_map/ppermute | solution.py:103
  24.5 9.9 %collective-permute-start.1 = (bf16[512,384]{1,0:T(8,128)(2,1)S(1)}, bf16[512,384]{1,0:T(8,128)(2,1)S(1)}, u32[]{:S(2)}, u32[]{:S(2)}) collective-permute-start(bf16[512,384]{1,0:T(8,128)(2,1)S(1)} %get-tuple-element.24), channel_id=1, source_target_pairs={{3,1},{4,6},{11,9},{12,14},{19,17},{20,22},{27,25},{28,30}} | collective-permute-start | bytes 1179656 | tf_op jit(solution)/shard_map/ppermute | solution.py:103
  34.5 22.7 %collective-permute-start.5 = (bf16[256,2048]{1,0:T(8,128)(2,1)S(1)}, bf16[256,2048]{1,0:T(8,128)(2,1)S(1)}, u32[]{:S(2)}, u32[]{:S(2)}) collective-permute-start(bf16[256,2048]{1,0:T(8,128)(2,1)S(1)} %couple.2.coupled_ref.refs_0_), channel_id=1, source_target_pairs={{3,1},{4,6},{11,9},{12,14},{19,17},{20,22},{27,25},{28,30}} | collective-permute-start | bytes 3145736 | tf_op jit(solution)/shard_map/ppermute | solution.py:103
  51.6 5.6 %collective-permute-start.7 = (bf16[256,2048]{1,0:T(8,128)(2,1)S(1)}, bf16[256,2048]{1,0:T(8,128)(2,1)S(1)}, u32[]{:S(2)}, u32[]{:S(2)}) collective-permute-start(bf16[256,2048]{1,0:T(8,128)(2,1)S(1)} %couple.3.coupled_ref.refs_1_), channel_id=1, source_target_pairs={{3,1},{4,6},{11,9},{12,14},{19,17},{20,22},{27,25},{28,30}} | collective-permute-start | bytes 3145736 | tf_op jit(solution)/shard_map/ppermute | solution.py:103
  54.0 32.8 %collective-permute-start.9 = (bf16[512,1536]{1,0:T(8,128)(2,1)S(1)}, bf16[512,1536]{1,0:T(8,128)(2,1)S(1)}, u32[]{:S(2)}, u32[]{:S(2)}) collective-permute-start(bf16[512,1536]{1,0:T(8,128)(2,1)S(1)} %multiply.9.zero_ref.q01), channel_id=1, source_target_pairs={{1,0},{6,7},{9,8},{14,15},{17,16},{22,23},{25,24},{30,31}} | collective-permute-start | bytes 4718600 | tf_op jit(solution)/shard_map/ppermute | solution.py:103
  56.4 65.6 %collective-permute-start.13 = (bf16[512,1408]{1,0:T(8,128)(2,1)S(1)}, bf16[512,1408]{1,0:T(8,128)(2,1)S(1)}, u32[]{:S(2)}, u32[]{:S(2)}) collective-permute-start(bf16[512,1408]{1,0:T(8,128)(2,1)S(1)} %product_two.1.q21), channel_id=1, source_target_pairs={{1,2},{6,5},{9,10},{14,13},{17,18},{22,21},{25,26},{30,29}} | collective-permute-start | bytes 4325384 | tf_op jit(solution)/shard_map/ppermute | solution.py:103
  58.5 61.7 %collective-permute-start.10 = (bf16[512,512]{1,0:T(8,128)(2,1)S(1)}, bf16[512,512]{1,0:T(8,128)(2,1)S(1)}, u32[]{:S(2)}, u32[]{:S(2)}) collective-permute-start(bf16[512,512]{1,0:T(8,128)(2,1)S(1)} %multiply.7.zero_ref), channel_id=1, source_target_pairs={{1,0},{6,7},{9,8},{14,15},{17,16},{22,23},{25,24},{30,31}} | collective-permute-start | bytes 1572872 | tf_op jit(solution)/shard_map/ppermute | solution.py:103
  60.3 60.9 %collective-permute-start.8 = (bf16[512,512]{1,0:T(8,128)(2,1)S(1)}, bf16[512,512]{1,0:T(8,128)(2,1)S(1)}, u32[]{:S(2)}, u32[]{:S(2)}) collective-permute-start(bf16[512,512]{1,0:T(8,128)(2,1)S(1)} %multiply.8), channel_id=1, source_target_pairs={{1,3},{6,4},{9,11},{14,12},{17,19},{22,20},{25,27},{30,28}} | collective-permute-start | bytes 1572872 | tf_op jit(solution)/shard_map/ppermute | solution.py:103
  63.4 61.3 %collective-permute-start.12 = (bf16[512,1408]{1,0:T(8,128)(2,1)S(1)}, bf16[512,1408]{1,0:T(8,128)(2,1)S(1)}, u32[]{:S(2)}, u32[]{:S(2)}) collective-permute-start(bf16[512,1408]{1,0:T(8,128)(2,1)S(1)} %product_rest.1.q31), channel_id=1, source_target_pairs={{1,3},{6,4},{9,11},{14,12},{17,19},{22,20},{25,27},{30,28}} | collective-permute-start | bytes 4325384 | tf_op jit(solution)/shard_map/ppermute | solution.py:103
  87.9 34.1 %copy-start.1 = (bf16[1,512,2048]{2,1,0:T(8,128)(2,1)S(1)}, bf16[1,512,2048]{2,1,0:T(8,128)(2,1)}, u32[]{:S(2)}) copy-start(bf16[1,512,2048]{2,1,0:T(8,128)(2,1)} %param.9) | copy-start | bytes 6291460
  121.3 3.4 %collective-permute-start.11 = (bf16[512,512]{1,0:T(8,128)(2,1)S(1)}, bf16[512,512]{1,0:T(8,128)(2,1)S(1)}, u32[]{:S(2)}, u32[]{:S(2)}) collective-permute-start(bf16[512,512]{1,0:T(8,128)(2,1)S(1)} %collective-permute-done.8.q3_two), channel_id=1, source_target_pairs={{3,2},{4,5},{11,10},{12,13},{19,18},{20,21},{27,26},{28,29}} | collective-permute-start | bytes 1572872 | tf_op jit(solution)/shard_map/ppermute | solution.py:103

commit v13 on v12

--- a/solution.py
+++ b/solution.py
@@ -313,7 +313,7 @@
 
     @pl.when(place_ref[1] == 1)
     def _():
-        out_ref[:, pl.ds(pl.multiple_of(odd * width, 128), width)] = zero_ref[...]
+        out_ref[:, pl.ds(pl.multiple_of(odd * width, 128), width)] = zero_ref[...].T
         out_ref[:, pl.ds(pl.multiple_of((1 - odd) * width, 128), width)] = product(1 + odd)
         pack(product(3 - 3 * odd), out_ref, 2 * width)
 
@@ -508,7 +508,7 @@
     @pl.when(active & (place == 0))
     def _():
         add(at(odd, 3), q0[...])
-        add(at(turned(3, odd)), q0_last[:, pl.ds(here, rows)].T)
+        add(at(turned(3, odd)), q0_last[...])
         trace(q0[:, own(2 * odd)])
 
     @pl.when(active & (place == 1))
@@ -562,7 +562,6 @@
             ),
         )
 
-    whole = lambda block: pl.BlockSpec((rows, width), lambda i, place: (0, block))
     return pl.pallas_call(
         finish_kernel,
         out_shape=(
@@ -578,7 +577,7 @@
                     (chunk, nodes), lambda i, place: (jnp.where(place[4] == 0, i, 0), 0)
                 ),
                 picked(0, 3),
-                whole(0),
+                picked(0, 1),
                 pl.BlockSpec((rows, 11 * width // 4), lambda i, place: (0, 0)),
                 picked(3, 1),
                 turned_block(lambda odd: 1),
@@ -723,14 +722,14 @@
     q2_own = product_two(place, h2, across, q0_own)
     q2 = moved(q2_own, 1, 2)
 
-    h3 = multiply(place, c3, prior)
-    q30 = multiply(place, [h3], across, lambda odd: 3 * odd, 1)
-    q0_last = moved(q30, 1, 0)
-    q32 = multiply(place, [after(h3, q30)], across, lambda odd: 2 - odd, 1)
+    across = turn(place, 3, 0, c3[0], after(across, q2_own))
+    across = turn(place, 3, 1, c3[1], across)
+    q03 = multiply(place, [h0], across, lambda odd: 3 - 3 * odd, 1)
+    q0_last = moved(q03, 1, 0)
+    h3 = multiply(place, [after(c3[0], q03), c3[1]], prior)
+    q32 = multiply(place, [h3], across, lambda odd: 2 - odd, 1)
     q3_two = moved(q32, 1, 3)
-    across = turn(place, 3, 0, c3[0], after(across, q32))
-    across = turn(place, 3, 1, c3[1], across)
-    q3_own = product_rest(place, h3, across, q30)
+    q3_own = product_rest(place, after(h3, q32), across, q03)
     q3 = moved(q3_own, 1, 3)
     h1 = multiply(place, [after(c1[0], q3_own), c1[1]], prior)
     q11 = multiply(place, [h1], across, lambda odd: 1 + odd, 1)

time: 127 us -> 122 us (0.961)
  the two profiles are of different devices: /device:TPU:0 before, /device:TPU:1 now
where the time goes in v13:
time: 122 us
  waiting for transfers between devices  55.8 us (46%)
  Pallas kernels  30.8 us (25%)
  starting transfers between devices  30 us (25%)
  between operations  3.12 us (3%)
  local copies, waits for them, and re-layouts  2.39 us (2%)
    ppermute x13, waiting for transfers between devices, moved(): lax.ppermute(value, ('dom', 'col'), route(source, target, lax.axis_size('...  43 us
    ppermute x13, starting transfers between devices, moved(): lax.ppermute(value, ('dom', 'col'), route(source, target, lax.axis_size('...  28 us
    ppermute x1, waiting for transfers between devices, passed_along(): lax.ppermute(value, axis, [(source, source + steps) for source in range(i...  12.8 us
    pallas_call x6, Pallas kernels, turn(): pl.pallas_call(turn_kernel, out_shape=jax.ShapeDtypeStruct((nodes, nodes)...  5.98 us
    pallas_call x2, Pallas kernels, couple(): pl.pallas_call(couple_kernel, out_shape=jax.ShapeDtypeStruct((rows, nodes...  4.81 us
    pallas_call x6, Pallas kernels, multiply(): pl.pallas_call(functools.partial(multiply_kernel, first, count, len(lefts...  3.48 us
    pallas_call x2, Pallas kernels, couple_here(): pl.pallas_call(kernel, out_shape=jax.ShapeDtypeStruct((rows, nodes), BF16...  3.45 us
    pallas_call x1, Pallas kernels, finish_last(): pl.pallas_call(last_kernel, out_shape=(jax.ShapeDtypeStruct((rows, nodes)...  2.63 us
  transfers between devices with their start and end apart: 14, of which 7 were waited for; matrix products, arithmetic and copies ran while one was open for 0% of the time, Pallas kernels for 23%

profile of v13, /device:TPU:1, one launch (start us, length us, event | category | flops | bytes accessed | tf_op | source)
XLA Modules:
  0.0 122.2 jit_solution(2572778357269993544)
XLA Ops:
  0.6 2.0 %collective-permute-start = (bf16[1,512,2048]{2,1,0:T(8,128)(2,1)}, bf16[1,512,2048]{2,1,0:T(8,128)(2,1)}, u32[]{:S(2)}, u32[]{:S(2)}) collective-permute-start(bf16[1,512,2048]{2,1,0:T(8,128)(2,1)} %param.8), channel_id=1, source_target_pairs={{4,0},{8,4},{12,8},{5,1},{9,5},{13,9},{6,2},{10,6},{14,10},{7,3},{... | collective-permute-start | bytes 6291464 | tf_op jit(solution)/shard_map/ppermute | solution.py:20
  2.6 2.0 %collective-permute-start.4 = (bf16[512,2048]{1,0:T(8,128)(2,1)}, bf16[512,2048]{1,0:T(8,128)(2,1)}, u32[]{:S(2)}, u32[]{:S(2)}) collective-permute-start(bf16[512,2048]{1,0:T(8,128)(2,1)} %bitcast.8), channel_id=1, source_target_pairs={{2,1},{5,6},{10,9},{13,14},{18,17},{21,22},{26,25},{29,30}} | collective-permute-start | bytes 6291464 | tf_op jit(solution)/shard_map/ppermute | solution.py:103
  7.4 1.6 %copy-done = bf16[1,512,2048]{2,1,0:T(8,128)(2,1)S(1)} copy-done((bf16[1,512,2048]{2,1,0:T(8,128)(2,1)S(1)}, bf16[1,512,2048]{2,1,0:T(8,128)(2,1)}, u32[]{:S(2)}) %copy-start) | copy-done | bytes 2097176
  9.7 2.4 %couple.3.coupled_ref.refs_1_ = bf16[256,2048]{1,0:T(8,128)(2,1)S(1)} custom-call(f32[1]{0:T(128)S(6)} %copy.21.rate_ref.refs_0_, s32[1,2048]{1,0:T(1,128)S(1)} %bitcast.16, bf16[512,2048]{1,0:T(8,128)(2,1)S(1)} %bitcast.10), custom_call_target="tpu_custom_call" | custom-call | flops 1048576 | bytes 65536 | tf_op jit(solution)/shard_map/couple/pallas_call | solution.py:73
  12.1 2.4 %couple.2.coupled_ref.refs_0_ = bf16[256,2048]{1,0:T(8,128)(2,1)S(1)} custom-call(f32[1]{0:T(128)S(6)} %copy.21.rate_ref.refs_0_, s32[1,2048]{1,0:T(1,128)S(1)} %bitcast.17, bf16[512,2048]{1,0:T(8,128)(2,1)S(1)} %bitcast.11), custom_call_target="tpu_custom_call" | custom-call | flops 1048576 | bytes 65536 | tf_op jit(solution)/shard_map/couple/pallas_call | solution.py:73
  16.3 12.8 %collective-permute-done = bf16[1,512,2048]{2,1,0:T(8,128)(2,1)} collective-permute-done((bf16[1,512,2048]{2,1,0:T(8,128)(2,1)}, bf16[1,512,2048]{2,1,0:T(8,128)(2,1)}, u32[]{:S(2)}, u32[]{:S(2)}) %collective-permute-start) | collective-permute-done | bytes 2097184 | tf_op jit(solution)/shard_map/ppermute | solution.py:20
  29.2 2.3 %prior_parts.1 = (bf16[512,2048]{1,0:T(8,128)(2,1)S(1)}, bf16[512,1408]{1,0:T(8,128)(2,1)S(1)}, bf16[512,896]{1,0:T(8,128)(2,1)S(1)}, bf16[512,384]{1,0:T(8,128)(2,1)S(1)}) custom-call(s32[5]{0:T(128)S(1)} %stack.16.place_ref, bf16[512,2048]{1,0:T(8,128)(2,1)} %bitcast.5.shifted_ref, bf16[512,2048]{1,0:T(8,128)(2,1)S(1)} %bitcast.14), custom_call_target="tpu_custom_call" | custom-call | flops 1048576 | bytes 65536 | tf_op jit(solution)/shard_map/prior_parts/pallas_call | solution.py:398
  33.0 5.3 %collective-permute-start.1 = (bf16[512,384]{1,0:T(8,128)(2,1)S(1)}, bf16[512,384]{1,0:T(8,128)(2,1)S(1)}, u32[]{:S(2)}, u32[]{:S(2)}) collective-permute-start(bf16[512,384]{1,0:T(8,128)(2,1)S(1)} %get-tuple-element.25), channel_id=1, source_target_pairs={{3,1},{4,6},{11,9},{12,14},{19,17},{20,22},{27,25},{28,30}} | collective-permute-start | bytes 1179656 | tf_op jit(solution)/shard_map/ppermute | solution.py:103
  38.3 2.8 %couple_here.2.coupled_ref.second_ref.left_ref = bf16[512,2048]{1,0:T(8,128)(2,1)S(1)} custom-call(s32[5]{0:T(128)S(1)} %stack.16.place_ref, f32[1]{0:T(128)S(6)} %copy.21.rate_ref.refs_0_, s32[1,2048]{1,0:T(1,128)S(1)} %bitcast.18, bf16[512,2048]{1,0:T(8,128)(2,1)} %collective-permute-done.4.refs_2_), custom_call_target="tpu_custom_call" | custom-call | flops 1048576 | bytes 65536 | tf_op jit(solution)/shard_map/couple_here/pallas_call | solution.py:115
  41.2 1.2 turn.8.refs_0_
  43.0 1.2 turn.9.refs_1_.right_ref.refs_0_
  44.8 2.5 %collective-permute-done.1.last_three = bf16[512,384]{1,0:T(8,128)(2,1)S(1)} collective-permute-done((bf16[512,384]{1,0:T(8,128)(2,1)S(1)}, bf16[512,384]{1,0:T(8,128)(2,1)S(1)}, u32[]{:S(2)}, u32[]{:S(2)}) %collective-permute-start.1) | collective-permute-done | bytes 393248 | tf_op jit(solution)/shard_map/ppermute | solution.py:103
  47.3 11.0 %collective-permute-start.5 = (bf16[256,2048]{1,0:T(8,128)(2,1)S(1)}, bf16[256,2048]{1,0:T(8,128)(2,1)S(1)}, u32[]{:S(2)}, u32[]{:S(2)}) collective-permute-start(bf16[256,2048]{1,0:T(8,128)(2,1)S(1)} %couple.2.coupled_ref.refs_0_), channel_id=1, source_target_pairs={{3,1},{4,6},{11,9},{12,14},{19,17},{20,22},{27,25},{28,30}} | collective-permute-start | bytes 3145736 | tf_op jit(solution)/shard_map/ppermute | solution.py:103
  58.3 1.4 %collective-permute-start.7 = (bf16[256,2048]{1,0:T(8,128)(2,1)S(1)}, bf16[256,2048]{1,0:T(8,128)(2,1)S(1)}, u32[]{:S(2)}, u32[]{:S(2)}) collective-permute-start(bf16[256,2048]{1,0:T(8,128)(2,1)S(1)} %couple.3.coupled_ref.refs_1_), channel_id=1, source_target_pairs={{3,1},{4,6},{11,9},{12,14},{19,17},{20,22},{27,25},{28,30}} | collective-permute-start | bytes 3145736 | tf_op jit(solution)/shard_map/ppermute | solution.py:103
  64.0 6.0 %collective-permute-done.5.coupled_ref.refs_0_ = bf16[256,2048]{1,0:T(8,128)(2,1)S(1)} collective-permute-done((bf16[256,2048]{1,0:T(8,128)(2,1)S(1)}, bf16[256,2048]{1,0:T(8,128)(2,1)S(1)}, u32[]{:S(2)}, u32[]{:S(2)}) %collective-permute-start.5) | collective-permute-done | bytes 1048608 | tf_op jit(solution)/shard_map/ppermute | solution.py:103
  70.9 10.4 %collective-permute-done.7.coupled_ref.refs_1_ = bf16[256,2048]{1,0:T(8,128)(2,1)S(1)} collective-permute-done((bf16[256,2048]{1,0:T(8,128)(2,1)S(1)}, bf16[256,2048]{1,0:T(8,128)(2,1)S(1)}, u32[]{:S(2)}, u32[]{:S(2)}) %collective-permute-start.7) | collective-permute-done | bytes 1048608 | tf_op jit(solution)/shard_map/ppermute | solution.py:103
  84.7 1.3 %collective-permute-start.8 = (bf16[512,512]{1,0:T(8,128)(2,1)S(1)}, bf16[512,512]{1,0:T(8,128)(2,1)S(1)}, u32[]{:S(2)}, u32[]{:S(2)}) collective-permute-start(bf16[512,512]{1,0:T(8,128)(2,1)S(1)} %multiply.9), channel_id=1, source_target_pairs={{1,3},{6,4},{9,11},{14,12},{17,19},{22,20},{25,27},{30,28}} | collective-permute-start | bytes 1572872 | tf_op jit(solution)/shard_map/ppermute | solution.py:103
  86.6 1.3 %collective-permute-start.12 = (bf16[512,1408]{1,0:T(8,128)(2,1)S(1)}, bf16[512,1408]{1,0:T(8,128)(2,1)S(1)}, u32[]{:S(2)}, u32[]{:S(2)}) collective-permute-start(bf16[512,1408]{1,0:T(8,128)(2,1)S(1)} %product_rest.1.q31), channel_id=1, source_target_pairs={{1,3},{6,4},{9,11},{14,12},{17,19},{22,20},{25,27},{30,28}} | collective-permute-start | bytes 4325384 | tf_op jit(solution)/shard_map/ppermute | solution.py:103
  91.3 12.7 %collective-permute-done.8.q3_two = bf16[512,512]{1,0:T(8,128)(2,1)S(1)} collective-permute-done((bf16[512,512]{1,0:T(8,128)(2,1)S(1)}, bf16[512,512]{1,0:T(8,128)(2,1)S(1)}, u32[]{:S(2)}, u32[]{:S(2)}) %collective-permute-start.8) | collective-permute-done | bytes 524320 | tf_op jit(solution)/shard_map/ppermute | solution.py:103
  104.0 1.3 %collective-permute-start.11 = (bf16[512,512]{1,0:T(8,128)(2,1)S(1)}, bf16[512,512]{1,0:T(8,128)(2,1)S(1)}, u32[]{:S(2)}, u32[]{:S(2)}) collective-permute-start(bf16[512,512]{1,0:T(8,128)(2,1)S(1)} %collective-permute-done.8.q3_two), channel_id=1, source_target_pairs={{3,2},{4,5},{11,10},{12,13},{19,18},{20,21},{27,26},{28,29}} | collective-permute-start | bytes 1572872 | tf_op jit(solution)/shard_map/ppermute | solution.py:103
  105.3 2.6 %finish.1 = (bf16[512,2048]{1,0:T(8,128)(2,1)}, f32[1,512]{1,0:T(1,128)S(1)}) custom-call(s32[5]{0:T(128)S(1)} %tick.3.place_ref, bf16[512,2048]{1,0:T(8,128)(2,1)S(1)} %bitcast.12, bf16[512,2048]{1,0:T(8,128)(2,1)S(1)} %bitcast.15, bf16[512,1536]{1,0:T(8,128)(2,1)S(1)} %collective-permute-done.9.refs_0_.q0, ...), custom_call_target="tpu_custom_call" | custom-call | flops 14000000000 | bytes 65536 | tf_op jit(solution)/shard_map/finish/pallas_call | solution.py:565
  107.9 3.5 %collective-permute-done.11.q2_last = bf16[512,512]{1,0:T(8,128)(2,1)S(1)} collective-permute-done((bf16[512,512]{1,0:T(8,128)(2,1)S(1)}, bf16[512,512]{1,0:T(8,128)(2,1)S(1)}, u32[]{:S(2)}, u32[]{:S(2)}) %collective-permute-start.11) | collective-permute-done | bytes 524320 | tf_op jit(solution)/shard_map/ppermute | solution.py:103
  111.4 8.1 %collective-permute-done.12.q3 = bf16[512,1408]{1,0:T(8,128)(2,1)S(1)} collective-permute-done((bf16[512,1408]{1,0:T(8,128)(2,1)S(1)}, bf16[512,1408]{1,0:T(8,128)(2,1)S(1)}, u32[]{:S(2)}, u32[]{:S(2)}) %collective-permute-start.12) | collective-permute-done | bytes 1441824 | tf_op jit(solution)/shard_map/ppermute | solution.py:103
  119.4 2.6 %finish_last.1 = (bf16[512,2048]{1,0:T(8,128)(2,1)}, f32[1,512]{1,0:T(1,128)}) custom-call(s32[5]{0:T(128)S(1)} %stack.16.place_ref, bf16[512,2048]{1,0:T(8,128)(2,1)S(1)} %bitcast.13, bf16[512,512]{1,0:T(8,128)(2,1)S(1)} %collective-permute-done.11.q2_last, bf16[512,1408]{1,0:T(8,128)(2,1)S(1)} %collective-permute-done.12.q3, ...), custom_call_target="tpu_custom_call", output_to_operand_aliasing={{0}: (4, {})} | custom-call | flops 1048576 | bytes 65536 | tf_op jit(solution)/shard_map/finish_last/pallas_call | solution.py:670
  (42 shorter events, 18.5 us)
Async XLA Ops:
  0.6 28.5 %collective-permute-start = (bf16[1,512,2048]{2,1,0:T(8,128)(2,1)}, bf16[1,512,2048]{2,1,0:T(8,128)(2,1)}, u32[]{:S(2)}, u32[]{:S(2)}) collective-permute-start(bf16[1,512,2048]{2,1,0:T(8,128)(2,1)} %param.8), channel_id=1, source_target_pairs={{4,0},{8,4},{12,8},{5,1},{9,5},{13,9},{6,2},{10,6},{14,10},{7,3},{... | collective-permute-start | bytes 6291464 | tf_op jit(solution)/shard_map/ppermute | solution.py:20
  2.6 35.7 %collective-permute-start.4 = (bf16[512,2048]{1,0:T(8,128)(2,1)}, bf16[512,2048]{1,0:T(8,128)(2,1)}, u32[]{:S(2)}, u32[]{:S(2)}) collective-permute-start(bf16[512,2048]{1,0:T(8,128)(2,1)} %bitcast.8), channel_id=1, source_target_pairs={{2,1},{5,6},{10,9},{13,14},{18,17},{21,22},{26,25},{29,30}} | collective-permute-start | bytes 6291464 | tf_op jit(solution)/shard_map/ppermute | solution.py:103
  4.6 37.8 %collective-permute-start.3 = (bf16[512,2048]{1,0:T(8,128)(2,1)}, bf16[512,2048]{1,0:T(8,128)(2,1)S(1)}, u32[]{:S(2)}, u32[]{:S(2)}) collective-permute-start(bf16[512,2048]{1,0:T(8,128)(2,1)} %bitcast.9), channel_id=1, source_target_pairs={{0,1},{7,6},{8,9},{15,14},{16,17},{23,22},{24,25},{31,30}} | collective-permute-start | bytes 6291464 | tf_op jit(solution)/shard_map/ppermute | solution.py:103
  7.4 1.6 %copy-start = (bf16[1,512,2048]{2,1,0:T(8,128)(2,1)S(1)}, bf16[1,512,2048]{2,1,0:T(8,128)(2,1)}, u32[]{:S(2)}) copy-start(bf16[1,512,2048]{2,1,0:T(8,128)(2,1)} %param.9) | copy-start | bytes 6291460
  9.0 0.7 copy-start.3
  15.4 13.8 %copy-start.2 = (bf16[1,512,2048]{2,1,0:T(8,128)(2,1)S(1)}, bf16[1,512,2048]{2,1,0:T(8,128)(2,1)}, u32[]{:S(2)}) copy-start(bf16[1,512,2048]{2,1,0:T(8,128)(2,1)} %param.7) | copy-start | bytes 6291460
  29.2 9.2 %copy-start.4 = (s32[2048]{0:T(1024)S(1)}, s32[2048]{0:T(1024)}, u32[]{:S(2)}) copy-start(s32[2048]{0:T(1024)} %param.13) | copy-start | bytes 24580
  31.5 26.8 %collective-permute-start.6 = (bf16[512,1408]{1,0:T(8,128)(2,1)S(1)}, bf16[512,1408]{1,0:T(8,128)(2,1)S(1)}, u32[]{:S(2)}, u32[]{:S(2)}) collective-permute-start(bf16[512,1408]{1,0:T(8,128)(2,1)S(1)} %get-tuple-element.32), channel_id=1, source_target_pairs={{0,1},{7,6},{8,9},{15,14},{16,17},{23,22},{24,25},{31,30}} | collective-permute-start | bytes 4325384 | tf_op jit(solution)/shard_map/ppermute | solution.py:103
  32.2 15.0 %collective-permute-start.2 = (bf16[512,896]{1,0:T(8,128)(2,1)S(1)}, bf16[512,896]{1,0:T(8,128)(2,1)S(1)}, u32[]{:S(2)}, u32[]{:S(2)}) collective-permute-start(bf16[512,896]{1,0:T(8,128)(2,1)S(1)} %get-tuple-element.26), channel_id=1, source_target_pairs={{2,1},{5,6},{10,9},{13,14},{18,17},{21,22},{26,25},{29,30}} | collective-permute-start | bytes 2752520 | tf_op jit(solution)/shard_map/ppermute | solution.py:103
  33.0 14.3 %collective-permute-start.1 = (bf16[512,384]{1,0:T(8,128)(2,1)S(1)}, bf16[512,384]{1,0:T(8,128)(2,1)S(1)}, u32[]{:S(2)}, u32[]{:S(2)}) collective-permute-start(bf16[512,384]{1,0:T(8,128)(2,1)S(1)} %get-tuple-element.25), channel_id=1, source_target_pairs={{3,1},{4,6},{11,9},{12,14},{19,17},{20,22},{27,25},{28,30}} | collective-permute-start | bytes 1179656 | tf_op jit(solution)/shard_map/ppermute | solution.py:103
  47.3 22.7 %collective-permute-start.5 = (bf16[256,2048]{1,0:T(8,128)(2,1)S(1)}, bf16[256,2048]{1,0:T(8,128)(2,1)S(1)}, u32[]{:S(2)}, u32[]{:S(2)}) collective-permute-start(bf16[256,2048]{1,0:T(8,128)(2,1)S(1)} %couple.2.coupled_ref.refs_0_), channel_id=1, source_target_pairs={{3,1},{4,6},{11,9},{12,14},{19,17},{20,22},{27,25},{28,30}} | collective-permute-start | bytes 3145736 | tf_op jit(solution)/shard_map/ppermute | solution.py:103
  58.3 22.9 %collective-permute-start.7 = (bf16[256,2048]{1,0:T(8,128)(2,1)S(1)}, bf16[256,2048]{1,0:T(8,128)(2,1)S(1)}, u32[]{:S(2)}, u32[]{:S(2)}) collective-permute-start(bf16[256,2048]{1,0:T(8,128)(2,1)S(1)} %couple.3.coupled_ref.refs_1_), channel_id=1, source_target_pairs={{3,1},{4,6},{11,9},{12,14},{19,17},{20,22},{27,25},{28,30}} | collective-permute-start | bytes 3145736 | tf_op jit(solution)/shard_map/ppermute | solution.py:103
  61.4 27.6 %collective-permute-start.9 = (bf16[512,1536]{1,0:T(8,128)(2,1)S(1)}, bf16[512,1536]{1,0:T(8,128)(2,1)S(1)}, u32[]{:S(2)}, u32[]{:S(2)}) collective-permute-start(bf16[512,1536]{1,0:T(8,128)(2,1)S(1)} %multiply.6.zero_ref.q01), channel_id=1, source_target_pairs={{1,0},{6,7},{9,8},{14,15},{17,16},{22,23},{25,24},{30,31}} | collective-permute-start | bytes 4718600 | tf_op jit(solution)/shard_map/ppermute | solution.py:103
  63.2 42.0 %collective-permute-start.13 = (bf16[512,1408]{1,0:T(8,128)(2,1)S(1)}, bf16[512,1408]{1,0:T(8,128)(2,1)S(1)}, u32[]{:S(2)}, u32[]{:S(2)}) collective-permute-start(bf16[512,1408]{1,0:T(8,128)(2,1)S(1)} %product_two.1.q21), channel_id=1, source_target_pairs={{1,2},{6,5},{9,10},{14,13},{17,18},{22,21},{25,26},{30,29}} | collective-permute-start | bytes 4325384 | tf_op jit(solution)/shard_map/ppermute | solution.py:103
  82.7 7.4 %collective-permute-start.10 = (bf16[512,512]{1,0:T(8,128)(2,1)S(1)}, bf16[512,512]{1,0:T(8,128)(2,1)S(1)}, u32[]{:S(2)}, u32[]{:S(2)}) collective-permute-start(bf16[512,512]{1,0:T(8,128)(2,1)S(1)} %multiply.7.zero_ref), channel_id=1, source_target_pairs={{1,0},{6,7},{9,8},{14,15},{17,16},{22,23},{25,24},{30,31}} | collective-permute-start | bytes 1572872 | tf_op jit(solution)/shard_map/ppermute | solution.py:103
  84.7 19.3 %collective-permute-start.8 = (bf16[512,512]{1,0:T(8,128)(2,1)S(1)}, bf16[512,512]{1,0:T(8,128)(2,1)S(1)}, u32[]{:S(2)}, u32[]{:S(2)}) collective-permute-start(bf16[512,512]{1,0:T(8,128)(2,1)S(1)} %multiply.9), channel_id=1, source_target_pairs={{1,3},{6,4},{9,11},{14,12},{17,19},{22,20},{25,27},{30,28}} | collective-permute-start | bytes 1572872 | tf_op jit(solution)/shard_map/ppermute | solution.py:103
  86.6 32.9 %collective-permute-start.12 = (bf16[512,1408]{1,0:T(8,128)(2,1)S(1)}, bf16[512,1408]{1,0:T(8,128)(2,1)S(1)}, u32[]{:S(2)}, u32[]{:S(2)}) collective-permute-start(bf16[512,1408]{1,0:T(8,128)(2,1)S(1)} %product_rest.1.q31), channel_id=1, source_target_pairs={{1,3},{6,4},{9,11},{14,12},{17,19},{22,20},{25,27},{30,28}} | collective-permute-start | bytes 4325384 | tf_op jit(solution)/shard_map/ppermute | solution.py:103
  90.1 15.2 %copy-start.1 = (bf16[1,512,2048]{2,1,0:T(8,128)(2,1)S(1)}, bf16[1,512,2048]{2,1,0:T(8,128)(2,1)}, u32[]{:S(2)}) copy-start(bf16[1,512,2048]{2,1,0:T(8,128)(2,1)} %param.9) | copy-start | bytes 6291460
  104.0 7.4 %collective-permute-start.11 = (bf16[512,512]{1,0:T(8,128)(2,1)S(1)}, bf16[512,512]{1,0:T(8,128)(2,1)S(1)}, u32[]{:S(2)}, u32[]{:S(2)}) collective-permute-start(bf16[512,512]{1,0:T(8,128)(2,1)S(1)} %collective-permute-done.8.q3_two), channel_id=1, source_target_pairs={{3,2},{4,5},{11,10},{12,13},{19,18},{20,21},{27,26},{28,29}} | collective-permute-start | bytes 1572872 | tf_op jit(solution)/shard_map/ppermute | solution.py:103

commit v14 on v13

--- a/solution.py
+++ b/solution.py
@@ -302,11 +302,12 @@
     )(place, own, first, second)
 
 
-def rest_kernel(place_ref, left_ref, right_ref, zero_ref, out_ref):
+def rest_kernel(place_ref, upper_ref, lower_ref, right_ref, zero_ref, out_ref):
     odd = place_ref[0]
     width = zero_ref.shape[1]
-
-    def product(block):
+    half = width // 2
+
+    def product(left_ref, block):
         columns = pl.ds(pl.multiple_of(block * width, 128), width)
         value = jnp.dot(left_ref[...], right_ref[:, columns], preferred_element_type=F32)
         return value.astype(BF16)
@@ -314,23 +315,25 @@
     @pl.when(place_ref[1] == 1)
     def _():
         out_ref[:, pl.ds(pl.multiple_of(odd * width, 128), width)] = zero_ref[...].T
-        out_ref[:, pl.ds(pl.multiple_of((1 - odd) * width, 128), width)] = product(1 + odd)
-        pack(product(3 - 3 * odd), out_ref, 2 * width)
-
-
-def product_rest(place, half, across, zero):
-    rows = half.shape[0]
-    width = across.shape[0] // 4
+        other = pl.ds(pl.multiple_of((1 - odd) * width, 128), width)
+        for part, left_ref in enumerate((upper_ref, lower_ref)):
+            rows = pl.ds(part * half, half)
+            out_ref[rows, other] = product(left_ref, 1 + odd)
+            pack_rows(part, product(left_ref, 3 - 3 * odd), out_ref.at[rows], 2 * width)
+
+
+def product_rest(place, halves, across, zero):
+    rows, width = zero.shape
     vmem = pl.BlockSpec(memory_space=pltpu.VMEM)
     return pl.pallas_call(
         rest_kernel,
         out_shape=jax.ShapeDtypeStruct((rows, 11 * width // 4), BF16),
-        in_specs=[pl.BlockSpec(memory_space=pltpu.SMEM)] + [vmem] * 3,
+        in_specs=[pl.BlockSpec(memory_space=pltpu.SMEM)] + [vmem] * 4,
         out_specs=vmem,
         compiler_params=pltpu.CompilerParams(vmem_limit_bytes=6 * MIB),
         cost_estimate=LIGHT,
         name="product_rest",
-    )(place, half, across, zero)
+    )(place, *halves, across, zero)
 
 
 def pack_rows(part, value, out_ref, column):
@@ -708,7 +711,7 @@
     across = turn(place, 2, 0, c2, across)
     c0 = couple_here(place, after(p0, across), node_class, coupling_rate)
     across = turn(place, 0, 0, c0, across)
-    column, h0_one, h2_one = own_column(place, row, c0, c2)
+    column, h0_one, h2_one = own_column(place, after(row, last_three, near_two), c0, c2)
     c3 = [
         moved(after(c1[0], last_three, near_two, across), 3, 1),
         moved(after(c1[1], far_zero, h2_one), 3, 1),
@@ -723,13 +726,14 @@
     q2 = moved(q2_own, 1, 2)
 
     across = turn(place, 3, 0, c3[0], after(across, q2_own))
-    across = turn(place, 3, 1, c3[1], across)
+    upper = multiply(place, [c3[0]], prior)
+    across = turn(place, 3, 1, c3[1], after(across, upper))
     q03 = multiply(place, [h0], across, lambda odd: 3 - 3 * odd, 1)
     q0_last = moved(q03, 1, 0)
-    h3 = multiply(place, [after(c3[0], q03), c3[1]], prior)
-    q32 = multiply(place, [h3], across, lambda odd: 2 - odd, 1)
+    h3 = [upper, multiply(place, [after(c3[1], q03)], prior)]
+    q32 = multiply(place, h3, across, lambda odd: 2 - odd, 1)
     q3_two = moved(q32, 1, 3)
-    q3_own = product_rest(place, after(h3, q32), across, q03)
+    q3_own = product_rest(place, h3, across, after(q03, q32))
     q3 = moved(q3_own, 1, 3)
     h1 = multiply(place, [after(c1[0], q3_own), c1[1]], prior)
     q11 = multiply(place, [h1], across, lambda odd: 1 + odd, 1)

time: 122 us -> 120 us (0.984)
  waiting for transfers between devices: 55.8 us -> 53.8 us
    ppermute x13, waiting for transfers between devices: 43 us -> 40.9 us  [moved(): lax.ppermute(value, ('dom', 'col'), route(source, target, lax.axis_size('...]
    pallas_call x6 -> x7, Pallas kernels: 3.48 us -> 4.03 us  [multiply(): pl.pallas_call(functools.partial(multiply_kernel, first, count, len(lefts...]
  transfers between devices with their start and end apart: 14 -> 14, of which waited for: 7 -> 7; matrix products, arithmetic and copies ran while one was open for 0% -> 0% of each run, Pallas kernels for 23% -> 24%
where the time goes in v14:
time: 120 us
  waiting for transfers between devices  53.8 us (45%)
  Pallas kernels  31.4 us (26%)
  starting transfers between devices  29.5 us (25%)
  between operations  3.13 us (3%)
  local copies, waits for them, and re-layouts  2.39 us (2%)
    ppermute x13, waiting for transfers between devices, moved(): lax.ppermute(value, ('dom', 'col'), route(source, target, lax.axis_size('...  40.9 us
    ppermute x13, starting transfers between devices, moved(): lax.ppermute(value, ('dom', 'col'), route(source, target, lax.axis_size('...  27.5 us
    ppermute x1, waiting for transfers between devices, passed_along(): lax.ppermute(value, axis, [(source, source + steps) for source in range(i...  12.8 us
    pallas_call x6, Pallas kernels, turn(): pl.pallas_call(turn_kernel, out_shape=jax.ShapeDtypeStruct((nodes, nodes)...  5.99 us
    pallas_call x2, Pallas kernels, couple(): pl.pallas_call(couple_kernel, out_shape=jax.ShapeDtypeStruct((rows, nodes...  4.81 us
    pallas_call x7, Pallas kernels, multiply(): pl.pallas_call(functools.partial(multiply_kernel, first, count, len(lefts...  4.03 us
    pallas_call x2, Pallas kernels, couple_here(): pl.pallas_call(kernel, out_shape=jax.ShapeDtypeStruct((rows, nodes), BF16...  3.45 us
    pallas_call x1, Pallas kernels, finish_last(): pl.pallas_call(last_kernel, out_shape=(jax.ShapeDtypeStruct((rows, nodes)...  2.63 us
  transfers between devices with their start and end apart: 14, of which 7 were waited for; matrix products, arithmetic and copies ran while one was open for 0% of the time, Pallas kernels for 24%

profile of v14, /device:TPU:1, one launch (start us, length us, event | category | flops | bytes accessed | tf_op | source)
XLA Modules:
  0.0 120.1 jit_solution(4614932176641009394)
XLA Ops:
  0.6 2.0 %collective-permute-start = (bf16[1,512,2048]{2,1,0:T(8,128)(2,1)}, bf16[1,512,2048]{2,1,0:T(8,128)(2,1)}, u32[]{:S(2)}, u32[]{:S(2)}) collective-permute-start(bf16[1,512,2048]{2,1,0:T(8,128)(2,1)} %param.8), channel_id=1, source_target_pairs={{4,0},{8,4},{12,8},{5,1},{9,5},{13,9},{6,2},{10,6},{14,10},{7,3},{... | collective-permute-start | bytes 6291464 | tf_op jit(solution)/shard_map/ppermute | solution.py:20
  2.6 2.0 %collective-permute-start.4 = (bf16[512,2048]{1,0:T(8,128)(2,1)}, bf16[512,2048]{1,0:T(8,128)(2,1)}, u32[]{:S(2)}, u32[]{:S(2)}) collective-permute-start(bf16[512,2048]{1,0:T(8,128)(2,1)} %bitcast.8), channel_id=1, source_target_pairs={{2,1},{5,6},{10,9},{13,14},{18,17},{21,22},{26,25},{29,30}} | collective-permute-start | bytes 6291464 | tf_op jit(solution)/shard_map/ppermute | solution.py:103
  7.4 1.6 %copy-done = bf16[1,512,2048]{2,1,0:T(8,128)(2,1)S(1)} copy-done((bf16[1,512,2048]{2,1,0:T(8,128)(2,1)S(1)}, bf16[1,512,2048]{2,1,0:T(8,128)(2,1)}, u32[]{:S(2)}) %copy-start) | copy-done | bytes 2097176
  9.7 2.4 %couple.3.coupled_ref.refs_1_ = bf16[256,2048]{1,0:T(8,128)(2,1)S(1)} custom-call(f32[1]{0:T(128)S(6)} %copy.21.rate_ref.refs_0_, s32[1,2048]{1,0:T(1,128)S(1)} %bitcast.16, bf16[512,2048]{1,0:T(8,128)(2,1)S(1)} %bitcast.10), custom_call_target="tpu_custom_call" | custom-call | flops 1048576 | bytes 65536 | tf_op jit(solution)/shard_map/couple/pallas_call | solution.py:73
  12.1 2.4 %couple.2.coupled_ref.refs_0_ = bf16[256,2048]{1,0:T(8,128)(2,1)S(1)} custom-call(f32[1]{0:T(128)S(6)} %copy.21.rate_ref.refs_0_, s32[1,2048]{1,0:T(1,128)S(1)} %bitcast.17, bf16[512,2048]{1,0:T(8,128)(2,1)S(1)} %bitcast.11), custom_call_target="tpu_custom_call" | custom-call | flops 1048576 | bytes 65536 | tf_op jit(solution)/shard_map/couple/pallas_call | solution.py:73
  16.3 12.8 %collective-permute-done = bf16[1,512,2048]{2,1,0:T(8,128)(2,1)} collective-permute-done((bf16[1,512,2048]{2,1,0:T(8,128)(2,1)}, bf16[1,512,2048]{2,1,0:T(8,128)(2,1)}, u32[]{:S(2)}, u32[]{:S(2)}) %collective-permute-start) | collective-permute-done | bytes 2097184 | tf_op jit(solution)/shard_map/ppermute | solution.py:20
  29.2 2.3 %prior_parts.1 = (bf16[512,2048]{1,0:T(8,128)(2,1)S(1)}, bf16[512,1408]{1,0:T(8,128)(2,1)S(1)}, bf16[512,896]{1,0:T(8,128)(2,1)S(1)}, bf16[512,384]{1,0:T(8,128)(2,1)S(1)}) custom-call(s32[5]{0:T(128)S(1)} %stack.16.place_ref, bf16[512,2048]{1,0:T(8,128)(2,1)} %bitcast.5.shifted_ref, bf16[512,2048]{1,0:T(8,128)(2,1)S(1)} %bitcast.14), custom_call_target="tpu_custom_call" | custom-call | flops 1048576 | bytes 65536 | tf_op jit(solution)/shard_map/prior_parts/pallas_call | solution.py:401
  33.0 5.3 %collective-permute-start.1 = (bf16[512,384]{1,0:T(8,128)(2,1)S(1)}, bf16[512,384]{1,0:T(8,128)(2,1)S(1)}, u32[]{:S(2)}, u32[]{:S(2)}) collective-permute-start(bf16[512,384]{1,0:T(8,128)(2,1)S(1)} %get-tuple-element.27), channel_id=1, source_target_pairs={{3,1},{4,6},{11,9},{12,14},{19,17},{20,22},{27,25},{28,30}} | collective-permute-start | bytes 1179656 | tf_op jit(solution)/shard_map/ppermute | solution.py:103
  38.3 2.8 %couple_here.2.coupled_ref.second_ref.left_ref = bf16[512,2048]{1,0:T(8,128)(2,1)S(1)} custom-call(s32[5]{0:T(128)S(1)} %stack.16.place_ref, f32[1]{0:T(128)S(6)} %copy.21.rate_ref.refs_0_, s32[1,2048]{1,0:T(1,128)S(1)} %bitcast.18, bf16[512,2048]{1,0:T(8,128)(2,1)} %collective-permute-done.4.refs_2_), custom_call_target="tpu_custom_call" | custom-call | flops 1048576 | bytes 65536 | tf_op jit(solution)/shard_map/couple_here/pallas_call | solution.py:115
  41.2 1.2 %turn.8.refs_0_ = bf16[2048,2048]{1,0:T(8,128)(2,1)S(1)} custom-call(s32[5]{0:T(128)S(1)} %stack.16.place_ref, bf16[512,2048]{1,0:T(8,128)(2,1)S(1)} %couple_here.2.coupled_ref.second_ref.left_ref, bf16[2048,2048]{1,0:T(8,128)(2,1)S(1)} %turn.7.refs_0_), custom_call_target="tpu_custom_call", output_to_operand_aliasing={{}: (2, {})} | custom-call | flops 1048576 | bytes 65536 | tf_op jit(solution)/shard_map/turn/pallas_call | solution.py:146
  43.0 1.2 %turn.9.refs_1_.right_ref.refs_0_ = bf16[2048,2048]{1,0:T(8,128)(2,1)S(1)} custom-call(s32[5]{0:T(128)S(1)} %stack.16.place_ref, bf16[512,2048]{1,0:T(8,128)(2,1)S(1)} %couple_here.3.coupled_ref.first_ref.left_ref, bf16[2048,2048]{1,0:T(8,128)(2,1)S(1)} %turn.8.refs_0_), custom_call_target="tpu_custom_call", output_to_operand_aliasing={{}: (2, {})} | custom-call | flops 1048576 | bytes 65536 | tf_op jit(solution)/shard_map/turn/pallas_call | solution.py:146
  44.3 3.0 %collective-permute-done.1.last_three = bf16[512,384]{1,0:T(8,128)(2,1)S(1)} collective-permute-done((bf16[512,384]{1,0:T(8,128)(2,1)S(1)}, bf16[512,384]{1,0:T(8,128)(2,1)S(1)}, u32[]{:S(2)}, u32[]{:S(2)}) %collective-permute-start.1) | collective-permute-done | bytes 393248 | tf_op jit(solution)/shard_map/ppermute | solution.py:103
  47.3 8.1 %collective-permute-start.5 = (bf16[256,2048]{1,0:T(8,128)(2,1)S(1)}, bf16[256,2048]{1,0:T(8,128)(2,1)S(1)}, u32[]{:S(2)}, u32[]{:S(2)}) collective-permute-start(bf16[256,2048]{1,0:T(8,128)(2,1)S(1)} %couple.2.coupled_ref.refs_0_), channel_id=1, source_target_pairs={{3,1},{4,6},{11,9},{12,14},{19,17},{20,22},{27,25},{28,30}} | collective-permute-start | bytes 3145736 | tf_op jit(solution)/shard_map/ppermute | solution.py:103
  56.0 3.7 %collective-permute-start.7 = (bf16[256,2048]{1,0:T(8,128)(2,1)S(1)}, bf16[256,2048]{1,0:T(8,128)(2,1)S(1)}, u32[]{:S(2)}, u32[]{:S(2)}) collective-permute-start(bf16[256,2048]{1,0:T(8,128)(2,1)S(1)} %couple.3.coupled_ref.refs_1_), channel_id=1, source_target_pairs={{3,1},{4,6},{11,9},{12,14},{19,17},{20,22},{27,25},{28,30}} | collective-permute-start | bytes 3145736 | tf_op jit(solution)/shard_map/ppermute | solution.py:103
  64.0 3.1 %collective-permute-done.5.refs_0_.coupled_ref = bf16[256,2048]{1,0:T(8,128)(2,1)S(1)} collective-permute-done((bf16[256,2048]{1,0:T(8,128)(2,1)S(1)}, bf16[256,2048]{1,0:T(8,128)(2,1)S(1)}, u32[]{:S(2)}, u32[]{:S(2)}) %collective-permute-start.5) | collective-permute-done | bytes 1048608 | tf_op jit(solution)/shard_map/ppermute | solution.py:103
  68.5 9.8 %collective-permute-done.7.coupled_ref.refs_0_ = bf16[256,2048]{1,0:T(8,128)(2,1)S(1)} collective-permute-done((bf16[256,2048]{1,0:T(8,128)(2,1)S(1)}, bf16[256,2048]{1,0:T(8,128)(2,1)S(1)}, u32[]{:S(2)}, u32[]{:S(2)}) %collective-permute-start.7) | collective-permute-done | bytes 1048608 | tf_op jit(solution)/shard_map/ppermute | solution.py:103
  81.8 1.3 %collective-permute-start.8 = (bf16[512,512]{1,0:T(8,128)(2,1)S(1)}, bf16[512,512]{1,0:T(8,128)(2,1)S(1)}, u32[]{:S(2)}, u32[]{:S(2)}) collective-permute-start(bf16[512,512]{1,0:T(8,128)(2,1)S(1)} %multiply.11), channel_id=1, source_target_pairs={{1,3},{6,4},{9,11},{14,12},{17,19},{22,20},{25,27},{30,28}} | collective-permute-start | bytes 1572872 | tf_op jit(solution)/shard_map/ppermute | solution.py:103
  83.6 1.3 %collective-permute-start.12 = (bf16[512,1408]{1,0:T(8,128)(2,1)S(1)}, bf16[512,1408]{1,0:T(8,128)(2,1)S(1)}, u32[]{:S(2)}, u32[]{:S(2)}) collective-permute-start(bf16[512,1408]{1,0:T(8,128)(2,1)S(1)} %product_rest.1.q31), channel_id=1, source_target_pairs={{1,3},{6,4},{9,11},{14,12},{17,19},{22,20},{25,27},{30,28}} | collective-permute-start | bytes 4325384 | tf_op jit(solution)/shard_map/ppermute | solution.py:103
  88.4 13.5 %collective-permute-done.8.q3_two = bf16[512,512]{1,0:T(8,128)(2,1)S(1)} collective-permute-done((bf16[512,512]{1,0:T(8,128)(2,1)S(1)}, bf16[512,512]{1,0:T(8,128)(2,1)S(1)}, u32[]{:S(2)}, u32[]{:S(2)}) %collective-permute-start.8) | collective-permute-done | bytes 524320 | tf_op jit(solution)/shard_map/ppermute | solution.py:103
  101.9 1.3 %collective-permute-start.11 = (bf16[512,512]{1,0:T(8,128)(2,1)S(1)}, bf16[512,512]{1,0:T(8,128)(2,1)S(1)}, u32[]{:S(2)}, u32[]{:S(2)}) collective-permute-start(bf16[512,512]{1,0:T(8,128)(2,1)S(1)} %collective-permute-done.8.q3_two), channel_id=1, source_target_pairs={{3,2},{4,5},{11,10},{12,13},{19,18},{20,21},{27,26},{28,29}} | collective-permute-start | bytes 1572872 | tf_op jit(solution)/shard_map/ppermute | solution.py:103
  103.2 2.6 %finish.1 = (bf16[512,2048]{1,0:T(8,128)(2,1)}, f32[1,512]{1,0:T(1,128)S(1)}) custom-call(s32[5]{0:T(128)S(1)} %tick.3.place_ref, bf16[512,2048]{1,0:T(8,128)(2,1)S(1)} %bitcast.12, bf16[512,2048]{1,0:T(8,128)(2,1)S(1)} %bitcast.15, bf16[512,1536]{1,0:T(8,128)(2,1)S(1)} %collective-permute-done.9.refs_0_.q0, ...), custom_call_target="tpu_custom_call" | custom-call | flops 14000000000 | bytes 65536 | tf_op jit(solution)/shard_map/finish/pallas_call | solution.py:568
  105.8 3.5 %collective-permute-done.11.q2_last = bf16[512,512]{1,0:T(8,128)(2,1)S(1)} collective-permute-done((bf16[512,512]{1,0:T(8,128)(2,1)S(1)}, bf16[512,512]{1,0:T(8,128)(2,1)S(1)}, u32[]{:S(2)}, u32[]{:S(2)}) %collective-permute-start.11) | collective-permute-done | bytes 524320 | tf_op jit(solution)/shard_map/ppermute | solution.py:103
  109.3 8.1 %collective-permute-done.12.q3 = bf16[512,1408]{1,0:T(8,128)(2,1)S(1)} collective-permute-done((bf16[512,1408]{1,0:T(8,128)(2,1)S(1)}, bf16[512,1408]{1,0:T(8,128)(2,1)S(1)}, u32[]{:S(2)}, u32[]{:S(2)}) %collective-permute-start.12) | collective-permute-done | bytes 1441824 | tf_op jit(solution)/shard_map/ppermute | solution.py:103
  117.3 2.6 %finish_last.1 = (bf16[512,2048]{1,0:T(8,128)(2,1)}, f32[1,512]{1,0:T(1,128)}) custom-call(s32[5]{0:T(128)S(1)} %stack.16.place_ref, bf16[512,2048]{1,0:T(8,128)(2,1)S(1)} %bitcast.13, bf16[512,512]{1,0:T(8,128)(2,1)S(1)} %collective-permute-done.11.q2_last, bf16[512,1408]{1,0:T(8,128)(2,1)S(1)} %collective-permute-done.12.q3, ...), custom_call_target="tpu_custom_call", output_to_operand_aliasing={{0}: (4, {})} | custom-call | flops 1048576 | bytes 65536 | tf_op jit(solution)/shard_map/finish_last/pallas_call | solution.py:673
  (43 shorter events, 19.1 us)
Async XLA Ops:
  0.6 28.5 %collective-permute-start = (bf16[1,512,2048]{2,1,0:T(8,128)(2,1)}, bf16[1,512,2048]{2,1,0:T(8,128)(2,1)}, u32[]{:S(2)}, u32[]{:S(2)}) collective-permute-start(bf16[1,512,2048]{2,1,0:T(8,128)(2,1)} %param.8), channel_id=1, source_target_pairs={{4,0},{8,4},{12,8},{5,1},{9,5},{13,9},{6,2},{10,6},{14,10},{7,3},{... | collective-permute-start | bytes 6291464 | tf_op jit(solution)/shard_map/ppermute | solution.py:20
  2.6 35.7 %collective-permute-start.4 = (bf16[512,2048]{1,0:T(8,128)(2,1)}, bf16[512,2048]{1,0:T(8,128)(2,1)}, u32[]{:S(2)}, u32[]{:S(2)}) collective-permute-start(bf16[512,2048]{1,0:T(8,128)(2,1)} %bitcast.8), channel_id=1, source_target_pairs={{2,1},{5,6},{10,9},{13,14},{18,17},{21,22},{26,25},{29,30}} | collective-permute-start | bytes 6291464 | tf_op jit(solution)/shard_map/ppermute | solution.py:103
  4.6 37.8 %collective-permute-start.3 = (bf16[512,2048]{1,0:T(8,128)(2,1)}, bf16[512,2048]{1,0:T(8,128)(2,1)S(1)}, u32[]{:S(2)}, u32[]{:S(2)}) collective-permute-start(bf16[512,2048]{1,0:T(8,128)(2,1)} %bitcast.9), channel_id=1, source_target_pairs={{0,1},{7,6},{8,9},{15,14},{16,17},{23,22},{24,25},{31,30}} | collective-permute-start | bytes 6291464 | tf_op jit(solution)/shard_map/ppermute | solution.py:103
  7.4 1.6 %copy-start = (bf16[1,512,2048]{2,1,0:T(8,128)(2,1)S(1)}, bf16[1,512,2048]{2,1,0:T(8,128)(2,1)}, u32[]{:S(2)}) copy-start(bf16[1,512,2048]{2,1,0:T(8,128)(2,1)} %param.9) | copy-start | bytes 6291460
  9.0 0.7 copy-start.3
  15.4 13.8 %copy-start.2 = (bf16[1,512,2048]{2,1,0:T(8,128)(2,1)S(1)}, bf16[1,512,2048]{2,1,0:T(8,128)(2,1)}, u32[]{:S(2)}) copy-start(bf16[1,512,2048]{2,1,0:T(8,128)(2,1)} %param.7) | copy-start | bytes 6291460
  29.2 9.2 %copy-start.4 = (s32[2048]{0:T(1024)S(1)}, s32[2048]{0:T(1024)}, u32[]{:S(2)}) copy-start(s32[2048]{0:T(1024)} %param.13) | copy-start | bytes 24580
  31.5 24.5 %collective-permute-start.6 = (bf16[512,1408]{1,0:T(8,128)(2,1)S(1)}, bf16[512,1408]{1,0:T(8,128)(2,1)S(1)}, u32[]{:S(2)}, u32[]{:S(2)}) collective-permute-start(bf16[512,1408]{1,0:T(8,128)(2,1)S(1)} %get-tuple-element.35), channel_id=1, source_target_pairs={{0,1},{7,6},{8,9},{15,14},{16,17},{23,22},{24,25},{31,30}} | collective-permute-start | bytes 4325384 | tf_op jit(solution)/shard_map/ppermute | solution.py:103
  32.2 15.0 %collective-permute-start.2 = (bf16[512,896]{1,0:T(8,128)(2,1)S(1)}, bf16[512,896]{1,0:T(8,128)(2,1)S(1)}, u32[]{:S(2)}, u32[]{:S(2)}) collective-permute-start(bf16[512,896]{1,0:T(8,128)(2,1)S(1)} %get-tuple-element.28), channel_id=1, source_target_pairs={{2,1},{5,6},{10,9},{13,14},{18,17},{21,22},{26,25},{29,30}} | collective-permute-start | bytes 2752520 | tf_op jit(solution)/shard_map/ppermute | solution.py:103
  33.0 14.3 %collective-permute-start.1 = (bf16[512,384]{1,0:T(8,128)(2,1)S(1)}, bf16[512,384]{1,0:T(8,128)(2,1)S(1)}, u32[]{:S(2)}, u32[]{:S(2)}) collective-permute-start(bf16[512,384]{1,0:T(8,128)(2,1)S(1)} %get-tuple-element.27), channel_id=1, source_target_pairs={{3,1},{4,6},{11,9},{12,14},{19,17},{20,22},{27,25},{28,30}} | collective-permute-start | bytes 1179656 | tf_op jit(solution)/shard_map/ppermute | solution.py:103
  47.3 19.8 %collective-permute-start.5 = (bf16[256,2048]{1,0:T(8,128)(2,1)S(1)}, bf16[256,2048]{1,0:T(8,128)(2,1)S(1)}, u32[]{:S(2)}, u32[]{:S(2)}) collective-permute-start(bf16[256,2048]{1,0:T(8,128)(2,1)S(1)} %couple.2.coupled_ref.refs_0_), channel_id=1, source_target_pairs={{3,1},{4,6},{11,9},{12,14},{19,17},{20,22},{27,25},{28,30}} | collective-permute-start | bytes 3145736 | tf_op jit(solution)/shard_map/ppermute | solution.py:103
  56.0 22.4 %collective-permute-start.7 = (bf16[256,2048]{1,0:T(8,128)(2,1)S(1)}, bf16[256,2048]{1,0:T(8,128)(2,1)S(1)}, u32[]{:S(2)}, u32[]{:S(2)}) collective-permute-start(bf16[256,2048]{1,0:T(8,128)(2,1)S(1)} %couple.3.coupled_ref.refs_1_), channel_id=1, source_target_pairs={{3,1},{4,6},{11,9},{12,14},{19,17},{20,22},{27,25},{28,30}} | collective-permute-start | bytes 3145736 | tf_op jit(solution)/shard_map/ppermute | solution.py:103
  61.4 24.7 %collective-permute-start.9 = (bf16[512,1536]{1,0:T(8,128)(2,1)S(1)}, bf16[512,1536]{1,0:T(8,128)(2,1)S(1)}, u32[]{:S(2)}, u32[]{:S(2)}) collective-permute-start(bf16[512,1536]{1,0:T(8,128)(2,1)S(1)} %multiply.8.zero_ref.q01), channel_id=1, source_target_pairs={{1,0},{6,7},{9,8},{14,15},{17,16},{22,23},{25,24},{30,31}} | collective-permute-start | bytes 4718600 | tf_op jit(solution)/shard_map/ppermute | solution.py:103
  63.2 40.0 %collective-permute-start.13 = (bf16[512,1408]{1,0:T(8,128)(2,1)S(1)}, bf16[512,1408]{1,0:T(8,128)(2,1)S(1)}, u32[]{:S(2)}, u32[]{:S(2)}) collective-permute-start(bf16[512,1408]{1,0:T(8,128)(2,1)S(1)} %product_two.1.q21), channel_id=1, source_target_pairs={{1,2},{6,5},{9,10},{14,13},{17,18},{22,21},{25,26},{30,29}} | collective-permute-start | bytes 4325384 | tf_op jit(solution)/shard_map/ppermute | solution.py:103
  80.0 7.3 %collective-permute-start.10 = (bf16[512,512]{1,0:T(8,128)(2,1)S(1)}, bf16[512,512]{1,0:T(8,128)(2,1)S(1)}, u32[]{:S(2)}, u32[]{:S(2)}) collective-permute-start(bf16[512,512]{1,0:T(8,128)(2,1)S(1)} %multiply.9.zero_ref), channel_id=1, source_target_pairs={{1,0},{6,7},{9,8},{14,15},{17,16},{22,23},{25,24},{30,31}} | collective-permute-start | bytes 1572872 | tf_op jit(solution)/shard_map/ppermute | solution.py:103
  81.8 20.1 %collective-permute-start.8 = (bf16[512,512]{1,0:T(8,128)(2,1)S(1)}, bf16[512,512]{1,0:T(8,128)(2,1)S(1)}, u32[]{:S(2)}, u32[]{:S(2)}) collective-permute-start(bf16[512,512]{1,0:T(8,128)(2,1)S(1)} %multiply.11), channel_id=1, source_target_pairs={{1,3},{6,4},{9,11},{14,12},{17,19},{22,20},{25,27},{30,28}} | collective-permute-start | bytes 1572872 | tf_op jit(solution)/shard_map/ppermute | solution.py:103
  83.6 33.7 %collective-permute-start.12 = (bf16[512,1408]{1,0:T(8,128)(2,1)S(1)}, bf16[512,1408]{1,0:T(8,128)(2,1)S(1)}, u32[]{:S(2)}, u32[]{:S(2)}) collective-permute-start(bf16[512,1408]{1,0:T(8,128)(2,1)S(1)} %product_rest.1.q31), channel_id=1, source_target_pairs={{1,3},{6,4},{9,11},{14,12},{17,19},{22,20},{25,27},{30,28}} | collective-permute-start | bytes 4325384 | tf_op jit(solution)/shard_map/ppermute | solution.py:103
  87.2 16.0 %copy-start.1 = (bf16[1,512,2048]{2,1,0:T(8,128)(2,1)S(1)}, bf16[1,512,2048]{2,1,0:T(8,128)(2,1)}, u32[]{:S(2)}) copy-start(bf16[1,512,2048]{2,1,0:T(8,128)(2,1)} %param.9) | copy-start | bytes 6291460
  101.9 7.4 %collective-permute-start.11 = (bf16[512,512]{1,0:T(8,128)(2,1)S(1)}, bf16[512,512]{1,0:T(8,128)(2,1)S(1)}, u32[]{:S(2)}, u32[]{:S(2)}) collective-permute-start(bf16[512,512]{1,0:T(8,128)(2,1)S(1)} %collective-permute-done.8.q3_two), channel_id=1, source_target_pairs={{3,2},{4,5},{11,10},{12,13},{19,18},{20,21},{27,26},{28,29}} | collective-permute-start | bytes 1572872 | tf_op jit(solution)/shard_map/ppermute | solution.py:103

commit v15 on v14

--- a/solution.py
+++ b/solution.py
@@ -25,66 +25,86 @@
 HEAVY = pl.CostEstimate(flops=14000000000, bytes_accessed=1 << 16, transcendentals=0)
 
 
-def couple_kernel(rate_ref, class_ref, pivot_ref, out_ref, weight_ref):
-    nodes = pivot_ref.shape[1]
-
-    @pl.when(pl.program_id(0) == 0)
-    def _():
-        kind = class_ref[...]
+BLOCK = 256
+SPAN = 512
+
+
+def window(block, nodes):
+    return pl.multiple_of(jnp.clip(block * BLOCK - (SPAN - BLOCK) // 2, 0, nodes - SPAN), 128)
+
+
+def weight_kernel(class_ref, out_ref):
+    nodes = class_ref.shape[1]
+
+    def fill(block, carry):
+        first = pl.multiple_of(block * BLOCK, BLOCK)
+        kind = class_ref[:, pl.ds(first, BLOCK)]
         across = jnp.where(
             kind == 0, 0.25, jnp.where(kind == 1, 0.375, jnp.where(kind == 2, 0.125, 0.5))
         ).astype(F32)
         along = jnp.where(
             kind == 0, 0.25, jnp.where(kind == 1, 0.125, jnp.where(kind == 2, 0.375, 0.0))
         ).astype(F32)
-        node = lax.broadcasted_iota(jnp.int32, (1, nodes), 1)
-        column = node % GX
-        parts = (
-            jnp.where(column > 0, across, 0.0),
-            jnp.where(column < GX - 1, across, 0.0),
-            jnp.where(node >= GX, along, 0.0),
-            jnp.where(node < nodes - GX, along, 0.0),
+        column = (first + lax.broadcasted_iota(jnp.int32, (1, BLOCK), 1)) % GX
+        left = jnp.where(column > 0, across, 0.0)
+        right = jnp.where(column < GX - 1, across, 0.0)
+        shape = (SPAN, BLOCK)
+        offset = (
+            lax.broadcasted_iota(jnp.int32, shape, 0)
+            - lax.broadcasted_iota(jnp.int32, shape, 1)
+            + (window(block, nodes) - first)
         )
-        for which, part in enumerate(parts):
-            weight_ref[which] = jnp.broadcast_to(part, (16, nodes))
-
-    rate = rate_ref[0]
-
-    def group(step, carry):
-        rows = pl.ds(pl.multiple_of(step * 16, 16), 16)
-        value = pivot_ref[rows, :].astype(F32)
-        total = (
-            value
-            + weight_ref[0] * pltpu.roll(value, 1, 1)
-            + weight_ref[1] * pltpu.roll(value, nodes - 1, 1)
-            + weight_ref[2] * pltpu.roll(value, GX, 1)
-            + weight_ref[3] * pltpu.roll(value, nodes - GX, 1)
+        value = jnp.where(jnp.abs(offset) == GX, along, 0.0)
+        value = jnp.where(offset == -1, left, value)
+        value = jnp.where(offset == 1, right, value)
+        value = jnp.where(offset == 0, 1.0, value)
+        out_ref[block] = value.astype(BF16)
+        return carry
+
+    lax.fori_loop(0, nodes // BLOCK, fill, 0)
+
+
+def coupling(node_class):
+    nodes = node_class.shape[0]
+    vmem = pl.BlockSpec(memory_space=pltpu.VMEM)
+    return pl.pallas_call(
+        weight_kernel,
+        out_shape=jax.ShapeDtypeStruct((nodes // BLOCK, SPAN, BLOCK), BF16),
+        in_specs=[vmem],
+        out_specs=vmem,
+        compiler_params=pltpu.CompilerParams(vmem_limit_bytes=6 * MIB),
+        cost_estimate=LIGHT,
+        name="coupling",
+    )(node_class.reshape(1, nodes))
+
+
+def couple_kernel(first, rate_ref, weight_ref, pivot_ref, out_ref):
+    rows, nodes = out_ref.shape
+
+    def block_of(block, carry):
+        source = pl.ds(window(block, nodes), SPAN)
+        target = pl.ds(pl.multiple_of(block * BLOCK, BLOCK), BLOCK)
+        value = jnp.dot(
+            pivot_ref[first : first + rows, source], weight_ref[block], preferred_element_type=F32
         )
-        out_ref[rows, :] = (rate * total).astype(BF16)
+        out_ref[:, target] = (rate_ref[0] * value).astype(BF16)
         return carry
 
-    lax.fori_loop(0, pivot_ref.shape[0] // 16, group, 0)
-
-
-def couple(pivot, node_class, rate, part=0, parts=1):
+    lax.fori_loop(0, nodes // BLOCK, block_of, 0)
+
+
+def couple(pivot, weights, rate, part=0, parts=1):
     rows, nodes = pivot.shape[0] // parts, pivot.shape[1]
-    chunk = min(rows, 128)
-    steps = rows // chunk
-    return pl.pallas_call(
-        couple_kernel,
+    vmem = pl.BlockSpec(memory_space=pltpu.VMEM)
+    return pl.pallas_call(
+        functools.partial(couple_kernel, part * rows),
         out_shape=jax.ShapeDtypeStruct((rows, nodes), BF16),
-        grid=(steps,),
-        in_specs=[
-            pl.BlockSpec(memory_space=pltpu.SMEM),
-            pl.BlockSpec((1, nodes), lambda i: (0, 0)),
-            pl.BlockSpec((chunk, nodes), lambda i: (part * steps + i, 0)),
-        ],
-        out_specs=pl.BlockSpec((chunk, nodes), lambda i: (i, 0)),
-        scratch_shapes=[pltpu.VMEM((4, 16, nodes), F32)],
-        compiler_params=pltpu.CompilerParams(vmem_limit_bytes=6 * MIB),
+        in_specs=[pl.BlockSpec(memory_space=pltpu.SMEM), vmem, vmem],
+        out_specs=vmem,
+        compiler_params=pltpu.CompilerParams(vmem_limit_bytes=8 * MIB),
         cost_estimate=LIGHT,
         name="couple",
-    )(rate, node_class.reshape(1, nodes), pivot)
+    )(rate, weights, pivot)
 
 
 def turned(block, odd):
@@ -103,33 +123,22 @@
     return lax.ppermute(value, ("dom", "col"), route(source, target, lax.axis_size("dom")))
 
 
-def couple_here(place, pivot, node_class, rate):
-    rows, nodes = pivot.shape
-    chunk = 128
-
+def couple_here(place, pivot, weights, rate):
     def kernel(place_ref, *refs):
         @pl.when(place_ref[1] == 1)
         def _():
-            couple_kernel(*refs)
-
+            couple_kernel(0, *refs)
+
+    scalars, vmem = pl.BlockSpec(memory_space=pltpu.SMEM), pl.BlockSpec(memory_space=pltpu.VMEM)
     return pl.pallas_call(
         kernel,
-        out_shape=jax.ShapeDtypeStruct((rows, nodes), BF16),
-        grid_spec=pltpu.PrefetchScalarGridSpec(
-            num_scalar_prefetch=1,
-            grid=(rows // chunk,),
-            in_specs=[
-                pl.BlockSpec(memory_space=pltpu.SMEM),
-                pl.BlockSpec((1, nodes), lambda i, place: (0, 0)),
-                pl.BlockSpec((chunk, nodes), lambda i, place: (i, 0)),
-            ],
-            out_specs=pl.BlockSpec((chunk, nodes), lambda i, place: (i, 0)),
-            scratch_shapes=[pltpu.VMEM((4, 16, nodes), F32)],
-        ),
+        out_shape=jax.ShapeDtypeStruct(pivot.shape, BF16),
+        in_specs=[scalars, scalars, vmem, vmem],
+        out_specs=vmem,
         compiler_params=pltpu.CompilerParams(vmem_limit_bytes=8 * MIB),
         cost_estimate=LIGHT,
         name="couple_here",
-    )(place, rate, node_class.reshape(1, nodes), pivot)
+    )(place, rate, weights, pivot)
 
 
 def turn_kernel(place_ref, coupled_ref, *refs):
@@ -381,14 +390,15 @@
         return pl.ds(pl.multiple_of(block * width, 128), count * width)
 
     prior_kernel(place_ref, shifted_ref, sigma_ref, row_ref)
-    far_ref[:, : 2 * width] = row_ref[:, at(2 - 2 * odd, 2)]
+    far_ref[:, :width] = row_ref[:, at(3 - 3 * odd)]
     near_ref[:, :width] = row_ref[:, at(3 - 3 * odd)]
+    near_ref[:, width : 2 * width] = row_ref[:, at(3 * odd)]
     for part in range(2):
 
         @pl.when(pl.program_id(0) == part)
         def _():
-            pack_rows(part, row_ref[:, at(3 * odd)], far_ref, 2 * width)
-            pack_rows(part, row_ref[:, at(2 - odd)], near_ref, width)
+            pack_rows(part, row_ref[:, at(3 * odd)], far_ref, width)
+            pack_rows(part, row_ref[:, at(2 - odd)], near_ref, 2 * width)
             pack_rows(part, row_ref[:, at(3 - 3 * odd)], last_ref, 0)
 
 
@@ -400,7 +410,7 @@
     spec = lambda quarters: pl.BlockSpec((chunk, quarters * width // 4), lambda i, place: (i, 0))
     return pl.pallas_call(
         parts_kernel,
-        out_shape=(out(16), out(11), out(7), out(3)),
+        out_shape=(out(16), out(7), out(11), out(3)),
         grid_spec=pltpu.PrefetchScalarGridSpec(
             num_scalar_prefetch=1,
             grid=(rows // chunk,),
@@ -412,7 +422,7 @@
                     (chunk, nodes), lambda i, place: (jnp.where(place[3] == 0, 0, i), 0)
                 ),
             ],
-            out_specs=(spec(16), spec(11), spec(7), spec(3)),
+            out_specs=(spec(16), spec(7), spec(11), spec(3)),
         ),
         compiler_params=pltpu.CompilerParams(vmem_limit_bytes=14 * MIB),
         cost_estimate=LIGHT,
@@ -430,17 +440,16 @@
         def at(block, count=1):
             return pl.ds(pl.multiple_of(block * width, 128), count * width)
 
-        near = 2 * (1 - odd)
         row = [turned(block, odd) for block in range(4)]
         out_ref[at(row[1]), :] = own[...]
-        out_ref[at(row[2]), at(row[3])] = near_two[:, :width]
-        out_ref[at(row[3]), at(row[2])] = near_two[:, :width].T
-        out_ref[at(row[0]), at(near, 2)] = far_zero[:, : 2 * width]
-        for step in range(2):
-            out_ref[at(near + step), at(row[0])] = far_zero[:, step * width : (1 + step) * width].T
+        pairs = ((2, 3, near_two, 0), (2, 0, near_two, width), (0, 3, far_zero, 0))
+        for first, second, ref, start in pairs:
+            value = ref[:, start : start + width]
+            out_ref[at(row[first]), at(row[second])] = value
+            out_ref[at(row[second]), at(row[first])] = value.T
         for block in (0, 2, 3):
             out_ref[at(row[block]), at(row[1])] = column[at(row[block]), :]
-        packed = ((0, far_zero, 2 * width), (2, near_two, width), (3, last_three, 0))
+        packed = ((0, far_zero, width), (2, near_two, 2 * width), (3, last_three, 0))
         for block, packed_ref, start in packed:
             for part in range(4):
                 rows = pl.ds(pl.multiple_of(row[block] * width + part * quarter, 128), quarter)
@@ -700,18 +709,19 @@
     shifted = passed_along(separator, "dom", -1)[0]
     p2 = moved(pivot, 2, 1)
     p0 = moved(pivot, 0, 1)
-    c1 = [couple(pivot, node_class, coupling_rate, part, 2) for part in range(2)]
+    weights = coupling(node_class)
+    c1 = [couple(pivot, weights, coupling_rate, part, 2) for part in range(2)]
     across = turn(place, 1, 0, c1[0], None)
     across = turn(place, 1, 1, c1[1], across)
 
     row, far, near, last = prior_parts(place, after(shifted, across), sigma)
     far_zero, near_two, last_three = moved(far, 0, 1), moved(near, 2, 1), moved(last, 3, 1)
 
-    c2 = couple_here(place, after(p2, last), node_class, coupling_rate)
+    c2 = couple_here(place, after(p2, last), weights, coupling_rate)
     across = turn(place, 2, 0, c2, across)
-    c0 = couple_here(place, after(p0, across), node_class, coupling_rate)
+    c0 = couple_here(place, after(p0, across), weights, coupling_rate)
     across = turn(place, 0, 0, c0, across)
-    column, h0_one, h2_one = own_column(place, after(row, last_three, near_two), c0, c2)
+    column, h0_one, h2_one = own_column(place, row, c0, c2)
     c3 = [
         moved(after(c1[0], last_three, near_two, across), 3, 1),
         moved(after(c1[1], far_zero, h2_one), 3, 1),
@@ -750,7 +760,7 @@
     shifted = passed_along(separator, "dom", -1)
     prior = jnp.where(step_index[0] == 0, shifted[0], sigma_next[0])
     pivot = inverse_pivot[0].astype(F32)
-    coupled = couple(inverse_pivot[0], node_class, coupling_rate)
+    coupled = couple(inverse_pivot[0], coupling(node_class), coupling_rate)
     rows = coupled.shape[0]
     half = jnp.dot(
         coupled,

time: 120 us -> 124 us (1.033); the launches traced: 120 us -> 122 us
  starting transfers between devices: 29.5 us -> 34.4 us
  waiting for transfers between devices: 53.8 us -> 51.4 us
  local copies, waits for them, and re-layouts: 2.39 us -> 0.79 us
    ppermute x13, starting transfers between devices: 27.5 us -> 32.3 us  [moved(): lax.ppermute(value, ('dom', 'col'), route(source, target, lax.axis_size('...]
    ppermute x13, waiting for transfers between devices: 40.9 us -> 39 us  [moved(): lax.ppermute(value, ('dom', 'col'), route(source, target, lax.axis_size('...]
    unnamed x10 -> x6, local copies, waits for them, and re-layouts: 2.3 us -> 0.71 us
    pallas_call x5 -> x6, Pallas kernels: 10.6 us -> 11.1 us  [the longest x2 3.75 us: couple(): pl.pallas_call(functools.partial(couple_kernel, part * rows), out_shape=j...]
where the time goes in v15:
time: 124 us; the launch traced here: 122 us
  waiting for transfers between devices  51.4 us (41%)
  starting transfers between devices  34.4 us (28%)
  Pallas kernels  31.9 us (26%)
  between operations  3.12 us (3%)
    ppermute x13, waiting for transfers between devices, moved(): lax.ppermute(value, ('dom', 'col'), route(source, target, lax.axis_size('...  39 us
    ppermute x13, starting transfers between devices, moved(): lax.ppermute(value, ('dom', 'col'), route(source, target, lax.axis_size('...  32.3 us
    ppermute x1, waiting for transfers between devices, passed_along(): lax.ppermute(value, axis, [(source, source + steps) for source in range(i...  12.4 us
    pallas_call x6, Pallas kernels, turn(): pl.pallas_call(turn_kernel, out_shape=jax.ShapeDtypeStruct((nodes, nodes)...  5.99 us
    pallas_call x7, Pallas kernels, multiply(): pl.pallas_call(functools.partial(multiply_kernel, first, count, len(lefts...  4.03 us
    pallas_call x2, Pallas kernels, couple(): pl.pallas_call(functools.partial(couple_kernel, part * rows), out_shape=j...  3.75 us
    pallas_call x2, Pallas kernels, couple_here(): pl.pallas_call(kernel, out_shape=jax.ShapeDtypeStruct(pivot.shape, BF16),...  3.23 us
    pallas_call x1, Pallas kernels, finish_last(): pl.pallas_call(last_kernel, out_shape=(jax.ShapeDtypeStruct((rows, nodes)...  2.63 us
  transfers between devices with their start and end apart: 14, of which 7 were waited for; matrix products, arithmetic and copies ran while one was open for 0% of the time, Pallas kernels for 24%

profile of v15, /device:TPU:1, one launch (start us, length us, event | category | flops | bytes accessed | tf_op | source)
XLA Modules:
  0.0 121.7 jit_solution(3444146637863911766)
XLA Ops:
  0.6 2.1 %collective-permute-start = (bf16[1,512,2048]{2,1,0:T(8,128)(2,1)}, bf16[1,512,2048]{2,1,0:T(8,128)(2,1)}, u32[]{:S(2)}, u32[]{:S(2)}) collective-permute-start(bf16[1,512,2048]{2,1,0:T(8,128)(2,1)} %param.8), channel_id=1, source_target_pairs={{4,0},{8,4},{12,8},{5,1},{9,5},{13,9},{6,2},{10,6},{14,10},{7,3},{... | collective-permute-start | bytes 6291464 | tf_op jit(solution)/shard_map/ppermute | solution.py:20
  2.7 2.0 %collective-permute-start.4 = (bf16[512,2048]{1,0:T(8,128)(2,1)}, bf16[512,2048]{1,0:T(8,128)(2,1)}, u32[]{:S(2)}, u32[]{:S(2)}) collective-permute-start(bf16[512,2048]{1,0:T(8,128)(2,1)} %bitcast.8), channel_id=1, source_target_pairs={{2,1},{5,6},{10,9},{13,14},{18,17},{21,22},{26,25},{29,30}} | collective-permute-start | bytes 6291464 | tf_op jit(solution)/shard_map/ppermute | solution.py:123
  4.8 2.0 %collective-permute-start.3 = (bf16[512,2048]{1,0:T(8,128)(2,1)}, bf16[512,2048]{1,0:T(8,128)(2,1)}, u32[]{:S(2)}, u32[]{:S(2)}) collective-permute-start(bf16[512,2048]{1,0:T(8,128)(2,1)} %bitcast.9), channel_id=1, source_target_pairs={{0,1},{7,6},{8,9},{15,14},{16,17},{23,22},{24,25},{31,30}} | collective-permute-start | bytes 6291464 | tf_op jit(solution)/shard_map/ppermute | solution.py:123
  9.5 1.8 %coupling.1.weight_ref.refs_1_ = bf16[8,512,256]{2,1,0:T(8,128)(2,1)S(1)} custom-call(s32[1,2048]{1,0:T(1,128)S(1)} %bitcast.16), custom_call_target="tpu_custom_call" | custom-call | flops 1048576 | bytes 65536 | tf_op jit(solution)/shard_map/coupling/pallas_call | solution.py:70
  11.3 1.9 %couple.3.coupled_ref.refs_1_ = bf16[256,2048]{1,0:T(8,128)(2,1)S(1)} custom-call(f32[1]{0:T(128)S(6)} %copy.21.rate_ref.refs_0_, bf16[8,512,256]{2,1,0:T(8,128)(2,1)S(1)} %coupling.1.weight_ref.refs_1_, bf16[512,2048]{1,0:T(8,128)(2,1)S(1)} %bitcast.10), custom_call_target="tpu_custom_call" | custom-call | flops 1048576 | bytes 65536 | tf_op jit(solution)/shard_map/couple/pallas_call | solution.py:99
  13.2 1.9 %couple.2.coupled_ref.refs_0_ = bf16[256,2048]{1,0:T(8,128)(2,1)S(1)} custom-call(f32[1]{0:T(128)S(6)} %copy.21.rate_ref.refs_0_, bf16[8,512,256]{2,1,0:T(8,128)(2,1)S(1)} %coupling.1.weight_ref.refs_1_, bf16[512,2048]{1,0:T(8,128)(2,1)S(1)} %bitcast.11), custom_call_target="tpu_custom_call" | custom-call | flops 1048576 | bytes 65536 | tf_op jit(solution)/shard_map/couple/pallas_call | solution.py:99
  16.9 12.4 %collective-permute-done = bf16[1,512,2048]{2,1,0:T(8,128)(2,1)} collective-permute-done((bf16[1,512,2048]{2,1,0:T(8,128)(2,1)}, bf16[1,512,2048]{2,1,0:T(8,128)(2,1)}, u32[]{:S(2)}, u32[]{:S(2)}) %collective-permute-start) | collective-permute-done | bytes 2097184 | tf_op jit(solution)/shard_map/ppermute | solution.py:20
  29.3 2.3 %prior_parts.1 = (bf16[512,2048]{1,0:T(8,128)(2,1)S(1)}, bf16[512,896]{1,0:T(8,128)(2,1)S(1)}, bf16[512,1408]{1,0:T(8,128)(2,1)S(1)}, bf16[512,384]{1,0:T(8,128)(2,1)S(1)}) custom-call(s32[5]{0:T(128)S(1)} %stack.16.place_ref, bf16[512,2048]{1,0:T(8,128)(2,1)} %bitcast.5.shifted_ref, bf16[512,2048]{1,0:T(8,128)(2,1)S(1)} %bitcast.14), custom_call_target="tpu_custom_call" | custom-call | flops 1048576 | bytes 65536 | tf_op jit(solution)/shard_map/prior_parts/pallas_call | solution.py:411
  33.1 5.3 %collective-permute-start.1 = (bf16[512,384]{1,0:T(8,128)(2,1)S(1)}, bf16[512,384]{1,0:T(8,128)(2,1)S(1)}, u32[]{:S(2)}, u32[]{:S(2)}) collective-permute-start(bf16[512,384]{1,0:T(8,128)(2,1)S(1)} %get-tuple-element.26), channel_id=1, source_target_pairs={{3,1},{4,6},{11,9},{12,14},{19,17},{20,22},{27,25},{28,30}} | collective-permute-start | bytes 1179656 | tf_op jit(solution)/shard_map/ppermute | solution.py:123
  38.5 1.6 %couple_here.2.coupled_ref.second_ref.left_ref = bf16[512,2048]{1,0:T(8,128)(2,1)S(1)} custom-call(s32[5]{0:T(128)S(1)} %stack.16.place_ref, f32[1]{0:T(128)S(6)} %copy.21.rate_ref.refs_0_, bf16[8,512,256]{2,1,0:T(8,128)(2,1)S(1)} %coupling.1.weight_ref.refs_1_, bf16[512,2048]{1,0:T(8,128)(2,1)} %collective-permute-done.4.refs_2_), custom_call_target="tpu_custom_call" | custom-call | flops 1048576 | bytes 65536 | tf_op jit(solution)/shard_map/couple_here/pallas_call | solution.py:133
  40.1 1.2 %turn.8.refs_0_ = bf16[2048,2048]{1,0:T(8,128)(2,1)S(1)} custom-call(s32[5]{0:T(128)S(1)} %stack.16.place_ref, bf16[512,2048]{1,0:T(8,128)(2,1)S(1)} %couple_here.2.coupled_ref.second_ref.left_ref, bf16[2048,2048]{1,0:T(8,128)(2,1)S(1)} %turn.7.refs_0_), custom_call_target="tpu_custom_call", output_to_operand_aliasing={{}: (2, {})} | custom-call | flops 1048576 | bytes 65536 | tf_op jit(solution)/shard_map/turn/pallas_call | solution.py:155
  41.3 1.6 %couple_here.3.coupled_ref.first_ref.left_ref = bf16[512,2048]{1,0:T(8,128)(2,1)S(1)} custom-call(s32[5]{0:T(128)S(1)} %stack.16.place_ref, f32[1]{0:T(128)S(6)} %copy.21.rate_ref.refs_0_, bf16[8,512,256]{2,1,0:T(8,128)(2,1)S(1)} %coupling.1.weight_ref.refs_1_, bf16[512,2048]{1,0:T(8,128)(2,1)} %collective-permute-done.3.refs_2_), custom_call_target="tpu_custom_call" | custom-call | flops 1048576 | bytes 65536 | tf_op jit(solution)/shard_map/couple_here/pallas_call | solution.py:133
  45.8 14.0 %collective-permute-start.5 = (bf16[256,2048]{1,0:T(8,128)(2,1)S(1)}, bf16[256,2048]{1,0:T(8,128)(2,1)S(1)}, u32[]{:S(2)}, u32[]{:S(2)}) collective-permute-start(bf16[256,2048]{1,0:T(8,128)(2,1)S(1)} %couple.2.coupled_ref.refs_0_), channel_id=1, source_target_pairs={{3,1},{4,6},{11,9},{12,14},{19,17},{20,22},{27,25},{28,30}} | collective-permute-start | bytes 3145736 | tf_op jit(solution)/shard_map/ppermute | solution.py:123
  59.9 1.4 %collective-permute-start.7 = (bf16[256,2048]{1,0:T(8,128)(2,1)S(1)}, bf16[256,2048]{1,0:T(8,128)(2,1)S(1)}, u32[]{:S(2)}, u32[]{:S(2)}) collective-permute-start(bf16[256,2048]{1,0:T(8,128)(2,1)S(1)} %couple.3.coupled_ref.refs_1_), channel_id=1, source_target_pairs={{3,1},{4,6},{11,9},{12,14},{19,17},{20,22},{27,25},{28,30}} | collective-permute-start | bytes 3145736 | tf_op jit(solution)/shard_map/ppermute | solution.py:123
  65.6 6.0 %collective-permute-done.5.refs_0_.coupled_ref = bf16[256,2048]{1,0:T(8,128)(2,1)S(1)} collective-permute-done((bf16[256,2048]{1,0:T(8,128)(2,1)S(1)}, bf16[256,2048]{1,0:T(8,128)(2,1)S(1)}, u32[]{:S(2)}, u32[]{:S(2)}) %collective-permute-start.5) | collective-permute-done | bytes 1048608 | tf_op jit(solution)/shard_map/ppermute | solution.py:123
  73.0 9.8 %collective-permute-done.7.coupled_ref.refs_0_ = bf16[256,2048]{1,0:T(8,128)(2,1)S(1)} collective-permute-done((bf16[256,2048]{1,0:T(8,128)(2,1)S(1)}, bf16[256,2048]{1,0:T(8,128)(2,1)S(1)}, u32[]{:S(2)}, u32[]{:S(2)}) %collective-permute-start.7) | collective-permute-done | bytes 1048608 | tf_op jit(solution)/shard_map/ppermute | solution.py:123
  86.3 1.3 %collective-permute-start.8 = (bf16[512,512]{1,0:T(8,128)(2,1)S(1)}, bf16[512,512]{1,0:T(8,128)(2,1)S(1)}, u32[]{:S(2)}, u32[]{:S(2)}) collective-permute-start(bf16[512,512]{1,0:T(8,128)(2,1)S(1)} %multiply.11), channel_id=1, source_target_pairs={{1,3},{6,4},{9,11},{14,12},{17,19},{22,20},{25,27},{30,28}} | collective-permute-start | bytes 1572872 | tf_op jit(solution)/shard_map/ppermute | solution.py:123
  88.1 1.3 %collective-permute-start.12 = (bf16[512,1408]{1,0:T(8,128)(2,1)S(1)}, bf16[512,1408]{1,0:T(8,128)(2,1)S(1)}, u32[]{:S(2)}, u32[]{:S(2)}) collective-permute-start(bf16[512,1408]{1,0:T(8,128)(2,1)S(1)} %product_rest.1.q31), channel_id=1, source_target_pairs={{1,3},{6,4},{9,11},{14,12},{17,19},{22,20},{25,27},{30,28}} | collective-permute-start | bytes 4325384 | tf_op jit(solution)/shard_map/ppermute | solution.py:123
  92.8 10.6 %collective-permute-done.8.q3_two = bf16[512,512]{1,0:T(8,128)(2,1)S(1)} collective-permute-done((bf16[512,512]{1,0:T(8,128)(2,1)S(1)}, bf16[512,512]{1,0:T(8,128)(2,1)S(1)}, u32[]{:S(2)}, u32[]{:S(2)}) %collective-permute-start.8) | collective-permute-done | bytes 524320 | tf_op jit(solution)/shard_map/ppermute | solution.py:123
  103.4 1.3 %collective-permute-start.11 = (bf16[512,512]{1,0:T(8,128)(2,1)S(1)}, bf16[512,512]{1,0:T(8,128)(2,1)S(1)}, u32[]{:S(2)}, u32[]{:S(2)}) collective-permute-start(bf16[512,512]{1,0:T(8,128)(2,1)S(1)} %collective-permute-done.8.q3_two), channel_id=1, source_target_pairs={{3,2},{4,5},{11,10},{12,13},{19,18},{20,21},{27,26},{28,29}} | collective-permute-start | bytes 1572872 | tf_op jit(solution)/shard_map/ppermute | solution.py:123
  104.7 2.6 %finish.1 = (bf16[512,2048]{1,0:T(8,128)(2,1)}, f32[1,512]{1,0:T(1,128)S(1)}) custom-call(s32[5]{0:T(128)S(1)} %tick.3.place_ref, bf16[512,2048]{1,0:T(8,128)(2,1)S(1)} %bitcast.12, bf16[512,2048]{1,0:T(8,128)(2,1)S(1)} %bitcast.15, bf16[512,1536]{1,0:T(8,128)(2,1)S(1)} %collective-permute-done.9.refs_0_.q0, ...), custom_call_target="tpu_custom_call" | custom-call | flops 14000000000 | bytes 65536 | tf_op jit(solution)/shard_map/finish/pallas_call | solution.py:577
  107.3 3.5 %collective-permute-done.11.q2_last = bf16[512,512]{1,0:T(8,128)(2,1)S(1)} collective-permute-done((bf16[512,512]{1,0:T(8,128)(2,1)S(1)}, bf16[512,512]{1,0:T(8,128)(2,1)S(1)}, u32[]{:S(2)}, u32[]{:S(2)}) %collective-permute-start.11) | collective-permute-done | bytes 524320 | tf_op jit(solution)/shard_map/ppermute | solution.py:123
  110.8 8.1 %collective-permute-done.12.q3 = bf16[512,1408]{1,0:T(8,128)(2,1)S(1)} collective-permute-done((bf16[512,1408]{1,0:T(8,128)(2,1)S(1)}, bf16[512,1408]{1,0:T(8,128)(2,1)S(1)}, u32[]{:S(2)}, u32[]{:S(2)}) %collective-permute-start.12) | collective-permute-done | bytes 1441824 | tf_op jit(solution)/shard_map/ppermute | solution.py:123
  118.9 2.6 %finish_last.1 = (bf16[512,2048]{1,0:T(8,128)(2,1)}, f32[1,512]{1,0:T(1,128)}) custom-call(s32[5]{0:T(128)S(1)} %stack.16.place_ref, bf16[512,2048]{1,0:T(8,128)(2,1)S(1)} %bitcast.13, bf16[512,512]{1,0:T(8,128)(2,1)S(1)} %collective-permute-done.11.q2_last, bf16[512,1408]{1,0:T(8,128)(2,1)S(1)} %collective-permute-done.12.q3, ...), custom_call_target="tpu_custom_call", output_to_operand_aliasing={{0}: (4, {})} | custom-call | flops 1048576 | bytes 65536 | tf_op jit(solution)/shard_map/finish_last/pallas_call | solution.py:682
  (40 shorter events, 19.9 us)
Async XLA Ops:
  0.6 10.7 %copy-start = (bf16[1,512,2048]{2,1,0:T(8,128)(2,1)S(1)}, bf16[1,512,2048]{2,1,0:T(8,128)(2,1)}, u32[]{:S(2)}) copy-start(bf16[1,512,2048]{2,1,0:T(8,128)(2,1)} %param.9) | copy-start | bytes 6291460
  0.6 28.7 %collective-permute-start = (bf16[1,512,2048]{2,1,0:T(8,128)(2,1)}, bf16[1,512,2048]{2,1,0:T(8,128)(2,1)}, u32[]{:S(2)}, u32[]{:S(2)}) collective-permute-start(bf16[1,512,2048]{2,1,0:T(8,128)(2,1)} %param.8), channel_id=1, source_target_pairs={{4,0},{8,4},{12,8},{5,1},{9,5},{13,9},{6,2},{10,6},{14,10},{7,3},{... | collective-permute-start | bytes 6291464 | tf_op jit(solution)/shard_map/ppermute | solution.py:20
  2.7 35.7 %collective-permute-start.4 = (bf16[512,2048]{1,0:T(8,128)(2,1)}, bf16[512,2048]{1,0:T(8,128)(2,1)}, u32[]{:S(2)}, u32[]{:S(2)}) collective-permute-start(bf16[512,2048]{1,0:T(8,128)(2,1)} %bitcast.8), channel_id=1, source_target_pairs={{2,1},{5,6},{10,9},{13,14},{18,17},{21,22},{26,25},{29,30}} | collective-permute-start | bytes 6291464 | tf_op jit(solution)/shard_map/ppermute | solution.py:123
  4.8 36.6 %collective-permute-start.3 = (bf16[512,2048]{1,0:T(8,128)(2,1)}, bf16[512,2048]{1,0:T(8,128)(2,1)}, u32[]{:S(2)}, u32[]{:S(2)}) collective-permute-start(bf16[512,2048]{1,0:T(8,128)(2,1)} %bitcast.9), channel_id=1, source_target_pairs={{0,1},{7,6},{8,9},{15,14},{16,17},{23,22},{24,25},{31,30}} | collective-permute-start | bytes 6291464 | tf_op jit(solution)/shard_map/ppermute | solution.py:123
  8.8 0.7 copy-start.2
  16.0 13.3 %copy-start.1 = (bf16[1,512,2048]{2,1,0:T(8,128)(2,1)S(1)}, bf16[1,512,2048]{2,1,0:T(8,128)(2,1)}, u32[]{:S(2)}) copy-start(bf16[1,512,2048]{2,1,0:T(8,128)(2,1)} %param.7) | copy-start | bytes 6291460
  31.6 14.2 %collective-permute-start.2 = (bf16[512,1408]{1,0:T(8,128)(2,1)S(1)}, bf16[512,1408]{1,0:T(8,128)(2,1)S(1)}, u32[]{:S(2)}, u32[]{:S(2)}) collective-permute-start(bf16[512,1408]{1,0:T(8,128)(2,1)S(1)} %get-tuple-element.27), channel_id=1, source_target_pairs={{2,1},{5,6},{10,9},{13,14},{18,17},{21,22},{26,25},{29,30}} | collective-permute-start | bytes 4325384 | tf_op jit(solution)/shard_map/ppermute | solution.py:123
  32.4 12.4 %collective-permute-start.6 = (bf16[512,896]{1,0:T(8,128)(2,1)S(1)}, bf16[512,896]{1,0:T(8,128)(2,1)S(1)}, u32[]{:S(2)}, u32[]{:S(2)}) collective-permute-start(bf16[512,896]{1,0:T(8,128)(2,1)S(1)} %get-tuple-element.33), channel_id=1, source_target_pairs={{0,1},{7,6},{8,9},{15,14},{16,17},{23,22},{24,25},{31,30}} | collective-permute-start | bytes 2752520 | tf_op jit(solution)/shard_map/ppermute | solution.py:123
  33.1 12.7 %collective-permute-start.1 = (bf16[512,384]{1,0:T(8,128)(2,1)S(1)}, bf16[512,384]{1,0:T(8,128)(2,1)S(1)}, u32[]{:S(2)}, u32[]{:S(2)}) collective-permute-start(bf16[512,384]{1,0:T(8,128)(2,1)S(1)} %get-tuple-element.26), channel_id=1, source_target_pairs={{3,1},{4,6},{11,9},{12,14},{19,17},{20,22},{27,25},{28,30}} | collective-permute-start | bytes 1179656 | tf_op jit(solution)/shard_map/ppermute | solution.py:123
  45.8 25.7 %collective-permute-start.5 = (bf16[256,2048]{1,0:T(8,128)(2,1)S(1)}, bf16[256,2048]{1,0:T(8,128)(2,1)S(1)}, u32[]{:S(2)}, u32[]{:S(2)}) collective-permute-start(bf16[256,2048]{1,0:T(8,128)(2,1)S(1)} %couple.2.coupled_ref.refs_0_), channel_id=1, source_target_pairs={{3,1},{4,6},{11,9},{12,14},{19,17},{20,22},{27,25},{28,30}} | collective-permute-start | bytes 3145736 | tf_op jit(solution)/shard_map/ppermute | solution.py:123
  59.9 22.9 %collective-permute-start.7 = (bf16[256,2048]{1,0:T(8,128)(2,1)S(1)}, bf16[256,2048]{1,0:T(8,128)(2,1)S(1)}, u32[]{:S(2)}, u32[]{:S(2)}) collective-permute-start(bf16[256,2048]{1,0:T(8,128)(2,1)S(1)} %couple.3.coupled_ref.refs_1_), channel_id=1, source_target_pairs={{3,1},{4,6},{11,9},{12,14},{19,17},{20,22},{27,25},{28,30}} | collective-permute-start | bytes 3145736 | tf_op jit(solution)/shard_map/ppermute | solution.py:123
  62.9 27.6 %collective-permute-start.9 = (bf16[512,1536]{1,0:T(8,128)(2,1)S(1)}, bf16[512,1536]{1,0:T(8,128)(2,1)S(1)}, u32[]{:S(2)}, u32[]{:S(2)}) collective-permute-start(bf16[512,1536]{1,0:T(8,128)(2,1)S(1)} %multiply.8.zero_ref.q01), channel_id=1, source_target_pairs={{1,0},{6,7},{9,8},{14,15},{17,16},{22,23},{25,24},{30,31}} | collective-permute-start | bytes 4718600 | tf_op jit(solution)/shard_map/ppermute | solution.py:123
  64.8 39.9 %collective-permute-start.13 = (bf16[512,1408]{1,0:T(8,128)(2,1)S(1)}, bf16[512,1408]{1,0:T(8,128)(2,1)S(1)}, u32[]{:S(2)}, u32[]{:S(2)}) collective-permute-start(bf16[512,1408]{1,0:T(8,128)(2,1)S(1)} %product_two.1.q21), channel_id=1, source_target_pairs={{1,2},{6,5},{9,10},{14,13},{17,18},{22,21},{25,26},{30,29}} | collective-permute-start | bytes 4325384 | tf_op jit(solution)/shard_map/ppermute | solution.py:123
  84.4 7.3 %collective-permute-start.10 = (bf16[512,512]{1,0:T(8,128)(2,1)S(1)}, bf16[512,512]{1,0:T(8,128)(2,1)S(1)}, u32[]{:S(2)}, u32[]{:S(2)}) collective-permute-start(bf16[512,512]{1,0:T(8,128)(2,1)S(1)} %multiply.9.zero_ref), channel_id=1, source_target_pairs={{1,0},{6,7},{9,8},{14,15},{17,16},{22,23},{25,24},{30,31}} | collective-permute-start | bytes 1572872 | tf_op jit(solution)/shard_map/ppermute | solution.py:123
  86.3 17.2 %collective-permute-start.8 = (bf16[512,512]{1,0:T(8,128)(2,1)S(1)}, bf16[512,512]{1,0:T(8,128)(2,1)S(1)}, u32[]{:S(2)}, u32[]{:S(2)}) collective-permute-start(bf16[512,512]{1,0:T(8,128)(2,1)S(1)} %multiply.11), channel_id=1, source_target_pairs={{1,3},{6,4},{9,11},{14,12},{17,19},{22,20},{25,27},{30,28}} | collective-permute-start | bytes 1572872 | tf_op jit(solution)/shard_map/ppermute | solution.py:123
  88.1 30.7 %collective-permute-start.12 = (bf16[512,1408]{1,0:T(8,128)(2,1)S(1)}, bf16[512,1408]{1,0:T(8,128)(2,1)S(1)}, u32[]{:S(2)}, u32[]{:S(2)}) collective-permute-start(bf16[512,1408]{1,0:T(8,128)(2,1)S(1)} %product_rest.1.q31), channel_id=1, source_target_pairs={{1,3},{6,4},{9,11},{14,12},{17,19},{22,20},{25,27},{30,28}} | collective-permute-start | bytes 4325384 | tf_op jit(solution)/shard_map/ppermute | solution.py:123
  103.4 7.4 %collective-permute-start.11 = (bf16[512,512]{1,0:T(8,128)(2,1)S(1)}, bf16[512,512]{1,0:T(8,128)(2,1)S(1)}, u32[]{:S(2)}, u32[]{:S(2)}) collective-permute-start(bf16[512,512]{1,0:T(8,128)(2,1)S(1)} %collective-permute-done.8.q3_two), channel_id=1, source_target_pairs={{3,2},{4,5},{11,10},{12,13},{19,18},{20,21},{27,26},{28,29}} | collective-permute-start | bytes 1572872 | tf_op jit(solution)/shard_map/ppermute | solution.py:123

commit v16 on v15

--- a/solution.py
+++ b/solution.py
@@ -390,15 +390,14 @@
         return pl.ds(pl.multiple_of(block * width, 128), count * width)
 
     prior_kernel(place_ref, shifted_ref, sigma_ref, row_ref)
-    far_ref[:, :width] = row_ref[:, at(3 - 3 * odd)]
+    far_ref[:, : 2 * width] = row_ref[:, at(2 - 2 * odd, 2)]
     near_ref[:, :width] = row_ref[:, at(3 - 3 * odd)]
-    near_ref[:, width : 2 * width] = row_ref[:, at(3 * odd)]
     for part in range(2):
 
         @pl.when(pl.program_id(0) == part)
         def _():
-            pack_rows(part, row_ref[:, at(3 * odd)], far_ref, width)
-            pack_rows(part, row_ref[:, at(2 - odd)], near_ref, 2 * width)
+            pack_rows(part, row_ref[:, at(3 * odd)], far_ref, 2 * width)
+            pack_rows(part, row_ref[:, at(2 - odd)], near_ref, width)
             pack_rows(part, row_ref[:, at(3 - 3 * odd)], last_ref, 0)
 
 
@@ -410,7 +409,7 @@
     spec = lambda quarters: pl.BlockSpec((chunk, quarters * width // 4), lambda i, place: (i, 0))
     return pl.pallas_call(
         parts_kernel,
-        out_shape=(out(16), out(7), out(11), out(3)),
+        out_shape=(out(16), out(11), out(7), out(3)),
         grid_spec=pltpu.PrefetchScalarGridSpec(
             num_scalar_prefetch=1,
             grid=(rows // chunk,),
@@ -422,7 +421,7 @@
                     (chunk, nodes), lambda i, place: (jnp.where(place[3] == 0, 0, i), 0)
                 ),
             ],
-            out_specs=(spec(16), spec(7), spec(11), spec(3)),
+            out_specs=(spec(16), spec(11), spec(7), spec(3)),
         ),
         compiler_params=pltpu.CompilerParams(vmem_limit_bytes=14 * MIB),
         cost_estimate=LIGHT,
@@ -440,16 +439,17 @@
         def at(block, count=1):
             return pl.ds(pl.multiple_of(block * width, 128), count * width)
 
+        near = 2 * (1 - odd)
         row = [turned(block, odd) for block in range(4)]
         out_ref[at(row[1]), :] = own[...]
-        pairs = ((2, 3, near_two, 0), (2, 0, near_two, width), (0, 3, far_zero, 0))
-        for first, second, ref, start in pairs:
-            value = ref[:, start : start + width]
-            out_ref[at(row[first]), at(row[second])] = value
-            out_ref[at(row[second]), at(row[first])] = value.T
+        out_ref[at(row[2]), at(row[3])] = near_two[:, :width]
+        out_ref[at(row[3]), at(row[2])] = near_two[:, :width].T
+        out_ref[at(row[0]), at(near, 2)] = far_zero[:, : 2 * width]
+        for step in range(2):
+            out_ref[at(near + step), at(row[0])] = far_zero[:, step * width : (1 + step) * width].T
         for block in (0, 2, 3):
             out_ref[at(row[block]), at(row[1])] = column[at(row[block]), :]
-        packed = ((0, far_zero, width), (2, near_two, 2 * width), (3, last_three, 0))
+        packed = ((0, far_zero, 2 * width), (2, near_two, width), (3, last_three, 0))
         for block, packed_ref, start in packed:
             for part in range(4):
                 rows = pl.ds(pl.multiple_of(row[block] * width + part * quarter, 128), quarter)
@@ -721,7 +721,7 @@
     across = turn(place, 2, 0, c2, across)
     c0 = couple_here(place, after(p0, across), weights, coupling_rate)
     across = turn(place, 0, 0, c0, across)
-    column, h0_one, h2_one = own_column(place, row, c0, c2)
+    column, h0_one, h2_one = own_column(place, after(row, last_three, near_two), c0, c2)
     c3 = [
         moved(after(c1[0], last_three, near_two, across), 3, 1),
         moved(after(c1[1], far_zero, h2_one), 3, 1),

time: 124 us -> 120 us (0.968); the launches traced: 122 us -> 120 us
  starting transfers between devices: 34.4 us -> 30.8 us
  waiting for transfers between devices: 51.4 us -> 53.6 us
    ppermute x13, starting transfers between devices: 32.3 us -> 28.7 us  [moved(): lax.ppermute(value, ('dom', 'col'), route(source, target, lax.axis_size('...]
    ppermute x13, waiting for transfers between devices: 39 us -> 41.2 us  [moved(): lax.ppermute(value, ('dom', 'col'), route(source, target, lax.axis_size('...]
where the time goes in v16:
time: 120 us
  waiting for transfers between devices  53.6 us (45%)
  Pallas kernels  31.8 us (26%)
  starting transfers between devices  30.8 us (26%)
  between operations  3.12 us (3%)
    ppermute x13, waiting for transfers between devices, moved(): lax.ppermute(value, ('dom', 'col'), route(source, target, lax.axis_size('...  41.2 us
    ppermute x13, starting transfers between devices, moved(): lax.ppermute(value, ('dom', 'col'), route(source, target, lax.axis_size('...  28.7 us
    ppermute x1, waiting for transfers between devices, passed_along(): lax.ppermute(value, axis, [(source, source + steps) for source in range(i...  12.4 us
    pallas_call x6, Pallas kernels, turn(): pl.pallas_call(turn_kernel, out_shape=jax.ShapeDtypeStruct((nodes, nodes)...  5.99 us
    pallas_call x7, Pallas kernels, multiply(): pl.pallas_call(functools.partial(multiply_kernel, first, count, len(lefts...  4.03 us
    pallas_call x2, Pallas kernels, couple(): pl.pallas_call(functools.partial(couple_kernel, part * rows), out_shape=j...  3.75 us
    pallas_call x2, Pallas kernels, couple_here(): pl.pallas_call(kernel, out_shape=jax.ShapeDtypeStruct(pivot.shape, BF16),...  3.23 us
    pallas_call x1, Pallas kernels, finish_last(): pl.pallas_call(last_kernel, out_shape=(jax.ShapeDtypeStruct((rows, nodes)...  2.63 us
  transfers between devices with their start and end apart: 14, of which 7 were waited for; matrix products, arithmetic and copies ran while one was open for 0% of the time, Pallas kernels for 24%

profile of v16, /device:TPU:1, one launch (start us, length us, event | category | flops | bytes accessed | tf_op | source)
XLA Modules:
  0.0 120.1 jit_solution(3112430286155941419)
XLA Ops:
  0.6 2.1 %collective-permute-start = (bf16[1,512,2048]{2,1,0:T(8,128)(2,1)}, bf16[1,512,2048]{2,1,0:T(8,128)(2,1)}, u32[]{:S(2)}, u32[]{:S(2)}) collective-permute-start(bf16[1,512,2048]{2,1,0:T(8,128)(2,1)} %param.8), channel_id=1, source_target_pairs={{4,0},{8,4},{12,8},{5,1},{9,5},{13,9},{6,2},{10,6},{14,10},{7,3},{... | collective-permute-start | bytes 6291464 | tf_op jit(solution)/shard_map/ppermute | solution.py:20
  2.7 2.0 %collective-permute-start.4 = (bf16[512,2048]{1,0:T(8,128)(2,1)}, bf16[512,2048]{1,0:T(8,128)(2,1)}, u32[]{:S(2)}, u32[]{:S(2)}) collective-permute-start(bf16[512,2048]{1,0:T(8,128)(2,1)} %bitcast.8), channel_id=1, source_target_pairs={{2,1},{5,6},{10,9},{13,14},{18,17},{21,22},{26,25},{29,30}} | collective-permute-start | bytes 6291464 | tf_op jit(solution)/shard_map/ppermute | solution.py:123
  4.8 2.0 %collective-permute-start.3 = (bf16[512,2048]{1,0:T(8,128)(2,1)}, bf16[512,2048]{1,0:T(8,128)(2,1)}, u32[]{:S(2)}, u32[]{:S(2)}) collective-permute-start(bf16[512,2048]{1,0:T(8,128)(2,1)} %bitcast.9), channel_id=1, source_target_pairs={{0,1},{7,6},{8,9},{15,14},{16,17},{23,22},{24,25},{31,30}} | collective-permute-start | bytes 6291464 | tf_op jit(solution)/shard_map/ppermute | solution.py:123
  9.5 1.8 %coupling.1.weight_ref.refs_1_ = bf16[8,512,256]{2,1,0:T(8,128)(2,1)S(1)} custom-call(s32[1,2048]{1,0:T(1,128)S(1)} %bitcast.16), custom_call_target="tpu_custom_call" | custom-call | flops 1048576 | bytes 65536 | tf_op jit(solution)/shard_map/coupling/pallas_call | solution.py:70
  11.3 1.9 %couple.3.coupled_ref.refs_1_ = bf16[256,2048]{1,0:T(8,128)(2,1)S(1)} custom-call(f32[1]{0:T(128)S(6)} %copy.21.rate_ref.refs_0_, bf16[8,512,256]{2,1,0:T(8,128)(2,1)S(1)} %coupling.1.weight_ref.refs_1_, bf16[512,2048]{1,0:T(8,128)(2,1)S(1)} %bitcast.10), custom_call_target="tpu_custom_call" | custom-call | flops 1048576 | bytes 65536 | tf_op jit(solution)/shard_map/couple/pallas_call | solution.py:99
  13.2 1.9 %couple.2.coupled_ref.refs_0_ = bf16[256,2048]{1,0:T(8,128)(2,1)S(1)} custom-call(f32[1]{0:T(128)S(6)} %copy.21.rate_ref.refs_0_, bf16[8,512,256]{2,1,0:T(8,128)(2,1)S(1)} %coupling.1.weight_ref.refs_1_, bf16[512,2048]{1,0:T(8,128)(2,1)S(1)} %bitcast.11), custom_call_target="tpu_custom_call" | custom-call | flops 1048576 | bytes 65536 | tf_op jit(solution)/shard_map/couple/pallas_call | solution.py:99
  16.9 12.4 %collective-permute-done = bf16[1,512,2048]{2,1,0:T(8,128)(2,1)} collective-permute-done((bf16[1,512,2048]{2,1,0:T(8,128)(2,1)}, bf16[1,512,2048]{2,1,0:T(8,128)(2,1)}, u32[]{:S(2)}, u32[]{:S(2)}) %collective-permute-start) | collective-permute-done | bytes 2097184 | tf_op jit(solution)/shard_map/ppermute | solution.py:20
  29.3 2.2 %prior_parts.1 = (bf16[512,2048]{1,0:T(8,128)(2,1)S(1)}, bf16[512,1408]{1,0:T(8,128)(2,1)S(1)}, bf16[512,896]{1,0:T(8,128)(2,1)S(1)}, bf16[512,384]{1,0:T(8,128)(2,1)S(1)}) custom-call(s32[5]{0:T(128)S(1)} %stack.16.place_ref, bf16[512,2048]{1,0:T(8,128)(2,1)} %bitcast.5.shifted_ref, bf16[512,2048]{1,0:T(8,128)(2,1)S(1)} %bitcast.14), custom_call_target="tpu_custom_call" | custom-call | flops 1048576 | bytes 65536 | tf_op jit(solution)/shard_map/prior_parts/pallas_call | solution.py:410
  33.0 5.3 %collective-permute-start.1 = (bf16[512,384]{1,0:T(8,128)(2,1)S(1)}, bf16[512,384]{1,0:T(8,128)(2,1)S(1)}, u32[]{:S(2)}, u32[]{:S(2)}) collective-permute-start(bf16[512,384]{1,0:T(8,128)(2,1)S(1)} %get-tuple-element.27), channel_id=1, source_target_pairs={{3,1},{4,6},{11,9},{12,14},{19,17},{20,22},{27,25},{28,30}} | collective-permute-start | bytes 1179656 | tf_op jit(solution)/shard_map/ppermute | solution.py:123
  38.4 1.6 %couple_here.2.coupled_ref.second_ref.left_ref = bf16[512,2048]{1,0:T(8,128)(2,1)S(1)} custom-call(s32[5]{0:T(128)S(1)} %stack.16.place_ref, f32[1]{0:T(128)S(6)} %copy.21.rate_ref.refs_0_, bf16[8,512,256]{2,1,0:T(8,128)(2,1)S(1)} %coupling.1.weight_ref.refs_1_, bf16[512,2048]{1,0:T(8,128)(2,1)} %collective-permute-done.4.refs_2_), custom_call_target="tpu_custom_call" | custom-call | flops 1048576 | bytes 65536 | tf_op jit(solution)/shard_map/couple_here/pallas_call | solution.py:133
  41.2 1.6 %couple_here.3.coupled_ref.first_ref.left_ref = bf16[512,2048]{1,0:T(8,128)(2,1)S(1)} custom-call(s32[5]{0:T(128)S(1)} %stack.16.place_ref, f32[1]{0:T(128)S(6)} %copy.21.rate_ref.refs_0_, bf16[8,512,256]{2,1,0:T(8,128)(2,1)S(1)} %coupling.1.weight_ref.refs_1_, bf16[512,2048]{1,0:T(8,128)(2,1)} %collective-permute-done.3.refs_2_), custom_call_target="tpu_custom_call" | custom-call | flops 1048576 | bytes 65536 | tf_op jit(solution)/shard_map/couple_here/pallas_call | solution.py:133
  44.1 3.2 %collective-permute-done.1.last_three = bf16[512,384]{1,0:T(8,128)(2,1)S(1)} collective-permute-done((bf16[512,384]{1,0:T(8,128)(2,1)S(1)}, bf16[512,384]{1,0:T(8,128)(2,1)S(1)}, u32[]{:S(2)}, u32[]{:S(2)}) %collective-permute-start.1) | collective-permute-done | bytes 393248 | tf_op jit(solution)/shard_map/ppermute | solution.py:123
  47.3 8.1 %collective-permute-start.5 = (bf16[256,2048]{1,0:T(8,128)(2,1)S(1)}, bf16[256,2048]{1,0:T(8,128)(2,1)S(1)}, u32[]{:S(2)}, u32[]{:S(2)}) collective-permute-start(bf16[256,2048]{1,0:T(8,128)(2,1)S(1)} %couple.2.coupled_ref.refs_0_), channel_id=1, source_target_pairs={{3,1},{4,6},{11,9},{12,14},{19,17},{20,22},{27,25},{28,30}} | collective-permute-start | bytes 3145736 | tf_op jit(solution)/shard_map/ppermute | solution.py:123
  56.0 3.7 %collective-permute-start.7 = (bf16[256,2048]{1,0:T(8,128)(2,1)S(1)}, bf16[256,2048]{1,0:T(8,128)(2,1)S(1)}, u32[]{:S(2)}, u32[]{:S(2)}) collective-permute-start(bf16[256,2048]{1,0:T(8,128)(2,1)S(1)} %couple.3.coupled_ref.refs_1_), channel_id=1, source_target_pairs={{3,1},{4,6},{11,9},{12,14},{19,17},{20,22},{27,25},{28,30}} | collective-permute-start | bytes 3145736 | tf_op jit(solution)/shard_map/ppermute | solution.py:123
  64.0 3.1 %collective-permute-done.5.refs_0_.coupled_ref = bf16[256,2048]{1,0:T(8,128)(2,1)S(1)} collective-permute-done((bf16[256,2048]{1,0:T(8,128)(2,1)S(1)}, bf16[256,2048]{1,0:T(8,128)(2,1)S(1)}, u32[]{:S(2)}, u32[]{:S(2)}) %collective-permute-start.5) | collective-permute-done | bytes 1048608 | tf_op jit(solution)/shard_map/ppermute | solution.py:123
  68.6 9.8 %collective-permute-done.7.coupled_ref.refs_0_ = bf16[256,2048]{1,0:T(8,128)(2,1)S(1)} collective-permute-done((bf16[256,2048]{1,0:T(8,128)(2,1)S(1)}, bf16[256,2048]{1,0:T(8,128)(2,1)S(1)}, u32[]{:S(2)}, u32[]{:S(2)}) %collective-permute-start.7) | collective-permute-done | bytes 1048608 | tf_op jit(solution)/shard_map/ppermute | solution.py:123
  81.8 1.3 %collective-permute-start.8 = (bf16[512,512]{1,0:T(8,128)(2,1)S(1)}, bf16[512,512]{1,0:T(8,128)(2,1)S(1)}, u32[]{:S(2)}, u32[]{:S(2)}) collective-permute-start(bf16[512,512]{1,0:T(8,128)(2,1)S(1)} %multiply.11), channel_id=1, source_target_pairs={{1,3},{6,4},{9,11},{14,12},{17,19},{22,20},{25,27},{30,28}} | collective-permute-start | bytes 1572872 | tf_op jit(solution)/shard_map/ppermute | solution.py:123
  83.7 1.3 %collective-permute-start.12 = (bf16[512,1408]{1,0:T(8,128)(2,1)S(1)}, bf16[512,1408]{1,0:T(8,128)(2,1)S(1)}, u32[]{:S(2)}, u32[]{:S(2)}) collective-permute-start(bf16[512,1408]{1,0:T(8,128)(2,1)S(1)} %product_rest.1.q31), channel_id=1, source_target_pairs={{1,3},{6,4},{9,11},{14,12},{17,19},{22,20},{25,27},{30,28}} | collective-permute-start | bytes 4325384 | tf_op jit(solution)/shard_map/ppermute | solution.py:123
  88.4 13.5 %collective-permute-done.8.q3_two = bf16[512,512]{1,0:T(8,128)(2,1)S(1)} collective-permute-done((bf16[512,512]{1,0:T(8,128)(2,1)S(1)}, bf16[512,512]{1,0:T(8,128)(2,1)S(1)}, u32[]{:S(2)}, u32[]{:S(2)}) %collective-permute-start.8) | collective-permute-done | bytes 524320 | tf_op jit(solution)/shard_map/ppermute | solution.py:123
  101.9 1.3 %collective-permute-start.11 = (bf16[512,512]{1,0:T(8,128)(2,1)S(1)}, bf16[512,512]{1,0:T(8,128)(2,1)S(1)}, u32[]{:S(2)}, u32[]{:S(2)}) collective-permute-start(bf16[512,512]{1,0:T(8,128)(2,1)S(1)} %collective-permute-done.8.q3_two), channel_id=1, source_target_pairs={{3,2},{4,5},{11,10},{12,13},{19,18},{20,21},{27,26},{28,29}} | collective-permute-start | bytes 1572872 | tf_op jit(solution)/shard_map/ppermute | solution.py:123
  103.2 2.6 %finish.1 = (bf16[512,2048]{1,0:T(8,128)(2,1)}, f32[1,512]{1,0:T(1,128)S(1)}) custom-call(s32[5]{0:T(128)S(1)} %tick.3.place_ref, bf16[512,2048]{1,0:T(8,128)(2,1)S(1)} %bitcast.12, bf16[512,2048]{1,0:T(8,128)(2,1)S(1)} %bitcast.15, bf16[512,1536]{1,0:T(8,128)(2,1)S(1)} %collective-permute-done.9.refs_0_.q0, ...), custom_call_target="tpu_custom_call" | custom-call | flops 14000000000 | bytes 65536 | tf_op jit(solution)/shard_map/finish/pallas_call | solution.py:577
  105.8 3.5 %collective-permute-done.11.q2_last = bf16[512,512]{1,0:T(8,128)(2,1)S(1)} collective-permute-done((bf16[512,512]{1,0:T(8,128)(2,1)S(1)}, bf16[512,512]{1,0:T(8,128)(2,1)S(1)}, u32[]{:S(2)}, u32[]{:S(2)}) %collective-permute-start.11) | collective-permute-done | bytes 524320 | tf_op jit(solution)/shard_map/ppermute | solution.py:123
  109.3 8.1 %collective-permute-done.12.q3 = bf16[512,1408]{1,0:T(8,128)(2,1)S(1)} collective-permute-done((bf16[512,1408]{1,0:T(8,128)(2,1)S(1)}, bf16[512,1408]{1,0:T(8,128)(2,1)S(1)}, u32[]{:S(2)}, u32[]{:S(2)}) %collective-permute-start.12) | collective-permute-done | bytes 1441824 | tf_op jit(solution)/shard_map/ppermute | solution.py:123
  117.4 2.6 %finish_last.1 = (bf16[512,2048]{1,0:T(8,128)(2,1)}, f32[1,512]{1,0:T(1,128)}) custom-call(s32[5]{0:T(128)S(1)} %stack.16.place_ref, bf16[512,2048]{1,0:T(8,128)(2,1)S(1)} %bitcast.13, bf16[512,512]{1,0:T(8,128)(2,1)S(1)} %collective-permute-done.11.q2_last, bf16[512,1408]{1,0:T(8,128)(2,1)S(1)} %collective-permute-done.12.q3, ...), custom_call_target="tpu_custom_call", output_to_operand_aliasing={{0}: (4, {})} | custom-call | flops 1048576 | bytes 65536 | tf_op jit(solution)/shard_map/finish_last/pallas_call | solution.py:682
  (40 shorter events, 20.1 us)
Async XLA Ops:
  0.6 10.7 %copy-start = (bf16[1,512,2048]{2,1,0:T(8,128)(2,1)S(1)}, bf16[1,512,2048]{2,1,0:T(8,128)(2,1)}, u32[]{:S(2)}) copy-start(bf16[1,512,2048]{2,1,0:T(8,128)(2,1)} %param.9) | copy-start | bytes 6291460
  0.6 28.7 %collective-permute-start = (bf16[1,512,2048]{2,1,0:T(8,128)(2,1)}, bf16[1,512,2048]{2,1,0:T(8,128)(2,1)}, u32[]{:S(2)}, u32[]{:S(2)}) collective-permute-start(bf16[1,512,2048]{2,1,0:T(8,128)(2,1)} %param.8), channel_id=1, source_target_pairs={{4,0},{8,4},{12,8},{5,1},{9,5},{13,9},{6,2},{10,6},{14,10},{7,3},{... | collective-permute-start | bytes 6291464 | tf_op jit(solution)/shard_map/ppermute | solution.py:20
  2.7 35.6 %collective-permute-start.4 = (bf16[512,2048]{1,0:T(8,128)(2,1)}, bf16[512,2048]{1,0:T(8,128)(2,1)}, u32[]{:S(2)}, u32[]{:S(2)}) collective-permute-start(bf16[512,2048]{1,0:T(8,128)(2,1)} %bitcast.8), channel_id=1, source_target_pairs={{2,1},{5,6},{10,9},{13,14},{18,17},{21,22},{26,25},{29,30}} | collective-permute-start | bytes 6291464 | tf_op jit(solution)/shard_map/ppermute | solution.py:123
  4.8 36.4 %collective-permute-start.3 = (bf16[512,2048]{1,0:T(8,128)(2,1)}, bf16[512,2048]{1,0:T(8,128)(2,1)}, u32[]{:S(2)}, u32[]{:S(2)}) collective-permute-start(bf16[512,2048]{1,0:T(8,128)(2,1)} %bitcast.9), channel_id=1, source_target_pairs={{0,1},{7,6},{8,9},{15,14},{16,17},{23,22},{24,25},{31,30}} | collective-permute-start | bytes 6291464 | tf_op jit(solution)/shard_map/ppermute | solution.py:123
  8.8 0.7 copy-start.2
  16.0 13.3 %copy-start.1 = (bf16[1,512,2048]{2,1,0:T(8,128)(2,1)S(1)}, bf16[1,512,2048]{2,1,0:T(8,128)(2,1)}, u32[]{:S(2)}) copy-start(bf16[1,512,2048]{2,1,0:T(8,128)(2,1)} %param.7) | copy-start | bytes 6291460
  31.5 24.5 %collective-permute-start.6 = (bf16[512,1408]{1,0:T(8,128)(2,1)S(1)}, bf16[512,1408]{1,0:T(8,128)(2,1)S(1)}, u32[]{:S(2)}, u32[]{:S(2)}) collective-permute-start(bf16[512,1408]{1,0:T(8,128)(2,1)S(1)} %get-tuple-element.35), channel_id=1, source_target_pairs={{0,1},{7,6},{8,9},{15,14},{16,17},{23,22},{24,25},{31,30}} | collective-permute-start | bytes 4325384 | tf_op jit(solution)/shard_map/ppermute | solution.py:123
  32.3 15.0 %collective-permute-start.2 = (bf16[512,896]{1,0:T(8,128)(2,1)S(1)}, bf16[512,896]{1,0:T(8,128)(2,1)S(1)}, u32[]{:S(2)}, u32[]{:S(2)}) collective-permute-start(bf16[512,896]{1,0:T(8,128)(2,1)S(1)} %get-tuple-element.28), channel_id=1, source_target_pairs={{2,1},{5,6},{10,9},{13,14},{18,17},{21,22},{26,25},{29,30}} | collective-permute-start | bytes 2752520 | tf_op jit(solution)/shard_map/ppermute | solution.py:123
  33.0 14.3 %collective-permute-start.1 = (bf16[512,384]{1,0:T(8,128)(2,1)S(1)}, bf16[512,384]{1,0:T(8,128)(2,1)S(1)}, u32[]{:S(2)}, u32[]{:S(2)}) collective-permute-start(bf16[512,384]{1,0:T(8,128)(2,1)S(1)} %get-tuple-element.27), channel_id=1, source_target_pairs={{3,1},{4,6},{11,9},{12,14},{19,17},{20,22},{27,25},{28,30}} | collective-permute-start | bytes 1179656 | tf_op jit(solution)/shard_map/ppermute | solution.py:123
  47.3 19.8 %collective-permute-start.5 = (bf16[256,2048]{1,0:T(8,128)(2,1)S(1)}, bf16[256,2048]{1,0:T(8,128)(2,1)S(1)}, u32[]{:S(2)}, u32[]{:S(2)}) collective-permute-start(bf16[256,2048]{1,0:T(8,128)(2,1)S(1)} %couple.2.coupled_ref.refs_0_), channel_id=1, source_target_pairs={{3,1},{4,6},{11,9},{12,14},{19,17},{20,22},{27,25},{28,30}} | collective-permute-start | bytes 3145736 | tf_op jit(solution)/shard_map/ppermute | solution.py:123
  56.0 22.4 %collective-permute-start.7 = (bf16[256,2048]{1,0:T(8,128)(2,1)S(1)}, bf16[256,2048]{1,0:T(8,128)(2,1)S(1)}, u32[]{:S(2)}, u32[]{:S(2)}) collective-permute-start(bf16[256,2048]{1,0:T(8,128)(2,1)S(1)} %couple.3.coupled_ref.refs_1_), channel_id=1, source_target_pairs={{3,1},{4,6},{11,9},{12,14},{19,17},{20,22},{27,25},{28,30}} | collective-permute-start | bytes 3145736 | tf_op jit(solution)/shard_map/ppermute | solution.py:123
  61.4 24.7 %collective-permute-start.9 = (bf16[512,1536]{1,0:T(8,128)(2,1)S(1)}, bf16[512,1536]{1,0:T(8,128)(2,1)S(1)}, u32[]{:S(2)}, u32[]{:S(2)}) collective-permute-start(bf16[512,1536]{1,0:T(8,128)(2,1)S(1)} %multiply.8.zero_ref.q01), channel_id=1, source_target_pairs={{1,0},{6,7},{9,8},{14,15},{17,16},{22,23},{25,24},{30,31}} | collective-permute-start | bytes 4718600 | tf_op jit(solution)/shard_map/ppermute | solution.py:123
  63.3 39.9 %collective-permute-start.13 = (bf16[512,1408]{1,0:T(8,128)(2,1)S(1)}, bf16[512,1408]{1,0:T(8,128)(2,1)S(1)}, u32[]{:S(2)}, u32[]{:S(2)}) collective-permute-start(bf16[512,1408]{1,0:T(8,128)(2,1)S(1)} %product_two.1.q21), channel_id=1, source_target_pairs={{1,2},{6,5},{9,10},{14,13},{17,18},{22,21},{25,26},{30,29}} | collective-permute-start | bytes 4325384 | tf_op jit(solution)/shard_map/ppermute | solution.py:123
  80.0 7.3 %collective-permute-start.10 = (bf16[512,512]{1,0:T(8,128)(2,1)S(1)}, bf16[512,512]{1,0:T(8,128)(2,1)S(1)}, u32[]{:S(2)}, u32[]{:S(2)}) collective-permute-start(bf16[512,512]{1,0:T(8,128)(2,1)S(1)} %multiply.9.zero_ref), channel_id=1, source_target_pairs={{1,0},{6,7},{9,8},{14,15},{17,16},{22,23},{25,24},{30,31}} | collective-permute-start | bytes 1572872 | tf_op jit(solution)/shard_map/ppermute | solution.py:123
  81.8 20.1 %collective-permute-start.8 = (bf16[512,512]{1,0:T(8,128)(2,1)S(1)}, bf16[512,512]{1,0:T(8,128)(2,1)S(1)}, u32[]{:S(2)}, u32[]{:S(2)}) collective-permute-start(bf16[512,512]{1,0:T(8,128)(2,1)S(1)} %multiply.11), channel_id=1, source_target_pairs={{1,3},{6,4},{9,11},{14,12},{17,19},{22,20},{25,27},{30,28}} | collective-permute-start | bytes 1572872 | tf_op jit(solution)/shard_map/ppermute | solution.py:123
  83.7 33.7 %collective-permute-start.12 = (bf16[512,1408]{1,0:T(8,128)(2,1)S(1)}, bf16[512,1408]{1,0:T(8,128)(2,1)S(1)}, u32[]{:S(2)}, u32[]{:S(2)}) collective-permute-start(bf16[512,1408]{1,0:T(8,128)(2,1)S(1)} %product_rest.1.q31), channel_id=1, source_target_pairs={{1,3},{6,4},{9,11},{14,12},{17,19},{22,20},{25,27},{30,28}} | collective-permute-start | bytes 4325384 | tf_op jit(solution)/shard_map/ppermute | solution.py:123
  101.9 7.4 %collective-permute-start.11 = (bf16[512,512]{1,0:T(8,128)(2,1)S(1)}, bf16[512,512]{1,0:T(8,128)(2,1)S(1)}, u32[]{:S(2)}, u32[]{:S(2)}) collective-permute-start(bf16[512,512]{1,0:T(8,128)(2,1)S(1)} %collective-permute-done.8.q3_two), channel_id=1, source_target_pairs={{3,2},{4,5},{11,10},{12,13},{19,18},{20,21},{27,26},{28,29}} | collective-permute-start | bytes 1572872 | tf_op jit(solution)/shard_map/ppermute | solution.py:123

commit v17 on v16

--- a/solution.py
+++ b/solution.py
@@ -311,7 +311,7 @@
     )(place, own, first, second)
 
 
-def rest_kernel(place_ref, upper_ref, lower_ref, right_ref, zero_ref, out_ref):
+def rest_kernel(place_ref, upper_ref, lower_ref, right_ref, zero_ref, out_ref, last_ref):
     odd = place_ref[0]
     width = zero_ref.shape[1]
     half = width // 2
@@ -328,7 +328,7 @@
         for part, left_ref in enumerate((upper_ref, lower_ref)):
             rows = pl.ds(part * half, half)
             out_ref[rows, other] = product(left_ref, 1 + odd)
-            pack_rows(part, product(left_ref, 3 - 3 * odd), out_ref.at[rows], 2 * width)
+            pack_rows(part, product(left_ref, 3 - 3 * odd), last_ref.at[rows], 0)
 
 
 def product_rest(place, halves, across, zero):
@@ -336,9 +336,12 @@
     vmem = pl.BlockSpec(memory_space=pltpu.VMEM)
     return pl.pallas_call(
         rest_kernel,
-        out_shape=jax.ShapeDtypeStruct((rows, 11 * width // 4), BF16),
+        out_shape=(
+            jax.ShapeDtypeStruct((rows, 2 * width), BF16),
+            jax.ShapeDtypeStruct((rows, 3 * width // 4), BF16),
+        ),
         in_specs=[pl.BlockSpec(memory_space=pltpu.SMEM)] + [vmem] * 4,
-        out_specs=vmem,
+        out_specs=(vmem, vmem),
         compiler_params=pltpu.CompilerParams(vmem_limit_bytes=6 * MIB),
         cost_estimate=LIGHT,
         name="product_rest",
@@ -608,62 +611,56 @@
     )(place, pivot, sigma, *received, *kept)
 
 
-def last_kernel(place_ref, pivot_ref, q2_last, q3, old_ref, old_var_ref, out_ref, var_ref, sum_ref, sems):
+def add_in_place(pivot_ref, out_ref, sum_ref, sems, column, product):
+    chunk = pivot_ref.shape[0] // 4
+    copies = []
+    for part in range(4):
+        here = pl.ds(part * chunk, chunk)
+        value = pivot_ref[here, column].astype(F32) + product(part, here).astype(F32)
+        sum_ref[here, :] = value.astype(BF16)
+        copies.append(
+            pltpu.make_async_copy(sum_ref.at[here], out_ref.at[here, column], sems.at[part])
+        )
+        copies[-1].start()
+    for copy in copies:
+        copy.wait()
+
+
+def other_kernel(place_ref, pivot_ref, q3_other, old_ref, out_ref, sum_ref, sems):
+    width = pivot_ref.shape[1] // 4
+    column = pl.ds(pl.multiple_of(2 * place_ref[0] * width, 128), 2 * width)
+
+    @pl.when((place_ref[4] != 0) & (place_ref[1] == 3))
+    def _():
+        add_in_place(
+            pivot_ref, out_ref, sum_ref, sems, column, lambda part, here: q3_other[here, :]
+        )
+
+
+def last_kernel(
+    place_ref, pivot_ref, q2_last, q3_last, old_ref, old_var_ref, out_ref, var_ref, sum_ref, sems
+):
     rows, nodes = pivot_ref.shape
     width = nodes // 4
-    chunk = 128
-    odd, place = place_ref[0], place_ref[1]
+    chunk = rows // 4
     active = place_ref[4] != 0
-
-    def at(block, count=1):
-        return pl.ds(pl.multiple_of(block * width, 128), count * width)
-
-    def copies(part, pieces):
-        here = pl.ds(part * chunk, chunk)
-        return [
-            pltpu.make_async_copy(
-                sum_ref.at[here, source], out_ref.at[here, target], sems.at[which, part]
-            )
-            for which, (source, target, _) in enumerate(pieces)
-        ]
-
-    def write(pieces):
-        for part in range(4):
-            here = pl.ds(part * chunk, chunk)
-            for source, target, product in pieces:
-                value = pivot_ref[here, target].astype(F32) + product(part, here).astype(F32)
-                sum_ref[here, source] = value.astype(BF16)
-            for copy in copies(part, pieces):
-                copy.start()
-        for part in range(4):
-            for copy in copies(part, pieces):
-                copy.wait()
-
+    column = pl.ds(pl.multiple_of(turned(3, place_ref[0]) * width, 128), width)
+    add = functools.partial(add_in_place, pivot_ref, out_ref, sum_ref, sems, column)
     var_ref[...] = old_var_ref[...]
 
-    @pl.when(active & (place == 2))
-    def _():
-        write([(pl.ds(0, width), at(3 - 3 * odd), lambda part, here: q2_last[:, here].T)])
-
-    @pl.when(active & (place == 3))
-    def _():
-        both, last = pl.ds(0, 2 * width), pl.ds(2 * width, width)
+    @pl.when(active & (place_ref[1] == 2))
+    def _():
+        add(lambda part, here: q2_last[:, here].T)
+
+    @pl.when(active & (place_ref[1] == 3))
+    def _():
+        add(lambda part, here: jnp.concatenate(unpacked_rows(part, q3_last, 0), axis=1))
         for start in range(0, rows, chunk):
             here = pl.ds(start, chunk)
             own = pl.ds(pl.multiple_of(place_ref[2] * width + start, 128), chunk)
             value = pivot_ref[here, own].astype(F32)
-            value = value + q3[here, pl.ds(2 * width + start % (2 * chunk), chunk)].astype(F32)
+            value = value + q3_last[here, pl.ds(start % (2 * chunk), chunk)].astype(F32)
             var_ref[:, here] = diagonal_of(chunk)(value)
-        write(
-            [
-                (both, at(2 * odd, 2), lambda part, here: q3[here, both]),
-                (
-                    last,
-                    at(3 - 3 * odd),
-                    lambda part, here: jnp.concatenate(unpacked_rows(part, q3, 2 * width), axis=1),
-                ),
-            ]
-        )
 
 
 def diagonal_of(rows):
@@ -674,9 +671,25 @@
     return lambda value: jnp.sum(jnp.where(on_diagonal, value, 0.0), axis=0, keepdims=True)
 
 
-def finish_last(place, pivot, q2_last, q3, covariance, variances):
+def finish_other(place, pivot, q3_other, covariance):
     rows, nodes = pivot.shape
-    width = nodes // 4
+    vmem = pl.BlockSpec(memory_space=pltpu.VMEM)
+    anywhere = pl.BlockSpec(memory_space=pl.ANY)
+    return pl.pallas_call(
+        other_kernel,
+        out_shape=jax.ShapeDtypeStruct((rows, nodes), BF16),
+        in_specs=[pl.BlockSpec(memory_space=pltpu.SMEM), vmem, vmem, anywhere],
+        out_specs=anywhere,
+        scratch_shapes=[pltpu.VMEM((rows, nodes // 2), BF16), pltpu.SemaphoreType.DMA((4,))],
+        input_output_aliases={3: 0},
+        compiler_params=pltpu.CompilerParams(vmem_limit_bytes=8 * MIB),
+        cost_estimate=LIGHT,
+        name="finish_other",
+    )(place, pivot, q3_other, covariance)
+
+
+def finish_last(place, pivot, q2_last, q3_last, covariance, variances):
+    rows, nodes = pivot.shape
     vmem = pl.BlockSpec(memory_space=pltpu.VMEM)
     anywhere = pl.BlockSpec(memory_space=pl.ANY)
     return pl.pallas_call(
@@ -687,15 +700,12 @@
         ),
         in_specs=[pl.BlockSpec(memory_space=pltpu.SMEM)] + [vmem] * 3 + [anywhere, vmem],
         out_specs=(anywhere, vmem),
-        scratch_shapes=[
-            pltpu.VMEM((rows, 3 * width), BF16),
-            pltpu.SemaphoreType.DMA((2, rows // 128)),
-        ],
+        scratch_shapes=[pltpu.VMEM((rows, nodes // 4), BF16), pltpu.SemaphoreType.DMA((4,))],
         input_output_aliases={4: 0},
         compiler_params=pltpu.CompilerParams(vmem_limit_bytes=8 * MIB),
         cost_estimate=LIGHT,
         name="finish_last",
-    )(place, pivot, q2_last, q3, covariance, variances)
+    )(place, pivot, q2_last, q3_last, covariance, variances)
 
 
 def owned(sigma_next, separator, inverse_pivot, coupling_rate, lengths, step_index, node_class):
@@ -721,7 +731,7 @@
     across = turn(place, 2, 0, c2, across)
     c0 = couple_here(place, after(p0, across), weights, coupling_rate)
     across = turn(place, 0, 0, c0, across)
-    column, h0_one, h2_one = own_column(place, after(row, last_three, near_two), c0, c2)
+    column, h0_one, h2_one = own_column(place, after(row, last_three), c0, c2)
     c3 = [
         moved(after(c1[0], last_three, near_two, across), 3, 1),
         moved(after(c1[1], far_zero, h2_one), 3, 1),
@@ -743,8 +753,8 @@
     h3 = [upper, multiply(place, [after(c3[1], q03)], prior)]
     q32 = multiply(place, h3, across, lambda odd: 2 - odd, 1)
     q3_two = moved(q32, 1, 3)
-    q3_own = product_rest(place, h3, across, after(q03, q32))
-    q3 = moved(q3_own, 1, 3)
+    q3_own, q33 = product_rest(place, h3, across, after(q03, q32))
+    q3_other, q3_last = moved(q3_own, 1, 3), moved(q33, 1, 3)
     h1 = multiply(place, [after(c1[0], q3_own), c1[1]], prior)
     q11 = multiply(place, [h1], across, lambda odd: 1 + odd, 1)
     received = (q0, q0_last, q2, q3_two)
@@ -752,7 +762,8 @@
     place_then = tick(tick(place, q0, cost=LIGHT), q0_last, cost=MEDIUM)
     q2_last = moved(after(q3_two, place_then), 3, 2)
     covariance, variances = finish(place_then, pivot, sigma, received, kept)
-    covariance, variances = finish_last(place, pivot, q2_last, q3, covariance, variances)
+    covariance = finish_other(place, pivot, q3_other, covariance)
+    covariance, variances = finish_last(place, pivot, q2_last, q3_last, covariance, variances)
     return (covariance[None], variances)
 
 

time: 120 us -> 118 us (0.983); the launches traced: 120 us -> 117 us
  starting transfers between devices: 30.8 us -> 29.2 us
    ppermute x13 -> x14, starting transfers between devices: 28.7 us -> 27.1 us  [moved(): lax.ppermute(value, ('dom', 'col'), route(source, target, lax.axis_size('...]
    pallas_call x1, Pallas kernels: 2.63 us -> 1.17 us  [finish_last(): pl.pallas_call(last_kernel, out_shape=(jax.ShapeDtypeStruct((rows, nodes)...]
    ppermute x13 -> x14, waiting for transfers between devices: 41.2 us -> 40.2 us  [moved(): lax.ppermute(value, ('dom', 'col'), route(source, target, lax.axis_size('...]
  transfers between devices with their start and end apart: 14 -> 15, of which waited for: 7 -> 7; matrix products, arithmetic and copies ran while one was open for 0% -> 0% of each run, Pallas kernels for 24% -> 26%
where the time goes in v17:
time: 118 us; the launch traced here: 117 us
  waiting for transfers between devices  52.6 us (45%)
  Pallas kernels  31 us (26%)
  starting transfers between devices  29.2 us (25%)
  between operations  3.14 us (3%)
    ppermute x14, waiting for transfers between devices, moved(): lax.ppermute(value, ('dom', 'col'), route(source, target, lax.axis_size('...  40.2 us
    ppermute x14, starting transfers between devices, moved(): lax.ppermute(value, ('dom', 'col'), route(source, target, lax.axis_size('...  27.1 us
    ppermute x1, waiting for transfers between devices, passed_along(): lax.ppermute(value, axis, [(source, source + steps) for source in range(i...  12.4 us
    pallas_call x6, Pallas kernels, turn(): pl.pallas_call(turn_kernel, out_shape=jax.ShapeDtypeStruct((nodes, nodes)...  5.99 us
    pallas_call x7, Pallas kernels, multiply(): pl.pallas_call(functools.partial(multiply_kernel, first, count, len(lefts...  4.03 us
    pallas_call x2, Pallas kernels, couple(): pl.pallas_call(functools.partial(couple_kernel, part * rows), out_shape=j...  3.75 us
    pallas_call x2, Pallas kernels, couple_here(): pl.pallas_call(kernel, out_shape=jax.ShapeDtypeStruct(pivot.shape, BF16),...  3.23 us
    pallas_call x1, Pallas kernels, finish(): pl.pallas_call(finish_kernel, out_shape=(jax.ShapeDtypeStruct((rows, node...  2.64 us
  transfers between devices with their start and end apart: 15, of which 7 were waited for; matrix products, arithmetic and copies ran while one was open for 0% of the time, Pallas kernels for 26%

profile of v17, /device:TPU:1, one launch (start us, length us, event | category | flops | bytes accessed | tf_op | source)
XLA Modules:
  0.0 116.8 jit_solution(7969658922411114137)
XLA Ops:
  0.6 2.1 %collective-permute-start = (bf16[1,512,2048]{2,1,0:T(8,128)(2,1)}, bf16[1,512,2048]{2,1,0:T(8,128)(2,1)}, u32[]{:S(2)}, u32[]{:S(2)}) collective-permute-start(bf16[1,512,2048]{2,1,0:T(8,128)(2,1)} %param.8), channel_id=1, source_target_pairs={{4,0},{8,4},{12,8},{5,1},{9,5},{13,9},{6,2},{10,6},{14,10},{7,3},{... | collective-permute-start | bytes 6291464 | tf_op jit(solution)/shard_map/ppermute | solution.py:20
  2.7 2.0 %collective-permute-start.4 = (bf16[512,2048]{1,0:T(8,128)(2,1)}, bf16[512,2048]{1,0:T(8,128)(2,1)}, u32[]{:S(2)}, u32[]{:S(2)}) collective-permute-start(bf16[512,2048]{1,0:T(8,128)(2,1)} %bitcast.8), channel_id=1, source_target_pairs={{2,1},{5,6},{10,9},{13,14},{18,17},{21,22},{26,25},{29,30}} | collective-permute-start | bytes 6291464 | tf_op jit(solution)/shard_map/ppermute | solution.py:123
  4.8 2.0 %collective-permute-start.3 = (bf16[512,2048]{1,0:T(8,128)(2,1)}, bf16[512,2048]{1,0:T(8,128)(2,1)}, u32[]{:S(2)}, u32[]{:S(2)}) collective-permute-start(bf16[512,2048]{1,0:T(8,128)(2,1)} %bitcast.9), channel_id=1, source_target_pairs={{0,1},{7,6},{8,9},{15,14},{16,17},{23,22},{24,25},{31,30}} | collective-permute-start | bytes 6291464 | tf_op jit(solution)/shard_map/ppermute | solution.py:123
  9.4 1.8 %coupling.1.weight_ref.refs_1_ = bf16[8,512,256]{2,1,0:T(8,128)(2,1)S(1)} custom-call(s32[1,2048]{1,0:T(1,128)S(1)} %bitcast.17), custom_call_target="tpu_custom_call" | custom-call | flops 1048576 | bytes 65536 | tf_op jit(solution)/shard_map/coupling/pallas_call | solution.py:70
  11.3 1.9 %couple.3.coupled_ref.refs_1_ = bf16[256,2048]{1,0:T(8,128)(2,1)S(1)} custom-call(f32[1]{0:T(128)S(6)} %copy.23.rate_ref.refs_0_, bf16[8,512,256]{2,1,0:T(8,128)(2,1)S(1)} %coupling.1.weight_ref.refs_1_, bf16[512,2048]{1,0:T(8,128)(2,1)S(1)} %bitcast.10), custom_call_target="tpu_custom_call" | custom-call | flops 1048576 | bytes 65536 | tf_op jit(solution)/shard_map/couple/pallas_call | solution.py:99
  13.2 1.9 %couple.2.coupled_ref.refs_0_ = bf16[256,2048]{1,0:T(8,128)(2,1)S(1)} custom-call(f32[1]{0:T(128)S(6)} %copy.23.rate_ref.refs_0_, bf16[8,512,256]{2,1,0:T(8,128)(2,1)S(1)} %coupling.1.weight_ref.refs_1_, bf16[512,2048]{1,0:T(8,128)(2,1)S(1)} %bitcast.11), custom_call_target="tpu_custom_call" | custom-call | flops 1048576 | bytes 65536 | tf_op jit(solution)/shard_map/couple/pallas_call | solution.py:99
  16.9 12.4 %collective-permute-done = bf16[1,512,2048]{2,1,0:T(8,128)(2,1)} collective-permute-done((bf16[1,512,2048]{2,1,0:T(8,128)(2,1)}, bf16[1,512,2048]{2,1,0:T(8,128)(2,1)}, u32[]{:S(2)}, u32[]{:S(2)}) %collective-permute-start) | collective-permute-done | bytes 2097184 | tf_op jit(solution)/shard_map/ppermute | solution.py:20
  29.3 2.2 %prior_parts.1 = (bf16[512,2048]{1,0:T(8,128)(2,1)S(1)}, bf16[512,1408]{1,0:T(8,128)(2,1)S(1)}, bf16[512,896]{1,0:T(8,128)(2,1)S(1)}, bf16[512,384]{1,0:T(8,128)(2,1)S(1)}) custom-call(s32[5]{0:T(128)S(1)} %stack.16.place_ref, bf16[512,2048]{1,0:T(8,128)(2,1)} %bitcast.5.shifted_ref, bf16[512,2048]{1,0:T(8,128)(2,1)S(1)} %bitcast.15), custom_call_target="tpu_custom_call" | custom-call | flops 1048576 | bytes 65536 | tf_op jit(solution)/shard_map/prior_parts/pallas_call | solution.py:413
  33.0 5.3 %collective-permute-start.1 = (bf16[512,384]{1,0:T(8,128)(2,1)S(1)}, bf16[512,384]{1,0:T(8,128)(2,1)S(1)}, u32[]{:S(2)}, u32[]{:S(2)}) collective-permute-start(bf16[512,384]{1,0:T(8,128)(2,1)S(1)} %get-tuple-element.29), channel_id=1, source_target_pairs={{3,1},{4,6},{11,9},{12,14},{19,17},{20,22},{27,25},{28,30}} | collective-permute-start | bytes 1179656 | tf_op jit(solution)/shard_map/ppermute | solution.py:123
  38.4 1.6 %couple_here.2.coupled_ref.second_ref.left_ref = bf16[512,2048]{1,0:T(8,128)(2,1)S(1)} custom-call(s32[5]{0:T(128)S(1)} %stack.16.place_ref, f32[1]{0:T(128)S(6)} %copy.23.rate_ref.refs_0_, bf16[8,512,256]{2,1,0:T(8,128)(2,1)S(1)} %coupling.1.weight_ref.refs_1_, bf16[512,2048]{1,0:T(8,128)(2,1)} %collective-permute-done.4.refs_2_), custom_call_target="tpu_custom_call" | custom-call | flops 1048576 | bytes 65536 | tf_op jit(solution)/shard_map/couple_here/pallas_call | solution.py:133
  41.2 1.6 %couple_here.3.coupled_ref.first_ref.left_ref = bf16[512,2048]{1,0:T(8,128)(2,1)S(1)} custom-call(s32[5]{0:T(128)S(1)} %stack.16.place_ref, f32[1]{0:T(128)S(6)} %copy.23.rate_ref.refs_0_, bf16[8,512,256]{2,1,0:T(8,128)(2,1)S(1)} %coupling.1.weight_ref.refs_1_, bf16[512,2048]{1,0:T(8,128)(2,1)} %collective-permute-done.3.refs_2_), custom_call_target="tpu_custom_call" | custom-call | flops 1048576 | bytes 65536 | tf_op jit(solution)/shard_map/couple_here/pallas_call | solution.py:133
  44.1 3.2 %collective-permute-done.1.last_three = bf16[512,384]{1,0:T(8,128)(2,1)S(1)} collective-permute-done((bf16[512,384]{1,0:T(8,128)(2,1)S(1)}, bf16[512,384]{1,0:T(8,128)(2,1)S(1)}, u32[]{:S(2)}, u32[]{:S(2)}) %collective-permute-start.1) | collective-permute-done | bytes 393248 | tf_op jit(solution)/shard_map/ppermute | solution.py:123
  47.9 7.6 %collective-permute-start.5 = (bf16[256,2048]{1,0:T(8,128)(2,1)S(1)}, bf16[256,2048]{1,0:T(8,128)(2,1)S(1)}, u32[]{:S(2)}, u32[]{:S(2)}) collective-permute-start(bf16[256,2048]{1,0:T(8,128)(2,1)S(1)} %couple.2.coupled_ref.refs_0_), channel_id=1, source_target_pairs={{3,1},{4,6},{11,9},{12,14},{19,17},{20,22},{27,25},{28,30}} | collective-permute-start | bytes 3145736 | tf_op jit(solution)/shard_map/ppermute | solution.py:123
  55.5 1.4 %collective-permute-start.7 = (bf16[256,2048]{1,0:T(8,128)(2,1)S(1)}, bf16[256,2048]{1,0:T(8,128)(2,1)S(1)}, u32[]{:S(2)}, u32[]{:S(2)}) collective-permute-start(bf16[256,2048]{1,0:T(8,128)(2,1)S(1)} %couple.3.coupled_ref.refs_1_), channel_id=1, source_target_pairs={{3,1},{4,6},{11,9},{12,14},{19,17},{20,22},{27,25},{28,30}} | collective-permute-start | bytes 3145736 | tf_op jit(solution)/shard_map/ppermute | solution.py:123
  61.1 6.0 %collective-permute-done.5.refs_0_.coupled_ref = bf16[256,2048]{1,0:T(8,128)(2,1)S(1)} collective-permute-done((bf16[256,2048]{1,0:T(8,128)(2,1)S(1)}, bf16[256,2048]{1,0:T(8,128)(2,1)S(1)}, u32[]{:S(2)}, u32[]{:S(2)}) %collective-permute-start.5) | collective-permute-done | bytes 1048608 | tf_op jit(solution)/shard_map/ppermute | solution.py:123
  68.6 9.8 %collective-permute-done.7.coupled_ref.refs_0_ = bf16[256,2048]{1,0:T(8,128)(2,1)S(1)} collective-permute-done((bf16[256,2048]{1,0:T(8,128)(2,1)S(1)}, bf16[256,2048]{1,0:T(8,128)(2,1)S(1)}, u32[]{:S(2)}, u32[]{:S(2)}) %collective-permute-start.7) | collective-permute-done | bytes 1048608 | tf_op jit(solution)/shard_map/ppermute | solution.py:123
  81.8 1.3 %collective-permute-start.8 = (bf16[512,512]{1,0:T(8,128)(2,1)S(1)}, bf16[512,512]{1,0:T(8,128)(2,1)S(1)}, u32[]{:S(2)}, u32[]{:S(2)}) collective-permute-start(bf16[512,512]{1,0:T(8,128)(2,1)S(1)} %multiply.11), channel_id=1, source_target_pairs={{1,3},{6,4},{9,11},{14,12},{17,19},{22,20},{25,27},{30,28}} | collective-permute-start | bytes 1572872 | tf_op jit(solution)/shard_map/ppermute | solution.py:123
  83.7 1.3 %collective-permute-start.13 = (bf16[512,1024]{1,0:T(8,128)(2,1)S(1)}, bf16[512,1024]{1,0:T(8,128)(2,1)S(1)}, u32[]{:S(2)}, u32[]{:S(2)}) collective-permute-start(bf16[512,1024]{1,0:T(8,128)(2,1)S(1)} %get-tuple-element.48.q31), channel_id=1, source_target_pairs={{1,3},{6,4},{9,11},{14,12},{17,19},{22,20},{25,27},{30,28}} | collective-permute-start | bytes 3145736 | tf_op jit(solution)/shard_map/ppermute | solution.py:123
  86.1 1.3 %collective-permute-start.12 = (bf16[512,384]{1,0:T(8,128)(2,1)S(1)}, bf16[512,384]{1,0:T(8,128)(2,1)S(1)}, u32[]{:S(2)}, u32[]{:S(2)}) collective-permute-start(bf16[512,384]{1,0:T(8,128)(2,1)S(1)} %get-tuple-element.47), channel_id=1, source_target_pairs={{1,3},{6,4},{9,11},{14,12},{17,19},{22,20},{25,27},{30,28}} | collective-permute-start | bytes 1179656 | tf_op jit(solution)/shard_map/ppermute | solution.py:123
  89.7 10.2 %collective-permute-done.8.q3_two = bf16[512,512]{1,0:T(8,128)(2,1)S(1)} collective-permute-done((bf16[512,512]{1,0:T(8,128)(2,1)S(1)}, bf16[512,512]{1,0:T(8,128)(2,1)S(1)}, u32[]{:S(2)}, u32[]{:S(2)}) %collective-permute-start.8) | collective-permute-done | bytes 524320 | tf_op jit(solution)/shard_map/ppermute | solution.py:123
  100.0 1.3 %collective-permute-start.11 = (bf16[512,512]{1,0:T(8,128)(2,1)S(1)}, bf16[512,512]{1,0:T(8,128)(2,1)S(1)}, u32[]{:S(2)}, u32[]{:S(2)}) collective-permute-start(bf16[512,512]{1,0:T(8,128)(2,1)S(1)} %collective-permute-done.8.q3_two), channel_id=1, source_target_pairs={{3,2},{4,5},{11,10},{12,13},{19,18},{20,21},{27,26},{28,29}} | collective-permute-start | bytes 1572872 | tf_op jit(solution)/shard_map/ppermute | solution.py:123
  101.3 2.6 %finish.1 = (bf16[512,2048]{1,0:T(8,128)(2,1)}, f32[1,512]{1,0:T(1,128)S(1)}) custom-call(s32[5]{0:T(128)S(1)} %tick.3.place_ref, bf16[512,2048]{1,0:T(8,128)(2,1)S(1)} %bitcast.12, bf16[512,2048]{1,0:T(8,128)(2,1)S(1)} %bitcast.16, bf16[512,1536]{1,0:T(8,128)(2,1)S(1)} %collective-permute-done.9.refs_0_.q0, ...), custom_call_target="tpu_custom_call" | custom-call | flops 14000000000 | bytes 65536 | tf_op jit(solution)/shard_map/finish/pallas_call | solution.py:580
  103.9 7.3 %collective-permute-done.13.q3_other = bf16[512,1024]{1,0:T(8,128)(2,1)S(1)} collective-permute-done((bf16[512,1024]{1,0:T(8,128)(2,1)S(1)}, bf16[512,1024]{1,0:T(8,128)(2,1)S(1)}, u32[]{:S(2)}, u32[]{:S(2)}) %collective-permute-start.13) | collective-permute-done | bytes 1048608 | tf_op jit(solution)/shard_map/ppermute | solution.py:123
  111.8 3.6 %collective-permute-done.12.q3_last = bf16[512,384]{1,0:T(8,128)(2,1)S(1)} collective-permute-done((bf16[512,384]{1,0:T(8,128)(2,1)S(1)}, bf16[512,384]{1,0:T(8,128)(2,1)S(1)}, u32[]{:S(2)}, u32[]{:S(2)}) %collective-permute-start.12) | collective-permute-done | bytes 393248 | tf_op jit(solution)/shard_map/ppermute | solution.py:123
  (43 shorter events, 21.9 us)
Async XLA Ops:
  0.6 10.7 %copy-start = (bf16[1,512,2048]{2,1,0:T(8,128)(2,1)S(1)}, bf16[1,512,2048]{2,1,0:T(8,128)(2,1)}, u32[]{:S(2)}) copy-start(bf16[1,512,2048]{2,1,0:T(8,128)(2,1)} %param.9) | copy-start | bytes 6291460
  0.6 28.7 %collective-permute-start = (bf16[1,512,2048]{2,1,0:T(8,128)(2,1)}, bf16[1,512,2048]{2,1,0:T(8,128)(2,1)}, u32[]{:S(2)}, u32[]{:S(2)}) collective-permute-start(bf16[1,512,2048]{2,1,0:T(8,128)(2,1)} %param.8), channel_id=1, source_target_pairs={{4,0},{8,4},{12,8},{5,1},{9,5},{13,9},{6,2},{10,6},{14,10},{7,3},{... | collective-permute-start | bytes 6291464 | tf_op jit(solution)/shard_map/ppermute | solution.py:20
  2.7 35.6 %collective-permute-start.4 = (bf16[512,2048]{1,0:T(8,128)(2,1)}, bf16[512,2048]{1,0:T(8,128)(2,1)}, u32[]{:S(2)}, u32[]{:S(2)}) collective-permute-start(bf16[512,2048]{1,0:T(8,128)(2,1)} %bitcast.8), channel_id=1, source_target_pairs={{2,1},{5,6},{10,9},{13,14},{18,17},{21,22},{26,25},{29,30}} | collective-permute-start | bytes 6291464 | tf_op jit(solution)/shard_map/ppermute | solution.py:123
  4.8 36.5 %collective-permute-start.3 = (bf16[512,2048]{1,0:T(8,128)(2,1)}, bf16[512,2048]{1,0:T(8,128)(2,1)}, u32[]{:S(2)}, u32[]{:S(2)}) collective-permute-start(bf16[512,2048]{1,0:T(8,128)(2,1)} %bitcast.9), channel_id=1, source_target_pairs={{0,1},{7,6},{8,9},{15,14},{16,17},{23,22},{24,25},{31,30}} | collective-permute-start | bytes 6291464 | tf_op jit(solution)/shard_map/ppermute | solution.py:123
  8.7 0.7 copy-start.2
  16.0 13.3 %copy-start.1 = (bf16[1,512,2048]{2,1,0:T(8,128)(2,1)S(1)}, bf16[1,512,2048]{2,1,0:T(8,128)(2,1)}, u32[]{:S(2)}) copy-start(bf16[1,512,2048]{2,1,0:T(8,128)(2,1)} %param.7) | copy-start | bytes 6291460
  31.5 23.9 %collective-permute-start.6 = (bf16[512,1408]{1,0:T(8,128)(2,1)S(1)}, bf16[512,1408]{1,0:T(8,128)(2,1)S(1)}, u32[]{:S(2)}, u32[]{:S(2)}) collective-permute-start(bf16[512,1408]{1,0:T(8,128)(2,1)S(1)} %get-tuple-element.37), channel_id=1, source_target_pairs={{0,1},{7,6},{8,9},{15,14},{16,17},{23,22},{24,25},{31,30}} | collective-permute-start | bytes 4325384 | tf_op jit(solution)/shard_map/ppermute | solution.py:123
  32.3 15.6 %collective-permute-start.2 = (bf16[512,896]{1,0:T(8,128)(2,1)S(1)}, bf16[512,896]{1,0:T(8,128)(2,1)S(1)}, u32[]{:S(2)}, u32[]{:S(2)}) collective-permute-start(bf16[512,896]{1,0:T(8,128)(2,1)S(1)} %get-tuple-element.30), channel_id=1, source_target_pairs={{2,1},{5,6},{10,9},{13,14},{18,17},{21,22},{26,25},{29,30}} | collective-permute-start | bytes 2752520 | tf_op jit(solution)/shard_map/ppermute | solution.py:123
  33.0 14.3 %collective-permute-start.1 = (bf16[512,384]{1,0:T(8,128)(2,1)S(1)}, bf16[512,384]{1,0:T(8,128)(2,1)S(1)}, u32[]{:S(2)}, u32[]{:S(2)}) collective-permute-start(bf16[512,384]{1,0:T(8,128)(2,1)S(1)} %get-tuple-element.29), channel_id=1, source_target_pairs={{3,1},{4,6},{11,9},{12,14},{19,17},{20,22},{27,25},{28,30}} | collective-permute-start | bytes 1179656 | tf_op jit(solution)/shard_map/ppermute | solution.py:123
  47.9 19.2 %collective-permute-start.5 = (bf16[256,2048]{1,0:T(8,128)(2,1)S(1)}, bf16[256,2048]{1,0:T(8,128)(2,1)S(1)}, u32[]{:S(2)}, u32[]{:S(2)}) collective-permute-start(bf16[256,2048]{1,0:T(8,128)(2,1)S(1)} %couple.2.coupled_ref.refs_0_), channel_id=1, source_target_pairs={{3,1},{4,6},{11,9},{12,14},{19,17},{20,22},{27,25},{28,30}} | collective-permute-start | bytes 3145736 | tf_op jit(solution)/shard_map/ppermute | solution.py:123
  55.5 22.9 %collective-permute-start.7 = (bf16[256,2048]{1,0:T(8,128)(2,1)S(1)}, bf16[256,2048]{1,0:T(8,128)(2,1)S(1)}, u32[]{:S(2)}, u32[]{:S(2)}) collective-permute-start(bf16[256,2048]{1,0:T(8,128)(2,1)S(1)} %couple.3.coupled_ref.refs_1_), channel_id=1, source_target_pairs={{3,1},{4,6},{11,9},{12,14},{19,17},{20,22},{27,25},{28,30}} | collective-permute-start | bytes 3145736 | tf_op jit(solution)/shard_map/ppermute | solution.py:123
  58.5 27.6 %collective-permute-start.9 = (bf16[512,1536]{1,0:T(8,128)(2,1)S(1)}, bf16[512,1536]{1,0:T(8,128)(2,1)S(1)}, u32[]{:S(2)}, u32[]{:S(2)}) collective-permute-start(bf16[512,1536]{1,0:T(8,128)(2,1)S(1)} %multiply.8.zero_ref.q01), channel_id=1, source_target_pairs={{1,0},{6,7},{9,8},{14,15},{17,16},{22,23},{25,24},{30,31}} | collective-permute-start | bytes 4718600 | tf_op jit(solution)/shard_map/ppermute | solution.py:123
  60.4 40.9 %collective-permute-start.14 = (bf16[512,1408]{1,0:T(8,128)(2,1)S(1)}, bf16[512,1408]{1,0:T(8,128)(2,1)S(1)}, u32[]{:S(2)}, u32[]{:S(2)}) collective-permute-start(bf16[512,1408]{1,0:T(8,128)(2,1)S(1)} %product_two.1.q21), channel_id=1, source_target_pairs={{1,2},{6,5},{9,10},{14,13},{17,18},{22,21},{25,26},{30,29}} | collective-permute-start | bytes 4325384 | tf_op jit(solution)/shard_map/ppermute | solution.py:123
  80.0 8.6 %collective-permute-start.10 = (bf16[512,512]{1,0:T(8,128)(2,1)S(1)}, bf16[512,512]{1,0:T(8,128)(2,1)S(1)}, u32[]{:S(2)}, u32[]{:S(2)}) collective-permute-start(bf16[512,512]{1,0:T(8,128)(2,1)S(1)} %multiply.9.zero_ref), channel_id=1, source_target_pairs={{1,0},{6,7},{9,8},{14,15},{17,16},{22,23},{25,24},{30,31}} | collective-permute-start | bytes 1572872 | tf_op jit(solution)/shard_map/ppermute | solution.py:123
  81.8 18.1 %collective-permute-start.8 = (bf16[512,512]{1,0:T(8,128)(2,1)S(1)}, bf16[512,512]{1,0:T(8,128)(2,1)S(1)}, u32[]{:S(2)}, u32[]{:S(2)}) collective-permute-start(bf16[512,512]{1,0:T(8,128)(2,1)S(1)} %multiply.11), channel_id=1, source_target_pairs={{1,3},{6,4},{9,11},{14,12},{17,19},{22,20},{25,27},{30,28}} | collective-permute-start | bytes 1572872 | tf_op jit(solution)/shard_map/ppermute | solution.py:123
  83.7 27.5 %collective-permute-start.13 = (bf16[512,1024]{1,0:T(8,128)(2,1)S(1)}, bf16[512,1024]{1,0:T(8,128)(2,1)S(1)}, u32[]{:S(2)}, u32[]{:S(2)}) collective-permute-start(bf16[512,1024]{1,0:T(8,128)(2,1)S(1)} %get-tuple-element.48.q31), channel_id=1, source_target_pairs={{1,3},{6,4},{9,11},{14,12},{17,19},{22,20},{25,27},{30,28}} | collective-permute-start | bytes 3145736 | tf_op jit(solution)/shard_map/ppermute | solution.py:123
  86.1 29.3 %collective-permute-start.12 = (bf16[512,384]{1,0:T(8,128)(2,1)S(1)}, bf16[512,384]{1,0:T(8,128)(2,1)S(1)}, u32[]{:S(2)}, u32[]{:S(2)}) collective-permute-start(bf16[512,384]{1,0:T(8,128)(2,1)S(1)} %get-tuple-element.47), channel_id=1, source_target_pairs={{1,3},{6,4},{9,11},{14,12},{17,19},{22,20},{25,27},{30,28}} | collective-permute-start | bytes 1179656 | tf_op jit(solution)/shard_map/ppermute | solution.py:123
  100.0 15.5 %collective-permute-start.11 = (bf16[512,512]{1,0:T(8,128)(2,1)S(1)}, bf16[512,512]{1,0:T(8,128)(2,1)S(1)}, u32[]{:S(2)}, u32[]{:S(2)}) collective-permute-start(bf16[512,512]{1,0:T(8,128)(2,1)S(1)} %collective-permute-done.8.q3_two), channel_id=1, source_target_pairs={{3,2},{4,5},{11,10},{12,13},{19,18},{20,21},{27,26},{28,29}} | collective-permute-start | bytes 1572872 | tf_op jit(solution)/shard_map/ppermute | solution.py:123

commit v18 on v17

--- a/solution.py
+++ b/solution.py
@@ -209,10 +209,10 @@
 
 
 def pack(value, out_ref, column):
-    half = value.shape[0] // 2
-    for part in range(2):
-        rows = pl.ds(part * half, half)
-        pack_rows(part, value[part * half : (part + 1) * half], out_ref.at[rows], column)
+    quarter = value.shape[1] // 4
+    for part in range(4):
+        rows = pl.ds(part * quarter, quarter)
+        pack_rows(part, value[part * quarter : (part + 1) * quarter], out_ref.at[rows], column)
 
 
 def two_kernel(place_ref, left_ref, right_ref, zero_ref, out_ref):
@@ -326,9 +326,13 @@
         out_ref[:, pl.ds(pl.multiple_of(odd * width, 128), width)] = zero_ref[...].T
         other = pl.ds(pl.multiple_of((1 - odd) * width, 128), width)
         for part, left_ref in enumerate((upper_ref, lower_ref)):
-            rows = pl.ds(part * half, half)
-            out_ref[rows, other] = product(left_ref, 1 + odd)
-            pack_rows(part, product(left_ref, 3 - 3 * odd), last_ref.at[rows], 0)
+            out_ref[pl.ds(part * half, half), other] = product(left_ref, 1 + odd)
+            value = product(left_ref, 3 - 3 * odd)
+            for quarter in range(2):
+                start = quarter * half // 2
+                rows = pl.ds(part * half + start, half // 2)
+                rows_of = value[start : start + half // 2]
+                pack_rows(2 * part + quarter, rows_of, last_ref.at[rows], 0)
 
 
 def product_rest(place, halves, across, zero):
@@ -349,30 +353,30 @@
 
 
 def pack_rows(part, value, out_ref, column):
-    half, width = value.shape
-    quarter = half // 2
-    if part == 0:
-        out_ref[:, column : column + half] = value[:, :half]
-        out_ref[:, column + half : column + half + quarter] = value[:, half : half + quarter]
-    else:
-        out_ref[:, column : column + half] = value[:, half:]
-        beside = slice(column + half, column + half + quarter)
-        out_ref[:quarter, beside] = value[quarter:, :quarter]
-        out_ref[quarter:, beside] = value[quarter:, quarter:half]
+    quarter, width = value.shape
+    half = width // 2
+    beside = (2, 3, 1, 0)[part] * quarter
+    out_ref[:, column : column + half] = value[:, part // 2 * half : (part // 2 + 1) * half]
+    out_ref[:, column + half : column + half + quarter] = value[:, beside : beside + quarter]
 
 
 def unpacked_rows(part, packed_ref, column):
     quarter = packed_ref.shape[0] // 4
     half = 2 * quarter
-    beside = slice(column + half, column + half + quarter)
+
+    def beside(which):
+        rows = slice(which * quarter, (which + 1) * quarter)
+        return packed_ref[rows, column + half : column + half + quarter]
+
     rows = slice(part * quarter, (part + 1) * quarter)
     diagonal = packed_ref[rows, column : column + half]
-    lower = [packed_ref[start : start + quarter, beside] for start in (half, half + quarter)]
-    if part < 2:
-        return diagonal, jnp.concatenate([packed_ref[rows, beside], lower[part].T], axis=1)
+    if part == 0:
+        return diagonal, jnp.concatenate([beside(0), beside(3).T], axis=1)
+    if part == 1:
+        return diagonal, jnp.concatenate([beside(2).T, beside(1)], axis=1)
     if part == 2:
-        return packed_ref[:half, beside].T, diagonal
-    return jnp.concatenate(lower, axis=1), diagonal
+        return jnp.concatenate([beside(0).T, beside(2)], axis=1), diagonal
+    return jnp.concatenate([beside(3), beside(1).T], axis=1), diagonal
 
 
 def prior_kernel(place_ref, shifted_ref, sigma_ref, out_ref):
@@ -395,7 +399,7 @@
     prior_kernel(place_ref, shifted_ref, sigma_ref, row_ref)
     far_ref[:, : 2 * width] = row_ref[:, at(2 - 2 * odd, 2)]
     near_ref[:, :width] = row_ref[:, at(3 - 3 * odd)]
-    for part in range(2):
+    for part in range(4):
 
         @pl.when(pl.program_id(0) == part)
         def _():
@@ -406,7 +410,7 @@
 
 def prior_parts(place, shifted, sigma):
     rows, nodes = sigma.shape
-    chunk = rows // 2
+    chunk = rows // 4
     width = nodes // 4
     out = lambda quarters: jax.ShapeDtypeStruct((rows, quarters * width // 4), BF16)
     spec = lambda quarters: pl.BlockSpec((chunk, quarters * width // 4), lambda i, place: (i, 0))
@@ -426,7 +430,7 @@
             ],
             out_specs=(spec(16), spec(11), spec(7), spec(3)),
         ),
-        compiler_params=pltpu.CompilerParams(vmem_limit_bytes=14 * MIB),
+        compiler_params=pltpu.CompilerParams(vmem_limit_bytes=8 * MIB),
         cost_estimate=LIGHT,
         name="prior_parts",
     )(place, shifted, sigma)
@@ -616,7 +620,7 @@
     copies = []
     for part in range(4):
         here = pl.ds(part * chunk, chunk)
-        value = pivot_ref[here, column].astype(F32) + product(part, here).astype(F32)
+        value = pivot_ref[here, :].astype(F32) + product(part, here).astype(F32)
         sum_ref[here, :] = value.astype(BF16)
         copies.append(
             pltpu.make_async_copy(sum_ref.at[here], out_ref.at[here, column], sems.at[part])
@@ -627,8 +631,8 @@
 
 
 def other_kernel(place_ref, pivot_ref, q3_other, old_ref, out_ref, sum_ref, sems):
-    width = pivot_ref.shape[1] // 4
-    column = pl.ds(pl.multiple_of(2 * place_ref[0] * width, 128), 2 * width)
+    both = pivot_ref.shape[1]
+    column = pl.ds(pl.multiple_of(place_ref[0] * both, 128), both)
 
     @pl.when((place_ref[4] != 0) & (place_ref[1] == 3))
     def _():
@@ -640,8 +644,7 @@
 def last_kernel(
     place_ref, pivot_ref, q2_last, q3_last, old_ref, old_var_ref, out_ref, var_ref, sum_ref, sems
 ):
-    rows, nodes = pivot_ref.shape
-    width = nodes // 4
+    rows, width = pivot_ref.shape
     chunk = rows // 4
     active = place_ref[4] != 0
     column = pl.ds(pl.multiple_of(turned(3, place_ref[0]) * width, 128), width)
@@ -657,8 +660,7 @@
         add(lambda part, here: jnp.concatenate(unpacked_rows(part, q3_last, 0), axis=1))
         for start in range(0, rows, chunk):
             here = pl.ds(start, chunk)
-            own = pl.ds(pl.multiple_of(place_ref[2] * width + start, 128), chunk)
-            value = pivot_ref[here, own].astype(F32)
+            value = pivot_ref[here, here].astype(F32)
             value = value + q3_last[here, pl.ds(start % (2 * chunk), chunk)].astype(F32)
             var_ref[:, here] = diagonal_of(chunk)(value)
 
@@ -678,9 +680,17 @@
     return pl.pallas_call(
         other_kernel,
         out_shape=jax.ShapeDtypeStruct((rows, nodes), BF16),
-        in_specs=[pl.BlockSpec(memory_space=pltpu.SMEM), vmem, vmem, anywhere],
-        out_specs=anywhere,
-        scratch_shapes=[pltpu.VMEM((rows, nodes // 2), BF16), pltpu.SemaphoreType.DMA((4,))],
+        grid_spec=pltpu.PrefetchScalarGridSpec(
+            num_scalar_prefetch=1,
+            grid=(1,),
+            in_specs=[
+                pl.BlockSpec((rows, nodes // 2), lambda i, place: (0, place[0])),
+                vmem,
+                anywhere,
+            ],
+            out_specs=anywhere,
+            scratch_shapes=[pltpu.VMEM((rows, nodes // 2), BF16), pltpu.SemaphoreType.DMA((4,))],
+        ),
         input_output_aliases={3: 0},
         compiler_params=pltpu.CompilerParams(vmem_limit_bytes=8 * MIB),
         cost_estimate=LIGHT,
@@ -698,9 +708,19 @@
             jax.ShapeDtypeStruct((rows, nodes), BF16),
             jax.ShapeDtypeStruct((1, rows), F32),
         ),
-        in_specs=[pl.BlockSpec(memory_space=pltpu.SMEM)] + [vmem] * 3 + [anywhere, vmem],
-        out_specs=(anywhere, vmem),
-        scratch_shapes=[pltpu.VMEM((rows, nodes // 4), BF16), pltpu.SemaphoreType.DMA((4,))],
+        grid_spec=pltpu.PrefetchScalarGridSpec(
+            num_scalar_prefetch=1,
+            grid=(1,),
+            in_specs=[
+                pl.BlockSpec((rows, nodes // 4), lambda i, place: (0, turned(3, place[0]))),
+                vmem,
+                vmem,
+                anywhere,
+                vmem,
+            ],
+            out_specs=(anywhere, vmem),
+            scratch_shapes=[pltpu.VMEM((rows, nodes // 4), BF16), pltpu.SemaphoreType.DMA((4,))],
+        ),
         input_output_aliases={4: 0},
         compiler_params=pltpu.CompilerParams(vmem_limit_bytes=8 * MIB),
         cost_estimate=LIGHT,

time: 118 us -> 119 us (level)
  transfers between devices with their start and end apart: 15 -> 15, of which waited for: 7 -> 7; matrix products, arithmetic and copies ran while one was open for 0% -> 0% of each run, Pallas kernels for 26% -> 25%
where the time goes in v18:
time: 119 us; the launch traced here: 117 us
  waiting for transfers between devices  52.8 us (44%)
  Pallas kernels  31 us (26%)
  starting transfers between devices  29.2 us (25%)
  between operations  3.14 us (3%)
    ppermute x14, waiting for transfers between devices, moved(): lax.ppermute(value, ('dom', 'col'), route(source, target, lax.axis_size('...  40.4 us
    ppermute x14, starting transfers between devices, moved(): lax.ppermute(value, ('dom', 'col'), route(source, target, lax.axis_size('...  27.1 us
    ppermute x1, waiting for transfers between devices, passed_along(): lax.ppermute(value, axis, [(source, source + steps) for source in range(i...  12.4 us
    pallas_call x6, Pallas kernels, turn(): pl.pallas_call(turn_kernel, out_shape=jax.ShapeDtypeStruct((nodes, nodes)...  5.99 us
    pallas_call x7, Pallas kernels, multiply(): pl.pallas_call(functools.partial(multiply_kernel, first, count, len(lefts...  4.03 us
    pallas_call x2, Pallas kernels, couple(): pl.pallas_call(functools.partial(couple_kernel, part * rows), out_shape=j...  3.75 us
    pallas_call x2, Pallas kernels, couple_here(): pl.pallas_call(kernel, out_shape=jax.ShapeDtypeStruct(pivot.shape, BF16),...  3.23 us
    pallas_call x1, Pallas kernels, finish(): pl.pallas_call(finish_kernel, out_shape=(jax.ShapeDtypeStruct((rows, node...  2.64 us
  transfers between devices with their start and end apart: 15, of which 7 were waited for; matrix products, arithmetic and copies ran while one was open for 0% of the time, Pallas kernels for 25%

profile of v18, /device:TPU:1, one launch (start us, length us, event | category | flops | bytes accessed | tf_op | source)
XLA Modules:
  0.0 117.0 jit_solution(10263119039196322106)
XLA Ops:
  0.6 2.1 %collective-permute-start = (bf16[1,512,2048]{2,1,0:T(8,128)(2,1)}, bf16[1,512,2048]{2,1,0:T(8,128)(2,1)}, u32[]{:S(2)}, u32[]{:S(2)}) collective-permute-start(bf16[1,512,2048]{2,1,0:T(8,128)(2,1)} %param.8), channel_id=1, source_target_pairs={{4,0},{8,4},{12,8},{5,1},{9,5},{13,9},{6,2},{10,6},{14,10},{7,3},{... | collective-permute-start | bytes 6291464 | tf_op jit(solution)/shard_map/ppermute | solution.py:20
  2.7 2.0 %collective-permute-start.4 = (bf16[512,2048]{1,0:T(8,128)(2,1)}, bf16[512,2048]{1,0:T(8,128)(2,1)}, u32[]{:S(2)}, u32[]{:S(2)}) collective-permute-start(bf16[512,2048]{1,0:T(8,128)(2,1)} %bitcast.8), channel_id=1, source_target_pairs={{2,1},{5,6},{10,9},{13,14},{18,17},{21,22},{26,25},{29,30}} | collective-permute-start | bytes 6291464 | tf_op jit(solution)/shard_map/ppermute | solution.py:123
  4.8 2.0 %collective-permute-start.3 = (bf16[512,2048]{1,0:T(8,128)(2,1)}, bf16[512,2048]{1,0:T(8,128)(2,1)}, u32[]{:S(2)}, u32[]{:S(2)}) collective-permute-start(bf16[512,2048]{1,0:T(8,128)(2,1)} %bitcast.9), channel_id=1, source_target_pairs={{0,1},{7,6},{8,9},{15,14},{16,17},{23,22},{24,25},{31,30}} | collective-permute-start | bytes 6291464 | tf_op jit(solution)/shard_map/ppermute | solution.py:123
  9.4 1.8 %coupling.1.weight_ref.refs_1_ = bf16[8,512,256]{2,1,0:T(8,128)(2,1)S(1)} custom-call(s32[1,2048]{1,0:T(1,128)S(1)} %bitcast.17), custom_call_target="tpu_custom_call" | custom-call | flops 1048576 | bytes 65536 | tf_op jit(solution)/shard_map/coupling/pallas_call | solution.py:70
  11.3 1.9 %couple.3.coupled_ref.refs_1_ = bf16[256,2048]{1,0:T(8,128)(2,1)S(1)} custom-call(f32[1]{0:T(128)S(6)} %copy.23.rate_ref.refs_0_, bf16[8,512,256]{2,1,0:T(8,128)(2,1)S(1)} %coupling.1.weight_ref.refs_1_, bf16[512,2048]{1,0:T(8,128)(2,1)S(1)} %bitcast.10), custom_call_target="tpu_custom_call" | custom-call | flops 1048576 | bytes 65536 | tf_op jit(solution)/shard_map/couple/pallas_call | solution.py:99
  13.2 1.9 %couple.2.coupled_ref.refs_0_ = bf16[256,2048]{1,0:T(8,128)(2,1)S(1)} custom-call(f32[1]{0:T(128)S(6)} %copy.23.rate_ref.refs_0_, bf16[8,512,256]{2,1,0:T(8,128)(2,1)S(1)} %coupling.1.weight_ref.refs_1_, bf16[512,2048]{1,0:T(8,128)(2,1)S(1)} %bitcast.11), custom_call_target="tpu_custom_call" | custom-call | flops 1048576 | bytes 65536 | tf_op jit(solution)/shard_map/couple/pallas_call | solution.py:99
  16.9 12.4 %collective-permute-done = bf16[1,512,2048]{2,1,0:T(8,128)(2,1)} collective-permute-done((bf16[1,512,2048]{2,1,0:T(8,128)(2,1)}, bf16[1,512,2048]{2,1,0:T(8,128)(2,1)}, u32[]{:S(2)}, u32[]{:S(2)}) %collective-permute-start) | collective-permute-done | bytes 2097184 | tf_op jit(solution)/shard_map/ppermute | solution.py:20
  29.3 2.1 %prior_parts.1 = (bf16[512,2048]{1,0:T(8,128)(2,1)S(1)}, bf16[512,1408]{1,0:T(8,128)(2,1)S(1)}, bf16[512,896]{1,0:T(8,128)(2,1)S(1)}, bf16[512,384]{1,0:T(8,128)(2,1)S(1)}) custom-call(s32[5]{0:T(128)S(1)} %stack.16.place_ref, bf16[512,2048]{1,0:T(8,128)(2,1)} %bitcast.5.shifted_ref, bf16[512,2048]{1,0:T(8,128)(2,1)S(1)} %bitcast.15), custom_call_target="tpu_custom_call" | custom-call | flops 1048576 | bytes 65536 | tf_op jit(solution)/shard_map/prior_parts/pallas_call | solution.py:417
  32.9 5.3 %collective-permute-start.1 = (bf16[512,384]{1,0:T(8,128)(2,1)S(1)}, bf16[512,384]{1,0:T(8,128)(2,1)S(1)}, u32[]{:S(2)}, u32[]{:S(2)}) collective-permute-start(bf16[512,384]{1,0:T(8,128)(2,1)S(1)} %get-tuple-element.29), channel_id=1, source_target_pairs={{3,1},{4,6},{11,9},{12,14},{19,17},{20,22},{27,25},{28,30}} | collective-permute-start | bytes 1179656 | tf_op jit(solution)/shard_map/ppermute | solution.py:123
  38.3 1.6 %couple_here.2.coupled_ref.second_ref.left_ref = bf16[512,2048]{1,0:T(8,128)(2,1)S(1)} custom-call(s32[5]{0:T(128)S(1)} %stack.16.place_ref, f32[1]{0:T(128)S(6)} %copy.23.rate_ref.refs_0_, bf16[8,512,256]{2,1,0:T(8,128)(2,1)S(1)} %coupling.1.weight_ref.refs_1_, bf16[512,2048]{1,0:T(8,128)(2,1)} %collective-permute-done.4.refs_2_), custom_call_target="tpu_custom_call" | custom-call | flops 1048576 | bytes 65536 | tf_op jit(solution)/shard_map/couple_here/pallas_call | solution.py:133
  41.2 1.6 %couple_here.3.coupled_ref.first_ref.left_ref = bf16[512,2048]{1,0:T(8,128)(2,1)S(1)} custom-call(s32[5]{0:T(128)S(1)} %stack.16.place_ref, f32[1]{0:T(128)S(6)} %copy.23.rate_ref.refs_0_, bf16[8,512,256]{2,1,0:T(8,128)(2,1)S(1)} %coupling.1.weight_ref.refs_1_, bf16[512,2048]{1,0:T(8,128)(2,1)} %collective-permute-done.3.refs_2_), custom_call_target="tpu_custom_call" | custom-call | flops 1048576 | bytes 65536 | tf_op jit(solution)/shard_map/couple_here/pallas_call | solution.py:133
  44.0 3.2 %collective-permute-done.1.last_three = bf16[512,384]{1,0:T(8,128)(2,1)S(1)} collective-permute-done((bf16[512,384]{1,0:T(8,128)(2,1)S(1)}, bf16[512,384]{1,0:T(8,128)(2,1)S(1)}, u32[]{:S(2)}, u32[]{:S(2)}) %collective-permute-start.1) | collective-permute-done | bytes 393248 | tf_op jit(solution)/shard_map/ppermute | solution.py:123
  47.8 7.6 %collective-permute-start.5 = (bf16[256,2048]{1,0:T(8,128)(2,1)S(1)}, bf16[256,2048]{1,0:T(8,128)(2,1)S(1)}, u32[]{:S(2)}, u32[]{:S(2)}) collective-permute-start(bf16[256,2048]{1,0:T(8,128)(2,1)S(1)} %couple.2.coupled_ref.refs_0_), channel_id=1, source_target_pairs={{3,1},{4,6},{11,9},{12,14},{19,17},{20,22},{27,25},{28,30}} | collective-permute-start | bytes 3145736 | tf_op jit(solution)/shard_map/ppermute | solution.py:123
  55.4 1.4 %collective-permute-start.7 = (bf16[256,2048]{1,0:T(8,128)(2,1)S(1)}, bf16[256,2048]{1,0:T(8,128)(2,1)S(1)}, u32[]{:S(2)}, u32[]{:S(2)}) collective-permute-start(bf16[256,2048]{1,0:T(8,128)(2,1)S(1)} %couple.3.coupled_ref.refs_1_), channel_id=1, source_target_pairs={{3,1},{4,6},{11,9},{12,14},{19,17},{20,22},{27,25},{28,30}} | collective-permute-start | bytes 3145736 | tf_op jit(solution)/shard_map/ppermute | solution.py:123
  61.1 6.0 %collective-permute-done.5.refs_0_.coupled_ref = bf16[256,2048]{1,0:T(8,128)(2,1)S(1)} collective-permute-done((bf16[256,2048]{1,0:T(8,128)(2,1)S(1)}, bf16[256,2048]{1,0:T(8,128)(2,1)S(1)}, u32[]{:S(2)}, u32[]{:S(2)}) %collective-permute-start.5) | collective-permute-done | bytes 1048608 | tf_op jit(solution)/shard_map/ppermute | solution.py:123
  68.5 9.8 %collective-permute-done.7.coupled_ref.refs_0_ = bf16[256,2048]{1,0:T(8,128)(2,1)S(1)} collective-permute-done((bf16[256,2048]{1,0:T(8,128)(2,1)S(1)}, bf16[256,2048]{1,0:T(8,128)(2,1)S(1)}, u32[]{:S(2)}, u32[]{:S(2)}) %collective-permute-start.7) | collective-permute-done | bytes 1048608 | tf_op jit(solution)/shard_map/ppermute | solution.py:123
  81.8 1.3 %collective-permute-start.8 = (bf16[512,512]{1,0:T(8,128)(2,1)S(1)}, bf16[512,512]{1,0:T(8,128)(2,1)S(1)}, u32[]{:S(2)}, u32[]{:S(2)}) collective-permute-start(bf16[512,512]{1,0:T(8,128)(2,1)S(1)} %multiply.11), channel_id=1, source_target_pairs={{1,3},{6,4},{9,11},{14,12},{17,19},{22,20},{25,27},{30,28}} | collective-permute-start | bytes 1572872 | tf_op jit(solution)/shard_map/ppermute | solution.py:123
  83.6 1.3 %collective-permute-start.13 = (bf16[512,1024]{1,0:T(8,128)(2,1)S(1)}, bf16[512,1024]{1,0:T(8,128)(2,1)S(1)}, u32[]{:S(2)}, u32[]{:S(2)}) collective-permute-start(bf16[512,1024]{1,0:T(8,128)(2,1)S(1)} %get-tuple-element.48.q31), channel_id=1, source_target_pairs={{1,3},{6,4},{9,11},{14,12},{17,19},{22,20},{25,27},{30,28}} | collective-permute-start | bytes 3145736 | tf_op jit(solution)/shard_map/ppermute | solution.py:123
  86.0 1.3 %collective-permute-start.12 = (bf16[512,384]{1,0:T(8,128)(2,1)S(1)}, bf16[512,384]{1,0:T(8,128)(2,1)S(1)}, u32[]{:S(2)}, u32[]{:S(2)}) collective-permute-start(bf16[512,384]{1,0:T(8,128)(2,1)S(1)} %get-tuple-element.47), channel_id=1, source_target_pairs={{1,3},{6,4},{9,11},{14,12},{17,19},{22,20},{25,27},{30,28}} | collective-permute-start | bytes 1179656 | tf_op jit(solution)/shard_map/ppermute | solution.py:123
  89.6 10.5 %collective-permute-done.8.q3_two = bf16[512,512]{1,0:T(8,128)(2,1)S(1)} collective-permute-done((bf16[512,512]{1,0:T(8,128)(2,1)S(1)}, bf16[512,512]{1,0:T(8,128)(2,1)S(1)}, u32[]{:S(2)}, u32[]{:S(2)}) %collective-permute-start.8) | collective-permute-done | bytes 524320 | tf_op jit(solution)/shard_map/ppermute | solution.py:123
  100.2 1.3 %collective-permute-start.11 = (bf16[512,512]{1,0:T(8,128)(2,1)S(1)}, bf16[512,512]{1,0:T(8,128)(2,1)S(1)}, u32[]{:S(2)}, u32[]{:S(2)}) collective-permute-start(bf16[512,512]{1,0:T(8,128)(2,1)S(1)} %collective-permute-done.8.q3_two), channel_id=1, source_target_pairs={{3,2},{4,5},{11,10},{12,13},{19,18},{20,21},{27,26},{28,29}} | collective-permute-start | bytes 1572872 | tf_op jit(solution)/shard_map/ppermute | solution.py:123
  101.5 2.6 %finish.1 = (bf16[512,2048]{1,0:T(8,128)(2,1)}, f32[1,512]{1,0:T(1,128)S(1)}) custom-call(s32[5]{0:T(128)S(1)} %tick.3.place_ref, bf16[512,2048]{1,0:T(8,128)(2,1)S(1)} %bitcast.12, bf16[512,2048]{1,0:T(8,128)(2,1)S(1)} %bitcast.16, bf16[512,1536]{1,0:T(8,128)(2,1)S(1)} %collective-permute-done.9.refs_0_.q0, ...), custom_call_target="tpu_custom_call" | custom-call | flops 14000000000 | bytes 65536 | tf_op jit(solution)/shard_map/finish/pallas_call | solution.py:584
  104.1 7.3 %collective-permute-done.13.q3_other = bf16[512,1024]{1,0:T(8,128)(2,1)S(1)} collective-permute-done((bf16[512,1024]{1,0:T(8,128)(2,1)S(1)}, bf16[512,1024]{1,0:T(8,128)(2,1)S(1)}, u32[]{:S(2)}, u32[]{:S(2)}) %collective-permute-start.13) | collective-permute-done | bytes 1048608 | tf_op jit(solution)/shard_map/ppermute | solution.py:123
  112.1 3.6 %collective-permute-done.12.q3_last = bf16[512,384]{1,0:T(8,128)(2,1)S(1)} collective-permute-done((bf16[512,384]{1,0:T(8,128)(2,1)S(1)}, bf16[512,384]{1,0:T(8,128)(2,1)S(1)}, u32[]{:S(2)}, u32[]{:S(2)}) %collective-permute-start.12) | collective-permute-done | bytes 393248 | tf_op jit(solution)/shard_map/ppermute | solution.py:123
  (43 shorter events, 21.9 us)
Async XLA Ops:
  0.6 10.7 %copy-start = (bf16[1,512,2048]{2,1,0:T(8,128)(2,1)S(1)}, bf16[1,512,2048]{2,1,0:T(8,128)(2,1)}, u32[]{:S(2)}) copy-start(bf16[1,512,2048]{2,1,0:T(8,128)(2,1)} %param.9) | copy-start | bytes 6291460
  0.6 28.7 %collective-permute-start = (bf16[1,512,2048]{2,1,0:T(8,128)(2,1)}, bf16[1,512,2048]{2,1,0:T(8,128)(2,1)}, u32[]{:S(2)}, u32[]{:S(2)}) collective-permute-start(bf16[1,512,2048]{2,1,0:T(8,128)(2,1)} %param.8), channel_id=1, source_target_pairs={{4,0},{8,4},{12,8},{5,1},{9,5},{13,9},{6,2},{10,6},{14,10},{7,3},{... | collective-permute-start | bytes 6291464 | tf_op jit(solution)/shard_map/ppermute | solution.py:20
  2.7 35.5 %collective-permute-start.4 = (bf16[512,2048]{1,0:T(8,128)(2,1)}, bf16[512,2048]{1,0:T(8,128)(2,1)}, u32[]{:S(2)}, u32[]{:S(2)}) collective-permute-start(bf16[512,2048]{1,0:T(8,128)(2,1)} %bitcast.8), channel_id=1, source_target_pairs={{2,1},{5,6},{10,9},{13,14},{18,17},{21,22},{26,25},{29,30}} | collective-permute-start | bytes 6291464 | tf_op jit(solution)/shard_map/ppermute | solution.py:123
  4.8 36.4 %collective-permute-start.3 = (bf16[512,2048]{1,0:T(8,128)(2,1)}, bf16[512,2048]{1,0:T(8,128)(2,1)}, u32[]{:S(2)}, u32[]{:S(2)}) collective-permute-start(bf16[512,2048]{1,0:T(8,128)(2,1)} %bitcast.9), channel_id=1, source_target_pairs={{0,1},{7,6},{8,9},{15,14},{16,17},{23,22},{24,25},{31,30}} | collective-permute-start | bytes 6291464 | tf_op jit(solution)/shard_map/ppermute | solution.py:123
  8.7 0.7 copy-start.2
  16.0 13.3 %copy-start.1 = (bf16[1,512,2048]{2,1,0:T(8,128)(2,1)S(1)}, bf16[1,512,2048]{2,1,0:T(8,128)(2,1)}, u32[]{:S(2)}) copy-start(bf16[1,512,2048]{2,1,0:T(8,128)(2,1)} %param.7) | copy-start | bytes 6291460
  31.4 23.9 %collective-permute-start.6 = (bf16[512,1408]{1,0:T(8,128)(2,1)S(1)}, bf16[512,1408]{1,0:T(8,128)(2,1)S(1)}, u32[]{:S(2)}, u32[]{:S(2)}) collective-permute-start(bf16[512,1408]{1,0:T(8,128)(2,1)S(1)} %get-tuple-element.37), channel_id=1, source_target_pairs={{0,1},{7,6},{8,9},{15,14},{16,17},{23,22},{24,25},{31,30}} | collective-permute-start | bytes 4325384 | tf_op jit(solution)/shard_map/ppermute | solution.py:123
  32.2 15.6 %collective-permute-start.2 = (bf16[512,896]{1,0:T(8,128)(2,1)S(1)}, bf16[512,896]{1,0:T(8,128)(2,1)S(1)}, u32[]{:S(2)}, u32[]{:S(2)}) collective-permute-start(bf16[512,896]{1,0:T(8,128)(2,1)S(1)} %get-tuple-element.30), channel_id=1, source_target_pairs={{2,1},{5,6},{10,9},{13,14},{18,17},{21,22},{26,25},{29,30}} | collective-permute-start | bytes 2752520 | tf_op jit(solution)/shard_map/ppermute | solution.py:123
  32.9 14.3 %collective-permute-start.1 = (bf16[512,384]{1,0:T(8,128)(2,1)S(1)}, bf16[512,384]{1,0:T(8,128)(2,1)S(1)}, u32[]{:S(2)}, u32[]{:S(2)}) collective-permute-start(bf16[512,384]{1,0:T(8,128)(2,1)S(1)} %get-tuple-element.29), channel_id=1, source_target_pairs={{3,1},{4,6},{11,9},{12,14},{19,17},{20,22},{27,25},{28,30}} | collective-permute-start | bytes 1179656 | tf_op jit(solution)/shard_map/ppermute | solution.py:123
  47.8 19.2 %collective-permute-start.5 = (bf16[256,2048]{1,0:T(8,128)(2,1)S(1)}, bf16[256,2048]{1,0:T(8,128)(2,1)S(1)}, u32[]{:S(2)}, u32[]{:S(2)}) collective-permute-start(bf16[256,2048]{1,0:T(8,128)(2,1)S(1)} %couple.2.coupled_ref.refs_0_), channel_id=1, source_target_pairs={{3,1},{4,6},{11,9},{12,14},{19,17},{20,22},{27,25},{28,30}} | collective-permute-start | bytes 3145736 | tf_op jit(solution)/shard_map/ppermute | solution.py:123
  55.4 22.9 %collective-permute-start.7 = (bf16[256,2048]{1,0:T(8,128)(2,1)S(1)}, bf16[256,2048]{1,0:T(8,128)(2,1)S(1)}, u32[]{:S(2)}, u32[]{:S(2)}) collective-permute-start(bf16[256,2048]{1,0:T(8,128)(2,1)S(1)} %couple.3.coupled_ref.refs_1_), channel_id=1, source_target_pairs={{3,1},{4,6},{11,9},{12,14},{19,17},{20,22},{27,25},{28,30}} | collective-permute-start | bytes 3145736 | tf_op jit(solution)/shard_map/ppermute | solution.py:123
  58.4 27.6 %collective-permute-start.9 = (bf16[512,1536]{1,0:T(8,128)(2,1)S(1)}, bf16[512,1536]{1,0:T(8,128)(2,1)S(1)}, u32[]{:S(2)}, u32[]{:S(2)}) collective-permute-start(bf16[512,1536]{1,0:T(8,128)(2,1)S(1)} %multiply.8.zero_ref.q01), channel_id=1, source_target_pairs={{1,0},{6,7},{9,8},{14,15},{17,16},{22,23},{25,24},{30,31}} | collective-permute-start | bytes 4718600 | tf_op jit(solution)/shard_map/ppermute | solution.py:123
  60.3 41.2 %collective-permute-start.14 = (bf16[512,1408]{1,0:T(8,128)(2,1)S(1)}, bf16[512,1408]{1,0:T(8,128)(2,1)S(1)}, u32[]{:S(2)}, u32[]{:S(2)}) collective-permute-start(bf16[512,1408]{1,0:T(8,128)(2,1)S(1)} %product_two.1.q21), channel_id=1, source_target_pairs={{1,2},{6,5},{9,10},{14,13},{17,18},{22,21},{25,26},{30,29}} | collective-permute-start | bytes 4325384 | tf_op jit(solution)/shard_map/ppermute | solution.py:123
  79.9 8.6 %collective-permute-start.10 = (bf16[512,512]{1,0:T(8,128)(2,1)S(1)}, bf16[512,512]{1,0:T(8,128)(2,1)S(1)}, u32[]{:S(2)}, u32[]{:S(2)}) collective-permute-start(bf16[512,512]{1,0:T(8,128)(2,1)S(1)} %multiply.9.zero_ref), channel_id=1, source_target_pairs={{1,0},{6,7},{9,8},{14,15},{17,16},{22,23},{25,24},{30,31}} | collective-permute-start | bytes 1572872 | tf_op jit(solution)/shard_map/ppermute | solution.py:123
  81.8 18.4 %collective-permute-start.8 = (bf16[512,512]{1,0:T(8,128)(2,1)S(1)}, bf16[512,512]{1,0:T(8,128)(2,1)S(1)}, u32[]{:S(2)}, u32[]{:S(2)}) collective-permute-start(bf16[512,512]{1,0:T(8,128)(2,1)S(1)} %multiply.11), channel_id=1, source_target_pairs={{1,3},{6,4},{9,11},{14,12},{17,19},{22,20},{25,27},{30,28}} | collective-permute-start | bytes 1572872 | tf_op jit(solution)/shard_map/ppermute | solution.py:123
  83.6 27.8 %collective-permute-start.13 = (bf16[512,1024]{1,0:T(8,128)(2,1)S(1)}, bf16[512,1024]{1,0:T(8,128)(2,1)S(1)}, u32[]{:S(2)}, u32[]{:S(2)}) collective-permute-start(bf16[512,1024]{1,0:T(8,128)(2,1)S(1)} %get-tuple-element.48.q31), channel_id=1, source_target_pairs={{1,3},{6,4},{9,11},{14,12},{17,19},{22,20},{25,27},{30,28}} | collective-permute-start | bytes 3145736 | tf_op jit(solution)/shard_map/ppermute | solution.py:123
  86.0 29.6 %collective-permute-start.12 = (bf16[512,384]{1,0:T(8,128)(2,1)S(1)}, bf16[512,384]{1,0:T(8,128)(2,1)S(1)}, u32[]{:S(2)}, u32[]{:S(2)}) collective-permute-start(bf16[512,384]{1,0:T(8,128)(2,1)S(1)} %get-tuple-element.47), channel_id=1, source_target_pairs={{1,3},{6,4},{9,11},{14,12},{17,19},{22,20},{25,27},{30,28}} | collective-permute-start | bytes 1179656 | tf_op jit(solution)/shard_map/ppermute | solution.py:123
  100.2 15.5 %collective-permute-start.11 = (bf16[512,512]{1,0:T(8,128)(2,1)S(1)}, bf16[512,512]{1,0:T(8,128)(2,1)S(1)}, u32[]{:S(2)}, u32[]{:S(2)}) collective-permute-start(bf16[512,512]{1,0:T(8,128)(2,1)S(1)} %collective-permute-done.8.q3_two), channel_id=1, source_target_pairs={{3,2},{4,5},{11,10},{12,13},{19,18},{20,21},{27,26},{28,29}} | collective-permute-start | bytes 1572872 | tf_op jit(solution)/shard_map/ppermute | solution.py:123

commit v19 on v18

--- a/solution.py
+++ b/solution.py
@@ -278,23 +278,25 @@
     )(place, left, right, one)
 
 
-def column_kernel(place_ref, own_ref, first_ref, second_ref, *refs):
+def column_kernel(place_ref, near_ref, other_ref, first_ref, second_ref, *refs):
     column_ref, out_refs = refs[0], refs[1:]
 
     @pl.when(place_ref[1] == 1)
     def _():
-        width = own_ref.shape[0]
-        for block in range(4):
-            rows = pl.ds(block * width, width)
-            column_ref[rows, :] = own_ref[:, rows].T
+        odd = place_ref[0]
+        width = near_ref.shape[0]
+        for half, half_ref in ((1 - odd, near_ref), (odd, other_ref)):
+            for block in range(2):
+                rows = pl.ds(pl.multiple_of((2 * half + block) * width, 128), width)
+                column_ref[rows, :] = half_ref[:, block * width : (block + 1) * width].T
         for left_ref, out_ref in zip((first_ref, second_ref), out_refs):
             out_ref[...] = jnp.dot(
                 left_ref[...], column_ref[...], preferred_element_type=F32
             ).astype(BF16)
 
 
-def own_column(place, own, first, second):
-    rows, nodes = own.shape
+def own_column(place, near, other, first, second):
+    rows, nodes = first.shape
     vmem = pl.BlockSpec(memory_space=pltpu.VMEM)
     return pl.pallas_call(
         column_kernel,
@@ -303,12 +305,12 @@
             jax.ShapeDtypeStruct((rows, rows), BF16),
             jax.ShapeDtypeStruct((rows, rows), BF16),
         ),
-        in_specs=[pl.BlockSpec(memory_space=pltpu.SMEM)] + [vmem] * 3,
+        in_specs=[pl.BlockSpec(memory_space=pltpu.SMEM)] + [vmem] * 4,
         out_specs=(vmem, vmem, vmem),
         compiler_params=pltpu.CompilerParams(vmem_limit_bytes=6 * MIB),
         cost_estimate=LIGHT,
         name="own_column",
-    )(place, own, first, second)
+    )(place, near, other, first, second)
 
 
 def rest_kernel(place_ref, upper_ref, lower_ref, right_ref, zero_ref, out_ref, last_ref):
@@ -389,74 +391,108 @@
         out_ref[...] = sigma_ref[...]
 
 
-def parts_kernel(place_ref, shifted_ref, sigma_ref, row_ref, far_ref, near_ref, last_ref):
+def halves_kernel(place_ref, first_ref, second_ref, near_ref, other_ref):
+    near_ref[...] = first_ref[...]
+    other_ref[...] = second_ref[...]
+
+
+def halves(place, separator):
+    rows, nodes = separator.shape
+    chunk = rows // 4
+    half = lambda side: pl.BlockSpec((chunk, nodes // 2), lambda i, place: (i, side(place[0])))
+    out = jax.ShapeDtypeStruct((rows, nodes // 2), BF16)
+    return pl.pallas_call(
+        halves_kernel,
+        out_shape=(out, out),
+        grid_spec=pltpu.PrefetchScalarGridSpec(
+            num_scalar_prefetch=1,
+            grid=(4,),
+            in_specs=[half(lambda odd: odd), half(lambda odd: 1 - odd)],
+            out_specs=(half(lambda odd: 0), half(lambda odd: 0)),
+        ),
+        compiler_params=pltpu.CompilerParams(vmem_limit_bytes=6 * MIB),
+        cost_estimate=LIGHT,
+        name="halves",
+    )(place, separator, separator)
+
+
+def near_kernel(place_ref, shifted_ref, sigma_ref, row_ref, near_ref, last_ref):
     odd = place_ref[0]
-    width = row_ref.shape[1] // 4
-
-    def at(block, count=1):
-        return pl.ds(pl.multiple_of(block * width, 128), count * width)
-
+    width = row_ref.shape[1] // 2
     prior_kernel(place_ref, shifted_ref, sigma_ref, row_ref)
-    far_ref[:, : 2 * width] = row_ref[:, at(2 - 2 * odd, 2)]
-    near_ref[:, :width] = row_ref[:, at(3 - 3 * odd)]
+    two = pl.ds(pl.multiple_of(odd * width, 128), width)
+    three = pl.ds(pl.multiple_of((1 - odd) * width, 128), width)
+    near_ref[:, :width] = row_ref[:, three]
     for part in range(4):
 
         @pl.when(pl.program_id(0) == part)
         def _():
-            pack_rows(part, row_ref[:, at(3 * odd)], far_ref, 2 * width)
-            pack_rows(part, row_ref[:, at(2 - odd)], near_ref, width)
-            pack_rows(part, row_ref[:, at(3 - 3 * odd)], last_ref, 0)
-
-
-def prior_parts(place, shifted, sigma):
+            pack_rows(part, row_ref[:, two], near_ref, width)
+            pack_rows(part, row_ref[:, three], last_ref, 0)
+
+
+def other_half_kernel(place_ref, shifted_ref, sigma_ref, row_ref, far_ref):
+    width = row_ref.shape[1] // 2
+    prior_kernel(place_ref, shifted_ref, sigma_ref, row_ref)
+    zero = pl.ds(pl.multiple_of(place_ref[0] * width, 128), width)
+    for part in range(4):
+
+        @pl.when(pl.program_id(0) == part)
+        def _():
+            pack_rows(part, row_ref[:, zero], far_ref, 0)
+
+
+def prior_half(kernel, side, sent, place, shifted, sigma):
     rows, nodes = sigma.shape
     chunk = rows // 4
-    width = nodes // 4
-    out = lambda quarters: jax.ShapeDtypeStruct((rows, quarters * width // 4), BF16)
-    spec = lambda quarters: pl.BlockSpec((chunk, quarters * width // 4), lambda i, place: (i, 0))
-    return pl.pallas_call(
-        parts_kernel,
-        out_shape=(out(16), out(11), out(7), out(3)),
+    quarters = (8,) + sent
+    out = lambda count: jax.ShapeDtypeStruct((rows, count * nodes // 16), BF16)
+    spec = lambda count: pl.BlockSpec((chunk, count * nodes // 16), lambda i, place: (i, 0))
+    return pl.pallas_call(
+        kernel,
+        out_shape=tuple(out(count) for count in quarters),
         grid_spec=pltpu.PrefetchScalarGridSpec(
             num_scalar_prefetch=1,
-            grid=(rows // chunk,),
+            grid=(4,),
             in_specs=[
                 pl.BlockSpec(
-                    (chunk, nodes), lambda i, place: (jnp.where(place[3] == 0, i, 0), 0)
+                    (chunk, nodes // 2), lambda i, place: (jnp.where(place[3] == 0, i, 0), 0)
                 ),
                 pl.BlockSpec(
-                    (chunk, nodes), lambda i, place: (jnp.where(place[3] == 0, 0, i), 0)
+                    (chunk, nodes // 2),
+                    lambda i, place: (jnp.where(place[3] == 0, 0, i), side(place[0])),
                 ),
             ],
-            out_specs=(spec(16), spec(11), spec(7), spec(3)),
-        ),
-        compiler_params=pltpu.CompilerParams(vmem_limit_bytes=8 * MIB),
-        cost_estimate=LIGHT,
-        name="prior_parts",
+            out_specs=tuple(spec(count) for count in quarters),
+        ),
+        compiler_params=pltpu.CompilerParams(vmem_limit_bytes=6 * MIB),
+        cost_estimate=LIGHT,
+        name="prior_half",
     )(place, shifted, sigma)
 
 
-def assemble_kernel(place_ref, own, column, near_two, last_three, far_zero, out_ref):
+def assemble_kernel(place_ref, near, other, column, near_two, last_three, near_zero, far_zero, out_ref):
     @pl.when(place_ref[1] == 1)
     def _():
         odd = place_ref[0]
-        width = own.shape[0]
+        width = near.shape[0]
         half, quarter = width // 2, width // 4
 
         def at(block, count=1):
             return pl.ds(pl.multiple_of(block * width, 128), count * width)
 
-        near = 2 * (1 - odd)
+        first = 2 * (1 - odd)
         row = [turned(block, odd) for block in range(4)]
-        out_ref[at(row[1]), :] = own[...]
+        out_ref[at(row[1]), at(first, 2)] = near[...]
+        out_ref[at(row[1]), at(2 * odd, 2)] = other[...]
         out_ref[at(row[2]), at(row[3])] = near_two[:, :width]
         out_ref[at(row[3]), at(row[2])] = near_two[:, :width].T
-        out_ref[at(row[0]), at(near, 2)] = far_zero[:, : 2 * width]
+        out_ref[at(row[0]), at(first, 2)] = near_zero[...]
         for step in range(2):
-            out_ref[at(near + step), at(row[0])] = far_zero[:, step * width : (1 + step) * width].T
+            out_ref[at(first + step), at(row[0])] = near_zero[:, step * width : (1 + step) * width].T
         for block in (0, 2, 3):
             out_ref[at(row[block]), at(row[1])] = column[at(row[block]), :]
-        packed = ((0, far_zero, 2 * width), (2, near_two, width), (3, last_three, 0))
+        packed = ((0, far_zero, 0), (2, near_two, width), (3, last_three, 0))
         for block, packed_ref, start in packed:
             for part in range(4):
                 rows = pl.ds(pl.multiple_of(row[block] * width + part * quarter, 128), quarter)
@@ -466,12 +502,12 @@
 
 
 def assemble(place, *parts):
-    nodes = parts[0].shape[1]
+    nodes = 2 * parts[0].shape[1]
     vmem = pl.BlockSpec(memory_space=pltpu.VMEM)
     return pl.pallas_call(
         assemble_kernel,
         out_shape=jax.ShapeDtypeStruct((nodes, nodes), BF16),
-        in_specs=[pl.BlockSpec(memory_space=pltpu.SMEM)] + [vmem] * 5,
+        in_specs=[pl.BlockSpec(memory_space=pltpu.SMEM)] + [vmem] * 7,
         out_specs=vmem,
         compiler_params=pltpu.CompilerParams(vmem_limit_bytes=6 * MIB),
         cost_estimate=LIGHT,
@@ -736,7 +772,6 @@
     place = jnp.stack([odd, turned(col, odd), col, step, step < lengths[0]]).astype(jnp.int32)
     after = lambda value, *others: lax.optimization_barrier((value, *others))[0]
 
-    shifted = passed_along(separator, "dom", -1)[0]
     p2 = moved(pivot, 2, 1)
     p0 = moved(pivot, 0, 1)
     weights = coupling(node_class)
@@ -744,19 +779,29 @@
     across = turn(place, 1, 0, c1[0], None)
     across = turn(place, 1, 1, c1[1], across)
 
-    row, far, near, last = prior_parts(place, after(shifted, across), sigma)
-    far_zero, near_two, last_three = moved(far, 0, 1), moved(near, 2, 1), moved(last, 3, 1)
+    near, other = halves(place, separator[0])
+    near, other = passed_along(near, "dom", -1), passed_along(other, "dom", -1)
+    sides = (lambda odd: 1 - odd, lambda odd: odd)
+    row_near, near, last = prior_half(
+        near_kernel, sides[0], (7, 3), place, after(near, across), sigma
+    )
+    near_zero, near_two = moved(row_near, 0, 1), moved(near, 2, 1)
+    last_three = moved(last, 3, 1)
+    row_other, far = prior_half(
+        other_half_kernel, sides[1], (3,), place, after(other, p0, p2), sigma
+    )
+    far_zero = moved(far, 0, 1)
 
     c2 = couple_here(place, after(p2, last), weights, coupling_rate)
     across = turn(place, 2, 0, c2, across)
     c0 = couple_here(place, after(p0, across), weights, coupling_rate)
     across = turn(place, 0, 0, c0, across)
-    column, h0_one, h2_one = own_column(place, after(row, last_three), c0, c2)
+    column, h0_one, h2_one = own_column(place, row_near, row_other, c0, c2)
     c3 = [
-        moved(after(c1[0], last_three, near_two, across), 3, 1),
+        moved(after(c1[0], last_three, near_two, near_zero, across), 3, 1),
         moved(after(c1[1], far_zero, h2_one), 3, 1),
     ]
-    prior = assemble(place, row, column, near_two, last_three, far_zero)
+    prior = assemble(place, row_near, row_other, column, near_two, last_three, near_zero, far_zero)
 
     h0 = half_product(place, c0, prior, h0_one)
     q0_own = multiply(place, [h0], across, lambda odd: odd, 3)

time: 119 us -> 121 us (1.017); the launches traced: 117 us -> 121 us
  starting transfers between devices: 29.2 us -> 34.2 us
  waiting for transfers between devices: 52.8 us -> 49.1 us
  Pallas kernels: 31 us -> 32.7 us
    ppermute x1 -> x2, starting transfers between devices: 2.1 us -> 8.78 us  [passed_along(): lax.ppermute(value, axis, [(source, source + steps) for source in range(i...]
    ppermute x14 -> x15, waiting for transfers between devices: 40.4 us -> 36.8 us  [moved(): lax.ppermute(value, ('dom', 'col'), route(source, target, lax.axis_size('...]
    ppermute x14 -> x15, starting transfers between devices: 27.1 us -> 25.5 us  [moved(): lax.ppermute(value, ('dom', 'col'), route(source, target, lax.axis_size('...]
    pallas_call x1 -> x3, Pallas kernels: 2.12 us -> 2.98 us  [the longest x2 2.01 us: prior_half(): pl.pallas_call(kernel, out_shape=tuple((out(count) for count in quarters)...]
    ppermute x1 -> x2, waiting for transfers between devices: 12.4 us -> 12.3 us  [passed_along(): lax.ppermute(value, axis, [(source, source + steps) for source in range(i...]
  transfers between devices with their start and end apart: 15 -> 17, of which waited for: 7 -> 8; matrix products, arithmetic and copies ran while one was open for 0% -> 0% of each run, Pallas kernels for 25% -> 25%
where the time goes in v19:
time: 121 us
  waiting for transfers between devices  49.1 us (41%)
  starting transfers between devices  34.2 us (28%)
  Pallas kernels  32.7 us (27%)
  between operations  3.19 us (3%)
  local copies, waits for them, and re-layouts  1.69 us (1%)
    ppermute x15, waiting for transfers between devices, moved(): lax.ppermute(value, ('dom', 'col'), route(source, target, lax.axis_size('...  36.8 us
    ppermute x15, starting transfers between devices, moved(): lax.ppermute(value, ('dom', 'col'), route(source, target, lax.axis_size('...  25.5 us
    ppermute x2, waiting for transfers between devices, passed_along(): lax.ppermute(value, axis, [(source, source + steps) for source in range(i...  12.3 us
    ppermute x2, starting transfers between devices, passed_along(): lax.ppermute(value, axis, [(source, source + steps) for source in range(i...  8.78 us
    pallas_call x6, Pallas kernels, turn(): pl.pallas_call(turn_kernel, out_shape=jax.ShapeDtypeStruct((nodes, nodes)...  5.99 us
    pallas_call x7, Pallas kernels, multiply(): pl.pallas_call(functools.partial(multiply_kernel, first, count, len(lefts...  4.03 us
    pallas_call x2, Pallas kernels, couple(): pl.pallas_call(functools.partial(couple_kernel, part * rows), out_shape=j...  3.73 us
    pallas_call x1, Pallas kernels, finish(): pl.pallas_call(finish_kernel, out_shape=(jax.ShapeDtypeStruct((rows, node...  2.6 us
  transfers between devices with their start and end apart: 17, of which 8 were waited for; matrix products, arithmetic and copies ran while one was open for 0% of the time, Pallas kernels for 25%

profile of v19, /device:TPU:1, one launch (start us, length us, event | category | flops | bytes accessed | tf_op | source)
XLA Modules:
  0.0 120.9 jit_solution(12104930271746179738)
XLA Ops:
  1.4 2.0 %collective-permute-start.4 = (bf16[512,2048]{1,0:T(8,128)(2,1)}, bf16[512,2048]{1,0:T(8,128)(2,1)}, u32[]{:S(2)}, u32[]{:S(2)}) collective-permute-start(bf16[512,2048]{1,0:T(8,128)(2,1)} %bitcast.9), channel_id=1, source_target_pairs={{0,1},{7,6},{8,9},{15,14},{16,17},{23,22},{24,25},{31,30}} | collective-permute-start | bytes 6291464 | tf_op jit(solution)/shard_map/ppermute | solution.py:123
  4.8 1.6 %copy-done.1 = bf16[1,512,2048]{2,1,0:T(8,128)(2,1)S(1)} copy-done((bf16[1,512,2048]{2,1,0:T(8,128)(2,1)S(1)}, bf16[1,512,2048]{2,1,0:T(8,128)(2,1)}, u32[]{:S(2)}) %copy-start.1) | copy-done | bytes 2097176
  7.4 6.9 %collective-permute-start = (bf16[512,1024]{1,0:T(8,128)(2,1)S(1)}, bf16[512,1024]{1,0:T(8,128)(2,1)S(1)}, u32[]{:S(2)}, u32[]{:S(2)}) collective-permute-start(bf16[512,1024]{1,0:T(8,128)(2,1)S(1)} %get-tuple-element.31), channel_id=1, source_target_pairs={{4,0},{8,4},{12,8},{5,1},{9,5},{13,9},{6,2},{10,6},{14,10},{7,3},{... | collective-permute-start | bytes 3145736 | tf_op jit(solution)/shard_map/ppermute | solution.py:20
  14.3 1.9 %collective-permute-start.7 = (bf16[512,1024]{1,0:T(8,128)(2,1)S(1)}, bf16[512,1024]{1,0:T(8,128)(2,1)S(1)}, u32[]{:S(2)}, u32[]{:S(2)}) collective-permute-start(bf16[512,1024]{1,0:T(8,128)(2,1)S(1)} %get-tuple-element.39), channel_id=1, source_target_pairs={{4,0},{8,4},{12,8},{5,1},{9,5},{13,9},{6,2},{10,6},{14,10},{7,3},{... | collective-permute-start | bytes 3145736 | tf_op jit(solution)/shard_map/ppermute | solution.py:20
  16.9 1.8 %coupling.1.weight_ref.refs_1_ = bf16[8,512,256]{2,1,0:T(8,128)(2,1)S(1)} custom-call(s32[1,2048]{1,0:T(1,128)S(1)} %bitcast.20), custom_call_target="tpu_custom_call" | custom-call | flops 1048576 | bytes 65536 | tf_op jit(solution)/shard_map/coupling/pallas_call | solution.py:70
  18.7 1.9 %couple.3.coupled_ref.refs_1_ = bf16[256,2048]{1,0:T(8,128)(2,1)S(1)} custom-call(f32[1]{0:T(128)S(6)} %copy.23.rate_ref.refs_0_, bf16[8,512,256]{2,1,0:T(8,128)(2,1)S(1)} %coupling.1.weight_ref.refs_1_, bf16[512,2048]{1,0:T(8,128)(2,1)S(1)} %bitcast.10), custom_call_target="tpu_custom_call" | custom-call | flops 1048576 | bytes 65536 | tf_op jit(solution)/shard_map/couple/pallas_call | solution.py:99
  20.6 1.9 %couple.2.coupled_ref.refs_0_ = bf16[256,2048]{1,0:T(8,128)(2,1)S(1)} custom-call(f32[1]{0:T(128)S(6)} %copy.23.rate_ref.refs_0_, bf16[8,512,256]{2,1,0:T(8,128)(2,1)S(1)} %coupling.1.weight_ref.refs_1_, bf16[512,2048]{1,0:T(8,128)(2,1)S(1)} %bitcast.11), custom_call_target="tpu_custom_call" | custom-call | flops 1048576 | bytes 65536 | tf_op jit(solution)/shard_map/couple/pallas_call | solution.py:99
  24.3 3.6 %collective-permute-done.shifted_ref = bf16[512,1024]{1,0:T(8,128)(2,1)S(1)} collective-permute-done((bf16[512,1024]{1,0:T(8,128)(2,1)S(1)}, bf16[512,1024]{1,0:T(8,128)(2,1)S(1)}, u32[]{:S(2)}, u32[]{:S(2)}) %collective-permute-start) | collective-permute-done | bytes 1048608 | tf_op jit(solution)/shard_map/ppermute | solution.py:20
  30.3 8.7 %collective-permute-done.7.shifted_ref = bf16[512,1024]{1,0:T(8,128)(2,1)S(1)} collective-permute-done((bf16[512,1024]{1,0:T(8,128)(2,1)S(1)}, bf16[512,1024]{1,0:T(8,128)(2,1)S(1)}, u32[]{:S(2)}, u32[]{:S(2)}) %collective-permute-start.7) | collective-permute-done | bytes 1048608 | tf_op jit(solution)/shard_map/ppermute | solution.py:20
  39.1 2.6 %collective-permute-start.1 = (bf16[512,384]{1,0:T(8,128)(2,1)S(1)}, bf16[512,384]{1,0:T(8,128)(2,1)S(1)}, u32[]{:S(2)}, u32[]{:S(2)}) collective-permute-start(bf16[512,384]{1,0:T(8,128)(2,1)S(1)} %get-tuple-element.33), channel_id=1, source_target_pairs={{3,1},{4,6},{11,9},{12,14},{19,17},{20,22},{27,25},{28,30}} | collective-permute-start | bytes 1179656 | tf_op jit(solution)/shard_map/ppermute | solution.py:123
  45.2 1.6 %couple_here.3.coupled_ref.first_ref.left_ref = bf16[512,2048]{1,0:T(8,128)(2,1)S(1)} custom-call(s32[5]{0:T(128)S(1)} %stack.16.place_ref, f32[1]{0:T(128)S(6)} %copy.23.rate_ref.refs_0_, bf16[8,512,256]{2,1,0:T(8,128)(2,1)S(1)} %coupling.1.weight_ref.refs_1_, bf16[512,2048]{1,0:T(8,128)(2,1)} %collective-permute-done.4.refs_2_), custom_call_target="tpu_custom_call" | custom-call | flops 1048576 | bytes 65536 | tf_op jit(solution)/shard_map/couple_here/pallas_call | solution.py:133
  48.0 1.9 %collective-permute-done.1.last_three = bf16[512,384]{1,0:T(8,128)(2,1)S(1)} collective-permute-done((bf16[512,384]{1,0:T(8,128)(2,1)S(1)}, bf16[512,384]{1,0:T(8,128)(2,1)S(1)}, u32[]{:S(2)}, u32[]{:S(2)}) %collective-permute-start.1) | collective-permute-done | bytes 393248 | tf_op jit(solution)/shard_map/ppermute | solution.py:123
  49.9 6.3 %collective-permute-start.6 = (bf16[256,2048]{1,0:T(8,128)(2,1)S(1)}, bf16[256,2048]{1,0:T(8,128)(2,1)S(1)}, u32[]{:S(2)}, u32[]{:S(2)}) collective-permute-start(bf16[256,2048]{1,0:T(8,128)(2,1)S(1)} %couple.2.coupled_ref.refs_0_), channel_id=1, source_target_pairs={{3,1},{4,6},{11,9},{12,14},{19,17},{20,22},{27,25},{28,30}} | collective-permute-start | bytes 3145736 | tf_op jit(solution)/shard_map/ppermute | solution.py:123
  56.9 4.2 %collective-permute-start.9 = (bf16[256,2048]{1,0:T(8,128)(2,1)S(1)}, bf16[256,2048]{1,0:T(8,128)(2,1)S(1)}, u32[]{:S(2)}, u32[]{:S(2)}) collective-permute-start(bf16[256,2048]{1,0:T(8,128)(2,1)S(1)} %couple.3.coupled_ref.refs_1_), channel_id=1, source_target_pairs={{3,1},{4,6},{11,9},{12,14},{19,17},{20,22},{27,25},{28,30}} | collective-permute-start | bytes 3145736 | tf_op jit(solution)/shard_map/ppermute | solution.py:123
  65.4 2.6 %collective-permute-done.6.refs_0_.coupled_ref = bf16[256,2048]{1,0:T(8,128)(2,1)S(1)} collective-permute-done((bf16[256,2048]{1,0:T(8,128)(2,1)S(1)}, bf16[256,2048]{1,0:T(8,128)(2,1)S(1)}, u32[]{:S(2)}, u32[]{:S(2)}) %collective-permute-start.6) | collective-permute-done | bytes 1048608 | tf_op jit(solution)/shard_map/ppermute | solution.py:123
  69.6 9.6 %collective-permute-done.9.coupled_ref.refs_0_ = bf16[256,2048]{1,0:T(8,128)(2,1)S(1)} collective-permute-done((bf16[256,2048]{1,0:T(8,128)(2,1)S(1)}, bf16[256,2048]{1,0:T(8,128)(2,1)S(1)}, u32[]{:S(2)}, u32[]{:S(2)}) %collective-permute-start.9) | collective-permute-done | bytes 1048608 | tf_op jit(solution)/shard_map/ppermute | solution.py:123
  82.5 1.3 %collective-permute-start.10 = (bf16[512,512]{1,0:T(8,128)(2,1)S(1)}, bf16[512,512]{1,0:T(8,128)(2,1)S(1)}, u32[]{:S(2)}, u32[]{:S(2)}) collective-permute-start(bf16[512,512]{1,0:T(8,128)(2,1)S(1)} %multiply.11), channel_id=1, source_target_pairs={{1,3},{6,4},{9,11},{14,12},{17,19},{22,20},{25,27},{30,28}} | collective-permute-start | bytes 1572872 | tf_op jit(solution)/shard_map/ppermute | solution.py:123
  90.4 12.8 %collective-permute-done.10.q3_two = bf16[512,512]{1,0:T(8,128)(2,1)S(1)} collective-permute-done((bf16[512,512]{1,0:T(8,128)(2,1)S(1)}, bf16[512,512]{1,0:T(8,128)(2,1)S(1)}, u32[]{:S(2)}, u32[]{:S(2)}) %collective-permute-start.10) | collective-permute-done | bytes 524320 | tf_op jit(solution)/shard_map/ppermute | solution.py:123
  103.2 1.3 %collective-permute-start.13 = (bf16[512,512]{1,0:T(8,128)(2,1)S(1)}, bf16[512,512]{1,0:T(8,128)(2,1)S(1)}, u32[]{:S(2)}, u32[]{:S(2)}) collective-permute-start(bf16[512,512]{1,0:T(8,128)(2,1)S(1)} %collective-permute-done.10.q3_two), channel_id=1, source_target_pairs={{3,2},{4,5},{11,10},{12,13},{19,18},{20,21},{27,26},{28,29}} | collective-permute-start | bytes 1572872 | tf_op jit(solution)/shard_map/ppermute | solution.py:123
  104.5 2.6 %finish.1 = (bf16[512,2048]{1,0:T(8,128)(2,1)}, f32[1,512]{1,0:T(1,128)S(1)}) custom-call(s32[5]{0:T(128)S(1)} %tick.3.place_ref, bf16[512,2048]{1,0:T(8,128)(2,1)S(1)} %bitcast.12, bf16[512,2048]{1,0:T(8,128)(2,1)S(1)} %bitcast.19, bf16[512,1536]{1,0:T(8,128)(2,1)S(1)} %collective-permute-done.11.refs_0_.q0, ...), custom_call_target="tpu_custom_call" | custom-call | flops 14000000000 | bytes 65536 | tf_op jit(solution)/shard_map/finish/pallas_call | solution.py:620
  107.1 7.3 %collective-permute-done.15.q3_other = bf16[512,1024]{1,0:T(8,128)(2,1)S(1)} collective-permute-done((bf16[512,1024]{1,0:T(8,128)(2,1)S(1)}, bf16[512,1024]{1,0:T(8,128)(2,1)S(1)}, u32[]{:S(2)}, u32[]{:S(2)}) %collective-permute-start.15) | collective-permute-done | bytes 1048608 | tf_op jit(solution)/shard_map/ppermute | solution.py:123
  114.4 1.7 %finish_other.1.old_ref = bf16[512,2048]{1,0:T(8,128)(2,1)} custom-call(s32[5]{0:T(128)S(1)} %stack.16.place_ref, bf16[512,2048]{1,0:T(8,128)(2,1)S(1)} %bitcast.13, bf16[512,1024]{1,0:T(8,128)(2,1)S(1)} %collective-permute-done.15.q3_other, bf16[512,2048]{1,0:T(8,128)(2,1)} %get-tuple-element.56.old_ref), custom_call_target="tpu_custom_call", output_to_operand_aliasing={{}: (3, {})} | custom-call | flops 1048576 | bytes 65536 | tf_op jit(solution)/shard_map/finish_other/pallas_call | solution.py:716
  116.1 2.5 %collective-permute-done.14.q3_last = bf16[512,384]{1,0:T(8,128)(2,1)S(1)} collective-permute-done((bf16[512,384]{1,0:T(8,128)(2,1)S(1)}, bf16[512,384]{1,0:T(8,128)(2,1)S(1)}, u32[]{:S(2)}, u32[]{:S(2)}) %collective-permute-start.14) | collective-permute-done | bytes 393248 | tf_op jit(solution)/shard_map/ppermute | solution.py:123
  118.7 2.1 %finish_last.1 = (bf16[512,2048]{1,0:T(8,128)(2,1)}, f32[1,512]{1,0:T(1,128)}) custom-call(s32[5]{0:T(128)S(1)} %stack.16.place_ref, bf16[512,2048]{1,0:T(8,128)(2,1)S(1)} %bitcast.14, bf16[512,512]{1,0:T(8,128)(2,1)S(1)} %collective-permute-done.13.q2_last, bf16[512,384]{1,0:T(8,128)(2,1)S(1)} %collective-permute-done.14.q3_last, ...), custom_call_target="tpu_custom_call", output_to_operand_aliasing={{0}: (4, {})} | custom-call | flops 1048576 | bytes 65536 | tf_op jit(solution)/shard_map/finish_last/pallas_call | solution.py:741
  (51 shorter events, 27.0 us)
Async XLA Ops:
  0.6 41.1 %collective-permute-start.5 = (bf16[512,2048]{1,0:T(8,128)(2,1)}, bf16[512,2048]{1,0:T(8,128)(2,1)S(1)}, u32[]{:S(2)}, u32[]{:S(2)}) collective-permute-start(bf16[512,2048]{1,0:T(8,128)(2,1)} %bitcast.8), channel_id=1, source_target_pairs={{2,1},{5,6},{10,9},{13,14},{18,17},{21,22},{26,25},{29,30}} | collective-permute-start | bytes 6291464 | tf_op jit(solution)/shard_map/ppermute | solution.py:123
  1.4 40.3 %collective-permute-start.4 = (bf16[512,2048]{1,0:T(8,128)(2,1)}, bf16[512,2048]{1,0:T(8,128)(2,1)}, u32[]{:S(2)}, u32[]{:S(2)}) collective-permute-start(bf16[512,2048]{1,0:T(8,128)(2,1)} %bitcast.9), channel_id=1, source_target_pairs={{0,1},{7,6},{8,9},{15,14},{16,17},{23,22},{24,25},{31,30}} | collective-permute-start | bytes 6291464 | tf_op jit(solution)/shard_map/ppermute | solution.py:123
  4.8 1.6 %copy-start.1 = (bf16[1,512,2048]{2,1,0:T(8,128)(2,1)S(1)}, bf16[1,512,2048]{2,1,0:T(8,128)(2,1)}, u32[]{:S(2)}) copy-start(bf16[1,512,2048]{2,1,0:T(8,128)(2,1)} %param.8) | copy-start | bytes 6291460
  6.4 10.4 %copy-start.3 = (s32[2048]{0:T(1024)S(1)}, s32[2048]{0:T(1024)}, u32[]{:S(2)}) copy-start(s32[2048]{0:T(1024)} %param.13) | copy-start | bytes 24580
  7.4 11.3 %copy-start = (bf16[1,512,2048]{2,1,0:T(8,128)(2,1)S(1)}, bf16[1,512,2048]{2,1,0:T(8,128)(2,1)}, u32[]{:S(2)}) copy-start(bf16[1,512,2048]{2,1,0:T(8,128)(2,1)} %param.9) | copy-start | bytes 6291460
  7.4 20.4 %collective-permute-start = (bf16[512,1024]{1,0:T(8,128)(2,1)S(1)}, bf16[512,1024]{1,0:T(8,128)(2,1)S(1)}, u32[]{:S(2)}, u32[]{:S(2)}) collective-permute-start(bf16[512,1024]{1,0:T(8,128)(2,1)S(1)} %get-tuple-element.31), channel_id=1, source_target_pairs={{4,0},{8,4},{12,8},{5,1},{9,5},{13,9},{6,2},{10,6},{14,10},{7,3},{... | collective-permute-start | bytes 3145736 | tf_op jit(solution)/shard_map/ppermute | solution.py:20
  14.3 24.8 %collective-permute-start.7 = (bf16[512,1024]{1,0:T(8,128)(2,1)S(1)}, bf16[512,1024]{1,0:T(8,128)(2,1)S(1)}, u32[]{:S(2)}, u32[]{:S(2)}) collective-permute-start(bf16[512,1024]{1,0:T(8,128)(2,1)S(1)} %get-tuple-element.39), channel_id=1, source_target_pairs={{4,0},{8,4},{12,8},{5,1},{9,5},{13,9},{6,2},{10,6},{14,10},{7,3},{... | collective-permute-start | bytes 3145736 | tf_op jit(solution)/shard_map/ppermute | solution.py:20
  23.4 4.5 %copy-start.2 = (bf16[1,512,2048]{2,1,0:T(8,128)(2,1)S(1)}, bf16[1,512,2048]{2,1,0:T(8,128)(2,1)}, u32[]{:S(2)}) copy-start(bf16[1,512,2048]{2,1,0:T(8,128)(2,1)} %param.7) | copy-start | bytes 6291460
  28.9 21.1 %collective-permute-start.3 = (bf16[512,1024]{1,0:T(8,128)(2,1)S(1)}, bf16[512,1024]{1,0:T(8,128)(2,1)S(1)}, u32[]{:S(2)}, u32[]{:S(2)}) collective-permute-start(bf16[512,1024]{1,0:T(8,128)(2,1)S(1)} %get-tuple-element.35.near_ref.near), channel_id=1, source_target_pairs={{0,1},{7,6},{8,9},{15,14},{16,17},{23,22},{24,25},{31,30}} | collective-permute-start | bytes 3145736 | tf_op jit(solution)/shard_map/ppermute | solution.py:123
  29.6 20.3 %collective-permute-start.2 = (bf16[512,896]{1,0:T(8,128)(2,1)S(1)}, bf16[512,896]{1,0:T(8,128)(2,1)S(1)}, u32[]{:S(2)}, u32[]{:S(2)}) collective-permute-start(bf16[512,896]{1,0:T(8,128)(2,1)S(1)} %get-tuple-element.34), channel_id=1, source_target_pairs={{2,1},{5,6},{10,9},{13,14},{18,17},{21,22},{26,25},{29,30}} | collective-permute-start | bytes 2752520 | tf_op jit(solution)/shard_map/ppermute | solution.py:123
  39.1 10.9 %collective-permute-start.1 = (bf16[512,384]{1,0:T(8,128)(2,1)S(1)}, bf16[512,384]{1,0:T(8,128)(2,1)S(1)}, u32[]{:S(2)}, u32[]{:S(2)}) collective-permute-start(bf16[512,384]{1,0:T(8,128)(2,1)S(1)} %get-tuple-element.33), channel_id=1, source_target_pairs={{3,1},{4,6},{11,9},{12,14},{19,17},{20,22},{27,25},{28,30}} | collective-permute-start | bytes 1179656 | tf_op jit(solution)/shard_map/ppermute | solution.py:123
  42.7 14.2 %collective-permute-start.8 = (bf16[512,384]{1,0:T(8,128)(2,1)S(1)}, bf16[512,384]{1,0:T(8,128)(2,1)S(1)}, u32[]{:S(2)}, u32[]{:S(2)}) collective-permute-start(bf16[512,384]{1,0:T(8,128)(2,1)S(1)} %get-tuple-element.43), channel_id=1, source_target_pairs={{0,1},{7,6},{8,9},{15,14},{16,17},{23,22},{24,25},{31,30}} | collective-permute-start | bytes 1179656 | tf_op jit(solution)/shard_map/ppermute | solution.py:123
  49.9 18.0 %collective-permute-start.6 = (bf16[256,2048]{1,0:T(8,128)(2,1)S(1)}, bf16[256,2048]{1,0:T(8,128)(2,1)S(1)}, u32[]{:S(2)}, u32[]{:S(2)}) collective-permute-start(bf16[256,2048]{1,0:T(8,128)(2,1)S(1)} %couple.2.coupled_ref.refs_0_), channel_id=1, source_target_pairs={{3,1},{4,6},{11,9},{12,14},{19,17},{20,22},{27,25},{28,30}} | collective-permute-start | bytes 3145736 | tf_op jit(solution)/shard_map/ppermute | solution.py:123
  56.9 22.4 %collective-permute-start.9 = (bf16[256,2048]{1,0:T(8,128)(2,1)S(1)}, bf16[256,2048]{1,0:T(8,128)(2,1)S(1)}, u32[]{:S(2)}, u32[]{:S(2)}) collective-permute-start(bf16[256,2048]{1,0:T(8,128)(2,1)S(1)} %couple.3.coupled_ref.refs_1_), channel_id=1, source_target_pairs={{3,1},{4,6},{11,9},{12,14},{19,17},{20,22},{27,25},{28,30}} | collective-permute-start | bytes 3145736 | tf_op jit(solution)/shard_map/ppermute | solution.py:123
  62.7 24.0 %collective-permute-start.11 = (bf16[512,1536]{1,0:T(8,128)(2,1)S(1)}, bf16[512,1536]{1,0:T(8,128)(2,1)S(1)}, u32[]{:S(2)}, u32[]{:S(2)}) collective-permute-start(bf16[512,1536]{1,0:T(8,128)(2,1)S(1)} %multiply.8.zero_ref.q01), channel_id=1, source_target_pairs={{1,0},{6,7},{9,8},{14,15},{17,16},{22,23},{25,24},{30,31}} | collective-permute-start | bytes 4718600 | tf_op jit(solution)/shard_map/ppermute | solution.py:123
  64.6 39.9 %collective-permute-start.16 = (bf16[512,1408]{1,0:T(8,128)(2,1)S(1)}, bf16[512,1408]{1,0:T(8,128)(2,1)S(1)}, u32[]{:S(2)}, u32[]{:S(2)}) collective-permute-start(bf16[512,1408]{1,0:T(8,128)(2,1)S(1)} %product_two.1.q21), channel_id=1, source_target_pairs={{1,2},{6,5},{9,10},{14,13},{17,18},{22,21},{25,26},{30,29}} | collective-permute-start | bytes 4325384 | tf_op jit(solution)/shard_map/ppermute | solution.py:123
  80.7 8.6 %collective-permute-start.12 = (bf16[512,512]{1,0:T(8,128)(2,1)S(1)}, bf16[512,512]{1,0:T(8,128)(2,1)S(1)}, u32[]{:S(2)}, u32[]{:S(2)}) collective-permute-start(bf16[512,512]{1,0:T(8,128)(2,1)S(1)} %multiply.9.zero_ref), channel_id=1, source_target_pairs={{1,0},{6,7},{9,8},{14,15},{17,16},{22,23},{25,24},{30,31}} | collective-permute-start | bytes 1572872 | tf_op jit(solution)/shard_map/ppermute | solution.py:123
  82.5 20.7 %collective-permute-start.10 = (bf16[512,512]{1,0:T(8,128)(2,1)S(1)}, bf16[512,512]{1,0:T(8,128)(2,1)S(1)}, u32[]{:S(2)}, u32[]{:S(2)}) collective-permute-start(bf16[512,512]{1,0:T(8,128)(2,1)S(1)} %multiply.11), channel_id=1, source_target_pairs={{1,3},{6,4},{9,11},{14,12},{17,19},{22,20},{25,27},{30,28}} | collective-permute-start | bytes 1572872 | tf_op jit(solution)/shard_map/ppermute | solution.py:123
  84.4 30.1 %collective-permute-start.15 = (bf16[512,1024]{1,0:T(8,128)(2,1)S(1)}, bf16[512,1024]{1,0:T(8,128)(2,1)S(1)}, u32[]{:S(2)}, u32[]{:S(2)}) collective-permute-start(bf16[512,1024]{1,0:T(8,128)(2,1)S(1)} %get-tuple-element.54.q31), channel_id=1, source_target_pairs={{1,3},{6,4},{9,11},{14,12},{17,19},{22,20},{25,27},{30,28}} | collective-permute-start | bytes 3145736 | tf_op jit(solution)/shard_map/ppermute | solution.py:123
  86.8 31.9 %collective-permute-start.14 = (bf16[512,384]{1,0:T(8,128)(2,1)S(1)}, bf16[512,384]{1,0:T(8,128)(2,1)S(1)}, u32[]{:S(2)}, u32[]{:S(2)}) collective-permute-start(bf16[512,384]{1,0:T(8,128)(2,1)S(1)} %get-tuple-element.53), channel_id=1, source_target_pairs={{1,3},{6,4},{9,11},{14,12},{17,19},{22,20},{25,27},{30,28}} | collective-permute-start | bytes 1179656 | tf_op jit(solution)/shard_map/ppermute | solution.py:123
  103.2 15.5 %collective-permute-start.13 = (bf16[512,512]{1,0:T(8,128)(2,1)S(1)}, bf16[512,512]{1,0:T(8,128)(2,1)S(1)}, u32[]{:S(2)}, u32[]{:S(2)}) collective-permute-start(bf16[512,512]{1,0:T(8,128)(2,1)S(1)} %collective-permute-done.10.q3_two), channel_id=1, source_target_pairs={{3,2},{4,5},{11,10},{12,13},{19,18},{20,21},{27,26},{28,29}} | collective-permute-start | bytes 1572872 | tf_op jit(solution)/shard_map/ppermute | solution.py:123

commit v20 on v19

--- a/solution.py
+++ b/solution.py
@@ -787,15 +787,14 @@
     )
     near_zero, near_two = moved(row_near, 0, 1), moved(near, 2, 1)
     last_three = moved(last, 3, 1)
-    row_other, far = prior_half(
-        other_half_kernel, sides[1], (3,), place, after(other, p0, p2), sigma
-    )
-    far_zero = moved(far, 0, 1)
-
     c2 = couple_here(place, after(p2, last), weights, coupling_rate)
     across = turn(place, 2, 0, c2, across)
     c0 = couple_here(place, after(p0, across), weights, coupling_rate)
     across = turn(place, 0, 0, c0, across)
+    row_other, far = prior_half(
+        other_half_kernel, sides[1], (3,), place, after(other, across), sigma
+    )
+    far_zero = moved(far, 0, 1)
     column, h0_one, h2_one = own_column(place, row_near, row_other, c0, c2)
     c3 = [
         moved(after(c1[0], last_three, near_two, near_zero, across), 3, 1),

time: 121 us -> 122 us (level)
  the two profiles are of different devices: /device:TPU:1 before, /device:TPU:6 now
where the time goes in v20:
time: 122 us; the launch traced here: 121 us
  waiting for transfers between devices  53.4 us (44%)
  starting transfers between devices  31.9 us (26%)
  Pallas kernels  31.1 us (25%)
  between operations  3.23 us (3%)
  local copies, waits for them, and re-layouts  1.69 us (1%)
    ppermute x15, waiting for transfers between devices, moved(): lax.ppermute(value, ('dom', 'col'), route(source, target, lax.axis_size('...  51.6 us
    ppermute x15, starting transfers between devices, moved(): lax.ppermute(value, ('dom', 'col'), route(source, target, lax.axis_size('...  27.3 us
    pallas_call x6, Pallas kernels, turn(): pl.pallas_call(turn_kernel, out_shape=jax.ShapeDtypeStruct((nodes, nodes)...  5.99 us
    ppermute x2, starting transfers between devices, passed_along(): lax.ppermute(value, axis, [(source, source + steps) for source in range(i...  4.6 us
    pallas_call x7, Pallas kernels, multiply(): pl.pallas_call(functools.partial(multiply_kernel, first, count, len(lefts...  4.03 us
    pallas_call x2, Pallas kernels, couple(): pl.pallas_call(functools.partial(couple_kernel, part * rows), out_shape=j...  3.77 us
    pallas_call x1, Pallas kernels, finish(): pl.pallas_call(finish_kernel, out_shape=(jax.ShapeDtypeStruct((rows, node...  2.89 us
  transfers between devices with their start and end apart: 17, of which 5 were waited for; matrix products, arithmetic and copies ran while one was open for 0% of the time, Pallas kernels for 25%

profile of v20, /device:TPU:6, one launch (start us, length us, event | category | flops | bytes accessed | tf_op | source)
XLA Modules:
  0.0 121.3 jit_solution(8535534595846947002)
XLA Ops:
  0.6 2.0 %collective-permute-start.5 = (bf16[512,2048]{1,0:T(8,128)(2,1)}, bf16[512,2048]{1,0:T(8,128)(2,1)}, u32[]{:S(2)}, u32[]{:S(2)}) collective-permute-start(bf16[512,2048]{1,0:T(8,128)(2,1)} %bitcast.8), channel_id=1, source_target_pairs={{2,1},{5,6},{10,9},{13,14},{18,17},{21,22},{26,25},{29,30}} | collective-permute-start | bytes 6291464 | tf_op jit(solution)/shard_map/ppermute | solution.py:123
  2.6 2.9 %collective-permute-start.4 = (bf16[512,2048]{1,0:T(8,128)(2,1)}, bf16[512,2048]{1,0:T(8,128)(2,1)S(1)}, u32[]{:S(2)}, u32[]{:S(2)}) collective-permute-start(bf16[512,2048]{1,0:T(8,128)(2,1)} %bitcast.9), channel_id=1, source_target_pairs={{0,1},{7,6},{8,9},{15,14},{16,17},{23,22},{24,25},{31,30}} | collective-permute-start | bytes 6291464 | tf_op jit(solution)/shard_map/ppermute | solution.py:123
  6.9 1.6 %copy-done.1 = bf16[1,512,2048]{2,1,0:T(8,128)(2,1)S(1)} copy-done((bf16[1,512,2048]{2,1,0:T(8,128)(2,1)S(1)}, bf16[1,512,2048]{2,1,0:T(8,128)(2,1)}, u32[]{:S(2)}) %copy-start.1) | copy-done | bytes 2097176
  9.5 2.1 %collective-permute-start = (bf16[512,1024]{1,0:T(8,128)(2,1)S(1)}, bf16[512,1024]{1,0:T(8,128)(2,1)S(1)}, u32[]{:S(2)}, u32[]{:S(2)}) collective-permute-start(bf16[512,1024]{1,0:T(8,128)(2,1)S(1)} %get-tuple-element.31), channel_id=1, source_target_pairs={{4,0},{8,4},{12,8},{5,1},{9,5},{13,9},{6,2},{10,6},{14,10},{7,3},{... | collective-permute-start | bytes 3145736 | tf_op jit(solution)/shard_map/ppermute | solution.py:20
  11.6 2.5 %collective-permute-start.7 = (bf16[512,1024]{1,0:T(8,128)(2,1)S(1)}, bf16[512,1024]{1,0:T(8,128)(2,1)S(1)}, u32[]{:S(2)}, u32[]{:S(2)}) collective-permute-start(bf16[512,1024]{1,0:T(8,128)(2,1)S(1)} %get-tuple-element.39), channel_id=1, source_target_pairs={{4,0},{8,4},{12,8},{5,1},{9,5},{13,9},{6,2},{10,6},{14,10},{7,3},{... | collective-permute-start | bytes 3145736 | tf_op jit(solution)/shard_map/ppermute | solution.py:20
  14.8 1.8 %coupling.1.weight_ref.refs_1_ = bf16[8,512,256]{2,1,0:T(8,128)(2,1)S(1)} custom-call(s32[1,2048]{1,0:T(1,128)S(1)} %bitcast.20), custom_call_target="tpu_custom_call" | custom-call | flops 1048576 | bytes 65536 | tf_op jit(solution)/shard_map/coupling/pallas_call | solution.py:70
  16.7 1.9 %couple.2.coupled_ref.refs_0_ = bf16[256,2048]{1,0:T(8,128)(2,1)S(1)} custom-call(f32[1]{0:T(128)S(6)} %copy.23.rate_ref.refs_0_, bf16[8,512,256]{2,1,0:T(8,128)(2,1)S(1)} %coupling.1.weight_ref.refs_1_, bf16[512,2048]{1,0:T(8,128)(2,1)S(1)} %bitcast.10), custom_call_target="tpu_custom_call" | custom-call | flops 1048576 | bytes 65536 | tf_op jit(solution)/shard_map/couple/pallas_call | solution.py:99
  18.6 1.9 %couple.3.coupled_ref.refs_1_ = bf16[256,2048]{1,0:T(8,128)(2,1)S(1)} custom-call(f32[1]{0:T(128)S(6)} %copy.23.rate_ref.refs_0_, bf16[8,512,256]{2,1,0:T(8,128)(2,1)S(1)} %coupling.1.weight_ref.refs_1_, bf16[512,2048]{1,0:T(8,128)(2,1)S(1)} %bitcast.11), custom_call_target="tpu_custom_call" | custom-call | flops 1048576 | bytes 65536 | tf_op jit(solution)/shard_map/couple/pallas_call | solution.py:99
  22.3 1.6 %collective-permute-done.shifted_ref = bf16[512,1024]{1,0:T(8,128)(2,1)S(1)} collective-permute-done((bf16[512,1024]{1,0:T(8,128)(2,1)S(1)}, bf16[512,1024]{1,0:T(8,128)(2,1)S(1)}, u32[]{:S(2)}, u32[]{:S(2)}) %collective-permute-start) | collective-permute-done | bytes 1048608 | tf_op jit(solution)/shard_map/ppermute | solution.py:20
  23.9 1.0 prior_half.2
  24.9 3.9 %collective-permute-start.3 = (bf16[512,1024]{1,0:T(8,128)(2,1)S(1)}, bf16[512,1024]{1,0:T(8,128)(2,1)S(1)}, u32[]{:S(2)}, u32[]{:S(2)}) collective-permute-start(bf16[512,1024]{1,0:T(8,128)(2,1)S(1)} %get-tuple-element.35.near_ref.near), channel_id=1, source_target_pairs={{0,1},{7,6},{8,9},{15,14},{16,17},{23,22},{24,25},{31,30}} | collective-permute-start | bytes 3145736 | tf_op jit(solution)/shard_map/ppermute | solution.py:123
  30.3 1.6 %couple_here.2.coupled_ref.second_ref.left_ref = bf16[512,2048]{1,0:T(8,128)(2,1)S(1)} custom-call(s32[5]{0:T(128)S(1)} %stack.16.place_ref, f32[1]{0:T(128)S(6)} %copy.23.rate_ref.refs_0_, bf16[8,512,256]{2,1,0:T(8,128)(2,1)S(1)} %coupling.1.weight_ref.refs_1_, bf16[512,2048]{1,0:T(8,128)(2,1)} %collective-permute-done.5.refs_2_), custom_call_target="tpu_custom_call" | custom-call | flops 1048576 | bytes 65536 | tf_op jit(solution)/shard_map/couple_here/pallas_call | solution.py:133
  31.9 1.2 %turn.8.refs_0_ = bf16[2048,2048]{1,0:T(8,128)(2,1)S(1)} custom-call(s32[5]{0:T(128)S(1)} %stack.16.place_ref, bf16[512,2048]{1,0:T(8,128)(2,1)S(1)} %couple_here.2.coupled_ref.second_ref.left_ref, bf16[2048,2048]{1,0:T(8,128)(2,1)S(1)} %turn.7.refs_0_), custom_call_target="tpu_custom_call", output_to_operand_aliasing={{}: (2, {})} | custom-call | flops 1048576 | bytes 65536 | tf_op jit(solution)/shard_map/turn/pallas_call | solution.py:155
  33.7 1.2 %turn.9.refs_1_.right_ref.refs_0_ = bf16[2048,2048]{1,0:T(8,128)(2,1)S(1)} custom-call(s32[5]{0:T(128)S(1)} %stack.16.place_ref, bf16[512,2048]{1,0:T(8,128)(2,1)S(1)} %couple_here.3.coupled_ref.first_ref.left_ref, bf16[2048,2048]{1,0:T(8,128)(2,1)S(1)} %turn.8.refs_0_), custom_call_target="tpu_custom_call", output_to_operand_aliasing={{}: (2, {})} | custom-call | flops 1048576 | bytes 65536 | tf_op jit(solution)/shard_map/turn/pallas_call | solution.py:155
  36.1 9.5 %collective-permute-start.8 = (bf16[512,384]{1,0:T(8,128)(2,1)S(1)}, bf16[512,384]{1,0:T(8,128)(2,1)S(1)}, u32[]{:S(2)}, u32[]{:S(2)}) collective-permute-start(bf16[512,384]{1,0:T(8,128)(2,1)S(1)} %get-tuple-element.43), channel_id=1, source_target_pairs={{0,1},{7,6},{8,9},{15,14},{16,17},{23,22},{24,25},{31,30}} | collective-permute-start | bytes 1179656 | tf_op jit(solution)/shard_map/ppermute | solution.py:123
  46.9 5.9 %collective-permute-done.8.far_zero = bf16[512,384]{1,0:T(8,128)(2,1)S(1)} collective-permute-done((bf16[512,384]{1,0:T(8,128)(2,1)S(1)}, bf16[512,384]{1,0:T(8,128)(2,1)S(1)}, u32[]{:S(2)}, u32[]{:S(2)}) %collective-permute-start.8) | collective-permute-done | bytes 393248 | tf_op jit(solution)/shard_map/ppermute | solution.py:123
  55.3 1.3 %collective-permute-start.11 = (bf16[512,1536]{1,0:T(8,128)(2,1)S(1)}, bf16[512,1536]{1,0:T(8,128)(2,1)S(1)}, u32[]{:S(2)}, u32[]{:S(2)}) collective-permute-start(bf16[512,1536]{1,0:T(8,128)(2,1)S(1)} %multiply.8.zero_ref.q01), channel_id=1, source_target_pairs={{1,0},{6,7},{9,8},{14,15},{17,16},{22,23},{25,24},{30,31}} | collective-permute-start | bytes 4718600 | tf_op jit(solution)/shard_map/ppermute | solution.py:123
  61.6 1.3 %collective-permute-start.12 = (bf16[512,512]{1,0:T(8,128)(2,1)S(1)}, bf16[512,512]{1,0:T(8,128)(2,1)S(1)}, u32[]{:S(2)}, u32[]{:S(2)}) collective-permute-start(bf16[512,512]{1,0:T(8,128)(2,1)S(1)} %multiply.9.zero_ref), channel_id=1, source_target_pairs={{1,0},{6,7},{9,8},{14,15},{17,16},{22,23},{25,24},{30,31}} | collective-permute-start | bytes 1572872 | tf_op jit(solution)/shard_map/ppermute | solution.py:123
  67.1 19.6 %collective-permute-done.11.refs_0_.q0 = bf16[512,1536]{1,0:T(8,128)(2,1)S(1)} collective-permute-done((bf16[512,1536]{1,0:T(8,128)(2,1)S(1)}, bf16[512,1536]{1,0:T(8,128)(2,1)S(1)}, u32[]{:S(2)}, u32[]{:S(2)}) %collective-permute-start.11) | collective-permute-done | bytes 1572896 | tf_op jit(solution)/shard_map/ppermute | solution.py:123
  87.3 1.1 tick.2.place_ref
  88.5 26.0 %collective-permute-done.12.refs_0_.q0_last = bf16[512,512]{1,0:T(8,128)(2,1)S(1)} collective-permute-done((bf16[512,512]{1,0:T(8,128)(2,1)S(1)}, bf16[512,512]{1,0:T(8,128)(2,1)S(1)}, u32[]{:S(2)}, u32[]{:S(2)}) %collective-permute-start.12) | collective-permute-done | bytes 524320 | tf_op jit(solution)/shard_map/ppermute | solution.py:123
  114.5 1.1 tick.3.place_ref
  116.4 2.9 %finish.1 = (bf16[512,2048]{1,0:T(8,128)(2,1)}, f32[1,512]{1,0:T(1,128)S(1)}) custom-call(s32[5]{0:T(128)S(1)} %tick.3.place_ref, bf16[512,2048]{1,0:T(8,128)(2,1)S(1)} %bitcast.12, bf16[512,2048]{1,0:T(8,128)(2,1)S(1)} %bitcast.19, bf16[512,1536]{1,0:T(8,128)(2,1)S(1)} %collective-permute-done.11.refs_0_.q0, ...), custom_call_target="tpu_custom_call" | custom-call | flops 14000000000 | bytes 65536 | tf_op jit(solution)/shard_map/finish/pallas_call | solution.py:620
  119.9 1.2 finish_last.1
  (51 shorter events, 20.8 us)
Async XLA Ops:
  0.6 29.0 %collective-permute-start.5 = (bf16[512,2048]{1,0:T(8,128)(2,1)}, bf16[512,2048]{1,0:T(8,128)(2,1)}, u32[]{:S(2)}, u32[]{:S(2)}) collective-permute-start(bf16[512,2048]{1,0:T(8,128)(2,1)} %bitcast.8), channel_id=1, source_target_pairs={{2,1},{5,6},{10,9},{13,14},{18,17},{21,22},{26,25},{29,30}} | collective-permute-start | bytes 6291464 | tf_op jit(solution)/shard_map/ppermute | solution.py:123
  2.6 30.5 %collective-permute-start.4 = (bf16[512,2048]{1,0:T(8,128)(2,1)}, bf16[512,2048]{1,0:T(8,128)(2,1)S(1)}, u32[]{:S(2)}, u32[]{:S(2)}) collective-permute-start(bf16[512,2048]{1,0:T(8,128)(2,1)} %bitcast.9), channel_id=1, source_target_pairs={{0,1},{7,6},{8,9},{15,14},{16,17},{23,22},{24,25},{31,30}} | collective-permute-start | bytes 6291464 | tf_op jit(solution)/shard_map/ppermute | solution.py:123
  6.9 1.6 %copy-start.1 = (bf16[1,512,2048]{2,1,0:T(8,128)(2,1)S(1)}, bf16[1,512,2048]{2,1,0:T(8,128)(2,1)}, u32[]{:S(2)}) copy-start(bf16[1,512,2048]{2,1,0:T(8,128)(2,1)} %param.8) | copy-start | bytes 6291460
  8.5 6.3 %copy-start.3 = (s32[2048]{0:T(1024)S(1)}, s32[2048]{0:T(1024)}, u32[]{:S(2)}) copy-start(s32[2048]{0:T(1024)} %param.13) | copy-start | bytes 24580
  9.5 7.1 %copy-start = (bf16[1,512,2048]{2,1,0:T(8,128)(2,1)S(1)}, bf16[1,512,2048]{2,1,0:T(8,128)(2,1)}, u32[]{:S(2)}) copy-start(bf16[1,512,2048]{2,1,0:T(8,128)(2,1)} %param.9) | copy-start | bytes 6291460
  9.5 14.4 %collective-permute-start = (bf16[512,1024]{1,0:T(8,128)(2,1)S(1)}, bf16[512,1024]{1,0:T(8,128)(2,1)S(1)}, u32[]{:S(2)}, u32[]{:S(2)}) collective-permute-start(bf16[512,1024]{1,0:T(8,128)(2,1)S(1)} %get-tuple-element.31), channel_id=1, source_target_pairs={{4,0},{8,4},{12,8},{5,1},{9,5},{13,9},{6,2},{10,6},{14,10},{7,3},{... | collective-permute-start | bytes 3145736 | tf_op jit(solution)/shard_map/ppermute | solution.py:20
  11.6 23.5 %collective-permute-start.7 = (bf16[512,1024]{1,0:T(8,128)(2,1)S(1)}, bf16[512,1024]{1,0:T(8,128)(2,1)S(1)}, u32[]{:S(2)}, u32[]{:S(2)}) collective-permute-start(bf16[512,1024]{1,0:T(8,128)(2,1)S(1)} %get-tuple-element.39), channel_id=1, source_target_pairs={{4,0},{8,4},{12,8},{5,1},{9,5},{13,9},{6,2},{10,6},{14,10},{7,3},{... | collective-permute-start | bytes 3145736 | tf_op jit(solution)/shard_map/ppermute | solution.py:20
  21.4 2.5 %copy-start.2 = (bf16[1,512,2048]{2,1,0:T(8,128)(2,1)S(1)}, bf16[1,512,2048]{2,1,0:T(8,128)(2,1)}, u32[]{:S(2)}) copy-start(bf16[1,512,2048]{2,1,0:T(8,128)(2,1)} %param.7) | copy-start | bytes 6291460
  24.9 20.7 %collective-permute-start.3 = (bf16[512,1024]{1,0:T(8,128)(2,1)S(1)}, bf16[512,1024]{1,0:T(8,128)(2,1)S(1)}, u32[]{:S(2)}, u32[]{:S(2)}) collective-permute-start(bf16[512,1024]{1,0:T(8,128)(2,1)S(1)} %get-tuple-element.35.near_ref.near), channel_id=1, source_target_pairs={{0,1},{7,6},{8,9},{15,14},{16,17},{23,22},{24,25},{31,30}} | collective-permute-start | bytes 3145736 | tf_op jit(solution)/shard_map/ppermute | solution.py:123
  28.9 16.8 %collective-permute-start.2 = (bf16[512,896]{1,0:T(8,128)(2,1)S(1)}, bf16[512,896]{1,0:T(8,128)(2,1)S(1)}, u32[]{:S(2)}, u32[]{:S(2)}) collective-permute-start(bf16[512,896]{1,0:T(8,128)(2,1)S(1)} %get-tuple-element.34), channel_id=1, source_target_pairs={{2,1},{5,6},{10,9},{13,14},{18,17},{21,22},{26,25},{29,30}} | collective-permute-start | bytes 2752520 | tf_op jit(solution)/shard_map/ppermute | solution.py:123
  29.6 16.0 %collective-permute-start.1 = (bf16[512,384]{1,0:T(8,128)(2,1)S(1)}, bf16[512,384]{1,0:T(8,128)(2,1)S(1)}, u32[]{:S(2)}, u32[]{:S(2)}) collective-permute-start(bf16[512,384]{1,0:T(8,128)(2,1)S(1)} %get-tuple-element.33), channel_id=1, source_target_pairs={{3,1},{4,6},{11,9},{12,14},{19,17},{20,22},{27,25},{28,30}} | collective-permute-start | bytes 1179656 | tf_op jit(solution)/shard_map/ppermute | solution.py:123
  36.1 16.8 %collective-permute-start.8 = (bf16[512,384]{1,0:T(8,128)(2,1)S(1)}, bf16[512,384]{1,0:T(8,128)(2,1)S(1)}, u32[]{:S(2)}, u32[]{:S(2)}) collective-permute-start(bf16[512,384]{1,0:T(8,128)(2,1)S(1)} %get-tuple-element.43), channel_id=1, source_target_pairs={{0,1},{7,6},{8,9},{15,14},{16,17},{23,22},{24,25},{31,30}} | collective-permute-start | bytes 1179656 | tf_op jit(solution)/shard_map/ppermute | solution.py:123
  45.6 12.8 %collective-permute-start.6 = (bf16[256,2048]{1,0:T(8,128)(2,1)S(1)}, bf16[256,2048]{1,0:T(8,128)(2,1)S(1)}, u32[]{:S(2)}, u32[]{:S(2)}) collective-permute-start(bf16[256,2048]{1,0:T(8,128)(2,1)S(1)} %couple.2.coupled_ref.refs_0_), channel_id=1, source_target_pairs={{3,1},{4,6},{11,9},{12,14},{19,17},{20,22},{27,25},{28,30}} | collective-permute-start | bytes 3145736 | tf_op jit(solution)/shard_map/ppermute | solution.py:123
  52.9 7.2 %collective-permute-start.9 = (bf16[256,2048]{1,0:T(8,128)(2,1)S(1)}, bf16[256,2048]{1,0:T(8,128)(2,1)S(1)}, u32[]{:S(2)}, u32[]{:S(2)}) collective-permute-start(bf16[256,2048]{1,0:T(8,128)(2,1)S(1)} %couple.3.coupled_ref.refs_1_), channel_id=1, source_target_pairs={{3,1},{4,6},{11,9},{12,14},{19,17},{20,22},{27,25},{28,30}} | collective-permute-start | bytes 3145736 | tf_op jit(solution)/shard_map/ppermute | solution.py:123
  55.3 31.4 %collective-permute-start.11 = (bf16[512,1536]{1,0:T(8,128)(2,1)S(1)}, bf16[512,1536]{1,0:T(8,128)(2,1)S(1)}, u32[]{:S(2)}, u32[]{:S(2)}) collective-permute-start(bf16[512,1536]{1,0:T(8,128)(2,1)S(1)} %multiply.8.zero_ref.q01), channel_id=1, source_target_pairs={{1,0},{6,7},{9,8},{14,15},{17,16},{22,23},{25,24},{30,31}} | collective-permute-start | bytes 4718600 | tf_op jit(solution)/shard_map/ppermute | solution.py:123
  57.7 58.7 %collective-permute-start.16 = (bf16[512,1408]{1,0:T(8,128)(2,1)S(1)}, bf16[512,1408]{1,0:T(8,128)(2,1)S(1)}, u32[]{:S(2)}, u32[]{:S(2)}) collective-permute-start(bf16[512,1408]{1,0:T(8,128)(2,1)S(1)} %product_two.1.q21), channel_id=1, source_target_pairs={{1,2},{6,5},{9,10},{14,13},{17,18},{22,21},{25,26},{30,29}} | collective-permute-start | bytes 4325384 | tf_op jit(solution)/shard_map/ppermute | solution.py:123
  61.6 52.9 %collective-permute-start.12 = (bf16[512,512]{1,0:T(8,128)(2,1)S(1)}, bf16[512,512]{1,0:T(8,128)(2,1)S(1)}, u32[]{:S(2)}, u32[]{:S(2)}) collective-permute-start(bf16[512,512]{1,0:T(8,128)(2,1)S(1)} %multiply.9.zero_ref), channel_id=1, source_target_pairs={{1,0},{6,7},{9,8},{14,15},{17,16},{22,23},{25,24},{30,31}} | collective-permute-start | bytes 1572872 | tf_op jit(solution)/shard_map/ppermute | solution.py:123
  64.0 51.7 %collective-permute-start.10 = (bf16[512,512]{1,0:T(8,128)(2,1)S(1)}, bf16[512,512]{1,0:T(8,128)(2,1)S(1)}, u32[]{:S(2)}, u32[]{:S(2)}) collective-permute-start(bf16[512,512]{1,0:T(8,128)(2,1)S(1)} %multiply.11), channel_id=1, source_target_pairs={{1,3},{6,4},{9,11},{14,12},{17,19},{22,20},{25,27},{30,28}} | collective-permute-start | bytes 1572872 | tf_op jit(solution)/shard_map/ppermute | solution.py:123
  65.2 54.0 %collective-permute-start.15 = (bf16[512,1024]{1,0:T(8,128)(2,1)S(1)}, bf16[512,1024]{1,0:T(8,128)(2,1)S(1)}, u32[]{:S(2)}, u32[]{:S(2)}) collective-permute-start(bf16[512,1024]{1,0:T(8,128)(2,1)S(1)} %get-tuple-element.54.q31), channel_id=1, source_target_pairs={{1,3},{6,4},{9,11},{14,12},{17,19},{22,20},{25,27},{30,28}} | collective-permute-start | bytes 3145736 | tf_op jit(solution)/shard_map/ppermute | solution.py:123
  86.7 33.3 %collective-permute-start.14 = (bf16[512,384]{1,0:T(8,128)(2,1)S(1)}, bf16[512,384]{1,0:T(8,128)(2,1)S(1)}, u32[]{:S(2)}, u32[]{:S(2)}) collective-permute-start(bf16[512,384]{1,0:T(8,128)(2,1)S(1)} %get-tuple-element.53), channel_id=1, source_target_pairs={{1,3},{6,4},{9,11},{14,12},{17,19},{22,20},{25,27},{30,28}} | collective-permute-start | bytes 1179656 | tf_op jit(solution)/shard_map/ppermute | solution.py:123
  115.7 4.3 %collective-permute-start.13 = (bf16[512,512]{1,0:T(8,128)(2,1)S(1)}, bf16[512,512]{1,0:T(8,128)(2,1)S(1)}, u32[]{:S(2)}, u32[]{:S(2)}) collective-permute-start(bf16[512,512]{1,0:T(8,128)(2,1)S(1)} %collective-permute-done.10.q3_two), channel_id=1, source_target_pairs={{3,2},{4,5},{11,10},{12,13},{19,18},{20,21},{27,26},{28,29}} | collective-permute-start | bytes 1572872 | tf_op jit(solution)/shard_map/ppermute | solution.py:123

commit v21 on v20

--- a/solution.py
+++ b/solution.py
@@ -789,12 +789,12 @@
     last_three = moved(last, 3, 1)
     c2 = couple_here(place, after(p2, last), weights, coupling_rate)
     across = turn(place, 2, 0, c2, across)
-    c0 = couple_here(place, after(p0, across), weights, coupling_rate)
-    across = turn(place, 0, 0, c0, across)
     row_other, far = prior_half(
         other_half_kernel, sides[1], (3,), place, after(other, across), sigma
     )
     far_zero = moved(far, 0, 1)
+    c0 = couple_here(place, after(p0, across, far), weights, coupling_rate)
+    across = turn(place, 0, 0, c0, across)
     column, h0_one, h2_one = own_column(place, row_near, row_other, c0, c2)
     c3 = [
         moved(after(c1[0], last_three, near_two, near_zero, across), 3, 1),

time: 122 us -> 116 us (0.951)
  the two profiles are of different devices: /device:TPU:6 before, /device:TPU:1 now
where the time goes in v21:
time: 116 us
  waiting for transfers between devices  41 us (35%)
  starting transfers between devices  37.3 us (32%)
  Pallas kernels  32.8 us (28%)
  between operations  3.19 us (3%)
  local copies, waits for them, and re-layouts  1.69 us (1%)
    ppermute x15, waiting for transfers between devices, moved(): lax.ppermute(value, ('dom', 'col'), route(source, target, lax.axis_size('...  36.6 us
    ppermute x15, starting transfers between devices, moved(): lax.ppermute(value, ('dom', 'col'), route(source, target, lax.axis_size('...  29.7 us
    ppermute x2, starting transfers between devices, passed_along(): lax.ppermute(value, axis, [(source, source + steps) for source in range(i...  7.6 us
    pallas_call x6, Pallas kernels, turn(): pl.pallas_call(turn_kernel, out_shape=jax.ShapeDtypeStruct((nodes, nodes)...  5.99 us
    ppermute x2, waiting for transfers between devices, passed_along(): lax.ppermute(value, axis, [(source, source + steps) for source in range(i...  4.44 us
    pallas_call x7, Pallas kernels, multiply(): pl.pallas_call(functools.partial(multiply_kernel, first, count, len(lefts...  4.03 us
    pallas_call x2, Pallas kernels, couple(): pl.pallas_call(functools.partial(couple_kernel, part * rows), out_shape=j...  3.77 us
    pallas_call x1, Pallas kernels, finish(): pl.pallas_call(finish_kernel, out_shape=(jax.ShapeDtypeStruct((rows, node...  2.6 us
  transfers between devices with their start and end apart: 17, of which 8 were waited for; matrix products, arithmetic and copies ran while one was open for 0% of the time, Pallas kernels for 26%

profile of v21, /device:TPU:1, one launch (start us, length us, event | category | flops | bytes accessed | tf_op | source)
XLA Modules:
  0.0 115.9 jit_solution(17459143237585147699)
XLA Ops:
  0.6 2.0 %collective-permute-start.5 = (bf16[512,2048]{1,0:T(8,128)(2,1)}, bf16[512,2048]{1,0:T(8,128)(2,1)}, u32[]{:S(2)}, u32[]{:S(2)}) collective-permute-start(bf16[512,2048]{1,0:T(8,128)(2,1)} %bitcast.8), channel_id=1, source_target_pairs={{2,1},{5,6},{10,9},{13,14},{18,17},{21,22},{26,25},{29,30}} | collective-permute-start | bytes 6291464 | tf_op jit(solution)/shard_map/ppermute | solution.py:123
  4.8 1.6 %copy-done.1 = bf16[1,512,2048]{2,1,0:T(8,128)(2,1)S(1)} copy-done((bf16[1,512,2048]{2,1,0:T(8,128)(2,1)S(1)}, bf16[1,512,2048]{2,1,0:T(8,128)(2,1)}, u32[]{:S(2)}) %copy-start.1) | copy-done | bytes 2097176
  7.4 5.7 %collective-permute-start = (bf16[512,1024]{1,0:T(8,128)(2,1)S(1)}, bf16[512,1024]{1,0:T(8,128)(2,1)S(1)}, u32[]{:S(2)}, u32[]{:S(2)}) collective-permute-start(bf16[512,1024]{1,0:T(8,128)(2,1)S(1)} %get-tuple-element.31), channel_id=1, source_target_pairs={{4,0},{8,4},{12,8},{5,1},{9,5},{13,9},{6,2},{10,6},{14,10},{7,3},{... | collective-permute-start | bytes 3145736 | tf_op jit(solution)/shard_map/ppermute | solution.py:20
  13.1 1.9 %collective-permute-start.6 = (bf16[512,1024]{1,0:T(8,128)(2,1)S(1)}, bf16[512,1024]{1,0:T(8,128)(2,1)S(1)}, u32[]{:S(2)}, u32[]{:S(2)}) collective-permute-start(bf16[512,1024]{1,0:T(8,128)(2,1)S(1)} %get-tuple-element.37), channel_id=1, source_target_pairs={{4,0},{8,4},{12,8},{5,1},{9,5},{13,9},{6,2},{10,6},{14,10},{7,3},{... | collective-permute-start | bytes 3145736 | tf_op jit(solution)/shard_map/ppermute | solution.py:20
  15.7 1.8 %coupling.1.weight_ref.refs_1_ = bf16[8,512,256]{2,1,0:T(8,128)(2,1)S(1)} custom-call(s32[1,2048]{1,0:T(1,128)S(1)} %bitcast.20), custom_call_target="tpu_custom_call" | custom-call | flops 1048576 | bytes 65536 | tf_op jit(solution)/shard_map/coupling/pallas_call | solution.py:70
  17.5 1.9 %couple.3.coupled_ref.refs_1_ = bf16[256,2048]{1,0:T(8,128)(2,1)S(1)} custom-call(f32[1]{0:T(128)S(6)} %copy.23.rate_ref.refs_0_, bf16[8,512,256]{2,1,0:T(8,128)(2,1)S(1)} %coupling.1.weight_ref.refs_1_, bf16[512,2048]{1,0:T(8,128)(2,1)S(1)} %bitcast.10), custom_call_target="tpu_custom_call" | custom-call | flops 1048576 | bytes 65536 | tf_op jit(solution)/shard_map/couple/pallas_call | solution.py:99
  19.4 1.9 %couple.2.coupled_ref.refs_0_ = bf16[256,2048]{1,0:T(8,128)(2,1)S(1)} custom-call(f32[1]{0:T(128)S(6)} %copy.23.rate_ref.refs_0_, bf16[8,512,256]{2,1,0:T(8,128)(2,1)S(1)} %coupling.1.weight_ref.refs_1_, bf16[512,2048]{1,0:T(8,128)(2,1)S(1)} %bitcast.11), custom_call_target="tpu_custom_call" | custom-call | flops 1048576 | bytes 65536 | tf_op jit(solution)/shard_map/couple/pallas_call | solution.py:99
  23.1 3.5 %collective-permute-done.shifted_ref = bf16[512,1024]{1,0:T(8,128)(2,1)S(1)} collective-permute-done((bf16[512,1024]{1,0:T(8,128)(2,1)S(1)}, bf16[512,1024]{1,0:T(8,128)(2,1)S(1)}, u32[]{:S(2)}, u32[]{:S(2)}) %collective-permute-start) | collective-permute-done | bytes 1048608 | tf_op jit(solution)/shard_map/ppermute | solution.py:20
  29.2 4.9 %collective-permute-start.1 = (bf16[512,384]{1,0:T(8,128)(2,1)S(1)}, bf16[512,384]{1,0:T(8,128)(2,1)S(1)}, u32[]{:S(2)}, u32[]{:S(2)}) collective-permute-start(bf16[512,384]{1,0:T(8,128)(2,1)S(1)} %get-tuple-element.33), channel_id=1, source_target_pairs={{3,1},{4,6},{11,9},{12,14},{19,17},{20,22},{27,25},{28,30}} | collective-permute-start | bytes 1179656 | tf_op jit(solution)/shard_map/ppermute | solution.py:123
  34.1 1.6 %couple_here.2.coupled_ref.second_ref.left_ref = bf16[512,2048]{1,0:T(8,128)(2,1)S(1)} custom-call(s32[5]{0:T(128)S(1)} %stack.16.place_ref, f32[1]{0:T(128)S(6)} %copy.23.rate_ref.refs_0_, bf16[8,512,256]{2,1,0:T(8,128)(2,1)S(1)} %coupling.1.weight_ref.refs_1_, bf16[512,2048]{1,0:T(8,128)(2,1)} %collective-permute-done.5.refs_2_), custom_call_target="tpu_custom_call" | custom-call | flops 1048576 | bytes 65536 | tf_op jit(solution)/shard_map/couple_here/pallas_call | solution.py:133
  41.3 1.7 %collective-permute-done.1.last_three = bf16[512,384]{1,0:T(8,128)(2,1)S(1)} collective-permute-done((bf16[512,384]{1,0:T(8,128)(2,1)S(1)}, bf16[512,384]{1,0:T(8,128)(2,1)S(1)}, u32[]{:S(2)}, u32[]{:S(2)}) %collective-permute-start.1) | collective-permute-done | bytes 393248 | tf_op jit(solution)/shard_map/ppermute | solution.py:123
  43.1 8.2 %collective-permute-start.7 = (bf16[256,2048]{1,0:T(8,128)(2,1)S(1)}, bf16[256,2048]{1,0:T(8,128)(2,1)S(1)}, u32[]{:S(2)}, u32[]{:S(2)}) collective-permute-start(bf16[256,2048]{1,0:T(8,128)(2,1)S(1)} %couple.2.coupled_ref.refs_0_), channel_id=1, source_target_pairs={{3,1},{4,6},{11,9},{12,14},{19,17},{20,22},{27,25},{28,30}} | collective-permute-start | bytes 3145736 | tf_op jit(solution)/shard_map/ppermute | solution.py:123
  51.9 4.2 %collective-permute-start.9 = (bf16[256,2048]{1,0:T(8,128)(2,1)S(1)}, bf16[256,2048]{1,0:T(8,128)(2,1)S(1)}, u32[]{:S(2)}, u32[]{:S(2)}) collective-permute-start(bf16[256,2048]{1,0:T(8,128)(2,1)S(1)} %couple.3.coupled_ref.refs_1_), channel_id=1, source_target_pairs={{3,1},{4,6},{11,9},{12,14},{19,17},{20,22},{27,25},{28,30}} | collective-permute-start | bytes 3145736 | tf_op jit(solution)/shard_map/ppermute | solution.py:123
  60.4 2.6 %collective-permute-done.7.refs_0_.coupled_ref = bf16[256,2048]{1,0:T(8,128)(2,1)S(1)} collective-permute-done((bf16[256,2048]{1,0:T(8,128)(2,1)S(1)}, bf16[256,2048]{1,0:T(8,128)(2,1)S(1)}, u32[]{:S(2)}, u32[]{:S(2)}) %collective-permute-start.7) | collective-permute-done | bytes 1048608 | tf_op jit(solution)/shard_map/ppermute | solution.py:123
  64.6 9.6 %collective-permute-done.9.coupled_ref.refs_0_ = bf16[256,2048]{1,0:T(8,128)(2,1)S(1)} collective-permute-done((bf16[256,2048]{1,0:T(8,128)(2,1)S(1)}, bf16[256,2048]{1,0:T(8,128)(2,1)S(1)}, u32[]{:S(2)}, u32[]{:S(2)}) %collective-permute-start.9) | collective-permute-done | bytes 1048608 | tf_op jit(solution)/shard_map/ppermute | solution.py:123
  79.3 1.3 %collective-permute-start.15 = (bf16[512,1024]{1,0:T(8,128)(2,1)S(1)}, bf16[512,1024]{1,0:T(8,128)(2,1)S(1)}, u32[]{:S(2)}, u32[]{:S(2)}) collective-permute-start(bf16[512,1024]{1,0:T(8,128)(2,1)S(1)} %get-tuple-element.54.q31), channel_id=1, source_target_pairs={{1,3},{6,4},{9,11},{14,12},{17,19},{22,20},{25,27},{30,28}} | collective-permute-start | bytes 3145736 | tf_op jit(solution)/shard_map/ppermute | solution.py:123
  81.7 1.3 %collective-permute-start.14 = (bf16[512,384]{1,0:T(8,128)(2,1)S(1)}, bf16[512,384]{1,0:T(8,128)(2,1)S(1)}, u32[]{:S(2)}, u32[]{:S(2)}) collective-permute-start(bf16[512,384]{1,0:T(8,128)(2,1)S(1)} %get-tuple-element.53), channel_id=1, source_target_pairs={{1,3},{6,4},{9,11},{14,12},{17,19},{22,20},{25,27},{30,28}} | collective-permute-start | bytes 1179656 | tf_op jit(solution)/shard_map/ppermute | solution.py:123
  85.3 12.9 %collective-permute-done.10.q3_two = bf16[512,512]{1,0:T(8,128)(2,1)S(1)} collective-permute-done((bf16[512,512]{1,0:T(8,128)(2,1)S(1)}, bf16[512,512]{1,0:T(8,128)(2,1)S(1)}, u32[]{:S(2)}, u32[]{:S(2)}) %collective-permute-start.10) | collective-permute-done | bytes 524320 | tf_op jit(solution)/shard_map/ppermute | solution.py:123
  98.2 1.3 %collective-permute-start.13 = (bf16[512,512]{1,0:T(8,128)(2,1)S(1)}, bf16[512,512]{1,0:T(8,128)(2,1)S(1)}, u32[]{:S(2)}, u32[]{:S(2)}) collective-permute-start(bf16[512,512]{1,0:T(8,128)(2,1)S(1)} %collective-permute-done.10.q3_two), channel_id=1, source_target_pairs={{3,2},{4,5},{11,10},{12,13},{19,18},{20,21},{27,26},{28,29}} | collective-permute-start | bytes 1572872 | tf_op jit(solution)/shard_map/ppermute | solution.py:123
  99.5 2.6 %finish.1 = (bf16[512,2048]{1,0:T(8,128)(2,1)}, f32[1,512]{1,0:T(1,128)S(1)}) custom-call(s32[5]{0:T(128)S(1)} %tick.3.place_ref, bf16[512,2048]{1,0:T(8,128)(2,1)S(1)} %bitcast.12, bf16[512,2048]{1,0:T(8,128)(2,1)S(1)} %bitcast.19, bf16[512,1536]{1,0:T(8,128)(2,1)S(1)} %collective-permute-done.11.refs_0_.q0, ...), custom_call_target="tpu_custom_call" | custom-call | flops 14000000000 | bytes 65536 | tf_op jit(solution)/shard_map/finish/pallas_call | solution.py:620
  102.1 7.3 %collective-permute-done.15.q3_other = bf16[512,1024]{1,0:T(8,128)(2,1)S(1)} collective-permute-done((bf16[512,1024]{1,0:T(8,128)(2,1)S(1)}, bf16[512,1024]{1,0:T(8,128)(2,1)S(1)}, u32[]{:S(2)}, u32[]{:S(2)}) %collective-permute-start.15) | collective-permute-done | bytes 1048608 | tf_op jit(solution)/shard_map/ppermute | solution.py:123
  109.5 1.7 %finish_other.1.old_ref = bf16[512,2048]{1,0:T(8,128)(2,1)} custom-call(s32[5]{0:T(128)S(1)} %stack.16.place_ref, bf16[512,2048]{1,0:T(8,128)(2,1)S(1)} %bitcast.13, bf16[512,1024]{1,0:T(8,128)(2,1)S(1)} %collective-permute-done.15.q3_other, bf16[512,2048]{1,0:T(8,128)(2,1)} %get-tuple-element.56.old_ref), custom_call_target="tpu_custom_call", output_to_operand_aliasing={{}: (3, {})} | custom-call | flops 1048576 | bytes 65536 | tf_op jit(solution)/shard_map/finish_other/pallas_call | solution.py:716
  111.1 2.5 %collective-permute-done.14.q3_last = bf16[512,384]{1,0:T(8,128)(2,1)S(1)} collective-permute-done((bf16[512,384]{1,0:T(8,128)(2,1)S(1)}, bf16[512,384]{1,0:T(8,128)(2,1)S(1)}, u32[]{:S(2)}, u32[]{:S(2)}) %collective-permute-start.14) | collective-permute-done | bytes 393248 | tf_op jit(solution)/shard_map/ppermute | solution.py:123
  113.7 2.1 %finish_last.1 = (bf16[512,2048]{1,0:T(8,128)(2,1)}, f32[1,512]{1,0:T(1,128)}) custom-call(s32[5]{0:T(128)S(1)} %stack.16.place_ref, bf16[512,2048]{1,0:T(8,128)(2,1)S(1)} %bitcast.14, bf16[512,512]{1,0:T(8,128)(2,1)S(1)} %collective-permute-done.13.q2_last, bf16[512,384]{1,0:T(8,128)(2,1)S(1)} %collective-permute-done.14.q3_last, ...), custom_call_target="tpu_custom_call", output_to_operand_aliasing={{0}: (4, {})} | custom-call | flops 1048576 | bytes 65536 | tf_op jit(solution)/shard_map/finish_last/pallas_call | solution.py:741
  (51 shorter events, 26.6 us)
Async XLA Ops:
  0.6 28.5 %collective-permute-start.5 = (bf16[512,2048]{1,0:T(8,128)(2,1)}, bf16[512,2048]{1,0:T(8,128)(2,1)}, u32[]{:S(2)}, u32[]{:S(2)}) collective-permute-start(bf16[512,2048]{1,0:T(8,128)(2,1)} %bitcast.8), channel_id=1, source_target_pairs={{2,1},{5,6},{10,9},{13,14},{18,17},{21,22},{26,25},{29,30}} | collective-permute-start | bytes 6291464 | tf_op jit(solution)/shard_map/ppermute | solution.py:123
  2.6 36.9 %collective-permute-start.4 = (bf16[512,2048]{1,0:T(8,128)(2,1)}, bf16[512,2048]{1,0:T(8,128)(2,1)S(1)}, u32[]{:S(2)}, u32[]{:S(2)}) collective-permute-start(bf16[512,2048]{1,0:T(8,128)(2,1)} %bitcast.9), channel_id=1, source_target_pairs={{0,1},{7,6},{8,9},{15,14},{16,17},{23,22},{24,25},{31,30}} | collective-permute-start | bytes 6291464 | tf_op jit(solution)/shard_map/ppermute | solution.py:123
  4.8 1.6 %copy-start.1 = (bf16[1,512,2048]{2,1,0:T(8,128)(2,1)S(1)}, bf16[1,512,2048]{2,1,0:T(8,128)(2,1)}, u32[]{:S(2)}) copy-start(bf16[1,512,2048]{2,1,0:T(8,128)(2,1)} %param.8) | copy-start | bytes 6291460
  6.4 9.3 %copy-start.3 = (s32[2048]{0:T(1024)S(1)}, s32[2048]{0:T(1024)}, u32[]{:S(2)}) copy-start(s32[2048]{0:T(1024)} %param.13) | copy-start | bytes 24580
  7.4 10.1 %copy-start = (bf16[1,512,2048]{2,1,0:T(8,128)(2,1)S(1)}, bf16[1,512,2048]{2,1,0:T(8,128)(2,1)}, u32[]{:S(2)}) copy-start(bf16[1,512,2048]{2,1,0:T(8,128)(2,1)} %param.9) | copy-start | bytes 6291460
  7.4 19.2 %collective-permute-start = (bf16[512,1024]{1,0:T(8,128)(2,1)S(1)}, bf16[512,1024]{1,0:T(8,128)(2,1)S(1)}, u32[]{:S(2)}, u32[]{:S(2)}) collective-permute-start(bf16[512,1024]{1,0:T(8,128)(2,1)S(1)} %get-tuple-element.31), channel_id=1, source_target_pairs={{4,0},{8,4},{12,8},{5,1},{9,5},{13,9},{6,2},{10,6},{14,10},{7,3},{... | collective-permute-start | bytes 3145736 | tf_op jit(solution)/shard_map/ppermute | solution.py:20
  13.1 24.8 %collective-permute-start.6 = (bf16[512,1024]{1,0:T(8,128)(2,1)S(1)}, bf16[512,1024]{1,0:T(8,128)(2,1)S(1)}, u32[]{:S(2)}, u32[]{:S(2)}) collective-permute-start(bf16[512,1024]{1,0:T(8,128)(2,1)S(1)} %get-tuple-element.37), channel_id=1, source_target_pairs={{4,0},{8,4},{12,8},{5,1},{9,5},{13,9},{6,2},{10,6},{14,10},{7,3},{... | collective-permute-start | bytes 3145736 | tf_op jit(solution)/shard_map/ppermute | solution.py:20
  22.2 4.4 %copy-start.2 = (bf16[1,512,2048]{2,1,0:T(8,128)(2,1)S(1)}, bf16[1,512,2048]{2,1,0:T(8,128)(2,1)}, u32[]{:S(2)}) copy-start(bf16[1,512,2048]{2,1,0:T(8,128)(2,1)} %param.7) | copy-start | bytes 6291460
  27.7 15.4 %collective-permute-start.3 = (bf16[512,1024]{1,0:T(8,128)(2,1)S(1)}, bf16[512,1024]{1,0:T(8,128)(2,1)S(1)}, u32[]{:S(2)}, u32[]{:S(2)}) collective-permute-start(bf16[512,1024]{1,0:T(8,128)(2,1)S(1)} %get-tuple-element.35.near_ref.near), channel_id=1, source_target_pairs={{0,1},{7,6},{8,9},{15,14},{16,17},{23,22},{24,25},{31,30}} | collective-permute-start | bytes 3145736 | tf_op jit(solution)/shard_map/ppermute | solution.py:123
  28.4 14.6 %collective-permute-start.2 = (bf16[512,896]{1,0:T(8,128)(2,1)S(1)}, bf16[512,896]{1,0:T(8,128)(2,1)S(1)}, u32[]{:S(2)}, u32[]{:S(2)}) collective-permute-start(bf16[512,896]{1,0:T(8,128)(2,1)S(1)} %get-tuple-element.34), channel_id=1, source_target_pairs={{2,1},{5,6},{10,9},{13,14},{18,17},{21,22},{26,25},{29,30}} | collective-permute-start | bytes 2752520 | tf_op jit(solution)/shard_map/ppermute | solution.py:123
  29.2 13.9 %collective-permute-start.1 = (bf16[512,384]{1,0:T(8,128)(2,1)S(1)}, bf16[512,384]{1,0:T(8,128)(2,1)S(1)}, u32[]{:S(2)}, u32[]{:S(2)}) collective-permute-start(bf16[512,384]{1,0:T(8,128)(2,1)S(1)} %get-tuple-element.33), channel_id=1, source_target_pairs={{3,1},{4,6},{11,9},{12,14},{19,17},{20,22},{27,25},{28,30}} | collective-permute-start | bytes 1179656 | tf_op jit(solution)/shard_map/ppermute | solution.py:123
  38.9 13.0 %collective-permute-start.8 = (bf16[512,384]{1,0:T(8,128)(2,1)S(1)}, bf16[512,384]{1,0:T(8,128)(2,1)S(1)}, u32[]{:S(2)}, u32[]{:S(2)}) collective-permute-start(bf16[512,384]{1,0:T(8,128)(2,1)S(1)} %get-tuple-element.39), channel_id=1, source_target_pairs={{0,1},{7,6},{8,9},{15,14},{16,17},{23,22},{24,25},{31,30}} | collective-permute-start | bytes 1179656 | tf_op jit(solution)/shard_map/ppermute | solution.py:123
  43.1 19.9 %collective-permute-start.7 = (bf16[256,2048]{1,0:T(8,128)(2,1)S(1)}, bf16[256,2048]{1,0:T(8,128)(2,1)S(1)}, u32[]{:S(2)}, u32[]{:S(2)}) collective-permute-start(bf16[256,2048]{1,0:T(8,128)(2,1)S(1)} %couple.2.coupled_ref.refs_0_), channel_id=1, source_target_pairs={{3,1},{4,6},{11,9},{12,14},{19,17},{20,22},{27,25},{28,30}} | collective-permute-start | bytes 3145736 | tf_op jit(solution)/shard_map/ppermute | solution.py:123
  51.9 22.3 %collective-permute-start.9 = (bf16[256,2048]{1,0:T(8,128)(2,1)S(1)}, bf16[256,2048]{1,0:T(8,128)(2,1)S(1)}, u32[]{:S(2)}, u32[]{:S(2)}) collective-permute-start(bf16[256,2048]{1,0:T(8,128)(2,1)S(1)} %couple.3.coupled_ref.refs_1_), channel_id=1, source_target_pairs={{3,1},{4,6},{11,9},{12,14},{19,17},{20,22},{27,25},{28,30}} | collective-permute-start | bytes 3145736 | tf_op jit(solution)/shard_map/ppermute | solution.py:123
  57.7 24.0 %collective-permute-start.11 = (bf16[512,1536]{1,0:T(8,128)(2,1)S(1)}, bf16[512,1536]{1,0:T(8,128)(2,1)S(1)}, u32[]{:S(2)}, u32[]{:S(2)}) collective-permute-start(bf16[512,1536]{1,0:T(8,128)(2,1)S(1)} %multiply.8.zero_ref.q01), channel_id=1, source_target_pairs={{1,0},{6,7},{9,8},{14,15},{17,16},{22,23},{25,24},{30,31}} | collective-permute-start | bytes 4718600 | tf_op jit(solution)/shard_map/ppermute | solution.py:123
  59.6 39.9 %collective-permute-start.16 = (bf16[512,1408]{1,0:T(8,128)(2,1)S(1)}, bf16[512,1408]{1,0:T(8,128)(2,1)S(1)}, u32[]{:S(2)}, u32[]{:S(2)}) collective-permute-start(bf16[512,1408]{1,0:T(8,128)(2,1)S(1)} %product_two.1.q21), channel_id=1, source_target_pairs={{1,2},{6,5},{9,10},{14,13},{17,18},{22,21},{25,26},{30,29}} | collective-permute-start | bytes 4325384 | tf_op jit(solution)/shard_map/ppermute | solution.py:123
  75.6 8.6 %collective-permute-start.12 = (bf16[512,512]{1,0:T(8,128)(2,1)S(1)}, bf16[512,512]{1,0:T(8,128)(2,1)S(1)}, u32[]{:S(2)}, u32[]{:S(2)}) collective-permute-start(bf16[512,512]{1,0:T(8,128)(2,1)S(1)} %multiply.9.zero_ref), channel_id=1, source_target_pairs={{1,0},{6,7},{9,8},{14,15},{17,16},{22,23},{25,24},{30,31}} | collective-permute-start | bytes 1572872 | tf_op jit(solution)/shard_map/ppermute | solution.py:123
  77.5 20.8 %collective-permute-start.10 = (bf16[512,512]{1,0:T(8,128)(2,1)S(1)}, bf16[512,512]{1,0:T(8,128)(2,1)S(1)}, u32[]{:S(2)}, u32[]{:S(2)}) collective-permute-start(bf16[512,512]{1,0:T(8,128)(2,1)S(1)} %multiply.11), channel_id=1, source_target_pairs={{1,3},{6,4},{9,11},{14,12},{17,19},{22,20},{25,27},{30,28}} | collective-permute-start | bytes 1572872 | tf_op jit(solution)/shard_map/ppermute | solution.py:123
  79.3 30.1 %collective-permute-start.15 = (bf16[512,1024]{1,0:T(8,128)(2,1)S(1)}, bf16[512,1024]{1,0:T(8,128)(2,1)S(1)}, u32[]{:S(2)}, u32[]{:S(2)}) collective-permute-start(bf16[512,1024]{1,0:T(8,128)(2,1)S(1)} %get-tuple-element.54.q31), channel_id=1, source_target_pairs={{1,3},{6,4},{9,11},{14,12},{17,19},{22,20},{25,27},{30,28}} | collective-permute-start | bytes 3145736 | tf_op jit(solution)/shard_map/ppermute | solution.py:123
  81.7 31.9 %collective-permute-start.14 = (bf16[512,384]{1,0:T(8,128)(2,1)S(1)}, bf16[512,384]{1,0:T(8,128)(2,1)S(1)}, u32[]{:S(2)}, u32[]{:S(2)}) collective-permute-start(bf16[512,384]{1,0:T(8,128)(2,1)S(1)} %get-tuple-element.53), channel_id=1, source_target_pairs={{1,3},{6,4},{9,11},{14,12},{17,19},{22,20},{25,27},{30,28}} | collective-permute-start | bytes 1179656 | tf_op jit(solution)/shard_map/ppermute | solution.py:123
  98.2 15.5 %collective-permute-start.13 = (bf16[512,512]{1,0:T(8,128)(2,1)S(1)}, bf16[512,512]{1,0:T(8,128)(2,1)S(1)}, u32[]{:S(2)}, u32[]{:S(2)}) collective-permute-start(bf16[512,512]{1,0:T(8,128)(2,1)S(1)} %collective-permute-done.10.q3_two), channel_id=1, source_target_pairs={{3,2},{4,5},{11,10},{12,13},{19,18},{20,21},{27,26},{28,29}} | collective-permute-start | bytes 1572872 | tf_op jit(solution)/shard_map/ppermute | solution.py:123

commit v22 on v21

--- a/solution.py
+++ b/solution.py
@@ -662,8 +662,7 @@
             pltpu.make_async_copy(sum_ref.at[here], out_ref.at[here, column], sems.at[part])
         )
         copies[-1].start()
-    for copy in copies:
-        copy.wait()
+    return copies
 
 
 def other_kernel(place_ref, pivot_ref, q3_other, old_ref, out_ref, sum_ref, sems):
@@ -672,9 +671,9 @@
 
     @pl.when((place_ref[4] != 0) & (place_ref[1] == 3))
     def _():
-        add_in_place(
-            pivot_ref, out_ref, sum_ref, sems, column, lambda part, here: q3_other[here, :]
-        )
+        product = lambda part, here: q3_other[here, :]
+        for copy in add_in_place(pivot_ref, out_ref, sum_ref, sems, column, product):
+            copy.wait()
 
 
 def last_kernel(
@@ -689,16 +688,19 @@
 
     @pl.when(active & (place_ref[1] == 2))
     def _():
-        add(lambda part, here: q2_last[:, here].T)
+        for copy in add(lambda part, here: q2_last[:, here].T):
+            copy.wait()
 
     @pl.when(active & (place_ref[1] == 3))
     def _():
-        add(lambda part, here: jnp.concatenate(unpacked_rows(part, q3_last, 0), axis=1))
+        copies = add(lambda part, here: jnp.concatenate(unpacked_rows(part, q3_last, 0), axis=1))
         for start in range(0, rows, chunk):
             here = pl.ds(start, chunk)
             value = pivot_ref[here, here].astype(F32)
             value = value + q3_last[here, pl.ds(start % (2 * chunk), chunk)].astype(F32)
             var_ref[:, here] = diagonal_of(chunk)(value)
+        for copy in copies:
+            copy.wait()
 
 
 def diagonal_of(rows):
@@ -810,11 +812,10 @@
     q2 = moved(q2_own, 1, 2)
 
     across = turn(place, 3, 0, c3[0], after(across, q2_own))
-    upper = multiply(place, [c3[0]], prior)
-    across = turn(place, 3, 1, c3[1], after(across, upper))
+    across = turn(place, 3, 1, c3[1], across)
     q03 = multiply(place, [h0], across, lambda odd: 3 - 3 * odd, 1)
     q0_last = moved(q03, 1, 0)
-    h3 = [upper, multiply(place, [after(c3[1], q03)], prior)]
+    h3 = [multiply(place, [after(panel, q03)], prior) for panel in c3]
     q32 = multiply(place, h3, across, lambda odd: 2 - odd, 1)
     q3_two = moved(q32, 1, 3)
     q3_own, q33 = product_rest(place, h3, across, after(q03, q32))

time: 116 us -> 116 us (level)
  no operation moved by 1% of the time
where the time goes in v22:
time: 116 us
  waiting for transfers between devices  41.1 us (35%)
  starting transfers between devices  37.3 us (32%)
  Pallas kernels  32.6 us (28%)
  between operations  3.19 us (3%)
  local copies, waits for them, and re-layouts  1.69 us (1%)
    ppermute x15, waiting for transfers between devices, moved(): lax.ppermute(value, ('dom', 'col'), route(source, target, lax.axis_size('...  36.6 us
    ppermute x15, starting transfers between devices, moved(): lax.ppermute(value, ('dom', 'col'), route(source, target, lax.axis_size('...  29.7 us
    ppermute x2, starting transfers between devices, passed_along(): lax.ppermute(value, axis, [(source, source + steps) for source in range(i...  7.6 us
    pallas_call x6, Pallas kernels, turn(): pl.pallas_call(turn_kernel, out_shape=jax.ShapeDtypeStruct((nodes, nodes)...  5.99 us
    ppermute x2, waiting for transfers between devices, passed_along(): lax.ppermute(value, axis, [(source, source + steps) for source in range(i...  4.49 us
    pallas_call x7, Pallas kernels, multiply(): pl.pallas_call(functools.partial(multiply_kernel, first, count, len(lefts...  4.03 us
    pallas_call x2, Pallas kernels, couple(): pl.pallas_call(functools.partial(couple_kernel, part * rows), out_shape=j...  3.77 us
    pallas_call x1, Pallas kernels, finish(): pl.pallas_call(finish_kernel, out_shape=(jax.ShapeDtypeStruct((rows, node...  2.6 us
  transfers between devices with their start and end apart: 17, of which 8 were waited for; matrix products, arithmetic and copies ran while one was open for 0% of the time, Pallas kernels for 26%

profile of v22, /device:TPU:1, one launch (start us, length us, event | category | flops | bytes accessed | tf_op | source)
XLA Modules:
  0.0 115.8 jit_solution(10239230029233214783)
XLA Ops:
  0.6 2.0 %collective-permute-start.5 = (bf16[512,2048]{1,0:T(8,128)(2,1)}, bf16[512,2048]{1,0:T(8,128)(2,1)}, u32[]{:S(2)}, u32[]{:S(2)}) collective-permute-start(bf16[512,2048]{1,0:T(8,128)(2,1)} %bitcast.8), channel_id=1, source_target_pairs={{2,1},{5,6},{10,9},{13,14},{18,17},{21,22},{26,25},{29,30}} | collective-permute-start | bytes 6291464 | tf_op jit(solution)/shard_map/ppermute | solution.py:123
  4.8 1.6 %copy-done.1 = bf16[1,512,2048]{2,1,0:T(8,128)(2,1)S(1)} copy-done((bf16[1,512,2048]{2,1,0:T(8,128)(2,1)S(1)}, bf16[1,512,2048]{2,1,0:T(8,128)(2,1)}, u32[]{:S(2)}) %copy-start.1) | copy-done | bytes 2097176
  7.4 5.7 %collective-permute-start = (bf16[512,1024]{1,0:T(8,128)(2,1)S(1)}, bf16[512,1024]{1,0:T(8,128)(2,1)S(1)}, u32[]{:S(2)}, u32[]{:S(2)}) collective-permute-start(bf16[512,1024]{1,0:T(8,128)(2,1)S(1)} %get-tuple-element.31), channel_id=1, source_target_pairs={{4,0},{8,4},{12,8},{5,1},{9,5},{13,9},{6,2},{10,6},{14,10},{7,3},{... | collective-permute-start | bytes 3145736 | tf_op jit(solution)/shard_map/ppermute | solution.py:20
  13.1 1.9 %collective-permute-start.6 = (bf16[512,1024]{1,0:T(8,128)(2,1)S(1)}, bf16[512,1024]{1,0:T(8,128)(2,1)S(1)}, u32[]{:S(2)}, u32[]{:S(2)}) collective-permute-start(bf16[512,1024]{1,0:T(8,128)(2,1)S(1)} %get-tuple-element.37), channel_id=1, source_target_pairs={{4,0},{8,4},{12,8},{5,1},{9,5},{13,9},{6,2},{10,6},{14,10},{7,3},{... | collective-permute-start | bytes 3145736 | tf_op jit(solution)/shard_map/ppermute | solution.py:20
  15.7 1.8 %coupling.1.weight_ref.refs_1_ = bf16[8,512,256]{2,1,0:T(8,128)(2,1)S(1)} custom-call(s32[1,2048]{1,0:T(1,128)S(1)} %bitcast.20), custom_call_target="tpu_custom_call" | custom-call | flops 1048576 | bytes 65536 | tf_op jit(solution)/shard_map/coupling/pallas_call | solution.py:70
  17.5 1.9 %couple.3.coupled_ref.refs_1_ = bf16[256,2048]{1,0:T(8,128)(2,1)S(1)} custom-call(f32[1]{0:T(128)S(6)} %copy.23.rate_ref.refs_0_, bf16[8,512,256]{2,1,0:T(8,128)(2,1)S(1)} %coupling.1.weight_ref.refs_1_, bf16[512,2048]{1,0:T(8,128)(2,1)S(1)} %bitcast.10), custom_call_target="tpu_custom_call" | custom-call | flops 1048576 | bytes 65536 | tf_op jit(solution)/shard_map/couple/pallas_call | solution.py:99
  19.4 1.9 %couple.2.coupled_ref.refs_0_ = bf16[256,2048]{1,0:T(8,128)(2,1)S(1)} custom-call(f32[1]{0:T(128)S(6)} %copy.23.rate_ref.refs_0_, bf16[8,512,256]{2,1,0:T(8,128)(2,1)S(1)} %coupling.1.weight_ref.refs_1_, bf16[512,2048]{1,0:T(8,128)(2,1)S(1)} %bitcast.11), custom_call_target="tpu_custom_call" | custom-call | flops 1048576 | bytes 65536 | tf_op jit(solution)/shard_map/couple/pallas_call | solution.py:99
  23.1 3.5 %collective-permute-done.shifted_ref = bf16[512,1024]{1,0:T(8,128)(2,1)S(1)} collective-permute-done((bf16[512,1024]{1,0:T(8,128)(2,1)S(1)}, bf16[512,1024]{1,0:T(8,128)(2,1)S(1)}, u32[]{:S(2)}, u32[]{:S(2)}) %collective-permute-start) | collective-permute-done | bytes 1048608 | tf_op jit(solution)/shard_map/ppermute | solution.py:20
  29.1 4.9 %collective-permute-start.1 = (bf16[512,384]{1,0:T(8,128)(2,1)S(1)}, bf16[512,384]{1,0:T(8,128)(2,1)S(1)}, u32[]{:S(2)}, u32[]{:S(2)}) collective-permute-start(bf16[512,384]{1,0:T(8,128)(2,1)S(1)} %get-tuple-element.33), channel_id=1, source_target_pairs={{3,1},{4,6},{11,9},{12,14},{19,17},{20,22},{27,25},{28,30}} | collective-permute-start | bytes 1179656 | tf_op jit(solution)/shard_map/ppermute | solution.py:123
  34.1 1.6 %couple_here.2.coupled_ref.second_ref.left_ref = bf16[512,2048]{1,0:T(8,128)(2,1)S(1)} custom-call(s32[5]{0:T(128)S(1)} %stack.16.place_ref, f32[1]{0:T(128)S(6)} %copy.23.rate_ref.refs_0_, bf16[8,512,256]{2,1,0:T(8,128)(2,1)S(1)} %coupling.1.weight_ref.refs_1_, bf16[512,2048]{1,0:T(8,128)(2,1)} %collective-permute-done.5.refs_2_), custom_call_target="tpu_custom_call" | custom-call | flops 1048576 | bytes 65536 | tf_op jit(solution)/shard_map/couple_here/pallas_call | solution.py:133
  41.3 1.7 %collective-permute-done.1.last_three = bf16[512,384]{1,0:T(8,128)(2,1)S(1)} collective-permute-done((bf16[512,384]{1,0:T(8,128)(2,1)S(1)}, bf16[512,384]{1,0:T(8,128)(2,1)S(1)}, u32[]{:S(2)}, u32[]{:S(2)}) %collective-permute-start.1) | collective-permute-done | bytes 393248 | tf_op jit(solution)/shard_map/ppermute | solution.py:123
  43.0 8.2 %collective-permute-start.7 = (bf16[256,2048]{1,0:T(8,128)(2,1)S(1)}, bf16[256,2048]{1,0:T(8,128)(2,1)S(1)}, u32[]{:S(2)}, u32[]{:S(2)}) collective-permute-start(bf16[256,2048]{1,0:T(8,128)(2,1)S(1)} %couple.2.coupled_ref.refs_0_), channel_id=1, source_target_pairs={{3,1},{4,6},{11,9},{12,14},{19,17},{20,22},{27,25},{28,30}} | collective-permute-start | bytes 3145736 | tf_op jit(solution)/shard_map/ppermute | solution.py:123
  51.8 4.2 %collective-permute-start.9 = (bf16[256,2048]{1,0:T(8,128)(2,1)S(1)}, bf16[256,2048]{1,0:T(8,128)(2,1)S(1)}, u32[]{:S(2)}, u32[]{:S(2)}) collective-permute-start(bf16[256,2048]{1,0:T(8,128)(2,1)S(1)} %couple.3.coupled_ref.refs_1_), channel_id=1, source_target_pairs={{3,1},{4,6},{11,9},{12,14},{19,17},{20,22},{27,25},{28,30}} | collective-permute-start | bytes 3145736 | tf_op jit(solution)/shard_map/ppermute | solution.py:123
  60.3 2.6 %collective-permute-done.7.coupled_ref.refs_0_ = bf16[256,2048]{1,0:T(8,128)(2,1)S(1)} collective-permute-done((bf16[256,2048]{1,0:T(8,128)(2,1)S(1)}, bf16[256,2048]{1,0:T(8,128)(2,1)S(1)}, u32[]{:S(2)}, u32[]{:S(2)}) %collective-permute-start.7) | collective-permute-done | bytes 1048608 | tf_op jit(solution)/shard_map/ppermute | solution.py:123
  63.8 10.3 %collective-permute-done.9.coupled_ref.refs_0_ = bf16[256,2048]{1,0:T(8,128)(2,1)S(1)} collective-permute-done((bf16[256,2048]{1,0:T(8,128)(2,1)S(1)}, bf16[256,2048]{1,0:T(8,128)(2,1)S(1)}, u32[]{:S(2)}, u32[]{:S(2)}) %collective-permute-start.9) | collective-permute-done | bytes 1048608 | tf_op jit(solution)/shard_map/ppermute | solution.py:123
  78.1 1.3 %collective-permute-start.10 = (bf16[512,512]{1,0:T(8,128)(2,1)S(1)}, bf16[512,512]{1,0:T(8,128)(2,1)S(1)}, u32[]{:S(2)}, u32[]{:S(2)}) collective-permute-start(bf16[512,512]{1,0:T(8,128)(2,1)S(1)} %multiply.11), channel_id=1, source_target_pairs={{1,3},{6,4},{9,11},{14,12},{17,19},{22,20},{25,27},{30,28}} | collective-permute-start | bytes 1572872 | tf_op jit(solution)/shard_map/ppermute | solution.py:123
  80.0 1.3 %collective-permute-start.15 = (bf16[512,1024]{1,0:T(8,128)(2,1)S(1)}, bf16[512,1024]{1,0:T(8,128)(2,1)S(1)}, u32[]{:S(2)}, u32[]{:S(2)}) collective-permute-start(bf16[512,1024]{1,0:T(8,128)(2,1)S(1)} %get-tuple-element.54.q31), channel_id=1, source_target_pairs={{1,3},{6,4},{9,11},{14,12},{17,19},{22,20},{25,27},{30,28}} | collective-permute-start | bytes 3145736 | tf_op jit(solution)/shard_map/ppermute | solution.py:123
  86.0 12.1 %collective-permute-done.10.q3_two = bf16[512,512]{1,0:T(8,128)(2,1)S(1)} collective-permute-done((bf16[512,512]{1,0:T(8,128)(2,1)S(1)}, bf16[512,512]{1,0:T(8,128)(2,1)S(1)}, u32[]{:S(2)}, u32[]{:S(2)}) %collective-permute-start.10) | collective-permute-done | bytes 524320 | tf_op jit(solution)/shard_map/ppermute | solution.py:123
  98.2 1.3 %collective-permute-start.13 = (bf16[512,512]{1,0:T(8,128)(2,1)S(1)}, bf16[512,512]{1,0:T(8,128)(2,1)S(1)}, u32[]{:S(2)}, u32[]{:S(2)}) collective-permute-start(bf16[512,512]{1,0:T(8,128)(2,1)S(1)} %collective-permute-done.10.q3_two), channel_id=1, source_target_pairs={{3,2},{4,5},{11,10},{12,13},{19,18},{20,21},{27,26},{28,29}} | collective-permute-start | bytes 1572872 | tf_op jit(solution)/shard_map/ppermute | solution.py:123
  99.5 2.6 %finish.1 = (bf16[512,2048]{1,0:T(8,128)(2,1)}, f32[1,512]{1,0:T(1,128)S(1)}) custom-call(s32[5]{0:T(128)S(1)} %tick.3.place_ref, bf16[512,2048]{1,0:T(8,128)(2,1)S(1)} %bitcast.12, bf16[512,2048]{1,0:T(8,128)(2,1)S(1)} %bitcast.19, bf16[512,1536]{1,0:T(8,128)(2,1)S(1)} %collective-permute-done.11.refs_0_.q0, ...), custom_call_target="tpu_custom_call" | custom-call | flops 14000000000 | bytes 65536 | tf_op jit(solution)/shard_map/finish/pallas_call | solution.py:620
  102.1 7.3 %collective-permute-done.15.q3_other = bf16[512,1024]{1,0:T(8,128)(2,1)S(1)} collective-permute-done((bf16[512,1024]{1,0:T(8,128)(2,1)S(1)}, bf16[512,1024]{1,0:T(8,128)(2,1)S(1)}, u32[]{:S(2)}, u32[]{:S(2)}) %collective-permute-start.15) | collective-permute-done | bytes 1048608 | tf_op jit(solution)/shard_map/ppermute | solution.py:123
  109.4 1.7 %finish_other.1.old_ref = bf16[512,2048]{1,0:T(8,128)(2,1)} custom-call(s32[5]{0:T(128)S(1)} %stack.16.place_ref, bf16[512,2048]{1,0:T(8,128)(2,1)S(1)} %bitcast.13, bf16[512,1024]{1,0:T(8,128)(2,1)S(1)} %collective-permute-done.15.q3_other, bf16[512,2048]{1,0:T(8,128)(2,1)} %get-tuple-element.56.old_ref), custom_call_target="tpu_custom_call", output_to_operand_aliasing={{}: (3, {})} | custom-call | flops 1048576 | bytes 65536 | tf_op jit(solution)/shard_map/finish_other/pallas_call | solution.py:718
  111.1 2.5 %collective-permute-done.14.q3_last = bf16[512,384]{1,0:T(8,128)(2,1)S(1)} collective-permute-done((bf16[512,384]{1,0:T(8,128)(2,1)S(1)}, bf16[512,384]{1,0:T(8,128)(2,1)S(1)}, u32[]{:S(2)}, u32[]{:S(2)}) %collective-permute-start.14) | collective-permute-done | bytes 393248 | tf_op jit(solution)/shard_map/ppermute | solution.py:123
  113.6 2.1 %finish_last.1 = (bf16[512,2048]{1,0:T(8,128)(2,1)}, f32[1,512]{1,0:T(1,128)}) custom-call(s32[5]{0:T(128)S(1)} %stack.16.place_ref, bf16[512,2048]{1,0:T(8,128)(2,1)S(1)} %bitcast.14, bf16[512,512]{1,0:T(8,128)(2,1)S(1)} %collective-permute-done.13.q2_last, bf16[512,384]{1,0:T(8,128)(2,1)S(1)} %collective-permute-done.14.q3_last, ...), custom_call_target="tpu_custom_call", output_to_operand_aliasing={{0}: (4, {})} | custom-call | flops 1048576 | bytes 65536 | tf_op jit(solution)/shard_map/finish_last/pallas_call | solution.py:743
  (51 shorter events, 26.6 us)
Async XLA Ops:
  0.6 28.5 %collective-permute-start.5 = (bf16[512,2048]{1,0:T(8,128)(2,1)}, bf16[512,2048]{1,0:T(8,128)(2,1)}, u32[]{:S(2)}, u32[]{:S(2)}) collective-permute-start(bf16[512,2048]{1,0:T(8,128)(2,1)} %bitcast.8), channel_id=1, source_target_pairs={{2,1},{5,6},{10,9},{13,14},{18,17},{21,22},{26,25},{29,30}} | collective-permute-start | bytes 6291464 | tf_op jit(solution)/shard_map/ppermute | solution.py:123
  2.6 36.9 %collective-permute-start.4 = (bf16[512,2048]{1,0:T(8,128)(2,1)}, bf16[512,2048]{1,0:T(8,128)(2,1)S(1)}, u32[]{:S(2)}, u32[]{:S(2)}) collective-permute-start(bf16[512,2048]{1,0:T(8,128)(2,1)} %bitcast.9), channel_id=1, source_target_pairs={{0,1},{7,6},{8,9},{15,14},{16,17},{23,22},{24,25},{31,30}} | collective-permute-start | bytes 6291464 | tf_op jit(solution)/shard_map/ppermute | solution.py:123
  4.8 1.6 %copy-start.1 = (bf16[1,512,2048]{2,1,0:T(8,128)(2,1)S(1)}, bf16[1,512,2048]{2,1,0:T(8,128)(2,1)}, u32[]{:S(2)}) copy-start(bf16[1,512,2048]{2,1,0:T(8,128)(2,1)} %param.8) | copy-start | bytes 6291460
  6.4 9.3 %copy-start.3 = (s32[2048]{0:T(1024)S(1)}, s32[2048]{0:T(1024)}, u32[]{:S(2)}) copy-start(s32[2048]{0:T(1024)} %param.13) | copy-start | bytes 24580
  7.4 10.1 %copy-start = (bf16[1,512,2048]{2,1,0:T(8,128)(2,1)S(1)}, bf16[1,512,2048]{2,1,0:T(8,128)(2,1)}, u32[]{:S(2)}) copy-start(bf16[1,512,2048]{2,1,0:T(8,128)(2,1)} %param.9) | copy-start | bytes 6291460
  7.4 19.2 %collective-permute-start = (bf16[512,1024]{1,0:T(8,128)(2,1)S(1)}, bf16[512,1024]{1,0:T(8,128)(2,1)S(1)}, u32[]{:S(2)}, u32[]{:S(2)}) collective-permute-start(bf16[512,1024]{1,0:T(8,128)(2,1)S(1)} %get-tuple-element.31), channel_id=1, source_target_pairs={{4,0},{8,4},{12,8},{5,1},{9,5},{13,9},{6,2},{10,6},{14,10},{7,3},{... | collective-permute-start | bytes 3145736 | tf_op jit(solution)/shard_map/ppermute | solution.py:20
  13.1 24.8 %collective-permute-start.6 = (bf16[512,1024]{1,0:T(8,128)(2,1)S(1)}, bf16[512,1024]{1,0:T(8,128)(2,1)S(1)}, u32[]{:S(2)}, u32[]{:S(2)}) collective-permute-start(bf16[512,1024]{1,0:T(8,128)(2,1)S(1)} %get-tuple-element.37), channel_id=1, source_target_pairs={{4,0},{8,4},{12,8},{5,1},{9,5},{13,9},{6,2},{10,6},{14,10},{7,3},{... | collective-permute-start | bytes 3145736 | tf_op jit(solution)/shard_map/ppermute | solution.py:20
  22.2 4.4 %copy-start.2 = (bf16[1,512,2048]{2,1,0:T(8,128)(2,1)S(1)}, bf16[1,512,2048]{2,1,0:T(8,128)(2,1)}, u32[]{:S(2)}) copy-start(bf16[1,512,2048]{2,1,0:T(8,128)(2,1)} %param.7) | copy-start | bytes 6291460
  27.6 15.4 %collective-permute-start.3 = (bf16[512,1024]{1,0:T(8,128)(2,1)S(1)}, bf16[512,1024]{1,0:T(8,128)(2,1)S(1)}, u32[]{:S(2)}, u32[]{:S(2)}) collective-permute-start(bf16[512,1024]{1,0:T(8,128)(2,1)S(1)} %get-tuple-element.35.near_ref.near), channel_id=1, source_target_pairs={{0,1},{7,6},{8,9},{15,14},{16,17},{23,22},{24,25},{31,30}} | collective-permute-start | bytes 3145736 | tf_op jit(solution)/shard_map/ppermute | solution.py:123
  28.4 14.6 %collective-permute-start.2 = (bf16[512,896]{1,0:T(8,128)(2,1)S(1)}, bf16[512,896]{1,0:T(8,128)(2,1)S(1)}, u32[]{:S(2)}, u32[]{:S(2)}) collective-permute-start(bf16[512,896]{1,0:T(8,128)(2,1)S(1)} %get-tuple-element.34), channel_id=1, source_target_pairs={{2,1},{5,6},{10,9},{13,14},{18,17},{21,22},{26,25},{29,30}} | collective-permute-start | bytes 2752520 | tf_op jit(solution)/shard_map/ppermute | solution.py:123
  29.1 13.9 %collective-permute-start.1 = (bf16[512,384]{1,0:T(8,128)(2,1)S(1)}, bf16[512,384]{1,0:T(8,128)(2,1)S(1)}, u32[]{:S(2)}, u32[]{:S(2)}) collective-permute-start(bf16[512,384]{1,0:T(8,128)(2,1)S(1)} %get-tuple-element.33), channel_id=1, source_target_pairs={{3,1},{4,6},{11,9},{12,14},{19,17},{20,22},{27,25},{28,30}} | collective-permute-start | bytes 1179656 | tf_op jit(solution)/shard_map/ppermute | solution.py:123
  38.8 13.0 %collective-permute-start.8 = (bf16[512,384]{1,0:T(8,128)(2,1)S(1)}, bf16[512,384]{1,0:T(8,128)(2,1)S(1)}, u32[]{:S(2)}, u32[]{:S(2)}) collective-permute-start(bf16[512,384]{1,0:T(8,128)(2,1)S(1)} %get-tuple-element.39), channel_id=1, source_target_pairs={{0,1},{7,6},{8,9},{15,14},{16,17},{23,22},{24,25},{31,30}} | collective-permute-start | bytes 1179656 | tf_op jit(solution)/shard_map/ppermute | solution.py:123
  43.0 19.9 %collective-permute-start.7 = (bf16[256,2048]{1,0:T(8,128)(2,1)S(1)}, bf16[256,2048]{1,0:T(8,128)(2,1)S(1)}, u32[]{:S(2)}, u32[]{:S(2)}) collective-permute-start(bf16[256,2048]{1,0:T(8,128)(2,1)S(1)} %couple.2.coupled_ref.refs_0_), channel_id=1, source_target_pairs={{3,1},{4,6},{11,9},{12,14},{19,17},{20,22},{27,25},{28,30}} | collective-permute-start | bytes 3145736 | tf_op jit(solution)/shard_map/ppermute | solution.py:123
  51.8 22.3 %collective-permute-start.9 = (bf16[256,2048]{1,0:T(8,128)(2,1)S(1)}, bf16[256,2048]{1,0:T(8,128)(2,1)S(1)}, u32[]{:S(2)}, u32[]{:S(2)}) collective-permute-start(bf16[256,2048]{1,0:T(8,128)(2,1)S(1)} %couple.3.coupled_ref.refs_1_), channel_id=1, source_target_pairs={{3,1},{4,6},{11,9},{12,14},{19,17},{20,22},{27,25},{28,30}} | collective-permute-start | bytes 3145736 | tf_op jit(solution)/shard_map/ppermute | solution.py:123
  57.7 24.7 %collective-permute-start.11 = (bf16[512,1536]{1,0:T(8,128)(2,1)S(1)}, bf16[512,1536]{1,0:T(8,128)(2,1)S(1)}, u32[]{:S(2)}, u32[]{:S(2)}) collective-permute-start(bf16[512,1536]{1,0:T(8,128)(2,1)S(1)} %multiply.7.zero_ref.q01), channel_id=1, source_target_pairs={{1,0},{6,7},{9,8},{14,15},{17,16},{22,23},{25,24},{30,31}} | collective-permute-start | bytes 4718600 | tf_op jit(solution)/shard_map/ppermute | solution.py:123
  59.6 39.9 %collective-permute-start.16 = (bf16[512,1408]{1,0:T(8,128)(2,1)S(1)}, bf16[512,1408]{1,0:T(8,128)(2,1)S(1)}, u32[]{:S(2)}, u32[]{:S(2)}) collective-permute-start(bf16[512,1408]{1,0:T(8,128)(2,1)S(1)} %product_two.1.q21), channel_id=1, source_target_pairs={{1,2},{6,5},{9,10},{14,13},{17,18},{22,21},{25,26},{30,29}} | collective-permute-start | bytes 4325384 | tf_op jit(solution)/shard_map/ppermute | solution.py:123
  75.8 9.1 %collective-permute-start.12 = (bf16[512,512]{1,0:T(8,128)(2,1)S(1)}, bf16[512,512]{1,0:T(8,128)(2,1)S(1)}, u32[]{:S(2)}, u32[]{:S(2)}) collective-permute-start(bf16[512,512]{1,0:T(8,128)(2,1)S(1)} %multiply.8.zero_ref), channel_id=1, source_target_pairs={{1,0},{6,7},{9,8},{14,15},{17,16},{22,23},{25,24},{30,31}} | collective-permute-start | bytes 1572872 | tf_op jit(solution)/shard_map/ppermute | solution.py:123
  78.1 20.0 %collective-permute-start.10 = (bf16[512,512]{1,0:T(8,128)(2,1)S(1)}, bf16[512,512]{1,0:T(8,128)(2,1)S(1)}, u32[]{:S(2)}, u32[]{:S(2)}) collective-permute-start(bf16[512,512]{1,0:T(8,128)(2,1)S(1)} %multiply.11), channel_id=1, source_target_pairs={{1,3},{6,4},{9,11},{14,12},{17,19},{22,20},{25,27},{30,28}} | collective-permute-start | bytes 1572872 | tf_op jit(solution)/shard_map/ppermute | solution.py:123
  80.0 29.4 %collective-permute-start.15 = (bf16[512,1024]{1,0:T(8,128)(2,1)S(1)}, bf16[512,1024]{1,0:T(8,128)(2,1)S(1)}, u32[]{:S(2)}, u32[]{:S(2)}) collective-permute-start(bf16[512,1024]{1,0:T(8,128)(2,1)S(1)} %get-tuple-element.54.q31), channel_id=1, source_target_pairs={{1,3},{6,4},{9,11},{14,12},{17,19},{22,20},{25,27},{30,28}} | collective-permute-start | bytes 3145736 | tf_op jit(solution)/shard_map/ppermute | solution.py:123
  82.4 31.2 %collective-permute-start.14 = (bf16[512,384]{1,0:T(8,128)(2,1)S(1)}, bf16[512,384]{1,0:T(8,128)(2,1)S(1)}, u32[]{:S(2)}, u32[]{:S(2)}) collective-permute-start(bf16[512,384]{1,0:T(8,128)(2,1)S(1)} %get-tuple-element.53), channel_id=1, source_target_pairs={{1,3},{6,4},{9,11},{14,12},{17,19},{22,20},{25,27},{30,28}} | collective-permute-start | bytes 1179656 | tf_op jit(solution)/shard_map/ppermute | solution.py:123
  98.2 15.5 %collective-permute-start.13 = (bf16[512,512]{1,0:T(8,128)(2,1)S(1)}, bf16[512,512]{1,0:T(8,128)(2,1)S(1)}, u32[]{:S(2)}, u32[]{:S(2)}) collective-permute-start(bf16[512,512]{1,0:T(8,128)(2,1)S(1)} %collective-permute-done.10.q3_two), channel_id=1, source_target_pairs={{3,2},{4,5},{11,10},{12,13},{19,18},{20,21},{27,26},{28,29}} | collective-permute-start | bytes 1572872 | tf_op jit(solution)/shard_map/ppermute | solution.py:123

commit v23 on v22

--- a/solution.py
+++ b/solution.py
@@ -313,31 +313,28 @@
     )(place, near, other, first, second)
 
 
-def rest_kernel(place_ref, upper_ref, lower_ref, right_ref, zero_ref, out_ref, last_ref):
+def rest_kernel(place_ref, left_ref, right_ref, zero_ref, out_ref, last_ref):
     odd = place_ref[0]
     width = zero_ref.shape[1]
     half = width // 2
 
-    def product(left_ref, block):
+    def product(rows, block):
         columns = pl.ds(pl.multiple_of(block * width, 128), width)
-        value = jnp.dot(left_ref[...], right_ref[:, columns], preferred_element_type=F32)
+        value = jnp.dot(left_ref[rows, :], right_ref[:, columns], preferred_element_type=F32)
         return value.astype(BF16)
 
     @pl.when(place_ref[1] == 1)
     def _():
         out_ref[:, pl.ds(pl.multiple_of(odd * width, 128), width)] = zero_ref[...].T
         other = pl.ds(pl.multiple_of((1 - odd) * width, 128), width)
-        for part, left_ref in enumerate((upper_ref, lower_ref)):
-            out_ref[pl.ds(part * half, half), other] = product(left_ref, 1 + odd)
-            value = product(left_ref, 3 - 3 * odd)
-            for quarter in range(2):
-                start = quarter * half // 2
-                rows = pl.ds(part * half + start, half // 2)
-                rows_of = value[start : start + half // 2]
-                pack_rows(2 * part + quarter, rows_of, last_ref.at[rows], 0)
-
-
-def product_rest(place, halves, across, zero):
+        out_ref[:, other] = product(pl.ds(0, width), 1 + odd)
+        value = product(pl.ds(0, width), 3 - 3 * odd)
+        for part in range(4):
+            rows = pl.ds(part * half // 2, half // 2)
+            pack_rows(part, value[part * half // 2 : (part + 1) * half // 2], last_ref.at[rows], 0)
+
+
+def product_rest(place, left, across, zero):
     rows, width = zero.shape
     vmem = pl.BlockSpec(memory_space=pltpu.VMEM)
     return pl.pallas_call(
@@ -346,12 +343,12 @@
             jax.ShapeDtypeStruct((rows, 2 * width), BF16),
             jax.ShapeDtypeStruct((rows, 3 * width // 4), BF16),
         ),
-        in_specs=[pl.BlockSpec(memory_space=pltpu.SMEM)] + [vmem] * 4,
+        in_specs=[pl.BlockSpec(memory_space=pltpu.SMEM)] + [vmem] * 3,
         out_specs=(vmem, vmem),
         compiler_params=pltpu.CompilerParams(vmem_limit_bytes=6 * MIB),
         cost_estimate=LIGHT,
         name="product_rest",
-    )(place, *halves, across, zero)
+    )(place, left, across, zero)
 
 
 def pack_rows(part, value, out_ref, column):
@@ -799,7 +796,7 @@
     across = turn(place, 0, 0, c0, across)
     column, h0_one, h2_one = own_column(place, row_near, row_other, c0, c2)
     c3 = [
-        moved(after(c1[0], last_three, near_two, near_zero, across), 3, 1),
+        moved(after(c1[0], last_three, near_two, near_zero, h2_one, across), 3, 1),
         moved(after(c1[1], far_zero, h2_one), 3, 1),
     ]
     prior = assemble(place, row_near, row_other, column, near_two, last_three, near_zero, far_zero)
@@ -815,8 +812,8 @@
     across = turn(place, 3, 1, c3[1], across)
     q03 = multiply(place, [h0], across, lambda odd: 3 - 3 * odd, 1)
     q0_last = moved(q03, 1, 0)
-    h3 = [multiply(place, [after(panel, q03)], prior) for panel in c3]
-    q32 = multiply(place, h3, across, lambda odd: 2 - odd, 1)
+    h3 = multiply(place, [after(c3[0], q03), c3[1]], prior)
+    q32 = multiply(place, [h3], across, lambda odd: 2 - odd, 1)
     q3_two = moved(q32, 1, 3)
     q3_own, q33 = product_rest(place, h3, across, after(q03, q32))
     q3_other, q3_last = moved(q3_own, 1, 3), moved(q33, 1, 3)

time: 116 us -> 116 us (level)
  Pallas kernels: 32.6 us -> 30.3 us
  waiting for transfers between devices: 41.1 us -> 43 us
    ppermute x15, waiting for transfers between devices: 36.6 us -> 38.5 us  [moved(): lax.ppermute(value, ('dom', 'col'), route(source, target, lax.axis_size('...]
    pallas_call x7 -> x6, Pallas kernels: 4.03 us -> 3.48 us  [multiply(): pl.pallas_call(functools.partial(multiply_kernel, first, count, len(lefts...]
  transfers between devices with their start and end apart: 17 -> 17, of which waited for: 8 -> 8; matrix products, arithmetic and copies ran while one was open for 0% -> 0% of each run, Pallas kernels for 26% -> 25%
where the time goes in v23:
time: 116 us; the launch traced here: 115 us
  waiting for transfers between devices  43 us (37%)
  starting transfers between devices  37.2 us (32%)
  Pallas kernels  30.3 us (26%)
  between operations  3.19 us (3%)
  local copies, waits for them, and re-layouts  1.69 us (1%)
    ppermute x15, waiting for transfers between devices, moved(): lax.ppermute(value, ('dom', 'col'), route(source, target, lax.axis_size('...  38.5 us
    ppermute x15, starting transfers between devices, moved(): lax.ppermute(value, ('dom', 'col'), route(source, target, lax.axis_size('...  29.7 us
    ppermute x2, starting transfers between devices, passed_along(): lax.ppermute(value, axis, [(source, source + steps) for source in range(i...  7.6 us
    pallas_call x6, Pallas kernels, turn(): pl.pallas_call(turn_kernel, out_shape=jax.ShapeDtypeStruct((nodes, nodes)...  5.99 us
    ppermute x2, waiting for transfers between devices, passed_along(): lax.ppermute(value, axis, [(source, source + steps) for source in range(i...  4.44 us
    pallas_call x2, Pallas kernels, couple(): pl.pallas_call(functools.partial(couple_kernel, part * rows), out_shape=j...  3.77 us
    pallas_call x6, Pallas kernels, multiply(): pl.pallas_call(functools.partial(multiply_kernel, first, count, len(lefts...  3.48 us
    pallas_call x1, Pallas kernels, finish(): pl.pallas_call(finish_kernel, out_shape=(jax.ShapeDtypeStruct((rows, node...  2.64 us
  transfers between devices with their start and end apart: 17, of which 8 were waited for; matrix products, arithmetic and copies ran while one was open for 0% of the time, Pallas kernels for 25%

profile of v23, /device:TPU:1, one launch (start us, length us, event | category | flops | bytes accessed | tf_op | source)
XLA Modules:
  0.0 115.4 jit_solution(17489495885053277379)
XLA Ops:
  0.6 2.0 %collective-permute-start.5 = (bf16[512,2048]{1,0:T(8,128)(2,1)}, bf16[512,2048]{1,0:T(8,128)(2,1)}, u32[]{:S(2)}, u32[]{:S(2)}) collective-permute-start(bf16[512,2048]{1,0:T(8,128)(2,1)} %bitcast.8), channel_id=1, source_target_pairs={{2,1},{5,6},{10,9},{13,14},{18,17},{21,22},{26,25},{29,30}} | collective-permute-start | bytes 6291464 | tf_op jit(solution)/shard_map/ppermute | solution.py:123
  4.8 1.6 %copy-done.1 = bf16[1,512,2048]{2,1,0:T(8,128)(2,1)S(1)} copy-done((bf16[1,512,2048]{2,1,0:T(8,128)(2,1)S(1)}, bf16[1,512,2048]{2,1,0:T(8,128)(2,1)}, u32[]{:S(2)}) %copy-start.1) | copy-done | bytes 2097176
  7.4 5.7 %collective-permute-start = (bf16[512,1024]{1,0:T(8,128)(2,1)S(1)}, bf16[512,1024]{1,0:T(8,128)(2,1)S(1)}, u32[]{:S(2)}, u32[]{:S(2)}) collective-permute-start(bf16[512,1024]{1,0:T(8,128)(2,1)S(1)} %get-tuple-element.30), channel_id=1, source_target_pairs={{4,0},{8,4},{12,8},{5,1},{9,5},{13,9},{6,2},{10,6},{14,10},{7,3},{... | collective-permute-start | bytes 3145736 | tf_op jit(solution)/shard_map/ppermute | solution.py:20
  13.1 1.9 %collective-permute-start.4 = (bf16[512,1024]{1,0:T(8,128)(2,1)S(1)}, bf16[512,1024]{1,0:T(8,128)(2,1)S(1)}, u32[]{:S(2)}, u32[]{:S(2)}) collective-permute-start(bf16[512,1024]{1,0:T(8,128)(2,1)S(1)} %get-tuple-element.35), channel_id=1, source_target_pairs={{4,0},{8,4},{12,8},{5,1},{9,5},{13,9},{6,2},{10,6},{14,10},{7,3},{... | collective-permute-start | bytes 3145736 | tf_op jit(solution)/shard_map/ppermute | solution.py:20
  15.7 1.8 %coupling.1.weight_ref.refs_1_ = bf16[8,512,256]{2,1,0:T(8,128)(2,1)S(1)} custom-call(s32[1,2048]{1,0:T(1,128)S(1)} %bitcast.20), custom_call_target="tpu_custom_call" | custom-call | flops 1048576 | bytes 65536 | tf_op jit(solution)/shard_map/coupling/pallas_call | solution.py:70
  17.5 1.9 %couple.3.coupled_ref.refs_1_ = bf16[256,2048]{1,0:T(8,128)(2,1)S(1)} custom-call(f32[1]{0:T(128)S(6)} %copy.23.rate_ref.refs_0_, bf16[8,512,256]{2,1,0:T(8,128)(2,1)S(1)} %coupling.1.weight_ref.refs_1_, bf16[512,2048]{1,0:T(8,128)(2,1)S(1)} %bitcast.10), custom_call_target="tpu_custom_call" | custom-call | flops 1048576 | bytes 65536 | tf_op jit(solution)/shard_map/couple/pallas_call | solution.py:99
  19.4 1.9 %couple.2.coupled_ref.refs_0_ = bf16[256,2048]{1,0:T(8,128)(2,1)S(1)} custom-call(f32[1]{0:T(128)S(6)} %copy.23.rate_ref.refs_0_, bf16[8,512,256]{2,1,0:T(8,128)(2,1)S(1)} %coupling.1.weight_ref.refs_1_, bf16[512,2048]{1,0:T(8,128)(2,1)S(1)} %bitcast.11), custom_call_target="tpu_custom_call" | custom-call | flops 1048576 | bytes 65536 | tf_op jit(solution)/shard_map/couple/pallas_call | solution.py:99
  23.1 3.5 %collective-permute-done.shifted_ref = bf16[512,1024]{1,0:T(8,128)(2,1)S(1)} collective-permute-done((bf16[512,1024]{1,0:T(8,128)(2,1)S(1)}, bf16[512,1024]{1,0:T(8,128)(2,1)S(1)}, u32[]{:S(2)}, u32[]{:S(2)}) %collective-permute-start) | collective-permute-done | bytes 1048608 | tf_op jit(solution)/shard_map/ppermute | solution.py:20
  29.2 4.9 %collective-permute-start.1 = (bf16[512,384]{1,0:T(8,128)(2,1)S(1)}, bf16[512,384]{1,0:T(8,128)(2,1)S(1)}, u32[]{:S(2)}, u32[]{:S(2)}) collective-permute-start(bf16[512,384]{1,0:T(8,128)(2,1)S(1)} %get-tuple-element.32), channel_id=1, source_target_pairs={{3,1},{4,6},{11,9},{12,14},{19,17},{20,22},{27,25},{28,30}} | collective-permute-start | bytes 1179656 | tf_op jit(solution)/shard_map/ppermute | solution.py:123
  34.1 1.6 %couple_here.2.coupled_ref.second_ref.left_ref = bf16[512,2048]{1,0:T(8,128)(2,1)S(1)} custom-call(s32[5]{0:T(128)S(1)} %stack.16.place_ref, f32[1]{0:T(128)S(6)} %copy.23.rate_ref.refs_0_, bf16[8,512,256]{2,1,0:T(8,128)(2,1)S(1)} %coupling.1.weight_ref.refs_1_, bf16[512,2048]{1,0:T(8,128)(2,1)} %collective-permute-done.5.refs_2_), custom_call_target="tpu_custom_call" | custom-call | flops 1048576 | bytes 65536 | tf_op jit(solution)/shard_map/couple_here/pallas_call | solution.py:133
  35.7 1.2 %turn.8.refs_0_ = bf16[2048,2048]{1,0:T(8,128)(2,1)S(1)} custom-call(s32[5]{0:T(128)S(1)} %stack.16.place_ref, bf16[512,2048]{1,0:T(8,128)(2,1)S(1)} %couple_here.2.coupled_ref.second_ref.left_ref, bf16[2048,2048]{1,0:T(8,128)(2,1)S(1)} %turn.7.refs_0_), custom_call_target="tpu_custom_call", output_to_operand_aliasing={{}: (2, {})} | custom-call | flops 1048576 | bytes 65536 | tf_op jit(solution)/shard_map/turn/pallas_call | solution.py:155
  40.1 1.2 %turn.9.refs_1_.right_ref.refs_0_ = bf16[2048,2048]{1,0:T(8,128)(2,1)S(1)} custom-call(s32[5]{0:T(128)S(1)} %stack.16.place_ref, bf16[512,2048]{1,0:T(8,128)(2,1)S(1)} %couple_here.3.first_ref.coupled_ref.left_ref, bf16[2048,2048]{1,0:T(8,128)(2,1)S(1)} %turn.8.refs_0_), custom_call_target="tpu_custom_call", output_to_operand_aliasing={{}: (2, {})} | custom-call | flops 1048576 | bytes 65536 | tf_op jit(solution)/shard_map/turn/pallas_call | solution.py:155
  43.1 9.4 %collective-permute-start.7 = (bf16[256,2048]{1,0:T(8,128)(2,1)S(1)}, bf16[256,2048]{1,0:T(8,128)(2,1)S(1)}, u32[]{:S(2)}, u32[]{:S(2)}) collective-permute-start(bf16[256,2048]{1,0:T(8,128)(2,1)S(1)} %couple.2.coupled_ref.refs_0_), channel_id=1, source_target_pairs={{3,1},{4,6},{11,9},{12,14},{19,17},{20,22},{27,25},{28,30}} | collective-permute-start | bytes 3145736 | tf_op jit(solution)/shard_map/ppermute | solution.py:123
  52.5 3.0 %collective-permute-start.9 = (bf16[256,2048]{1,0:T(8,128)(2,1)S(1)}, bf16[256,2048]{1,0:T(8,128)(2,1)S(1)}, u32[]{:S(2)}, u32[]{:S(2)}) collective-permute-start(bf16[256,2048]{1,0:T(8,128)(2,1)S(1)} %couple.3.coupled_ref.refs_1_), channel_id=1, source_target_pairs={{3,1},{4,6},{11,9},{12,14},{19,17},{20,22},{27,25},{28,30}} | collective-permute-start | bytes 3145736 | tf_op jit(solution)/shard_map/ppermute | solution.py:123
  59.8 4.3 %collective-permute-done.7.coupled_ref.refs_0_ = bf16[256,2048]{1,0:T(8,128)(2,1)S(1)} collective-permute-done((bf16[256,2048]{1,0:T(8,128)(2,1)S(1)}, bf16[256,2048]{1,0:T(8,128)(2,1)S(1)}, u32[]{:S(2)}, u32[]{:S(2)}) %collective-permute-start.7) | collective-permute-done | bytes 1048608 | tf_op jit(solution)/shard_map/ppermute | solution.py:123
  65.0 10.3 %collective-permute-done.9.coupled_ref.refs_1_ = bf16[256,2048]{1,0:T(8,128)(2,1)S(1)} collective-permute-done((bf16[256,2048]{1,0:T(8,128)(2,1)S(1)}, bf16[256,2048]{1,0:T(8,128)(2,1)S(1)}, u32[]{:S(2)}, u32[]{:S(2)}) %collective-permute-start.9) | collective-permute-done | bytes 1048608 | tf_op jit(solution)/shard_map/ppermute | solution.py:123
  78.8 1.3 %collective-permute-start.10 = (bf16[512,512]{1,0:T(8,128)(2,1)S(1)}, bf16[512,512]{1,0:T(8,128)(2,1)S(1)}, u32[]{:S(2)}, u32[]{:S(2)}) collective-permute-start(bf16[512,512]{1,0:T(8,128)(2,1)S(1)} %multiply.9), channel_id=1, source_target_pairs={{1,3},{6,4},{9,11},{14,12},{17,19},{22,20},{25,27},{30,28}} | collective-permute-start | bytes 1572872 | tf_op jit(solution)/shard_map/ppermute | solution.py:123
  80.7 1.3 %collective-permute-start.15 = (bf16[512,1024]{1,0:T(8,128)(2,1)S(1)}, bf16[512,1024]{1,0:T(8,128)(2,1)S(1)}, u32[]{:S(2)}, u32[]{:S(2)}) collective-permute-start(bf16[512,1024]{1,0:T(8,128)(2,1)S(1)} %get-tuple-element.52.q31), channel_id=1, source_target_pairs={{1,3},{6,4},{9,11},{14,12},{17,19},{22,20},{25,27},{30,28}} | collective-permute-start | bytes 3145736 | tf_op jit(solution)/shard_map/ppermute | solution.py:123
  83.1 1.3 %collective-permute-start.14 = (bf16[512,384]{1,0:T(8,128)(2,1)S(1)}, bf16[512,384]{1,0:T(8,128)(2,1)S(1)}, u32[]{:S(2)}, u32[]{:S(2)}) collective-permute-start(bf16[512,384]{1,0:T(8,128)(2,1)S(1)} %get-tuple-element.51), channel_id=1, source_target_pairs={{1,3},{6,4},{9,11},{14,12},{17,19},{22,20},{25,27},{30,28}} | collective-permute-start | bytes 1179656 | tf_op jit(solution)/shard_map/ppermute | solution.py:123
  86.7 11.9 %collective-permute-done.10.q3_two = bf16[512,512]{1,0:T(8,128)(2,1)S(1)} collective-permute-done((bf16[512,512]{1,0:T(8,128)(2,1)S(1)}, bf16[512,512]{1,0:T(8,128)(2,1)S(1)}, u32[]{:S(2)}, u32[]{:S(2)}) %collective-permute-start.10) | collective-permute-done | bytes 524320 | tf_op jit(solution)/shard_map/ppermute | solution.py:123
  98.6 1.3 %collective-permute-start.13 = (bf16[512,512]{1,0:T(8,128)(2,1)S(1)}, bf16[512,512]{1,0:T(8,128)(2,1)S(1)}, u32[]{:S(2)}, u32[]{:S(2)}) collective-permute-start(bf16[512,512]{1,0:T(8,128)(2,1)S(1)} %collective-permute-done.10.q3_two), channel_id=1, source_target_pairs={{3,2},{4,5},{11,10},{12,13},{19,18},{20,21},{27,26},{28,29}} | collective-permute-start | bytes 1572872 | tf_op jit(solution)/shard_map/ppermute | solution.py:123
  99.9 2.6 %finish.1 = (bf16[512,2048]{1,0:T(8,128)(2,1)}, f32[1,512]{1,0:T(1,128)S(1)}) custom-call(s32[5]{0:T(128)S(1)} %tick.3.place_ref, bf16[512,2048]{1,0:T(8,128)(2,1)S(1)} %bitcast.12, bf16[512,2048]{1,0:T(8,128)(2,1)S(1)} %bitcast.19, bf16[512,1536]{1,0:T(8,128)(2,1)S(1)} %collective-permute-done.11.refs_0_.q0, ...), custom_call_target="tpu_custom_call" | custom-call | flops 14000000000 | bytes 65536 | tf_op jit(solution)/shard_map/finish/pallas_call | solution.py:617
  102.6 7.3 %collective-permute-done.15.q3_other = bf16[512,1024]{1,0:T(8,128)(2,1)S(1)} collective-permute-done((bf16[512,1024]{1,0:T(8,128)(2,1)S(1)}, bf16[512,1024]{1,0:T(8,128)(2,1)S(1)}, u32[]{:S(2)}, u32[]{:S(2)}) %collective-permute-start.15) | collective-permute-done | bytes 1048608 | tf_op jit(solution)/shard_map/ppermute | solution.py:123
  110.5 3.6 %collective-permute-done.14.q3_last = bf16[512,384]{1,0:T(8,128)(2,1)S(1)} collective-permute-done((bf16[512,384]{1,0:T(8,128)(2,1)S(1)}, bf16[512,384]{1,0:T(8,128)(2,1)S(1)}, u32[]{:S(2)}, u32[]{:S(2)}) %collective-permute-start.14) | collective-permute-done | bytes 393248 | tf_op jit(solution)/shard_map/ppermute | solution.py:123
  (50 shorter events, 25.3 us)
Async XLA Ops:
  0.6 28.5 %collective-permute-start.5 = (bf16[512,2048]{1,0:T(8,128)(2,1)}, bf16[512,2048]{1,0:T(8,128)(2,1)}, u32[]{:S(2)}, u32[]{:S(2)}) collective-permute-start(bf16[512,2048]{1,0:T(8,128)(2,1)} %bitcast.8), channel_id=1, source_target_pairs={{2,1},{5,6},{10,9},{13,14},{18,17},{21,22},{26,25},{29,30}} | collective-permute-start | bytes 6291464 | tf_op jit(solution)/shard_map/ppermute | solution.py:123
  2.6 36.9 %collective-permute-start.6 = (bf16[512,2048]{1,0:T(8,128)(2,1)}, bf16[512,2048]{1,0:T(8,128)(2,1)S(1)}, u32[]{:S(2)}, u32[]{:S(2)}) collective-permute-start(bf16[512,2048]{1,0:T(8,128)(2,1)} %bitcast.9), channel_id=1, source_target_pairs={{0,1},{7,6},{8,9},{15,14},{16,17},{23,22},{24,25},{31,30}} | collective-permute-start | bytes 6291464 | tf_op jit(solution)/shard_map/ppermute | solution.py:123
  4.8 1.6 %copy-start.1 = (bf16[1,512,2048]{2,1,0:T(8,128)(2,1)S(1)}, bf16[1,512,2048]{2,1,0:T(8,128)(2,1)}, u32[]{:S(2)}) copy-start(bf16[1,512,2048]{2,1,0:T(8,128)(2,1)} %param.8) | copy-start | bytes 6291460
  6.4 9.3 %copy-start.3 = (s32[2048]{0:T(1024)S(1)}, s32[2048]{0:T(1024)}, u32[]{:S(2)}) copy-start(s32[2048]{0:T(1024)} %param.13) | copy-start | bytes 24580
  7.4 10.1 %copy-start = (bf16[1,512,2048]{2,1,0:T(8,128)(2,1)S(1)}, bf16[1,512,2048]{2,1,0:T(8,128)(2,1)}, u32[]{:S(2)}) copy-start(bf16[1,512,2048]{2,1,0:T(8,128)(2,1)} %param.9) | copy-start | bytes 6291460
  7.4 19.2 %collective-permute-start = (bf16[512,1024]{1,0:T(8,128)(2,1)S(1)}, bf16[512,1024]{1,0:T(8,128)(2,1)S(1)}, u32[]{:S(2)}, u32[]{:S(2)}) collective-permute-start(bf16[512,1024]{1,0:T(8,128)(2,1)S(1)} %get-tuple-element.30), channel_id=1, source_target_pairs={{4,0},{8,4},{12,8},{5,1},{9,5},{13,9},{6,2},{10,6},{14,10},{7,3},{... | collective-permute-start | bytes 3145736 | tf_op jit(solution)/shard_map/ppermute | solution.py:20
  13.1 24.8 %collective-permute-start.4 = (bf16[512,1024]{1,0:T(8,128)(2,1)S(1)}, bf16[512,1024]{1,0:T(8,128)(2,1)S(1)}, u32[]{:S(2)}, u32[]{:S(2)}) collective-permute-start(bf16[512,1024]{1,0:T(8,128)(2,1)S(1)} %get-tuple-element.35), channel_id=1, source_target_pairs={{4,0},{8,4},{12,8},{5,1},{9,5},{13,9},{6,2},{10,6},{14,10},{7,3},{... | collective-permute-start | bytes 3145736 | tf_op jit(solution)/shard_map/ppermute | solution.py:20
  22.2 4.4 %copy-start.2 = (bf16[1,512,2048]{2,1,0:T(8,128)(2,1)S(1)}, bf16[1,512,2048]{2,1,0:T(8,128)(2,1)}, u32[]{:S(2)}) copy-start(bf16[1,512,2048]{2,1,0:T(8,128)(2,1)} %param.7) | copy-start | bytes 6291460
  27.7 15.4 %collective-permute-start.3 = (bf16[512,1024]{1,0:T(8,128)(2,1)S(1)}, bf16[512,1024]{1,0:T(8,128)(2,1)S(1)}, u32[]{:S(2)}, u32[]{:S(2)}) collective-permute-start(bf16[512,1024]{1,0:T(8,128)(2,1)S(1)} %get-tuple-element.34.near_ref.near), channel_id=1, source_target_pairs={{0,1},{7,6},{8,9},{15,14},{16,17},{23,22},{24,25},{31,30}} | collective-permute-start | bytes 3145736 | tf_op jit(solution)/shard_map/ppermute | solution.py:123
  28.4 14.6 %collective-permute-start.2 = (bf16[512,896]{1,0:T(8,128)(2,1)S(1)}, bf16[512,896]{1,0:T(8,128)(2,1)S(1)}, u32[]{:S(2)}, u32[]{:S(2)}) collective-permute-start(bf16[512,896]{1,0:T(8,128)(2,1)S(1)} %get-tuple-element.33), channel_id=1, source_target_pairs={{2,1},{5,6},{10,9},{13,14},{18,17},{21,22},{26,25},{29,30}} | collective-permute-start | bytes 2752520 | tf_op jit(solution)/shard_map/ppermute | solution.py:123
  29.2 13.9 %collective-permute-start.1 = (bf16[512,384]{1,0:T(8,128)(2,1)S(1)}, bf16[512,384]{1,0:T(8,128)(2,1)S(1)}, u32[]{:S(2)}, u32[]{:S(2)}) collective-permute-start(bf16[512,384]{1,0:T(8,128)(2,1)S(1)} %get-tuple-element.32), channel_id=1, source_target_pairs={{3,1},{4,6},{11,9},{12,14},{19,17},{20,22},{27,25},{28,30}} | collective-permute-start | bytes 1179656 | tf_op jit(solution)/shard_map/ppermute | solution.py:123
  38.9 13.6 %collective-permute-start.8 = (bf16[512,384]{1,0:T(8,128)(2,1)S(1)}, bf16[512,384]{1,0:T(8,128)(2,1)S(1)}, u32[]{:S(2)}, u32[]{:S(2)}) collective-permute-start(bf16[512,384]{1,0:T(8,128)(2,1)S(1)} %get-tuple-element.39), channel_id=1, source_target_pairs={{0,1},{7,6},{8,9},{15,14},{16,17},{23,22},{24,25},{31,30}} | collective-permute-start | bytes 1179656 | tf_op jit(solution)/shard_map/ppermute | solution.py:123
  43.1 21.0 %collective-permute-start.7 = (bf16[256,2048]{1,0:T(8,128)(2,1)S(1)}, bf16[256,2048]{1,0:T(8,128)(2,1)S(1)}, u32[]{:S(2)}, u32[]{:S(2)}) collective-permute-start(bf16[256,2048]{1,0:T(8,128)(2,1)S(1)} %couple.2.coupled_ref.refs_0_), channel_id=1, source_target_pairs={{3,1},{4,6},{11,9},{12,14},{19,17},{20,22},{27,25},{28,30}} | collective-permute-start | bytes 3145736 | tf_op jit(solution)/shard_map/ppermute | solution.py:123
  52.5 22.9 %collective-permute-start.9 = (bf16[256,2048]{1,0:T(8,128)(2,1)S(1)}, bf16[256,2048]{1,0:T(8,128)(2,1)S(1)}, u32[]{:S(2)}, u32[]{:S(2)}) collective-permute-start(bf16[256,2048]{1,0:T(8,128)(2,1)S(1)} %couple.3.coupled_ref.refs_1_), channel_id=1, source_target_pairs={{3,1},{4,6},{11,9},{12,14},{19,17},{20,22},{27,25},{28,30}} | collective-permute-start | bytes 3145736 | tf_op jit(solution)/shard_map/ppermute | solution.py:123
  57.2 25.9 %collective-permute-start.11 = (bf16[512,1536]{1,0:T(8,128)(2,1)S(1)}, bf16[512,1536]{1,0:T(8,128)(2,1)S(1)}, u32[]{:S(2)}, u32[]{:S(2)}) collective-permute-start(bf16[512,1536]{1,0:T(8,128)(2,1)S(1)} %multiply.6.zero_ref.q01), channel_id=1, source_target_pairs={{1,0},{6,7},{9,8},{14,15},{17,16},{22,23},{25,24},{30,31}} | collective-permute-start | bytes 4718600 | tf_op jit(solution)/shard_map/ppermute | solution.py:123
  59.1 40.8 %collective-permute-start.16 = (bf16[512,1408]{1,0:T(8,128)(2,1)S(1)}, bf16[512,1408]{1,0:T(8,128)(2,1)S(1)}, u32[]{:S(2)}, u32[]{:S(2)}) collective-permute-start(bf16[512,1408]{1,0:T(8,128)(2,1)S(1)} %product_two.1.q21), channel_id=1, source_target_pairs={{1,2},{6,5},{9,10},{14,13},{17,18},{22,21},{25,26},{30,29}} | collective-permute-start | bytes 4325384 | tf_op jit(solution)/shard_map/ppermute | solution.py:123
  77.0 8.6 %collective-permute-start.12 = (bf16[512,512]{1,0:T(8,128)(2,1)S(1)}, bf16[512,512]{1,0:T(8,128)(2,1)S(1)}, u32[]{:S(2)}, u32[]{:S(2)}) collective-permute-start(bf16[512,512]{1,0:T(8,128)(2,1)S(1)} %multiply.7.zero_ref), channel_id=1, source_target_pairs={{1,0},{6,7},{9,8},{14,15},{17,16},{22,23},{25,24},{30,31}} | collective-permute-start | bytes 1572872 | tf_op jit(solution)/shard_map/ppermute | solution.py:123
  78.8 19.8 %collective-permute-start.10 = (bf16[512,512]{1,0:T(8,128)(2,1)S(1)}, bf16[512,512]{1,0:T(8,128)(2,1)S(1)}, u32[]{:S(2)}, u32[]{:S(2)}) collective-permute-start(bf16[512,512]{1,0:T(8,128)(2,1)S(1)} %multiply.9), channel_id=1, source_target_pairs={{1,3},{6,4},{9,11},{14,12},{17,19},{22,20},{25,27},{30,28}} | collective-permute-start | bytes 1572872 | tf_op jit(solution)/shard_map/ppermute | solution.py:123
  80.7 29.1 %collective-permute-start.15 = (bf16[512,1024]{1,0:T(8,128)(2,1)S(1)}, bf16[512,1024]{1,0:T(8,128)(2,1)S(1)}, u32[]{:S(2)}, u32[]{:S(2)}) collective-permute-start(bf16[512,1024]{1,0:T(8,128)(2,1)S(1)} %get-tuple-element.52.q31), channel_id=1, source_target_pairs={{1,3},{6,4},{9,11},{14,12},{17,19},{22,20},{25,27},{30,28}} | collective-permute-start | bytes 3145736 | tf_op jit(solution)/shard_map/ppermute | solution.py:123
  83.1 30.9 %collective-permute-start.14 = (bf16[512,384]{1,0:T(8,128)(2,1)S(1)}, bf16[512,384]{1,0:T(8,128)(2,1)S(1)}, u32[]{:S(2)}, u32[]{:S(2)}) collective-permute-start(bf16[512,384]{1,0:T(8,128)(2,1)S(1)} %get-tuple-element.51), channel_id=1, source_target_pairs={{1,3},{6,4},{9,11},{14,12},{17,19},{22,20},{25,27},{30,28}} | collective-permute-start | bytes 1179656 | tf_op jit(solution)/shard_map/ppermute | solution.py:123
  98.6 15.5 %collective-permute-start.13 = (bf16[512,512]{1,0:T(8,128)(2,1)S(1)}, bf16[512,512]{1,0:T(8,128)(2,1)S(1)}, u32[]{:S(2)}, u32[]{:S(2)}) collective-permute-start(bf16[512,512]{1,0:T(8,128)(2,1)S(1)} %collective-permute-done.10.q3_two), channel_id=1, source_target_pairs={{3,2},{4,5},{11,10},{12,13},{19,18},{20,21},{27,26},{28,29}} | collective-permute-start | bytes 1572872 | tf_op jit(solution)/shard_map/ppermute | solution.py:123

commit v24 on v23

--- a/solution.py
+++ b/solution.py
@@ -388,29 +388,30 @@
         out_ref[...] = sigma_ref[...]
 
 
-def halves_kernel(place_ref, first_ref, second_ref, near_ref, other_ref):
-    near_ref[...] = first_ref[...]
-    other_ref[...] = second_ref[...]
+def halves_kernel(place_ref, separator_ref, near_ref, other_ref, sems):
+    half = near_ref.shape[1]
+    copies = []
+    for which, (side, out_ref) in enumerate(((place_ref[0], near_ref), (1 - place_ref[0], other_ref))):
+        source = separator_ref.at[:, pl.ds(pl.multiple_of(side * half, 128), half)]
+        copies.append(pltpu.make_async_copy(source, out_ref, sems.at[which]))
+        copies[-1].start()
+    for copy in copies:
+        copy.wait()
 
 
 def halves(place, separator):
     rows, nodes = separator.shape
-    chunk = rows // 4
-    half = lambda side: pl.BlockSpec((chunk, nodes // 2), lambda i, place: (i, side(place[0])))
-    out = jax.ShapeDtypeStruct((rows, nodes // 2), BF16)
+    vmem = pl.BlockSpec(memory_space=pltpu.VMEM)
     return pl.pallas_call(
         halves_kernel,
-        out_shape=(out, out),
-        grid_spec=pltpu.PrefetchScalarGridSpec(
-            num_scalar_prefetch=1,
-            grid=(4,),
-            in_specs=[half(lambda odd: odd), half(lambda odd: 1 - odd)],
-            out_specs=(half(lambda odd: 0), half(lambda odd: 0)),
-        ),
+        out_shape=(jax.ShapeDtypeStruct((rows, nodes // 2), BF16),) * 2,
+        in_specs=[pl.BlockSpec(memory_space=pltpu.SMEM), pl.BlockSpec(memory_space=pltpu.HBM)],
+        out_specs=(vmem, vmem),
+        scratch_shapes=[pltpu.SemaphoreType.DMA((2,))],
         compiler_params=pltpu.CompilerParams(vmem_limit_bytes=6 * MIB),
         cost_estimate=LIGHT,
         name="halves",
-    )(place, separator, separator)
+    )(place, separator)
 
 
 def near_kernel(place_ref, shifted_ref, sigma_ref, row_ref, near_ref, last_ref):
@@ -796,7 +797,7 @@
     across = turn(place, 0, 0, c0, across)
     column, h0_one, h2_one = own_column(place, row_near, row_other, c0, c2)
     c3 = [
-        moved(after(c1[0], last_three, near_two, near_zero, h2_one, across), 3, 1),
+        moved(after(c1[0], last_three, near_two, near_zero, across), 3, 1),
         moved(after(c1[1], far_zero, h2_one), 3, 1),
     ]
     prior = assemble(place, row_near, row_other, column, near_two, last_three, near_zero, far_zero)

time: 116 us -> 115 us (level)
  waiting for transfers between devices: 43 us -> 41.1 us
  Pallas kernels: 30.3 us -> 32.1 us
    ppermute x15, waiting for transfers between devices: 38.5 us -> 36.7 us  [moved(): lax.ppermute(value, ('dom', 'col'), route(source, target, lax.axis_size('...]
  transfers between devices with their start and end apart: 17 -> 17, of which waited for: 8 -> 8; matrix products, arithmetic and copies ran while one was open for 0% -> 0% of each run, Pallas kernels for 25% -> 26%
where the time goes in v24:
time: 115 us
  waiting for transfers between devices  41.1 us (36%)
  starting transfers between devices  37.1 us (32%)
  Pallas kernels  32.1 us (28%)
  between operations  3.19 us (3%)
  local copies, waits for them, and re-layouts  1.69 us (1%)
    ppermute x15, waiting for transfers between devices, moved(): lax.ppermute(value, ('dom', 'col'), route(source, target, lax.axis_size('...  36.7 us
    ppermute x15, starting transfers between devices, moved(): lax.ppermute(value, ('dom', 'col'), route(source, target, lax.axis_size('...  29.7 us
    ppermute x2, starting transfers between devices, passed_along(): lax.ppermute(value, axis, [(source, source + steps) for source in range(i...  7.47 us
    pallas_call x6, Pallas kernels, turn(): pl.pallas_call(turn_kernel, out_shape=jax.ShapeDtypeStruct((nodes, nodes)...  5.99 us
    ppermute x2, waiting for transfers between devices, passed_along(): lax.ppermute(value, axis, [(source, source + steps) for source in range(i...  4.44 us
    pallas_call x2, Pallas kernels, couple(): pl.pallas_call(functools.partial(couple_kernel, part * rows), out_shape=j...  3.77 us
    pallas_call x6, Pallas kernels, multiply(): pl.pallas_call(functools.partial(multiply_kernel, first, count, len(lefts...  3.48 us
    pallas_call x1, Pallas kernels, finish(): pl.pallas_call(finish_kernel, out_shape=(jax.ShapeDtypeStruct((rows, node...  2.6 us
  transfers between devices with their start and end apart: 17, of which 8 were waited for; matrix products, arithmetic and copies ran while one was open for 0% of the time, Pallas kernels for 26%

profile of v24, /device:TPU:1, one launch (start us, length us, event | category | flops | bytes accessed | tf_op | source)
XLA Modules:
  0.0 115.3 jit_solution(1986791751379221528)
XLA Ops:
  0.6 2.0 %collective-permute-start.5 = (bf16[512,2048]{1,0:T(8,128)(2,1)}, bf16[512,2048]{1,0:T(8,128)(2,1)}, u32[]{:S(2)}, u32[]{:S(2)}) collective-permute-start(bf16[512,2048]{1,0:T(8,128)(2,1)} %bitcast.8), channel_id=1, source_target_pairs={{2,1},{5,6},{10,9},{13,14},{18,17},{21,22},{26,25},{29,30}} | collective-permute-start | bytes 6291464 | tf_op jit(solution)/shard_map/ppermute | solution.py:123
  4.8 1.6 %copy-done.2 = bf16[1,512,2048]{2,1,0:T(8,128)(2,1)S(1)} copy-done((bf16[1,512,2048]{2,1,0:T(8,128)(2,1)S(1)}, bf16[1,512,2048]{2,1,0:T(8,128)(2,1)}, u32[]{:S(2)}) %copy-start.2) | copy-done | bytes 2097176
  7.4 5.5 %collective-permute-start = (bf16[512,1024]{1,0:T(8,128)(2,1)S(1)}, bf16[512,1024]{1,0:T(8,128)(2,1)S(1)}, u32[]{:S(2)}, u32[]{:S(2)}) collective-permute-start(bf16[512,1024]{1,0:T(8,128)(2,1)S(1)} %get-tuple-element.30), channel_id=1, source_target_pairs={{4,0},{8,4},{12,8},{5,1},{9,5},{13,9},{6,2},{10,6},{14,10},{7,3},{... | collective-permute-start | bytes 3145736 | tf_op jit(solution)/shard_map/ppermute | solution.py:20
  12.9 1.9 %collective-permute-start.6 = (bf16[512,1024]{1,0:T(8,128)(2,1)S(1)}, bf16[512,1024]{1,0:T(8,128)(2,1)S(1)}, u32[]{:S(2)}, u32[]{:S(2)}) collective-permute-start(bf16[512,1024]{1,0:T(8,128)(2,1)S(1)} %get-tuple-element.36), channel_id=1, source_target_pairs={{4,0},{8,4},{12,8},{5,1},{9,5},{13,9},{6,2},{10,6},{14,10},{7,3},{... | collective-permute-start | bytes 3145736 | tf_op jit(solution)/shard_map/ppermute | solution.py:20
  15.5 1.8 %coupling.1.weight_ref.refs_1_ = bf16[8,512,256]{2,1,0:T(8,128)(2,1)S(1)} custom-call(s32[1,2048]{1,0:T(1,128)S(1)} %bitcast.19), custom_call_target="tpu_custom_call" | custom-call | flops 1048576 | bytes 65536 | tf_op jit(solution)/shard_map/coupling/pallas_call | solution.py:70
  17.4 1.9 %couple.3.coupled_ref.refs_1_ = bf16[256,2048]{1,0:T(8,128)(2,1)S(1)} custom-call(f32[1]{0:T(128)S(6)} %copy.23.rate_ref.refs_0_, bf16[8,512,256]{2,1,0:T(8,128)(2,1)S(1)} %coupling.1.weight_ref.refs_1_, bf16[512,2048]{1,0:T(8,128)(2,1)S(1)} %bitcast.10), custom_call_target="tpu_custom_call" | custom-call | flops 1048576 | bytes 65536 | tf_op jit(solution)/shard_map/couple/pallas_call | solution.py:99
  19.3 1.9 %couple.2.coupled_ref.refs_0_ = bf16[256,2048]{1,0:T(8,128)(2,1)S(1)} custom-call(f32[1]{0:T(128)S(6)} %copy.23.rate_ref.refs_0_, bf16[8,512,256]{2,1,0:T(8,128)(2,1)S(1)} %coupling.1.weight_ref.refs_1_, bf16[512,2048]{1,0:T(8,128)(2,1)S(1)} %bitcast.11), custom_call_target="tpu_custom_call" | custom-call | flops 1048576 | bytes 65536 | tf_op jit(solution)/shard_map/couple/pallas_call | solution.py:99
  23.0 3.5 %collective-permute-done.shifted_ref = bf16[512,1024]{1,0:T(8,128)(2,1)S(1)} collective-permute-done((bf16[512,1024]{1,0:T(8,128)(2,1)S(1)}, bf16[512,1024]{1,0:T(8,128)(2,1)S(1)}, u32[]{:S(2)}, u32[]{:S(2)}) %collective-permute-start) | collective-permute-done | bytes 1048608 | tf_op jit(solution)/shard_map/ppermute | solution.py:20
  29.0 4.9 %collective-permute-start.1 = (bf16[512,384]{1,0:T(8,128)(2,1)S(1)}, bf16[512,384]{1,0:T(8,128)(2,1)S(1)}, u32[]{:S(2)}, u32[]{:S(2)}) collective-permute-start(bf16[512,384]{1,0:T(8,128)(2,1)S(1)} %get-tuple-element.32), channel_id=1, source_target_pairs={{3,1},{4,6},{11,9},{12,14},{19,17},{20,22},{27,25},{28,30}} | collective-permute-start | bytes 1179656 | tf_op jit(solution)/shard_map/ppermute | solution.py:123
  34.0 1.6 %couple_here.2.coupled_ref.second_ref.left_ref = bf16[512,2048]{1,0:T(8,128)(2,1)S(1)} custom-call(s32[5]{0:T(128)S(1)} %stack.16.place_ref, f32[1]{0:T(128)S(6)} %copy.23.rate_ref.refs_0_, bf16[8,512,256]{2,1,0:T(8,128)(2,1)S(1)} %coupling.1.weight_ref.refs_1_, bf16[512,2048]{1,0:T(8,128)(2,1)} %collective-permute-done.5.refs_2_), custom_call_target="tpu_custom_call" | custom-call | flops 1048576 | bytes 65536 | tf_op jit(solution)/shard_map/couple_here/pallas_call | solution.py:133
  41.2 1.7 %collective-permute-done.1.last_three = bf16[512,384]{1,0:T(8,128)(2,1)S(1)} collective-permute-done((bf16[512,384]{1,0:T(8,128)(2,1)S(1)}, bf16[512,384]{1,0:T(8,128)(2,1)S(1)}, u32[]{:S(2)}, u32[]{:S(2)}) %collective-permute-start.1) | collective-permute-done | bytes 393248 | tf_op jit(solution)/shard_map/ppermute | solution.py:123
  42.9 8.2 %collective-permute-start.7 = (bf16[256,2048]{1,0:T(8,128)(2,1)S(1)}, bf16[256,2048]{1,0:T(8,128)(2,1)S(1)}, u32[]{:S(2)}, u32[]{:S(2)}) collective-permute-start(bf16[256,2048]{1,0:T(8,128)(2,1)S(1)} %couple.2.coupled_ref.refs_0_), channel_id=1, source_target_pairs={{3,1},{4,6},{11,9},{12,14},{19,17},{20,22},{27,25},{28,30}} | collective-permute-start | bytes 3145736 | tf_op jit(solution)/shard_map/ppermute | solution.py:123
  51.7 4.2 %collective-permute-start.9 = (bf16[256,2048]{1,0:T(8,128)(2,1)S(1)}, bf16[256,2048]{1,0:T(8,128)(2,1)S(1)}, u32[]{:S(2)}, u32[]{:S(2)}) collective-permute-start(bf16[256,2048]{1,0:T(8,128)(2,1)S(1)} %couple.3.coupled_ref.refs_1_), channel_id=1, source_target_pairs={{3,1},{4,6},{11,9},{12,14},{19,17},{20,22},{27,25},{28,30}} | collective-permute-start | bytes 3145736 | tf_op jit(solution)/shard_map/ppermute | solution.py:123
  60.2 2.6 %collective-permute-done.7.coupled_ref.refs_0_ = bf16[256,2048]{1,0:T(8,128)(2,1)S(1)} collective-permute-done((bf16[256,2048]{1,0:T(8,128)(2,1)S(1)}, bf16[256,2048]{1,0:T(8,128)(2,1)S(1)}, u32[]{:S(2)}, u32[]{:S(2)}) %collective-permute-start.7) | collective-permute-done | bytes 1048608 | tf_op jit(solution)/shard_map/ppermute | solution.py:123
  63.7 10.3 %collective-permute-done.9.coupled_ref.refs_1_ = bf16[256,2048]{1,0:T(8,128)(2,1)S(1)} collective-permute-done((bf16[256,2048]{1,0:T(8,128)(2,1)S(1)}, bf16[256,2048]{1,0:T(8,128)(2,1)S(1)}, u32[]{:S(2)}, u32[]{:S(2)}) %collective-permute-start.9) | collective-permute-done | bytes 1048608 | tf_op jit(solution)/shard_map/ppermute | solution.py:123
  77.5 1.3 %collective-permute-start.10 = (bf16[512,512]{1,0:T(8,128)(2,1)S(1)}, bf16[512,512]{1,0:T(8,128)(2,1)S(1)}, u32[]{:S(2)}, u32[]{:S(2)}) collective-permute-start(bf16[512,512]{1,0:T(8,128)(2,1)S(1)} %multiply.9), channel_id=1, source_target_pairs={{1,3},{6,4},{9,11},{14,12},{17,19},{22,20},{25,27},{30,28}} | collective-permute-start | bytes 1572872 | tf_op jit(solution)/shard_map/ppermute | solution.py:123
  79.3 1.3 %collective-permute-start.15 = (bf16[512,1024]{1,0:T(8,128)(2,1)S(1)}, bf16[512,1024]{1,0:T(8,128)(2,1)S(1)}, u32[]{:S(2)}, u32[]{:S(2)}) collective-permute-start(bf16[512,1024]{1,0:T(8,128)(2,1)S(1)} %get-tuple-element.52.q31), channel_id=1, source_target_pairs={{1,3},{6,4},{9,11},{14,12},{17,19},{22,20},{25,27},{30,28}} | collective-permute-start | bytes 3145736 | tf_op jit(solution)/shard_map/ppermute | solution.py:123
  85.4 12.2 %collective-permute-done.10.q3_two = bf16[512,512]{1,0:T(8,128)(2,1)S(1)} collective-permute-done((bf16[512,512]{1,0:T(8,128)(2,1)S(1)}, bf16[512,512]{1,0:T(8,128)(2,1)S(1)}, u32[]{:S(2)}, u32[]{:S(2)}) %collective-permute-start.10) | collective-permute-done | bytes 524320 | tf_op jit(solution)/shard_map/ppermute | solution.py:123
  97.6 1.3 %collective-permute-start.13 = (bf16[512,512]{1,0:T(8,128)(2,1)S(1)}, bf16[512,512]{1,0:T(8,128)(2,1)S(1)}, u32[]{:S(2)}, u32[]{:S(2)}) collective-permute-start(bf16[512,512]{1,0:T(8,128)(2,1)S(1)} %collective-permute-done.10.q3_two), channel_id=1, source_target_pairs={{3,2},{4,5},{11,10},{12,13},{19,18},{20,21},{27,26},{28,29}} | collective-permute-start | bytes 1572872 | tf_op jit(solution)/shard_map/ppermute | solution.py:123
  98.9 2.6 %finish.1 = (bf16[512,2048]{1,0:T(8,128)(2,1)}, f32[1,512]{1,0:T(1,128)S(1)}) custom-call(s32[5]{0:T(128)S(1)} %tick.3.place_ref, bf16[512,2048]{1,0:T(8,128)(2,1)S(1)} %bitcast.12, bf16[512,2048]{1,0:T(8,128)(2,1)S(1)} %bitcast.17, bf16[512,1536]{1,0:T(8,128)(2,1)S(1)} %collective-permute-done.11.refs_0_.q0, ...), custom_call_target="tpu_custom_call" | custom-call | flops 14000000000 | bytes 65536 | tf_op jit(solution)/shard_map/finish/pallas_call | solution.py:618
  101.5 7.3 %collective-permute-done.15.q3_other = bf16[512,1024]{1,0:T(8,128)(2,1)S(1)} collective-permute-done((bf16[512,1024]{1,0:T(8,128)(2,1)S(1)}, bf16[512,1024]{1,0:T(8,128)(2,1)S(1)}, u32[]{:S(2)}, u32[]{:S(2)}) %collective-permute-start.15) | collective-permute-done | bytes 1048608 | tf_op jit(solution)/shard_map/ppermute | solution.py:123
  108.8 1.7 %finish_other.1.old_ref = bf16[512,2048]{1,0:T(8,128)(2,1)} custom-call(s32[5]{0:T(128)S(1)} %stack.16.place_ref, bf16[512,2048]{1,0:T(8,128)(2,1)S(1)} %bitcast.13, bf16[512,1024]{1,0:T(8,128)(2,1)S(1)} %collective-permute-done.15.q3_other, bf16[512,2048]{1,0:T(8,128)(2,1)} %get-tuple-element.54.old_ref), custom_call_target="tpu_custom_call", output_to_operand_aliasing={{}: (3, {})} | custom-call | flops 1048576 | bytes 65536 | tf_op jit(solution)/shard_map/finish_other/pallas_call | solution.py:716
  110.5 2.5 %collective-permute-done.14.q3_last = bf16[512,384]{1,0:T(8,128)(2,1)S(1)} collective-permute-done((bf16[512,384]{1,0:T(8,128)(2,1)S(1)}, bf16[512,384]{1,0:T(8,128)(2,1)S(1)}, u32[]{:S(2)}, u32[]{:S(2)}) %collective-permute-start.14) | collective-permute-done | bytes 393248 | tf_op jit(solution)/shard_map/ppermute | solution.py:123
  113.0 2.1 %finish_last.1 = (bf16[512,2048]{1,0:T(8,128)(2,1)}, f32[1,512]{1,0:T(1,128)}) custom-call(s32[5]{0:T(128)S(1)} %stack.16.place_ref, bf16[512,2048]{1,0:T(8,128)(2,1)S(1)} %bitcast.14, bf16[512,512]{1,0:T(8,128)(2,1)S(1)} %collective-permute-done.13.q2_last, bf16[512,384]{1,0:T(8,128)(2,1)S(1)} %collective-permute-done.14.q3_last, ...), custom_call_target="tpu_custom_call", output_to_operand_aliasing={{0}: (4, {})} | custom-call | flops 1048576 | bytes 65536 | tf_op jit(solution)/shard_map/finish_last/pallas_call | solution.py:741
  (50 shorter events, 26.0 us)
Async XLA Ops:
  0.6 14.9 %copy-start.3 = (s32[2048]{0:T(1024)S(1)}, s32[2048]{0:T(1024)}, u32[]{:S(2)}) copy-start(s32[2048]{0:T(1024)} %param.13) | copy-start | bytes 24580
  0.6 28.4 %collective-permute-start.5 = (bf16[512,2048]{1,0:T(8,128)(2,1)}, bf16[512,2048]{1,0:T(8,128)(2,1)}, u32[]{:S(2)}, u32[]{:S(2)}) collective-permute-start(bf16[512,2048]{1,0:T(8,128)(2,1)} %bitcast.8), channel_id=1, source_target_pairs={{2,1},{5,6},{10,9},{13,14},{18,17},{21,22},{26,25},{29,30}} | collective-permute-start | bytes 6291464 | tf_op jit(solution)/shard_map/ppermute | solution.py:123
  2.6 36.8 %collective-permute-start.4 = (bf16[512,2048]{1,0:T(8,128)(2,1)}, bf16[512,2048]{1,0:T(8,128)(2,1)S(1)}, u32[]{:S(2)}, u32[]{:S(2)}) collective-permute-start(bf16[512,2048]{1,0:T(8,128)(2,1)} %bitcast.9), channel_id=1, source_target_pairs={{0,1},{7,6},{8,9},{15,14},{16,17},{23,22},{24,25},{31,30}} | collective-permute-start | bytes 6291464 | tf_op jit(solution)/shard_map/ppermute | solution.py:123
  4.8 1.6 %copy-start.2 = (bf16[1,512,2048]{2,1,0:T(8,128)(2,1)S(1)}, bf16[1,512,2048]{2,1,0:T(8,128)(2,1)}, u32[]{:S(2)}) copy-start(bf16[1,512,2048]{2,1,0:T(8,128)(2,1)} %param.8) | copy-start | bytes 6291460
  6.4 11.0 %copy-start = (bf16[1,512,2048]{2,1,0:T(8,128)(2,1)S(1)}, bf16[1,512,2048]{2,1,0:T(8,128)(2,1)}, u32[]{:S(2)}) copy-start(bf16[1,512,2048]{2,1,0:T(8,128)(2,1)} %param.9) | copy-start | bytes 6291460
  7.4 19.1 %collective-permute-start = (bf16[512,1024]{1,0:T(8,128)(2,1)S(1)}, bf16[512,1024]{1,0:T(8,128)(2,1)S(1)}, u32[]{:S(2)}, u32[]{:S(2)}) collective-permute-start(bf16[512,1024]{1,0:T(8,128)(2,1)S(1)} %get-tuple-element.30), channel_id=1, source_target_pairs={{4,0},{8,4},{12,8},{5,1},{9,5},{13,9},{6,2},{10,6},{14,10},{7,3},{... | collective-permute-start | bytes 3145736 | tf_op jit(solution)/shard_map/ppermute | solution.py:20
  12.9 24.8 %collective-permute-start.6 = (bf16[512,1024]{1,0:T(8,128)(2,1)S(1)}, bf16[512,1024]{1,0:T(8,128)(2,1)S(1)}, u32[]{:S(2)}, u32[]{:S(2)}) collective-permute-start(bf16[512,1024]{1,0:T(8,128)(2,1)S(1)} %get-tuple-element.36), channel_id=1, source_target_pairs={{4,0},{8,4},{12,8},{5,1},{9,5},{13,9},{6,2},{10,6},{14,10},{7,3},{... | collective-permute-start | bytes 3145736 | tf_op jit(solution)/shard_map/ppermute | solution.py:20
  22.1 4.4 %copy-start.1 = (bf16[1,512,2048]{2,1,0:T(8,128)(2,1)S(1)}, bf16[1,512,2048]{2,1,0:T(8,128)(2,1)}, u32[]{:S(2)}) copy-start(bf16[1,512,2048]{2,1,0:T(8,128)(2,1)} %param.7) | copy-start | bytes 6291460
  27.5 15.4 %collective-permute-start.3 = (bf16[512,1024]{1,0:T(8,128)(2,1)S(1)}, bf16[512,1024]{1,0:T(8,128)(2,1)S(1)}, u32[]{:S(2)}, u32[]{:S(2)}) collective-permute-start(bf16[512,1024]{1,0:T(8,128)(2,1)S(1)} %get-tuple-element.34.near_ref.near), channel_id=1, source_target_pairs={{0,1},{7,6},{8,9},{15,14},{16,17},{23,22},{24,25},{31,30}} | collective-permute-start | bytes 3145736 | tf_op jit(solution)/shard_map/ppermute | solution.py:123
  28.3 14.6 %collective-permute-start.2 = (bf16[512,896]{1,0:T(8,128)(2,1)S(1)}, bf16[512,896]{1,0:T(8,128)(2,1)S(1)}, u32[]{:S(2)}, u32[]{:S(2)}) collective-permute-start(bf16[512,896]{1,0:T(8,128)(2,1)S(1)} %get-tuple-element.33), channel_id=1, source_target_pairs={{2,1},{5,6},{10,9},{13,14},{18,17},{21,22},{26,25},{29,30}} | collective-permute-start | bytes 2752520 | tf_op jit(solution)/shard_map/ppermute | solution.py:123
  29.0 13.9 %collective-permute-start.1 = (bf16[512,384]{1,0:T(8,128)(2,1)S(1)}, bf16[512,384]{1,0:T(8,128)(2,1)S(1)}, u32[]{:S(2)}, u32[]{:S(2)}) collective-permute-start(bf16[512,384]{1,0:T(8,128)(2,1)S(1)} %get-tuple-element.32), channel_id=1, source_target_pairs={{3,1},{4,6},{11,9},{12,14},{19,17},{20,22},{27,25},{28,30}} | collective-permute-start | bytes 1179656 | tf_op jit(solution)/shard_map/ppermute | solution.py:123
  38.7 13.0 %collective-permute-start.8 = (bf16[512,384]{1,0:T(8,128)(2,1)S(1)}, bf16[512,384]{1,0:T(8,128)(2,1)S(1)}, u32[]{:S(2)}, u32[]{:S(2)}) collective-permute-start(bf16[512,384]{1,0:T(8,128)(2,1)S(1)} %get-tuple-element.38), channel_id=1, source_target_pairs={{0,1},{7,6},{8,9},{15,14},{16,17},{23,22},{24,25},{31,30}} | collective-permute-start | bytes 1179656 | tf_op jit(solution)/shard_map/ppermute | solution.py:123
  42.9 19.9 %collective-permute-start.7 = (bf16[256,2048]{1,0:T(8,128)(2,1)S(1)}, bf16[256,2048]{1,0:T(8,128)(2,1)S(1)}, u32[]{:S(2)}, u32[]{:S(2)}) collective-permute-start(bf16[256,2048]{1,0:T(8,128)(2,1)S(1)} %couple.2.coupled_ref.refs_0_), channel_id=1, source_target_pairs={{3,1},{4,6},{11,9},{12,14},{19,17},{20,22},{27,25},{28,30}} | collective-permute-start | bytes 3145736 | tf_op jit(solution)/shard_map/ppermute | solution.py:123
  51.7 22.3 %collective-permute-start.9 = (bf16[256,2048]{1,0:T(8,128)(2,1)S(1)}, bf16[256,2048]{1,0:T(8,128)(2,1)S(1)}, u32[]{:S(2)}, u32[]{:S(2)}) collective-permute-start(bf16[256,2048]{1,0:T(8,128)(2,1)S(1)} %couple.3.coupled_ref.refs_1_), channel_id=1, source_target_pairs={{3,1},{4,6},{11,9},{12,14},{19,17},{20,22},{27,25},{28,30}} | collective-permute-start | bytes 3145736 | tf_op jit(solution)/shard_map/ppermute | solution.py:123
  57.6 24.2 %collective-permute-start.11 = (bf16[512,1536]{1,0:T(8,128)(2,1)S(1)}, bf16[512,1536]{1,0:T(8,128)(2,1)S(1)}, u32[]{:S(2)}, u32[]{:S(2)}) collective-permute-start(bf16[512,1536]{1,0:T(8,128)(2,1)S(1)} %multiply.6.zero_ref.q01), channel_id=1, source_target_pairs={{1,0},{6,7},{9,8},{14,15},{17,16},{22,23},{25,24},{30,31}} | collective-permute-start | bytes 4718600 | tf_op jit(solution)/shard_map/ppermute | solution.py:123
  59.5 39.4 %collective-permute-start.16 = (bf16[512,1408]{1,0:T(8,128)(2,1)S(1)}, bf16[512,1408]{1,0:T(8,128)(2,1)S(1)}, u32[]{:S(2)}, u32[]{:S(2)}) collective-permute-start(bf16[512,1408]{1,0:T(8,128)(2,1)S(1)} %product_two.1.q21), channel_id=1, source_target_pairs={{1,2},{6,5},{9,10},{14,13},{17,18},{22,21},{25,26},{30,29}} | collective-permute-start | bytes 4325384 | tf_op jit(solution)/shard_map/ppermute | solution.py:123
  75.7 8.6 %collective-permute-start.12 = (bf16[512,512]{1,0:T(8,128)(2,1)S(1)}, bf16[512,512]{1,0:T(8,128)(2,1)S(1)}, u32[]{:S(2)}, u32[]{:S(2)}) collective-permute-start(bf16[512,512]{1,0:T(8,128)(2,1)S(1)} %multiply.7.zero_ref), channel_id=1, source_target_pairs={{1,0},{6,7},{9,8},{14,15},{17,16},{22,23},{25,24},{30,31}} | collective-permute-start | bytes 1572872 | tf_op jit(solution)/shard_map/ppermute | solution.py:123
  77.5 20.1 %collective-permute-start.10 = (bf16[512,512]{1,0:T(8,128)(2,1)S(1)}, bf16[512,512]{1,0:T(8,128)(2,1)S(1)}, u32[]{:S(2)}, u32[]{:S(2)}) collective-permute-start(bf16[512,512]{1,0:T(8,128)(2,1)S(1)} %multiply.9), channel_id=1, source_target_pairs={{1,3},{6,4},{9,11},{14,12},{17,19},{22,20},{25,27},{30,28}} | collective-permute-start | bytes 1572872 | tf_op jit(solution)/shard_map/ppermute | solution.py:123
  79.3 29.5 %collective-permute-start.15 = (bf16[512,1024]{1,0:T(8,128)(2,1)S(1)}, bf16[512,1024]{1,0:T(8,128)(2,1)S(1)}, u32[]{:S(2)}, u32[]{:S(2)}) collective-permute-start(bf16[512,1024]{1,0:T(8,128)(2,1)S(1)} %get-tuple-element.52.q31), channel_id=1, source_target_pairs={{1,3},{6,4},{9,11},{14,12},{17,19},{22,20},{25,27},{30,28}} | collective-permute-start | bytes 3145736 | tf_op jit(solution)/shard_map/ppermute | solution.py:123
  81.8 31.3 %collective-permute-start.14 = (bf16[512,384]{1,0:T(8,128)(2,1)S(1)}, bf16[512,384]{1,0:T(8,128)(2,1)S(1)}, u32[]{:S(2)}, u32[]{:S(2)}) collective-permute-start(bf16[512,384]{1,0:T(8,128)(2,1)S(1)} %get-tuple-element.51), channel_id=1, source_target_pairs={{1,3},{6,4},{9,11},{14,12},{17,19},{22,20},{25,27},{30,28}} | collective-permute-start | bytes 1179656 | tf_op jit(solution)/shard_map/ppermute | solution.py:123
  97.6 15.5 %collective-permute-start.13 = (bf16[512,512]{1,0:T(8,128)(2,1)S(1)}, bf16[512,512]{1,0:T(8,128)(2,1)S(1)}, u32[]{:S(2)}, u32[]{:S(2)}) collective-permute-start(bf16[512,512]{1,0:T(8,128)(2,1)S(1)} %collective-permute-done.10.q3_two), channel_id=1, source_target_pairs={{3,2},{4,5},{11,10},{12,13},{19,18},{20,21},{27,26},{28,29}} | collective-permute-start | bytes 1572872 | tf_op jit(solution)/shard_map/ppermute | solution.py:123

commit v25 on v24

--- a/solution.py
+++ b/solution.py
@@ -775,9 +775,8 @@
     p2 = moved(pivot, 2, 1)
     p0 = moved(pivot, 0, 1)
     weights = coupling(node_class)
-    c1 = [couple(pivot, weights, coupling_rate, part, 2) for part in range(2)]
-    across = turn(place, 1, 0, c1[0], None)
-    across = turn(place, 1, 1, c1[1], across)
+    c1 = couple(pivot, weights, coupling_rate)
+    across = turn(place, 1, 0, c1, None)
 
     near, other = halves(place, separator[0])
     near, other = passed_along(near, "dom", -1), passed_along(other, "dom", -1)
@@ -796,10 +795,7 @@
     c0 = couple_here(place, after(p0, across, far), weights, coupling_rate)
     across = turn(place, 0, 0, c0, across)
     column, h0_one, h2_one = own_column(place, row_near, row_other, c0, c2)
-    c3 = [
-        moved(after(c1[0], last_three, near_two, near_zero, across), 3, 1),
-        moved(after(c1[1], far_zero, h2_one), 3, 1),
-    ]
+    c3 = moved(after(c1, last_three, near_two, near_zero, far_zero, across), 3, 1)
     prior = assemble(place, row_near, row_other, column, near_two, last_three, near_zero, far_zero)
 
     h0 = half_product(place, c0, prior, h0_one)
@@ -809,16 +805,15 @@
     q2_own = product_two(place, h2, across, q0_own)
     q2 = moved(q2_own, 1, 2)
 
-    across = turn(place, 3, 0, c3[0], after(across, q2_own))
-    across = turn(place, 3, 1, c3[1], across)
+    across = turn(place, 3, 0, c3, after(across, q2_own))
     q03 = multiply(place, [h0], across, lambda odd: 3 - 3 * odd, 1)
     q0_last = moved(q03, 1, 0)
-    h3 = multiply(place, [after(c3[0], q03), c3[1]], prior)
+    h3 = multiply(place, [after(c3, q03)], prior)
     q32 = multiply(place, [h3], across, lambda odd: 2 - odd, 1)
     q3_two = moved(q32, 1, 3)
     q3_own, q33 = product_rest(place, h3, across, after(q03, q32))
     q3_other, q3_last = moved(q3_own, 1, 3), moved(q33, 1, 3)
-    h1 = multiply(place, [after(c1[0], q3_own), c1[1]], prior)
+    h1 = multiply(place, [after(c1, q3_own)], prior)
     q11 = multiply(place, [h1], across, lambda odd: 1 + odd, 1)
     received = (q0, q0_last, q2, q3_two)
     kept = (q0_own, q11, q2_own, q3_own)

time: 115 us -> 120 us (1.043); the launches traced: 115 us -> 119 us
  waiting for transfers between devices: 41.1 us -> 48.7 us
  Pallas kernels: 32.1 us -> 27.8 us
    ppermute x15 -> x14, waiting for transfers between devices: 36.7 us -> 42.3 us  [moved(): lax.ppermute(value, ('dom', 'col'), route(source, target, lax.axis_size('...]
    ppermute x2, waiting for transfers between devices: 4.44 us -> 6.37 us  [passed_along(): lax.ppermute(value, axis, [(source, source + steps) for source in range(i...]
    pallas_call x2 -> x1, Pallas kernels: 3.77 us -> 2.42 us  [couple(): pl.pallas_call(functools.partial(couple_kernel, part * rows), out_shape=j...]
    pallas_call x6 -> x4, Pallas kernels: 5.99 us -> 4.85 us  [turn(): pl.pallas_call(turn_kernel, out_shape=jax.ShapeDtypeStruct((nodes, nodes)...]
    ppermute x15 -> x14, starting transfers between devices: 29.7 us -> 29.7 us  [moved(): lax.ppermute(value, ('dom', 'col'), route(source, target, lax.axis_size('...]
  transfers between devices with their start and end apart: 17 -> 16, of which waited for: 8 -> 7; matrix products, arithmetic and copies ran while one was open for 0% -> 0% of each run, Pallas kernels for 26% -> 22%
where the time goes in v25:
time: 120 us; the launch traced here: 119 us
  waiting for transfers between devices  48.7 us (41%)
  starting transfers between devices  37.2 us (31%)
  Pallas kernels  27.8 us (23%)
  between operations  3.15 us (3%)
  local copies, waits for them, and re-layouts  1.69 us (1%)
    ppermute x14, waiting for transfers between devices, moved(): lax.ppermute(value, ('dom', 'col'), route(source, target, lax.axis_size('...  42.3 us
    ppermute x14, starting transfers between devices, moved(): lax.ppermute(value, ('dom', 'col'), route(source, target, lax.axis_size('...  29.7 us
    ppermute x2, starting transfers between devices, passed_along(): lax.ppermute(value, axis, [(source, source + steps) for source in range(i...  7.47 us
    ppermute x2, waiting for transfers between devices, passed_along(): lax.ppermute(value, axis, [(source, source + steps) for source in range(i...  6.37 us
    pallas_call x4, Pallas kernels, turn(): pl.pallas_call(turn_kernel, out_shape=jax.ShapeDtypeStruct((nodes, nodes)...  4.85 us
    pallas_call x6, Pallas kernels, multiply(): pl.pallas_call(functools.partial(multiply_kernel, first, count, len(lefts...  3.48 us
    pallas_call x1, Pallas kernels, finish(): pl.pallas_call(finish_kernel, out_shape=(jax.ShapeDtypeStruct((rows, node...  2.64 us
    pallas_call x1, Pallas kernels, couple(): pl.pallas_call(functools.partial(couple_kernel, part * rows), out_shape=j...  2.42 us
  transfers between devices with their start and end apart: 16, of which 7 were waited for; matrix products, arithmetic and copies ran while one was open for 0% of the time, Pallas kernels for 22%

profile of v25, /device:TPU:1, one launch (start us, length us, event | category | flops | bytes accessed | tf_op | source)
XLA Modules:
  0.0 118.5 jit_solution(9582197546163378687)
XLA Ops:
  0.6 2.0 %collective-permute-start.5 = (bf16[512,2048]{1,0:T(8,128)(2,1)}, bf16[512,2048]{1,0:T(8,128)(2,1)}, u32[]{:S(2)}, u32[]{:S(2)}) collective-permute-start(bf16[512,2048]{1,0:T(8,128)(2,1)} %bitcast.8), channel_id=1, source_target_pairs={{2,1},{5,6},{10,9},{13,14},{18,17},{21,22},{26,25},{29,30}} | collective-permute-start | bytes 6291464 | tf_op jit(solution)/shard_map/ppermute | solution.py:123
  4.8 1.6 %copy-done.2 = bf16[1,512,2048]{2,1,0:T(8,128)(2,1)S(1)} copy-done((bf16[1,512,2048]{2,1,0:T(8,128)(2,1)S(1)}, bf16[1,512,2048]{2,1,0:T(8,128)(2,1)}, u32[]{:S(2)}) %copy-start.2) | copy-done | bytes 2097176
  7.4 5.5 %collective-permute-start = (bf16[512,1024]{1,0:T(8,128)(2,1)S(1)}, bf16[512,1024]{1,0:T(8,128)(2,1)S(1)}, u32[]{:S(2)}, u32[]{:S(2)}) collective-permute-start(bf16[512,1024]{1,0:T(8,128)(2,1)S(1)} %get-tuple-element.29), channel_id=1, source_target_pairs={{4,0},{8,4},{12,8},{5,1},{9,5},{13,9},{6,2},{10,6},{14,10},{7,3},{... | collective-permute-start | bytes 3145736 | tf_op jit(solution)/shard_map/ppermute | solution.py:20
  12.9 1.9 %collective-permute-start.4 = (bf16[512,1024]{1,0:T(8,128)(2,1)S(1)}, bf16[512,1024]{1,0:T(8,128)(2,1)S(1)}, u32[]{:S(2)}, u32[]{:S(2)}) collective-permute-start(bf16[512,1024]{1,0:T(8,128)(2,1)S(1)} %get-tuple-element.34), channel_id=1, source_target_pairs={{4,0},{8,4},{12,8},{5,1},{9,5},{13,9},{6,2},{10,6},{14,10},{7,3},{... | collective-permute-start | bytes 3145736 | tf_op jit(solution)/shard_map/ppermute | solution.py:20
  15.5 1.8 %coupling.1.weight_ref.refs_1_ = bf16[8,512,256]{2,1,0:T(8,128)(2,1)S(1)} custom-call(s32[1,2048]{1,0:T(1,128)S(1)} %bitcast.18), custom_call_target="tpu_custom_call" | custom-call | flops 1048576 | bytes 65536 | tf_op jit(solution)/shard_map/coupling/pallas_call | solution.py:70
  17.4 2.4 %couple.1.coupled_ref.refs_0_ = bf16[512,2048]{1,0:T(8,128)(2,1)S(1)} custom-call(f32[1]{0:T(128)S(6)} %copy.19.rate_ref.refs_0_, bf16[8,512,256]{2,1,0:T(8,128)(2,1)S(1)} %coupling.1.weight_ref.refs_1_, bf16[512,2048]{1,0:T(8,128)(2,1)S(1)} %bitcast.10), custom_call_target="tpu_custom_call" | custom-call | flops 1048576 | bytes 65536 | tf_op jit(solution)/shard_map/couple/pallas_call | solution.py:99
  19.8 1.2 %turn.4.refs_0_ = bf16[2048,2048]{1,0:T(8,128)(2,1)S(1)} custom-call(s32[5]{0:T(128)S(1)} %stack.16.place_ref, bf16[512,2048]{1,0:T(8,128)(2,1)S(1)} %couple.1.coupled_ref.refs_0_), custom_call_target="tpu_custom_call" | custom-call | flops 1048576 | bytes 65536 | tf_op jit(solution)/shard_map/turn/pallas_call | solution.py:155
  21.0 5.5 %collective-permute-done.shifted_ref = bf16[512,1024]{1,0:T(8,128)(2,1)S(1)} collective-permute-done((bf16[512,1024]{1,0:T(8,128)(2,1)S(1)}, bf16[512,1024]{1,0:T(8,128)(2,1)S(1)}, u32[]{:S(2)}, u32[]{:S(2)}) %collective-permute-start) | collective-permute-done | bytes 1048608 | tf_op jit(solution)/shard_map/ppermute | solution.py:20
  29.0 4.9 %collective-permute-start.1 = (bf16[512,384]{1,0:T(8,128)(2,1)S(1)}, bf16[512,384]{1,0:T(8,128)(2,1)S(1)}, u32[]{:S(2)}, u32[]{:S(2)}) collective-permute-start(bf16[512,384]{1,0:T(8,128)(2,1)S(1)} %get-tuple-element.31), channel_id=1, source_target_pairs={{3,1},{4,6},{11,9},{12,14},{19,17},{20,22},{27,25},{28,30}} | collective-permute-start | bytes 1179656 | tf_op jit(solution)/shard_map/ppermute | solution.py:123
  34.0 1.6 %couple_here.2.coupled_ref.second_ref.left_ref = bf16[512,2048]{1,0:T(8,128)(2,1)S(1)} custom-call(s32[5]{0:T(128)S(1)} %stack.16.place_ref, f32[1]{0:T(128)S(6)} %copy.19.rate_ref.refs_0_, bf16[8,512,256]{2,1,0:T(8,128)(2,1)S(1)} %coupling.1.weight_ref.refs_1_, bf16[512,2048]{1,0:T(8,128)(2,1)} %collective-permute-done.5.refs_2_), custom_call_target="tpu_custom_call" | custom-call | flops 1048576 | bytes 65536 | tf_op jit(solution)/shard_map/couple_here/pallas_call | solution.py:133
  35.6 1.2 %turn.5.refs_0_ = bf16[2048,2048]{1,0:T(8,128)(2,1)S(1)} custom-call(s32[5]{0:T(128)S(1)} %stack.16.place_ref, bf16[512,2048]{1,0:T(8,128)(2,1)S(1)} %couple_here.2.coupled_ref.second_ref.left_ref, bf16[2048,2048]{1,0:T(8,128)(2,1)S(1)} %turn.4.refs_0_), custom_call_target="tpu_custom_call", output_to_operand_aliasing={{}: (2, {})} | custom-call | flops 1048576 | bytes 65536 | tf_op jit(solution)/shard_map/turn/pallas_call | solution.py:155
  40.0 1.2 %turn.6.refs_1_.right_ref.refs_0_ = bf16[2048,2048]{1,0:T(8,128)(2,1)S(1)} custom-call(s32[5]{0:T(128)S(1)} %stack.16.place_ref, bf16[512,2048]{1,0:T(8,128)(2,1)S(1)} %couple_here.3.coupled_ref.first_ref.left_ref, bf16[2048,2048]{1,0:T(8,128)(2,1)S(1)} %turn.5.refs_0_), custom_call_target="tpu_custom_call", output_to_operand_aliasing={{}: (2, {})} | custom-call | flops 1048576 | bytes 65536 | tf_op jit(solution)/shard_map/turn/pallas_call | solution.py:155
  41.2 1.7 %collective-permute-done.1.last_three = bf16[512,384]{1,0:T(8,128)(2,1)S(1)} collective-permute-done((bf16[512,384]{1,0:T(8,128)(2,1)S(1)}, bf16[512,384]{1,0:T(8,128)(2,1)S(1)}, u32[]{:S(2)}, u32[]{:S(2)}) %collective-permute-start.1) | collective-permute-done | bytes 393248 | tf_op jit(solution)/shard_map/ppermute | solution.py:123
  42.9 12.5 %collective-permute-start.8 = (bf16[512,2048]{1,0:T(8,128)(2,1)S(1)}, bf16[512,2048]{1,0:T(8,128)(2,1)S(1)}, u32[]{:S(2)}, u32[]{:S(2)}) collective-permute-start(bf16[512,2048]{1,0:T(8,128)(2,1)S(1)} %couple.1.coupled_ref.refs_0_), channel_id=1, source_target_pairs={{3,1},{4,6},{11,9},{12,14},{19,17},{20,22},{27,25},{28,30}} | collective-permute-start | bytes 6291464 | tf_op jit(solution)/shard_map/ppermute | solution.py:123
  60.3 17.9 %collective-permute-done.8.coupled_ref.refs_0_ = bf16[512,2048]{1,0:T(8,128)(2,1)S(1)} collective-permute-done((bf16[512,2048]{1,0:T(8,128)(2,1)S(1)}, bf16[512,2048]{1,0:T(8,128)(2,1)S(1)}, u32[]{:S(2)}, u32[]{:S(2)}) %collective-permute-start.8) | collective-permute-done | bytes 2097184 | tf_op jit(solution)/shard_map/ppermute | solution.py:123
  78.2 1.2 %turn.7.refs_1_.right_ref = bf16[2048,2048]{1,0:T(8,128)(2,1)S(1)} custom-call(s32[5]{0:T(128)S(1)} %stack.16.place_ref, bf16[512,2048]{1,0:T(8,128)(2,1)S(1)} %collective-permute-done.8.coupled_ref.refs_0_, bf16[2048,2048]{1,0:T(8,128)(2,1)S(1)} %turn.6.refs_1_.right_ref.refs_0_), custom_call_target="tpu_custom_call", output_to_operand_aliasing={{}: (2, {})} | custom-call | flops 1048576 | bytes 65536 | tf_op jit(solution)/shard_map/turn/pallas_call | solution.py:155
  82.0 1.3 %collective-permute-start.9 = (bf16[512,512]{1,0:T(8,128)(2,1)S(1)}, bf16[512,512]{1,0:T(8,128)(2,1)S(1)}, u32[]{:S(2)}, u32[]{:S(2)}) collective-permute-start(bf16[512,512]{1,0:T(8,128)(2,1)S(1)} %multiply.9), channel_id=1, source_target_pairs={{1,3},{6,4},{9,11},{14,12},{17,19},{22,20},{25,27},{30,28}} | collective-permute-start | bytes 1572872 | tf_op jit(solution)/shard_map/ppermute | solution.py:123
  85.0 1.3 %collective-permute-start.14 = (bf16[512,1024]{1,0:T(8,128)(2,1)S(1)}, bf16[512,1024]{1,0:T(8,128)(2,1)S(1)}, u32[]{:S(2)}, u32[]{:S(2)}) collective-permute-start(bf16[512,1024]{1,0:T(8,128)(2,1)S(1)} %get-tuple-element.50.q31), channel_id=1, source_target_pairs={{1,3},{6,4},{9,11},{14,12},{17,19},{22,20},{25,27},{30,28}} | collective-permute-start | bytes 3145736 | tf_op jit(solution)/shard_map/ppermute | solution.py:123
  86.3 1.3 %collective-permute-start.13 = (bf16[512,384]{1,0:T(8,128)(2,1)S(1)}, bf16[512,384]{1,0:T(8,128)(2,1)S(1)}, u32[]{:S(2)}, u32[]{:S(2)}) collective-permute-start(bf16[512,384]{1,0:T(8,128)(2,1)S(1)} %get-tuple-element.49), channel_id=1, source_target_pairs={{1,3},{6,4},{9,11},{14,12},{17,19},{22,20},{25,27},{30,28}} | collective-permute-start | bytes 1179656 | tf_op jit(solution)/shard_map/ppermute | solution.py:123
  89.9 11.8 %collective-permute-done.9.q3_two = bf16[512,512]{1,0:T(8,128)(2,1)S(1)} collective-permute-done((bf16[512,512]{1,0:T(8,128)(2,1)S(1)}, bf16[512,512]{1,0:T(8,128)(2,1)S(1)}, u32[]{:S(2)}, u32[]{:S(2)}) %collective-permute-start.9) | collective-permute-done | bytes 524320 | tf_op jit(solution)/shard_map/ppermute | solution.py:123
  101.7 1.3 %collective-permute-start.12 = (bf16[512,512]{1,0:T(8,128)(2,1)S(1)}, bf16[512,512]{1,0:T(8,128)(2,1)S(1)}, u32[]{:S(2)}, u32[]{:S(2)}) collective-permute-start(bf16[512,512]{1,0:T(8,128)(2,1)S(1)} %collective-permute-done.9.q3_two), channel_id=1, source_target_pairs={{3,2},{4,5},{11,10},{12,13},{19,18},{20,21},{27,26},{28,29}} | collective-permute-start | bytes 1572872 | tf_op jit(solution)/shard_map/ppermute | solution.py:123
  103.0 2.6 %finish.1 = (bf16[512,2048]{1,0:T(8,128)(2,1)}, f32[1,512]{1,0:T(1,128)S(1)}) custom-call(s32[5]{0:T(128)S(1)} %tick.3.place_ref, bf16[512,2048]{1,0:T(8,128)(2,1)S(1)} %bitcast.11, bf16[512,2048]{1,0:T(8,128)(2,1)S(1)} %bitcast.16, bf16[512,1536]{1,0:T(8,128)(2,1)S(1)} %collective-permute-done.10.refs_0_.q0, ...), custom_call_target="tpu_custom_call" | custom-call | flops 14000000000 | bytes 65536 | tf_op jit(solution)/shard_map/finish/pallas_call | solution.py:618
  105.7 7.3 %collective-permute-done.14.q3_other = bf16[512,1024]{1,0:T(8,128)(2,1)S(1)} collective-permute-done((bf16[512,1024]{1,0:T(8,128)(2,1)S(1)}, bf16[512,1024]{1,0:T(8,128)(2,1)S(1)}, u32[]{:S(2)}, u32[]{:S(2)}) %collective-permute-start.14) | collective-permute-done | bytes 1048608 | tf_op jit(solution)/shard_map/ppermute | solution.py:123
  113.6 3.6 %collective-permute-done.13.q3_last = bf16[512,384]{1,0:T(8,128)(2,1)S(1)} collective-permute-done((bf16[512,384]{1,0:T(8,128)(2,1)S(1)}, bf16[512,384]{1,0:T(8,128)(2,1)S(1)}, u32[]{:S(2)}, u32[]{:S(2)}) %collective-permute-start.13) | collective-permute-done | bytes 393248 | tf_op jit(solution)/shard_map/ppermute | solution.py:123
  (45 shorter events, 20.6 us)
Async XLA Ops:
  0.6 14.9 %copy-start.3 = (s32[2048]{0:T(1024)S(1)}, s32[2048]{0:T(1024)}, u32[]{:S(2)}) copy-start(s32[2048]{0:T(1024)} %param.13) | copy-start | bytes 24580
  0.6 28.4 %collective-permute-start.5 = (bf16[512,2048]{1,0:T(8,128)(2,1)}, bf16[512,2048]{1,0:T(8,128)(2,1)}, u32[]{:S(2)}, u32[]{:S(2)}) collective-permute-start(bf16[512,2048]{1,0:T(8,128)(2,1)} %bitcast.8), channel_id=1, source_target_pairs={{2,1},{5,6},{10,9},{13,14},{18,17},{21,22},{26,25},{29,30}} | collective-permute-start | bytes 6291464 | tf_op jit(solution)/shard_map/ppermute | solution.py:123
  2.6 36.8 %collective-permute-start.7 = (bf16[512,2048]{1,0:T(8,128)(2,1)}, bf16[512,2048]{1,0:T(8,128)(2,1)S(1)}, u32[]{:S(2)}, u32[]{:S(2)}) collective-permute-start(bf16[512,2048]{1,0:T(8,128)(2,1)} %bitcast.9), channel_id=1, source_target_pairs={{0,1},{7,6},{8,9},{15,14},{16,17},{23,22},{24,25},{31,30}} | collective-permute-start | bytes 6291464 | tf_op jit(solution)/shard_map/ppermute | solution.py:123
  4.8 1.6 %copy-start.2 = (bf16[1,512,2048]{2,1,0:T(8,128)(2,1)S(1)}, bf16[1,512,2048]{2,1,0:T(8,128)(2,1)}, u32[]{:S(2)}) copy-start(bf16[1,512,2048]{2,1,0:T(8,128)(2,1)} %param.8) | copy-start | bytes 6291460
  6.4 11.0 %copy-start = (bf16[1,512,2048]{2,1,0:T(8,128)(2,1)S(1)}, bf16[1,512,2048]{2,1,0:T(8,128)(2,1)}, u32[]{:S(2)}) copy-start(bf16[1,512,2048]{2,1,0:T(8,128)(2,1)} %param.9) | copy-start | bytes 6291460
  7.4 19.1 %collective-permute-start = (bf16[512,1024]{1,0:T(8,128)(2,1)S(1)}, bf16[512,1024]{1,0:T(8,128)(2,1)S(1)}, u32[]{:S(2)}, u32[]{:S(2)}) collective-permute-start(bf16[512,1024]{1,0:T(8,128)(2,1)S(1)} %get-tuple-element.29), channel_id=1, source_target_pairs={{4,0},{8,4},{12,8},{5,1},{9,5},{13,9},{6,2},{10,6},{14,10},{7,3},{... | collective-permute-start | bytes 3145736 | tf_op jit(solution)/shard_map/ppermute | solution.py:20
  12.9 24.8 %collective-permute-start.4 = (bf16[512,1024]{1,0:T(8,128)(2,1)S(1)}, bf16[512,1024]{1,0:T(8,128)(2,1)S(1)}, u32[]{:S(2)}, u32[]{:S(2)}) collective-permute-start(bf16[512,1024]{1,0:T(8,128)(2,1)S(1)} %get-tuple-element.34), channel_id=1, source_target_pairs={{4,0},{8,4},{12,8},{5,1},{9,5},{13,9},{6,2},{10,6},{14,10},{7,3},{... | collective-permute-start | bytes 3145736 | tf_op jit(solution)/shard_map/ppermute | solution.py:20
  19.8 6.7 %copy-start.1 = (bf16[1,512,2048]{2,1,0:T(8,128)(2,1)S(1)}, bf16[1,512,2048]{2,1,0:T(8,128)(2,1)}, u32[]{:S(2)}) copy-start(bf16[1,512,2048]{2,1,0:T(8,128)(2,1)} %param.7) | copy-start | bytes 6291460
  27.5 15.4 %collective-permute-start.3 = (bf16[512,1024]{1,0:T(8,128)(2,1)S(1)}, bf16[512,1024]{1,0:T(8,128)(2,1)S(1)}, u32[]{:S(2)}, u32[]{:S(2)}) collective-permute-start(bf16[512,1024]{1,0:T(8,128)(2,1)S(1)} %get-tuple-element.33.near_ref.near), channel_id=1, source_target_pairs={{0,1},{7,6},{8,9},{15,14},{16,17},{23,22},{24,25},{31,30}} | collective-permute-start | bytes 3145736 | tf_op jit(solution)/shard_map/ppermute | solution.py:123
  28.3 14.6 %collective-permute-start.2 = (bf16[512,896]{1,0:T(8,128)(2,1)S(1)}, bf16[512,896]{1,0:T(8,128)(2,1)S(1)}, u32[]{:S(2)}, u32[]{:S(2)}) collective-permute-start(bf16[512,896]{1,0:T(8,128)(2,1)S(1)} %get-tuple-element.32), channel_id=1, source_target_pairs={{2,1},{5,6},{10,9},{13,14},{18,17},{21,22},{26,25},{29,30}} | collective-permute-start | bytes 2752520 | tf_op jit(solution)/shard_map/ppermute | solution.py:123
  29.0 13.9 %collective-permute-start.1 = (bf16[512,384]{1,0:T(8,128)(2,1)S(1)}, bf16[512,384]{1,0:T(8,128)(2,1)S(1)}, u32[]{:S(2)}, u32[]{:S(2)}) collective-permute-start(bf16[512,384]{1,0:T(8,128)(2,1)S(1)} %get-tuple-element.31), channel_id=1, source_target_pairs={{3,1},{4,6},{11,9},{12,14},{19,17},{20,22},{27,25},{28,30}} | collective-permute-start | bytes 1179656 | tf_op jit(solution)/shard_map/ppermute | solution.py:123
  38.7 4.2 %collective-permute-start.6 = (bf16[512,384]{1,0:T(8,128)(2,1)S(1)}, bf16[512,384]{1,0:T(8,128)(2,1)S(1)}, u32[]{:S(2)}, u32[]{:S(2)}) collective-permute-start(bf16[512,384]{1,0:T(8,128)(2,1)S(1)} %get-tuple-element.37), channel_id=1, source_target_pairs={{0,1},{7,6},{8,9},{15,14},{16,17},{23,22},{24,25},{31,30}} | collective-permute-start | bytes 1179656 | tf_op jit(solution)/shard_map/ppermute | solution.py:123
  42.9 35.3 %collective-permute-start.8 = (bf16[512,2048]{1,0:T(8,128)(2,1)S(1)}, bf16[512,2048]{1,0:T(8,128)(2,1)S(1)}, u32[]{:S(2)}, u32[]{:S(2)}) collective-permute-start(bf16[512,2048]{1,0:T(8,128)(2,1)S(1)} %couple.1.coupled_ref.refs_0_), channel_id=1, source_target_pairs={{3,1},{4,6},{11,9},{12,14},{19,17},{20,22},{27,25},{28,30}} | collective-permute-start | bytes 6291464 | tf_op jit(solution)/shard_map/ppermute | solution.py:123
  57.7 25.7 %collective-permute-start.10 = (bf16[512,1536]{1,0:T(8,128)(2,1)S(1)}, bf16[512,1536]{1,0:T(8,128)(2,1)S(1)}, u32[]{:S(2)}, u32[]{:S(2)}) collective-permute-start(bf16[512,1536]{1,0:T(8,128)(2,1)S(1)} %multiply.6.zero_ref.q01), channel_id=1, source_target_pairs={{1,0},{6,7},{9,8},{14,15},{17,16},{22,23},{25,24},{30,31}} | collective-permute-start | bytes 4718600 | tf_op jit(solution)/shard_map/ppermute | solution.py:123
  59.5 43.5 %collective-permute-start.15 = (bf16[512,1408]{1,0:T(8,128)(2,1)S(1)}, bf16[512,1408]{1,0:T(8,128)(2,1)S(1)}, u32[]{:S(2)}, u32[]{:S(2)}) collective-permute-start(bf16[512,1408]{1,0:T(8,128)(2,1)S(1)} %product_two.1.q21), channel_id=1, source_target_pairs={{1,2},{6,5},{9,10},{14,13},{17,18},{22,21},{25,26},{30,29}} | collective-permute-start | bytes 4325384 | tf_op jit(solution)/shard_map/ppermute | solution.py:123
  80.0 8.7 %collective-permute-start.11 = (bf16[512,512]{1,0:T(8,128)(2,1)S(1)}, bf16[512,512]{1,0:T(8,128)(2,1)S(1)}, u32[]{:S(2)}, u32[]{:S(2)}) collective-permute-start(bf16[512,512]{1,0:T(8,128)(2,1)S(1)} %multiply.7.zero_ref), channel_id=1, source_target_pairs={{1,0},{6,7},{9,8},{14,15},{17,16},{22,23},{25,24},{30,31}} | collective-permute-start | bytes 1572872 | tf_op jit(solution)/shard_map/ppermute | solution.py:123
  82.0 19.7 %collective-permute-start.9 = (bf16[512,512]{1,0:T(8,128)(2,1)S(1)}, bf16[512,512]{1,0:T(8,128)(2,1)S(1)}, u32[]{:S(2)}, u32[]{:S(2)}) collective-permute-start(bf16[512,512]{1,0:T(8,128)(2,1)S(1)} %multiply.9), channel_id=1, source_target_pairs={{1,3},{6,4},{9,11},{14,12},{17,19},{22,20},{25,27},{30,28}} | collective-permute-start | bytes 1572872 | tf_op jit(solution)/shard_map/ppermute | solution.py:123
  85.0 27.9 %collective-permute-start.14 = (bf16[512,1024]{1,0:T(8,128)(2,1)S(1)}, bf16[512,1024]{1,0:T(8,128)(2,1)S(1)}, u32[]{:S(2)}, u32[]{:S(2)}) collective-permute-start(bf16[512,1024]{1,0:T(8,128)(2,1)S(1)} %get-tuple-element.50.q31), channel_id=1, source_target_pairs={{1,3},{6,4},{9,11},{14,12},{17,19},{22,20},{25,27},{30,28}} | collective-permute-start | bytes 3145736 | tf_op jit(solution)/shard_map/ppermute | solution.py:123
  86.3 30.8 %collective-permute-start.13 = (bf16[512,384]{1,0:T(8,128)(2,1)S(1)}, bf16[512,384]{1,0:T(8,128)(2,1)S(1)}, u32[]{:S(2)}, u32[]{:S(2)}) collective-permute-start(bf16[512,384]{1,0:T(8,128)(2,1)S(1)} %get-tuple-element.49), channel_id=1, source_target_pairs={{1,3},{6,4},{9,11},{14,12},{17,19},{22,20},{25,27},{30,28}} | collective-permute-start | bytes 1179656 | tf_op jit(solution)/shard_map/ppermute | solution.py:123
  101.7 15.5 %collective-permute-start.12 = (bf16[512,512]{1,0:T(8,128)(2,1)S(1)}, bf16[512,512]{1,0:T(8,128)(2,1)S(1)}, u32[]{:S(2)}, u32[]{:S(2)}) collective-permute-start(bf16[512,512]{1,0:T(8,128)(2,1)S(1)} %collective-permute-done.9.q3_two), channel_id=1, source_target_pairs={{3,2},{4,5},{11,10},{12,13},{19,18},{20,21},{27,26},{28,29}} | collective-permute-start | bytes 1572872 | tf_op jit(solution)/shard_map/ppermute | solution.py:123
